TPU v7x, 128 devices: a whole 4x4x4 slice. The times are simulated.
128 devices in a mesh: section: 2 (over z_hi), dp: 16 (over y, z_lo, core), tensor: 4 (over x).
Axes of the slice: x: 4, y: 4, z: 4 (z_hi: 2, z_lo: 2; z = z_hi * 2 + z_lo), core: 2. Of those that a mesh axis runs over, the one named last changes fastest.
Arguments:
- block_input: bfloat16 [2, 4096, 2048], P(None, ('dp', 'tensor')), may hold values from -6 to 6
- cotangent: bfloat16 [2, 4096, 2048], P(None, ('dp', 'tensor')), may hold values from -6 to 6
- doc_lengths: int32 [2, 6], replicated, may hold values from 1 to 4091, as said below
- bank_choice: int32 [2], replicated, may hold values from 0 to 7
- first_gain: bfloat16 [2, 2048], P('section'), may hold values from 0.5 to 1.5
- first_shift: bfloat16 [2, 2048], P('section'), may hold values from -1 to 1
- query_weight: bfloat16 [2, 2048, 2048], P('section', 'dp', 'tensor'), may hold values from -0.125 to 0.125
- query_bias: bfloat16 [2, 2048], P('section', 'tensor'), may hold values from -1 to 1
- keyval_weight: bfloat16 [2, 2048, 256], P('section', 'dp'), may hold values from -0.125 to 0.125
- value_bias: bfloat16 [2, 128], P('section'), may hold values from -2.5 to 2.5
- output_weight: bfloat16 [2, 2048, 2048], P('section', 'tensor', 'dp'), may hold values from -1 to 1
- output_bias: bfloat16 [2, 2048], P('section'), may hold values from -1 to 1
- second_gain: bfloat16 [2, 2048], P('section'), may hold values from 0.5 to 1.5
- second_shift: bfloat16 [2, 2048], P('section'), may hold values from -1 to 1
- upward_weight: bfloat16 [2, 2048, 8192], P('section', 'dp', 'tensor'), may hold values from -0.125 to 0.125
- upward_bias: bfloat16 [2, 8192], P('section', 'tensor'), may hold values from -2.5 to 2.5
- downward_weight: bfloat16 [2, 8192, 2048], P('section', 'tensor', 'dp'), may hold values from -0.0625 to 0.0625
- downward_bias: bfloat16 [2, 2048], P('section'), may hold values from -1 to 1
- query_shrink: bfloat16 [2, 8, 2048, 16], P('section'), may hold values from -0.125 to 0.125
- query_expand: bfloat16 [2, 8, 16, 2048], P('section', None, None, 'tensor'), may hold values from -0.75 to 0.75
- keyval_shrink: bfloat16 [2, 8, 2048, 16], P('section'), may hold values from -0.125 to 0.125
- keyval_expand: bfloat16 [2, 8, 16, 256], P('section'), may hold values from -0.75 to 0.75
- output_shrink: bfloat16 [2, 8, 2048, 16], P('section', None, 'tensor'), may hold values from -1 to 1
- output_expand: bfloat16 [2, 8, 16, 2048], P('section'), may hold values from -0.75 to 0.75
- upward_shrink: bfloat16 [2, 8, 2048, 16], P('section'), may hold values from -0.125 to 0.125
- upward_expand: bfloat16 [2, 8, 16, 8192], P('section', None, None, 'tensor'), may hold values from -0.75 to 0.75
- downward_shrink: bfloat16 [2, 8, 8192, 16], P('section', None, 'tensor'), may hold values from -0.0625 to 0.0625
- downward_expand: bfloat16 [2, 8, 16, 2048], P('section'), may hold values from -0.75 to 0.75
Outputs:
- section_outputs: bfloat16 [2, 2, 4096, 2048], P('section', None, ('dp', 'tensor'))
- input_grads: float32 [2, 2, 4096, 2048], P('section', None, ('dp', 'tensor'))
- query_shrink_grad: float32 [2, 8, 2048, 16], P('section')
- query_expand_grad: float32 [2, 8, 16, 2048], P('section', None, None, 'tensor')
- keyval_shrink_grad: float32 [2, 8, 2048, 16], P('section')
- keyval_expand_grad: float32 [2, 8, 16, 256], P('section')
- output_shrink_grad: float32 [2, 8, 2048, 16], P('section', None, 'tensor')
- output_expand_grad: float32 [2, 8, 16, 2048], P('section')
- upward_shrink_grad: float32 [2, 8, 2048, 16], P('section')
- upward_expand_grad: float32 [2, 8, 16, 8192], P('section', None, None, 'tensor')
- downward_shrink_grad: float32 [2, 8, 8192, 16], P('section', None, 'tensor')
- downward_expand_grad: float32 [2, 8, 16, 2048], P('section')
Inputs may be any that keep to these rules, and one draw needn't show every extreme that they name: `doc_lengths`: row i holds, in order, the lengths of the 6 documents packed into sequence i; every row sums to 4096.
All inputs are finite; a program needn't handle non-finite values.
Results may differ from a plain program's by a relative error of at most 0.025.
Values may be sent and summed in bfloat16 or wider, within the bound.
No kernel may reach another device: no remote copies, remote signals or barrier semaphores. Data moves between devices by JAX's collectives and lax.ppermute only.
A program may use at most 192 MiB of HBM per device.

v0:
```python
from functools import partial
import math

import jax
import jax.numpy as jnp
from jax import lax
from jax.sharding import PartitionSpec as P

WINDOW = 1024


epsilon = 1e-05
masked_score = -1e30


def passed_along(block, axis, distance):
    devices = range(lax.axis_size(axis))
    route = [(i - distance, i) for i in devices if i - distance in devices]
    return lax.ppermute(block, axis, route)


def as_sent(value):

    def short(part):
        return part.astype(jnp.bfloat16) if part.dtype == jnp.float32 else part

    return jax.tree.map(short, value)


def layer_norm(value, gain, shift):
    centred = value - jnp.mean(value, axis=-1, keepdims=True)
    variance = jnp.mean(centred * centred, axis=-1, keepdims=True)
    return centred * lax.rsqrt(variance + epsilon) * gain + shift


def plain(left, right):
    return jnp.dot(left, right, preferred_element_type=jnp.float32)


def precise(left, right):
    return jnp.dot(left, right, precision=lax.Precision.HIGHEST, preferred_element_type=jnp.float32)


def against(left, right):
    return lax.dot_general(
        left, right, (((1,), (1,)), ((), ())), preferred_element_type=jnp.float32
    )


def across(left, right):
    return lax.dot_general(
        left, right, (((0,), (0,)), ((), ())), preferred_element_type=jnp.float32
    )


def against_fine(left, right):
    return jnp.einsum(
        "tr,ir->ti",
        left,
        right,
        precision=lax.Precision.HIGHEST,
        preferred_element_type=jnp.float32,
    )


def across_fine(left, right):
    return jnp.einsum(
        "ti,tr->ir",
        left,
        right,
        precision=lax.Precision.HIGHEST,
        preferred_element_type=jnp.float32,
    )


def document_ids(lengths, positions):
    doc_ends = jnp.cumsum(lengths)
    return jnp.sum((positions[:, None] >= doc_ends[None, :]).astype(jnp.int32), axis=1)


def per_device(
    block_input,
    cotangent,
    doc_lengths,
    bank_choice,
    first_gain,
    first_shift,
    query_weight,
    query_bias,
    keyval_weight,
    value_bias,
    output_weight,
    output_bias,
    second_gain,
    second_shift,
    upward_weight,
    upward_bias,
    downward_weight,
    downward_bias,
    query_shrink,
    query_expand,
    keyval_shrink,
    keyval_expand,
    output_shrink,
    output_expand,
    upward_shrink,
    upward_expand,
    downward_shrink,
    downward_expand,
):
    section_rank = lax.axis_index("section")
    data_rank = lax.axis_index("dp")
    tensor_rank = lax.axis_index("tensor")
    data_size = lax.axis_size("dp")
    tensor_size = lax.axis_size("tensor")
    micro_count = block_input.shape[0]
    tok_rows = block_input.shape[1]
    model_width = block_input.shape[2]
    head_size = value_bias.shape[1]
    local_heads = query_bias.shape[1] // head_size
    group_count = data_size // data_size
    span_rows = tok_rows * tensor_size
    reach_count = WINDOW // span_rows
    base_position = data_rank % data_size * span_rows
    group_index = data_rank // data_size
    score_scale = 1.0 / math.sqrt(head_size)
    query_place = base_position + jnp.arange(span_rows, dtype=jnp.int32)
    key_place = (
        base_position
        - reach_count * span_rows
        + jnp.arange((reach_count + 1) * span_rows, dtype=jnp.int32)
    )
    own_start = tensor_rank * tok_rows
    frozen_vectors = tuple(
        (
            table[0].astype(jnp.float32)
            for table in (
                first_gain,
                first_shift,
                query_bias,
                value_bias,
                output_bias,
                second_gain,
                second_shift,
                upward_bias,
                downward_bias,
            )
        )
    )
    tables = tuple(
        (
            table[0]
            for table in (
                query_shrink,
                query_expand,
                keyval_shrink,
                keyval_expand,
                output_shrink,
                output_expand,
                upward_shrink,
                upward_expand,
                downward_shrink,
                downward_expand,
            )
        )
    )
    shards = (
        query_weight[0],
        keyval_weight[0],
        upward_weight[0],
        output_weight[0],
        downward_weight[0],
    )

    def fetch_frozen():
        return (
            lax.all_gather(shards[0], "dp", axis=0, tiled=True),
            lax.all_gather(shards[1], "dp", axis=0, tiled=True),
            lax.all_gather(shards[2], "dp", axis=0, tiled=True),
            lax.all_gather(shards[3], "dp", axis=1, tiled=True),
            lax.all_gather(shards[4], "dp", axis=1, tiled=True),
        )

    def spread(rows):
        return lax.all_gather(rows, "tensor", axis=0, tiled=True)

    def reduce_rows(partial_rows):
        return lax.psum_scatter(
            partial_rows.astype(jnp.bfloat16), "tensor", scatter_dimension=0, tiled=True
        ).astype(jnp.float32)

    def context(slot_index):
        sequence = slot_index * group_count + group_index
        lengths = lax.dynamic_index_in_dim(doc_lengths, sequence, 0, keepdims=False)
        bank_index = lax.dynamic_index_in_dim(bank_choice, sequence, 0, keepdims=False)
        query_doc = document_ids(lengths, query_place)
        key_doc = document_ids(lengths, key_place)
        distance = query_place[:, None] - key_place[None, :]
        allowed = (
            (key_place[None, :] >= 0)
            & (distance >= 0)
            & (distance < WINDOW)
            & (query_doc[:, None] == key_doc[None, :])
        )
        chosen = tuple(
            (lax.dynamic_index_in_dim(table, bank_index, 0, keepdims=False) for table in tables)
        )
        onehot = (jnp.arange(tables[0].shape[0]) == bank_index).astype(jnp.float32)
        return (allowed, chosen, onehot)

    def masked_scores(queries, keys_only, allowed):
        query_rows = queries.reshape(span_rows * local_heads, head_size)
        scores = (against(query_rows, keys_only) * score_scale).reshape(span_rows, local_heads, -1)
        return (query_rows, jnp.where(allowed[:, None, :], scores, masked_score))

    def forward(hidden, weights, allowed, chosen):
        query_matrix, keyval_matrix, upward_matrix, output_matrix, downward_matrix = weights
        (
            shrink_query,
            expand_query,
            shrink_keyval,
            expand_keyval,
            shrink_output,
            expand_output,
            shrink_upward,
            expand_upward,
            shrink_downward,
            expand_downward,
        ) = chosen
        keyval_bias = jnp.concatenate([jnp.zeros_like(frozen_vectors[3]), frozen_vectors[3]])
        normed_rows = layer_norm(hidden, frozen_vectors[0], frozen_vectors[1]).astype(jnp.bfloat16)
        normed = spread(normed_rows)
        low_rank = plain(normed, shrink_keyval)
        keyval = (
            plain(normed, keyval_matrix)
            + keyval_bias
            + precise(low_rank, expand_keyval.astype(jnp.float32))
        ).astype(jnp.bfloat16)
        query_low = plain(normed, shrink_query)
        queries = (
            plain(normed, query_matrix)
            + frozen_vectors[2]
            + precise(query_low, expand_query.astype(jnp.float32))
        ).astype(jnp.bfloat16)
        pieces = [keyval]
        for offset in range(1, reach_count + 1):
            pieces.insert(0, passed_along(keyval, "dp", offset))
        key_block = jnp.concatenate(pieces, axis=0)
        query_rows, scores = masked_scores(queries, key_block[:, :head_size], allowed)
        row_top = jnp.max(scores, axis=-1, keepdims=True)
        lifted = jnp.exp(scores - row_top)
        row_total = jnp.sum(lifted, axis=-1, keepdims=True)
        probabilities = (
            (lifted / row_total).astype(jnp.bfloat16).reshape(span_rows * local_heads, -1)
        )
        mixed_heads = plain(probabilities, key_block[:, head_size:]).reshape(
            span_rows, local_heads * head_size
        )
        mixed_heads = mixed_heads.astype(jnp.bfloat16)
        log_totals = row_top + jnp.log(row_total)
        output_low = plain(mixed_heads, shrink_output)
        attended = (
            reduce_rows(
                plain(mixed_heads, output_matrix)
                + precise(output_low, expand_output.astype(jnp.float32))
            )
            + frozen_vectors[4]
        )
        middle = hidden + attended
        second_rows = layer_norm(middle, frozen_vectors[5], frozen_vectors[6]).astype(jnp.bfloat16)
        second = spread(second_rows)
        upward_low = plain(second, shrink_upward)
        upward = (
            plain(second, upward_matrix)
            + frozen_vectors[7]
            + precise(upward_low, expand_upward.astype(jnp.float32))
        )
        activated = jax.nn.gelu(upward, approximate=True).astype(jnp.bfloat16)
        downward_low = plain(activated, shrink_downward)
        result = (
            middle
            + reduce_rows(
                plain(activated, downward_matrix)
                + precise(downward_low, expand_downward.astype(jnp.float32))
            )
            + frozen_vectors[8]
        )
        kept_values = (
            hidden,
            normed,
            query_low,
            queries,
            key_block,
            log_totals,
            mixed_heads,
            output_low,
            middle,
            second,
            upward_low,
            upward,
            activated,
            downward_low,
        )
        return (result, kept_values)

    def backward(kept_values, grad_out, weights, allowed, chosen):
        query_matrix, keyval_matrix, upward_matrix, output_matrix, downward_matrix = weights
        (
            shrink_query,
            expand_query,
            shrink_keyval,
            expand_keyval,
            shrink_output,
            expand_output,
            shrink_upward,
            expand_upward,
            shrink_downward,
            expand_downward,
        ) = chosen
        (
            hidden,
            normed,
            query_low,
            queries,
            key_block,
            log_totals,
            mixed_heads,
            output_low,
            middle,
            second,
            upward_low,
            upward,
            activated,
            downward_low,
        ) = kept_values
        grad_branch = spread(grad_out.astype(jnp.bfloat16))
        downward_inner = against(grad_branch, expand_downward)
        grad_activated = against(grad_branch, downward_matrix) + against_fine(
            downward_inner, shrink_downward
        )
        grad_shrink_downward = across_fine(activated, downward_inner)
        grad_expand_downward = across_fine(downward_low, grad_branch)
        gelu_back = jax.vjp(partial(jax.nn.gelu, approximate=True), upward)[1]
        grad_upward = gelu_back(grad_activated)[0].astype(jnp.bfloat16)
        upward_inner = against(grad_upward, expand_upward)
        grad_second = reduce_rows(
            against(grad_upward, upward_matrix) + against_fine(upward_inner, shrink_upward)
        )
        grad_shrink_upward = across_fine(second, upward_inner)
        grad_expand_upward = across_fine(upward_low, grad_upward)
        second_back = jax.vjp(
            lambda value: layer_norm(value, frozen_vectors[5], frozen_vectors[6]), middle
        )[1]
        grad_middle = grad_out + second_back(grad_second)[0]
        grad_attended = spread(grad_middle.astype(jnp.bfloat16))
        output_inner = against(grad_attended, expand_output)
        grad_mixed = (
            against(grad_attended, output_matrix) + against_fine(output_inner, shrink_output)
        ).astype(jnp.bfloat16)
        grad_shrink_output = across_fine(mixed_heads, output_inner)
        grad_expand_output = across_fine(output_low, grad_attended)
        keys_only = key_block[:, :head_size]
        values_only = key_block[:, head_size:]
        query_rows, scores = masked_scores(queries, keys_only, allowed)
        probabilities = jnp.exp(scores - log_totals)
        probs_low = probabilities.astype(jnp.bfloat16).reshape(span_rows * local_heads, -1)
        grad_rows = grad_mixed.reshape(span_rows * local_heads, head_size)
        grad_probs = against(grad_rows, values_only).reshape(span_rows, local_heads, -1)
        row_delta = jnp.sum(grad_probs * probabilities, axis=-1, keepdims=True)
        grad_scores = (
            (probabilities * (grad_probs - row_delta))
            .astype(jnp.bfloat16)
            .reshape(span_rows * local_heads, -1)
        )
        grad_queries = (
            (plain(grad_scores, keys_only) * score_scale)
            .reshape(span_rows, -1)
            .astype(jnp.bfloat16)
        )
        grad_keys = across(grad_scores, query_rows) * score_scale
        grad_values = across(probs_low, grad_rows)
        grad_block = jnp.concatenate([grad_keys, grad_values], axis=1)
        own_grads = grad_block[reach_count * span_rows :]
        for offset in range(1, reach_count + 1):
            begin = (reach_count - offset) * span_rows
            own_grads = own_grads + passed_along(
                grad_block[begin : begin + span_rows].astype(jnp.bfloat16), "dp", -offset
            ).astype(jnp.float32)
        query_inner = against(grad_queries, expand_query)
        grad_normed = against(grad_queries, query_matrix) + against_fine(query_inner, shrink_query)
        grad_shrink_query = across_fine(normed, query_inner)
        grad_expand_query = across_fine(query_low, grad_queries)
        grad_rows_in, grad_keyval = (
            lax.psum_scatter(
                grad_normed.astype(jnp.bfloat16), "tensor", scatter_dimension=0, tiled=True
            ).astype(jnp.float32),
            lax.psum_scatter(
                own_grads.astype(jnp.bfloat16), "tensor", scatter_dimension=0, tiled=True
            ).astype(jnp.float32),
        )
        grad_keyval = grad_keyval.astype(jnp.bfloat16)
        normed_rows = lax.dynamic_slice_in_dim(normed, own_start, tok_rows, 0)
        keyval_inner = against(grad_keyval, expand_keyval)
        grad_rows_in = (
            grad_rows_in
            + against(grad_keyval, keyval_matrix)
            + against_fine(keyval_inner, shrink_keyval)
        )
        grad_shrink_keyval = across_fine(normed_rows, keyval_inner)
        grad_expand_keyval = across_fine(plain(normed_rows, shrink_keyval), grad_keyval)
        first_back = jax.vjp(
            lambda value: layer_norm(value, frozen_vectors[0], frozen_vectors[1]), hidden
        )[1]
        grad_hidden = grad_middle + first_back(grad_rows_in)[0]
        return (
            grad_hidden,
            (
                grad_shrink_query,
                grad_expand_query,
                grad_shrink_keyval,
                grad_expand_keyval,
                grad_shrink_output,
                grad_expand_output,
                grad_shrink_upward,
                grad_expand_upward,
                grad_shrink_downward,
                grad_expand_downward,
            ),
        )

    def forward_step(received, step_index):
        slot_index = jnp.clip(step_index - section_rank, 0, micro_count - 1)
        allowed, chosen, onehot = context(slot_index)
        fresh_input = lax.dynamic_index_in_dim(block_input, slot_index, 0, keepdims=False).astype(
            jnp.float32
        )
        hidden = jnp.where(section_rank == 0, fresh_input, received.astype(jnp.float32))
        result, kept_values = forward(hidden, fetch_frozen(), allowed, chosen)
        sent_rows = result.astype(jnp.bfloat16)
        return (passed_along(sent_rows, "section", 1), (sent_rows, kept_values))

    empty_rows = jnp.zeros((tok_rows, model_width), jnp.bfloat16)
    last_received, (outputs_all, kept_all) = lax.scan(
        forward_step, empty_rows, jnp.arange(micro_count + 1)
    )

    def backward_step(carried, step_index):
        received, grad_totals = carried
        forward_index = step_index - 1 + section_rank
        slot_index = jnp.clip(forward_index, 0, micro_count - 1)
        valid_weight = ((forward_index >= 0) & (forward_index < micro_count)).astype(jnp.float32)
        allowed, chosen, onehot = context(slot_index)
        kept_values = jax.tree.map(
            lambda stacked: lax.dynamic_index_in_dim(
                stacked, slot_index + section_rank, 0, keepdims=False
            ),
            kept_all,
        )
        given_grad = lax.dynamic_index_in_dim(cotangent, slot_index, 0, keepdims=False).astype(
            jnp.float32
        )
        grad_out = jnp.where(section_rank == 1, given_grad, received)
        grad_hidden, fresh_grads = backward(kept_values, grad_out, fetch_frozen(), allowed, chosen)
        bank_weight = onehot * valid_weight
        grad_totals = tuple(
            (
                running_total
                + bank_weight.reshape((-1,) + (1,) * fresh_grad.ndim) * fresh_grad[None]
                for running_total, fresh_grad in zip(grad_totals, fresh_grads)
            )
        )
        sent_grad = passed_along(as_sent(grad_hidden), "section", -1).astype(grad_hidden.dtype)
        return ((sent_grad, grad_totals), grad_hidden)

    empty_grads = jnp.zeros((tok_rows, model_width), jnp.float32)
    zero_totals = tuple((jnp.zeros(table.shape, jnp.float32) for table in tables))
    (last_grad, grad_totals), hidden_grads = lax.scan(
        backward_step, (empty_grads, zero_totals), jnp.arange(micro_count + 1)
    )
    summed_all = lax.psum(
        (
            grad_totals[0],
            grad_totals[2],
            grad_totals[3],
            grad_totals[5],
            grad_totals[6],
            grad_totals[9],
        ),
        ("dp", "tensor"),
    )
    summed_data = (
        lax.psum(grad_totals[1].astype(jnp.bfloat16), "dp").astype(jnp.float32),
        lax.psum(grad_totals[4].astype(jnp.bfloat16), "dp").astype(jnp.float32),
        lax.psum(grad_totals[7].astype(jnp.bfloat16), "dp").astype(jnp.float32),
        lax.psum(grad_totals[8].astype(jnp.bfloat16), "dp").astype(jnp.float32),
    )
    section_outputs = lax.dynamic_slice_in_dim(outputs_all, section_rank, micro_count, 0)[None]
    input_grads = lax.dynamic_slice_in_dim(hidden_grads, 1 - section_rank, micro_count, 0)[None]
    return (
        section_outputs,
        input_grads,
        summed_all[0][None],
        summed_data[0][None],
        summed_all[1][None],
        summed_all[2][None],
        summed_data[1][None],
        summed_all[3][None],
        summed_all[4][None],
        summed_data[2][None],
        summed_data[3][None],
        summed_all[5][None],
    )


def solution(mesh):
    return jax.shard_map(
        per_device,
        mesh=mesh,
        in_specs=(
            P(None, ("dp", "tensor"), None),
            P(None, ("dp", "tensor"), None),
            P(),
            P(),
            P("section", None),
            P("section", None),
            P("section", "dp", "tensor"),
            P("section", "tensor"),
            P("section", "dp", None),
            P("section", None),
            P("section", "tensor", "dp"),
            P("section", None),
            P("section", None),
            P("section", None),
            P("section", "dp", "tensor"),
            P("section", "tensor"),
            P("section", "tensor", "dp"),
            P("section", None),
            P("section", None, None, None),
            P("section", None, None, "tensor"),
            P("section", None, None, None),
            P("section", None, None, None),
            P("section", None, "tensor", None),
            P("section", None, None, None),
            P("section", None, None, None),
            P("section", None, None, "tensor"),
            P("section", None, "tensor", None),
            P("section", None, None, None),
        ),
        out_specs=(
            P("section", None, ("dp", "tensor"), None),
            P("section", None, ("dp", "tensor"), None),
            P("section", None, None, None),
            P("section", None, None, "tensor"),
            P("section", None, None, None),
            P("section", None, None, None),
            P("section", None, "tensor", None),
            P("section", None, None, None),
            P("section", None, None, None),
            P("section", None, None, "tensor"),
            P("section", None, "tensor", None),
            P("section", None, None, None),
        ),
        check_vma=False,
    )
```

profile of v0, /device:TPU:0, one launch (start us, length us, event | category | flops | bytes accessed | tf_op | source)
XLA Modules:
  0.0 2960.0 jit_solution(8710921705137282957)
XLA Ops:
  17.4 1067.4 %while.78 = (s32[]{:T(128)}, bf16[64,2048]{1,0:T(8,128)(2,1)S(1)}, bf16[3,64,2048]{2,1,0:T(8,128)(2,1)}, f32[3,64,2048]{2,1,0:T(8,128)}, bf16[3,256,2048]{2,1,0:...) while((s32[]{:T(128)}, bf16[64,2048]{1,0:T(8,128)(2,1)S(1)}, ...), condition=%wide.region_12.13_spmd.clone, body=%wide.region_0.12_spmd.clone.sunk | while | flops 6745518592 | bytes 195845680 | solution.py:443
  28.7 18.2 all-gather.15.cloned.1.call-done
  50.8 30.7 %all-gather.19.cloned.1.call-done = bf16[2048,256]{1,0:T(8,128)(2,1)} async-done(((bf16[128,256]{1,0:T(8,128)(2,1)}), bf16[2048,256]{1,0:T(8,128)(2,1)}) %all-gather.19.cloned.1.call-update) | async-done | bytes 1048592 | tf_op jit(solution)/shard_map/while/body/eval_jaxpr/all_gather | solution.py:178
  129.8 27.5 all-gather.21.cloned.1.call-done
  162.5 23.7 reduce-scatter.10.cloned.1.call-done
  191.1 22.3 all-gather.23.cloned.1.call-done
  215.6 52.1 %all-gather.25.cloned.1.call-done = bf16[2048,2048]{1,0:T(8,128)(2,1)} async-done(((bf16[128,2048]{1,0:T(8,128)(2,1)}), bf16[2048,2048]{1,0:T(8,128)(2,1)}) %all-gather.25.cloned.1.call-update) | async-done | bytes 8388624 | tf_op jit(solution)/shard_map/while/body/eval_jaxpr/all_gather | solution.py:179
  279.8 51.1 %all-gather.27.cloned.1.call-done = bf16[2048,2048]{1,0:T(8,128)(2,1)} async-done(((bf16[2048,128]{1,0:T(8,128)(2,1)}), bf16[2048,2048]{1,0:T(8,128)(2,1)}) %all-gather.27.cloned.1.call-update) | async-done | bytes 8388624 | tf_op jit(solution)/shard_map/while/body/eval_jaxpr/all_gather | solution.py:181
  345.5 17.9 reduce-scatter.12.cloned.1.call-done
  385.7 16.0 all-gather.15.cloned.1.call-done
  405.6 30.7 %all-gather.19.cloned.1.call-done = bf16[2048,256]{1,0:T(8,128)(2,1)} async-done(((bf16[128,256]{1,0:T(8,128)(2,1)}), bf16[2048,256]{1,0:T(8,128)(2,1)}) %all-gather.19.cloned.1.call-update) | async-done | bytes 1048592 | tf_op jit(solution)/shard_map/while/body/eval_jaxpr/all_gather | solution.py:178
  484.3 27.8 all-gather.21.cloned.1.call-done
  517.3 23.7 reduce-scatter.10.cloned.1.call-done
  545.6 22.6 all-gather.23.cloned.1.call-done
  570.5 52.0 %all-gather.25.cloned.1.call-done = bf16[2048,2048]{1,0:T(8,128)(2,1)} async-done(((bf16[128,2048]{1,0:T(8,128)(2,1)}), bf16[2048,2048]{1,0:T(8,128)(2,1)}) %all-gather.25.cloned.1.call-update) | async-done | bytes 8388624 | tf_op jit(solution)/shard_map/while/body/eval_jaxpr/all_gather | solution.py:179
  634.5 51.2 %all-gather.27.cloned.1.call-done = bf16[2048,2048]{1,0:T(8,128)(2,1)} async-done(((bf16[2048,128]{1,0:T(8,128)(2,1)}), bf16[2048,2048]{1,0:T(8,128)(2,1)}) %all-gather.27.cloned.1.call-update) | async-done | bytes 8388624 | tf_op jit(solution)/shard_map/while/body/eval_jaxpr/all_gather | solution.py:181
  700.2 17.7 reduce-scatter.12.cloned.1.call-done
  740.1 16.4 all-gather.15.cloned.1.call-done
  760.4 30.5 %all-gather.19.cloned.1.call-done = bf16[2048,256]{1,0:T(8,128)(2,1)} async-done(((bf16[128,256]{1,0:T(8,128)(2,1)}), bf16[2048,256]{1,0:T(8,128)(2,1)}) %all-gather.19.cloned.1.call-update) | async-done | bytes 1048592 | tf_op jit(solution)/shard_map/while/body/eval_jaxpr/all_gather | solution.py:178
  812.1 15.9 all-gather.17.cloned.1.call-done
  839.2 27.6 all-gather.21.cloned.1.call-done
  872.1 23.7 reduce-scatter.10.cloned.1.call-done
  900.5 22.5 all-gather.23.cloned.1.call-done
  925.3 52.1 %all-gather.25.cloned.1.call-done = bf16[2048,2048]{1,0:T(8,128)(2,1)} async-done(((bf16[128,2048]{1,0:T(8,128)(2,1)}), bf16[2048,2048]{1,0:T(8,128)(2,1)}) %all-gather.25.cloned.1.call-update) | async-done | bytes 8388624 | tf_op jit(solution)/shard_map/while/body/eval_jaxpr/all_gather | solution.py:179
  989.5 51.6 %all-gather.27.cloned.1.call-done = bf16[2048,2048]{1,0:T(8,128)(2,1)} async-done(((bf16[2048,128]{1,0:T(8,128)(2,1)}), bf16[2048,2048]{1,0:T(8,128)(2,1)}) %all-gather.27.cloned.1.call-update) | async-done | bytes 8388624 | tf_op jit(solution)/shard_map/while/body/eval_jaxpr/all_gather | solution.py:181
  1055.6 18.0 reduce-scatter.12.cloned.1.call-done
  1086.6 1162.8 %while.79 = (s32[]{:T(128)}, f32[64,2048]{1,0:T(8,128)}, f32[8,2048,16]{1,2,0:T(8,128)}, f32[8,16,512]{2,1,0:T(8,128)}, f32[8,2048,16]{1,2,0:T(8,128)}, /*index=...) while((s32[]{:T(128)}, f32[64,2048]{1,0:T(8,128)}, ...), condition=%wide.region_29.30_spmd.clone, body=%wide.region_13.29_spmd.clone.sunk | while | flops 8590163968 | bytes 310082304 | solution.py:477
  1116.1 20.6 all-gather.29.cloned.1.call-done
  1138.3 61.0 %all-gather.31.cloned.1.call-done = bf16[2048,2048]{1,0:T(8,128)(2,1)} async-done(((bf16[2048,128]{1,0:T(8,128)(2,1)}), bf16[2048,2048]{1,0:T(8,128)(2,1)}) %all-gather.31.cloned.1.call-update) | async-done | bytes 8388624 | tf_op jit(solution)/shard_map/while/body/eval_jaxpr/all_gather | solution.py:181
  1210.7 42.4 %all-gather.33.cloned.1.call-done = bf16[2048,2048]{1,0:T(8,128)(2,1)} async-done(((bf16[128,2048]{1,0:T(8,128)(2,1)}), bf16[2048,2048]{1,0:T(8,128)(2,1)}) %all-gather.33.cloned.1.call-update) | async-done | bytes 8388624 | tf_op jit(solution)/shard_map/while/body/eval_jaxpr/all_gather | solution.py:179
  1262.1 24.3 reduce-scatter.14.cloned.1.call-done
  1317.5 36.5 %all-gather.37.cloned.1.call-done = bf16[512,2048]{1,0:T(8,128)(2,1)} async-done(((bf16[512,128]{1,0:T(8,128)(2,1)}), bf16[512,2048]{1,0:T(8,128)(2,1)}) %all-gather.37.cloned.1.call-update) | async-done | bytes 2097168 | tf_op jit(solution)/shard_map/while/body/eval_jaxpr/all_gather | solution.py:180
  1434.0 16.5 all-gather.39.cloned.1.call-done
  1450.5 26.3 reduce-scatter.18.cloned.1.call-done
  1497.7 18.5 all-gather.29.cloned.1.call-done
  1517.8 60.9 %all-gather.31.cloned.1.call-done = bf16[2048,2048]{1,0:T(8,128)(2,1)} async-done(((bf16[2048,128]{1,0:T(8,128)(2,1)}), bf16[2048,2048]{1,0:T(8,128)(2,1)}) %all-gather.31.cloned.1.call-update) | async-done | bytes 8388624 | tf_op jit(solution)/shard_map/while/body/eval_jaxpr/all_gather | solution.py:181
  1590.1 42.5 %all-gather.33.cloned.1.call-done = bf16[2048,2048]{1,0:T(8,128)(2,1)} async-done(((bf16[128,2048]{1,0:T(8,128)(2,1)}), bf16[2048,2048]{1,0:T(8,128)(2,1)}) %all-gather.33.cloned.1.call-update) | async-done | bytes 8388624 | tf_op jit(solution)/shard_map/while/body/eval_jaxpr/all_gather | solution.py:179
  1641.6 24.3 reduce-scatter.14.cloned.1.call-done
  1696.9 36.6 %all-gather.37.cloned.1.call-done = bf16[512,2048]{1,0:T(8,128)(2,1)} async-done(((bf16[512,128]{1,0:T(8,128)(2,1)}), bf16[512,2048]{1,0:T(8,128)(2,1)}) %all-gather.37.cloned.1.call-update) | async-done | bytes 2097168 | tf_op jit(solution)/shard_map/while/body/eval_jaxpr/all_gather | solution.py:180
  1830.0 26.3 reduce-scatter.18.cloned.1.call-done
  1877.3 18.5 all-gather.29.cloned.1.call-done
  1897.4 60.9 %all-gather.31.cloned.1.call-done = bf16[2048,2048]{1,0:T(8,128)(2,1)} async-done(((bf16[2048,128]{1,0:T(8,128)(2,1)}), bf16[2048,2048]{1,0:T(8,128)(2,1)}) %all-gather.31.cloned.1.call-update) | async-done | bytes 8388624 | tf_op jit(solution)/shard_map/while/body/eval_jaxpr/all_gather | solution.py:181
  1969.6 42.5 %all-gather.33.cloned.1.call-done = bf16[2048,2048]{1,0:T(8,128)(2,1)} async-done(((bf16[128,2048]{1,0:T(8,128)(2,1)}), bf16[2048,2048]{1,0:T(8,128)(2,1)}) %all-gather.33.cloned.1.call-update) | async-done | bytes 8388624 | tf_op jit(solution)/shard_map/while/body/eval_jaxpr/all_gather | solution.py:179
  2021.2 24.3 reduce-scatter.14.cloned.1.call-done
  2076.5 36.6 %all-gather.37.cloned.1.call-done = bf16[512,2048]{1,0:T(8,128)(2,1)} async-done(((bf16[512,128]{1,0:T(8,128)(2,1)}), bf16[512,2048]{1,0:T(8,128)(2,1)}) %all-gather.37.cloned.1.call-update) | async-done | bytes 2097168 | tf_op jit(solution)/shard_map/while/body/eval_jaxpr/all_gather | solution.py:180
  2209.7 26.5 reduce-scatter.18.cloned.1.call-done
  2258.9 115.9 %all-reduce.8.cloned.1.call-done = (bf16[1,8,16,512]{3,2,1,0:T(8,128)(2,1)}, bf16[1,8,512,16]{2,3,1,0:T(8,128)(2,1)}, bf16[1,8,16,2048]{3,2,1,0:T(8,128)(2,1)}, bf16[1,8,2048,16]{2,3,1,0:T(8,128)(2,1)}) async-done(((bf16[1,8,16,512]{3,2,1,0:T(8,128)(2,1)}, bf16[1,8,512,16]{2,3,1,0:T(8,128)(2,1)}, bf16[1,8,16,2048]{3,2,1,0:T(8,128)(2,1)}, bf16[1,8,2048,16]{2,3,1,0:T(8,128)(2,1)}), ...) | async-done | bytes 1310736 | tf_op jit(solution)/shard_map/psum | solution.py:492
  2381.3 564.2 %all-reduce.6.cloned.1.call-done = (f32[1,8,2048,16]{2,3,1,0:T(8,128)}, f32[1,8,2048,16]{2,3,1,0:T(8,128)}, f32[1,8,16,256]{3,2,1,0:T(8,128)}, f32[1,8,16,2048]{...) async-done(((f32[1,8,2048,16]{2,3,1,0:T(8,128)}, f32[1,8,2048,16]{2,3,1,0:T(8,128)}, f32[1,8,16,256]{3,2,1,0:T(8,128)}, ...) | async-done | bytes 5373968 | tf_op jit(solution)/shard_map/psum | solution.py:480
  (889 shorter events, 834.6 us)
Async XLA Ops:
  19.9 61.5 %all-gather.19.cloned.1.call-start = ((), (), s32[]{:S(2)}) async-start(), calls=%async_computation.9 | async-start | bytes 1114112 | tf_op jit(solution)/shard_map/while/body/eval_jaxpr/all_gather | solution.py:178
  20.7 97.8 %all-gather.17.cloned.1.call-start = ((), (), s32[]{:S(2)}) async-start(), calls=%async_computation.8 | async-start | bytes 2228224 | tf_op jit(solution)/shard_map/while/body/eval_jaxpr/all_gather | solution.py:177
  21.4 135.8 %all-gather.21.cloned.1.call-start = ((), (), s32[]{:S(2)}) async-start(), calls=%async_computation.10 | async-start | bytes 2228224 | tf_op jit(solution)/shard_map/while/body/eval_jaxpr/all_gather | solution.py:180
  22.0 164.2 %reduce-scatter.10.cloned.1.call-start = ((), (), s32[]{:S(2)}) async-start(), calls=%async_computation.11 | async-start | bytes 1310720 | tf_op jit(solution)/shard_map/while/body/eval_jaxpr/reduce_scatter | solution.py:188
  189.6 78.2 %all-gather.25.cloned.1.call-start = ((), (), s32[]{:S(2)}) async-start(), calls=%async_computation.13 | async-start | bytes 8912896 | tf_op jit(solution)/shard_map/while/body/eval_jaxpr/all_gather | solution.py:179
  190.3 140.6 %all-gather.27.cloned.1.call-start = ((), (), s32[]{:S(2)}) async-start(), calls=%async_computation.14 | async-start | bytes 8912896 | tf_op jit(solution)/shard_map/while/body/eval_jaxpr/all_gather | solution.py:181
  191.1 172.2 %reduce-scatter.12.cloned.1.call-start = ((), (), s32[]{:S(2)}) async-start(), calls=%async_computation.15 | async-start | bytes 1310720 | tf_op jit(solution)/shard_map/while/body/eval_jaxpr/reduce_scatter | solution.py:188
  376.9 59.4 %all-gather.19.cloned.1.call-start = ((), (), s32[]{:S(2)}) async-start(), calls=%async_computation.9 | async-start | bytes 1114112 | tf_op jit(solution)/shard_map/while/body/eval_jaxpr/all_gather | solution.py:178
  377.7 95.4 %all-gather.17.cloned.1.call-start = ((), (), s32[]{:S(2)}) async-start(), calls=%async_computation.8 | async-start | bytes 2228224 | tf_op jit(solution)/shard_map/while/body/eval_jaxpr/all_gather | solution.py:177
  378.2 133.8 %all-gather.21.cloned.1.call-start = ((), (), s32[]{:S(2)}) async-start(), calls=%async_computation.10 | async-start | bytes 2228224 | tf_op jit(solution)/shard_map/while/body/eval_jaxpr/all_gather | solution.py:180
  379.0 162.0 %reduce-scatter.10.cloned.1.call-start = ((), (), s32[]{:S(2)}) async-start(), calls=%async_computation.11 | async-start | bytes 1310720 | tf_op jit(solution)/shard_map/while/body/eval_jaxpr/reduce_scatter | solution.py:188
  544.4 78.1 %all-gather.25.cloned.1.call-start = ((), (), s32[]{:S(2)}) async-start(), calls=%async_computation.13 | async-start | bytes 8912896 | tf_op jit(solution)/shard_map/while/body/eval_jaxpr/all_gather | solution.py:179
  545.0 140.7 %all-gather.27.cloned.1.call-start = ((), (), s32[]{:S(2)}) async-start(), calls=%async_computation.14 | async-start | bytes 8912896 | tf_op jit(solution)/shard_map/while/body/eval_jaxpr/all_gather | solution.py:181
  545.6 172.3 %reduce-scatter.12.cloned.1.call-start = ((), (), s32[]{:S(2)}) async-start(), calls=%async_computation.15 | async-start | bytes 1310720 | tf_op jit(solution)/shard_map/while/body/eval_jaxpr/reduce_scatter | solution.py:188
  731.4 59.6 %all-gather.19.cloned.1.call-start = ((), (), s32[]{:S(2)}) async-start(), calls=%async_computation.9 | async-start | bytes 1114112 | tf_op jit(solution)/shard_map/while/body/eval_jaxpr/all_gather | solution.py:178
  732.0 96.0 %all-gather.17.cloned.1.call-start = ((), (), s32[]{:S(2)}) async-start(), calls=%async_computation.8 | async-start | bytes 2228224 | tf_op jit(solution)/shard_map/while/body/eval_jaxpr/all_gather | solution.py:177
  732.7 134.2 %all-gather.21.cloned.1.call-start = ((), (), s32[]{:S(2)}) async-start(), calls=%async_computation.10 | async-start | bytes 2228224 | tf_op jit(solution)/shard_map/while/body/eval_jaxpr/all_gather | solution.py:180
  733.4 162.4 %reduce-scatter.10.cloned.1.call-start = ((), (), s32[]{:S(2)}) async-start(), calls=%async_computation.11 | async-start | bytes 1310720 | tf_op jit(solution)/shard_map/while/body/eval_jaxpr/reduce_scatter | solution.py:188
  899.2 78.2 %all-gather.25.cloned.1.call-start = ((), (), s32[]{:S(2)}) async-start(), calls=%async_computation.13 | async-start | bytes 8912896 | tf_op jit(solution)/shard_map/while/body/eval_jaxpr/all_gather | solution.py:179
  899.9 141.2 %all-gather.27.cloned.1.call-start = ((), (), s32[]{:S(2)}) async-start(), calls=%async_computation.14 | async-start | bytes 8912896 | tf_op jit(solution)/shard_map/while/body/eval_jaxpr/all_gather | solution.py:181
  900.5 173.1 %reduce-scatter.12.cloned.1.call-start = ((), (), s32[]{:S(2)}) async-start(), calls=%async_computation.15 | async-start | bytes 1310720 | tf_op jit(solution)/shard_map/while/body/eval_jaxpr/reduce_scatter | solution.py:188
  1112.2 87.1 %all-gather.31.cloned.1.call-start = ((), (), s32[]{:S(2)}) async-start(), calls=%async_computation.17 | async-start | bytes 8912896 | tf_op jit(solution)/shard_map/while/body/eval_jaxpr/all_gather | solution.py:181
  1113.0 140.1 %all-gather.33.cloned.1.call-start = ((), (), s32[]{:S(2)}) async-start(), calls=%async_computation.18 | async-start | bytes 8912896 | tf_op jit(solution)/shard_map/while/body/eval_jaxpr/all_gather | solution.py:179
  1113.6 172.8 %reduce-scatter.14.cloned.1.call-start = ((), (), s32[]{:S(2)}) async-start(), calls=%async_computation.19 | async-start | bytes 1310720 | tf_op jit(solution)/shard_map/while/body/eval_jaxpr/reduce_scatter | solution.py:188
  1261.9 52.9 %all-gather.35.cloned.1.call-start = ((), (), s32[]{:S(2)}) async-start(), calls=%async_computation.20 | async-start | bytes 1310720 | tf_op jit(solution)/shard_map/while/body/eval_jaxpr/all_gather | solution.py:185
  1290.8 63.1 %all-gather.37.cloned.1.call-start = ((), (), s32[]{:S(2)}) async-start(), calls=%async_computation.21 | async-start | bytes 2228224 | tf_op jit(solution)/shard_map/while/body/eval_jaxpr/all_gather | solution.py:180
  1291.4 120.2 %all-gather.41.cloned.1.call-start = ((), (), s32[]{:S(2)}) async-start(), calls=%async_computation.24 | async-start | bytes 2228224 | tf_op jit(solution)/shard_map/while/body/eval_jaxpr/all_gather | solution.py:177
  1292.2 133.5 %reduce-scatter.16.cloned.1.call-start = ((), (), s32[]{:S(2)}) async-start(), calls=%async_computation.22 | async-start | bytes 163840 | tf_op jit(solution)/shard_map/while
  1391.4 59.0 %all-gather.39.cloned.1.call-start = ((), (), s32[]{:S(2)}) async-start(), calls=%async_computation.23 | async-start | bytes 1114112 | tf_op jit(solution)/shard_map/while/body/eval_jaxpr/all_gather | solution.py:178
  1392.0 84.7 %reduce-scatter.18.cloned.1.call-start = ((), (), s32[]{:S(2)}) async-start(), calls=%async_computation.25 | async-start | bytes 1310720 | tf_op jit(solution)/shard_map/while/body/eval_jaxpr/reduce_scatter | solution.py:394
  1493.9 84.8 %all-gather.31.cloned.1.call-start = ((), (), s32[]{:S(2)}) async-start(), calls=%async_computation.17 | async-start | bytes 8912896 | tf_op jit(solution)/shard_map/while/body/eval_jaxpr/all_gather | solution.py:181
  1494.5 138.2 %all-gather.33.cloned.1.call-start = ((), (), s32[]{:S(2)}) async-start(), calls=%async_computation.18 | async-start | bytes 8912896 | tf_op jit(solution)/shard_map/while/body/eval_jaxpr/all_gather | solution.py:179
  1495.2 170.7 %reduce-scatter.14.cloned.1.call-start = ((), (), s32[]{:S(2)}) async-start(), calls=%async_computation.19 | async-start | bytes 1310720 | tf_op jit(solution)/shard_map/while/body/eval_jaxpr/reduce_scatter | solution.py:188
  1670.4 63.2 %all-gather.37.cloned.1.call-start = ((), (), s32[]{:S(2)}) async-start(), calls=%async_computation.21 | async-start | bytes 2228224 | tf_op jit(solution)/shard_map/while/body/eval_jaxpr/all_gather | solution.py:180
  1671.0 120.2 %all-gather.41.cloned.1.call-start = ((), (), s32[]{:S(2)}) async-start(), calls=%async_computation.24 | async-start | bytes 2228224 | tf_op jit(solution)/shard_map/while/body/eval_jaxpr/all_gather | solution.py:177
  1671.7 135.0 %reduce-scatter.16.cloned.1.call-start = ((), (), s32[]{:S(2)}) async-start(), calls=%async_computation.22 | async-start | bytes 163840 | tf_op jit(solution)/shard_map/while
  1771.0 59.0 %all-gather.39.cloned.1.call-start = ((), (), s32[]{:S(2)}) async-start(), calls=%async_computation.23 | async-start | bytes 1114112 | tf_op jit(solution)/shard_map/while/body/eval_jaxpr/all_gather | solution.py:178
  1771.6 84.8 %reduce-scatter.18.cloned.1.call-start = ((), (), s32[]{:S(2)}) async-start(), calls=%async_computation.25 | async-start | bytes 1310720 | tf_op jit(solution)/shard_map/while/body/eval_jaxpr/reduce_scatter | solution.py:394
  1873.4 84.8 %all-gather.31.cloned.1.call-start = ((), (), s32[]{:S(2)}) async-start(), calls=%async_computation.17 | async-start | bytes 8912896 | tf_op jit(solution)/shard_map/while/body/eval_jaxpr/all_gather | solution.py:181
  1874.0 138.2 %all-gather.33.cloned.1.call-start = ((), (), s32[]{:S(2)}) async-start(), calls=%async_computation.18 | async-start | bytes 8912896 | tf_op jit(solution)/shard_map/while/body/eval_jaxpr/all_gather | solution.py:179
  1874.8 170.7 %reduce-scatter.14.cloned.1.call-start = ((), (), s32[]{:S(2)}) async-start(), calls=%async_computation.19 | async-start | bytes 1310720 | tf_op jit(solution)/shard_map/while/body/eval_jaxpr/reduce_scatter | solution.py:188
  2049.9 63.1 %all-gather.37.cloned.1.call-start = ((), (), s32[]{:S(2)}) async-start(), calls=%async_computation.21 | async-start | bytes 2228224 | tf_op jit(solution)/shard_map/while/body/eval_jaxpr/all_gather | solution.py:180
  2050.5 120.4 %all-gather.41.cloned.1.call-start = ((), (), s32[]{:S(2)}) async-start(), calls=%async_computation.24 | async-start | bytes 2228224 | tf_op jit(solution)/shard_map/while/body/eval_jaxpr/all_gather | solution.py:177
  2051.3 135.1 %reduce-scatter.16.cloned.1.call-start = ((), (), s32[]{:S(2)}) async-start(), calls=%async_computation.22 | async-start | bytes 163840 | tf_op jit(solution)/shard_map/while
  2150.5 59.2 %all-gather.39.cloned.1.call-start = ((), (), s32[]{:S(2)}) async-start(), calls=%async_computation.23 | async-start | bytes 1114112 | tf_op jit(solution)/shard_map/while/body/eval_jaxpr/all_gather | solution.py:178
  2151.3 84.9 %reduce-scatter.18.cloned.1.call-start = ((), (), s32[]{:S(2)}) async-start(), calls=%async_computation.25 | async-start | bytes 1310720 | tf_op jit(solution)/shard_map/while/body/eval_jaxpr/reduce_scatter | solution.py:394
  2249.5 125.3 %all-reduce.8.cloned.1.call-start = ((), (), s32[]{:S(2)}) async-start(), calls=%async_computation.6 | async-start | bytes 2621440 | tf_op jit(solution)/shard_map/psum | solution.py:492
  2255.8 689.7 %all-reduce.6.cloned.1.call-start = ((), (), s32[]{:S(2)}) async-start(), calls=%async_computation.5 | async-start | bytes 10747904 | tf_op jit(solution)/shard_map/psum | solution.py:480
  (154 other events, 2963.0 us)
Sparse Core Ops, SparseCore 0:
  20.4 26.3 all-gather.14
  48.6 32.8 all-gather.18
  83.2 35.2 all-gather.16
  120.0 37.2 all-gather.20
  162.6 23.5 reduce-scatter.9
  189.7 23.6 all-gather.22
  215.2 52.4 all-gather.24
  269.5 61.4 all-gather.26
  339.7 23.5 reduce-scatter.11
  377.1 24.5 all-gather.14
  403.4 32.8 all-gather.18
  437.9 35.1 all-gather.16
  474.7 37.3 all-gather.20
  517.4 23.5 reduce-scatter.9
  544.5 23.6 all-gather.22
  569.9 52.4 all-gather.24
  624.0 61.5 all-gather.26
  731.9 24.5 all-gather.14
  758.1 32.8 all-gather.18
  792.6 35.3 all-gather.16
  829.6 37.2 all-gather.20
  872.2 23.5 reduce-scatter.9
  899.3 23.7 all-gather.22
  924.9 52.4 all-gather.24
  979.0 62.0 all-gather.26
  1049.9 23.6 reduce-scatter.11
  1112.4 24.2 all-gather.28
  1138.3 60.9 all-gather.30
  1200.9 52.1 all-gather.32
  1262.0 24.3 reduce-scatter.13
  1291.0 23.7 all-gather.34
  1316.3 37.6 all-gather.36
  1355.8 35.0 all-gather.40
  1418.2 32.2 all-gather.38
  1517.7 60.9 all-gather.30
  1580.4 52.1 all-gather.32
  1641.5 24.3 reduce-scatter.13
  1670.5 23.6 all-gather.34
  1695.7 37.7 all-gather.36
  1735.4 35.0 all-gather.40
  1797.7 32.2 all-gather.38
  1897.3 60.9 all-gather.30
  1959.9 52.1 all-gather.32
  2021.1 24.3 reduce-scatter.13
  2050.1 23.6 all-gather.34
  2075.3 37.7 all-gather.36
  2114.9 35.0 all-gather.40
  2177.3 32.3 all-gather.38
  (9 shorter events, 207.3 us)
Sparse Core Ops, SparseCore 1:
  2255.9 118.8 all-reduce.7
  2378.8 566.7 all-reduce.5
where the time goes:
time: 2980 us; the launch traced here: 2960 us
  waiting for transfers between devices  2210 us (74%)
  matrix products  355 us (12%)
  local copies, waits for them, and re-layouts  159 us (5%)
  other arithmetic  115 us (4%)
  starting transfers between devices  68.8 us (2%)
  loops' own time  40.3 us (1%)
    psum x1, waiting for transfers between devices, per_device(): lax.psum((grad_totals[0], grad_totals[2], grad_totals[3], grad_totals[5],...  564 us
    all_gather x6, waiting for transfers between devices, fetch_frozen(): lax.all_gather(shards[4], 'dp', axis=1, tiled=True)  337 us
    all_gather x6, waiting for transfers between devices, fetch_frozen(): lax.all_gather(shards[2], 'dp', axis=0, tiled=True)  284 us
    reduce_scatter x9, waiting for transfers between devices, reduce_rows(): lax.psum_scatter(partial_rows.astype(jnp.bfloat16), 'tensor', scatter_dim...  197 us
    all_gather x6, waiting for transfers between devices, fetch_frozen(): lax.all_gather(shards[3], 'dp', axis=1, tiled=True)  193 us
    all_gather x12, waiting for transfers between devices, spread(): return lax.all_gather(rows, 'tensor', axis=0, tiled=True)  183 us
    all_gather x6, waiting for transfers between devices, fetch_frozen(): lax.all_gather(shards[1], 'dp', axis=0, tiled=True)  133 us
    psum x1, waiting for transfers between devices, per_device(): lax.psum(grad_totals[1].astype(jnp.bfloat16), 'dp').astype(jnp.float32)  116 us
  transfers between devices with their start and end apart: 89, of which 68 were waited for; matrix products, arithmetic and copies ran while one was open for 16% of the time, Pallas kernels for 0%

commit v1 on v0

v1 whole, which is shorter than its diff:
```python
import math

import jax
import jax.numpy as jnp
from jax import lax
from jax.experimental import pallas as pl
from jax.experimental.pallas import tpu as pltpu
from jax.sharding import PartitionSpec as P

WINDOW = 1024
epsilon = 1e-05
masked_score = -1e30
bf16 = jnp.bfloat16
f32 = jnp.float32


def plain(left, right):
    return jnp.dot(left, right, preferred_element_type=f32)


def against(left, right):
    return lax.dot_general(left, right, (((1,), (1,)), ((), ())), preferred_element_type=f32)


def across(left, right):
    return lax.dot_general(left, right, (((0,), (0,)), ((), ())), preferred_element_type=f32)


def around(block, axis, distance):
    size = lax.axis_size(axis)
    return lax.ppermute(block, axis, [(i, (i + distance) % size) for i in range(size)])


def along(block, axis, distance):
    size = lax.axis_size(axis)
    route = [(i, i + distance) for i in range(size) if 0 <= i + distance < size]
    return lax.ppermute(block, axis, route)


def flipped(block, axis, bit):
    size = lax.axis_size(axis)
    return lax.ppermute(block, axis, [(i, i ^ bit) for i in range(size)])


def pick(table, index, size=1):
    return lax.dynamic_slice_in_dim(table, index, size, 0)


def norm_parts(value):
    centred = value - jnp.mean(value, axis=-1, keepdims=True)
    spread = lax.rsqrt(jnp.mean(centred * centred, axis=-1, keepdims=True) + epsilon)
    return centred * spread, spread


def norm_back(unit, spread, scaled):
    inner = jnp.mean(scaled * unit, axis=-1, keepdims=True)
    return spread * (scaled - jnp.mean(scaled, axis=-1, keepdims=True) - unit * inner)


def gelu_parts(value):
    rate = math.sqrt(2.0 / math.pi)
    square = value * value
    bend = jnp.tanh(rate * (value + 0.044715 * value * square))
    rising = 0.5 * (1.0 + bend)
    slope = rising + 0.5 * value * (1.0 - bend * bend) * (rate * (1.0 + 3 * 0.044715 * square))
    return value * rising, slope


def attend_kernel(scale, query_ref, keyval_ref, bias_ref, prob_ref, mixed_ref):
    head = query_ref.shape[1]
    scores = against(query_ref[...], keyval_ref[:, :head]) * scale + bias_ref[...].astype(f32)
    top = jnp.max(scores, axis=-1, keepdims=True)
    lifted = jnp.exp(scores - top)
    total = jnp.sum(lifted, axis=-1, keepdims=True)
    probs = (lifted * (1.0 / total)).astype(bf16)
    prob_ref[0] = probs
    mixed_ref[...] = plain(probs, keyval_ref[:, head:]).astype(bf16)


def attend(queries, key_block, bias, head):
    rows, width = queries.shape
    keys = key_block.shape[0]
    heads = width // head
    whole = lambda shape: pl.BlockSpec(shape, lambda h: (0, 0))
    column = pl.BlockSpec((rows, head), lambda h: (0, h))
    return pl.pallas_call(
        lambda *refs: attend_kernel(1.0 / math.sqrt(head), *refs),
        grid=(heads,),
        in_specs=[column, whole((keys, 2 * head)), whole((rows, keys))],
        out_specs=[pl.BlockSpec((1, rows, keys), lambda h: (h, 0, 0)), column],
        out_shape=[
            jax.ShapeDtypeStruct((heads, rows, keys), bf16),
            jax.ShapeDtypeStruct((rows, width), bf16),
        ],
        compiler_params=pltpu.CompilerParams(vmem_limit_bytes=40 * 2**20),
        name="attend",
    )(queries, key_block, bias)


def attend_back_kernel(
    scale, grad_ref, prob_ref, query_ref, mixed_ref, keyval_ref, dq_ref, dkv_ref, key_sum, value_sum
):
    step = pl.program_id(0)
    head = query_ref.shape[1]
    grad = grad_ref[...]
    probs = prob_ref[0]
    delta = jnp.sum(grad.astype(f32) * mixed_ref[...].astype(f32), axis=-1, keepdims=True)
    grad_probs = against(grad, keyval_ref[:, head:])
    grad_scores = (probs.astype(f32) * (grad_probs - delta)).astype(bf16)
    dq_ref[...] = (plain(grad_scores, keyval_ref[:, :head]) * scale).astype(bf16)
    keys = across(grad_scores, query_ref[...])
    values = across(probs, grad)

    @pl.when(step == 0)
    def _():
        key_sum[...] = keys
        value_sum[...] = values

    @pl.when(step > 0)
    def _():
        key_sum[...] += keys
        value_sum[...] += values

    @pl.when(step == pl.num_programs(0) - 1)
    def _():
        dkv_ref[:, :head] = (key_sum[...] * scale).astype(bf16)
        dkv_ref[:, head:] = value_sum[...].astype(bf16)


def attend_back(grad_mixed, probs, queries, mixed, key_block, head):
    rows, width = queries.shape
    keys = key_block.shape[0]
    heads = width // head
    column = pl.BlockSpec((rows, head), lambda h: (0, h))
    whole = pl.BlockSpec((keys, 2 * head), lambda h: (0, 0))
    return pl.pallas_call(
        lambda *refs: attend_back_kernel(1.0 / math.sqrt(head), *refs),
        grid=(heads,),
        in_specs=[
            column,
            pl.BlockSpec((1, rows, keys), lambda h: (h, 0, 0)),
            column,
            column,
            whole,
        ],
        out_specs=[column, whole],
        out_shape=[
            jax.ShapeDtypeStruct((rows, width), bf16),
            jax.ShapeDtypeStruct((keys, 2 * head), bf16),
        ],
        scratch_shapes=[pltpu.VMEM((keys, head), f32), pltpu.VMEM((keys, head), f32)],
        compiler_params=pltpu.CompilerParams(vmem_limit_bytes=40 * 2**20),
        name="attend_back",
    )(grad_mixed, probs, queries, mixed, key_block)


def per_device(
    block_input,
    cotangent,
    doc_lengths,
    bank_choice,
    first_gain,
    first_shift,
    query_weight,
    query_bias,
    keyval_weight,
    value_bias,
    output_weight,
    output_bias,
    second_gain,
    second_shift,
    upward_weight,
    upward_bias,
    downward_weight,
    downward_bias,
    query_shrink,
    query_expand,
    keyval_shrink,
    keyval_expand,
    output_shrink,
    output_expand,
    upward_shrink,
    upward_expand,
    downward_shrink,
    downward_expand,
):
    section = lax.axis_index("section")
    data = lax.axis_index("dp")
    tensor = lax.axis_index("tensor")
    low_section = section == 0
    width = block_input.shape[2]
    rows = block_input.shape[1]
    ranks = lax.axis_size("tensor")
    span = rows * ranks
    head = value_bias.shape[1]
    local_q = query_bias.shape[1]
    local_f = upward_bias.shape[1]
    rank = query_expand.shape[2]
    banks = query_expand.shape[1]
    reach = WINDOW // span
    sides = [(0, 1), (1, 0)]

    def swap(value):
        return lax.ppermute(value, "section", sides)

    def by_layer(own, other):
        return jnp.where(low_section, own, other), jnp.where(low_section, other, own)

    def spread(block):
        parts = [block] + [around(block, "tensor", -j) for j in range(1, ranks)]
        return jnp.concatenate(parts, axis=0)

    def reduce_rows(partial):
        low = partial.astype(bf16)
        total = partial[:rows]
        for j in range(1, ranks):
            total = total + around(low[j * rows : (j + 1) * rows], "tensor", j).astype(f32)
        return total

    def chosen(table, bank, transpose):
        block = lax.dynamic_index_in_dim(table[0], bank, 0, keepdims=False)
        return block.T if transpose else block

    def early_pack(bank):
        return jnp.concatenate(
            [
                chosen(query_shrink, bank, True),
                chosen(keyval_shrink, bank, True),
                chosen(query_expand, bank, False),
                chosen(keyval_expand, bank, False),
            ],
            axis=1,
        )

    def late_pack(bank):
        return jnp.concatenate(
            [
                chosen(output_shrink, bank, True),
                chosen(output_expand, bank, False),
                chosen(upward_shrink, bank, True),
                chosen(upward_expand, bank, False),
                chosen(downward_shrink, bank, True),
                chosen(downward_expand, bank, False),
            ],
            axis=1,
        )

    own_bank = lax.dynamic_index_in_dim(bank_choice, section, 0, keepdims=False)
    other_bank = lax.dynamic_index_in_dim(bank_choice, 1 - section, 0, keepdims=False)

    vectors = jnp.concatenate(
        [
            first_gain,
            first_shift,
            query_bias,
            jnp.zeros_like(value_bias),
            value_bias,
            output_bias,
            second_gain,
            second_shift,
            upward_bias,
            downward_bias,
        ],
        axis=1,
    )
    vector_sizes = [width, width, local_q, 2 * head, width, width, width, local_f, width]

    shard_qkv = jnp.concatenate([query_weight[0], keyval_weight[0]], axis=1)
    shard_rest = jnp.concatenate(
        [output_weight[0].T, upward_weight[0], downward_weight[0].T], axis=1
    )
    qkv_layers = by_layer(shard_qkv, swap(shard_qkv))
    vector_layers = by_layer(vectors, swap(vectors))
    early_layers = by_layer(early_pack(own_bank), swap(early_pack(other_bank)))
    rest_layers = by_layer(shard_rest, swap(shard_rest))
    late_layers = by_layer(late_pack(own_bank), swap(late_pack(other_bank)))

    def gather(shard):
        return lax.all_gather(shard, "dp", axis=0, tiled=True)

    first = gather(qkv_layers[0])
    second_shard = jnp.concatenate(
        [rest_layers[0], qkv_layers[1], rest_layers[1][:, :local_q]], axis=1
    )
    first, second_shard = lax.optimization_barrier((first, second_shard))
    middle_all = gather(second_shard)
    third_shard = rest_layers[1][:, local_q:]
    middle_all, third_shard = lax.optimization_barrier((middle_all, third_shard))
    last_all = gather(third_shard)

    def split(table, sizes):
        cuts = [0]
        for size in sizes:
            cuts.append(cuts[-1] + size)
        return [table[:, a:b] for a, b in zip(cuts[:-1], cuts[1:])]

    wide = local_q + 2 * head
    out_zero, up_zero, down_zero, qkv_one, out_one = split(
        middle_all, [local_q, local_f, local_f, wide, local_q]
    )
    up_one, down_one = split(last_all, [local_f, local_f])
    weights = [
        (first, out_zero, up_zero, down_zero),
        (qkv_one, out_one, up_one, down_one),
    ]
    small = [
        [part.astype(f32) for part in split(vector_layers[layer], vector_sizes)]
        for layer in range(2)
    ]
    adapters = [
        split(early_layers[layer], [width, width, local_q, 2 * head])
        + split(late_layers[layer], [local_q, width, width, local_f, local_f, width])
        for layer in range(2)
    ]

    place = (
        ((tensor + jnp.arange(ranks, dtype=jnp.int32)) % ranks)[:, None] * rows
        + jnp.arange(rows, dtype=jnp.int32)[None, :]
    ).reshape(-1)
    query_place = data * span + place
    key_place = jnp.concatenate([(data - back) * span + place for back in range(reach, -1, -1)])
    lengths = lax.dynamic_index_in_dim(doc_lengths, section, 0, keepdims=False)
    ends = jnp.cumsum(lengths)
    query_doc = jnp.sum((query_place[:, None] >= ends[None, :]).astype(jnp.int32), axis=1)
    key_doc = jnp.sum((key_place[:, None] >= ends[None, :]).astype(jnp.int32), axis=1)
    distance = query_place[:, None] - key_place[None, :]
    allowed = (
        (key_place[None, :] >= 0)
        & (distance >= 0)
        & (distance < WINDOW)
        & (query_doc[:, None] == key_doc[None, :])
    )
    bias = jnp.where(allowed, 0.0, masked_score).astype(bf16)

    def forward(layer, hidden):
        qkv_w, out_w, up_w, down_w = weights[layer]
        gain1, shift1, q_bias, kv_bias, out_bias, gain2, shift2, up_bias, down_bias = small[layer]
        sq, skv, eq, ekv, so, eo, su, eu, sd, ed = adapters[layer]
        unit1, rsd1 = norm_parts(hidden)
        normed = spread((unit1 * gain1 + shift1).astype(bf16))
        low_q = against(normed, sq).astype(bf16)
        low_kv = against(normed, skv).astype(bf16)
        both = plain(normed, qkv_w)
        keyval = (both[:, local_q:] + kv_bias + plain(low_kv, ekv)).astype(bf16)
        pieces = [along(keyval, "dp", back) for back in range(reach, 0, -1)] + [keyval]
        queries = (both[:, :local_q] + q_bias + plain(low_q, eq)).astype(bf16)
        key_block = jnp.concatenate(pieces, axis=0)
        probs, mixed = attend(queries, key_block, bias, head)
        low_o = against(mixed, so).astype(bf16)
        attended = reduce_rows(against(mixed, out_w) + plain(low_o, eo))
        middle = hidden + (attended + out_bias)
        unit2, rsd2 = norm_parts(middle)
        second = spread((unit2 * gain2 + shift2).astype(bf16))
        low_u = against(second, su).astype(bf16)
        upward = plain(second, up_w) + up_bias + plain(low_u, eu)
        active, slope = gelu_parts(upward)
        active = active.astype(bf16)
        slope = slope.astype(bf16)
        low_d = against(active, sd).astype(bf16)
        result = middle + (reduce_rows(against(active, down_w) + plain(low_d, ed)) + down_bias)
        kept = (
            unit1,
            rsd1,
            normed,
            low_q,
            low_kv,
            queries,
            key_block,
            probs,
            mixed,
            low_o,
            unit2,
            rsd2,
            second,
            low_u,
            active,
            slope,
            low_d,
        )
        return result, kept

    def tiles(block):
        return block.reshape(rank, -1, 128).transpose(1, 0, 2)

    def flat(block):
        return block.transpose(1, 0, 2).reshape(rank, -1)

    def reduce_grads(shared, owned):
        pile = jnp.concatenate([tiles(part) for part in shared], axis=0).astype(bf16)
        lack = -pile.shape[0] % ranks
        if lack:
            pile = jnp.concatenate([pile, jnp.zeros((lack,) + pile.shape[1:], bf16)], axis=0)
        each = pile.shape[0] // ranks
        total = pick(pile, tensor * each, each).astype(f32)
        for j in range(1, ranks):
            block = pick(pile, ((tensor + j) % ranks) * each, each)
            total = total + around(block, "tensor", j).astype(f32)
        pile = jnp.concatenate([total] + [tiles(part) for part in owned], axis=0).astype(bf16)
        if pile.shape[0] % 2:
            pile = jnp.concatenate([pile, jnp.zeros((1,) + pile.shape[1:], bf16)], axis=0)
        half = pile.shape[0] // 2
        core = data % 2
        got = flipped(pick(pile, (1 - core) * half, half), "dp", 1)
        mine = (pick(pile, core * half, half).astype(f32) + got.astype(f32)).astype(bf16)
        got = flipped(mine, "dp", 2)
        mine = (mine.astype(f32) + got.astype(f32)).astype(bf16)
        parts = jnp.stack([mine] + [around(mine, "dp", 4 * k) for k in range(1, 4)])
        turn = data // 4
        total = sum(
            lax.dynamic_index_in_dim(parts, (turn - r) % 4, 0, keepdims=False).astype(f32)
            for r in range(4)
        )
        return total.astype(bf16)

    def spread_grads(mine, shared_sizes, owned_sizes):
        shared_count = sum(shared_sizes) // 128
        each = -(-shared_count // ranks)
        owned_count = sum(owned_sizes) // 128
        core = data % 2
        other = flipped(mine, "dp", 1)
        lower = jnp.where(core == 0, mine, other)
        upper = jnp.where(core == 0, other, mine)
        pile = jnp.concatenate([lower, upper], axis=1)
        own = pile[:, :each]
        parts = jnp.stack([own] + [around(own, "tensor", k) for k in range(1, ranks)])
        ordered = jnp.concatenate(
            [
                lax.dynamic_index_in_dim(parts, (tensor - r) % ranks, 0, keepdims=False)
                for r in range(ranks)
            ],
            axis=1,
        )
        results = []
        begin = 0
        for size in shared_sizes:
            count = size // 128
            results.append([flat(ordered[m, begin : begin + count]) for m in range(2)])
            begin += count
        begin = each
        owned = []
        for size in owned_sizes:
            count = size // 128
            owned.append([flat(pile[m, begin : begin + count]) for m in range(2)])
            begin += count
        return results, owned

    def backward_feed(layer, kept, grad):
        up_w, down_w = weights[layer][2:]
        gain2 = small[layer][5]
        so, eo, su, eu, sd, ed = adapters[layer][4:]
        unit2, rsd2, second, low_u, active, slope, low_d = kept[10:]
        branch = spread(grad.astype(bf16))
        inner_d = against(branch, ed).astype(bf16)
        grad_up = ((plain(branch, down_w) + plain(inner_d, sd)) * slope.astype(f32)).astype(bf16)
        inner_u = against(grad_up, eu).astype(bf16)
        grad_second = reduce_rows(against(grad_up, up_w) + plain(inner_u, su))
        grad_middle = grad + norm_back(unit2, rsd2, grad_second * gain2)
        shared = [across(inner_u, second), across(low_d, branch)]
        owned = [across(low_u, grad_up), across(inner_d, active)]
        return grad_middle, shared, owned

    def backward_attend(layer, kept, grad_middle):
        qkv_w, out_w = weights[layer][:2]
        gain1 = small[layer][0]
        sq, skv, eq, ekv, so, eo = adapters[layer][:6]
        unit1, rsd1, normed, low_q, low_kv, queries, key_block, probs, mixed, low_o = kept[:10]
        branch = spread(grad_middle.astype(bf16))
        inner_o = against(branch, eo).astype(bf16)
        grad_mixed = (plain(branch, out_w) + plain(inner_o, so)).astype(bf16)
        grad_q, grad_block = attend_back(grad_mixed, probs, queries, mixed, key_block, head)
        own = grad_block[reach * span :].astype(f32)
        for back in range(1, reach + 1):
            begin = (reach - back) * span
            own = own + along(grad_block[begin : begin + span], "dp", -back).astype(f32)
        grad_kv = own.astype(bf16)
        inner_q = against(grad_q, eq).astype(bf16)
        inner_kv = against(grad_kv, ekv).astype(bf16)
        grad_normed = (
            against(grad_q, qkv_w[:, :local_q])
            + plain(inner_q, sq)
            + against(grad_kv, qkv_w[:, local_q:])
            + plain(inner_kv, skv)
        )
        grad_hidden = grad_middle + norm_back(unit1, rsd1, reduce_rows(grad_normed) * gain1)
        out_grads = ([across(low_o, branch)], [across(inner_o, mixed)])
        shared = [across(inner_q, normed), across(inner_kv, normed), across(low_kv, grad_kv)]
        owned = [across(low_q, grad_q)]
        return grad_hidden, out_grads, (shared, owned)

    def to_upper(value):
        return lax.ppermute(value, "section", [(0, 1)])

    def to_lower(value):
        return lax.ppermute(value, "section", [(1, 0)])

    fresh = lax.dynamic_index_in_dim(block_input, section, 0, keepdims=False).astype(f32)
    result_zero, kept_zero = forward(0, fresh)
    passed = result_zero.astype(bf16)
    result_one, kept_one = forward(1, passed.astype(f32))
    final = result_one.astype(bf16)

    given = lax.dynamic_index_in_dim(cotangent, section, 0, keepdims=False).astype(f32)
    grad_middle_one, feed_shared, feed_owned = backward_feed(1, kept_one, given)
    grad_one, out_one_grads, qkv_one_grads = backward_attend(1, kept_one, grad_middle_one)
    late_one = reduce_grads(feed_shared + out_one_grads[0], feed_owned + out_one_grads[1])
    early_one = reduce_grads(*qkv_one_grads)
    grad_middle_zero, feed_shared, feed_owned = backward_feed(0, kept_zero, grad_one)
    grad_zero, out_zero_grads, qkv_zero_grads = backward_attend(0, kept_zero, grad_middle_zero)
    late_zero = reduce_grads(feed_shared + out_zero_grads[0], feed_owned + out_zero_grads[1])
    early_zero = reduce_grads(*qkv_zero_grads)

    def both_micros(zero, one):
        received = jnp.where(low_section, to_lower(zero), to_upper(one))
        own = jnp.where(low_section, zero, one)
        return jnp.where(
            low_section, jnp.stack([own, received]), jnp.stack([received, own])
        )

    section_outputs = both_micros(passed, final)
    received = jnp.where(
        low_section, to_lower(grad_zero.astype(bf16)), to_upper(grad_one.astype(bf16))
    ).astype(f32)
    own = jnp.where(low_section, grad_zero, grad_one)
    input_grads = jnp.where(
        low_section, jnp.stack([own, received]), jnp.stack([received, own])
    )

    late_shared, late_owned = spread_grads(
        both_micros(late_zero, late_one), [width, width, width], [local_f, local_f, local_q]
    )
    early_shared, early_owned = spread_grads(
        both_micros(early_zero, early_one), [width, width, 2 * head], [local_q]
    )
    onehot = (bank_choice[:, None] == jnp.arange(banks)[None, :]).astype(f32)

    def placed(pair, transpose):
        out = sum(
            onehot[m][:, None, None] * pair[m].astype(f32)[None] for m in range(2)
        )
        return (out.transpose(0, 2, 1) if transpose else out)[None]

    up_shrink_grad, down_expand_grad, out_expand_grad = late_shared
    up_expand_grad, down_shrink_grad, out_shrink_grad = late_owned
    q_shrink_grad, kv_shrink_grad, kv_expand_grad = early_shared
    (q_expand_grad,) = early_owned
    return (
        section_outputs[None],
        input_grads[None],
        placed(q_shrink_grad, True),
        placed(q_expand_grad, False),
        placed(kv_shrink_grad, True),
        placed(kv_expand_grad, False),
        placed(out_shrink_grad, True),
        placed(out_expand_grad, False),
        placed(up_shrink_grad, True),
        placed(up_expand_grad, False),
        placed(down_shrink_grad, True),
        placed(down_expand_grad, False),
    )


def solution(mesh):
    return jax.shard_map(
        per_device,
        mesh=mesh,
        in_specs=(
            P(None, ("dp", "tensor"), None),
            P(None, ("dp", "tensor"), None),
            P(),
            P(),
            P("section", None),
            P("section", None),
            P("section", "dp", "tensor"),
            P("section", "tensor"),
            P("section", "dp", None),
            P("section", None),
            P("section", "tensor", "dp"),
            P("section", None),
            P("section", None),
            P("section", None),
            P("section", "dp", "tensor"),
            P("section", "tensor"),
            P("section", "tensor", "dp"),
            P("section", None),
            P("section", None, None, None),
            P("section", None, None, "tensor"),
            P("section", None, None, None),
            P("section", None, None, None),
            P("section", None, "tensor", None),
            P("section", None, None, None),
            P("section", None, None, None),
            P("section", None, None, "tensor"),
            P("section", None, "tensor", None),
            P("section", None, None, None),
        ),
        out_specs=(
            P("section", None, ("dp", "tensor"), None),
            P("section", None, ("dp", "tensor"), None),
            P("section", None, None, None),
            P("section", None, None, "tensor"),
            P("section", None, None, None),
            P("section", None, None, None),
            P("section", None, "tensor", None),
            P("section", None, None, None),
            P("section", None, None, None),
            P("section", None, None, "tensor"),
            P("section", None, "tensor", None),
            P("section", None, None, None),
        ),
        check_vma=False,
    )
```

time: 2980 us -> 772 us (0.26)
  waiting for transfers between devices: 2210 us -> 320 us
  matrix products: 355 us -> 111 us
  starting transfers between devices: 68.8 us -> 229 us
  local copies, waits for them, and re-layouts: 159 us -> 30.7 us
  other arithmetic: 115 us -> 32.3 us
  loops' own time: 40.3 us -> 0 us
    all_gather x42 -> x3, waiting for transfers between devices: 1180 us -> 140 us  [gather(): return lax.all_gather(shard, 'dp', axis=0, tiled=True)]
    psum x2 -> x0, waiting for transfers between devices: 680 us -> none  [the longest x1 564 us: per_device(): lax.psum((grad_totals[0], grad_totals[2], grad_totals[3], grad_totals[5],...]
    reduce_scatter x12 -> x0, waiting for transfers between devices: 277 us -> none  [the longest x9 197 us: reduce_rows(): lax.psum_scatter(partial_rows.astype(jnp.bfloat16), 'tensor', scatter_dim...]
    dot_general x99 -> x28, matrix products: 225 us -> 54.1 us  [plain(): return jnp.dot(left, right, preferred_element_type=f32)]
    ppermute x30 -> x117, starting transfers between devices: 66.5 us -> 229 us  [the longest x78 132 us: around(): lax.ppermute(block, axis, [(i, (i + distance) % size) for i in range(size)])]
    ppermute x30 -> x117, waiting for transfers between devices: 52.3 us -> 180 us  [the longest x78 113 us: around(): lax.ppermute(block, axis, [(i, (i + distance) % size) for i in range(size)])]
    dot_general x36 -> x30, matrix products: 90.9 us -> 48.3 us  [against(): lax.dot_general(left, right, (((1,), (1,)), ((), ())), preferred_element_...]
    another operation x2 -> x0, loops' own time: 40.3 us -> none  [the longest x1 31.6 us: per_device(): lax.scan(backward_step, (empty_grads, zero_totals), jnp.arange(micro_coun...]
  transfers between devices with their start and end apart: 89 -> 120, of which waited for: 68 -> 57; matrix products, arithmetic and copies ran while one was open for 16% -> 19% of each run, Pallas kernels for 0% -> 2%
where the time goes in v1:
time: 772 us; the launch traced here: 761 us
  waiting for transfers between devices  320 us (41%)
  starting transfers between devices  229 us (30%)
  matrix products  111 us (14%)
  other arithmetic  32.3 us (4%)
  local copies, waits for them, and re-layouts  30.7 us (4%)
  between operations  21 us (3%)
  Pallas kernels  17 us (2%)
    all_gather x3, waiting for transfers between devices, gather(): return lax.all_gather(shard, 'dp', axis=0, tiled=True)  140 us
    ppermute x78, starting transfers between devices, around(): lax.ppermute(block, axis, [(i, (i + distance) % size) for i in range(size)])  132 us
    ppermute x78, waiting for transfers between devices, around(): lax.ppermute(block, axis, [(i, (i + distance) % size) for i in range(size)])  113 us
    dot_general x28, matrix products, plain(): return jnp.dot(left, right, preferred_element_type=f32)  54.1 us
    ppermute x16, starting transfers between devices, along(): return lax.ppermute(block, axis, route)  49.1 us
    dot_general x30, matrix products, against(): lax.dot_general(left, right, (((1,), (1,)), ((), ())), preferred_element_...  48.3 us
    ppermute x5, waiting for transfers between devices, swap(): return lax.ppermute(value, 'section', sides)  41.9 us
    ppermute x16, waiting for transfers between devices, along(): return lax.ppermute(block, axis, route)  17.8 us
  transfers between devices with their start and end apart: 120, of which 57 were waited for; matrix products, arithmetic and copies ran while one was open for 19% of the time, Pallas kernels for 2%

profile of v1, /device:TPU:0, one launch (start us, length us, event | category | flops | bytes accessed | tf_op | source)
XLA Modules:
  0.0 760.7 jit_solution(7818934397454911342)
XLA Ops:
  9.4 4.0 collective-permute-start.4
  13.4 4.9 collective-permute-done.4
  22.9 37.0 %collective-permute-done.5 = bf16[128,4608]{0,1:T(8,128)(2,1)S(1)} collective-permute-done((bf16[128,4608]{0,1:T(8,128)(2,1)S(1)}, bf16[128,4608]{0,1:T(8,128)(2,1)S(1)}, u32[]{:S(2)}, u32[]{:S(2)}) %collective-permute-start.5) | collective-permute-done | bytes 1179680 | tf_op jit(solution)/shard_map/ppermute | solution.py:204
  61.8 4.3 all-gather.4.cloned.1.call-done
  67.3 135.3 %all-gather.6.cloned.1.call-done = bf16[2048,5888]{0,1:T(8,128)(2,1)} async-done(((bf16[128,5888]{0,1:T(8,128)(2,1)}), bf16[2048,5888]{0,1:T(8,128)(2,1)}) %all-gather.6.cloned.1.call-update) | async-done | bytes 24117264 | tf_op jit(solution)/shard_map/all_gather | solution.py:279
  230.8 3.8 collective-permute-done.3
  234.6 5.8 collective-permute-done.2
  248.3 4.1 collective-permute-start.8
  255.8 6.3 collective-permute-done.7
  262.2 4.3 attend.2
  274.8 5.2 collective-permute-done.12
  280.0 4.3 collective-permute-done.14
  290.6 7.1 collective-permute-done.17
  302.2 7.8 %multiply_convert_fusion.1 = (bf16[256,2048]{1,0:T(8,128)(2,1)S(1)}, f32[256,2048]{1,0:T(8,128)}) fusion(f32[256,2048]{1,0:T(8,128)S(1)} %fusion.216, f32[2048]{0:T(1024)S(1)} %bitcast.697, bf16[2048,5888]{0,1:T(8,128)(2,1)} %all-gather.6.cloned.1.call-done, bf16[64,2048]{1,0:T(8,128)(2,1)S(1)} %collective-permute-done.17, ...), kind=kOutput, calls=%fused_computation.62 | convolution fusion | flops 2157445120 | bytes 14688256 | tf_op jit(solution)/shard_map/dot_general | solution.py:18
  310.4 5.8 fusion.10
  327.2 9.5 %collective-permute-done.20 = bf16[64,2048]{1,0:T(8,128)(2,1)S(1)} collective-permute-done((bf16[64,2048]{1,0:T(8,128)(2,1)S(1)}, bf16[64,2048]{1,0:T(8,128)(2,1)S(1)}, u32[]{:S(2)}, u32[]{:S(2)}) %collective-permute-start.20) | collective-permute-done | bytes 262176 | tf_op jit(solution)/shard_map/ppermute | solution.py:31
  337.6 8.0 %collective-permute-start.22 = (bf16[64,2048]{1,0:T(8,128)(2,1)S(1)}, bf16[64,2048]{1,0:T(8,128)(2,1)S(1)}, u32[]{:S(2)}, u32[]{:S(2)}) collective-permute-start(bf16[64,2048]{1,0:T(8,128)(2,1)S(1)} %fusion.106), channel_id=1, source_target_pairs={{0,2},{1,3},{2,0},{3,1},{4,6},{5,7},{6,4},{7,5},{8,10},{9,11},{10,... | collective-permute-start | bytes 786440 | tf_op jit(solution)/shard_map/ppermute | solution.py:31
  345.6 4.7 collective-permute-done.23
  360.5 5.2 collective-permute-start.24
  368.1 17.3 %collective-permute-start.26 = (bf16[256,256]{1,0:T(8,128)(2,1)S(1)}, bf16[256,256]{1,0:T(8,128)(2,1)S(1)}, u32[]{:S(2)}, u32[]{:S(2)}) collective-permute-start(bf16[256,256]{1,0:T(8,128)(2,1)S(1)} %fusion.158), channel_id=1, source_target_pairs={{0,8},{4,12},{8,16},{12,20},{16,24},{20,28},{24,32},{28,36},{32,40... | collective-permute-start | bytes 393224 | tf_op jit(solution)/shard_map/ppermute | solution.py:37
  385.4 3.9 collective-permute-start.27
  390.3 4.3 attend.3
  395.2 3.9 fusion.307
  406.1 4.6 collective-permute-done.28
  410.7 5.0 collective-permute-done.30
  428.8 6.3 collective-permute-done.32
  437.7 7.4 multiply_convert_fusion
  445.2 7.1 fusion.46
  456.6 5.7 fusion.4
  466.8 5.7 fusion.2
  483.0 6.1 collective-permute-done.34
  493.2 4.2 collective-permute-start.45
  511.4 4.2 attend_back.2
  548.9 4.2 fusion.310
  562.5 4.2 collective-permute-start.88
  566.7 4.9 collective-permute-start.87
  576.3 3.5 collective-permute-start.56
  584.2 4.5 collective-permute-done.109
  591.5 6.7 fusion.49
  598.6 5.7 fusion.12
  609.4 4.3 collective-permute-done.58
  615.2 4.9 collective-permute-done.59
  626.8 3.8 collective-permute-done.63
  630.6 4.2 collective-permute-done.62
  638.9 4.2 attend_back.3
  680.8 3.8 collective-permute-start.77
  698.8 6.0 collective-permute-start.90
  729.1 6.1 collective-permute-start.112
  (728 shorter events, 315.1 us)
Async XLA Ops:
  7.2 58.9 %all-gather.4.cloned.1.call-start = ((), (), s32[]{:S(2)}) async-start(), calls=%async_computation | async-start | bytes 3342336 | tf_op jit(solution)/shard_map/all_gather | solution.py:279
  19.1 183.6 %all-gather.6.cloned.1.call-start = ((), (), s32[]{:S(2)}) async-start(), calls=%async_computation.1 | async-start | bytes 25624576 | tf_op jit(solution)/shard_map/all_gather | solution.py:279
  19.6 40.4 %collective-permute-start.5 = (bf16[128,4608]{0,1:T(8,128)(2,1)S(1)}, bf16[128,4608]{0,1:T(8,128)(2,1)S(1)}, u32[]{:S(2)}, u32[]{:S(2)}) collective-permute-start(bf16[128,4608]{0,1:T(8,128)(2,1)S(1)} %pad_maximum_fusion.1), channel_id=1, source_target_pairs={{0,64},{64,0},{1,65},{65,1},{2,66},{66,2},{3,67},{67,3},{4,68},{68... | collective-permute-start | bytes 3538952 | tf_op jit(solution)/shard_map/ppermute | solution.py:204
  66.1 371.6 %all-gather.8.cloned.1.call-start = ((), (), s32[]{:S(2)}) async-start(), calls=%async_computation.2 | async-start | bytes 17825792 | tf_op jit(solution)/shard_map/all_gather | solution.py:279
  202.9 21.1 %collective-permute-start = (bf16[1,15104]{1,0:T(2,128)(2,1)S(1)}, bf16[1,15104]{1,0:T(2,128)(2,1)S(1)}, u32[]{:S(2)}, u32[]{:S(2)}) collective-permute-start(bf16[1,15104]{1,0:T(2,128)(2,1)S(1)} %constant_dynamic-update-slice_fusion), channel_id=1, source_target_pairs={{0,64},{64,0},{1,65},{65,1},{2,66},{66,2},{3,67},{67,3},{4,68},{68... | collective-permute-start | bytes 90632 | tf_op jit(solution)/shard_map/ppermute | solution.py:204
  213.0 17.7 %collective-permute-start.6 = (bf16[16,4864]{1,0:T(8,128)(2,1)S(1)}, bf16[16,4864]{1,0:T(8,128)(2,1)S(1)}, u32[]{:S(2)}, u32[]{:S(2)}) collective-permute-start(bf16[16,4864]{1,0:T(8,128)(2,1)S(1)} %pad_maximum_fusion.20), channel_id=1, source_target_pairs={{0,64},{64,0},{1,65},{65,1},{2,66},{66,2},{3,67},{67,3},{4,68},{68... | collective-permute-start | bytes 466952 | tf_op jit(solution)/shard_map/ppermute | solution.py:204
  218.7 22.6 %collective-permute-start.11 = (bf16[16,10752]{1,0:T(8,128)(2,1)S(1)}, bf16[16,10752]{1,0:T(8,128)(2,1)S(1)}, u32[]{:S(2)}, u32[]{:S(2)}) collective-permute-start(bf16[16,10752]{1,0:T(8,128)(2,1)S(1)} %get-tuple-element.114), channel_id=1, source_target_pairs={{0,64},{64,0},{1,65},{65,1},{2,66},{66,2},{3,67},{67,3},{4,68},{68... | collective-permute-start | bytes 1032200 | tf_op jit(solution)/shard_map/ppermute | solution.py:204
  226.5 13.9 %collective-permute-start.2 = (bf16[64,2048]{1,0:T(8,128)(2,1)S(1)}, bf16[64,2048]{1,0:T(8,128)(2,1)S(1)}, u32[]{:S(2)}, u32[]{:S(2)}) collective-permute-start(bf16[64,2048]{1,0:T(8,128)(2,1)S(1)} %fusion.113), channel_id=1, source_target_pairs={{0,2},{1,3},{2,0},{3,1},{4,6},{5,7},{6,4},{7,5},{8,10},{9,11},{10,... | collective-permute-start | bytes 786440 | tf_op jit(solution)/shard_map/ppermute | solution.py:31
  244.3 17.9 %collective-permute-start.10 = (bf16[256,256]{1,0:T(8,128)(2,1)S(1)}, bf16[256,256]{1,0:T(8,128)(2,1)S(1)}, u32[]{:S(2)}, u32[]{:S(2)}) collective-permute-start(bf16[256,256]{1,0:T(8,128)(2,1)S(1)} %fusion.160), channel_id=1, source_target_pairs={{0,4},{4,8},{8,12},{12,16},{16,20},{20,24},{24,28},{28,32},{32,36}... | collective-permute-start | bytes 393224 | tf_op jit(solution)/shard_map/ppermute | solution.py:37
  245.6 16.6 %collective-permute-start.9 = (bf16[256,256]{1,0:T(8,128)(2,1)S(1)}, bf16[256,256]{1,0:T(8,128)(2,1)S(1)}, u32[]{:S(2)}, u32[]{:S(2)}) collective-permute-start(bf16[256,256]{1,0:T(8,128)(2,1)S(1)} %fusion.160), channel_id=1, source_target_pairs={{0,8},{4,12},{8,16},{12,20},{16,24},{20,28},{24,32},{28,36},{32,40... | collective-permute-start | bytes 393224 | tf_op jit(solution)/shard_map/ppermute | solution.py:37
  248.3 13.9 %collective-permute-start.8 = (bf16[256,256]{1,0:T(8,128)(2,1)S(1)}, bf16[256,256]{1,0:T(8,128)(2,1)S(1)}, u32[]{:S(2)}, u32[]{:S(2)}) collective-permute-start(bf16[256,256]{1,0:T(8,128)(2,1)S(1)} %fusion.160), channel_id=1, source_target_pairs={{0,12},{4,16},{8,20},{12,24},{16,28},{20,32},{24,36},{28,40},{32,4... | collective-permute-start | bytes 393224 | tf_op jit(solution)/shard_map/ppermute | solution.py:37
  287.8 12.9 %collective-permute-start.16 = (bf16[64,2048]{1,0:T(8,128)(2,1)S(1)}, bf16[64,2048]{1,0:T(8,128)(2,1)S(1)}, u32[]{:S(2)}, u32[]{:S(2)}) collective-permute-start(bf16[64,2048]{1,0:T(8,128)(2,1)S(1)} %add_convert_fusion.3), channel_id=1, source_target_pairs={{0,2},{1,3},{2,0},{3,1},{4,6},{5,7},{6,4},{7,5},{8,10},{9,11},{10,... | collective-permute-start | bytes 786440 | tf_op jit(solution)/shard_map/ppermute | solution.py:31
  317.6 19.2 %collective-permute-start.20 = (bf16[64,2048]{1,0:T(8,128)(2,1)S(1)}, bf16[64,2048]{1,0:T(8,128)(2,1)S(1)}, u32[]{:S(2)}, u32[]{:S(2)}) collective-permute-start(bf16[64,2048]{1,0:T(8,128)(2,1)S(1)} %get-tuple-element.91), channel_id=1, source_target_pairs={{0,3},{1,0},{2,1},{3,2},{4,7},{5,4},{6,5},{7,6},{8,11},{9,8},{10,9... | collective-permute-start | bytes 786440 | tf_op jit(solution)/shard_map/ppermute | solution.py:31
  320.1 16.6 %collective-permute-start.19 = (bf16[64,2048]{1,0:T(8,128)(2,1)S(1)}, bf16[64,2048]{1,0:T(8,128)(2,1)S(1)}, u32[]{:S(2)}, u32[]{:S(2)}) collective-permute-start(bf16[64,2048]{1,0:T(8,128)(2,1)S(1)} %get-tuple-element.92), channel_id=1, source_target_pairs={{0,2},{1,3},{2,0},{3,1},{4,6},{5,7},{6,4},{7,5},{8,10},{9,11},{10,... | collective-permute-start | bytes 786440 | tf_op jit(solution)/shard_map/ppermute | solution.py:31
  321.7 81.6 %collective-permute-start.41 = (bf16[64,2048]{1,0:T(8,128)(2,1)}, bf16[64,2048]{1,0:T(8,128)(2,1)}, u32[]{:S(2)}, u32[]{:S(2)}) collective-permute-start(bf16[64,2048]{1,0:T(8,128)(2,1)} %dynamic-slice_bitcast_fusion), channel_id=1, source_target_pairs={{0,1},{1,2},{2,3},{3,0},{4,5},{5,6},{6,7},{7,4},{8,9},{9,10},{10,1... | collective-permute-start | bytes 786440 | tf_op jit(solution)/shard_map/ppermute | solution.py:31
  323.1 81.4 %collective-permute-start.40 = (bf16[64,2048]{1,0:T(8,128)(2,1)}, bf16[64,2048]{1,0:T(8,128)(2,1)}, u32[]{:S(2)}, u32[]{:S(2)}) collective-permute-start(bf16[64,2048]{1,0:T(8,128)(2,1)} %dynamic-slice_bitcast_fusion), channel_id=1, source_target_pairs={{0,2},{1,3},{2,0},{3,1},{4,6},{5,7},{6,4},{7,5},{8,10},{9,11},{10,... | collective-permute-start | bytes 786440 | tf_op jit(solution)/shard_map/ppermute | solution.py:31
  337.6 17.9 %collective-permute-start.22 = (bf16[64,2048]{1,0:T(8,128)(2,1)S(1)}, bf16[64,2048]{1,0:T(8,128)(2,1)S(1)}, u32[]{:S(2)}, u32[]{:S(2)}) collective-permute-start(bf16[64,2048]{1,0:T(8,128)(2,1)S(1)} %fusion.106), channel_id=1, source_target_pairs={{0,2},{1,3},{2,0},{3,1},{4,6},{5,7},{6,4},{7,5},{8,10},{9,11},{10,... | collective-permute-start | bytes 786440 | tf_op jit(solution)/shard_map/ppermute | solution.py:31
  350.3 54.2 %collective-permute-start.39 = (bf16[64,2048]{1,0:T(8,128)(2,1)}, bf16[64,2048]{1,0:T(8,128)(2,1)}, u32[]{:S(2)}, u32[]{:S(2)}) collective-permute-start(bf16[64,2048]{1,0:T(8,128)(2,1)} %dynamic-slice_bitcast_fusion), channel_id=1, source_target_pairs={{0,3},{1,0},{2,1},{3,2},{4,7},{5,4},{6,5},{7,6},{8,11},{9,8},{10,9... | collective-permute-start | bytes 786440 | tf_op jit(solution)/shard_map/ppermute | solution.py:31
  359.2 26.2 %collective-permute-start.25 = (bf16[256,256]{1,0:T(8,128)(2,1)S(1)}, bf16[256,256]{1,0:T(8,128)(2,1)S(1)}, u32[]{:S(2)}, u32[]{:S(2)}) collective-permute-start(bf16[256,256]{1,0:T(8,128)(2,1)S(1)} %fusion.158), channel_id=1, source_target_pairs={{0,12},{4,16},{8,20},{12,24},{16,28},{20,32},{24,36},{28,40},{32,4... | collective-permute-start | bytes 393224 | tf_op jit(solution)/shard_map/ppermute | solution.py:37
  368.1 21.2 %collective-permute-start.26 = (bf16[256,256]{1,0:T(8,128)(2,1)S(1)}, bf16[256,256]{1,0:T(8,128)(2,1)S(1)}, u32[]{:S(2)}, u32[]{:S(2)}) collective-permute-start(bf16[256,256]{1,0:T(8,128)(2,1)S(1)} %fusion.158), channel_id=1, source_target_pairs={{0,8},{4,12},{8,16},{12,20},{16,24},{20,28},{24,32},{28,36},{32,40... | collective-permute-start | bytes 393224 | tf_op jit(solution)/shard_map/ppermute | solution.py:37
  400.1 15.6 %collective-permute-start.30 = (bf16[64,2048]{1,0:T(8,128)(2,1)}, bf16[64,2048]{1,0:T(8,128)(2,1)S(1)}, u32[]{:S(2)}, u32[]{:S(2)}) collective-permute-start(bf16[64,2048]{1,0:T(8,128)(2,1)} %get-tuple-element.88), channel_id=1, source_target_pairs={{0,3},{1,0},{2,1},{3,2},{4,7},{5,4},{6,5},{7,6},{8,11},{9,8},{10,9... | collective-permute-start | bytes 786440 | tf_op jit(solution)/shard_map/ppermute | solution.py:31
  403.3 13.7 %collective-permute-start.29 = (bf16[64,2048]{1,0:T(8,128)(2,1)}, bf16[64,2048]{1,0:T(8,128)(2,1)}, u32[]{:S(2)}, u32[]{:S(2)}) collective-permute-start(bf16[64,2048]{1,0:T(8,128)(2,1)} %get-tuple-element.89), channel_id=1, source_target_pairs={{0,2},{1,3},{2,0},{3,1},{4,6},{5,7},{6,4},{7,5},{8,10},{9,11},{10,... | collective-permute-start | bytes 786440 | tf_op jit(solution)/shard_map/ppermute | solution.py:31
  420.2 14.9 %collective-permute-start.32 = (bf16[64,2048]{1,0:T(8,128)(2,1)S(1)}, bf16[64,2048]{1,0:T(8,128)(2,1)S(1)}, u32[]{:S(2)}, u32[]{:S(2)}) collective-permute-start(bf16[64,2048]{1,0:T(8,128)(2,1)S(1)} %add_convert_fusion.2), channel_id=1, source_target_pairs={{0,2},{1,3},{2,0},{3,1},{4,6},{5,7},{6,4},{7,5},{8,10},{9,11},{10,... | collective-permute-start | bytes 786440 | tf_op jit(solution)/shard_map/ppermute | solution.py:31
  425.3 94.0 %collective-permute-start.37 = (bf16[64,2048]{1,0:T(8,128)(2,1)S(1)}, bf16[64,2048]{1,0:T(8,128)(2,1)}, u32[]{:S(2)}, u32[]{:S(2)}) collective-permute-start(bf16[64,2048]{1,0:T(8,128)(2,1)S(1)} %get-tuple-element.67), channel_id=1, source_target_pairs={{64,0},{65,1},{66,2},{67,3},{68,4},{69,5},{70,6},{71,7},{72,8},{73... | collective-permute-start | bytes 786440 | tf_op jit(solution)/shard_map/ppermute | solution.py:494
  463.2 13.7 %collective-permute-start.44 = (bf16[64,2048]{1,0:T(8,128)(2,1)S(1)}, bf16[64,2048]{1,0:T(8,128)(2,1)S(1)}, u32[]{:S(2)}, u32[]{:S(2)}) collective-permute-start(bf16[64,2048]{1,0:T(8,128)(2,1)S(1)} %get-tuple-element.82), channel_id=1, source_target_pairs={{0,3},{1,0},{2,1},{3,2},{4,7},{5,4},{6,5},{7,6},{8,11},{9,8},{10,9... | collective-permute-start | bytes 786440 | tf_op jit(solution)/shard_map/ppermute | solution.py:31
  466.2 13.2 %collective-permute-start.43 = (bf16[64,2048]{1,0:T(8,128)(2,1)S(1)}, bf16[64,2048]{1,0:T(8,128)(2,1)S(1)}, u32[]{:S(2)}, u32[]{:S(2)}) collective-permute-start(bf16[64,2048]{1,0:T(8,128)(2,1)S(1)} %get-tuple-element.83), channel_id=1, source_target_pairs={{0,2},{1,3},{2,0},{3,1},{4,6},{5,7},{6,4},{7,5},{8,10},{9,11},{10,... | collective-permute-start | bytes 786440 | tf_op jit(solution)/shard_map/ppermute | solution.py:31
  473.1 16.0 %collective-permute-start.34 = (bf16[64,2048]{1,0:T(8,128)(2,1)S(1)}, bf16[64,2048]{1,0:T(8,128)(2,1)S(1)}, u32[]{:S(2)}, u32[]{:S(2)}) collective-permute-start(bf16[64,2048]{1,0:T(8,128)(2,1)S(1)} %get-tuple-element.84), channel_id=1, source_target_pairs={{0,1},{1,2},{2,3},{3,0},{4,5},{5,6},{6,7},{7,4},{8,9},{9,10},{10,1... | collective-permute-start | bytes 786440 | tf_op jit(solution)/shard_map/ppermute | solution.py:31
  474.6 18.6 %collective-permute-start.36 = (bf16[64,2048]{1,0:T(8,128)(2,1)S(1)}, bf16[64,2048]{1,0:T(8,128)(2,1)S(1)}, u32[]{:S(2)}, u32[]{:S(2)}) collective-permute-start(bf16[64,2048]{1,0:T(8,128)(2,1)S(1)} %get-tuple-element.85), channel_id=1, source_target_pairs={{0,3},{1,0},{2,1},{3,2},{4,7},{5,4},{6,5},{7,6},{8,11},{9,8},{10,9... | collective-permute-start | bytes 786440 | tf_op jit(solution)/shard_map/ppermute | solution.py:31
  476.9 20.5 %collective-permute-start.35 = (bf16[64,2048]{1,0:T(8,128)(2,1)S(1)}, bf16[64,2048]{1,0:T(8,128)(2,1)S(1)}, u32[]{:S(2)}, u32[]{:S(2)}) collective-permute-start(bf16[64,2048]{1,0:T(8,128)(2,1)S(1)} %get-tuple-element.86), channel_id=1, source_target_pairs={{0,2},{1,3},{2,0},{3,1},{4,6},{5,7},{6,4},{7,5},{8,10},{9,11},{10,... | collective-permute-start | bytes 786440 | tf_op jit(solution)/shard_map/ppermute | solution.py:31
  480.9 20.1 %collective-permute-start.47 = (bf16[64,2048]{1,0:T(8,128)(2,1)S(1)}, bf16[64,2048]{1,0:T(8,128)(2,1)S(1)}, u32[]{:S(2)}, u32[]{:S(2)}) collective-permute-start(bf16[64,2048]{1,0:T(8,128)(2,1)S(1)} %get-tuple-element.59), channel_id=1, source_target_pairs={{0,1},{1,2},{2,3},{3,0},{4,5},{5,6},{6,7},{7,4},{8,9},{9,10},{10,1... | collective-permute-start | bytes 786440 | tf_op jit(solution)/shard_map/ppermute | solution.py:31
  498.3 22.2 %collective-permute-start.38 = (bf16[64,2048]{1,0:T(8,128)(2,1)S(1)}, bf16[64,2048]{1,0:T(8,128)(2,1)S(1)}, u32[]{:S(2)}, u32[]{:S(2)}) collective-permute-start(bf16[64,2048]{1,0:T(8,128)(2,1)S(1)} %get-tuple-element.63), channel_id=1, source_target_pairs={{0,64},{1,65},{2,66},{3,67},{4,68},{5,69},{6,70},{7,71},{8,72},{9,... | collective-permute-start | bytes 786440 | tf_op jit(solution)/shard_map/ppermute | solution.py:491
  503.7 20.6 %collective-permute-start.103 = (bf16[12,16,128]{2,0,1:T(8,128)(2,1)}, bf16[12,16,128]{2,0,1:T(8,128)(2,1)}, u32[]{:S(2)}, u32[]{:S(2)}) collective-permute-start(bf16[12,16,128]{2,0,1:T(8,128)(2,1)} %get-tuple-element.155), channel_id=1, source_target_pairs={{0,1},{1,2},{2,3},{3,0},{4,5},{5,6},{6,7},{7,4},{8,9},{9,10},{10,1... | collective-permute-start | bytes 147464 | tf_op jit(solution)/shard_map/ppermute | solution.py:31
  504.5 21.1 %collective-permute-start.105 = (bf16[12,16,128]{2,0,1:T(8,128)(2,1)}, bf16[12,16,128]{2,0,1:T(8,128)(2,1)}, u32[]{:S(2)}, u32[]{:S(2)}) collective-permute-start(bf16[12,16,128]{2,0,1:T(8,128)(2,1)} %get-tuple-element.156), channel_id=1, source_target_pairs={{0,3},{1,0},{2,1},{3,2},{4,7},{5,4},{6,5},{7,6},{8,11},{9,8},{10,9... | collective-permute-start | bytes 147464 | tf_op jit(solution)/shard_map/ppermute | solution.py:31
  507.4 19.5 %collective-permute-start.104 = (bf16[12,16,128]{2,0,1:T(8,128)(2,1)}, bf16[12,16,128]{2,0,1:T(8,128)(2,1)}, u32[]{:S(2)}, u32[]{:S(2)}) collective-permute-start(bf16[12,16,128]{2,0,1:T(8,128)(2,1)} %get-tuple-element.157), channel_id=1, source_target_pairs={{0,2},{1,3},{2,0},{3,1},{4,6},{5,7},{6,4},{7,5},{8,10},{9,11},{10,... | collective-permute-start | bytes 147464 | tf_op jit(solution)/shard_map/ppermute | solution.py:31
  529.4 31.2 %collective-permute-start.106 = (bf16[24,16,128]{2,0,1:T(8,128)(2,1)}, bf16[24,16,128]{2,0,1:T(8,128)(2,1)}, u32[]{:S(2)}, u32[]{:S(2)}) collective-permute-start(bf16[24,16,128]{2,0,1:T(8,128)(2,1)} %constant_dynamic-slice_fusion), channel_id=1, source_target_pairs={{0,4},{4,0},{8,12},{12,8},{16,20},{20,16},{24,28},{28,24},{32,36},... | collective-permute-start | bytes 294920 | tf_op jit(solution)/shard_map/ppermute | solution.py:42
  553.6 18.1 %collective-permute-start.52 = (bf16[64,2048]{1,0:T(8,128)(2,1)S(1)}, bf16[64,2048]{1,0:T(8,128)(2,1)S(1)}, u32[]{:S(2)}, u32[]{:S(2)}) collective-permute-start(bf16[64,2048]{1,0:T(8,128)(2,1)S(1)} %get-tuple-element.78), channel_id=1, source_target_pairs={{0,1},{1,2},{2,3},{3,0},{4,5},{5,6},{6,7},{7,4},{8,9},{9,10},{10,1... | collective-permute-start | bytes 786440 | tf_op jit(solution)/shard_map/ppermute | solution.py:31
  553.7 19.6 %collective-permute-start.54 = (bf16[64,2048]{1,0:T(8,128)(2,1)S(1)}, bf16[64,2048]{1,0:T(8,128)(2,1)S(1)}, u32[]{:S(2)}, u32[]{:S(2)}) collective-permute-start(bf16[64,2048]{1,0:T(8,128)(2,1)S(1)} %get-tuple-element.79), channel_id=1, source_target_pairs={{0,3},{1,0},{2,1},{3,2},{4,7},{5,4},{6,5},{7,6},{8,11},{9,8},{10,9... | collective-permute-start | bytes 786440 | tf_op jit(solution)/shard_map/ppermute | solution.py:31
  556.9 18.1 %collective-permute-start.53 = (bf16[64,2048]{1,0:T(8,128)(2,1)S(1)}, bf16[64,2048]{1,0:T(8,128)(2,1)S(1)}, u32[]{:S(2)}, u32[]{:S(2)}) collective-permute-start(bf16[64,2048]{1,0:T(8,128)(2,1)S(1)} %get-tuple-element.80), channel_id=1, source_target_pairs={{0,2},{1,3},{2,0},{3,1},{4,6},{5,7},{6,4},{7,5},{8,10},{9,11},{10,... | collective-permute-start | bytes 786440 | tf_op jit(solution)/shard_map/ppermute | solution.py:31
  562.5 13.7 %collective-permute-start.88 = (bf16[7,16,128]{2,0,1:T(8,128)(2,1)S(1)}, bf16[7,16,128]{2,0,1:T(8,128)(2,1)S(1)}, u32[]{:S(2)}, u32[]{:S(2)}) collective-permute-start(bf16[7,16,128]{2,0,1:T(8,128)(2,1)S(1)} %add_convert_fusion.17), channel_id=1, source_target_pairs={{0,48},{4,52},{8,56},{12,60},{16,0},{20,4},{24,8},{28,12},{32,16},... | collective-permute-start | bytes 86024 | tf_op jit(solution)/shard_map/ppermute | solution.py:31
  566.7 13.0 %collective-permute-start.87 = (bf16[7,16,128]{2,0,1:T(8,128)(2,1)S(1)}, bf16[7,16,128]{2,0,1:T(8,128)(2,1)S(1)}, u32[]{:S(2)}, u32[]{:S(2)}) collective-permute-start(bf16[7,16,128]{2,0,1:T(8,128)(2,1)S(1)} %add_convert_fusion.17), channel_id=1, source_target_pairs={{0,32},{4,36},{8,40},{12,44},{16,48},{20,52},{24,56},{28,60},{32,0... | collective-permute-start | bytes 86024 | tf_op jit(solution)/shard_map/ppermute | solution.py:31
  575.7 14.0 %collective-permute-start.57 = (bf16[64,2048]{1,0:T(8,128)(2,1)S(1)}, bf16[64,2048]{1,0:T(8,128)(2,1)S(1)}, u32[]{:S(2)}, u32[]{:S(2)}) collective-permute-start(bf16[64,2048]{1,0:T(8,128)(2,1)S(1)} %get-tuple-element.56), channel_id=1, source_target_pairs={{0,1},{1,2},{2,3},{3,0},{4,5},{5,6},{6,7},{7,4},{8,9},{9,10},{10,1... | collective-permute-start | bytes 786440 | tf_op jit(solution)/shard_map/ppermute | solution.py:31
  576.3 14.4 %collective-permute-start.56 = (bf16[64,2048]{1,0:T(8,128)(2,1)S(1)}, bf16[64,2048]{1,0:T(8,128)(2,1)S(1)}, u32[]{:S(2)}, u32[]{:S(2)}) collective-permute-start(bf16[64,2048]{1,0:T(8,128)(2,1)S(1)} %get-tuple-element.56), channel_id=1, source_target_pairs={{0,2},{1,3},{2,0},{3,1},{4,6},{5,7},{6,4},{7,5},{8,10},{9,11},{10,... | collective-permute-start | bytes 786440 | tf_op jit(solution)/shard_map/ppermute | solution.py:31
  646.2 13.1 %collective-permute-start.97 = (bf16[12,16,128]{2,0,1:T(8,128)(2,1)}, bf16[12,16,128]{2,0,1:T(8,128)(2,1)}, u32[]{:S(2)}, u32[]{:S(2)}) collective-permute-start(bf16[12,16,128]{2,0,1:T(8,128)(2,1)} %get-tuple-element.153), channel_id=1, source_target_pairs={{0,3},{1,0},{2,1},{3,2},{4,7},{5,4},{6,5},{7,6},{8,11},{9,8},{10,9... | collective-permute-start | bytes 147464 | tf_op jit(solution)/shard_map/ppermute | solution.py:31
  663.3 35.5 %collective-permute-start.98 = (bf16[24,16,128]{2,0,1:T(8,128)(2,1)}, bf16[24,16,128]{2,0,1:T(8,128)(2,1)}, u32[]{:S(2)}, u32[]{:S(2)}) collective-permute-start(bf16[24,16,128]{2,0,1:T(8,128)(2,1)} %constant_dynamic-slice_fusion.4), channel_id=1, source_target_pairs={{0,4},{4,0},{8,12},{12,8},{16,20},{20,16},{24,28},{28,24},{32,36},... | collective-permute-start | bytes 294920 | tf_op jit(solution)/shard_map/ppermute | solution.py:42
  691.8 31.1 %collective-permute-start.68 = (bf16[64,2048]{1,0:T(8,128)(2,1)S(1)}, bf16[64,2048]{1,0:T(8,128)(2,1)S(1)}, u32[]{:S(2)}, u32[]{:S(2)}) collective-permute-start(bf16[64,2048]{1,0:T(8,128)(2,1)S(1)} %get-tuple-element.72), channel_id=1, source_target_pairs={{0,1},{1,2},{2,3},{3,0},{4,5},{5,6},{6,7},{7,4},{8,9},{9,10},{10,1... | collective-permute-start | bytes 786440 | tf_op jit(solution)/shard_map/ppermute | solution.py:31
  693.3 31.6 %collective-permute-start.70 = (bf16[64,2048]{1,0:T(8,128)(2,1)S(1)}, bf16[64,2048]{1,0:T(8,128)(2,1)S(1)}, u32[]{:S(2)}, u32[]{:S(2)}) collective-permute-start(bf16[64,2048]{1,0:T(8,128)(2,1)S(1)} %get-tuple-element.73), channel_id=1, source_target_pairs={{0,3},{1,0},{2,1},{3,2},{4,7},{5,4},{6,5},{7,6},{8,11},{9,8},{10,9... | collective-permute-start | bytes 786440 | tf_op jit(solution)/shard_map/ppermute | solution.py:31
  695.4 31.7 %collective-permute-start.69 = (bf16[64,2048]{1,0:T(8,128)(2,1)S(1)}, bf16[64,2048]{1,0:T(8,128)(2,1)S(1)}, u32[]{:S(2)}, u32[]{:S(2)}) collective-permute-start(bf16[64,2048]{1,0:T(8,128)(2,1)S(1)} %get-tuple-element.74), channel_id=1, source_target_pairs={{0,2},{1,3},{2,0},{3,1},{4,6},{5,7},{6,4},{7,5},{8,10},{9,11},{10,... | collective-permute-start | bytes 786440 | tf_op jit(solution)/shard_map/ppermute | solution.py:31
  719.1 24.9 %collective-permute-start.72 = (bf16[64,2048]{1,0:T(8,128)(2,1)S(1)}, bf16[64,2048]{1,0:T(8,128)(2,1)S(1)}, u32[]{:S(2)}, u32[]{:S(2)}) collective-permute-start(bf16[64,2048]{1,0:T(8,128)(2,1)S(1)} %copy-done.43), channel_id=1, source_target_pairs={{0,64},{1,65},{2,66},{3,67},{4,68},{5,69},{6,70},{7,71},{8,72},{9,... | collective-permute-start | bytes 786440 | tf_op jit(solution)/shard_map/ppermute | solution.py:491
  (186 other events, 3411.0 us)
Sparse Core Ops, SparseCore 0:
  19.2 46.8 all-gather.3
  67.7 134.8 all-gather.5
  204.9 119.5 all-gather.7

commit v2 on v1

--- a/solution.py
+++ b/solution.py
@@ -72,9 +72,9 @@
     top = jnp.max(scores, axis=-1, keepdims=True)
     lifted = jnp.exp(scores - top)
     total = jnp.sum(lifted, axis=-1, keepdims=True)
-    probs = (lifted * (1.0 / total)).astype(bf16)
+    probs = lifted * (1.0 / total)
     prob_ref[0] = probs
-    mixed_ref[...] = plain(probs, keyval_ref[:, head:]).astype(bf16)
+    mixed_ref[...] = plain(probs.astype(bf16), keyval_ref[:, head:]).astype(bf16)
 
 
 def attend(queries, key_block, bias, head):
@@ -89,7 +89,7 @@
         in_specs=[column, whole((keys, 2 * head)), whole((rows, keys))],
         out_specs=[pl.BlockSpec((1, rows, keys), lambda h: (h, 0, 0)), column],
         out_shape=[
-            jax.ShapeDtypeStruct((heads, rows, keys), bf16),
+            jax.ShapeDtypeStruct((heads, rows, keys), f32),
             jax.ShapeDtypeStruct((rows, width), bf16),
         ],
         compiler_params=pltpu.CompilerParams(vmem_limit_bytes=40 * 2**20),
@@ -98,18 +98,18 @@
 
 
 def attend_back_kernel(
-    scale, grad_ref, prob_ref, query_ref, mixed_ref, keyval_ref, dq_ref, dkv_ref, key_sum, value_sum
+    scale, grad_ref, prob_ref, query_ref, keyval_ref, dq_ref, dkv_ref, key_sum, value_sum
 ):
     step = pl.program_id(0)
     head = query_ref.shape[1]
     grad = grad_ref[...]
     probs = prob_ref[0]
-    delta = jnp.sum(grad.astype(f32) * mixed_ref[...].astype(f32), axis=-1, keepdims=True)
     grad_probs = against(grad, keyval_ref[:, head:])
-    grad_scores = (probs.astype(f32) * (grad_probs - delta)).astype(bf16)
+    delta = jnp.sum(grad_probs * probs, axis=-1, keepdims=True)
+    grad_scores = (probs * (grad_probs - delta)).astype(bf16)
     dq_ref[...] = (plain(grad_scores, keyval_ref[:, :head]) * scale).astype(bf16)
     keys = across(grad_scores, query_ref[...])
-    values = across(probs, grad)
+    values = across(probs.astype(bf16), grad)
 
     @pl.when(step == 0)
     def _():
@@ -127,7 +127,7 @@
         dkv_ref[:, head:] = value_sum[...].astype(bf16)
 
 
-def attend_back(grad_mixed, probs, queries, mixed, key_block, head):
+def attend_back(grad_mixed, probs, queries, key_block, head):
     rows, width = queries.shape
     keys = key_block.shape[0]
     heads = width // head
@@ -140,7 +140,6 @@
             column,
             pl.BlockSpec((1, rows, keys), lambda h: (h, 0, 0)),
             column,
-            column,
             whole,
         ],
         out_specs=[column, whole],
@@ -151,7 +150,167 @@
         scratch_shapes=[pltpu.VMEM((keys, head), f32), pltpu.VMEM((keys, head), f32)],
         compiler_params=pltpu.CompilerParams(vmem_limit_bytes=40 * 2**20),
         name="attend_back",
-    )(grad_mixed, probs, queries, mixed, key_block)
+    )(grad_mixed, probs, queries, key_block)
+
+
+def weight_copies(table_ref, up_buf, down_buf, sems):
+    count, width, tile = up_buf.shape
+    each = count // 2
+    copies = []
+    for j in range(count):
+        rows = pl.ds(j // each * width, width)
+        begin = j % each * tile
+        for k, buf in enumerate((up_buf, down_buf)):
+            columns = pl.ds(begin + k * each * tile, tile)
+            copies.append(
+                pltpu.make_async_copy(table_ref.at[rows, columns], buf.at[j], sems.at[k, j])
+            )
+    return copies
+
+
+def feed_kernel(
+    second_ref, table_ref, bias_ref, eu_ref, sd_ref, su_ref, ed_ref,
+    active_ref, slope_ref, low_u_ref, low_d_ref, out_ref, up_buf, down_buf, total, sems,
+):
+    count, width, tile = up_buf.shape
+    copies = weight_copies(table_ref, up_buf, down_buf, sems)
+    for copy in copies:
+        copy.start()
+    second = second_ref[...]
+    low_u = against(second, su_ref[...]).astype(bf16)
+    low_u_ref[...] = low_u
+    low = 0.0
+    for j in range(count):
+        columns = pl.ds(j * tile, tile)
+        copies[2 * j].wait()
+        upward = plain(second, up_buf[j]) + plain(low_u, eu_ref[:, columns]) + bias_ref[:, columns]
+        active, slope = gelu_parts(upward)
+        active = active.astype(bf16)
+        active_ref[:, columns] = active
+        slope_ref[:, columns] = slope.astype(bf16)
+        low = low + against(active, sd_ref[:, columns])
+        copies[2 * j + 1].wait()
+        part = against(active, down_buf[j])
+        if j == 0:
+            total[...] = part
+        elif j < count - 1:
+            total[...] += part
+    low_d = low.astype(bf16)
+    low_d_ref[...] = low_d
+    out_ref[...] = (total[...] + part + plain(low_d, ed_ref[...])).astype(bf16)
+
+
+def feed_scratch(rows, width, hidden, tile):
+    return [
+        pltpu.VMEM((hidden // tile, width, tile), bf16),
+        pltpu.VMEM((hidden // tile, width, tile), bf16),
+        pltpu.VMEM((rows, width), f32),
+        pltpu.SemaphoreType.DMA((2, hidden // tile)),
+    ]
+
+
+def feed(second, table, bias, eu, sd, su, ed):
+    rows, width = second.shape
+    rank, hidden = eu.shape
+    held = pl.BlockSpec(memory_space=pltpu.VMEM)
+    return pl.pallas_call(
+        feed_kernel,
+        in_specs=[held, pl.BlockSpec(memory_space=pl.ANY)] + [held] * 5,
+        out_specs=[held] * 5,
+        out_shape=[
+            jax.ShapeDtypeStruct((rows, hidden), bf16),
+            jax.ShapeDtypeStruct((rows, hidden), bf16),
+            jax.ShapeDtypeStruct((rows, rank), bf16),
+            jax.ShapeDtypeStruct((rows, rank), bf16),
+            jax.ShapeDtypeStruct((rows, width), bf16),
+        ],
+        scratch_shapes=feed_scratch(rows, width, hidden, 512),
+        compiler_params=pltpu.CompilerParams(vmem_limit_bytes=40 * 2**20),
+        cost_estimate=pl.CostEstimate(
+            flops=4 * rows * width * hidden,
+            bytes_accessed=4 * width * hidden + 8 * rows * hidden,
+            transcendentals=rows * hidden,
+        ),
+        name="feed",
+    )(second, table, bias, eu, sd, su, ed)
+
+
+def feed_back_kernel(
+    branch_ref, table_ref, slope_ref, eu_ref, sd_ref, su_ref, ed_ref,
+    grad_up_ref, inner_d_ref, inner_u_ref, out_ref, up_buf, down_buf, total, sems,
+):
+    count, width, tile = up_buf.shape
+    copies = weight_copies(table_ref, up_buf, down_buf, sems)
+    for j in range(count):
+        copies[2 * j + 1].start()
+        copies[2 * j].start()
+    branch = branch_ref[...]
+    inner_d = against(branch, ed_ref[...]).astype(bf16)
+    inner_d_ref[...] = inner_d
+    inner = 0.0
+    for j in range(count):
+        columns = pl.ds(j * tile, tile)
+        copies[2 * j + 1].wait()
+        grad = plain(branch, down_buf[j]) + plain(inner_d, sd_ref[:, columns])
+        grad = (grad * slope_ref[:, columns].astype(f32)).astype(bf16)
+        grad_up_ref[:, columns] = grad
+        inner = inner + against(grad, eu_ref[:, columns])
+        copies[2 * j].wait()
+        part = against(grad, up_buf[j])
+        if j == 0:
+            total[...] = part
+        elif j < count - 1:
+            total[...] += part
+    inner_u = inner.astype(bf16)
+    inner_u_ref[...] = inner_u
+    out_ref[...] = (total[...] + part + plain(inner_u, su_ref[...])).astype(bf16)
+
+
+def feed_back(branch, table, slope, eu, sd, su, ed):
+    rows, width = branch.shape
+    rank, hidden = eu.shape
+    held = pl.BlockSpec(memory_space=pltpu.VMEM)
+    return pl.pallas_call(
+        feed_back_kernel,
+        in_specs=[held, pl.BlockSpec(memory_space=pl.ANY)] + [held] * 5,
+        out_specs=[held] * 4,
+        out_shape=[
+            jax.ShapeDtypeStruct((rows, hidden), bf16),
+            jax.ShapeDtypeStruct((rows, rank), bf16),
+            jax.ShapeDtypeStruct((rows, rank), bf16),
+            jax.ShapeDtypeStruct((rows, width), bf16),
+        ],
+        scratch_shapes=feed_scratch(rows, width, hidden, 512),
+        compiler_params=pltpu.CompilerParams(vmem_limit_bytes=40 * 2**20),
+        cost_estimate=pl.CostEstimate(
+            flops=4 * rows * width * hidden,
+            bytes_accessed=4 * width * hidden + 4 * rows * hidden,
+            transcendentals=0,
+        ),
+        name="feed_back",
+    )(branch, table, slope, eu, sd, su, ed)
+
+
+def place_kernel(rank_ref, mine_ref, other_ref, out_ref):
+    core = rank_ref[0] % 2
+    out_ref[0, pl.ds(core, 1)] = mine_ref[...]
+    out_ref[0, pl.ds(1 - core, 1)] = other_ref[...]
+
+
+def by_rank(rank, mine, other):
+    chips, rows, columns = mine.shape
+    block = pl.BlockSpec((1, rows, columns), lambda i, r: (i, 0, 0))
+    return pl.pallas_call(
+        place_kernel,
+        grid_spec=pltpu.PrefetchScalarGridSpec(
+            num_scalar_prefetch=1,
+            grid=(chips,),
+            in_specs=[block, block],
+            out_specs=pl.BlockSpec((1, 2, rows, columns), lambda i, r: (i ^ (r[0] // 2), 0, 0, 0)),
+        ),
+        out_shape=jax.ShapeDtypeStruct((chips, 2, rows, columns), bf16),
+        name="place",
+    )(rank.reshape(1).astype(jnp.int32), mine, other)
 
 
 def per_device(
@@ -212,7 +371,7 @@
 
     def reduce_rows(partial):
         low = partial.astype(bf16)
-        total = partial[:rows]
+        total = partial[:rows].astype(f32)
         for j in range(1, ranks):
             total = total + around(low[j * rows : (j + 1) * rows], "tensor", j).astype(f32)
         return total
@@ -265,28 +424,41 @@
     )
     vector_sizes = [width, width, local_q, 2 * head, width, width, width, local_f, width]
 
-    shard_qkv = jnp.concatenate([query_weight[0], keyval_weight[0]], axis=1)
-    shard_rest = jnp.concatenate(
-        [output_weight[0].T, upward_weight[0], downward_weight[0].T], axis=1
+    both = ("section", "dp")
+    shard_early = jnp.concatenate(
+        [query_weight[0], keyval_weight[0], output_weight[0].T], axis=1
     )
-    qkv_layers = by_layer(shard_qkv, swap(shard_qkv))
+
+    def mask_flip(block, mask):
+        return lax.ppermute(block, both, [(i, i ^ mask) for i in range(2 * lax.axis_size("dp"))])
+
+    pair_near = jnp.stack([shard_early, mask_flip(shard_early, 2)])
+    pair_far = jnp.stack([mask_flip(shard_early, 16), mask_flip(shard_early, 18)])
+
+    def early_table(pair):
+        quad = jnp.concatenate([pair] + [mask_flip(pair, 4 * k) for k in range(1, 4)], axis=0)
+        table = by_rank(data, quad, mask_flip(quad, 1))
+        return table.reshape(width, -1)
+
+    early_tables = [early_table(pair) for pair in by_layer(pair_near, pair_far)]
     vector_layers = by_layer(vectors, swap(vectors))
     early_layers = by_layer(early_pack(own_bank), swap(early_pack(other_bank)))
-    rest_layers = by_layer(shard_rest, swap(shard_rest))
     late_layers = by_layer(late_pack(own_bank), swap(late_pack(other_bank)))
-
-    def gather(shard):
-        return lax.all_gather(shard, "dp", axis=0, tiled=True)
-
-    first = gather(qkv_layers[0])
-    second_shard = jnp.concatenate(
-        [rest_layers[0], qkv_layers[1], rest_layers[1][:, :local_q]], axis=1
-    )
-    first, second_shard = lax.optimization_barrier((first, second_shard))
-    middle_all = gather(second_shard)
-    third_shard = rest_layers[1][:, local_q:]
-    middle_all, third_shard = lax.optimization_barrier((middle_all, third_shard))
-    last_all = gather(third_shard)
+    half = local_f // 2
+    shard_up = upward_weight[0]
+    shard_down = downward_weight[0].T
+    halves = [
+        jnp.concatenate(
+            [shard_up[:, h * half : (h + 1) * half], shard_down[:, h * half : (h + 1) * half]],
+            axis=1,
+        )
+        for h in range(2)
+    ]
+    keep = jnp.where(low_section, halves[0], halves[1])
+    gained = swap(jnp.where(low_section, halves[1], halves[0]))
+    feed_zero, feed_one = by_layer(keep, gained)
+    feed_zero = lax.all_gather(feed_zero, both, axis=0, tiled=True)
+    feed_one = lax.all_gather(feed_one, both, axis=0, tiled=True)
 
     def split(table, sizes):
         cuts = [0]
@@ -295,13 +467,9 @@
         return [table[:, a:b] for a, b in zip(cuts[:-1], cuts[1:])]
 
     wide = local_q + 2 * head
-    out_zero, up_zero, down_zero, qkv_one, out_one = split(
-        middle_all, [local_q, local_f, local_f, wide, local_q]
-    )
-    up_one, down_one = split(last_all, [local_f, local_f])
     weights = [
-        (first, out_zero, up_zero, down_zero),
-        (qkv_one, out_one, up_one, down_one),
+        split(early_tables[layer], [wide, local_q]) + [table]
+        for layer, table in enumerate([feed_zero, feed_one])
     ]
     small = [
         [part.astype(f32) for part in split(vector_layers[layer], vector_sizes)]
@@ -333,7 +501,7 @@
     bias = jnp.where(allowed, 0.0, masked_score).astype(bf16)
 
     def forward(layer, hidden):
-        qkv_w, out_w, up_w, down_w = weights[layer]
+        qkv_w, out_w, feed_w = weights[layer]
         gain1, shift1, q_bias, kv_bias, out_bias, gain2, shift2, up_bias, down_bias = small[layer]
         sq, skv, eq, ekv, so, eo, su, eu, sd, ed = adapters[layer]
         unit1, rsd1 = norm_parts(hidden)
@@ -351,13 +519,8 @@
         middle = hidden + (attended + out_bias)
         unit2, rsd2 = norm_parts(middle)
         second = spread((unit2 * gain2 + shift2).astype(bf16))
-        low_u = against(second, su).astype(bf16)
-        upward = plain(second, up_w) + up_bias + plain(low_u, eu)
-        active, slope = gelu_parts(upward)
-        active = active.astype(bf16)
-        slope = slope.astype(bf16)
-        low_d = against(active, sd).astype(bf16)
-        result = middle + (reduce_rows(against(active, down_w) + plain(low_d, ed)) + down_bias)
+        active, slope, low_u, low_d, partial = feed(second, feed_w, up_bias, eu, sd, su, ed)
+        result = middle + (reduce_rows(partial) + down_bias)
         kept = (
             unit1,
             rsd1,
@@ -411,6 +574,38 @@
             for r in range(4)
         )
         return total.astype(bf16)
+
+    def to_upper(value):
+        return lax.ppermute(value, "section", [(0, 1)])
+
+    def to_lower(value):
+        return lax.ppermute(value, "section", [(1, 0)])
+
+    def offloaded_grads(shared, owned):
+        pile = jnp.concatenate([tiles(part) for part in shared], axis=0).astype(bf16)
+        lack = -pile.shape[0] % ranks
+        pile = jnp.concatenate([pile, jnp.zeros((lack,) + pile.shape[1:], bf16)], axis=0)
+        mine = lax.psum_scatter(pile, "tensor", scatter_dimension=0, tiled=True)
+        pile = jnp.concatenate([mine] + [tiles(part).astype(bf16) for part in owned], axis=0)
+        lack = -pile.shape[0] % lax.axis_size("dp")
+        pile = jnp.concatenate([pile, jnp.zeros((lack,) + pile.shape[1:], bf16)], axis=0)
+        mine = lax.psum_scatter(pile, "dp", scatter_dimension=0, tiled=True)
+        pair = jnp.stack([to_upper(mine), mine], axis=1)
+        pile = lax.all_gather(pair, "dp", axis=0, tiled=True)
+        shared_sizes = [part.shape[1] for part in shared]
+        each = -(-(sum(shared_sizes) // 128) // ranks)
+        ordered = lax.all_gather(pile[:each], "tensor", axis=0, tiled=True)
+        results, begin = [], 0
+        for size in shared_sizes:
+            count = size // 128
+            results.append([flat(ordered[begin : begin + count, m]) for m in range(2)])
+            begin += count
+        begin, others = each, []
+        for part in owned:
+            count = part.shape[1] // 128
+            others.append([flat(pile[begin : begin + count, m]) for m in range(2)])
+            begin += count
+        return results + others
 
     def spread_grads(mine, shared_sizes, owned_sizes):
         shared_count = sum(shared_sizes) // 128
@@ -445,15 +640,13 @@
         return results, owned
 
     def backward_feed(layer, kept, grad):
-        up_w, down_w = weights[layer][2:]
+        feed_w = weights[layer][2]
         gain2 = small[layer][5]
-        so, eo, su, eu, sd, ed = adapters[layer][4:]
+        su, eu, sd, ed = adapters[layer][6:]
         unit2, rsd2, second, low_u, active, slope, low_d = kept[10:]
         branch = spread(grad.astype(bf16))
-        inner_d = against(branch, ed).astype(bf16)
-        grad_up = ((plain(branch, down_w) + plain(inner_d, sd)) * slope.astype(f32)).astype(bf16)
-        inner_u = against(grad_up, eu).astype(bf16)
-        grad_second = reduce_rows(against(grad_up, up_w) + plain(inner_u, su))
+        grad_up, inner_d, inner_u, partial = feed_back(branch, feed_w, slope, eu, sd, su, ed)
+        grad_second = reduce_rows(partial)
         grad_middle = grad + norm_back(unit2, rsd2, grad_second * gain2)
         shared = [across(inner_u, second), across(low_d, branch)]
         owned = [across(low_u, grad_up), across(inner_d, active)]
@@ -467,7 +660,7 @@
         branch = spread(grad_middle.astype(bf16))
         inner_o = against(branch, eo).astype(bf16)
         grad_mixed = (plain(branch, out_w) + plain(inner_o, so)).astype(bf16)
-        grad_q, grad_block = attend_back(grad_mixed, probs, queries, mixed, key_block, head)
+        grad_q, grad_block = attend_back(grad_mixed, probs, queries, key_block, head)
         own = grad_block[reach * span :].astype(f32)
         for back in range(1, reach + 1):
             begin = (reach - back) * span
@@ -487,12 +680,6 @@
         owned = [across(low_q, grad_q)]
         return grad_hidden, out_grads, (shared, owned)
 
-    def to_upper(value):
-        return lax.ppermute(value, "section", [(0, 1)])
-
-    def to_lower(value):
-        return lax.ppermute(value, "section", [(1, 0)])
-
     fresh = lax.dynamic_index_in_dim(block_input, section, 0, keepdims=False).astype(f32)
     result_zero, kept_zero = forward(0, fresh)
     passed = result_zero.astype(bf16)
@@ -502,12 +689,21 @@
     given = lax.dynamic_index_in_dim(cotangent, section, 0, keepdims=False).astype(f32)
     grad_middle_one, feed_shared, feed_owned = backward_feed(1, kept_one, given)
     grad_one, out_one_grads, qkv_one_grads = backward_attend(1, kept_one, grad_middle_one)
-    late_one = reduce_grads(feed_shared + out_one_grads[0], feed_owned + out_one_grads[1])
-    early_one = reduce_grads(*qkv_one_grads)
+    grads_one = offloaded_grads(
+        feed_shared + out_one_grads[0] + qkv_one_grads[0],
+        feed_owned + out_one_grads[1] + qkv_one_grads[1],
+    )
     grad_middle_zero, feed_shared, feed_owned = backward_feed(0, kept_zero, grad_one)
     grad_zero, out_zero_grads, qkv_zero_grads = backward_attend(0, kept_zero, grad_middle_zero)
-    late_zero = reduce_grads(feed_shared + out_zero_grads[0], feed_owned + out_zero_grads[1])
-    early_zero = reduce_grads(*qkv_zero_grads)
+    shared = feed_shared + out_zero_grads[0] + qkv_zero_grads[0]
+    owned = feed_owned + out_zero_grads[1] + qkv_zero_grads[1]
+    mine = reduce_grads(shared, owned)
+    grads_zero = spread_grads(
+        jnp.stack([mine, to_lower(mine)]),
+        [part.shape[1] for part in shared],
+        [part.shape[1] for part in owned],
+    )
+    grads_zero = grads_zero[0] + grads_zero[1]
 
     def both_micros(zero, one):
         received = jnp.where(low_section, to_lower(zero), to_upper(one))
@@ -525,12 +721,6 @@
         low_section, jnp.stack([own, received]), jnp.stack([received, own])
     )
 
-    late_shared, late_owned = spread_grads(
-        both_micros(late_zero, late_one), [width, width, width], [local_f, local_f, local_q]
-    )
-    early_shared, early_owned = spread_grads(
-        both_micros(early_zero, early_one), [width, width, 2 * head], [local_q]
-    )
     onehot = (bank_choice[:, None] == jnp.arange(banks)[None, :]).astype(f32)
 
     def placed(pair, transpose):
@@ -539,10 +729,21 @@
         )
         return (out.transpose(0, 2, 1) if transpose else out)[None]
 
-    up_shrink_grad, down_expand_grad, out_expand_grad = late_shared
-    up_expand_grad, down_shrink_grad, out_shrink_grad = late_owned
-    q_shrink_grad, kv_shrink_grad, kv_expand_grad = early_shared
-    (q_expand_grad,) = early_owned
+    (
+        up_shrink_grad,
+        down_expand_grad,
+        out_expand_grad,
+        q_shrink_grad,
+        kv_shrink_grad,
+        kv_expand_grad,
+        up_expand_grad,
+        down_shrink_grad,
+        out_shrink_grad,
+        q_expand_grad,
+    ) = [
+        [jnp.where(low_section, zero[m], one[m]) for m in range(2)]
+        for zero, one in zip(grads_zero, grads_one)
+    ]
     return (
         section_outputs[None],
         input_grads[None],

time: 772 us -> 717 us (0.929)
  matrix products: 111 us -> 39.2 us
  Pallas kernels: 17 us -> 81.8 us
  starting transfers between devices: 229 us -> 169 us
  waiting for transfers between devices: 320 us -> 281 us
  blocking collectives: 0 us -> 31.8 us
  other arithmetic: 32.3 us -> 45.2 us
  local copies, waits for them, and re-layouts: 30.7 us -> 39.8 us
    all_gather x3 -> x2, waiting for transfers between devices: 140 us -> 0.04 us  [the longest x1 0.02 us: per_device(): feed_zero = lax.all_gather(feed_zero, both, axis=0, tiled=True)]
    ppermute x0 -> x11, waiting for transfers between devices: none -> 103 us  [mask_flip(): lax.ppermute(block, both, [(i, i ^ mask) for i in range(2 * lax.axis_size...]
    pallas_call x0 -> x6, Pallas kernels: none -> 62.9 us  [the longest x2 24.9 us: feed(): pl.pallas_call(feed_kernel, in_specs=[held, pl.BlockSpec(memory_space=pl....]
    ppermute x78 -> x57, starting transfers between devices: 132 us -> 78.7 us  [around(): lax.ppermute(block, axis, [(i, (i + distance) % size) for i in range(size)])]
    dot_general x28 -> x16, matrix products: 54.1 us -> 14.8 us  [plain(): return jnp.dot(left, right, preferred_element_type=f32)]
    dot_general x30 -> x18, matrix products: 48.3 us -> 14.9 us  [against(): lax.dot_general(left, right, (((1,), (1,)), ((), ())), preferred_element_...]
    all_gather x0 -> x2, blocking collectives: none -> 31.8 us  [the longest x1 17.8 us: offloaded_grads(): pile = lax.all_gather(pair, 'dp', axis=0, tiled=True)]
    reduce_scatter x0 -> x2, waiting for transfers between devices: none -> 23 us  [the longest x1 23 us: offloaded_grads(): mine = lax.psum_scatter(pile, 'dp', scatter_dimension=0, tiled=True)]
  transfers between devices with their start and end apart: 120 -> 101, of which waited for: 57 -> 52; matrix products, arithmetic and copies ran while one was open for 19% -> 14% of each run, Pallas kernels for 2% -> 12%
where the time goes in v2:
time: 717 us; the launch traced here: 708 us
  waiting for transfers between devices  281 us (39%)
  starting transfers between devices  169 us (24%)
  Pallas kernels  81.8 us (11%)
  other arithmetic  45.2 us (6%)
  local copies, waits for them, and re-layouts  39.8 us (6%)
  matrix products  39.2 us (5%)
  blocking collectives  31.8 us (4%)
  between operations  20.5 us (3%)
    ppermute x57, waiting for transfers between devices, around(): lax.ppermute(block, axis, [(i, (i + distance) % size) for i in range(size)])  125 us
    ppermute x11, waiting for transfers between devices, mask_flip(): lax.ppermute(block, both, [(i, i ^ mask) for i in range(2 * lax.axis_size...  103 us
    ppermute x57, starting transfers between devices, around(): lax.ppermute(block, axis, [(i, (i + distance) % size) for i in range(size)])  78.7 us
    ppermute x16, starting transfers between devices, along(): return lax.ppermute(block, axis, route)  42.6 us
    pallas_call x2, Pallas kernels, feed(): pl.pallas_call(feed_kernel, in_specs=[held, pl.BlockSpec(memory_space=pl....  24.9 us
    unnamed x294, local copies, waits for them, and re-layouts  24.5 us
    pallas_call x2, Pallas kernels, feed_back(): pl.pallas_call(feed_back_kernel, in_specs=[held, pl.BlockSpec(memory_spac...  23.2 us
    reduce_scatter x1, waiting for transfers between devices, offloaded_grads(): mine = lax.psum_scatter(pile, 'dp', scatter_dimension=0, tiled=True)  23 us
  transfers between devices with their start and end apart: 101, of which 52 were waited for; matrix products, arithmetic and copies ran while one was open for 14% of the time, Pallas kernels for 12%

profile of v2, /device:TPU:0, one launch (start us, length us, event | category | flops | bytes accessed | tf_op | source)
XLA Modules:
  0.0 708.0 jit_solution(16887263411227585592)
XLA Ops:
  9.9 4.0 collective-permute-start.23
  14.0 11.9 %collective-permute-done.23 = bf16[128,2048]{1,0:T(8,128)(2,1)S(1)} collective-permute-done((bf16[128,2048]{1,0:T(8,128)(2,1)S(1)}, bf16[128,2048]{1,0:T(8,128)(2,1)S(1)}, u32[]{:S(2)}, u32[]{:S(2)}) %collective-permute-start.23) | collective-permute-done | bytes 524320 | tf_op jit(solution)/shard_map/ppermute | solution.py:363
  53.9 7.8 %collective-permute-done = bf16[1,15104]{1,0:T(2,128)(2,1)S(1)} collective-permute-done((bf16[1,15104]{1,0:T(2,128)(2,1)S(1)}, bf16[1,15104]{1,0:T(2,128)(2,1)S(1)}, u32[]{:S(2)}, u32[]{:S(2)}) %collective-permute-start) | collective-permute-done | bytes 30240 | tf_op jit(solution)/shard_map/ppermute | solution.py:363
  79.5 13.4 %collective-permute-done.9 = bf16[2,128,1280]{2,1,0:T(8,128)(2,1)S(1)} collective-permute-done((bf16[2,128,1280]{2,1,0:T(8,128)(2,1)S(1)}, bf16[2,128,1280]{2,1,0:T(8,128)(2,1)S(1)}, u32[]{:S(2)}, u32[]{:S(2)}) %collective-permute-start.9) | collective-permute-done | bytes 655392 | tf_op jit(solution)/shard_map/ppermute | solution.py:433
  92.9 11.8 %collective-permute-done.8 = bf16[2,128,1280]{2,1,0:T(8,128)(2,1)S(1)} collective-permute-done((bf16[2,128,1280]{2,1,0:T(8,128)(2,1)S(1)}, bf16[2,128,1280]{2,1,0:T(8,128)(2,1)S(1)}, u32[]{:S(2)}, u32[]{:S(2)}) %collective-permute-start.8) | collective-permute-done | bytes 655392 | tf_op jit(solution)/shard_map/ppermute | solution.py:433
  104.8 24.5 %collective-permute-done.7 = bf16[2,128,1280]{2,1,0:T(8,128)(2,1)S(1)} collective-permute-done((bf16[2,128,1280]{2,1,0:T(8,128)(2,1)S(1)}, bf16[2,128,1280]{2,1,0:T(8,128)(2,1)S(1)}, u32[]{:S(2)}, u32[]{:S(2)}) %collective-permute-start.7) | collective-permute-done | bytes 655392 | tf_op jit(solution)/shard_map/ppermute | solution.py:433
  132.6 3.6 collective-permute-done.10.other_ref
  137.8 7.4 %place.2 = bf16[8,2,128,1280]{3,2,1,0:T(8,128)(2,1)} custom-call(s32[1]{0:T(128)} %bitcast.3.rank_ref, bf16[8,128,1280]{2,1,0:T(8,128)(2,1)} %copy-done.41, bf16[8,128,1280]{2,1,0:T(8,128)(2,1)} %copy-done.45), custom_call_target="tpu_custom_call" | custom-call | tf_op jit(solution)/shard_map/place/pallas_call | solution.py:303
  148.4 4.2 collective-permute-start.12
  153.8 3.6 collective-permute-start.14
  158.9 13.6 %collective-permute-start.15 = (bf16[256,256]{1,0:T(8,128)(2,1)S(1)}, bf16[256,256]{1,0:T(8,128)(2,1)S(1)}, u32[]{:S(2)}, u32[]{:S(2)}) collective-permute-start(bf16[256,256]{1,0:T(8,128)(2,1)S(1)} %fusion.100), channel_id=1, source_target_pairs={{0,4},{4,8},{8,12},{12,16},{16,20},{20,24},{24,28},{28,32},{32,36}... | collective-permute-start | bytes 393224 | tf_op jit(solution)/shard_map/ppermute | solution.py:37
  172.6 4.3 attend.2
  184.4 6.6 collective-permute-done.19
  191.0 13.1 %collective-permute-start.31 = (bf16[2,128,1280]{2,1,0:T(8,128)(2,1)}, bf16[2,128,1280]{2,1,0:T(8,128)(2,1)S(1)}, u32[]{:S(2)}, u32[]{:S(2)}) collective-permute-start(bf16[2,128,1280]{2,1,0:T(8,128)(2,1)} %get-tuple-element.94), channel_id=1, source_target_pairs={{0,32},{4,36},{8,40},{12,44},{16,48},{20,52},{24,56},{28,60},{32,0... | collective-permute-start | bytes 1966088 | tf_op jit(solution)/shard_map/ppermute | solution.py:433
  204.8 5.3 collective-permute-start.22
  211.0 22.8 %collective-permute-done.31 = bf16[2,128,1280]{2,1,0:T(8,128)(2,1)S(1)} collective-permute-done((bf16[2,128,1280]{2,1,0:T(8,128)(2,1)}, bf16[2,128,1280]{2,1,0:T(8,128)(2,1)S(1)}, u32[]{:S(2)}, u32[]{:S(2)}) %collective-permute-start.31) | collective-permute-done | bytes 655392 | tf_op jit(solution)/shard_map/ppermute | solution.py:433
  234.4 26.3 %collective-permute-done.30 = bf16[2,128,1280]{2,1,0:T(8,128)(2,1)S(1)} collective-permute-done((bf16[2,128,1280]{2,1,0:T(8,128)(2,1)}, bf16[2,128,1280]{2,1,0:T(8,128)(2,1)S(1)}, u32[]{:S(2)}, u32[]{:S(2)}) %collective-permute-start.30) | collective-permute-done | bytes 655392 | tf_op jit(solution)/shard_map/ppermute | solution.py:433
  263.7 12.5 %feed.2 = (bf16[256,2048]{1,0:T(8,128)(2,1)S(1)}, bf16[256,2048]{1,0:T(8,128)(2,1)S(1)}, bf16[256,16]{1,0:T(8,128)(2,1)S(1)}, bf16[256,16]{1,0:T(8,128)(2,1)S(1)}, bf16[256,2048]{1,0:T(8,128)(2,1)S(1)}) custom-call(bf16[256,2048]{1,0:T(8,128)(2,1)S(1)} %pad_maximum_fusion.3.second_ref, bf16[4096,2048]{1,0:T(8,128)(2,1)} %all-gather.3.cloned.1.call-done.table_ref, ...), custom_call_target="tpu_custom_call" | custom-call | flops 4294967296 | bytes 20971520 | tf_op jit(solution)/shard_map/feed/pallas_call | solution.py:216
  277.4 6.7 collective-permute-start.25
  284.7 4.4 collective-permute-done.26
  291.2 5.1 collective-permute-done.24
  306.0 7.3 %place.3 = bf16[8,2,128,1280]{3,2,1,0:T(8,128)(2,1)} custom-call(s32[1]{0:T(128)} %bitcast.3.rank_ref, bf16[8,128,1280]{2,1,0:T(8,128)(2,1)} %pad_maximum_fusion.1.mine_ref, bf16[8,128,1280]{2,1,0:T(8,128)(2,1)} %collective-permute-done.33.other_ref), custom_call_target="tpu_custom_call" | custom-call | tf_op jit(solution)/shard_map/place/pallas_call | solution.py:303
  313.4 7.1 collective-permute-done.29
  324.1 4.3 collective-permute-start.34
  335.8 4.3 attend.3
  340.9 4.9 fusion.210
  346.7 4.1 collective-permute-start.39
  355.3 6.4 collective-permute-done.38
  369.1 9.5 %collective-permute-done.43 = bf16[64,2048]{1,0:T(8,128)(2,1)S(1)} collective-permute-done((bf16[64,2048]{1,0:T(8,128)(2,1)S(1)}, bf16[64,2048]{1,0:T(8,128)(2,1)S(1)}, u32[]{:S(2)}, u32[]{:S(2)}) %collective-permute-start.43) | collective-permute-done | bytes 262176 | tf_op jit(solution)/shard_map/ppermute | solution.py:31
  383.0 12.4 %feed.3 = (bf16[256,2048]{1,0:T(8,128)(2,1)S(1)}, bf16[256,2048]{1,0:T(8,128)(2,1)S(1)}, bf16[256,16]{1,0:T(8,128)(2,1)S(1)}, bf16[256,16]{1,0:T(8,128)(2,1)S(1)}, bf16[256,2048]{1,0:T(8,128)(2,1)S(1)}) custom-call(bf16[256,2048]{1,0:T(8,128)(2,1)S(1)} %pad_maximum_fusion.5.second_ref, bf16[4096,2048]{1,0:T(8,128)(2,1)} %all-gather.5.cloned.1.call-done.table_ref, ...), custom_call_target="tpu_custom_call" | custom-call | flops 4294967296 | bytes 20971520 | tf_op jit(solution)/shard_map/feed/pallas_call | solution.py:216
  395.5 3.6 collective-permute-start.46
  399.1 11.6 %feed_back.2 = (bf16[256,2048]{1,0:T(8,128)(2,1)S(1)}, bf16[256,16]{1,0:T(8,128)(2,1)S(1)}, bf16[256,16]{1,0:T(8,128)(2,1)S(1)}, bf16[256,2048]{1,0:T(8,128)(2,1)S(1)}) custom-call(bf16[256,2048]{1,0:T(8,128)(2,1)S(1)} %pad_maximum_fusion.6.branch_ref, bf16[4096,2048]{1,0:T(8,128)(2,1)} %all-gather.5.cloned.1.call-done.table_ref, ...), custom_call_target="tpu_custom_call" | custom-call | flops 4294967296 | bytes 18874368 | tf_op jit(solution)/shard_map/feed_back/pallas_call | solution.py:273
  415.3 4.7 collective-permute-done.54
  433.3 4.3 collective-permute-done.44
  444.1 4.6 collective-permute-done.56
  452.6 5.1 attend_back.2
  473.6 6.1 collective-permute-done.64
  481.4 5.9 collective-permute-done.62
  495.3 4.7 collective-permute-start.82
  500.0 6.0 collective-permute-done.67
  509.4 11.6 %feed_back.3 = (bf16[256,2048]{1,0:T(8,128)(2,1)S(1)}, bf16[256,16]{1,0:T(8,128)(2,1)S(1)}, bf16[256,16]{1,0:T(8,128)(2,1)S(1)}, bf16[256,2048]{1,0:T(8,128)(2,1)S(1)}) custom-call(bf16[256,2048]{1,0:T(8,128)(2,1)S(1)} %pad_maximum_fusion.8.branch_ref, bf16[4096,2048]{1,0:T(8,128)(2,1)} %all-gather.3.cloned.1.call-done.table_ref, ...), custom_call_target="tpu_custom_call" | custom-call | flops 4294967296 | bytes 18874368 | tf_op jit(solution)/shard_map/feed_back/pallas_call | solution.py:273
  530.6 5.3 collective-permute-done.70
  546.1 10.6 %collective-permute-done.73 = bf16[64,2048]{1,0:T(8,128)(2,1)S(1)} collective-permute-done((bf16[64,2048]{1,0:T(8,128)(2,1)S(1)}, bf16[64,2048]{1,0:T(8,128)(2,1)S(1)}, u32[]{:S(2)}, u32[]{:S(2)}) %collective-permute-start.73) | collective-permute-done | bytes 262176 | tf_op jit(solution)/shard_map/ppermute | solution.py:31
  562.2 5.2 attend_back.3
  589.2 23.0 %reduce-scatter.5.cloned.1.call-done = bf16[4,16,128]{2,1,0:T(8,128)(2,1)} async-done(((bf16[64,16,128]{2,1,0:T(8,128)(2,1)}), bf16[4,16,128]{2,1,0:T(8,128)(2,1)}) %reduce-scatter.5.cloned.1.call-update) | async-done | bytes 16400 | tf_op jit(solution)/shard_map/reduce_scatter | solution.py:592
  612.2 4.6 collective-permute-start.96
  633.4 17.8 %all_gather.14 = bf16[64,2,16,128]{3,2,1,0:T(8,128)(2,1)S(1)} all-gather(bf16[4,2,16,128]{3,2,1,0:T(8,128)(2,1)S(1)} %copy.168), channel_id=1, replica_groups=mesh['section'=2,'dp'=16,'tensor'=4] {'dp'}, dimensions={0}, use_global_device_ids=true | all-gather | bytes 557056 | tf_op jit(solution)/shard_map/all_gather | solution.py:594
  668.2 13.9 %all_gather.15 = bf16[84,2,16,128]{3,2,1,0:T(8,128)(2,1)S(1)} all-gather(bf16[21,2,16,128]{3,2,1,0:T(8,128)(2,1)S(1)} %slice.659), channel_id=1, replica_groups=mesh['section'=2,'dp'=16,'tensor'=4] {'tensor'}, dimensions={0}, use_global_device_ids=true | all-gather | bytes 860160 | tf_op jit(solution)/shard_map/all_gather | solution.py:597
  (677 shorter events, 265.3 us)
Async XLA Ops:
  7.2 256.5 %all-gather.3.cloned.1.call-start = ((), (), s32[]{:S(2)}) async-start(), calls=%async_computation.2 | async-start | bytes 17301504 | tf_op jit(solution)/shard_map/all_gather | solution.py:460
  9.9 16.0 %collective-permute-start.23 = (bf16[128,2048]{1,0:T(8,128)(2,1)S(1)}, bf16[128,2048]{1,0:T(8,128)(2,1)S(1)}, u32[]{:S(2)}, u32[]{:S(2)}) collective-permute-start(bf16[128,2048]{1,0:T(8,128)(2,1)S(1)} %broadcast_select_fusion.4), channel_id=1, source_target_pairs={{0,64},{64,0},{1,65},{65,1},{2,66},{66,2},{3,67},{67,3},{4,68},{68... | collective-permute-start | bytes 1572872 | tf_op jit(solution)/shard_map/ppermute | solution.py:363
  27.2 352.4 %all-gather.5.cloned.1.call-start = ((), (), s32[]{:S(2)}) async-start(), calls=%async_computation.3 | async-start | bytes 17301504 | tf_op jit(solution)/shard_map/all_gather | solution.py:461
  28.0 501.0 %reduce-scatter.3.cloned.1.call-start = ((), (), s32[]{:S(2)}) async-start(), calls=%async_computation.4 | async-start | bytes 430080 | tf_op jit(solution)/shard_map/reduce_scatter | solution.py:588
  28.2 37.8 %collective-permute-start.6 = (bf16[128,1280]{1,0:T(8,128)(2,1)S(1)}, bf16[128,1280]{1,0:T(8,128)(2,1)}, u32[]{:S(2)}, u32[]{:S(2)}) collective-permute-start(bf16[128,1280]{1,0:T(8,128)(2,1)S(1)} %get-tuple-element.190), channel_id=1, source_target_pairs={{0,72},{4,76},{8,64},{12,68},{16,88},{20,92},{24,80},{28,84},{32,1... | collective-permute-start | bytes 983048 | tf_op jit(solution)/shard_map/ppermute | solution.py:433
  31.7 37.1 %collective-permute-start.5 = (bf16[128,1280]{1,0:T(8,128)(2,1)S(1)}, bf16[128,1280]{1,0:T(8,128)(2,1)}, u32[]{:S(2)}, u32[]{:S(2)}) collective-permute-start(bf16[128,1280]{1,0:T(8,128)(2,1)S(1)} %get-tuple-element.190), channel_id=1, source_target_pairs={{0,64},{4,68},{8,72},{12,76},{16,80},{20,84},{24,88},{28,92},{32,9... | collective-permute-start | bytes 983048 | tf_op jit(solution)/shard_map/ppermute | solution.py:433
  31.7 38.5 %collective-permute-start.4 = (bf16[128,1280]{1,0:T(8,128)(2,1)S(1)}, bf16[128,1280]{1,0:T(8,128)(2,1)}, u32[]{:S(2)}, u32[]{:S(2)}) collective-permute-start(bf16[128,1280]{1,0:T(8,128)(2,1)S(1)} %get-tuple-element.190), channel_id=1, source_target_pairs={{0,8},{4,12},{8,0},{12,4},{16,24},{20,28},{24,16},{28,20},{32,40},... | collective-permute-start | bytes 983048 | tf_op jit(solution)/shard_map/ppermute | solution.py:433
  32.9 28.8 %collective-permute-start = (bf16[1,15104]{1,0:T(2,128)(2,1)S(1)}, bf16[1,15104]{1,0:T(2,128)(2,1)S(1)}, u32[]{:S(2)}, u32[]{:S(2)}) collective-permute-start(bf16[1,15104]{1,0:T(2,128)(2,1)S(1)} %constant_dynamic-update-slice_fusion), channel_id=1, source_target_pairs={{0,64},{64,0},{1,65},{65,1},{2,66},{66,2},{3,67},{67,3},{4,68},{68... | collective-permute-start | bytes 90632 | tf_op jit(solution)/shard_map/ppermute | solution.py:363
  44.8 30.9 %collective-permute-start.11 = (bf16[16,4864]{1,0:T(8,128)(2,1)}, bf16[16,4864]{1,0:T(8,128)(2,1)}, u32[]{:S(2)}, u32[]{:S(2)}) collective-permute-start(bf16[16,4864]{1,0:T(8,128)(2,1)} %pad_maximum_fusion.19), channel_id=1, source_target_pairs={{0,64},{64,0},{1,65},{65,1},{2,66},{66,2},{3,67},{67,3},{4,68},{68... | collective-permute-start | bytes 466952 | tf_op jit(solution)/shard_map/ppermute | solution.py:363
  72.3 20.6 %collective-permute-start.9 = (bf16[2,128,1280]{2,1,0:T(8,128)(2,1)S(1)}, bf16[2,128,1280]{2,1,0:T(8,128)(2,1)S(1)}, u32[]{:S(2)}, u32[]{:S(2)}) collective-permute-start(bf16[2,128,1280]{2,1,0:T(8,128)(2,1)S(1)} %get-tuple-element.95), channel_id=1, source_target_pairs={{0,48},{4,52},{8,56},{12,60},{16,32},{20,36},{24,40},{28,44},{32,1... | collective-permute-start | bytes 1966088 | tf_op jit(solution)/shard_map/ppermute | solution.py:433
  75.6 29.1 %collective-permute-start.8 = (bf16[2,128,1280]{2,1,0:T(8,128)(2,1)S(1)}, bf16[2,128,1280]{2,1,0:T(8,128)(2,1)S(1)}, u32[]{:S(2)}, u32[]{:S(2)}) collective-permute-start(bf16[2,128,1280]{2,1,0:T(8,128)(2,1)S(1)} %get-tuple-element.95), channel_id=1, source_target_pairs={{0,32},{4,36},{8,40},{12,44},{16,48},{20,52},{24,56},{28,60},{32,0... | collective-permute-start | bytes 1966088 | tf_op jit(solution)/shard_map/ppermute | solution.py:433
  75.7 53.6 %collective-permute-start.7 = (bf16[2,128,1280]{2,1,0:T(8,128)(2,1)S(1)}, bf16[2,128,1280]{2,1,0:T(8,128)(2,1)S(1)}, u32[]{:S(2)}, u32[]{:S(2)}) collective-permute-start(bf16[2,128,1280]{2,1,0:T(8,128)(2,1)S(1)} %get-tuple-element.95), channel_id=1, source_target_pairs={{0,16},{4,20},{8,24},{12,28},{16,0},{20,4},{24,8},{28,12},{32,48},... | collective-permute-start | bytes 1966088 | tf_op jit(solution)/shard_map/ppermute | solution.py:433
  78.3 53.5 %collective-permute-start.16 = (bf16[16,10752]{1,0:T(8,128)(2,1)S(1)}, bf16[16,10752]{1,0:T(8,128)(2,1)S(1)}, u32[]{:S(2)}, u32[]{:S(2)}) collective-permute-start(bf16[16,10752]{1,0:T(8,128)(2,1)S(1)} %get-tuple-element.162), channel_id=1, source_target_pairs={{0,64},{64,0},{1,65},{65,1},{2,66},{66,2},{3,67},{67,3},{4,68},{68... | collective-permute-start | bytes 1032200 | tf_op jit(solution)/shard_map/ppermute | solution.py:363
  78.3 272.5 %collective-permute-start.51 = (bf16[64,2048]{1,0:T(8,128)(2,1)}, bf16[64,2048]{1,0:T(8,128)(2,1)}, u32[]{:S(2)}, u32[]{:S(2)}) collective-permute-start(bf16[64,2048]{1,0:T(8,128)(2,1)} %dynamic-slice_bitcast_fusion), channel_id=1, source_target_pairs={{0,1},{1,2},{2,3},{3,0},{4,5},{5,6},{6,7},{7,4},{8,9},{9,10},{10,1... | collective-permute-start | bytes 786440 | tf_op jit(solution)/shard_map/ppermute | solution.py:31
  131.5 78.6 %collective-permute-start.32 = (bf16[2,128,1280]{2,1,0:T(8,128)(2,1)}, bf16[2,128,1280]{2,1,0:T(8,128)(2,1)}, u32[]{:S(2)}, u32[]{:S(2)}) collective-permute-start(bf16[2,128,1280]{2,1,0:T(8,128)(2,1)} %get-tuple-element.94), channel_id=1, source_target_pairs={{0,48},{4,52},{8,56},{12,60},{16,32},{20,36},{24,40},{28,44},{32,1... | collective-permute-start | bytes 1966088 | tf_op jit(solution)/shard_map/ppermute | solution.py:433
  152.5 20.0 %collective-permute-start.13 = (bf16[256,256]{1,0:T(8,128)(2,1)S(1)}, bf16[256,256]{1,0:T(8,128)(2,1)S(1)}, u32[]{:S(2)}, u32[]{:S(2)}) collective-permute-start(bf16[256,256]{1,0:T(8,128)(2,1)S(1)} %fusion.100), channel_id=1, source_target_pairs={{0,12},{4,16},{8,20},{12,24},{16,28},{20,32},{24,36},{28,40},{32,4... | collective-permute-start | bytes 393224 | tf_op jit(solution)/shard_map/ppermute | solution.py:37
  153.8 18.7 %collective-permute-start.14 = (bf16[256,256]{1,0:T(8,128)(2,1)S(1)}, bf16[256,256]{1,0:T(8,128)(2,1)S(1)}, u32[]{:S(2)}, u32[]{:S(2)}) collective-permute-start(bf16[256,256]{1,0:T(8,128)(2,1)S(1)} %fusion.100), channel_id=1, source_target_pairs={{0,8},{4,12},{8,16},{12,20},{16,24},{20,28},{24,32},{28,36},{32,40... | collective-permute-start | bytes 393224 | tf_op jit(solution)/shard_map/ppermute | solution.py:37
  181.8 22.2 %collective-permute-start.18 = (bf16[64,2048]{1,0:T(8,128)(2,1)S(1)}, bf16[64,2048]{1,0:T(8,128)(2,1)S(1)}, u32[]{:S(2)}, u32[]{:S(2)}) collective-permute-start(bf16[64,2048]{1,0:T(8,128)(2,1)S(1)} %get-tuple-element.119), channel_id=1, source_target_pairs={{0,2},{1,3},{2,0},{3,1},{4,6},{5,7},{6,4},{7,5},{8,10},{9,11},{10,... | collective-permute-start | bytes 786440 | tf_op jit(solution)/shard_map/ppermute | solution.py:31
  184.3 19.8 %collective-permute-start.17 = (bf16[64,2048]{1,0:T(8,128)(2,1)S(1)}, bf16[64,2048]{1,0:T(8,128)(2,1)S(1)}, u32[]{:S(2)}, u32[]{:S(2)}) collective-permute-start(bf16[64,2048]{1,0:T(8,128)(2,1)S(1)} %get-tuple-element.117), channel_id=1, source_target_pairs={{0,1},{1,2},{2,3},{3,0},{4,5},{5,6},{6,7},{7,4},{8,9},{9,10},{10,1... | collective-permute-start | bytes 786440 | tf_op jit(solution)/shard_map/ppermute | solution.py:31
  191.0 42.9 %collective-permute-start.31 = (bf16[2,128,1280]{2,1,0:T(8,128)(2,1)}, bf16[2,128,1280]{2,1,0:T(8,128)(2,1)S(1)}, u32[]{:S(2)}, u32[]{:S(2)}) collective-permute-start(bf16[2,128,1280]{2,1,0:T(8,128)(2,1)} %get-tuple-element.94), channel_id=1, source_target_pairs={{0,32},{4,36},{8,40},{12,44},{16,48},{20,52},{24,56},{28,60},{32,0... | collective-permute-start | bytes 1966088 | tf_op jit(solution)/shard_map/ppermute | solution.py:433
  204.1 56.6 %collective-permute-start.30 = (bf16[2,128,1280]{2,1,0:T(8,128)(2,1)}, bf16[2,128,1280]{2,1,0:T(8,128)(2,1)S(1)}, u32[]{:S(2)}, u32[]{:S(2)}) collective-permute-start(bf16[2,128,1280]{2,1,0:T(8,128)(2,1)} %get-tuple-element.94), channel_id=1, source_target_pairs={{0,16},{4,20},{8,24},{12,28},{16,0},{20,4},{24,8},{28,12},{32,48},... | collective-permute-start | bytes 1966088 | tf_op jit(solution)/shard_map/ppermute | solution.py:433
  204.8 58.8 %collective-permute-start.22 = (bf16[64,2048]{1,0:T(8,128)(2,1)S(1)}, bf16[64,2048]{1,0:T(8,128)(2,1)S(1)}, u32[]{:S(2)}, u32[]{:S(2)}) collective-permute-start(bf16[64,2048]{1,0:T(8,128)(2,1)S(1)} %add_convert_fusion.3), channel_id=1, source_target_pairs={{0,1},{1,2},{2,3},{3,0},{4,5},{5,6},{6,7},{7,4},{8,9},{9,10},{10,1... | collective-permute-start | bytes 786440 | tf_op jit(solution)/shard_map/ppermute | solution.py:31
  210.1 53.5 %collective-permute-start.21 = (bf16[64,2048]{1,0:T(8,128)(2,1)S(1)}, bf16[64,2048]{1,0:T(8,128)(2,1)S(1)}, u32[]{:S(2)}, u32[]{:S(2)}) collective-permute-start(bf16[64,2048]{1,0:T(8,128)(2,1)S(1)} %add_convert_fusion.3), channel_id=1, source_target_pairs={{0,2},{1,3},{2,0},{3,1},{4,6},{5,7},{6,4},{7,5},{8,10},{9,11},{10,... | collective-permute-start | bytes 786440 | tf_op jit(solution)/shard_map/ppermute | solution.py:31
  233.9 29.7 %collective-permute-start.20 = (bf16[64,2048]{1,0:T(8,128)(2,1)S(1)}, bf16[64,2048]{1,0:T(8,128)(2,1)S(1)}, u32[]{:S(2)}, u32[]{:S(2)}) collective-permute-start(bf16[64,2048]{1,0:T(8,128)(2,1)S(1)} %add_convert_fusion.3), channel_id=1, source_target_pairs={{0,3},{1,0},{2,1},{3,2},{4,7},{5,4},{6,5},{7,6},{8,11},{9,8},{10,9... | collective-permute-start | bytes 786440 | tf_op jit(solution)/shard_map/ppermute | solution.py:31
  263.5 40.8 %collective-permute-start.33 = (bf16[8,128,1280]{2,1,0:T(8,128)(2,1)}, bf16[8,128,1280]{2,1,0:T(8,128)(2,1)}, u32[]{:S(2)}, u32[]{:S(2)}) collective-permute-start(bf16[8,128,1280]{2,1,0:T(8,128)(2,1)} %pad_maximum_fusion.1.mine_ref), channel_id=1, source_target_pairs={{0,4},{4,0},{8,12},{12,8},{16,20},{20,16},{24,28},{28,24},{32,36},... | collective-permute-start | bytes 7864328 | tf_op jit(solution)/shard_map/ppermute | solution.py:433
  299.7 20.7 %collective-permute-start.29 = (bf16[64,2048]{1,0:T(8,128)(2,1)S(1)}, bf16[64,2048]{1,0:T(8,128)(2,1)S(1)}, u32[]{:S(2)}, u32[]{:S(2)}) collective-permute-start(bf16[64,2048]{1,0:T(8,128)(2,1)S(1)} %fusion.68), channel_id=1, source_target_pairs={{0,1},{1,2},{2,3},{3,0},{4,5},{5,6},{6,7},{7,4},{8,9},{9,10},{10,1... | collective-permute-start | bytes 786440 | tf_op jit(solution)/shard_map/ppermute | solution.py:31
  301.5 18.9 %collective-permute-start.28 = (bf16[64,2048]{1,0:T(8,128)(2,1)S(1)}, bf16[64,2048]{1,0:T(8,128)(2,1)S(1)}, u32[]{:S(2)}, u32[]{:S(2)}) collective-permute-start(bf16[64,2048]{1,0:T(8,128)(2,1)S(1)} %fusion.68), channel_id=1, source_target_pairs={{0,2},{1,3},{2,0},{3,1},{4,6},{5,7},{6,4},{7,5},{8,10},{9,11},{10,... | collective-permute-start | bytes 786440 | tf_op jit(solution)/shard_map/ppermute | solution.py:31
  302.1 18.3 %collective-permute-start.27 = (bf16[64,2048]{1,0:T(8,128)(2,1)S(1)}, bf16[64,2048]{1,0:T(8,128)(2,1)S(1)}, u32[]{:S(2)}, u32[]{:S(2)}) collective-permute-start(bf16[64,2048]{1,0:T(8,128)(2,1)S(1)} %fusion.68), channel_id=1, source_target_pairs={{0,3},{1,0},{2,1},{3,2},{4,7},{5,4},{6,5},{7,6},{8,11},{9,8},{10,9... | collective-permute-start | bytes 786440 | tf_op jit(solution)/shard_map/ppermute | solution.py:31
  304.3 47.0 %collective-permute-start.50 = (bf16[64,2048]{1,0:T(8,128)(2,1)}, bf16[64,2048]{1,0:T(8,128)(2,1)}, u32[]{:S(2)}, u32[]{:S(2)}) collective-permute-start(bf16[64,2048]{1,0:T(8,128)(2,1)} %dynamic-slice_bitcast_fusion), channel_id=1, source_target_pairs={{0,2},{1,3},{2,0},{3,1},{4,6},{5,7},{6,4},{7,5},{8,10},{9,11},{10,... | collective-permute-start | bytes 786440 | tf_op jit(solution)/shard_map/ppermute | solution.py:31
  320.4 30.9 %collective-permute-start.49 = (bf16[64,2048]{1,0:T(8,128)(2,1)}, bf16[64,2048]{1,0:T(8,128)(2,1)}, u32[]{:S(2)}, u32[]{:S(2)}) collective-permute-start(bf16[64,2048]{1,0:T(8,128)(2,1)} %dynamic-slice_bitcast_fusion), channel_id=1, source_target_pairs={{0,3},{1,0},{2,1},{3,2},{4,7},{5,4},{6,5},{7,6},{8,11},{9,8},{10,9... | collective-permute-start | bytes 786440 | tf_op jit(solution)/shard_map/ppermute | solution.py:31
  367.8 94.8 %collective-permute-start.47 = (bf16[64,2048]{1,0:T(8,128)(2,1)}, bf16[64,2048]{1,0:T(8,128)(2,1)}, u32[]{:S(2)}, u32[]{:S(2)}) collective-permute-start(bf16[64,2048]{1,0:T(8,128)(2,1)} %get-tuple-element.89), channel_id=1, source_target_pairs={{64,0},{65,1},{66,2},{67,3},{68,4},{69,5},{70,6},{71,7},{72,8},{73... | collective-permute-start | bytes 786440 | tf_op jit(solution)/shard_map/ppermute | solution.py:582
  395.5 32.7 %collective-permute-start.46 = (bf16[64,2048]{1,0:T(8,128)(2,1)S(1)}, bf16[64,2048]{1,0:T(8,128)(2,1)S(1)}, u32[]{:S(2)}, u32[]{:S(2)}) collective-permute-start(bf16[64,2048]{1,0:T(8,128)(2,1)S(1)} %get-tuple-element.109), channel_id=1, source_target_pairs={{0,3},{1,0},{2,1},{3,2},{4,7},{5,4},{6,5},{7,6},{8,11},{9,8},{10,9... | collective-permute-start | bytes 786440 | tf_op jit(solution)/shard_map/ppermute | solution.py:31
  411.6 15.8 %collective-permute-start.52 = (bf16[64,2048]{1,0:T(8,128)(2,1)S(1)}, bf16[64,2048]{1,0:T(8,128)(2,1)S(1)}, u32[]{:S(2)}, u32[]{:S(2)}) collective-permute-start(bf16[64,2048]{1,0:T(8,128)(2,1)S(1)} %get-tuple-element.105), channel_id=1, source_target_pairs={{0,1},{1,2},{2,3},{3,0},{4,5},{5,6},{6,7},{7,4},{8,9},{9,10},{10,1... | collective-permute-start | bytes 786440 | tf_op jit(solution)/shard_map/ppermute | solution.py:31
  421.7 15.9 %collective-permute-start.44 = (bf16[64,2048]{1,0:T(8,128)(2,1)S(1)}, bf16[64,2048]{1,0:T(8,128)(2,1)S(1)}, u32[]{:S(2)}, u32[]{:S(2)}) collective-permute-start(bf16[64,2048]{1,0:T(8,128)(2,1)S(1)} %get-tuple-element.108), channel_id=1, source_target_pairs={{0,1},{1,2},{2,3},{3,0},{4,5},{5,6},{6,7},{7,4},{8,9},{9,10},{10,1... | collective-permute-start | bytes 786440 | tf_op jit(solution)/shard_map/ppermute | solution.py:31
  428.1 16.0 %collective-permute-start.57 = (bf16[64,2048]{1,0:T(8,128)(2,1)S(1)}, bf16[64,2048]{1,0:T(8,128)(2,1)S(1)}, u32[]{:S(2)}, u32[]{:S(2)}) collective-permute-start(bf16[64,2048]{1,0:T(8,128)(2,1)S(1)} %get-tuple-element.81), channel_id=1, source_target_pairs={{0,1},{1,2},{2,3},{3,0},{4,5},{5,6},{6,7},{7,4},{8,9},{9,10},{10,1... | collective-permute-start | bytes 786440 | tf_op jit(solution)/shard_map/ppermute | solution.py:31
  428.2 20.5 %collective-permute-start.56 = (bf16[64,2048]{1,0:T(8,128)(2,1)S(1)}, bf16[64,2048]{1,0:T(8,128)(2,1)S(1)}, u32[]{:S(2)}, u32[]{:S(2)}) collective-permute-start(bf16[64,2048]{1,0:T(8,128)(2,1)S(1)} %get-tuple-element.81), channel_id=1, source_target_pairs={{0,2},{1,3},{2,0},{3,1},{4,6},{5,7},{6,4},{7,5},{8,10},{9,11},{10,... | collective-permute-start | bytes 786440 | tf_op jit(solution)/shard_map/ppermute | solution.py:31
  433.0 15.7 %collective-permute-start.55 = (bf16[64,2048]{1,0:T(8,128)(2,1)S(1)}, bf16[64,2048]{1,0:T(8,128)(2,1)S(1)}, u32[]{:S(2)}, u32[]{:S(2)}) collective-permute-start(bf16[64,2048]{1,0:T(8,128)(2,1)S(1)} %get-tuple-element.81), channel_id=1, source_target_pairs={{0,3},{1,0},{2,1},{3,2},{4,7},{5,4},{6,5},{7,6},{8,11},{9,8},{10,9... | collective-permute-start | bytes 786440 | tf_op jit(solution)/shard_map/ppermute | solution.py:31
  438.8 25.1 %collective-permute-start.48 = (bf16[64,2048]{1,0:T(8,128)(2,1)S(1)}, bf16[64,2048]{1,0:T(8,128)(2,1)S(1)}, u32[]{:S(2)}, u32[]{:S(2)}) collective-permute-start(bf16[64,2048]{1,0:T(8,128)(2,1)S(1)} %get-tuple-element.85), channel_id=1, source_target_pairs={{0,64},{1,65},{2,66},{3,67},{4,68},{5,69},{6,70},{7,71},{8,72},{9,... | collective-permute-start | bytes 786440 | tf_op jit(solution)/shard_map/ppermute | solution.py:579
  490.7 15.4 %collective-permute-start.67 = (bf16[64,2048]{1,0:T(8,128)(2,1)}, bf16[64,2048]{1,0:T(8,128)(2,1)S(1)}, u32[]{:S(2)}, u32[]{:S(2)}) collective-permute-start(bf16[64,2048]{1,0:T(8,128)(2,1)} %get-tuple-element.78), channel_id=1, source_target_pairs={{0,1},{1,2},{2,3},{3,0},{4,5},{5,6},{6,7},{7,4},{8,9},{9,10},{10,1... | collective-permute-start | bytes 786440 | tf_op jit(solution)/shard_map/ppermute | solution.py:31
  490.7 15.4 %collective-permute-start.66 = (bf16[64,2048]{1,0:T(8,128)(2,1)}, bf16[64,2048]{1,0:T(8,128)(2,1)S(1)}, u32[]{:S(2)}, u32[]{:S(2)}) collective-permute-start(bf16[64,2048]{1,0:T(8,128)(2,1)} %get-tuple-element.78), channel_id=1, source_target_pairs={{0,2},{1,3},{2,0},{3,1},{4,6},{5,7},{6,4},{7,5},{8,10},{9,11},{10,... | collective-permute-start | bytes 786440 | tf_op jit(solution)/shard_map/ppermute | solution.py:31
  495.3 116.9 %reduce-scatter.5.cloned.1.call-start = ((), (), s32[]{:S(2)}) async-start(), calls=%async_computation.5 | async-start | bytes 278528 | tf_op jit(solution)/shard_map/reduce_scatter | solution.py:592
  495.3 187.1 %collective-permute-start.82 = (bf16[64,2048]{1,0:T(8,128)(2,1)}, bf16[64,2048]{1,0:T(8,128)(2,1)}, u32[]{:S(2)}, u32[]{:S(2)}) collective-permute-start(bf16[64,2048]{1,0:T(8,128)(2,1)} %get-tuple-element.78), channel_id=1, source_target_pairs={{0,64},{1,65},{2,66},{3,67},{4,68},{5,69},{6,70},{7,71},{8,72},{9,... | collective-permute-start | bytes 786440 | tf_op jit(solution)/shard_map/ppermute | solution.py:579
  584.2 68.9 %collective-permute-start.80 = (bf16[64,2048]{1,0:T(8,128)(2,1)}, bf16[64,2048]{1,0:T(8,128)(2,1)}, u32[]{:S(2)}, u32[]{:S(2)}) collective-permute-start(bf16[64,2048]{1,0:T(8,128)(2,1)} %get-tuple-element.97), channel_id=1, source_target_pairs={{0,3},{1,0},{2,1},{3,2},{4,7},{5,4},{6,5},{7,6},{8,11},{9,8},{10,9... | collective-permute-start | bytes 786440 | tf_op jit(solution)/shard_map/ppermute | solution.py:31
  626.3 26.8 %collective-permute-start.79 = (bf16[64,2048]{1,0:T(8,128)(2,1)}, bf16[64,2048]{1,0:T(8,128)(2,1)S(1)}, u32[]{:S(2)}, u32[]{:S(2)}) collective-permute-start(bf16[64,2048]{1,0:T(8,128)(2,1)} %get-tuple-element.98), channel_id=1, source_target_pairs={{0,2},{1,3},{2,0},{3,1},{4,6},{5,7},{6,4},{7,5},{8,10},{9,11},{10,... | collective-permute-start | bytes 786440 | tf_op jit(solution)/shard_map/ppermute | solution.py:31
  627.5 25.6 %collective-permute-start.78 = (bf16[64,2048]{1,0:T(8,128)(2,1)}, bf16[64,2048]{1,0:T(8,128)(2,1)S(1)}, u32[]{:S(2)}, u32[]{:S(2)}) collective-permute-start(bf16[64,2048]{1,0:T(8,128)(2,1)} %get-tuple-element.96), channel_id=1, source_target_pairs={{0,1},{1,2},{2,3},{3,0},{4,5},{5,6},{6,7},{7,4},{8,9},{9,10},{10,1... | collective-permute-start | bytes 786440 | tf_op jit(solution)/shard_map/ppermute | solution.py:31
  633.3 17.9 %collective-permute-start.86 = (bf16[31,16,128]{2,1,0:T(8,128)(2,1)S(1)}, bf16[31,16,128]{2,1,0:T(8,128)(2,1)S(1)}, u32[]{:S(2)}, u32[]{:S(2)}) collective-permute-start(bf16[31,16,128]{2,1,0:T(8,128)(2,1)S(1)} %pad_dynamic-slice_fusion.4), channel_id=1, source_target_pairs={{0,4},{4,0},{8,12},{12,8},{16,20},{20,16},{24,28},{28,24},{32,36},... | collective-permute-start | bytes 380936 | tf_op jit(solution)/shard_map/ppermute | solution.py:42
  659.5 22.9 %collective-permute-start.81 = (bf16[64,2048]{1,0:T(8,128)(2,1)S(1)}, bf16[64,2048]{1,0:T(8,128)(2,1)S(1)}, u32[]{:S(2)}, u32[]{:S(2)}) collective-permute-start(bf16[64,2048]{1,0:T(8,128)(2,1)S(1)} %get-tuple-element.73), channel_id=1, source_target_pairs={{64,0},{65,1},{66,2},{67,3},{68,4},{69,5},{70,6},{71,7},{72,8},{73... | collective-permute-start | bytes 786440 | tf_op jit(solution)/shard_map/ppermute | solution.py:582
  666.9 15.3 %collective-permute-start.91 = (bf16[31,16,128]{2,1,0:T(8,128)(2,1)S(1)}, bf16[31,16,128]{2,1,0:T(8,128)(2,1)S(1)}, u32[]{:S(2)}, u32[]{:S(2)}) collective-permute-start(bf16[31,16,128]{2,1,0:T(8,128)(2,1)S(1)} %fusion.281), channel_id=1, source_target_pairs={{64,0},{65,1},{66,2},{67,3},{68,4},{69,5},{70,6},{71,7},{72,8},{73... | collective-permute-start | bytes 380936 | tf_op jit(solution)/shard_map/ppermute | solution.py:582
  (177 other events, 3023.9 us)
Sparse Core Ops, SparseCore 0:
  27.3 147.4 all-gather.2
  177.1 134.3 all-gather.4
  495.4 25.6 reduce-scatter.2
  546.3 65.8 reduce-scatter.4

commit v3 on v2

--- a/solution.py
+++ b/solution.py
@@ -153,44 +153,34 @@
     )(grad_mixed, probs, queries, key_block)
 
 
-def weight_copies(table_ref, up_buf, down_buf, sems):
-    count, width, tile = up_buf.shape
-    each = count // 2
-    copies = []
-    for j in range(count):
-        rows = pl.ds(j // each * width, width)
-        begin = j % each * tile
-        for k, buf in enumerate((up_buf, down_buf)):
-            columns = pl.ds(begin + k * each * tile, tile)
-            copies.append(
-                pltpu.make_async_copy(table_ref.at[rows, columns], buf.at[j], sems.at[k, j])
-            )
-    return copies
+def weight_tile(table_ref, hidden, tile, j, second):
+    width = table_ref.shape[0] // 2
+    half = hidden // 2
+    row = j * tile // half * width
+    column = j * tile % half + second * half
+    return table_ref[row : row + width, column : column + tile]
 
 
 def feed_kernel(
-    second_ref, table_ref, bias_ref, eu_ref, sd_ref, su_ref, ed_ref,
-    active_ref, slope_ref, low_u_ref, low_d_ref, out_ref, up_buf, down_buf, total, sems,
+    tile, second_ref, table_ref, bias_ref, eu_ref, sd_ref, su_ref, ed_ref,
+    active_ref, slope_ref, low_u_ref, low_d_ref, out_ref, total,
 ):
-    count, width, tile = up_buf.shape
-    copies = weight_copies(table_ref, up_buf, down_buf, sems)
-    for copy in copies:
-        copy.start()
+    hidden = eu_ref.shape[1]
+    count = hidden // tile
     second = second_ref[...]
     low_u = against(second, su_ref[...]).astype(bf16)
     low_u_ref[...] = low_u
     low = 0.0
     for j in range(count):
         columns = pl.ds(j * tile, tile)
-        copies[2 * j].wait()
-        upward = plain(second, up_buf[j]) + plain(low_u, eu_ref[:, columns]) + bias_ref[:, columns]
+        upward = plain(second, weight_tile(table_ref, hidden, tile, j, 0))
+        upward = upward + plain(low_u, eu_ref[:, columns]) + bias_ref[:, columns]
         active, slope = gelu_parts(upward)
         active = active.astype(bf16)
         active_ref[:, columns] = active
         slope_ref[:, columns] = slope.astype(bf16)
         low = low + against(active, sd_ref[:, columns])
-        copies[2 * j + 1].wait()
-        part = against(active, down_buf[j])
+        part = against(active, weight_tile(table_ref, hidden, tile, j, 1))
         if j == 0:
             total[...] = part
         elif j < count - 1:
@@ -200,13 +190,8 @@
     out_ref[...] = (total[...] + part + plain(low_d, ed_ref[...])).astype(bf16)
 
 
-def feed_scratch(rows, width, hidden, tile):
-    return [
-        pltpu.VMEM((hidden // tile, width, tile), bf16),
-        pltpu.VMEM((hidden // tile, width, tile), bf16),
-        pltpu.VMEM((rows, width), f32),
-        pltpu.SemaphoreType.DMA((2, hidden // tile)),
-    ]
+def feed_limit(table):
+    return table.size * 2 + 12 * 2**20
 
 
 def feed(second, table, bias, eu, sd, su, ed):
@@ -214,8 +199,8 @@
     rank, hidden = eu.shape
     held = pl.BlockSpec(memory_space=pltpu.VMEM)
     return pl.pallas_call(
-        feed_kernel,
-        in_specs=[held, pl.BlockSpec(memory_space=pl.ANY)] + [held] * 5,
+        lambda *refs: feed_kernel(512, *refs),
+        in_specs=[held] * 7,
         out_specs=[held] * 5,
         out_shape=[
             jax.ShapeDtypeStruct((rows, hidden), bf16),
@@ -224,8 +209,8 @@
             jax.ShapeDtypeStruct((rows, rank), bf16),
             jax.ShapeDtypeStruct((rows, width), bf16),
         ],
-        scratch_shapes=feed_scratch(rows, width, hidden, 512),
-        compiler_params=pltpu.CompilerParams(vmem_limit_bytes=40 * 2**20),
+        scratch_shapes=[pltpu.VMEM((rows, width), f32)],
+        compiler_params=pltpu.CompilerParams(vmem_limit_bytes=feed_limit(table)),
         cost_estimate=pl.CostEstimate(
             flops=4 * rows * width * hidden,
             bytes_accessed=4 * width * hidden + 8 * rows * hidden,
@@ -236,27 +221,23 @@
 
 
 def feed_back_kernel(
-    branch_ref, table_ref, slope_ref, eu_ref, sd_ref, su_ref, ed_ref,
-    grad_up_ref, inner_d_ref, inner_u_ref, out_ref, up_buf, down_buf, total, sems,
+    tile, branch_ref, table_ref, slope_ref, eu_ref, sd_ref, su_ref, ed_ref,
+    grad_up_ref, inner_d_ref, inner_u_ref, out_ref, total,
 ):
-    count, width, tile = up_buf.shape
-    copies = weight_copies(table_ref, up_buf, down_buf, sems)
-    for j in range(count):
-        copies[2 * j + 1].start()
-        copies[2 * j].start()
+    hidden = eu_ref.shape[1]
+    count = hidden // tile
     branch = branch_ref[...]
     inner_d = against(branch, ed_ref[...]).astype(bf16)
     inner_d_ref[...] = inner_d
     inner = 0.0
     for j in range(count):
         columns = pl.ds(j * tile, tile)
-        copies[2 * j + 1].wait()
-        grad = plain(branch, down_buf[j]) + plain(inner_d, sd_ref[:, columns])
+        grad = plain(branch, weight_tile(table_ref, hidden, tile, j, 1))
+        grad = grad + plain(inner_d, sd_ref[:, columns])
         grad = (grad * slope_ref[:, columns].astype(f32)).astype(bf16)
         grad_up_ref[:, columns] = grad
         inner = inner + against(grad, eu_ref[:, columns])
-        copies[2 * j].wait()
-        part = against(grad, up_buf[j])
+        part = against(grad, weight_tile(table_ref, hidden, tile, j, 0))
         if j == 0:
             total[...] = part
         elif j < count - 1:
@@ -271,8 +252,8 @@
     rank, hidden = eu.shape
     held = pl.BlockSpec(memory_space=pltpu.VMEM)
     return pl.pallas_call(
-        feed_back_kernel,
-        in_specs=[held, pl.BlockSpec(memory_space=pl.ANY)] + [held] * 5,
+        lambda *refs: feed_back_kernel(512, *refs),
+        in_specs=[held] * 7,
         out_specs=[held] * 4,
         out_shape=[
             jax.ShapeDtypeStruct((rows, hidden), bf16),
@@ -280,8 +261,8 @@
             jax.ShapeDtypeStruct((rows, rank), bf16),
             jax.ShapeDtypeStruct((rows, width), bf16),
         ],
-        scratch_shapes=feed_scratch(rows, width, hidden, 512),
-        compiler_params=pltpu.CompilerParams(vmem_limit_bytes=40 * 2**20),
+        scratch_shapes=[pltpu.VMEM((rows, width), f32)],
+        compiler_params=pltpu.CompilerParams(vmem_limit_bytes=feed_limit(table)),
         cost_estimate=pl.CostEstimate(
             flops=4 * rows * width * hidden,
             bytes_accessed=4 * width * hidden + 4 * rows * hidden,
@@ -289,28 +270,6 @@
         ),
         name="feed_back",
     )(branch, table, slope, eu, sd, su, ed)
-
-
-def place_kernel(rank_ref, mine_ref, other_ref, out_ref):
-    core = rank_ref[0] % 2
-    out_ref[0, pl.ds(core, 1)] = mine_ref[...]
-    out_ref[0, pl.ds(1 - core, 1)] = other_ref[...]
-
-
-def by_rank(rank, mine, other):
-    chips, rows, columns = mine.shape
-    block = pl.BlockSpec((1, rows, columns), lambda i, r: (i, 0, 0))
-    return pl.pallas_call(
-        place_kernel,
-        grid_spec=pltpu.PrefetchScalarGridSpec(
-            num_scalar_prefetch=1,
-            grid=(chips,),
-            in_specs=[block, block],
-            out_specs=pl.BlockSpec((1, 2, rows, columns), lambda i, r: (i ^ (r[0] // 2), 0, 0, 0)),
-        ),
-        out_shape=jax.ShapeDtypeStruct((chips, 2, rows, columns), bf16),
-        name="place",
-    )(rank.reshape(1).astype(jnp.int32), mine, other)
 
 
 def per_device(
@@ -425,40 +384,35 @@
     vector_sizes = [width, width, local_q, 2 * head, width, width, width, local_f, width]
 
     both = ("section", "dp")
+
+    def gather(shard, axes):
+        return lax.all_gather(shard, axes, axis=0, tiled=True)
+
+    def halves(shard):
+        cut = shard.shape[1] // 2
+        return shard[:, :cut], shard[:, cut:]
+
     shard_early = jnp.concatenate(
         [query_weight[0], keyval_weight[0], output_weight[0].T], axis=1
     )
-
-    def mask_flip(block, mask):
-        return lax.ppermute(block, both, [(i, i ^ mask) for i in range(2 * lax.axis_size("dp"))])
-
-    pair_near = jnp.stack([shard_early, mask_flip(shard_early, 2)])
-    pair_far = jnp.stack([mask_flip(shard_early, 16), mask_flip(shard_early, 18)])
-
-    def early_table(pair):
-        quad = jnp.concatenate([pair] + [mask_flip(pair, 4 * k) for k in range(1, 4)], axis=0)
-        table = by_rank(data, quad, mask_flip(quad, 1))
-        return table.reshape(width, -1)
-
-    early_tables = [early_table(pair) for pair in by_layer(pair_near, pair_far)]
+    early_zero = gather(jnp.where(low_section, shard_early, swap(shard_early)), "dp")
     vector_layers = by_layer(vectors, swap(vectors))
     early_layers = by_layer(early_pack(own_bank), swap(early_pack(other_bank)))
     late_layers = by_layer(late_pack(own_bank), swap(late_pack(other_bank)))
-    half = local_f // 2
-    shard_up = upward_weight[0]
-    shard_down = downward_weight[0].T
-    halves = [
-        jnp.concatenate(
-            [shard_up[:, h * half : (h + 1) * half], shard_down[:, h * half : (h + 1) * half]],
-            axis=1,
-        )
-        for h in range(2)
+    up_halves = halves(upward_weight[0])
+    down_halves = halves(downward_weight[0].T)
+    early_halves = halves(shard_early)
+    side = [
+        jnp.concatenate([up_halves[h], down_halves[h], early_halves[h]], axis=1) for h in range(2)
     ]
-    keep = jnp.where(low_section, halves[0], halves[1])
-    gained = swap(jnp.where(low_section, halves[1], halves[0]))
-    feed_zero, feed_one = by_layer(keep, gained)
-    feed_zero = lax.all_gather(feed_zero, both, axis=0, tiled=True)
-    feed_one = lax.all_gather(feed_one, both, axis=0, tiled=True)
+    keep = jnp.where(low_section, side[0], side[1])
+    gained = swap(jnp.where(low_section, side[1], side[0]))
+    side_zero, side_one = by_layer(keep, gained)
+    feed_zero = gather(
+        jnp.concatenate([side_zero[:, :local_f], side_one[:, local_f:]], axis=1), both
+    )
+    feed_one = gather(side_one[:, :local_f], both)
+    early_one = jnp.concatenate([feed_zero[:width, local_f:], feed_zero[width:, local_f:]], axis=1)
 
     def split(table, sizes):
         cuts = [0]
@@ -468,8 +422,8 @@
 
     wide = local_q + 2 * head
     weights = [
-        split(early_tables[layer], [wide, local_q]) + [table]
-        for layer, table in enumerate([feed_zero, feed_one])
+        split(early, [wide, local_q]) + [table]
+        for early, table in [(early_zero, feed_zero), (early_one, feed_one)]
     ]
     small = [
         [part.astype(f32) for part in split(vector_layers[layer], vector_sizes)]
@@ -548,96 +502,70 @@
     def flat(block):
         return block.transpose(1, 0, 2).reshape(rank, -1)
 
-    def reduce_grads(shared, owned):
-        pile = jnp.concatenate([tiles(part) for part in shared], axis=0).astype(bf16)
-        lack = -pile.shape[0] % ranks
-        if lack:
-            pile = jnp.concatenate([pile, jnp.zeros((lack,) + pile.shape[1:], bf16)], axis=0)
+    chips = lax.axis_size("dp") // 4
+    turn, plane, core = data // 4, data // 2 % 2, data % 2
+
+    def padded(pile, multiple):
+        lack = -pile.shape[0] % multiple
+        if not lack:
+            return pile
+        return jnp.concatenate([pile, jnp.zeros((lack,) + pile.shape[1:], pile.dtype)], axis=0)
+
+    def piled(shared):
+        return padded(jnp.concatenate([tiles(part) for part in shared], axis=0).astype(bf16), ranks)
+
+    def owned_pile(mine, owned):
+        pile = jnp.concatenate([mine] + [tiles(part) for part in owned], axis=0).astype(bf16)
+        return padded(pile, lax.axis_size("dp"))
+
+    def at(block, index, axis):
+        return lax.dynamic_index_in_dim(block, index, axis, keepdims=False)
+
+    def offloaded_grads(shared, owned):
+        mine = lax.psum_scatter(piled(shared), "tensor", scatter_dimension=0, tiled=True)
+        return lax.psum_scatter(owned_pile(mine, owned), "dp", scatter_dimension=0, tiled=True)
+
+    def scattered_grads(shared, owned):
+        pile = piled(shared)
         each = pile.shape[0] // ranks
-        total = pick(pile, tensor * each, each).astype(f32)
+        mine = pick(pile, tensor * each, each).astype(f32)
         for j in range(1, ranks):
             block = pick(pile, ((tensor + j) % ranks) * each, each)
-            total = total + around(block, "tensor", j).astype(f32)
-        pile = jnp.concatenate([total] + [tiles(part) for part in owned], axis=0).astype(bf16)
-        if pile.shape[0] % 2:
-            pile = jnp.concatenate([pile, jnp.zeros((1,) + pile.shape[1:], bf16)], axis=0)
-        half = pile.shape[0] // 2
-        core = data % 2
-        got = flipped(pick(pile, (1 - core) * half, half), "dp", 1)
-        mine = (pick(pile, core * half, half).astype(f32) + got.astype(f32)).astype(bf16)
-        got = flipped(mine, "dp", 2)
-        mine = (mine.astype(f32) + got.astype(f32)).astype(bf16)
-        parts = jnp.stack([mine] + [around(mine, "dp", 4 * k) for k in range(1, 4)])
-        turn = data // 4
-        total = sum(
-            lax.dynamic_index_in_dim(parts, (turn - r) % 4, 0, keepdims=False).astype(f32)
-            for r in range(4)
+            mine = mine + around(block, "tensor", j).astype(f32)
+        pile = owned_pile(mine, owned)
+        pile = pile.reshape((chips, 2, 2, -1) + pile.shape[1:])
+        got = flipped(at(pile, 1 - core, 2), "dp", 1)
+        pile = (at(pile, core, 2).astype(f32) + got.astype(f32)).astype(bf16)
+        got = flipped(at(pile, 1 - plane, 1), "dp", 2)
+        pile = (at(pile, plane, 1).astype(f32) + got.astype(f32)).astype(bf16)
+        mine = at(pile, turn, 0).astype(f32)
+        for k in range(1, chips):
+            mine = mine + flipped(at(pile, turn ^ k, 0), "dp", 4 * k).astype(f32)
+        return mine.astype(bf16)
+
+    def spread_grads(pair, shared_sizes, owned_sizes):
+        parts = jnp.stack([pair] + [flipped(pair, "dp", 4 * k) for k in range(1, chips)])
+        parts = jnp.stack([at(parts, turn ^ k, 0) for k in range(chips)])
+        other = flipped(parts, "dp", 2)
+        parts = jnp.stack(
+            [jnp.where(plane == 0, parts, other), jnp.where(plane == 0, other, parts)], axis=1
         )
-        return total.astype(bf16)
-
-    def to_upper(value):
-        return lax.ppermute(value, "section", [(0, 1)])
-
-    def to_lower(value):
-        return lax.ppermute(value, "section", [(1, 0)])
-
-    def offloaded_grads(shared, owned):
-        pile = jnp.concatenate([tiles(part) for part in shared], axis=0).astype(bf16)
-        lack = -pile.shape[0] % ranks
-        pile = jnp.concatenate([pile, jnp.zeros((lack,) + pile.shape[1:], bf16)], axis=0)
-        mine = lax.psum_scatter(pile, "tensor", scatter_dimension=0, tiled=True)
-        pile = jnp.concatenate([mine] + [tiles(part).astype(bf16) for part in owned], axis=0)
-        lack = -pile.shape[0] % lax.axis_size("dp")
-        pile = jnp.concatenate([pile, jnp.zeros((lack,) + pile.shape[1:], bf16)], axis=0)
-        mine = lax.psum_scatter(pile, "dp", scatter_dimension=0, tiled=True)
-        pair = jnp.stack([to_upper(mine), mine], axis=1)
-        pile = lax.all_gather(pair, "dp", axis=0, tiled=True)
-        shared_sizes = [part.shape[1] for part in shared]
+        other = flipped(parts, "dp", 1)
+        parts = jnp.stack(
+            [jnp.where(core == 0, parts, other), jnp.where(core == 0, other, parts)], axis=2
+        )
+        pile = jnp.moveaxis(parts, 3, 0).reshape((2, -1) + parts.shape[5:])
         each = -(-(sum(shared_sizes) // 128) // ranks)
-        ordered = lax.all_gather(pile[:each], "tensor", axis=0, tiled=True)
-        results, begin = [], 0
-        for size in shared_sizes:
-            count = size // 128
-            results.append([flat(ordered[begin : begin + count, m]) for m in range(2)])
-            begin += count
-        begin, others = each, []
-        for part in owned:
-            count = part.shape[1] // 128
-            others.append([flat(pile[begin : begin + count, m]) for m in range(2)])
-            begin += count
-        return results + others
-
-    def spread_grads(mine, shared_sizes, owned_sizes):
-        shared_count = sum(shared_sizes) // 128
-        each = -(-shared_count // ranks)
-        owned_count = sum(owned_sizes) // 128
-        core = data % 2
-        other = flipped(mine, "dp", 1)
-        lower = jnp.where(core == 0, mine, other)
-        upper = jnp.where(core == 0, other, mine)
-        pile = jnp.concatenate([lower, upper], axis=1)
         own = pile[:, :each]
         parts = jnp.stack([own] + [around(own, "tensor", k) for k in range(1, ranks)])
-        ordered = jnp.concatenate(
-            [
-                lax.dynamic_index_in_dim(parts, (tensor - r) % ranks, 0, keepdims=False)
-                for r in range(ranks)
-            ],
-            axis=1,
-        )
+        ordered = jnp.concatenate([at(parts, (tensor - r) % ranks, 0) for r in range(ranks)], axis=1)
         results = []
-        begin = 0
-        for size in shared_sizes:
-            count = size // 128
-            results.append([flat(ordered[m, begin : begin + count]) for m in range(2)])
-            begin += count
-        begin = each
-        owned = []
-        for size in owned_sizes:
-            count = size // 128
-            owned.append([flat(pile[m, begin : begin + count]) for m in range(2)])
-            begin += count
-        return results, owned
+        for whole, begin, sizes in [(ordered, 0, shared_sizes), (pile, each, owned_sizes)]:
+            for size in sizes:
+                count = size // 128
+                results.append([flat(whole[m, begin : begin + count]) for m in range(2)])
+                begin += count
+        return results
 
     def backward_feed(layer, kept, grad):
         feed_w = weights[layer][2]
@@ -689,7 +617,7 @@
     given = lax.dynamic_index_in_dim(cotangent, section, 0, keepdims=False).astype(f32)
     grad_middle_one, feed_shared, feed_owned = backward_feed(1, kept_one, given)
     grad_one, out_one_grads, qkv_one_grads = backward_attend(1, kept_one, grad_middle_one)
-    grads_one = offloaded_grads(
+    mine_one = offloaded_grads(
         feed_shared + out_one_grads[0] + qkv_one_grads[0],
         feed_owned + out_one_grads[1] + qkv_one_grads[1],
     )
@@ -697,13 +625,20 @@
     grad_zero, out_zero_grads, qkv_zero_grads = backward_attend(0, kept_zero, grad_middle_zero)
     shared = feed_shared + out_zero_grads[0] + qkv_zero_grads[0]
     owned = feed_owned + out_zero_grads[1] + qkv_zero_grads[1]
-    mine = reduce_grads(shared, owned)
-    grads_zero = spread_grads(
-        jnp.stack([mine, to_lower(mine)]),
-        [part.shape[1] for part in shared],
-        [part.shape[1] for part in owned],
-    )
-    grads_zero = grads_zero[0] + grads_zero[1]
+    mine_zero = scattered_grads(shared, owned)
+    received = swap(jnp.where(low_section, mine_one, mine_zero))
+    pair = jnp.where(
+        low_section, jnp.stack([mine_zero, received]), jnp.stack([received, mine_one])
+    )
+    grads = spread_grads(
+        pair, [part.shape[1] for part in shared], [part.shape[1] for part in owned]
+    )
+
+    def to_upper(value):
+        return lax.ppermute(value, "section", [(0, 1)])
+
+    def to_lower(value):
+        return lax.ppermute(value, "section", [(1, 0)])
 
     def both_micros(zero, one):
         received = jnp.where(low_section, to_lower(zero), to_upper(one))
@@ -740,10 +675,7 @@
         down_shrink_grad,
         out_shrink_grad,
         q_expand_grad,
-    ) = [
-        [jnp.where(low_section, zero[m], one[m]) for m in range(2)]
-        for zero, one in zip(grads_zero, grads_one)
-    ]
+    ) = grads
     return (
         section_outputs[None],
         input_grads[None],

time: 717 us -> 649 us (0.905)
  blocking collectives: 31.8 us -> 0 us
  Pallas kernels: 81.8 us -> 69.2 us
  starting transfers between devices: 169 us -> 158 us
    ppermute x11 -> x0, waiting for transfers between devices: 103 us -> none  [mask_flip(): lax.ppermute(block, both, [(i, i ^ mask) for i in range(2 * lax.axis_size...]
    all_gather x2 -> x3, waiting for transfers between devices: 0.04 us -> 43.9 us  [gather(): return lax.all_gather(shard, axes, axis=0, tiled=True)]
    all_gather x2 -> x0, blocking collectives: 31.8 us -> none  [the longest x1 17.8 us: offloaded_grads(): pile = lax.all_gather(pair, 'dp', axis=0, tiled=True)]
    ppermute x4 -> x6, waiting for transfers between devices: 19.8 us -> 46.3 us  [swap(): return lax.ppermute(value, 'section', sides)]
    ppermute x57 -> x54, waiting for transfers between devices: 125 us -> 148 us  [around(): lax.ppermute(block, axis, [(i, (i + distance) % size) for i in range(size)])]
    reduce_scatter x2, waiting for transfers between devices: 23 us -> 0.02 us  [the longest x1 0.02 us: offloaded_grads(): lax.psum_scatter(piled(shared), 'tensor', scatter_dimension=0, tiled=True)]
    ppermute x11 -> x0, starting transfers between devices: 22.1 us -> none  [mask_flip(): lax.ppermute(block, both, [(i, i ^ mask) for i in range(2 * lax.axis_size...]
    ppermute x3 -> x10, starting transfers between devices: 1.97 us -> 23.5 us  [flipped(): return lax.ppermute(block, axis, [(i, i ^ bit) for i in range(size)])]
  transfers between devices with their start and end apart: 101 -> 95, of which waited for: 52 -> 59; matrix products, arithmetic and copies ran while one was open for 14% -> 13% of each run, Pallas kernels for 12% -> 11%
where the time goes in v3:
time: 649 us; the launch traced here: 642 us
  waiting for transfers between devices  274 us (42%)
  starting transfers between devices  158 us (24%)
  Pallas kernels  69.2 us (11%)
  matrix products  40.3 us (6%)
  local copies, waits for them, and re-layouts  40.2 us (6%)
  other arithmetic  39.8 us (6%)
  between operations  20.7 us (3%)
    ppermute x54, waiting for transfers between devices, around(): lax.ppermute(block, axis, [(i, (i + distance) % size) for i in range(size)])  148 us
    ppermute x54, starting transfers between devices, around(): lax.ppermute(block, axis, [(i, (i + distance) % size) for i in range(size)])  67.7 us
    ppermute x6, waiting for transfers between devices, swap(): return lax.ppermute(value, 'section', sides)  46.3 us
    all_gather x3, waiting for transfers between devices, gather(): return lax.all_gather(shard, axes, axis=0, tiled=True)  43.9 us
    ppermute x16, starting transfers between devices, along(): return lax.ppermute(block, axis, route)  29.4 us
    pallas_call x2, Pallas kernels, feed(): pl.pallas_call(lambda *refs: feed_kernel(512, *refs), in_specs=[held] * 7...  25.8 us
    unnamed x301, local copies, waits for them, and re-layouts  25.4 us
    pallas_call x2, Pallas kernels, feed_back(): pl.pallas_call(lambda *refs: feed_back_kernel(512, *refs), in_specs=[held...  24.4 us
  transfers between devices with their start and end apart: 95, of which 59 were waited for; matrix products, arithmetic and copies ran while one was open for 13% of the time, Pallas kernels for 11%

profile of v3, /device:TPU:0, one launch (start us, length us, event | category | flops | bytes accessed | tf_op | source)
XLA Modules:
  0.0 642.1 jit_solution(13193391396454218304)
XLA Ops:
  9.3 4.0 collective-permute-start.4
  13.4 7.7 %collective-permute-done.4 = bf16[128,1280]{1,0:T(8,128)(2,1)S(1)} collective-permute-done((bf16[128,1280]{1,0:T(8,128)(2,1)S(1)}, bf16[128,1280]{1,0:T(8,128)(2,1)S(1)}, u32[]{:S(2)}, u32[]{:S(2)}) %collective-permute-start.4) | collective-permute-done | bytes 327712 | tf_op jit(solution)/shard_map/ppermute | solution.py:322
  26.7 22.7 %collective-permute-done.17 = bf16[128,2688]{1,0:T(8,128)(2,1)S(1)} collective-permute-done((bf16[128,2688]{1,0:T(8,128)(2,1)S(1)}, bf16[128,2688]{1,0:T(8,128)(2,1)S(1)}, u32[]{:S(2)}, u32[]{:S(2)}) %collective-permute-start.17) | collective-permute-done | bytes 688160 | tf_op jit(solution)/shard_map/ppermute | solution.py:322
  56.9 4.1 collective-permute-start
  81.1 6.2 collective-permute-done.3
  87.3 3.5 collective-permute-start.10
  91.7 11.7 %collective-permute-done.10 = bf16[16,10752]{1,0:T(8,128)(2,1)S(1)} collective-permute-done((bf16[16,10752]{1,0:T(8,128)(2,1)S(1)}, bf16[16,10752]{1,0:T(8,128)(2,1)S(1)}, u32[]{:S(2)}, u32[]{:S(2)}) %collective-permute-start.10) | collective-permute-done | bytes 344096 | tf_op jit(solution)/shard_map/ppermute | solution.py:322
  115.4 5.5 collective-permute-done.8
  121.1 4.3 attend.2
  126.1 3.6 fusion.201
  132.8 6.2 collective-permute-done.13
  140.7 4.7 collective-permute-done.11
  149.5 11.7 %collective-permute-done.16 = bf16[64,2048]{1,0:T(8,128)(2,1)S(1)} collective-permute-done((bf16[64,2048]{1,0:T(8,128)(2,1)S(1)}, bf16[64,2048]{1,0:T(8,128)(2,1)S(1)}, u32[]{:S(2)}, u32[]{:S(2)}) %collective-permute-start.16) | collective-permute-done | bytes 262176 | tf_op jit(solution)/shard_map/ppermute | solution.py:31
  162.0 43.9 %all-gather.6.cloned.1.call-done.refs_1_ = bf16[4096,2688]{1,0:T(8,128)(2,1)} async-done(((bf16[128,2688]{1,0:T(8,128)(2,1)}), bf16[4096,2688]{1,0:T(8,128)(2,1)}) %all-gather.6.cloned.1.call-update) | async-done | bytes 22020112 | tf_op jit(solution)/shard_map/all_gather | solution.py:389
  205.8 16.4 %feed.2 = (bf16[256,2048]{1,0:T(8,128)(2,1)S(1)}, bf16[256,2048]{1,0:T(8,128)(2,1)S(1)}, bf16[256,16]{1,0:T(8,128)(2,1)S(1)}, bf16[256,16]{1,0:T(8,128)(2,1)S(1)}, bf16[256,2048]{1,0:T(8,128)(2,1)S(1)}) custom-call(bf16[256,2048]{1,0:T(8,128)(2,1)S(1)} %pad_maximum_fusion.3.refs_0_, bf16[4096,2688]{1,0:T(8,128)(2,1)} %all-gather.6.cloned.1.call-done.refs_1_, ...), custom_call_target="tpu_custom_call" | custom-call | flops 4294967296 | bytes 20971520 | tf_op jit(solution)/shard_map/feed/pallas_call | solution.py:201
  225.9 5.8 collective-permute-done.20
  233.5 4.4 collective-permute-done.18
  247.8 8.7 %collective-permute-done.23 = bf16[64,2048]{1,0:T(8,128)(2,1)S(1)} collective-permute-done((bf16[64,2048]{1,0:T(8,128)(2,1)S(1)}, bf16[64,2048]{1,0:T(8,128)(2,1)S(1)}, u32[]{:S(2)}, u32[]{:S(2)}) %collective-permute-start.23) | collective-permute-done | bytes 262176 | tf_op jit(solution)/shard_map/ppermute | solution.py:31
  256.5 9.9 %collective-permute-start.39 = (bf16[64,2048]{1,0:T(8,128)(2,1)}, bf16[64,2048]{1,0:T(8,128)(2,1)}, u32[]{:S(2)}, u32[]{:S(2)}) collective-permute-start(bf16[64,2048]{1,0:T(8,128)(2,1)} %dynamic-slice_bitcast_fusion), channel_id=1, source_target_pairs={{0,3},{1,0},{2,1},{3,2},{4,7},{5,4},{6,5},{7,6},{8,11},{9,8},{10,9... | collective-permute-start | bytes 786440 | tf_op jit(solution)/shard_map/ppermute | solution.py:31
  269.5 5.1 collective-permute-start.25
  284.9 4.3 attend.3
  289.9 5.0 fusion.202
  295.9 3.7 collective-permute-start.29
  304.1 6.4 collective-permute-done.28
  317.7 9.7 %collective-permute-done.33 = bf16[64,2048]{1,0:T(8,128)(2,1)S(1)} collective-permute-done((bf16[64,2048]{1,0:T(8,128)(2,1)S(1)}, bf16[64,2048]{1,0:T(8,128)(2,1)S(1)}, u32[]{:S(2)}, u32[]{:S(2)}) %collective-permute-start.33) | collective-permute-done | bytes 262176 | tf_op jit(solution)/shard_map/ppermute | solution.py:31
  328.4 5.8 copy-done.2
  337.6 9.4 %feed.3 = (bf16[256,2048]{1,0:T(8,128)(2,1)S(1)}, bf16[256,2048]{1,0:T(8,128)(2,1)S(1)}, bf16[256,16]{1,0:T(8,128)(2,1)S(1)}, bf16[256,16]{1,0:T(8,128)(2,1)S(1)}, bf16[256,2048]{1,0:T(8,128)(2,1)S(1)}) custom-call(bf16[256,2048]{1,0:T(8,128)(2,1)S(1)} %pad_maximum_fusion.5.refs_0_, bf16[4096,2048]{1,0:T(8,128)(2,1)S(1)} %copy-done.2, ...), custom_call_target="tpu_custom_call" | custom-call | flops 4294967296 | bytes 20971520 | tf_op jit(solution)/shard_map/feed/pallas_call | solution.py:201
  350.3 5.8 copy-done.3
  356.1 8.6 %feed_back.2 = (bf16[256,2048]{1,0:T(8,128)(2,1)S(1)}, bf16[256,16]{1,0:T(8,128)(2,1)S(1)}, bf16[256,16]{1,0:T(8,128)(2,1)S(1)}, bf16[256,2048]{1,0:T(8,128)(2,1)S(1)}) custom-call(bf16[256,2048]{1,0:T(8,128)(2,1)S(1)} %pad_maximum_fusion.6.refs_0_, bf16[4096,2048]{1,0:T(8,128)(2,1)S(1)} %copy-done.3, bf16[256,2048]{1,0:T(8,128)(2,1)S(1)} %get-tuple-element.42.refs_2_, ...), custom_call_target="tpu_custom_call" | custom-call | flops 4294967296 | bytes 18874368 | tf_op jit(solution)/shard_map/feed_back/pallas_call | solution.py:254
  369.2 4.7 collective-permute-done.44
  387.9 4.1 collective-permute-done.34
  393.1 9.6 %collective-permute-start.38 = (bf16[64,2048]{1,0:T(8,128)(2,1)S(1)}, bf16[64,2048]{1,0:T(8,128)(2,1)S(1)}, u32[]{:S(2)}, u32[]{:S(2)}) collective-permute-start(bf16[64,2048]{1,0:T(8,128)(2,1)S(1)} %get-tuple-element.87), channel_id=1, source_target_pairs={{0,64},{1,65},{2,66},{3,67},{4,68},{5,69},{6,70},{7,71},{8,72},{9,... | collective-permute-start | bytes 786440 | tf_op jit(solution)/shard_map/ppermute | solution.py:638
  408.0 5.2 attend_back.2
  423.8 3.9 collective-permute-done.51
  433.8 5.2 collective-permute-done.54
  440.7 7.1 %collective-permute-done.52 = bf16[64,2048]{1,0:T(8,128)(2,1)S(1)} collective-permute-done((bf16[64,2048]{1,0:T(8,128)(2,1)S(1)}, bf16[64,2048]{1,0:T(8,128)(2,1)S(1)}, u32[]{:S(2)}, u32[]{:S(2)}) %collective-permute-start.52) | collective-permute-done | bytes 262176 | tf_op jit(solution)/shard_map/ppermute | solution.py:31
  455.5 8.4 %collective-permute-start.72 = (bf16[64,2048]{1,0:T(8,128)(2,1)}, bf16[64,2048]{1,0:T(8,128)(2,1)}, u32[]{:S(2)}, u32[]{:S(2)}) collective-permute-start(bf16[64,2048]{1,0:T(8,128)(2,1)} %get-tuple-element.80), channel_id=1, source_target_pairs={{0,64},{1,65},{2,66},{3,67},{4,68},{5,69},{6,70},{7,71},{8,72},{9,... | collective-permute-start | bytes 786440 | tf_op jit(solution)/shard_map/ppermute | solution.py:638
  470.0 15.9 %feed_back.3 = (bf16[256,2048]{1,0:T(8,128)(2,1)S(1)}, bf16[256,16]{1,0:T(8,128)(2,1)S(1)}, bf16[256,16]{1,0:T(8,128)(2,1)S(1)}, bf16[256,2048]{1,0:T(8,128)(2,1)S(1)}) custom-call(bf16[256,2048]{1,0:T(8,128)(2,1)S(1)} %pad_maximum_fusion.8.refs_0_, bf16[4096,2688]{1,0:T(8,128)(2,1)} %all-gather.6.cloned.1.call-done.refs_1_, ...), custom_call_target="tpu_custom_call" | custom-call | flops 4294967296 | bytes 18874368 | tf_op jit(solution)/shard_map/feed_back/pallas_call | solution.py:254
  492.8 7.7 %collective-permute-done.60 = bf16[64,2048]{1,0:T(8,128)(2,1)S(1)} collective-permute-done((bf16[64,2048]{1,0:T(8,128)(2,1)}, bf16[64,2048]{1,0:T(8,128)(2,1)S(1)}, u32[]{:S(2)}, u32[]{:S(2)}) %collective-permute-start.60) | collective-permute-done | bytes 262176 | tf_op jit(solution)/shard_map/ppermute | solution.py:31
  510.4 10.7 %collective-permute-done.63 = bf16[64,2048]{1,0:T(8,128)(2,1)S(1)} collective-permute-done((bf16[64,2048]{1,0:T(8,128)(2,1)S(1)}, bf16[64,2048]{1,0:T(8,128)(2,1)S(1)}, u32[]{:S(2)}, u32[]{:S(2)}) %collective-permute-start.63) | collective-permute-done | bytes 262176 | tf_op jit(solution)/shard_map/ppermute | solution.py:31
  526.6 5.2 attend_back.3
  539.5 6.1 collective-permute-done.67
  563.3 4.6 collective-permute-start.77
  572.2 4.7 collective-permute-done.68
  577.3 10.9 %collective-permute-start.80 = (bf16[4,16,128]{2,1,0:T(8,128)(2,1)S(1)}, bf16[4,16,128]{2,1,0:T(8,128)(2,1)S(1)}, u32[]{:S(2)}, u32[]{:S(2)}) collective-permute-start(bf16[4,16,128]{2,1,0:T(8,128)(2,1)S(1)} %get-tuple-element.208), channel_id=1, source_target_pairs={{0,48},{4,52},{8,56},{12,60},{16,32},{20,36},{24,40},{28,44},{32,1... | collective-permute-start | bytes 49160 | tf_op jit(solution)/shard_map/ppermute | solution.py:42
  589.8 3.5 collective-permute-done.79
  595.3 4.1 collective-permute-done.81
  612.1 6.9 %collective-permute-done.71 = bf16[64,2048]{1,0:T(8,128)(2,1)S(1)} collective-permute-done((bf16[64,2048]{1,0:T(8,128)(2,1)S(1)}, bf16[64,2048]{1,0:T(8,128)(2,1)S(1)}, u32[]{:S(2)}, u32[]{:S(2)}) %collective-permute-start.71) | collective-permute-done | bytes 262176 | tf_op jit(solution)/shard_map/ppermute | solution.py:641
  (677 shorter events, 244.2 us)
Async XLA Ops:
  7.2 97.0 %all-gather.4.cloned.1.call-start = ((), (), s32[]{:S(2)}) async-start(), calls=%async_computation.2 | async-start | bytes 5570560 | tf_op jit(solution)/shard_map/all_gather | solution.py:389
  22.8 183.0 %all-gather.6.cloned.1.call-start = ((), (), s32[]{:S(2)}) async-start(), calls=%async_computation.3 | async-start | bytes 22708224 | tf_op jit(solution)/shard_map/all_gather | solution.py:389
  23.4 26.0 %collective-permute-start.17 = (bf16[128,2688]{1,0:T(8,128)(2,1)S(1)}, bf16[128,2688]{1,0:T(8,128)(2,1)S(1)}, u32[]{:S(2)}, u32[]{:S(2)}) collective-permute-start(bf16[128,2688]{1,0:T(8,128)(2,1)S(1)} %broadcast_select_fusion.1), channel_id=1, source_target_pairs={{0,64},{64,0},{1,65},{65,1},{2,66},{66,2},{3,67},{67,3},{4,68},{68... | collective-permute-start | bytes 2064392 | tf_op jit(solution)/shard_map/ppermute | solution.py:322
  50.9 277.5 %all-gather.8.cloned.1.call-start = ((), (), s32[]{:S(2)}) async-start(), calls=%async_computation.4 | async-start | bytes 17301504 | tf_op jit(solution)/shard_map/all_gather | solution.py:389
  51.8 440.0 %reduce-scatter.3.cloned.1.call-start = ((), (), s32[]{:S(2)}) async-start(), calls=%async_computation.5 | async-start | bytes 430080 | tf_op jit(solution)/shard_map/reduce_scatter | solution.py:525
  52.6 247.0 %collective-permute-start.41 = (bf16[64,2048]{1,0:T(8,128)(2,1)}, bf16[64,2048]{1,0:T(8,128)(2,1)}, u32[]{:S(2)}, u32[]{:S(2)}) collective-permute-start(bf16[64,2048]{1,0:T(8,128)(2,1)} %dynamic-slice_bitcast_fusion), channel_id=1, source_target_pairs={{0,1},{1,2},{2,3},{3,0},{4,5},{5,6},{6,7},{7,4},{8,9},{9,10},{10,1... | collective-permute-start | bytes 786440 | tf_op jit(solution)/shard_map/ppermute | solution.py:31
  53.9 246.3 %collective-permute-start.40 = (bf16[64,2048]{1,0:T(8,128)(2,1)}, bf16[64,2048]{1,0:T(8,128)(2,1)}, u32[]{:S(2)}, u32[]{:S(2)}) collective-permute-start(bf16[64,2048]{1,0:T(8,128)(2,1)} %dynamic-slice_bitcast_fusion), channel_id=1, source_target_pairs={{0,2},{1,3},{2,0},{3,1},{4,6},{5,7},{6,4},{7,5},{8,10},{9,11},{10,... | collective-permute-start | bytes 786440 | tf_op jit(solution)/shard_map/ppermute | solution.py:31
  56.9 18.9 %collective-permute-start = (bf16[1,15104]{1,0:T(2,128)(2,1)S(1)}, bf16[1,15104]{1,0:T(2,128)(2,1)S(1)}, u32[]{:S(2)}, u32[]{:S(2)}) collective-permute-start(bf16[1,15104]{1,0:T(2,128)(2,1)S(1)} %constant_dynamic-update-slice_fusion), channel_id=1, source_target_pairs={{0,64},{64,0},{1,65},{65,1},{2,66},{66,2},{3,67},{67,3},{4,68},{68... | collective-permute-start | bytes 90632 | tf_op jit(solution)/shard_map/ppermute | solution.py:322
  77.0 13.8 %collective-permute-start.2 = (bf16[64,2048]{1,0:T(8,128)(2,1)S(1)}, bf16[64,2048]{1,0:T(8,128)(2,1)S(1)}, u32[]{:S(2)}, u32[]{:S(2)}) collective-permute-start(bf16[64,2048]{1,0:T(8,128)(2,1)S(1)} %fusion.80), channel_id=1, source_target_pairs={{0,2},{1,3},{2,0},{3,1},{4,6},{5,7},{6,4},{7,5},{8,10},{9,11},{10,... | collective-permute-start | bytes 786440 | tf_op jit(solution)/shard_map/ppermute | solution.py:31
  87.3 16.1 %collective-permute-start.10 = (bf16[16,10752]{1,0:T(8,128)(2,1)S(1)}, bf16[16,10752]{1,0:T(8,128)(2,1)S(1)}, u32[]{:S(2)}, u32[]{:S(2)}) collective-permute-start(bf16[16,10752]{1,0:T(8,128)(2,1)S(1)} %get-tuple-element.152), channel_id=1, source_target_pairs={{0,64},{64,0},{1,65},{65,1},{2,66},{66,2},{3,67},{67,3},{4,68},{68... | collective-permute-start | bytes 1032200 | tf_op jit(solution)/shard_map/ppermute | solution.py:322
  130.0 15.4 %collective-permute-start.11 = (bf16[64,2048]{1,0:T(8,128)(2,1)S(1)}, bf16[64,2048]{1,0:T(8,128)(2,1)S(1)}, u32[]{:S(2)}, u32[]{:S(2)}) collective-permute-start(bf16[64,2048]{1,0:T(8,128)(2,1)S(1)} %get-tuple-element.119), channel_id=1, source_target_pairs={{0,1},{1,2},{2,3},{3,0},{4,5},{5,6},{6,7},{7,4},{8,9},{9,10},{10,1... | collective-permute-start | bytes 786440 | tf_op jit(solution)/shard_map/ppermute | solution.py:31
  146.1 15.1 %collective-permute-start.16 = (bf16[64,2048]{1,0:T(8,128)(2,1)S(1)}, bf16[64,2048]{1,0:T(8,128)(2,1)S(1)}, u32[]{:S(2)}, u32[]{:S(2)}) collective-permute-start(bf16[64,2048]{1,0:T(8,128)(2,1)S(1)} %add_convert_fusion.3), channel_id=1, source_target_pairs={{0,1},{1,2},{2,3},{3,0},{4,5},{5,6},{6,7},{7,4},{8,9},{9,10},{10,1... | collective-permute-start | bytes 786440 | tf_op jit(solution)/shard_map/ppermute | solution.py:31
  146.2 15.0 %collective-permute-start.15 = (bf16[64,2048]{1,0:T(8,128)(2,1)S(1)}, bf16[64,2048]{1,0:T(8,128)(2,1)S(1)}, u32[]{:S(2)}, u32[]{:S(2)}) collective-permute-start(bf16[64,2048]{1,0:T(8,128)(2,1)S(1)} %add_convert_fusion.3), channel_id=1, source_target_pairs={{0,2},{1,3},{2,0},{3,1},{4,6},{5,7},{6,4},{7,5},{8,10},{9,11},{10,... | collective-permute-start | bytes 786440 | tf_op jit(solution)/shard_map/ppermute | solution.py:31
  148.7 13.1 %collective-permute-start.14 = (bf16[64,2048]{1,0:T(8,128)(2,1)S(1)}, bf16[64,2048]{1,0:T(8,128)(2,1)S(1)}, u32[]{:S(2)}, u32[]{:S(2)}) collective-permute-start(bf16[64,2048]{1,0:T(8,128)(2,1)S(1)} %add_convert_fusion.3), channel_id=1, source_target_pairs={{0,3},{1,0},{2,1},{3,2},{4,7},{5,4},{6,5},{7,6},{8,11},{9,8},{10,9... | collective-permute-start | bytes 786440 | tf_op jit(solution)/shard_map/ppermute | solution.py:31
  222.7 15.1 %collective-permute-start.18 = (bf16[64,2048]{1,0:T(8,128)(2,1)S(1)}, bf16[64,2048]{1,0:T(8,128)(2,1)S(1)}, u32[]{:S(2)}, u32[]{:S(2)}) collective-permute-start(bf16[64,2048]{1,0:T(8,128)(2,1)S(1)} %get-tuple-element.116), channel_id=1, source_target_pairs={{0,1},{1,2},{2,3},{3,0},{4,5},{5,6},{6,7},{7,4},{8,9},{9,10},{10,1... | collective-permute-start | bytes 786440 | tf_op jit(solution)/shard_map/ppermute | solution.py:31
  241.3 15.2 %collective-permute-start.23 = (bf16[64,2048]{1,0:T(8,128)(2,1)S(1)}, bf16[64,2048]{1,0:T(8,128)(2,1)S(1)}, u32[]{:S(2)}, u32[]{:S(2)}) collective-permute-start(bf16[64,2048]{1,0:T(8,128)(2,1)S(1)} %fusion.73), channel_id=1, source_target_pairs={{0,1},{1,2},{2,3},{3,0},{4,5},{5,6},{6,7},{7,4},{8,9},{9,10},{10,1... | collective-permute-start | bytes 786440 | tf_op jit(solution)/shard_map/ppermute | solution.py:31
  241.4 25.0 %collective-permute-start.22 = (bf16[64,2048]{1,0:T(8,128)(2,1)S(1)}, bf16[64,2048]{1,0:T(8,128)(2,1)S(1)}, u32[]{:S(2)}, u32[]{:S(2)}) collective-permute-start(bf16[64,2048]{1,0:T(8,128)(2,1)S(1)} %fusion.73), channel_id=1, source_target_pairs={{0,2},{1,3},{2,0},{3,1},{4,6},{5,7},{6,4},{7,5},{8,10},{9,11},{10,... | collective-permute-start | bytes 786440 | tf_op jit(solution)/shard_map/ppermute | solution.py:31
  243.7 22.6 %collective-permute-start.21 = (bf16[64,2048]{1,0:T(8,128)(2,1)S(1)}, bf16[64,2048]{1,0:T(8,128)(2,1)S(1)}, u32[]{:S(2)}, u32[]{:S(2)}) collective-permute-start(bf16[64,2048]{1,0:T(8,128)(2,1)S(1)} %fusion.73), channel_id=1, source_target_pairs={{0,3},{1,0},{2,1},{3,2},{4,7},{5,4},{6,5},{7,6},{8,11},{9,8},{10,9... | collective-permute-start | bytes 786440 | tf_op jit(solution)/shard_map/ppermute | solution.py:31
  256.5 43.7 %collective-permute-start.39 = (bf16[64,2048]{1,0:T(8,128)(2,1)}, bf16[64,2048]{1,0:T(8,128)(2,1)}, u32[]{:S(2)}, u32[]{:S(2)}) collective-permute-start(bf16[64,2048]{1,0:T(8,128)(2,1)} %dynamic-slice_bitcast_fusion), channel_id=1, source_target_pairs={{0,3},{1,0},{2,1},{3,2},{4,7},{5,4},{6,5},{7,6},{8,11},{9,8},{10,9... | collective-permute-start | bytes 786440 | tf_op jit(solution)/shard_map/ppermute | solution.py:31
  312.4 15.0 %collective-permute-start.33 = (bf16[64,2048]{1,0:T(8,128)(2,1)S(1)}, bf16[64,2048]{1,0:T(8,128)(2,1)S(1)}, u32[]{:S(2)}, u32[]{:S(2)}) collective-permute-start(bf16[64,2048]{1,0:T(8,128)(2,1)S(1)} %add_convert_fusion.1), channel_id=1, source_target_pairs={{0,1},{1,2},{2,3},{3,0},{4,5},{5,6},{6,7},{7,4},{8,9},{9,10},{10,1... | collective-permute-start | bytes 786440 | tf_op jit(solution)/shard_map/ppermute | solution.py:31
  312.5 14.9 %collective-permute-start.32 = (bf16[64,2048]{1,0:T(8,128)(2,1)S(1)}, bf16[64,2048]{1,0:T(8,128)(2,1)S(1)}, u32[]{:S(2)}, u32[]{:S(2)}) collective-permute-start(bf16[64,2048]{1,0:T(8,128)(2,1)S(1)} %add_convert_fusion.1), channel_id=1, source_target_pairs={{0,2},{1,3},{2,0},{3,1},{4,6},{5,7},{6,4},{7,5},{8,10},{9,11},{10,... | collective-permute-start | bytes 786440 | tf_op jit(solution)/shard_map/ppermute | solution.py:31
  313.4 15.0 %collective-permute-start.31 = (bf16[64,2048]{1,0:T(8,128)(2,1)S(1)}, bf16[64,2048]{1,0:T(8,128)(2,1)S(1)}, u32[]{:S(2)}, u32[]{:S(2)}) collective-permute-start(bf16[64,2048]{1,0:T(8,128)(2,1)S(1)} %add_convert_fusion.1), channel_id=1, source_target_pairs={{0,3},{1,0},{2,1},{3,2},{4,7},{5,4},{6,5},{7,6},{8,11},{9,8},{10,9... | collective-permute-start | bytes 786440 | tf_op jit(solution)/shard_map/ppermute | solution.py:31
  316.4 101.6 %collective-permute-start.37 = (bf16[64,2048]{1,0:T(8,128)(2,1)}, bf16[64,2048]{1,0:T(8,128)(2,1)}, u32[]{:S(2)}, u32[]{:S(2)}) collective-permute-start(bf16[64,2048]{1,0:T(8,128)(2,1)} %get-tuple-element.91), channel_id=1, source_target_pairs={{64,0},{65,1},{66,2},{67,3},{68,4},{69,5},{70,6},{71,7},{72,8},{73... | collective-permute-start | bytes 786440 | tf_op jit(solution)/shard_map/ppermute | solution.py:641
  347.0 34.8 %collective-permute-start.36 = (bf16[64,2048]{1,0:T(8,128)(2,1)S(1)}, bf16[64,2048]{1,0:T(8,128)(2,1)S(1)}, u32[]{:S(2)}, u32[]{:S(2)}) collective-permute-start(bf16[64,2048]{1,0:T(8,128)(2,1)S(1)} %get-tuple-element.111), channel_id=1, source_target_pairs={{0,3},{1,0},{2,1},{3,2},{4,7},{5,4},{6,5},{7,6},{8,11},{9,8},{10,9... | collective-permute-start | bytes 786440 | tf_op jit(solution)/shard_map/ppermute | solution.py:31
  365.9 15.2 %collective-permute-start.42 = (bf16[64,2048]{1,0:T(8,128)(2,1)S(1)}, bf16[64,2048]{1,0:T(8,128)(2,1)S(1)}, u32[]{:S(2)}, u32[]{:S(2)}) collective-permute-start(bf16[64,2048]{1,0:T(8,128)(2,1)S(1)} %get-tuple-element.107), channel_id=1, source_target_pairs={{0,1},{1,2},{2,3},{3,0},{4,5},{5,6},{6,7},{7,4},{8,9},{9,10},{10,1... | collective-permute-start | bytes 786440 | tf_op jit(solution)/shard_map/ppermute | solution.py:31
  373.9 12.9 %collective-permute-start.35 = (bf16[64,2048]{1,0:T(8,128)(2,1)S(1)}, bf16[64,2048]{1,0:T(8,128)(2,1)S(1)}, u32[]{:S(2)}, u32[]{:S(2)}) collective-permute-start(bf16[64,2048]{1,0:T(8,128)(2,1)S(1)} %get-tuple-element.112), channel_id=1, source_target_pairs={{0,2},{1,3},{2,0},{3,1},{4,6},{5,7},{6,4},{7,5},{8,10},{9,11},{10,... | collective-permute-start | bytes 786440 | tf_op jit(solution)/shard_map/ppermute | solution.py:31
  375.6 16.4 %collective-permute-start.34 = (bf16[64,2048]{1,0:T(8,128)(2,1)S(1)}, bf16[64,2048]{1,0:T(8,128)(2,1)S(1)}, u32[]{:S(2)}, u32[]{:S(2)}) collective-permute-start(bf16[64,2048]{1,0:T(8,128)(2,1)S(1)} %get-tuple-element.110), channel_id=1, source_target_pairs={{0,1},{1,2},{2,3},{3,0},{4,5},{5,6},{6,7},{7,4},{8,9},{9,10},{10,1... | collective-permute-start | bytes 786440 | tf_op jit(solution)/shard_map/ppermute | solution.py:31
  381.8 21.0 %collective-permute-start.47 = (bf16[64,2048]{1,0:T(8,128)(2,1)S(1)}, bf16[64,2048]{1,0:T(8,128)(2,1)S(1)}, u32[]{:S(2)}, u32[]{:S(2)}) collective-permute-start(bf16[64,2048]{1,0:T(8,128)(2,1)S(1)} %get-tuple-element.83), channel_id=1, source_target_pairs={{0,1},{1,2},{2,3},{3,0},{4,5},{5,6},{6,7},{7,4},{8,9},{9,10},{10,1... | collective-permute-start | bytes 786440 | tf_op jit(solution)/shard_map/ppermute | solution.py:31
  381.9 21.3 %collective-permute-start.46 = (bf16[64,2048]{1,0:T(8,128)(2,1)S(1)}, bf16[64,2048]{1,0:T(8,128)(2,1)S(1)}, u32[]{:S(2)}, u32[]{:S(2)}) collective-permute-start(bf16[64,2048]{1,0:T(8,128)(2,1)S(1)} %get-tuple-element.83), channel_id=1, source_target_pairs={{0,2},{1,3},{2,0},{3,1},{4,6},{5,7},{6,4},{7,5},{8,10},{9,11},{10,... | collective-permute-start | bytes 786440 | tf_op jit(solution)/shard_map/ppermute | solution.py:31
  386.8 16.3 %collective-permute-start.45 = (bf16[64,2048]{1,0:T(8,128)(2,1)S(1)}, bf16[64,2048]{1,0:T(8,128)(2,1)S(1)}, u32[]{:S(2)}, u32[]{:S(2)}) collective-permute-start(bf16[64,2048]{1,0:T(8,128)(2,1)S(1)} %get-tuple-element.83), channel_id=1, source_target_pairs={{0,3},{1,0},{2,1},{3,2},{4,7},{5,4},{6,5},{7,6},{8,11},{9,8},{10,9... | collective-permute-start | bytes 786440 | tf_op jit(solution)/shard_map/ppermute | solution.py:31
  393.1 26.2 %collective-permute-start.38 = (bf16[64,2048]{1,0:T(8,128)(2,1)S(1)}, bf16[64,2048]{1,0:T(8,128)(2,1)S(1)}, u32[]{:S(2)}, u32[]{:S(2)}) collective-permute-start(bf16[64,2048]{1,0:T(8,128)(2,1)S(1)} %get-tuple-element.87), channel_id=1, source_target_pairs={{0,64},{1,65},{2,66},{3,67},{4,68},{5,69},{6,70},{7,71},{8,72},{9,... | collective-permute-start | bytes 786440 | tf_op jit(solution)/shard_map/ppermute | solution.py:638
  413.2 14.5 %collective-permute-start.51 = (bf16[256,256]{1,0:T(8,128)(2,1)S(1)}, bf16[256,256]{1,0:T(8,128)(2,1)S(1)}, u32[]{:S(2)}, u32[]{:S(2)}) collective-permute-start(bf16[256,256]{1,0:T(8,128)(2,1)S(1)} %get-tuple-element.133), channel_id=1, source_target_pairs={{16,0},{20,4},{24,8},{28,12},{32,16},{36,20},{40,24},{44,28},{48,3... | collective-permute-start | bytes 393224 | tf_op jit(solution)/shard_map/ppermute | solution.py:37
  414.5 13.2 %collective-permute-start.50 = (bf16[256,256]{1,0:T(8,128)(2,1)S(1)}, bf16[256,256]{1,0:T(8,128)(2,1)S(1)}, u32[]{:S(2)}, u32[]{:S(2)}) collective-permute-start(bf16[256,256]{1,0:T(8,128)(2,1)S(1)} %get-tuple-element.134), channel_id=1, source_target_pairs={{12,0},{16,4},{20,8},{24,12},{28,16},{32,20},{36,24},{40,28},{44,3... | collective-permute-start | bytes 393224 | tf_op jit(solution)/shard_map/ppermute | solution.py:37
  432.0 15.8 %collective-permute-start.52 = (bf16[64,2048]{1,0:T(8,128)(2,1)S(1)}, bf16[64,2048]{1,0:T(8,128)(2,1)S(1)}, u32[]{:S(2)}, u32[]{:S(2)}) collective-permute-start(bf16[64,2048]{1,0:T(8,128)(2,1)S(1)} %get-tuple-element.104), channel_id=1, source_target_pairs={{0,1},{1,2},{2,3},{3,0},{4,5},{5,6},{6,7},{7,4},{8,9},{9,10},{10,1... | collective-permute-start | bytes 786440 | tf_op jit(solution)/shard_map/ppermute | solution.py:31
  451.3 15.4 %collective-permute-start.57 = (bf16[64,2048]{1,0:T(8,128)(2,1)}, bf16[64,2048]{1,0:T(8,128)(2,1)S(1)}, u32[]{:S(2)}, u32[]{:S(2)}) collective-permute-start(bf16[64,2048]{1,0:T(8,128)(2,1)} %get-tuple-element.80), channel_id=1, source_target_pairs={{0,1},{1,2},{2,3},{3,0},{4,5},{5,6},{6,7},{7,4},{8,9},{9,10},{10,1... | collective-permute-start | bytes 786440 | tf_op jit(solution)/shard_map/ppermute | solution.py:31
  451.3 15.4 %collective-permute-start.56 = (bf16[64,2048]{1,0:T(8,128)(2,1)}, bf16[64,2048]{1,0:T(8,128)(2,1)S(1)}, u32[]{:S(2)}, u32[]{:S(2)}) collective-permute-start(bf16[64,2048]{1,0:T(8,128)(2,1)} %get-tuple-element.80), channel_id=1, source_target_pairs={{0,2},{1,3},{2,0},{3,1},{4,6},{5,7},{6,4},{7,5},{8,10},{9,11},{10,... | collective-permute-start | bytes 786440 | tf_op jit(solution)/shard_map/ppermute | solution.py:31
  452.3 15.0 %collective-permute-start.55 = (bf16[64,2048]{1,0:T(8,128)(2,1)}, bf16[64,2048]{1,0:T(8,128)(2,1)S(1)}, u32[]{:S(2)}, u32[]{:S(2)}) collective-permute-start(bf16[64,2048]{1,0:T(8,128)(2,1)} %get-tuple-element.80), channel_id=1, source_target_pairs={{0,3},{1,0},{2,1},{3,2},{4,7},{5,4},{6,5},{7,6},{8,11},{9,8},{10,9... | collective-permute-start | bytes 786440 | tf_op jit(solution)/shard_map/ppermute | solution.py:31
  455.4 133.6 %reduce-scatter.5.cloned.1.call-start = ((), (), s32[]{:S(2)}) async-start(), calls=%async_computation.6 | async-start | bytes 278528 | tf_op jit(solution)/shard_map/reduce_scatter | solution.py:526
  455.5 156.6 %collective-permute-start.72 = (bf16[64,2048]{1,0:T(8,128)(2,1)}, bf16[64,2048]{1,0:T(8,128)(2,1)}, u32[]{:S(2)}, u32[]{:S(2)}) collective-permute-start(bf16[64,2048]{1,0:T(8,128)(2,1)} %get-tuple-element.80), channel_id=1, source_target_pairs={{0,64},{1,65},{2,66},{3,67},{4,68},{5,69},{6,70},{7,71},{8,72},{9,... | collective-permute-start | bytes 786440 | tf_op jit(solution)/shard_map/ppermute | solution.py:638
  486.8 13.7 %collective-permute-start.60 = (bf16[64,2048]{1,0:T(8,128)(2,1)}, bf16[64,2048]{1,0:T(8,128)(2,1)S(1)}, u32[]{:S(2)}, u32[]{:S(2)}) collective-permute-start(bf16[64,2048]{1,0:T(8,128)(2,1)} %get-tuple-element.102), channel_id=1, source_target_pairs={{0,3},{1,0},{2,1},{3,2},{4,7},{5,4},{6,5},{7,6},{8,11},{9,8},{10,9... | collective-permute-start | bytes 786440 | tf_op jit(solution)/shard_map/ppermute | solution.py:31
  489.1 14.8 %collective-permute-start.58 = (bf16[64,2048]{1,0:T(8,128)(2,1)}, bf16[64,2048]{1,0:T(8,128)(2,1)}, u32[]{:S(2)}, u32[]{:S(2)}) collective-permute-start(bf16[64,2048]{1,0:T(8,128)(2,1)} %get-tuple-element.101), channel_id=1, source_target_pairs={{0,1},{1,2},{2,3},{3,0},{4,5},{5,6},{6,7},{7,4},{8,9},{9,10},{10,1... | collective-permute-start | bytes 786440 | tf_op jit(solution)/shard_map/ppermute | solution.py:31
  506.3 14.8 %collective-permute-start.63 = (bf16[64,2048]{1,0:T(8,128)(2,1)S(1)}, bf16[64,2048]{1,0:T(8,128)(2,1)S(1)}, u32[]{:S(2)}, u32[]{:S(2)}) collective-permute-start(bf16[64,2048]{1,0:T(8,128)(2,1)S(1)} %get-tuple-element.77), channel_id=1, source_target_pairs={{0,1},{1,2},{2,3},{3,0},{4,5},{5,6},{6,7},{7,4},{8,9},{9,10},{10,1... | collective-permute-start | bytes 786440 | tf_op jit(solution)/shard_map/ppermute | solution.py:31
  506.4 14.7 %collective-permute-start.62 = (bf16[64,2048]{1,0:T(8,128)(2,1)S(1)}, bf16[64,2048]{1,0:T(8,128)(2,1)S(1)}, u32[]{:S(2)}, u32[]{:S(2)}) collective-permute-start(bf16[64,2048]{1,0:T(8,128)(2,1)S(1)} %get-tuple-element.77), channel_id=1, source_target_pairs={{0,2},{1,3},{2,0},{3,1},{4,6},{5,7},{6,4},{7,5},{8,10},{9,11},{10,... | collective-permute-start | bytes 786440 | tf_op jit(solution)/shard_map/ppermute | solution.py:31
  508.7 13.0 %collective-permute-start.61 = (bf16[64,2048]{1,0:T(8,128)(2,1)S(1)}, bf16[64,2048]{1,0:T(8,128)(2,1)S(1)}, u32[]{:S(2)}, u32[]{:S(2)}) collective-permute-start(bf16[64,2048]{1,0:T(8,128)(2,1)S(1)} %get-tuple-element.77), channel_id=1, source_target_pairs={{0,3},{1,0},{2,1},{3,2},{4,7},{5,4},{6,5},{7,6},{8,11},{9,8},{10,9... | collective-permute-start | bytes 786440 | tf_op jit(solution)/shard_map/ppermute | solution.py:31
  533.3 12.3 %collective-permute-start.67 = (bf16[256,256]{1,0:T(8,128)(2,1)S(1)}, bf16[256,256]{1,0:T(8,128)(2,1)S(1)}, u32[]{:S(2)}, u32[]{:S(2)}) collective-permute-start(bf16[256,256]{1,0:T(8,128)(2,1)S(1)} %get-tuple-element.129), channel_id=1, source_target_pairs={{16,0},{20,4},{24,8},{28,12},{32,16},{36,20},{40,24},{44,28},{48,3... | collective-permute-start | bytes 393224 | tf_op jit(solution)/shard_map/ppermute | solution.py:37
  561.7 15.2 %collective-permute-start.68 = (bf16[64,2048]{1,0:T(8,128)(2,1)S(1)}, bf16[64,2048]{1,0:T(8,128)(2,1)S(1)}, u32[]{:S(2)}, u32[]{:S(2)}) collective-permute-start(bf16[64,2048]{1,0:T(8,128)(2,1)S(1)} %get-tuple-element.98), channel_id=1, source_target_pairs={{0,1},{1,2},{2,3},{3,0},{4,5},{5,6},{6,7},{7,4},{8,9},{9,10},{10,1... | collective-permute-start | bytes 786440 | tf_op jit(solution)/shard_map/ppermute | solution.py:31
  563.3 13.9 %collective-permute-start.77 = (bf16[4,4,16,128]{3,2,1,0:T(8,128)(2,1)S(1)}, bf16[4,4,16,128]{3,2,1,0:T(8,128)(2,1)S(1)}, u32[]{:S(2)}, u32[]{:S(2)}) collective-permute-start(bf16[4,4,16,128]{3,2,1,0:T(8,128)(2,1)S(1)} %dynamic-slice_bitcast_fusion.6), channel_id=1, source_target_pairs={{0,8},{4,12},{8,0},{12,4},{16,24},{20,28},{24,16},{28,20},{32,40},... | collective-permute-start | bytes 196616 | tf_op jit(solution)/shard_map/ppermute | solution.py:42
  577.3 12.6 %collective-permute-start.80 = (bf16[4,16,128]{2,1,0:T(8,128)(2,1)S(1)}, bf16[4,16,128]{2,1,0:T(8,128)(2,1)S(1)}, u32[]{:S(2)}, u32[]{:S(2)}) collective-permute-start(bf16[4,16,128]{2,1,0:T(8,128)(2,1)S(1)} %get-tuple-element.208), channel_id=1, source_target_pairs={{0,48},{4,52},{8,56},{12,60},{16,32},{20,36},{24,40},{28,44},{32,1... | collective-permute-start | bytes 49160 | tf_op jit(solution)/shard_map/ppermute | solution.py:42
  (175 other events, 2374.8 us)
Sparse Core Ops, SparseCore 0:
  23.0 48.2 all-gather.3
  73.6 132.2 all-gather.5
  208.1 99.9 all-gather.7
  455.6 30.5 reduce-scatter.2
  510.5 71.0 reduce-scatter.4

commit v4 on v3

--- a/solution.py
+++ b/solution.py
@@ -66,99 +66,135 @@
     return value * rising, slope
 
 
-def attend_kernel(scale, query_ref, keyval_ref, bias_ref, prob_ref, mixed_ref):
-    head = query_ref.shape[1]
-    scores = against(query_ref[...], keyval_ref[:, :head]) * scale + bias_ref[...].astype(f32)
-    top = jnp.max(scores, axis=-1, keepdims=True)
-    lifted = jnp.exp(scores - top)
-    total = jnp.sum(lifted, axis=-1, keepdims=True)
-    probs = lifted * (1.0 / total)
-    prob_ref[0] = probs
-    mixed_ref[...] = plain(probs.astype(bf16), keyval_ref[:, head:]).astype(bf16)
-
-
-def attend(queries, key_block, bias, head):
+def attend_kernel(
+    head, query_ref, keyval_ref, bias_ref, out_ref, so_ref, eo_ref,
+    prob_ref, mixed_ref, low_ref, part_ref,
+):
+    scale = 1.0 / math.sqrt(head)
+    bias = bias_ref[...].astype(f32)
+    for h in range(query_ref.shape[1] // head):
+        columns = pl.ds(h * head, head)
+        scores = against(query_ref[:, columns], keyval_ref[:, :head]) * scale + bias
+        lifted = jnp.exp(scores - jnp.max(scores, axis=-1, keepdims=True))
+        probs = lifted * (1.0 / jnp.sum(lifted, axis=-1, keepdims=True))
+        prob_ref[h] = probs
+        mixed_ref[:, columns] = plain(probs.astype(bf16), keyval_ref[:, head:]).astype(bf16)
+    mixed = mixed_ref[...]
+    low = against(mixed, so_ref[...]).astype(bf16)
+    low_ref[...] = low
+    part_ref[...] = (against(mixed, out_ref[...]) + plain(low, eo_ref[...])).astype(bf16)
+
+
+def attend(queries, key_block, bias, out_w, so, eo, head):
     rows, width = queries.shape
     keys = key_block.shape[0]
     heads = width // head
-    whole = lambda shape: pl.BlockSpec(shape, lambda h: (0, 0))
-    column = pl.BlockSpec((rows, head), lambda h: (0, h))
+    rank = so.shape[0]
+    model = out_w.shape[0]
+    held = pl.BlockSpec(memory_space=pltpu.VMEM)
     return pl.pallas_call(
-        lambda *refs: attend_kernel(1.0 / math.sqrt(head), *refs),
-        grid=(heads,),
-        in_specs=[column, whole((keys, 2 * head)), whole((rows, keys))],
-        out_specs=[pl.BlockSpec((1, rows, keys), lambda h: (h, 0, 0)), column],
+        lambda *refs: attend_kernel(head, *refs),
+        in_specs=[held] * 6,
+        out_specs=[held] * 4,
         out_shape=[
             jax.ShapeDtypeStruct((heads, rows, keys), f32),
             jax.ShapeDtypeStruct((rows, width), bf16),
+            jax.ShapeDtypeStruct((rows, rank), bf16),
+            jax.ShapeDtypeStruct((rows, model), bf16),
         ],
-        compiler_params=pltpu.CompilerParams(vmem_limit_bytes=40 * 2**20),
+        compiler_params=pltpu.CompilerParams(vmem_limit_bytes=32 * 2**20),
+        cost_estimate=pl.CostEstimate(
+            flops=2 * rows * width * (2 * keys + model),
+            bytes_accessed=4 * heads * rows * keys,
+            transcendentals=heads * rows * keys,
+        ),
         name="attend",
-    )(queries, key_block, bias)
+    )(queries, key_block, bias, out_w, so, eo)
 
 
 def attend_back_kernel(
-    scale, grad_ref, prob_ref, query_ref, keyval_ref, dq_ref, dkv_ref, key_sum, value_sum
+    head, branch_ref, out_ref, so_ref, eo_ref, prob_ref, query_ref, keyval_ref, qw_ref, eq_ref, sq_ref,
+    dq_ref, dkv_ref, inner_o_ref, inner_q_ref, part_ref, key_sum, value_sum,
 ):
-    step = pl.program_id(0)
-    head = query_ref.shape[1]
-    grad = grad_ref[...]
-    probs = prob_ref[0]
-    grad_probs = against(grad, keyval_ref[:, head:])
-    delta = jnp.sum(grad_probs * probs, axis=-1, keepdims=True)
-    grad_scores = (probs * (grad_probs - delta)).astype(bf16)
-    dq_ref[...] = (plain(grad_scores, keyval_ref[:, :head]) * scale).astype(bf16)
-    keys = across(grad_scores, query_ref[...])
-    values = across(probs.astype(bf16), grad)
-
-    @pl.when(step == 0)
-    def _():
-        key_sum[...] = keys
-        value_sum[...] = values
-
-    @pl.when(step > 0)
-    def _():
-        key_sum[...] += keys
-        value_sum[...] += values
-
-    @pl.when(step == pl.num_programs(0) - 1)
-    def _():
-        dkv_ref[:, :head] = (key_sum[...] * scale).astype(bf16)
-        dkv_ref[:, head:] = value_sum[...].astype(bf16)
-
-
-def attend_back(grad_mixed, probs, queries, key_block, head):
+    scale = 1.0 / math.sqrt(head)
+    branch = branch_ref[...]
+    inner_o = against(branch, eo_ref[...]).astype(bf16)
+    inner_o_ref[...] = inner_o
+    grad_mixed = (plain(branch, out_ref[...]) + plain(inner_o, so_ref[...])).astype(bf16)
+    for h in range(query_ref.shape[1] // head):
+        columns = pl.ds(h * head, head)
+        grad = grad_mixed[:, h * head : (h + 1) * head]
+        probs = prob_ref[h]
+        grad_probs = against(grad, keyval_ref[:, head:])
+        delta = jnp.sum(grad_probs * probs, axis=-1, keepdims=True)
+        grad_scores = (probs * (grad_probs - delta)).astype(bf16)
+        dq_ref[:, columns] = (plain(grad_scores, keyval_ref[:, :head]) * scale).astype(bf16)
+        keys = across(grad_scores, query_ref[:, columns])
+        values = across(probs.astype(bf16), grad)
+        if h == 0:
+            key_sum[...] = keys
+            value_sum[...] = values
+        else:
+            key_sum[...] += keys
+            value_sum[...] += values
+    dkv_ref[:, :head] = (key_sum[...] * scale).astype(bf16)
+    dkv_ref[:, head:] = value_sum[...].astype(bf16)
+    grad_q = dq_ref[...]
+    inner_q = against(grad_q, eq_ref[...]).astype(bf16)
+    inner_q_ref[...] = inner_q
+    part_ref[...] = against(grad_q, qw_ref[...]) + plain(inner_q, sq_ref[...])
+
+
+def attend_back(branch, out_w, so, eo, probs, queries, key_block, query_w, eq, sq, head):
     rows, width = queries.shape
     keys = key_block.shape[0]
     heads = width // head
-    column = pl.BlockSpec((rows, head), lambda h: (0, h))
-    whole = pl.BlockSpec((keys, 2 * head), lambda h: (0, 0))
+    rank, model = eo.shape
+    held = pl.BlockSpec(memory_space=pltpu.VMEM)
     return pl.pallas_call(
-        lambda *refs: attend_back_kernel(1.0 / math.sqrt(head), *refs),
-        grid=(heads,),
-        in_specs=[
-            column,
-            pl.BlockSpec((1, rows, keys), lambda h: (h, 0, 0)),
-            column,
-            whole,
-        ],
-        out_specs=[column, whole],
+        lambda *refs: attend_back_kernel(head, *refs),
+        in_specs=[held] * 10,
+        out_specs=[held] * 5,
         out_shape=[
             jax.ShapeDtypeStruct((rows, width), bf16),
             jax.ShapeDtypeStruct((keys, 2 * head), bf16),
+            jax.ShapeDtypeStruct((rows, rank), bf16),
+            jax.ShapeDtypeStruct((rows, rank), bf16),
+            jax.ShapeDtypeStruct((rows, model), f32),
         ],
         scratch_shapes=[pltpu.VMEM((keys, head), f32), pltpu.VMEM((keys, head), f32)],
-        compiler_params=pltpu.CompilerParams(vmem_limit_bytes=40 * 2**20),
+        compiler_params=pltpu.CompilerParams(vmem_limit_bytes=32 * 2**20),
+        cost_estimate=pl.CostEstimate(
+            flops=2 * rows * width * (4 * keys + 2 * model),
+            bytes_accessed=4 * heads * rows * keys + 8 * model * width,
+            transcendentals=0,
+        ),
         name="attend_back",
-    )(grad_mixed, probs, queries, key_block)
+    )(branch, out_w, so, eo, probs, queries, key_block, query_w, eq, sq)
 
 
 def weight_tile(table_ref, hidden, tile, j, second):
-    width = table_ref.shape[0] // 2
     half = hidden // 2
-    row = j * tile // half * width
     column = j * tile % half + second * half
-    return table_ref[row : row + width, column : column + tile]
+    return [
+        table_ref[chunk, j * tile // half, :, column : column + tile]
+        for chunk in range(table_ref.shape[0])
+    ]
+
+
+def plain_chunks(left, tables):
+    rows = tables[0].shape[0]
+    return sum(plain(left[:, i * rows : (i + 1) * rows], t) for i, t in enumerate(tables))
+
+
+def add_against(total, left, tables, first):
+    rows = tables[0].shape[0]
+    for i, table in enumerate(tables):
+        columns = pl.ds(i * rows, rows)
+        if first:
+            total[:, columns] = against(left, table)
+        else:
+            total[:, columns] += against(left, table)
 
 
 def feed_kernel(
@@ -173,21 +209,17 @@
     low = 0.0
     for j in range(count):
         columns = pl.ds(j * tile, tile)
-        upward = plain(second, weight_tile(table_ref, hidden, tile, j, 0))
+        upward = plain_chunks(second, weight_tile(table_ref, hidden, tile, j, 0))
         upward = upward + plain(low_u, eu_ref[:, columns]) + bias_ref[:, columns]
         active, slope = gelu_parts(upward)
         active = active.astype(bf16)
         active_ref[:, columns] = active
         slope_ref[:, columns] = slope.astype(bf16)
         low = low + against(active, sd_ref[:, columns])
-        part = against(active, weight_tile(table_ref, hidden, tile, j, 1))
-        if j == 0:
-            total[...] = part
-        elif j < count - 1:
-            total[...] += part
+        add_against(total, active, weight_tile(table_ref, hidden, tile, j, 1), j == 0)
     low_d = low.astype(bf16)
     low_d_ref[...] = low_d
-    out_ref[...] = (total[...] + part + plain(low_d, ed_ref[...])).astype(bf16)
+    out_ref[...] = (total[...] + plain(low_d, ed_ref[...])).astype(bf16)
 
 
 def feed_limit(table):
@@ -232,19 +264,15 @@
     inner = 0.0
     for j in range(count):
         columns = pl.ds(j * tile, tile)
-        grad = plain(branch, weight_tile(table_ref, hidden, tile, j, 1))
+        grad = plain_chunks(branch, weight_tile(table_ref, hidden, tile, j, 1))
         grad = grad + plain(inner_d, sd_ref[:, columns])
         grad = (grad * slope_ref[:, columns].astype(f32)).astype(bf16)
         grad_up_ref[:, columns] = grad
         inner = inner + against(grad, eu_ref[:, columns])
-        part = against(grad, weight_tile(table_ref, hidden, tile, j, 0))
-        if j == 0:
-            total[...] = part
-        elif j < count - 1:
-            total[...] += part
+        add_against(total, grad, weight_tile(table_ref, hidden, tile, j, 0), j == 0)
     inner_u = inner.astype(bf16)
     inner_u_ref[...] = inner_u
-    out_ref[...] = (total[...] + part + plain(inner_u, su_ref[...])).astype(bf16)
+    out_ref[...] = (total[...] + plain(inner_u, su_ref[...])).astype(bf16)
 
 
 def feed_back(branch, table, slope, eu, sd, su, ed):
@@ -384,35 +412,34 @@
     vector_sizes = [width, width, local_q, 2 * head, width, width, width, local_f, width]
 
     both = ("section", "dp")
-
-    def gather(shard, axes):
-        return lax.all_gather(shard, axes, axis=0, tiled=True)
+    chips = lax.axis_size("dp") // 4
+    order = [
+        side * 4 * chips + chip * 4 + near
+        for chip in range(chips)
+        for side in range(2)
+        for near in range(4)
+    ]
+
+    def gather(shard):
+        table = lax.all_gather(shard, both, axis=0, tiled=True, axis_index_groups=[order])
+        return table.reshape(chips, 2, -1, shard.shape[1])
 
     def halves(shard):
         cut = shard.shape[1] // 2
         return shard[:, :cut], shard[:, cut:]
 
-    shard_early = jnp.concatenate(
-        [query_weight[0], keyval_weight[0], output_weight[0].T], axis=1
+    early_all = gather(
+        jnp.concatenate([query_weight[0], keyval_weight[0], output_weight[0].T], axis=1)
     )
-    early_zero = gather(jnp.where(low_section, shard_early, swap(shard_early)), "dp")
     vector_layers = by_layer(vectors, swap(vectors))
     early_layers = by_layer(early_pack(own_bank), swap(early_pack(other_bank)))
     late_layers = by_layer(late_pack(own_bank), swap(late_pack(other_bank)))
     up_halves = halves(upward_weight[0])
     down_halves = halves(downward_weight[0].T)
-    early_halves = halves(shard_early)
-    side = [
-        jnp.concatenate([up_halves[h], down_halves[h], early_halves[h]], axis=1) for h in range(2)
-    ]
+    side = [jnp.concatenate([up_halves[h], down_halves[h]], axis=1) for h in range(2)]
     keep = jnp.where(low_section, side[0], side[1])
     gained = swap(jnp.where(low_section, side[1], side[0]))
-    side_zero, side_one = by_layer(keep, gained)
-    feed_zero = gather(
-        jnp.concatenate([side_zero[:, :local_f], side_one[:, local_f:]], axis=1), both
-    )
-    feed_one = gather(side_one[:, :local_f], both)
-    early_one = jnp.concatenate([feed_zero[:width, local_f:], feed_zero[width:, local_f:]], axis=1)
+    feed_zero, feed_one = [gather(table) for table in by_layer(keep, gained)]
 
     def split(table, sizes):
         cuts = [0]
@@ -422,8 +449,13 @@
 
     wide = local_q + 2 * head
     weights = [
-        split(early, [wide, local_q]) + [table]
-        for early, table in [(early_zero, feed_zero), (early_one, feed_one)]
+        (
+            early_all[:, layer, :, :local_q].reshape(width, -1),
+            early_all[:, layer, :, local_q:wide].reshape(width, -1),
+            early_all[:, layer, :, wide:].reshape(width, -1),
+            table,
+        )
+        for layer, table in enumerate([feed_zero, feed_one])
     ]
     small = [
         [part.astype(f32) for part in split(vector_layers[layer], vector_sizes)]
@@ -455,21 +487,19 @@
     bias = jnp.where(allowed, 0.0, masked_score).astype(bf16)
 
     def forward(layer, hidden):
-        qkv_w, out_w, feed_w = weights[layer]
+        query_w, keyval_w, out_w, feed_w = weights[layer]
         gain1, shift1, q_bias, kv_bias, out_bias, gain2, shift2, up_bias, down_bias = small[layer]
         sq, skv, eq, ekv, so, eo, su, eu, sd, ed = adapters[layer]
         unit1, rsd1 = norm_parts(hidden)
         normed = spread((unit1 * gain1 + shift1).astype(bf16))
         low_q = against(normed, sq).astype(bf16)
         low_kv = against(normed, skv).astype(bf16)
-        both = plain(normed, qkv_w)
-        keyval = (both[:, local_q:] + kv_bias + plain(low_kv, ekv)).astype(bf16)
+        keyval = (plain(normed, keyval_w) + kv_bias + plain(low_kv, ekv)).astype(bf16)
         pieces = [along(keyval, "dp", back) for back in range(reach, 0, -1)] + [keyval]
-        queries = (both[:, :local_q] + q_bias + plain(low_q, eq)).astype(bf16)
+        queries = (plain(normed, query_w) + q_bias + plain(low_q, eq)).astype(bf16)
         key_block = jnp.concatenate(pieces, axis=0)
-        probs, mixed = attend(queries, key_block, bias, head)
-        low_o = against(mixed, so).astype(bf16)
-        attended = reduce_rows(against(mixed, out_w) + plain(low_o, eo))
+        probs, mixed, low_o, partial = attend(queries, key_block, bias, out_w, so, eo, head)
+        attended = reduce_rows(partial)
         middle = hidden + (attended + out_bias)
         unit2, rsd2 = norm_parts(middle)
         second = spread((unit2 * gain2 + shift2).astype(bf16))
@@ -502,8 +532,7 @@
     def flat(block):
         return block.transpose(1, 0, 2).reshape(rank, -1)
 
-    chips = lax.axis_size("dp") // 4
-    turn, plane, core = data // 4, data // 2 % 2, data % 2
+    turn, near = data // 4, data % 4
 
     def padded(pile, multiple):
         lack = -pile.shape[0] % multiple
@@ -533,24 +562,35 @@
             block = pick(pile, ((tensor + j) % ranks) * each, each)
             mine = mine + around(block, "tensor", j).astype(f32)
         pile = owned_pile(mine, owned)
-        pile = pile.reshape((chips, 2, 2, -1) + pile.shape[1:])
-        got = flipped(at(pile, 1 - core, 2), "dp", 1)
-        pile = (at(pile, core, 2).astype(f32) + got.astype(f32)).astype(bf16)
-        got = flipped(at(pile, 1 - plane, 1), "dp", 2)
-        pile = (at(pile, plane, 1).astype(f32) + got.astype(f32)).astype(bf16)
+        pile = pile.reshape((chips, 4, -1) + pile.shape[1:])
+        mine = at(pile, near, 1).astype(f32)
+        for k in range(1, 4):
+            mine = mine + flipped(at(pile, near ^ k, 1), "dp", k).astype(f32)
+        pile = mine.astype(bf16)
         mine = at(pile, turn, 0).astype(f32)
         for k in range(1, chips):
             mine = mine + flipped(at(pile, turn ^ k, 0), "dp", 4 * k).astype(f32)
         return mine.astype(bf16)
 
-    def spread_grads(pair, shared_sizes, owned_sizes):
+    def crossed(block, mask):
+        return lax.ppermute(block, both, [(i, i ^ mask) for i in range(8 * chips)])
+
+    def spread_grads(zero, one, shared_sizes, owned_sizes):
+        own = jnp.where(low_section, zero, one)
+        away = jnp.where(low_section, one, zero)
+        dp_size = 4 * chips
+        home = jnp.stack([own, flipped(own, "dp", 2)])
+        guest = jnp.stack([crossed(away, dp_size), crossed(away, dp_size + 2)])
+        home, guest = [
+            jnp.where(near // 2 == 0, block, block[::-1]) for block in (home, guest)
+        ]
+        pair = jnp.where(
+            low_section, jnp.stack([home, guest], axis=1), jnp.stack([guest, home], axis=1)
+        )
         parts = jnp.stack([pair] + [flipped(pair, "dp", 4 * k) for k in range(1, chips)])
         parts = jnp.stack([at(parts, turn ^ k, 0) for k in range(chips)])
-        other = flipped(parts, "dp", 2)
-        parts = jnp.stack(
-            [jnp.where(plane == 0, parts, other), jnp.where(plane == 0, other, parts)], axis=1
-        )
         other = flipped(parts, "dp", 1)
+        core = near % 2
         parts = jnp.stack(
             [jnp.where(core == 0, parts, other), jnp.where(core == 0, other, parts)], axis=2
         )
@@ -568,7 +608,7 @@
         return results
 
     def backward_feed(layer, kept, grad):
-        feed_w = weights[layer][2]
+        feed_w = weights[layer][3]
         gain2 = small[layer][5]
         su, eu, sd, ed = adapters[layer][6:]
         unit2, rsd2, second, low_u, active, slope, low_d = kept[10:]
@@ -581,27 +621,21 @@
         return grad_middle, shared, owned
 
     def backward_attend(layer, kept, grad_middle):
-        qkv_w, out_w = weights[layer][:2]
+        query_w, keyval_w, out_w = weights[layer][:3]
         gain1 = small[layer][0]
         sq, skv, eq, ekv, so, eo = adapters[layer][:6]
         unit1, rsd1, normed, low_q, low_kv, queries, key_block, probs, mixed, low_o = kept[:10]
         branch = spread(grad_middle.astype(bf16))
-        inner_o = against(branch, eo).astype(bf16)
-        grad_mixed = (plain(branch, out_w) + plain(inner_o, so)).astype(bf16)
-        grad_q, grad_block = attend_back(grad_mixed, probs, queries, key_block, head)
+        grad_q, grad_block, inner_o, inner_q, partial = attend_back(
+            branch, out_w, so, eo, probs, queries, key_block, query_w, eq, sq, head
+        )
         own = grad_block[reach * span :].astype(f32)
         for back in range(1, reach + 1):
             begin = (reach - back) * span
             own = own + along(grad_block[begin : begin + span], "dp", -back).astype(f32)
         grad_kv = own.astype(bf16)
-        inner_q = against(grad_q, eq).astype(bf16)
         inner_kv = against(grad_kv, ekv).astype(bf16)
-        grad_normed = (
-            against(grad_q, qkv_w[:, :local_q])
-            + plain(inner_q, sq)
-            + against(grad_kv, qkv_w[:, local_q:])
-            + plain(inner_kv, skv)
-        )
+        grad_normed = partial + against(grad_kv, keyval_w) + plain(inner_kv, skv)
         grad_hidden = grad_middle + norm_back(unit1, rsd1, reduce_rows(grad_normed) * gain1)
         out_grads = ([across(low_o, branch)], [across(inner_o, mixed)])
         shared = [across(inner_q, normed), across(inner_kv, normed), across(low_kv, grad_kv)]
@@ -626,36 +660,21 @@
     shared = feed_shared + out_zero_grads[0] + qkv_zero_grads[0]
     owned = feed_owned + out_zero_grads[1] + qkv_zero_grads[1]
     mine_zero = scattered_grads(shared, owned)
-    received = swap(jnp.where(low_section, mine_one, mine_zero))
-    pair = jnp.where(
-        low_section, jnp.stack([mine_zero, received]), jnp.stack([received, mine_one])
+    grads = spread_grads(
+        mine_zero,
+        mine_one,
+        [part.shape[1] for part in shared],
+        [part.shape[1] for part in owned],
     )
-    grads = spread_grads(
-        pair, [part.shape[1] for part in shared], [part.shape[1] for part in owned]
-    )
-
-    def to_upper(value):
-        return lax.ppermute(value, "section", [(0, 1)])
-
-    def to_lower(value):
-        return lax.ppermute(value, "section", [(1, 0)])
-
-    def both_micros(zero, one):
-        received = jnp.where(low_section, to_lower(zero), to_upper(one))
+
+    def both_micros(zero, one, kind):
         own = jnp.where(low_section, zero, one)
-        return jnp.where(
-            low_section, jnp.stack([own, received]), jnp.stack([received, own])
-        )
-
-    section_outputs = both_micros(passed, final)
-    received = jnp.where(
-        low_section, to_lower(grad_zero.astype(bf16)), to_upper(grad_one.astype(bf16))
-    ).astype(f32)
-    own = jnp.where(low_section, grad_zero, grad_one)
-    input_grads = jnp.where(
-        low_section, jnp.stack([own, received]), jnp.stack([received, own])
-    )
-
+        received = swap(jnp.where(low_section, one, zero).astype(bf16)).astype(kind)
+        return jnp.where(low_section, jnp.stack([own, received]), jnp.stack([received, own]))
+
+    passed, final, _ = lax.optimization_barrier((passed, final, grad_middle_zero))
+    section_outputs = both_micros(passed, final, bf16)
+    input_grads = both_micros(grad_zero, grad_one, f32)
     onehot = (bank_choice[:, None] == jnp.arange(banks)[None, :]).astype(f32)
 
     def placed(pair, transpose):

time: 649 us -> 604 us (0.931)
  local copies, waits for them, and re-layouts: 40.2 us -> 109 us
  waiting for transfers between devices: 274 us -> 208 us
  matrix products: 40.3 us -> 17.9 us
  Pallas kernels: 69.2 us -> 55.6 us
  other arithmetic: 39.8 us -> 32.6 us
    all_gather x0 -> x2, local copies, waits for them, and re-layouts: none -> 45.4 us  [gather(): lax.all_gather(shard, both, axis=0, tiled=True, axis_index_groups=[order])]
    ppermute x6, waiting for transfers between devices: 46.3 us -> 14.3 us  [swap(): return lax.ppermute(value, 'section', sides)]
    unnamed x301 -> x313, local copies, waits for them, and re-layouts: 25.4 us -> 46.1 us
    ppermute x4 -> x2, starting transfers between devices: 20.6 us -> 3.56 us  [crossed(): return lax.ppermute(block, both, [(i, i ^ mask) for i in range(8 * chips)])]
    ppermute x54, waiting for transfers between devices: 148 us -> 131 us  [around(): lax.ppermute(block, axis, [(i, (i + distance) % size) for i in range(size)])]
    all_gather x3, waiting for transfers between devices: 43.9 us -> 29.6 us  [gather(): lax.all_gather(shard, both, axis=0, tiled=True, axis_index_groups=[order])]
    dot_general x18 -> x8, matrix products: 17.9 us -> 3.57 us  [against(): lax.dot_general(left, right, (((1,), (1,)), ((), ())), preferred_element_...]
    ppermute x54, starting transfers between devices: 67.7 us -> 80.4 us  [around(): lax.ppermute(block, axis, [(i, (i + distance) % size) for i in range(size)])]
  transfers between devices with their start and end apart: 95 -> 94, of which waited for: 59 -> 54; matrix products, arithmetic and copies ran while one was open for 13% -> 19% of each run, Pallas kernels for 11% -> 5%
where the time goes in v4:
time: 604 us; the launch traced here: 596 us
  waiting for transfers between devices  208 us (34%)
  starting transfers between devices  152 us (25%)
  local copies, waits for them, and re-layouts  109 us (18%)
  Pallas kernels  55.6 us (9%)
  other arithmetic  32.6 us (5%)
  between operations  20.8 us (3%)
  matrix products  17.9 us (3%)
    ppermute x54, waiting for transfers between devices, around(): lax.ppermute(block, axis, [(i, (i + distance) % size) for i in range(size)])  131 us
    ppermute x54, starting transfers between devices, around(): lax.ppermute(block, axis, [(i, (i + distance) % size) for i in range(size)])  80.4 us
    unnamed x313, local copies, waits for them, and re-layouts  46.1 us
    all_gather x2, local copies, waits for them, and re-layouts, gather(): lax.all_gather(shard, both, axis=0, tiled=True, axis_index_groups=[order])  45.4 us
    ppermute x16, starting transfers between devices, along(): return lax.ppermute(block, axis, route)  35.6 us
    all_gather x3, waiting for transfers between devices, gather(): lax.all_gather(shard, both, axis=0, tiled=True, axis_index_groups=[order])  29.6 us
    ppermute x16, waiting for transfers between devices, along(): return lax.ppermute(block, axis, route)  20.4 us
    ppermute x11, starting transfers between devices, flipped(): return lax.ppermute(block, axis, [(i, i ^ bit) for i in range(size)])  17.5 us
  transfers between devices with their start and end apart: 94, of which 54 were waited for; matrix products, arithmetic and copies ran while one was open for 19% of the time, Pallas kernels for 5%

profile of v4, /device:TPU:0, one launch (start us, length us, event | category | flops | bytes accessed | tf_op | source)
XLA Modules:
  0.0 595.7 jit_solution(9455434347785929296)
XLA Ops:
  11.8 4.0 collective-permute-start.16
  15.8 12.9 %collective-permute-done.16 = bf16[128,2048]{0,1:T(8,128)(2,1)S(1)} collective-permute-done((bf16[128,2048]{0,1:T(8,128)(2,1)S(1)}, bf16[128,2048]{0,1:T(8,128)(2,1)S(1)}, u32[]{:S(2)}, u32[]{:S(2)}) %collective-permute-start.16) | collective-permute-done | bytes 524320 | tf_op jit(solution)/shard_map/ppermute | solution.py:350
  31.1 4.1 collective-permute-start
  51.1 3.6 collective-permute-start.9
  68.5 3.8 collective-permute-done.2
  75.3 4.4 all-gather.4.cloned.1.call-done
  87.6 4.1 collective-permute-start.6
  91.8 3.7 collective-permute-start.5
  95.5 4.9 fusion.122
  102.4 4.7 attend.2
  114.7 4.5 collective-permute-done.10
  119.2 4.2 collective-permute-done.12
  131.0 8.5 %collective-permute-done.15 = bf16[64,2048]{1,0:T(8,128)(2,1)S(1)} collective-permute-done((bf16[64,2048]{1,0:T(8,128)(2,1)S(1)}, bf16[64,2048]{1,0:T(8,128)(2,1)S(1)}, u32[]{:S(2)}, u32[]{:S(2)}) %collective-permute-start.15) | collective-permute-done | bytes 262176 | tf_op jit(solution)/shard_map/ppermute | solution.py:31
  140.2 25.2 %all-gather.6.cloned.1.call-done = bf16[4096,2048]{0,1:T(8,128)(2,1)} async-done(((bf16[128,2048]{0,1:T(8,128)(2,1)}), bf16[4096,2048]{0,1:T(8,128)(2,1)}) %all-gather.6.cloned.1.call-update) | async-done | bytes 16777232 | tf_op jit(solution)/shard_map/all_gather | solution.py:424
  165.4 22.6 %copy.152 = bf16[4096,2048]{1,0:T(8,128)(2,1)} copy(bf16[4096,2048]{0,1:T(8,128)(2,1)} %all-gather.6.cloned.1.call-done) | data formatting | bytes 33554432 | tf_op jit(solution)/shard_map/all_gather | solution.py:424
  188.0 5.9 copy-done.2
  193.9 8.7 %feed.2 = (bf16[256,2048]{1,0:T(8,128)(2,1)S(1)}, bf16[256,2048]{1,0:T(8,128)(2,1)S(1)}, bf16[256,16]{1,0:T(8,128)(2,1)S(1)}, bf16[256,16]{1,0:T(8,128)(2,1)S(1)}, bf16[256,2048]{1,0:T(8,128)(2,1)S(1)}) custom-call(bf16[256,2048]{1,0:T(8,128)(2,1)S(1)} %pad_maximum_fusion.1.refs_0_, bf16[4,2,512,2048]{3,2,1,0:T(8,128)(2,1)S(1)} %bitcast.719, ...), custom_call_target="tpu_custom_call" | custom-call | flops 4294967296 | bytes 20971520 | tf_op jit(solution)/shard_map/feed/pallas_call | solution.py:233
  212.5 4.9 collective-permute-done.19
  224.5 9.9 %collective-permute-done.22 = bf16[64,2048]{1,0:T(8,128)(2,1)S(1)} collective-permute-done((bf16[64,2048]{1,0:T(8,128)(2,1)S(1)}, bf16[64,2048]{1,0:T(8,128)(2,1)S(1)}, u32[]{:S(2)}, u32[]{:S(2)}) %collective-permute-start.22) | collective-permute-done | bytes 262176 | tf_op jit(solution)/shard_map/ppermute | solution.py:31
  237.9 3.7 collective-permute-start.25
  241.6 3.7 collective-permute-start.24
  251.4 4.7 attend.3
  265.7 6.8 %collective-permute-done.27 = bf16[64,2048]{1,0:T(8,128)(2,1)S(1)} collective-permute-done((bf16[64,2048]{1,0:T(8,128)(2,1)S(1)}, bf16[64,2048]{1,0:T(8,128)(2,1)S(1)}, u32[]{:S(2)}, u32[]{:S(2)}) %collective-permute-start.27) | collective-permute-done | bytes 262176 | tf_op jit(solution)/shard_map/ppermute | solution.py:31
  272.5 6.2 %collective-permute-done.29 = bf16[64,2048]{1,0:T(8,128)(2,1)S(1)} collective-permute-done((bf16[64,2048]{1,0:T(8,128)(2,1)S(1)}, bf16[64,2048]{1,0:T(8,128)(2,1)S(1)}, u32[]{:S(2)}, u32[]{:S(2)}) %collective-permute-start.29) | collective-permute-done | bytes 262176 | tf_op jit(solution)/shard_map/ppermute | solution.py:31
  280.2 5.7 collective-permute-start.31
  289.5 22.8 %copy.153 = bf16[4096,2048]{1,0:T(8,128)(2,1)} copy(bf16[4096,2048]{0,1:T(8,128)(2,1)} %all-gather.8.cloned.1.call-done) | data formatting | bytes 33554432 | tf_op jit(solution)/shard_map/all_gather | solution.py:424
  313.7 5.8 copy-done.4
  319.5 8.7 %feed.3 = (bf16[256,2048]{1,0:T(8,128)(2,1)S(1)}, bf16[256,2048]{1,0:T(8,128)(2,1)S(1)}, bf16[256,16]{1,0:T(8,128)(2,1)S(1)}, bf16[256,16]{1,0:T(8,128)(2,1)S(1)}, bf16[256,2048]{1,0:T(8,128)(2,1)S(1)}) custom-call(bf16[256,2048]{1,0:T(8,128)(2,1)S(1)} %pad_maximum_fusion.3.refs_0_, bf16[4,2,512,2048]{3,2,1,0:T(8,128)(2,1)S(1)} %bitcast.721, ...), custom_call_target="tpu_custom_call" | custom-call | flops 4294967296 | bytes 20971520 | tf_op jit(solution)/shard_map/feed/pallas_call | solution.py:233
  328.2 5.8 copy-done.5
  334.0 8.2 %feed_back.2 = (bf16[256,2048]{1,0:T(8,128)(2,1)S(1)}, bf16[256,16]{1,0:T(8,128)(2,1)S(1)}, bf16[256,16]{1,0:T(8,128)(2,1)S(1)}, bf16[256,2048]{1,0:T(8,128)(2,1)S(1)}) custom-call(bf16[256,2048]{1,0:T(8,128)(2,1)S(1)} %pad_maximum_fusion.4.refs_0_, bf16[4,2,512,2048]{3,2,1,0:T(8,128)(2,1)S(1)} %bitcast.722, ...), custom_call_target="tpu_custom_call" | custom-call | flops 4294967296 | bytes 18874368 | tf_op jit(solution)/shard_map/feed_back/pallas_call | solution.py:282
  344.6 4.2 collective-permute-start.41
  360.3 4.2 collective-permute-done.33
  369.7 4.4 collective-permute-start.43
  377.2 4.1 collective-permute-done.43
  381.7 6.4 %attend_back.2 = (bf16[256,512]{1,0:T(8,128)(2,1)S(1)}, bf16[1280,256]{1,0:T(8,128)(2,1)S(1)}, bf16[256,16]{1,0:T(8,128)(2,1)S(1)}, bf16[256,16]{1,0:T(8,128)(2,1)S(1)}, f32[256,2048]{1,0:T(8,128)S(1)}) custom-call(bf16[256,2048]{1,0:T(8,128)(2,1)S(1)} %pad_maximum_fusion.5.refs_0_, bf16[2048,512]{1,0:T(8,128)(2,1)S(1)} %bitcast.728, ...), custom_call_target="tpu_custom_call" | custom-call | flops 2415919104 | bytes 13631488 | tf_op jit(solution)/shard_map/attend_back/pallas_call | solution.py:154
  394.3 11.1 %collective-permute-done.48 = bf16[256,256]{1,0:T(8,128)(2,1)S(1)} collective-permute-done((bf16[256,256]{1,0:T(8,128)(2,1)S(1)}, bf16[256,256]{1,0:T(8,128)(2,1)S(1)}, u32[]{:S(2)}, u32[]{:S(2)}) %collective-permute-start.48) | collective-permute-done | bytes 131104 | tf_op jit(solution)/shard_map/ppermute | solution.py:37
  413.9 5.9 collective-permute-done.49
  419.8 5.0 collective-permute-done.51
  432.9 5.1 collective-permute-done.54
  438.0 5.0 collective-permute-done.53
  444.5 5.8 copy-done.3
  450.3 7.8 %feed_back.3 = (bf16[256,2048]{1,0:T(8,128)(2,1)S(1)}, bf16[256,16]{1,0:T(8,128)(2,1)S(1)}, bf16[256,16]{1,0:T(8,128)(2,1)S(1)}, bf16[256,2048]{1,0:T(8,128)(2,1)S(1)}) custom-call(bf16[256,2048]{1,0:T(8,128)(2,1)S(1)} %pad_maximum_fusion.6.refs_0_, bf16[4,2,512,2048]{3,2,1,0:T(8,128)(2,1)S(1)} %bitcast.720, bf16[256,2048]{1,0:T(8,128)(2,1)S(1)} %copy-done.18, ...), custom_call_target="tpu_custom_call" | custom-call | flops 4294967296 | bytes 18874368 | tf_op jit(solution)/shard_map/feed_back/pallas_call | solution.py:282
  470.4 5.5 collective-permute-done.56
  482.4 8.4 %collective-permute-done.61 = bf16[64,2048]{1,0:T(8,128)(2,1)S(1)} collective-permute-done((bf16[64,2048]{1,0:T(8,128)(2,1)S(1)}, bf16[64,2048]{1,0:T(8,128)(2,1)S(1)}, u32[]{:S(2)}, u32[]{:S(2)}) %collective-permute-start.61) | collective-permute-done | bytes 262176 | tf_op jit(solution)/shard_map/ppermute | solution.py:31
  494.1 6.4 %attend_back.3 = (bf16[256,512]{1,0:T(8,128)(2,1)S(1)}, bf16[1280,256]{1,0:T(8,128)(2,1)S(1)}, bf16[256,16]{1,0:T(8,128)(2,1)S(1)}, bf16[256,16]{1,0:T(8,128)(2,1)S(1)}, f32[256,2048]{1,0:T(8,128)S(1)}) custom-call(bf16[256,2048]{1,0:T(8,128)(2,1)S(1)} %pad_maximum_fusion.7.refs_0_, bf16[2048,512]{1,0:T(8,128)(2,1)S(1)} %bitcast.724, ...), custom_call_target="tpu_custom_call" | custom-call | flops 2415919104 | bytes 13631488 | tf_op jit(solution)/shard_map/attend_back/pallas_call | solution.py:154
  515.5 3.6 collective-permute-start.71
  524.6 5.0 collective-permute-start.75
  564.6 6.8 %collective-permute-done.67 = bf16[64,2048]{1,0:T(8,128)(2,1)S(1)} collective-permute-done((bf16[64,2048]{1,0:T(8,128)(2,1)S(1)}, bf16[64,2048]{1,0:T(8,128)(2,1)S(1)}, u32[]{:S(2)}, u32[]{:S(2)}) %collective-permute-start.67) | collective-permute-done | bytes 262176 | tf_op jit(solution)/shard_map/ppermute | solution.py:31
  (676 shorter events, 243.4 us)
Async XLA Ops:
  7.2 72.5 %all-gather.4.cloned.1.call-start = ((), (), s32[]{:S(2)}) async-start(), calls=%async_computation.2 | async-start | bytes 10813440 | tf_op jit(solution)/shard_map/all_gather | solution.py:424
  10.0 155.3 %all-gather.6.cloned.1.call-start = ((), (), s32[]{:S(2)}) async-start(), calls=%async_computation.3 | async-start | bytes 17301504 | tf_op jit(solution)/shard_map/all_gather | solution.py:424
  11.8 17.0 %collective-permute-start.16 = (bf16[128,2048]{0,1:T(8,128)(2,1)S(1)}, bf16[128,2048]{0,1:T(8,128)(2,1)S(1)}, u32[]{:S(2)}, u32[]{:S(2)}) collective-permute-start(bf16[128,2048]{0,1:T(8,128)(2,1)S(1)} %broadcast_select_fusion.2), channel_id=1, source_target_pairs={{0,64},{64,0},{1,65},{65,1},{2,66},{66,2},{3,67},{67,3},{4,68},{68... | collective-permute-start | bytes 1572872 | tf_op jit(solution)/shard_map/ppermute | solution.py:350
  30.0 259.5 %all-gather.8.cloned.1.call-start = ((), (), s32[]{:S(2)}) async-start(), calls=%async_computation.4 | async-start | bytes 17301504 | tf_op jit(solution)/shard_map/all_gather | solution.py:424
  30.7 435.1 %reduce-scatter.3.cloned.1.call-start = ((), (), s32[]{:S(2)}) async-start(), calls=%async_computation.5 | async-start | bytes 430080 | tf_op jit(solution)/shard_map/reduce_scatter | solution.py:554
  31.1 25.6 %collective-permute-start = (bf16[1,15104]{1,0:T(2,128)(2,1)S(1)}, bf16[1,15104]{1,0:T(2,128)(2,1)S(1)}, u32[]{:S(2)}, u32[]{:S(2)}) collective-permute-start(bf16[1,15104]{1,0:T(2,128)(2,1)S(1)} %constant_dynamic-update-slice_fusion), channel_id=1, source_target_pairs={{0,64},{64,0},{1,65},{65,1},{2,66},{66,2},{3,67},{67,3},{4,68},{68... | collective-permute-start | bytes 90632 | tf_op jit(solution)/shard_map/ppermute | solution.py:350
  42.1 22.5 %collective-permute-start.4 = (bf16[16,4864]{1,0:T(8,128)(2,1)S(1)}, bf16[16,4864]{1,0:T(8,128)(2,1)S(1)}, u32[]{:S(2)}, u32[]{:S(2)}) collective-permute-start(bf16[16,4864]{1,0:T(8,128)(2,1)S(1)} %pad_maximum_fusion.15), channel_id=1, source_target_pairs={{0,64},{64,0},{1,65},{65,1},{2,66},{66,2},{3,67},{67,3},{4,68},{68... | collective-permute-start | bytes 466952 | tf_op jit(solution)/shard_map/ppermute | solution.py:350
  51.1 23.4 %collective-permute-start.9 = (bf16[16,10752]{1,0:T(8,128)(2,1)}, bf16[16,10752]{1,0:T(8,128)(2,1)S(1)}, u32[]{:S(2)}, u32[]{:S(2)}) collective-permute-start(bf16[16,10752]{1,0:T(8,128)(2,1)} %get-tuple-element.179), channel_id=1, source_target_pairs={{0,64},{64,0},{1,65},{65,1},{2,66},{66,2},{3,67},{67,3},{4,68},{68... | collective-permute-start | bytes 1032200 | tf_op jit(solution)/shard_map/ppermute | solution.py:350
  59.9 12.4 %collective-permute-start.2 = (bf16[64,2048]{1,0:T(8,128)(2,1)S(1)}, bf16[64,2048]{1,0:T(8,128)(2,1)S(1)}, u32[]{:S(2)}, u32[]{:S(2)}) collective-permute-start(bf16[64,2048]{1,0:T(8,128)(2,1)S(1)} %fusion.51), channel_id=1, source_target_pairs={{0,2},{1,3},{2,0},{3,1},{4,6},{5,7},{6,4},{7,5},{8,10},{9,11},{10,... | collective-permute-start | bytes 786440 | tf_op jit(solution)/shard_map/ppermute | solution.py:31
  82.8 19.0 %collective-permute-start.8 = (bf16[256,256]{1,0:T(8,128)(2,1)S(1)}, bf16[256,256]{1,0:T(8,128)(2,1)S(1)}, u32[]{:S(2)}, u32[]{:S(2)}) collective-permute-start(bf16[256,256]{1,0:T(8,128)(2,1)S(1)} %fusion.9), channel_id=1, source_target_pairs={{0,4},{4,8},{8,12},{12,16},{16,20},{20,24},{24,28},{28,32},{32,36}... | collective-permute-start | bytes 393224 | tf_op jit(solution)/shard_map/ppermute | solution.py:37
  85.2 16.7 %collective-permute-start.7 = (bf16[256,256]{1,0:T(8,128)(2,1)S(1)}, bf16[256,256]{1,0:T(8,128)(2,1)S(1)}, u32[]{:S(2)}, u32[]{:S(2)}) collective-permute-start(bf16[256,256]{1,0:T(8,128)(2,1)S(1)} %fusion.9), channel_id=1, source_target_pairs={{0,8},{4,12},{8,16},{12,20},{16,24},{20,28},{24,32},{28,36},{32,40... | collective-permute-start | bytes 393224 | tf_op jit(solution)/shard_map/ppermute | solution.py:37
  87.6 14.2 %collective-permute-start.6 = (bf16[256,256]{1,0:T(8,128)(2,1)S(1)}, bf16[256,256]{1,0:T(8,128)(2,1)S(1)}, u32[]{:S(2)}, u32[]{:S(2)}) collective-permute-start(bf16[256,256]{1,0:T(8,128)(2,1)S(1)} %fusion.9), channel_id=1, source_target_pairs={{0,12},{4,16},{8,20},{12,24},{16,28},{20,32},{24,36},{28,40},{32,4... | collective-permute-start | bytes 393224 | tf_op jit(solution)/shard_map/ppermute | solution.py:37
  111.1 12.3 %collective-permute-start.12 = (bf16[64,2048]{1,0:T(8,128)(2,1)S(1)}, bf16[64,2048]{1,0:T(8,128)(2,1)S(1)}, u32[]{:S(2)}, u32[]{:S(2)}) collective-permute-start(bf16[64,2048]{1,0:T(8,128)(2,1)S(1)} %get-tuple-element.144), channel_id=1, source_target_pairs={{0,3},{1,0},{2,1},{3,2},{4,7},{5,4},{6,5},{7,6},{8,11},{9,8},{10,9... | collective-permute-start | bytes 786440 | tf_op jit(solution)/shard_map/ppermute | solution.py:31
  112.9 12.2 %collective-permute-start.11 = (bf16[64,2048]{1,0:T(8,128)(2,1)S(1)}, bf16[64,2048]{1,0:T(8,128)(2,1)S(1)}, u32[]{:S(2)}, u32[]{:S(2)}) collective-permute-start(bf16[64,2048]{1,0:T(8,128)(2,1)S(1)} %get-tuple-element.145), channel_id=1, source_target_pairs={{0,2},{1,3},{2,0},{3,1},{4,6},{5,7},{6,4},{7,5},{8,10},{9,11},{10,... | collective-permute-start | bytes 786440 | tf_op jit(solution)/shard_map/ppermute | solution.py:31
  125.9 13.6 %collective-permute-start.15 = (bf16[64,2048]{1,0:T(8,128)(2,1)S(1)}, bf16[64,2048]{1,0:T(8,128)(2,1)S(1)}, u32[]{:S(2)}, u32[]{:S(2)}) collective-permute-start(bf16[64,2048]{1,0:T(8,128)(2,1)S(1)} %add_convert_fusion.3), channel_id=1, source_target_pairs={{0,1},{1,2},{2,3},{3,0},{4,5},{5,6},{6,7},{7,4},{8,9},{9,10},{10,1... | collective-permute-start | bytes 786440 | tf_op jit(solution)/shard_map/ppermute | solution.py:31
  127.1 12.4 %collective-permute-start.14 = (bf16[64,2048]{1,0:T(8,128)(2,1)S(1)}, bf16[64,2048]{1,0:T(8,128)(2,1)S(1)}, u32[]{:S(2)}, u32[]{:S(2)}) collective-permute-start(bf16[64,2048]{1,0:T(8,128)(2,1)S(1)} %add_convert_fusion.3), channel_id=1, source_target_pairs={{0,2},{1,3},{2,0},{3,1},{4,6},{5,7},{6,4},{7,5},{8,10},{9,11},{10,... | collective-permute-start | bytes 786440 | tf_op jit(solution)/shard_map/ppermute | solution.py:31
  204.3 13.2 %collective-permute-start.19 = (bf16[64,2048]{1,0:T(8,128)(2,1)S(1)}, bf16[64,2048]{1,0:T(8,128)(2,1)S(1)}, u32[]{:S(2)}, u32[]{:S(2)}) collective-permute-start(bf16[64,2048]{1,0:T(8,128)(2,1)S(1)} %get-tuple-element.141), channel_id=1, source_target_pairs={{0,3},{1,0},{2,1},{3,2},{4,7},{5,4},{6,5},{7,6},{8,11},{9,8},{10,9... | collective-permute-start | bytes 786440 | tf_op jit(solution)/shard_map/ppermute | solution.py:31
  206.0 13.0 %collective-permute-start.18 = (bf16[64,2048]{1,0:T(8,128)(2,1)S(1)}, bf16[64,2048]{1,0:T(8,128)(2,1)S(1)}, u32[]{:S(2)}, u32[]{:S(2)}) collective-permute-start(bf16[64,2048]{1,0:T(8,128)(2,1)S(1)} %get-tuple-element.142), channel_id=1, source_target_pairs={{0,2},{1,3},{2,0},{3,1},{4,6},{5,7},{6,4},{7,5},{8,10},{9,11},{10,... | collective-permute-start | bytes 786440 | tf_op jit(solution)/shard_map/ppermute | solution.py:31
  219.9 14.6 %collective-permute-start.22 = (bf16[64,2048]{1,0:T(8,128)(2,1)S(1)}, bf16[64,2048]{1,0:T(8,128)(2,1)S(1)}, u32[]{:S(2)}, u32[]{:S(2)}) collective-permute-start(bf16[64,2048]{1,0:T(8,128)(2,1)S(1)} %fusion.44), channel_id=1, source_target_pairs={{0,1},{1,2},{2,3},{3,0},{4,5},{5,6},{6,7},{7,4},{8,9},{9,10},{10,1... | collective-permute-start | bytes 786440 | tf_op jit(solution)/shard_map/ppermute | solution.py:31
  221.1 13.4 %collective-permute-start.21 = (bf16[64,2048]{1,0:T(8,128)(2,1)S(1)}, bf16[64,2048]{1,0:T(8,128)(2,1)S(1)}, u32[]{:S(2)}, u32[]{:S(2)}) collective-permute-start(bf16[64,2048]{1,0:T(8,128)(2,1)S(1)} %fusion.44), channel_id=1, source_target_pairs={{0,2},{1,3},{2,0},{3,1},{4,6},{5,7},{6,4},{7,5},{8,10},{9,11},{10,... | collective-permute-start | bytes 786440 | tf_op jit(solution)/shard_map/ppermute | solution.py:31
  236.6 14.7 %collective-permute-start.26 = (bf16[256,256]{1,0:T(8,128)(2,1)S(1)}, bf16[256,256]{1,0:T(8,128)(2,1)S(1)}, u32[]{:S(2)}, u32[]{:S(2)}) collective-permute-start(bf16[256,256]{1,0:T(8,128)(2,1)S(1)} %fusion.10), channel_id=1, source_target_pairs={{0,4},{4,8},{8,12},{12,16},{16,20},{20,24},{24,28},{28,32},{32,36}... | collective-permute-start | bytes 393224 | tf_op jit(solution)/shard_map/ppermute | solution.py:37
  237.9 13.3 %collective-permute-start.25 = (bf16[256,256]{1,0:T(8,128)(2,1)S(1)}, bf16[256,256]{1,0:T(8,128)(2,1)S(1)}, u32[]{:S(2)}, u32[]{:S(2)}) collective-permute-start(bf16[256,256]{1,0:T(8,128)(2,1)S(1)} %fusion.10), channel_id=1, source_target_pairs={{0,8},{4,12},{8,16},{12,20},{16,24},{20,28},{24,32},{28,36},{32,40... | collective-permute-start | bytes 393224 | tf_op jit(solution)/shard_map/ppermute | solution.py:37
  258.6 13.9 %collective-permute-start.27 = (bf16[64,2048]{1,0:T(8,128)(2,1)S(1)}, bf16[64,2048]{1,0:T(8,128)(2,1)S(1)}, u32[]{:S(2)}, u32[]{:S(2)}) collective-permute-start(bf16[64,2048]{1,0:T(8,128)(2,1)S(1)} %get-tuple-element.137), channel_id=1, source_target_pairs={{0,1},{1,2},{2,3},{3,0},{4,5},{5,6},{6,7},{7,4},{8,9},{9,10},{10,1... | collective-permute-start | bytes 786440 | tf_op jit(solution)/shard_map/ppermute | solution.py:31
  259.3 19.5 %collective-permute-start.29 = (bf16[64,2048]{1,0:T(8,128)(2,1)S(1)}, bf16[64,2048]{1,0:T(8,128)(2,1)S(1)}, u32[]{:S(2)}, u32[]{:S(2)}) collective-permute-start(bf16[64,2048]{1,0:T(8,128)(2,1)S(1)} %get-tuple-element.138), channel_id=1, source_target_pairs={{0,3},{1,0},{2,1},{3,2},{4,7},{5,4},{6,5},{7,6},{8,11},{9,8},{10,9... | collective-permute-start | bytes 786440 | tf_op jit(solution)/shard_map/ppermute | solution.py:31
  261.9 16.9 %collective-permute-start.28 = (bf16[64,2048]{1,0:T(8,128)(2,1)S(1)}, bf16[64,2048]{1,0:T(8,128)(2,1)S(1)}, u32[]{:S(2)}, u32[]{:S(2)}) collective-permute-start(bf16[64,2048]{1,0:T(8,128)(2,1)S(1)} %get-tuple-element.139), channel_id=1, source_target_pairs={{0,2},{1,3},{2,0},{3,1},{4,6},{5,7},{6,4},{7,5},{8,10},{9,11},{10,... | collective-permute-start | bytes 786440 | tf_op jit(solution)/shard_map/ppermute | solution.py:31
  262.8 23.1 %collective-permute-start.38 = (bf16[64,2048]{1,0:T(8,128)(2,1)S(1)}, bf16[64,2048]{1,0:T(8,128)(2,1)S(1)}, u32[]{:S(2)}, u32[]{:S(2)}) collective-permute-start(bf16[64,2048]{1,0:T(8,128)(2,1)S(1)} %dynamic-slice_bitcast_fusion), channel_id=1, source_target_pairs={{0,1},{1,2},{2,3},{3,0},{4,5},{5,6},{6,7},{7,4},{8,9},{9,10},{10,1... | collective-permute-start | bytes 786440 | tf_op jit(solution)/shard_map/ppermute | solution.py:31
  264.3 23.6 %collective-permute-start.37 = (bf16[64,2048]{1,0:T(8,128)(2,1)S(1)}, bf16[64,2048]{1,0:T(8,128)(2,1)}, u32[]{:S(2)}, u32[]{:S(2)}) collective-permute-start(bf16[64,2048]{1,0:T(8,128)(2,1)S(1)} %dynamic-slice_bitcast_fusion), channel_id=1, source_target_pairs={{0,2},{1,3},{2,0},{3,1},{4,6},{5,7},{6,4},{7,5},{8,10},{9,11},{10,... | collective-permute-start | bytes 786440 | tf_op jit(solution)/shard_map/ppermute | solution.py:31
  272.5 15.7 %collective-permute-start.36 = (bf16[64,2048]{1,0:T(8,128)(2,1)S(1)}, bf16[64,2048]{1,0:T(8,128)(2,1)}, u32[]{:S(2)}, u32[]{:S(2)}) collective-permute-start(bf16[64,2048]{1,0:T(8,128)(2,1)S(1)} %dynamic-slice_bitcast_fusion), channel_id=1, source_target_pairs={{0,3},{1,0},{2,1},{3,2},{4,7},{5,4},{6,5},{7,6},{8,11},{9,8},{10,9... | collective-permute-start | bytes 786440 | tf_op jit(solution)/shard_map/ppermute | solution.py:31
  280.2 32.1 %collective-permute-start.32 = (bf16[64,2048]{1,0:T(8,128)(2,1)}, bf16[64,2048]{1,0:T(8,128)(2,1)}, u32[]{:S(2)}, u32[]{:S(2)}) collective-permute-start(bf16[64,2048]{1,0:T(8,128)(2,1)} %add_convert_fusion.1), channel_id=1, source_target_pairs={{0,1},{1,2},{2,3},{3,0},{4,5},{5,6},{6,7},{7,4},{8,9},{9,10},{10,1... | collective-permute-start | bytes 786440 | tf_op jit(solution)/shard_map/ppermute | solution.py:31
  280.2 32.1 %collective-permute-start.31 = (bf16[64,2048]{1,0:T(8,128)(2,1)}, bf16[64,2048]{1,0:T(8,128)(2,1)}, u32[]{:S(2)}, u32[]{:S(2)}) collective-permute-start(bf16[64,2048]{1,0:T(8,128)(2,1)} %add_convert_fusion.1), channel_id=1, source_target_pairs={{0,2},{1,3},{2,0},{3,1},{4,6},{5,7},{6,4},{7,5},{8,10},{9,11},{10,... | collective-permute-start | bytes 786440 | tf_op jit(solution)/shard_map/ppermute | solution.py:31
  286.6 25.7 %collective-permute-start.30 = (bf16[64,2048]{1,0:T(8,128)(2,1)}, bf16[64,2048]{1,0:T(8,128)(2,1)}, u32[]{:S(2)}, u32[]{:S(2)}) collective-permute-start(bf16[64,2048]{1,0:T(8,128)(2,1)} %add_convert_fusion.1), channel_id=1, source_target_pairs={{0,3},{1,0},{2,1},{3,2},{4,7},{5,4},{6,5},{7,6},{8,11},{9,8},{10,9... | collective-permute-start | bytes 786440 | tf_op jit(solution)/shard_map/ppermute | solution.py:31
  342.8 14.2 %collective-permute-start.39 = (bf16[64,2048]{1,0:T(8,128)(2,1)S(1)}, bf16[64,2048]{1,0:T(8,128)(2,1)S(1)}, u32[]{:S(2)}, u32[]{:S(2)}) collective-permute-start(bf16[64,2048]{1,0:T(8,128)(2,1)S(1)} %get-tuple-element.131), channel_id=1, source_target_pairs={{0,1},{1,2},{2,3},{3,0},{4,5},{5,6},{6,7},{7,4},{8,9},{9,10},{10,1... | collective-permute-start | bytes 786440 | tf_op jit(solution)/shard_map/ppermute | solution.py:31
  344.6 13.7 %collective-permute-start.41 = (bf16[64,2048]{1,0:T(8,128)(2,1)S(1)}, bf16[64,2048]{1,0:T(8,128)(2,1)S(1)}, u32[]{:S(2)}, u32[]{:S(2)}) collective-permute-start(bf16[64,2048]{1,0:T(8,128)(2,1)S(1)} %get-tuple-element.132), channel_id=1, source_target_pairs={{0,3},{1,0},{2,1},{3,2},{4,7},{5,4},{6,5},{7,6},{8,11},{9,8},{10,9... | collective-permute-start | bytes 786440 | tf_op jit(solution)/shard_map/ppermute | solution.py:31
  350.2 14.2 %collective-permute-start.33 = (bf16[64,2048]{1,0:T(8,128)(2,1)S(1)}, bf16[64,2048]{1,0:T(8,128)(2,1)S(1)}, u32[]{:S(2)}, u32[]{:S(2)}) collective-permute-start(bf16[64,2048]{1,0:T(8,128)(2,1)S(1)} %get-tuple-element.134), channel_id=1, source_target_pairs={{0,1},{1,2},{2,3},{3,0},{4,5},{5,6},{6,7},{7,4},{8,9},{9,10},{10,1... | collective-permute-start | bytes 786440 | tf_op jit(solution)/shard_map/ppermute | solution.py:31
  351.7 16.1 %collective-permute-start.35 = (bf16[64,2048]{1,0:T(8,128)(2,1)S(1)}, bf16[64,2048]{1,0:T(8,128)(2,1)S(1)}, u32[]{:S(2)}, u32[]{:S(2)}) collective-permute-start(bf16[64,2048]{1,0:T(8,128)(2,1)S(1)} %get-tuple-element.135), channel_id=1, source_target_pairs={{0,3},{1,0},{2,1},{3,2},{4,7},{5,4},{6,5},{7,6},{8,11},{9,8},{10,9... | collective-permute-start | bytes 786440 | tf_op jit(solution)/shard_map/ppermute | solution.py:31
  389.9 15.5 %collective-permute-start.48 = (bf16[256,256]{1,0:T(8,128)(2,1)S(1)}, bf16[256,256]{1,0:T(8,128)(2,1)S(1)}, u32[]{:S(2)}, u32[]{:S(2)}) collective-permute-start(bf16[256,256]{1,0:T(8,128)(2,1)S(1)} %get-tuple-element.157), channel_id=1, source_target_pairs={{16,0},{20,4},{24,8},{28,12},{32,16},{36,20},{40,24},{44,28},{48,3... | collective-permute-start | bytes 393224 | tf_op jit(solution)/shard_map/ppermute | solution.py:37
  391.2 14.4 %collective-permute-start.47 = (bf16[256,256]{1,0:T(8,128)(2,1)S(1)}, bf16[256,256]{1,0:T(8,128)(2,1)S(1)}, u32[]{:S(2)}, u32[]{:S(2)}) collective-permute-start(bf16[256,256]{1,0:T(8,128)(2,1)S(1)} %get-tuple-element.158), channel_id=1, source_target_pairs={{12,0},{16,4},{20,8},{24,12},{28,16},{32,20},{36,24},{40,28},{44,3... | collective-permute-start | bytes 393224 | tf_op jit(solution)/shard_map/ppermute | solution.py:37
  392.5 15.6 %collective-permute-start.46 = (bf16[256,256]{1,0:T(8,128)(2,1)S(1)}, bf16[256,256]{1,0:T(8,128)(2,1)S(1)}, u32[]{:S(2)}, u32[]{:S(2)}) collective-permute-start(bf16[256,256]{1,0:T(8,128)(2,1)S(1)} %get-tuple-element.159), channel_id=1, source_target_pairs={{8,0},{12,4},{16,8},{20,12},{24,16},{28,20},{32,24},{36,28},{40,32... | collective-permute-start | bytes 393224 | tf_op jit(solution)/shard_map/ppermute | solution.py:37
  410.0 14.7 %collective-permute-start.51 = (bf16[64,2048]{1,0:T(8,128)(2,1)S(1)}, bf16[64,2048]{1,0:T(8,128)(2,1)S(1)}, u32[]{:S(2)}, u32[]{:S(2)}) collective-permute-start(bf16[64,2048]{1,0:T(8,128)(2,1)S(1)} %get-tuple-element.129), channel_id=1, source_target_pairs={{0,3},{1,0},{2,1},{3,2},{4,7},{5,4},{6,5},{7,6},{8,11},{9,8},{10,9... | collective-permute-start | bytes 786440 | tf_op jit(solution)/shard_map/ppermute | solution.py:31
  412.7 13.4 %collective-permute-start.50 = (bf16[64,2048]{1,0:T(8,128)(2,1)S(1)}, bf16[64,2048]{1,0:T(8,128)(2,1)S(1)}, u32[]{:S(2)}, u32[]{:S(2)}) collective-permute-start(bf16[64,2048]{1,0:T(8,128)(2,1)S(1)} %get-tuple-element.130), channel_id=1, source_target_pairs={{0,2},{1,3},{2,0},{3,1},{4,6},{5,7},{6,4},{7,5},{8,10},{9,11},{10,... | collective-permute-start | bytes 786440 | tf_op jit(solution)/shard_map/ppermute | solution.py:31
  429.2 13.8 %collective-permute-start.53 = (bf16[64,2048]{1,0:T(8,128)(2,1)S(1)}, bf16[64,2048]{1,0:T(8,128)(2,1)S(1)}, u32[]{:S(2)}, u32[]{:S(2)}) collective-permute-start(bf16[64,2048]{1,0:T(8,128)(2,1)S(1)} %get-tuple-element.102), channel_id=1, source_target_pairs={{0,2},{1,3},{2,0},{3,1},{4,6},{5,7},{6,4},{7,5},{8,10},{9,11},{10,... | collective-permute-start | bytes 786440 | tf_op jit(solution)/shard_map/ppermute | solution.py:31
  432.8 111.1 %reduce-scatter.5.cloned.1.call-start = ((), (), s32[]{:S(2)}) async-start(), calls=%async_computation.6 | async-start | bytes 278528 | tf_op jit(solution)/shard_map/reduce_scatter | solution.py:555
  462.9 12.9 %collective-permute-start.56 = (bf16[64,2048]{1,0:T(8,128)(2,1)}, bf16[64,2048]{1,0:T(8,128)(2,1)S(1)}, u32[]{:S(2)}, u32[]{:S(2)}) collective-permute-start(bf16[64,2048]{1,0:T(8,128)(2,1)} %get-tuple-element.127), channel_id=1, source_target_pairs={{0,2},{1,3},{2,0},{3,1},{4,6},{5,7},{6,4},{7,5},{8,10},{9,11},{10,... | collective-permute-start | bytes 786440 | tf_op jit(solution)/shard_map/ppermute | solution.py:31
  476.6 14.3 %collective-permute-start.61 = (bf16[64,2048]{1,0:T(8,128)(2,1)S(1)}, bf16[64,2048]{1,0:T(8,128)(2,1)S(1)}, u32[]{:S(2)}, u32[]{:S(2)}) collective-permute-start(bf16[64,2048]{1,0:T(8,128)(2,1)S(1)} %get-tuple-element.99), channel_id=1, source_target_pairs={{0,1},{1,2},{2,3},{3,0},{4,5},{5,6},{6,7},{7,4},{8,9},{9,10},{10,1... | collective-permute-start | bytes 786440 | tf_op jit(solution)/shard_map/ppermute | solution.py:31
  477.8 13.1 %collective-permute-start.60 = (bf16[64,2048]{1,0:T(8,128)(2,1)S(1)}, bf16[64,2048]{1,0:T(8,128)(2,1)S(1)}, u32[]{:S(2)}, u32[]{:S(2)}) collective-permute-start(bf16[64,2048]{1,0:T(8,128)(2,1)S(1)} %get-tuple-element.99), channel_id=1, source_target_pairs={{0,2},{1,3},{2,0},{3,1},{4,6},{5,7},{6,4},{7,5},{8,10},{9,11},{10,... | collective-permute-start | bytes 786440 | tf_op jit(solution)/shard_map/ppermute | solution.py:31
  480.6 25.9 %collective-permute-start.58 = (bf16[64,2048]{1,0:T(8,128)(2,1)S(1)}, bf16[64,2048]{1,0:T(8,128)(2,1)S(1)}, u32[]{:S(2)}, u32[]{:S(2)}) collective-permute-start(bf16[64,2048]{1,0:T(8,128)(2,1)S(1)} %get-tuple-element.173), channel_id=1, source_target_pairs={{0,64},{64,0},{1,65},{65,1},{2,66},{66,2},{3,67},{67,3},{4,68},{68... | collective-permute-start | bytes 786440 | tf_op jit(solution)/shard_map/ppermute | solution.py:350
  550.1 14.4 %collective-permute-start.66 = (bf16[64,2048]{1,0:T(8,128)(2,1)S(1)}, bf16[64,2048]{1,0:T(8,128)(2,1)S(1)}, u32[]{:S(2)}, u32[]{:S(2)}) collective-permute-start(bf16[64,2048]{1,0:T(8,128)(2,1)S(1)} %get-tuple-element.122), channel_id=1, source_target_pairs={{0,1},{1,2},{2,3},{3,0},{4,5},{5,6},{6,7},{7,4},{8,9},{9,10},{10,1... | collective-permute-start | bytes 786440 | tf_op jit(solution)/shard_map/ppermute | solution.py:31
  550.2 14.3 %collective-permute-start.68 = (bf16[64,2048]{1,0:T(8,128)(2,1)S(1)}, bf16[64,2048]{1,0:T(8,128)(2,1)S(1)}, u32[]{:S(2)}, u32[]{:S(2)}) collective-permute-start(bf16[64,2048]{1,0:T(8,128)(2,1)S(1)} %get-tuple-element.123), channel_id=1, source_target_pairs={{0,3},{1,0},{2,1},{3,2},{4,7},{5,4},{6,5},{7,6},{8,11},{9,8},{10,9... | collective-permute-start | bytes 786440 | tf_op jit(solution)/shard_map/ppermute | solution.py:31
  (180 other events, 2659.1 us)
Sparse Core Ops, SparseCore 0:
  10.9 68.7 all-gather.3
  82.4 82.8 all-gather.5
  167.5 81.4 all-gather.7
  432.9 23.5 reduce-scatter.2
  469.4 64.6 reduce-scatter.4

commit v5 on v4

v5 whole, which is shorter than its diff:
```python
import math

import jax
import jax.numpy as jnp
from jax import lax
from jax.experimental import pallas as pl
from jax.experimental.layout import Layout, with_layout_constraint
from jax.experimental.pallas import tpu as pltpu
from jax.sharding import PartitionSpec as P

WINDOW = 1024
epsilon = 1e-05
masked_score = -1e30
bf16 = jnp.bfloat16
f32 = jnp.float32


def plain(left, right):
    return jnp.dot(left, right, preferred_element_type=f32)


def against(left, right):
    return lax.dot_general(left, right, (((1,), (1,)), ((), ())), preferred_element_type=f32)


def across(left, right):
    return lax.dot_general(left, right, (((0,), (0,)), ((), ())), preferred_element_type=f32)


def around(block, axis, distance):
    size = lax.axis_size(axis)
    return lax.ppermute(block, axis, [(i, (i + distance) % size) for i in range(size)])


def along(block, axis, distance):
    size = lax.axis_size(axis)
    route = [(i, i + distance) for i in range(size) if 0 <= i + distance < size]
    return lax.ppermute(block, axis, route)


def flipped(block, axis, bit):
    size = lax.axis_size(axis)
    return lax.ppermute(block, axis, [(i, i ^ bit) for i in range(size)])


def pick(table, index, size=1):
    return lax.dynamic_slice_in_dim(table, index, size, 0)


def norm_parts(value):
    centred = value - jnp.mean(value, axis=-1, keepdims=True)
    spread = lax.rsqrt(jnp.mean(centred * centred, axis=-1, keepdims=True) + epsilon)
    return centred * spread, spread


def norm_back(unit, spread, scaled):
    inner = jnp.mean(scaled * unit, axis=-1, keepdims=True)
    return spread * (scaled - jnp.mean(scaled, axis=-1, keepdims=True) - unit * inner)


def gelu_parts(value):
    rate = math.sqrt(2.0 / math.pi)
    square = value * value
    bend = jnp.tanh(rate * (value + 0.044715 * value * square))
    rising = 0.5 * (1.0 + bend)
    slope = rising + 0.5 * value * (1.0 - bend * bend) * (rate * (1.0 + 3 * 0.044715 * square))
    return value * rising, slope


def side_blocks(query_ref, group, head):
    begin = group * 4 * head
    return jnp.concatenate(
        [query_ref[:, begin + h * head : begin + (h + 1) * head] for h in range(4)], axis=0
    )


def put_blocks(out_ref, value, group, head):
    rows = value.shape[0] // 4
    for h in range(4):
        begin = (group * 4 + h) * head
        out_ref[:, begin : begin + head] = value[h * rows : (h + 1) * rows]


def table_copies(table_ref, buf, sem, layer, begin):
    ranks, chunks, _, width = buf.shape
    return [
        pltpu.make_async_copy(
            table_ref.at[x, y, layer, :, pl.ds(begin, width)], buf.at[x, y], sem.at[x, y]
        )
        for x in range(ranks)
        for y in range(chunks)
    ]


def query_kernel(layer, normed_ref, table_ref, bias_ref, eq_ref, sq_ref, out_ref, low_ref, buf, sem):
    ranks, chunks, rows, width = buf.shape
    copies = table_copies(table_ref, buf, sem, layer, 0)
    for copy in copies:
        copy.start()
    normed = normed_ref[...]
    low = against(normed, sq_ref[...]).astype(bf16)
    low_ref[...] = low
    for x in range(ranks):
        columns = pl.ds(x * width, width)
        total = bias_ref[:, columns] + plain(low, eq_ref[:, columns])
        for y in range(chunks):
            copies[x * chunks + y].wait()
            total = total + plain(normed[:, y * rows : (y + 1) * rows], buf[x, y])
        out_ref[:, columns] = total.astype(bf16)


def table_scratch(table, width):
    ranks, chunks, _, rows, _ = table.shape
    return [
        pltpu.VMEM((ranks, chunks, rows, width), bf16),
        pltpu.SemaphoreType.DMA((ranks, chunks)),
    ]


held = pl.BlockSpec(memory_space=pltpu.VMEM)
remote = pl.BlockSpec(memory_space=pl.ANY)


def project_queries(layer, normed, table, bias, eq, sq):
    rows, model = normed.shape
    rank = sq.shape[0]
    width = model // table.shape[0]
    return pl.pallas_call(
        lambda *refs: query_kernel(layer, *refs),
        in_specs=[held, remote, held, held, held],
        out_specs=[held] * 2,
        out_shape=[
            jax.ShapeDtypeStruct((rows, model), bf16),
            jax.ShapeDtypeStruct((rows, rank), bf16),
        ],
        scratch_shapes=table_scratch(table, width),
        compiler_params=pltpu.CompilerParams(vmem_limit_bytes=20 * 2**20),
        cost_estimate=pl.CostEstimate(
            flops=8 * rows * model * model, bytes_accessed=2 * model * model, transcendentals=0
        ),
        name="project_queries",
    )(normed, table, bias, eq, sq)


def attend_kernel(
    layer, head, query_ref, keyval_ref, bias_ref, table_ref, so_ref, eo_ref,
    prob_ref, mixed_ref, low_ref, out_ref, buf, sem,
):
    ranks, chunks, rows, width = buf.shape
    copies = table_copies(table_ref, buf, sem, layer, width)
    for copy in copies:
        copy.start()
    scale = 1.0 / math.sqrt(head)
    bias = jnp.concatenate([bias_ref[...].astype(f32)] * 4, axis=0)
    for g in range(prob_ref.shape[0]):
        queries = side_blocks(query_ref, g, head)
        scores = against(queries, keyval_ref[:, :head]) * scale + bias
        lifted = jnp.exp(scores - jnp.max(scores, axis=-1, keepdims=True))
        probs = lifted * (1.0 / jnp.sum(lifted, axis=-1, keepdims=True))
        prob_ref[g] = probs
        put_blocks(mixed_ref, plain(probs.astype(bf16), keyval_ref[:, head:]).astype(bf16), g, head)
    mixed = mixed_ref[...]
    low = against(mixed, so_ref[...]).astype(bf16)
    low_ref[...] = low
    for copy in copies:
        copy.wait()
    for y in range(chunks):
        columns = pl.ds(y * rows, rows)
        total = plain(low, eo_ref[:, columns])
        for x in range(ranks):
            total = total + against(mixed[:, x * width : (x + 1) * width], buf[x, y])
        out_ref[:, columns] = total


def attend(layer, queries, key_block, bias, table, so, eo, head):
    rows, model = queries.shape
    keys = key_block.shape[0]
    groups = model // head // 4
    rank = so.shape[0]
    return pl.pallas_call(
        lambda *refs: attend_kernel(layer, head, *refs),
        in_specs=[held, held, held, remote, held, held],
        out_specs=[held] * 4,
        out_shape=[
            jax.ShapeDtypeStruct((groups, 4 * rows, keys), f32),
            jax.ShapeDtypeStruct((rows, model), bf16),
            jax.ShapeDtypeStruct((rows, rank), bf16),
            jax.ShapeDtypeStruct((rows, model), f32),
        ],
        scratch_shapes=table_scratch(table, model // table.shape[0]),
        compiler_params=pltpu.CompilerParams(vmem_limit_bytes=36 * 2**20),
        cost_estimate=pl.CostEstimate(
            flops=4 * rows * model * (keys + 2 * model),
            bytes_accessed=2 * model * model,
            transcendentals=groups * 4 * rows * keys,
        ),
        name="attend",
    )(queries, key_block, bias, table, so, eo)


def attend_back_kernel(
    layer, head, branch_ref, table_ref, so_ref, eo_ref, prob_ref, query_ref, keyval_ref, eq_ref, sq_ref,
    dq_ref, dkv_ref, inner_o_ref, inner_q_ref, part_ref,
    out_buf, out_sem, query_buf, query_sem, mixed_buf, key_sum, value_sum,
):
    ranks, chunks, rows, width = out_buf.shape
    out_copies = table_copies(table_ref, out_buf, out_sem, layer, width)
    query_copies = table_copies(table_ref, query_buf, query_sem, layer, 0)
    for copy in out_copies + query_copies:
        copy.start()
    scale = 1.0 / math.sqrt(head)
    branch = branch_ref[...]
    inner_o = against(branch, eo_ref[...]).astype(bf16)
    inner_o_ref[...] = inner_o
    for g in range(prob_ref.shape[0]):
        columns = pl.ds(g * width, width)
        total = plain(inner_o, so_ref[:, columns])
        for y in range(chunks):
            out_copies[g * chunks + y].wait()
            total = total + plain(branch[:, y * rows : (y + 1) * rows], out_buf[g, y])
        mixed_buf[:, columns] = total.astype(bf16)
        grad = side_blocks(mixed_buf, g, head)
        probs = prob_ref[g]
        grad_probs = against(grad, keyval_ref[:, head:])
        delta = jnp.sum(grad_probs * probs, axis=-1, keepdims=True)
        grad_scores = (probs * (grad_probs - delta)).astype(bf16)
        put_blocks(dq_ref, (plain(grad_scores, keyval_ref[:, :head]) * scale).astype(bf16), g, head)
        keys = across(grad_scores, side_blocks(query_ref, g, head))
        values = across(probs.astype(bf16), grad)
        if g == 0:
            key_sum[...] = keys
            value_sum[...] = values
        else:
            key_sum[...] += keys
            value_sum[...] += values
    dkv_ref[:, :head] = (key_sum[...] * scale).astype(bf16)
    dkv_ref[:, head:] = value_sum[...].astype(bf16)
    grad_q = dq_ref[...]
    inner_q = against(grad_q, eq_ref[...]).astype(bf16)
    inner_q_ref[...] = inner_q
    for copy in query_copies:
        copy.wait()
    for y in range(chunks):
        columns = pl.ds(y * rows, rows)
        total = plain(inner_q, sq_ref[:, columns])
        for x in range(ranks):
            total = total + against(grad_q[:, x * width : (x + 1) * width], query_buf[x, y])
        part_ref[:, columns] = total


def attend_back(layer, branch, table, so, eo, probs, queries, key_block, eq, sq, head):
    rows, model = queries.shape
    keys = key_block.shape[0]
    groups = probs.shape[0]
    rank = so.shape[0]
    width = model // table.shape[0]
    return pl.pallas_call(
        lambda *refs: attend_back_kernel(layer, head, *refs),
        in_specs=[held, remote] + [held] * 7,
        out_specs=[held] * 5,
        out_shape=[
            jax.ShapeDtypeStruct((rows, model), bf16),
            jax.ShapeDtypeStruct((keys, 2 * head), bf16),
            jax.ShapeDtypeStruct((rows, rank), bf16),
            jax.ShapeDtypeStruct((rows, rank), bf16),
            jax.ShapeDtypeStruct((rows, model), f32),
        ],
        scratch_shapes=table_scratch(table, width)
        + table_scratch(table, width)
        + [
            pltpu.VMEM((rows, model), bf16),
            pltpu.VMEM((keys, head), f32),
            pltpu.VMEM((keys, head), f32),
        ],
        compiler_params=pltpu.CompilerParams(vmem_limit_bytes=44 * 2**20),
        cost_estimate=pl.CostEstimate(
            flops=8 * rows * model * (keys + 2 * model),
            bytes_accessed=4 * model * model + 4 * groups * 4 * rows * keys,
            transcendentals=0,
        ),
        name="attend_back",
    )(branch, table, so, eo, probs, queries, key_block, eq, sq)


def feed_copies(table_ref, buf, sems):
    _, count, chunks, rows, tile = buf.shape
    half = count // 2 * tile
    copies = []
    for j in range(count):
        pair = []
        for k in range(2):
            columns = pl.ds(j * tile % half + k * half, tile)
            pair.append(
                pltpu.make_async_copy(
                    table_ref.at[:, j * tile // half, :, columns], buf.at[k, j], sems.at[k, j]
                )
            )
        copies.append(pair)
    return copies


def plain_chunks(left, buf, k, j):
    rows = buf.shape[3]
    return sum(plain(left[:, i * rows : (i + 1) * rows], buf[k, j, i]) for i in range(buf.shape[2]))


def add_against(total, left, buf, k, j):
    rows = buf.shape[3]
    for i in range(buf.shape[2]):
        columns = pl.ds(i * rows, rows)
        if j == 0:
            total[:, columns] = against(left, buf[k, j, i])
        else:
            total[:, columns] += against(left, buf[k, j, i])


def feed_kernel(
    second_ref, table_ref, bias_ref, eu_ref, sd_ref, su_ref, ed_ref,
    active_ref, slope_ref, low_u_ref, low_d_ref, out_ref, buf, sems, total,
):
    _, count, _, _, tile = buf.shape
    copies = feed_copies(table_ref, buf, sems)
    for up, down in copies:
        up.start()
        down.start()
    second = second_ref[...]
    low_u = against(second, su_ref[...]).astype(bf16)
    low_u_ref[...] = low_u
    low = 0.0
    for j in range(count):
        columns = pl.ds(j * tile, tile)
        copies[j][0].wait()
        upward = plain_chunks(second, buf, 0, j)
        upward = upward + plain(low_u, eu_ref[:, columns]) + bias_ref[:, columns]
        active, slope = gelu_parts(upward)
        active = active.astype(bf16)
        active_ref[:, columns] = active
        slope_ref[:, columns] = slope.astype(bf16)
        low = low + against(active, sd_ref[:, columns])
        copies[j][1].wait()
        add_against(total, active, buf, 1, j)
    low_d = low.astype(bf16)
    low_d_ref[...] = low_d
    out_ref[...] = (total[...] + plain(low_d, ed_ref[...])).astype(bf16)


def feed_back_kernel(
    branch_ref, table_ref, slope_ref, eu_ref, sd_ref, su_ref, ed_ref,
    grad_up_ref, inner_d_ref, inner_u_ref, out_ref, buf, sems, total,
):
    _, count, _, _, tile = buf.shape
    copies = feed_copies(table_ref, buf, sems)
    for up, down in copies:
        down.start()
        up.start()
    branch = branch_ref[...]
    inner_d = against(branch, ed_ref[...]).astype(bf16)
    inner_d_ref[...] = inner_d
    inner = 0.0
    for j in range(count):
        columns = pl.ds(j * tile, tile)
        copies[j][1].wait()
        grad = plain_chunks(branch, buf, 1, j) + plain(inner_d, sd_ref[:, columns])
        grad = (grad * slope_ref[:, columns].astype(f32)).astype(bf16)
        grad_up_ref[:, columns] = grad
        inner = inner + against(grad, eu_ref[:, columns])
        copies[j][0].wait()
        add_against(total, grad, buf, 0, j)
    inner_u = inner.astype(bf16)
    inner_u_ref[...] = inner_u
    out_ref[...] = (total[...] + plain(inner_u, su_ref[...])).astype(bf16)


def feed_both_kernel(
    second_ref, branch_ref, table_ref, bias_ref, eu_ref, sd_ref, su_ref, ed_ref,
    active_ref, low_u_ref, low_d_ref, out_ref, grad_up_ref, inner_d_ref, inner_u_ref, back_ref,
    buf, sems, total, back_total,
):
    _, count, _, _, tile = buf.shape
    copies = feed_copies(table_ref, buf, sems)
    for up, down in copies:
        up.start()
        down.start()
    second = second_ref[...]
    branch = branch_ref[...]
    low_u = against(second, su_ref[...]).astype(bf16)
    low_u_ref[...] = low_u
    inner_d = against(branch, ed_ref[...]).astype(bf16)
    inner_d_ref[...] = inner_d
    low = 0.0
    inner = 0.0
    for j in range(count):
        columns = pl.ds(j * tile, tile)
        copies[j][0].wait()
        upward = plain_chunks(second, buf, 0, j)
        upward = upward + plain(low_u, eu_ref[:, columns]) + bias_ref[:, columns]
        active, slope = gelu_parts(upward)
        active = active.astype(bf16)
        active_ref[:, columns] = active
        low = low + against(active, sd_ref[:, columns])
        copies[j][1].wait()
        add_against(total, active, buf, 1, j)
        grad = plain_chunks(branch, buf, 1, j) + plain(inner_d, sd_ref[:, columns])
        grad = (grad * slope).astype(bf16)
        grad_up_ref[:, columns] = grad
        inner = inner + against(grad, eu_ref[:, columns])
        add_against(back_total, grad, buf, 0, j)
    inner_u = inner.astype(bf16)
    inner_u_ref[...] = inner_u
    back_ref[...] = (back_total[...] + plain(inner_u, su_ref[...])).astype(bf16)
    low_d = low.astype(bf16)
    low_d_ref[...] = low_d
    out_ref[...] = (total[...] + plain(low_d, ed_ref[...])).astype(bf16)


def feed_call(kernel, name, inputs, outputs, hidden, totals):
    table = [value for value in inputs if value.ndim == 4][0]
    rows, model = inputs[0].shape
    tile = 512
    chunks = table.shape[0]
    return pl.pallas_call(
        kernel,
        in_specs=[remote if value.ndim == 4 else held for value in inputs],
        out_specs=[held] * len(outputs),
        out_shape=[jax.ShapeDtypeStruct((rows, width), bf16) for width in outputs],
        scratch_shapes=[
            pltpu.VMEM((2, hidden // tile, chunks, model // chunks, tile), bf16),
            pltpu.SemaphoreType.DMA((2, hidden // tile)),
        ]
        + [pltpu.VMEM((rows, model), f32)] * totals,
        compiler_params=pltpu.CompilerParams(vmem_limit_bytes=44 * 2**20),
        cost_estimate=pl.CostEstimate(
            flops=4 * totals * rows * model * hidden,
            bytes_accessed=4 * model * hidden,
            transcendentals=rows * hidden,
        ),
        name=name,
    )(*inputs)


def per_device(
    block_input,
    cotangent,
    doc_lengths,
    bank_choice,
    first_gain,
    first_shift,
    query_weight,
    query_bias,
    keyval_weight,
    value_bias,
    output_weight,
    output_bias,
    second_gain,
    second_shift,
    upward_weight,
    upward_bias,
    downward_weight,
    downward_bias,
    query_shrink,
    query_expand,
    keyval_shrink,
    keyval_expand,
    output_shrink,
    output_expand,
    upward_shrink,
    upward_expand,
    downward_shrink,
    downward_expand,
):
    section = lax.axis_index("section")
    data = lax.axis_index("dp")
    tensor = lax.axis_index("tensor")
    low_section = section == 0
    width = block_input.shape[2]
    rows = block_input.shape[1]
    ranks = lax.axis_size("tensor")
    span = rows * ranks
    head = value_bias.shape[1]
    local_q = query_bias.shape[1]
    local_f = upward_bias.shape[1]
    rank = query_expand.shape[2]
    banks = query_expand.shape[1]
    reach = WINDOW // span
    sides = [(0, 1), (1, 0)]

    def swap(value):
        return lax.ppermute(value, "section", sides)

    def by_layer(own, other):
        return jnp.where(low_section, own, other), jnp.where(low_section, other, own)

    def spread(block):
        parts = [block] + [around(block, "tensor", -j) for j in range(1, ranks)]
        return jnp.concatenate(parts, axis=0)

    def reduce_rows(partial):
        low = partial.astype(bf16)
        total = partial[:rows].astype(f32)
        for j in range(1, ranks):
            total = total + around(low[j * rows : (j + 1) * rows], "tensor", j).astype(f32)
        return total

    own_bank = lax.dynamic_index_in_dim(bank_choice, section, 0, keepdims=False)
    other_bank = lax.dynamic_index_in_dim(bank_choice, 1 - section, 0, keepdims=False)

    chips = lax.axis_size("dp") // 4
    both = ("section", "dp")
    every = ("section", "dp", "tensor")
    order = [
        side * 4 * chips + chip * 4 + near
        for chip in range(chips)
        for side in range(2)
        for near in range(4)
    ]
    order_all = [place * ranks + x for x in range(ranks) for place in order]

    def row_major(block):
        return with_layout_constraint(block, Layout(major_to_minor=(0, 1)))

    def gather(shard):
        table = lax.all_gather(row_major(shard), both, axis=0, tiled=True, axis_index_groups=[order])
        return row_major(table).reshape(chips, 2, -1, shard.shape[1])

    def gather_all(shard):
        table = lax.all_gather(
            row_major(shard), every, axis=0, tiled=True, axis_index_groups=[order_all]
        )
        return row_major(table).reshape(ranks, chips, 2, -1, shard.shape[1])

    def halves(shard):
        cut = shard.shape[1] // 2
        return shard[:, :cut], shard[:, cut:]

    keyval_half = jnp.where(tensor % 2 == 0, keyval_weight[0][:, :head], keyval_weight[0][:, head:])
    early_all = gather_all(
        jnp.concatenate([query_weight[0], row_major(output_weight[0].T), keyval_half], axis=1)
    )
    keyval_ws = [
        jnp.concatenate(
            [early_all[x, :, layer, :, 2 * local_q :].reshape(width, head) for x in range(2)], axis=1
        )
        for layer in range(2)
    ]

    vectors = jnp.concatenate(
        [
            first_gain,
            first_shift,
            jnp.zeros_like(value_bias),
            value_bias,
            output_bias,
            second_gain,
            second_shift,
            upward_bias,
            downward_bias,
        ],
        axis=1,
    )
    vector_sizes = [width, width, 2 * head, width, width, width, local_f, width]
    vector_layers = by_layer(vectors, swap(vectors))

    def chosen(table, bank, transpose):
        block = lax.dynamic_index_in_dim(table[0], bank, 0, keepdims=False)
        return block.T if transpose else block

    def pack(bank, parts):
        return jnp.concatenate([chosen(table, bank, flip) for table, flip in parts], axis=1)

    def exchanged(parts):
        return by_layer(pack(own_bank, parts), swap(pack(other_bank, parts)))

    def cut_pack(parts):
        own = jnp.concatenate([pack(own_bank, parts), query_rows], axis=1)
        other = jnp.concatenate([pack(other_bank, parts), query_rows], axis=1)
        return by_layer(own, swap(other))

    query_rows = jnp.broadcast_to(query_bias, (rank, local_q))
    cut_layers = jnp.stack(cut_pack([(query_expand, False), (output_shrink, True)]))
    cut_parts = jnp.stack(
        [cut_layers] + [around(cut_layers, "tensor", j) for j in range(1, ranks)]
    )
    cut_whole = jnp.stack(
        [
            lax.dynamic_index_in_dim(cut_parts, (tensor - r) % ranks, 0, keepdims=False)
            for r in range(ranks)
        ],
        axis=2,
    ).reshape(2, rank, ranks, 3, local_q)
    eq_all, so_all, query_bias_all = [
        cut_whole[:, :, :, k].reshape(2, rank, ranks * local_q) for k in range(3)
    ]
    early_layers = exchanged([(query_shrink, True), (keyval_shrink, True), (keyval_expand, False)])
    late_layers = exchanged(
        [
            (output_expand, False),
            (upward_shrink, True),
            (upward_expand, False),
            (downward_shrink, True),
            (downward_expand, False),
        ]
    )

    up_halves = halves(upward_weight[0])
    down_halves = halves(row_major(downward_weight[0].T))
    side = [jnp.concatenate([up_halves[h], down_halves[h]], axis=1) for h in range(2)]
    keep = jnp.where(low_section, side[0], side[1])
    gained = swap(jnp.where(low_section, side[1], side[0]))
    feed_tables = [gather(table) for table in by_layer(keep, gained)]

    def split(table, sizes):
        cuts = [0]
        for size in sizes:
            cuts.append(cuts[-1] + size)
        return [table[:, a:b] for a, b in zip(cuts[:-1], cuts[1:])]

    small = [
        [part.astype(f32) for part in split(vector_layers[layer], vector_sizes)]
        for layer in range(2)
    ]
    adapters = [
        split(early_layers[layer], [width, width, 2 * head])
        + split(late_layers[layer], [width, width, local_f, local_f, width])
        for layer in range(2)
    ]

    inside = jnp.arange(rows, dtype=jnp.int32)
    query_place = data * span + tensor * rows + inside
    key_place = jnp.concatenate(
        [
            (data - back) * span + (tensor + j) % ranks * rows + inside
            for j in range(ranks)
            for back in range(reach, -1, -1)
        ]
    )
    lengths = lax.dynamic_index_in_dim(doc_lengths, section, 0, keepdims=False)
    ends = jnp.cumsum(lengths)
    query_doc = jnp.sum((query_place[:, None] >= ends[None, :]).astype(jnp.int32), axis=1)
    key_doc = jnp.sum((key_place[:, None] >= ends[None, :]).astype(jnp.int32), axis=1)
    distance = query_place[:, None] - key_place[None, :]
    allowed = (
        (key_place[None, :] >= 0)
        & (distance >= 0)
        & (distance < WINDOW)
        & (query_doc[:, None] == key_doc[None, :])
    )
    bias = jnp.where(allowed, 0.0, masked_score).astype(bf16)

    def forward_attend(layer, hidden):
        gain1, shift1, kv_bias, out_bias = small[layer][:4]
        sq, skv, ekv, eo = adapters[layer][:4]
        unit1, rsd1 = norm_parts(hidden)
        normed = (unit1 * gain1 + shift1).astype(bf16)
        low_kv = against(normed, skv).astype(bf16)
        keyval = (plain(normed, keyval_ws[layer]) + kv_bias + plain(low_kv, ekv)).astype(bf16)
        pieces = [along(keyval, "dp", back) for back in range(reach, 0, -1)] + [keyval]
        key_block = spread(jnp.concatenate(pieces, axis=0))
        queries, low_q = project_queries(
            layer, normed, early_all, query_bias_all[layer, :1].astype(f32), eq_all[layer], sq
        )
        probs, mixed, low_o, attended = attend(
            layer, queries, key_block, bias, early_all, so_all[layer], eo, head
        )
        middle = hidden + (attended + out_bias)
        return middle, (unit1, rsd1, normed, low_q, low_kv, queries, key_block, probs, mixed, low_o)

    def feed_inputs(layer, middle):
        gain2, shift2, up_bias = small[layer][4:7]
        unit2, rsd2 = norm_parts(middle)
        second = spread((unit2 * gain2 + shift2).astype(bf16))
        return unit2, rsd2, second, up_bias

    def feed_result(layer, middle, partial):
        return middle + (reduce_rows(partial) + small[layer][7])

    def tiles(block):
        return block.reshape(rank, -1, 128).transpose(1, 0, 2)

    def flat(block):
        return block.transpose(1, 0, 2).reshape(rank, -1)

    turn, near = data // 4, data % 4

    def padded(pile, multiple):
        lack = -pile.shape[0] % multiple
        if not lack:
            return pile
        return jnp.concatenate([pile, jnp.zeros((lack,) + pile.shape[1:], pile.dtype)], axis=0)

    def piled(shared, quartered):
        pile = padded(jnp.concatenate([tiles(part) for part in shared], axis=0), ranks)
        return jnp.concatenate(
            [block.reshape((ranks, -1) + block.shape[1:]) for block in [pile] + [tiles(part) for part in quartered]],
            axis=1,
        ).astype(bf16)

    def owned_pile(mine, owned):
        pile = jnp.concatenate([mine] + [tiles(part) for part in owned], axis=0).astype(bf16)
        return padded(pile, lax.axis_size("dp"))

    def at(block, index, axis):
        return lax.dynamic_index_in_dim(block, index, axis, keepdims=False)

    def offloaded_grads(shared, quartered, owned):
        pile = piled(shared, quartered)
        mine = lax.psum_scatter(
            pile.reshape((-1,) + pile.shape[2:]), "tensor", scatter_dimension=0, tiled=True
        )
        return lax.psum_scatter(owned_pile(mine, owned), "dp", scatter_dimension=0, tiled=True)

    def scattered_grads(shared, quartered, owned):
        pile = piled(shared, quartered)
        mine = at(pile, tensor, 0).astype(f32)
        for j in range(1, ranks):
            mine = mine + around(at(pile, (tensor + j) % ranks, 0), "tensor", j).astype(f32)
        pile = owned_pile(mine, owned)
        pile = pile.reshape((chips, 4, -1) + pile.shape[1:])
        mine = at(pile, near, 1).astype(f32)
        for k in range(1, 4):
            mine = mine + flipped(at(pile, near ^ k, 1), "dp", k).astype(f32)
        pile = mine.astype(bf16)
        mine = at(pile, turn, 0).astype(f32)
        for k in range(1, chips):
            mine = mine + flipped(at(pile, turn ^ k, 0), "dp", 4 * k).astype(f32)
        return mine.astype(bf16)

    def crossed(block, mask):
        return lax.ppermute(block, both, [(i, i ^ mask) for i in range(8 * chips)])

    def spread_grads(zero, one, shared, quartered, owned):
        own = jnp.where(low_section, zero, one)
        away = jnp.where(low_section, one, zero)
        dp_size = 4 * chips
        home = jnp.stack([own, flipped(own, "dp", 2)])
        guest = jnp.stack([crossed(away, dp_size), crossed(away, dp_size + 2)])
        home, guest = [
            jnp.where(near // 2 == 0, block, block[::-1]) for block in (home, guest)
        ]
        pair = jnp.where(
            low_section, jnp.stack([home, guest], axis=1), jnp.stack([guest, home], axis=1)
        )
        parts = jnp.stack([pair] + [flipped(pair, "dp", 4 * k) for k in range(1, chips)])
        parts = jnp.stack([at(parts, turn ^ k, 0) for k in range(chips)])
        other = flipped(parts, "dp", 1)
        core = near % 2
        parts = jnp.stack(
            [jnp.where(core == 0, parts, other), jnp.where(core == 0, other, parts)], axis=2
        )
        pile = jnp.moveaxis(parts, 3, 0).reshape((2, -1) + parts.shape[5:])
        shared_sizes = [part.shape[1] // 128 for part in shared]
        quarter_sizes = [part.shape[1] // 128 // ranks for part in quartered]
        owned_sizes = [part.shape[1] // 128 for part in owned]
        each = -(-sum(shared_sizes) // ranks)
        own = pile[:, :each]
        parts = jnp.stack([own] + [around(own, "tensor", k) for k in range(1, ranks)])
        ordered = jnp.concatenate([at(parts, (tensor - r) % ranks, 0) for r in range(ranks)], axis=1)
        results = []
        for whole, begin, sizes in [
            (ordered, 0, shared_sizes),
            (pile, each, quarter_sizes + owned_sizes),
        ]:
            for count in sizes:
                results.append([flat(whole[m, begin : begin + count]) for m in range(2)])
                begin += count
        return results

    def feed_grads(layer, grad, unit2, rsd2, partial):
        return grad + norm_back(unit2, rsd2, reduce_rows(partial) * small[layer][4])

    def feed_adapters(second, branch, low_u, low_d, inner_u, inner_d, active, grad_up):
        shared = [across(inner_u, second), across(low_d, branch)]
        owned = [across(low_u, grad_up), across(inner_d, active)]
        return shared, owned

    def backward_attend(layer, kept, grad_middle):
        gain1 = small[layer][0]
        sq, skv, ekv, eo = adapters[layer][:4]
        unit1, rsd1, normed, low_q, low_kv, queries, key_block, probs, mixed, low_o = kept
        branch = grad_middle.astype(bf16)
        grad_q, grad_block, inner_o, inner_q, partial = attend_back(
            layer, branch, early_all, so_all[layer], eo, probs, queries, key_block,
            eq_all[layer], sq, head,
        )
        count = (reach + 1) * rows
        blocks = grad_block[:count].astype(f32)
        for j in range(1, ranks):
            part = grad_block[j * count : (j + 1) * count]
            blocks = blocks + around(part, "tensor", j).astype(f32)
        own = blocks[reach * rows :]
        for back in range(1, reach + 1):
            begin = (reach - back) * rows
            own = own + along(blocks[begin : begin + rows].astype(bf16), "dp", -back).astype(f32)
        grad_kv = own.astype(bf16)
        inner_kv = against(grad_kv, ekv).astype(bf16)
        grad_normed = partial + against(grad_kv, keyval_ws[layer]) + plain(inner_kv, skv)
        grad_hidden = grad_middle + norm_back(unit1, rsd1, grad_normed * gain1)
        shared = [
            across(low_o, branch),
            across(inner_q, normed),
            across(inner_kv, normed),
            across(low_kv, grad_kv),
        ]
        quartered = [across(low_q, grad_q), across(inner_o, mixed)]
        return grad_hidden, shared, quartered

    fresh = lax.dynamic_index_in_dim(block_input, section, 0, keepdims=False).astype(f32)
    given = lax.dynamic_index_in_dim(cotangent, section, 0, keepdims=False).astype(f32)

    middle_zero, kept_zero = forward_attend(0, fresh)
    unit_zero, rsd_zero, second_zero, up_bias = feed_inputs(0, middle_zero)
    su, eu, sd, ed = adapters[0][4:]
    active_zero, slope_zero, low_u_zero, low_d_zero, partial = feed_call(
        feed_kernel,
        "feed",
        (second_zero, feed_tables[0], up_bias, eu, sd, su, ed),
        (local_f, local_f, rank, rank, width),
        local_f,
        1,
    )
    passed = feed_result(0, middle_zero, partial).astype(bf16)

    middle_one, kept_one = forward_attend(1, passed.astype(f32))
    unit_one, rsd_one, second_one, up_bias = feed_inputs(1, middle_one)
    su, eu, sd, ed = adapters[1][4:]
    branch_one = spread(given.astype(bf16))
    active, low_u, low_d, partial, grad_up, inner_d, inner_u, partial_back = feed_call(
        feed_both_kernel,
        "feed_both",
        (second_one, branch_one, feed_tables[1], up_bias, eu, sd, su, ed),
        (local_f, rank, rank, width, local_f, rank, rank, width),
        local_f,
        2,
    )
    shared, owned = feed_adapters(
        second_one, branch_one, low_u, low_d, inner_u, inner_d, active, grad_up
    )
    grad_middle = feed_grads(1, given, unit_one, rsd_one, partial_back)
    grad_one, more, quartered = backward_attend(1, kept_one, grad_middle)
    mine_one = offloaded_grads(shared + more, quartered, owned)

    su, eu, sd, ed = adapters[0][4:]
    branch_zero = spread(grad_one.astype(bf16))
    grad_up, inner_d, inner_u, partial_back = feed_call(
        feed_back_kernel,
        "feed_back",
        (branch_zero, feed_tables[0], slope_zero, eu, sd, su, ed),
        (local_f, rank, rank, width),
        local_f,
        1,
    )
    shared, owned = feed_adapters(
        second_zero, branch_zero, low_u_zero, low_d_zero, inner_u, inner_d, active_zero, grad_up
    )
    grad_middle_zero = feed_grads(0, grad_one, unit_zero, rsd_zero, partial_back)
    partial, _ = lax.optimization_barrier((partial, grad_middle_zero))
    final = feed_result(1, middle_one, partial).astype(bf16)
    grad_zero, more, quartered = backward_attend(0, kept_zero, grad_middle_zero)
    shared = shared + more
    mine_zero = scattered_grads(shared, quartered, owned)
    grads = spread_grads(mine_zero, mine_one, shared, quartered, owned)

    def both_micros(zero, one, kind):
        own = jnp.where(low_section, zero, one)
        received = swap(jnp.where(low_section, one, zero).astype(bf16)).astype(kind)
        return jnp.where(low_section, jnp.stack([own, received]), jnp.stack([received, own]))

    section_outputs = both_micros(passed, final, bf16)
    input_grads = both_micros(grad_zero, grad_one, f32)
    onehot = (bank_choice[:, None] == jnp.arange(banks)[None, :]).astype(f32)

    def placed(pair, transpose):
        out = sum(
            onehot[m][:, None, None] * pair[m].astype(f32)[None] for m in range(2)
        )
        return (out.transpose(0, 2, 1) if transpose else out)[None]

    (
        up_shrink_grad,
        down_expand_grad,
        out_expand_grad,
        q_shrink_grad,
        kv_shrink_grad,
        kv_expand_grad,
        q_expand_grad,
        out_shrink_grad,
        up_expand_grad,
        down_shrink_grad,
    ) = grads
    return (
        section_outputs[None],
        input_grads[None],
        placed(q_shrink_grad, True),
        placed(q_expand_grad, False),
        placed(kv_shrink_grad, True),
        placed(kv_expand_grad, False),
        placed(out_shrink_grad, True),
        placed(out_expand_grad, False),
        placed(up_shrink_grad, True),
        placed(up_expand_grad, False),
        placed(down_shrink_grad, True),
        placed(down_expand_grad, False),
    )


def solution(mesh):
    return jax.shard_map(
        per_device,
        mesh=mesh,
        in_specs=(
            P(None, ("dp", "tensor"), None),
            P(None, ("dp", "tensor"), None),
            P(),
            P(),
            P("section", None),
            P("section", None),
            P("section", "dp", "tensor"),
            P("section", "tensor"),
            P("section", "dp", None),
            P("section", None),
            P("section", "tensor", "dp"),
            P("section", None),
            P("section", None),
            P("section", None),
            P("section", "dp", "tensor"),
            P("section", "tensor"),
            P("section", "tensor", "dp"),
            P("section", None),
            P("section", None, None, None),
            P("section", None, None, "tensor"),
            P("section", None, None, None),
            P("section", None, None, None),
            P("section", None, "tensor", None),
            P("section", None, None, None),
            P("section", None, None, None),
            P("section", None, None, "tensor"),
            P("section", None, "tensor", None),
            P("section", None, None, None),
        ),
        out_specs=(
            P("section", None, ("dp", "tensor"), None),
            P("section", None, ("dp", "tensor"), None),
            P("section", None, None, None),
            P("section", None, None, "tensor"),
            P("section", None, None, None),
            P("section", None, None, None),
            P("section", None, "tensor", None),
            P("section", None, None, None),
            P("section", None, None, None),
            P("section", None, None, "tensor"),
            P("section", None, "tensor", None),
            P("section", None, None, None),
        ),
        check_vma=False,
    )
```

time: 604 us -> 606 us (level)
  local copies, waits for them, and re-layouts: 109 us -> 38.3 us
  waiting for transfers between devices: 208 us -> 273 us
  Pallas kernels: 55.6 us -> 92.4 us
  starting transfers between devices: 152 us -> 134 us
  matrix products: 17.9 us -> 7.71 us
    reduce_scatter x1, waiting for transfers between devices: 0.02 us -> 51.3 us  [offloaded_grads(): lax.psum_scatter(owned_pile(mine, owned), 'dp', scatter_dimension=0, tile...]
    all_gather x3, waiting for transfers between devices: 29.6 us -> 77.2 us  [the longest x1 64.5 us: gather_all(): lax.all_gather(row_major(shard), every, axis=0, tiled=True, axis_index_gr...]
    all_gather x2 -> x0, local copies, waits for them, and re-layouts: 45.4 us -> none  [gather(): lax.all_gather(shard, both, axis=0, tiled=True, axis_index_groups=[order])]
    pallas_call x8 -> x9, Pallas kernels: 55.6 us -> 92.4 us  [the longest x3 41 us: feed_call(): pl.pallas_call(kernel, in_specs=[remote if value.ndim == 4 else held for...]
    unnamed x313 -> x325, local copies, waits for them, and re-layouts: 46.1 us -> 24.1 us
    ppermute x54 -> x45, waiting for transfers between devices: 131 us -> 112 us  [around(): lax.ppermute(block, axis, [(i, (i + distance) % size) for i in range(size)])]
    ppermute x54 -> x45, starting transfers between devices: 80.4 us -> 63.4 us  [around(): lax.ppermute(block, axis, [(i, (i + distance) % size) for i in range(size)])]
    ppermute x16, waiting for transfers between devices: 20.4 us -> 6.9 us  [along(): return lax.ppermute(block, axis, route)]
  transfers between devices with their start and end apart: 94 -> 86, of which waited for: 54 -> 50; matrix products, arithmetic and copies ran while one was open for 19% -> 8% of each run, Pallas kernels for 5% -> 11%
where the time goes in v5:
time: 606 us; the launch traced here: 596 us
  waiting for transfers between devices  273 us (45%)
  starting transfers between devices  134 us (22%)
  Pallas kernels  92.4 us (15%)
  local copies, waits for them, and re-layouts  38.3 us (6%)
  other arithmetic  30.1 us (5%)
  between operations  20.9 us (3%)
  matrix products  7.71 us (1%)
    ppermute x45, waiting for transfers between devices, around(): lax.ppermute(block, axis, [(i, (i + distance) % size) for i in range(size)])  112 us
    all_gather x1, waiting for transfers between devices, gather_all(): lax.all_gather(row_major(shard), every, axis=0, tiled=True, axis_index_gr...  64.5 us
    ppermute x45, starting transfers between devices, around(): lax.ppermute(block, axis, [(i, (i + distance) % size) for i in range(size)])  63.4 us
    reduce_scatter x1, waiting for transfers between devices, offloaded_grads(): lax.psum_scatter(owned_pile(mine, owned), 'dp', scatter_dimension=0, tile...  51.3 us
    pallas_call x3, Pallas kernels, feed_call(): pl.pallas_call(kernel, in_specs=[remote if value.ndim == 4 else held for...  41 us
    ppermute x16, starting transfers between devices, along(): return lax.ppermute(block, axis, route)  32.3 us
    unnamed x325, local copies, waits for them, and re-layouts  24.1 us
    pallas_call x2, Pallas kernels, attend_back(): pl.pallas_call(lambda *refs: attend_back_kernel(layer, head, *refs), in_s...  23 us
  transfers between devices with their start and end apart: 86, of which 50 were waited for; matrix products, arithmetic and copies ran while one was open for 8% of the time, Pallas kernels for 11%

profile of v5, /device:TPU:0, one launch (start us, length us, event | category | flops | bytes accessed | tf_op | source)
XLA Modules:
  0.0 595.6 jit_solution(12868772283647677801)
XLA Ops:
  12.4 4.0 collective-permute-start.17
  16.5 12.2 %collective-permute-done.17 = bf16[128,2048]{1,0:T(8,128)(2,1)S(1)} collective-permute-done((bf16[128,2048]{1,0:T(8,128)(2,1)S(1)}, bf16[128,2048]{1,0:T(8,128)(2,1)S(1)}, u32[]{:S(2)}, u32[]{:S(2)}) %collective-permute-start.17) | collective-permute-done | bytes 524320 | tf_op jit(solution)/shard_map/ppermute | solution.py:488
  31.1 4.1 collective-permute-start
  43.0 3.6 collective-permute-start.5
  57.1 2.8 collective-permute-start.4
  64.3 3.2 collective-permute-done.3
  71.3 64.5 %all-gather.4.cloned.1.call-done = bf16[16384,1152]{1,0:T(8,128)(2,1)} async-done(((bf16[128,1152]{1,0:T(8,128)(2,1)}), bf16[16384,1152]{1,0:T(8,128)(2,1)}) %all-gather.4.cloned.1.call-update) | async-done | bytes 37748752 | tf_op jit(solution)/shard_map/all_gather | solution.py:526
  139.1 3.4 collective-permute-start.6
  144.8 4.1 collective-permute-start.8
  154.6 4.4 project_queries.2
  162.0 5.4 collective-permute-done.12
  167.5 10.3 %attend.2 = (f32[4,256,1280]{2,1,0:T(8,128)S(1)}, bf16[64,2048]{1,0:T(8,128)(2,1)S(1)}, bf16[64,16]{1,0:T(8,128)(2,1)S(1)}, f32[64,2048]{1,0:T(8,128)S(1)}) custom-call(bf16[64,2048]{1,0:T(8,128)(2,1)S(1)} %get-tuple-element.52.refs_0_.refs_5_, bf16[1280,256]{1,0:T(8,128)(2,1)S(1)} %constant_dynamic-update-slice_fusion.18.refs_1_.refs_6_, ...), custom_call_target="tpu_custom_call" | custom-call | flops 2818572288 | bytes 8388608 | tf_op jit(solution)/shard_map/attend/pallas_call | solution.py:180
  188.2 8.8 %collective-permute-done.16 = bf16[64,2048]{1,0:T(8,128)(2,1)S(1)} collective-permute-done((bf16[64,2048]{1,0:T(8,128)(2,1)S(1)}, bf16[64,2048]{1,0:T(8,128)(2,1)S(1)}, u32[]{:S(2)}, u32[]{:S(2)}) %collective-permute-start.16) | collective-permute-done | bytes 262176 | tf_op jit(solution)/shard_map/ppermute | solution.py:32
  197.9 12.7 %all-gather.6.cloned.1.call-done = bf16[4096,2048]{1,0:T(8,128)(2,1)} async-done(((bf16[128,2048]{1,0:T(8,128)(2,1)}), bf16[4096,2048]{1,0:T(8,128)(2,1)}) %all-gather.6.cloned.1.call-update) | async-done | bytes 16777232 | tf_op jit(solution)/shard_map/all_gather | solution.py:522
  210.7 12.1 %feed.1 = (bf16[256,2048]{1,0:T(8,128)(2,1)S(1)}, bf16[256,2048]{1,0:T(8,128)(2,1)S(1)}, bf16[256,16]{1,0:T(8,128)(2,1)S(1)}, bf16[256,16]{1,0:T(8,128)(2,1)S(1)}, bf16[256,2048]{1,0:T(8,128)(2,1)S(1)}) custom-call(bf16[256,2048]{1,0:T(8,128)(2,1)S(1)} %pad_maximum_fusion.1.second_ref, bf16[4,2,512,2048]{3,2,1,0:T(8,128)(2,1)} %bitcast.759, ...), custom_call_target="tpu_custom_call" | custom-call | flops 4294967296 | bytes 16777216 | tf_op jit(solution)/shard_map/feed/pallas_call | solution.py:421
  228.4 8.9 %collective-permute-done.20 = bf16[64,2048]{1,0:T(8,128)(2,1)S(1)} collective-permute-done((bf16[64,2048]{1,0:T(8,128)(2,1)S(1)}, bf16[64,2048]{1,0:T(8,128)(2,1)S(1)}, u32[]{:S(2)}, u32[]{:S(2)}) %collective-permute-start.20) | collective-permute-done | bytes 262176 | tf_op jit(solution)/shard_map/ppermute | solution.py:32
  237.3 3.7 collective-permute-start.31
  242.7 3.5 collective-permute-start.21
  248.2 4.7 collective-permute-start.23
  256.6 4.4 project_queries.3
  263.0 5.4 collective-permute-done.27
  268.4 9.3 %attend.3 = (f32[4,256,1280]{2,1,0:T(8,128)S(1)}, bf16[64,2048]{1,0:T(8,128)(2,1)S(1)}, bf16[64,16]{1,0:T(8,128)(2,1)S(1)}, f32[64,2048]{1,0:T(8,128)S(1)}) custom-call(bf16[64,2048]{1,0:T(8,128)(2,1)S(1)} %get-tuple-element.55.refs_0_.refs_5_, bf16[1280,256]{1,0:T(8,128)(2,1)S(1)} %constant_dynamic-update-slice_fusion.41.refs_1_.refs_6_, ...), custom_call_target="tpu_custom_call" | custom-call | flops 2818572288 | bytes 8388608 | tf_op jit(solution)/shard_map/attend/pallas_call | solution.py:180
  281.3 4.1 collective-permute-start.29
  287.4 3.9 collective-permute-done.30
  291.3 6.9 %collective-permute-done.29 = bf16[64,2048]{1,0:T(8,128)(2,1)} collective-permute-done((bf16[64,2048]{1,0:T(8,128)(2,1)S(1)}, bf16[64,2048]{1,0:T(8,128)(2,1)}, u32[]{:S(2)}, u32[]{:S(2)}) %collective-permute-start.29) | collective-permute-done | bytes 262176 | tf_op jit(solution)/shard_map/ppermute | solution.py:32
  303.6 17.7 %feed_both.1 = (bf16[256,2048]{1,0:T(8,128)(2,1)S(1)}, bf16[256,16]{1,0:T(8,128)(2,1)S(1)}, bf16[256,16]{1,0:T(8,128)(2,1)S(1)}, bf16[256,2048]{1,0:T(8,128)(2,1...) custom-call(bf16[256,2048]{1,0:T(8,128)(2,1)S(1)} %pad_maximum_fusio, ...), custom_call_target="tpu_custom_call" | custom-call | flops 8589934592 | bytes 16777216 | tf_op jit(solution)/shard_map/feed_both/pallas_call | solution.py:421
  321.4 3.0 collective-permute-start.36
  327.8 8.0 %collective-permute-done.36 = bf16[64,2048]{1,0:T(8,128)(2,1)S(1)} collective-permute-done((bf16[64,2048]{1,0:T(8,128)(2,1)S(1)}, bf16[64,2048]{1,0:T(8,128)(2,1)S(1)}, u32[]{:S(2)}, u32[]{:S(2)}) %collective-permute-start.36) | collective-permute-done | bytes 262176 | tf_op jit(solution)/shard_map/ppermute | solution.py:32
  335.8 3.4 collective-permute-done.34
  342.5 11.5 %attend_back.2 = (bf16[64,2048]{1,0:T(8,128)(2,1)S(1)}, bf16[1280,256]{1,0:T(8,128)(2,1)S(1)}, bf16[64,16]{1,0:T(8,128)(2,1)S(1)}, bf16[64,16]{1,0:T(8,128)(2,1)S(1)}, f32[64,2048]{1,0:T(8,128)S(1)}) custom-call(bf16[64,2048]{1,0:T(8,128)(2,1)S(1)} %get-tuple-element.113.refs_0_, bf16[4,4,2,512,1152]{4,3,2,1,0:T(8,128)(2,1)} %bitcast.757, ...), custom_call_target="tpu_custom_call" | custom-call | flops 5637144576 | bytes 22020096 | tf_op jit(solution)/shard_map/attend_back/pallas_call | solution.py:257
  356.9 4.4 collective-permute-done.39
  381.4 10.8 %collective-permute-done.46 = bf16[64,2048]{1,0:T(8,128)(2,1)} collective-permute-done((bf16[64,2048]{1,0:T(8,128)(2,1)}, bf16[64,2048]{1,0:T(8,128)(2,1)}, u32[]{:S(2)}, u32[]{:S(2)}) %collective-permute-start.46) | collective-permute-done | bytes 262176 | tf_op jit(solution)/shard_map/ppermute | solution.py:32
  394.6 11.2 %feed_back.1 = (bf16[256,2048]{1,0:T(8,128)(2,1)S(1)}, bf16[256,16]{1,0:T(8,128)(2,1)S(1)}, bf16[256,16]{1,0:T(8,128)(2,1)S(1)}, bf16[256,2048]{1,0:T(8,128)(2,1)S(1)}) custom-call(bf16[256,2048]{1,0:T(8,128)(2,1)S(1)} %pad_maximum_fusion.5.branch_ref, bf16[4,2,512,2048]{3,2,1,0:T(8,128)(2,1)} %bitcast.760, bf16[256,2048]{1,0:T(8,128)(2,1)S(1)} %copy-done.15, ...), custom_call_target="tpu_custom_call" | custom-call | flops 4294967296 | bytes 16777216 | tf_op jit(solution)/shard_map/feed_back/pallas_call | solution.py:421
  406.0 2.9 collective-permute-start.49
  411.0 9.3 %collective-permute-done.49 = bf16[64,2048]{1,0:T(8,128)(2,1)S(1)} collective-permute-done((bf16[64,2048]{1,0:T(8,128)(2,1)S(1)}, bf16[64,2048]{1,0:T(8,128)(2,1)S(1)}, u32[]{:S(2)}, u32[]{:S(2)}) %collective-permute-start.49) | collective-permute-done | bytes 262176 | tf_op jit(solution)/shard_map/ppermute | solution.py:32
  420.3 3.4 collective-permute-done.47
  428.2 11.6 %attend_back.3 = (bf16[64,2048]{1,0:T(8,128)(2,1)S(1)}, bf16[1280,256]{1,0:T(8,128)(2,1)S(1)}, bf16[64,16]{1,0:T(8,128)(2,1)S(1)}, bf16[64,16]{1,0:T(8,128)(2,1)S(1)}, f32[64,2048]{1,0:T(8,128)S(1)}) custom-call(bf16[64,2048]{1,0:T(8,128)(2,1)S(1)} %get-tuple-element.104.refs_0_, bf16[4,4,2,512,1152]{4,3,2,1,0:T(8,128)(2,1)} %bitcast.758, ...), custom_call_target="tpu_custom_call" | custom-call | flops 5637144576 | bytes 22020096 | tf_op jit(solution)/shard_map/attend_back/pallas_call | solution.py:257
  443.9 3.2 collective-permute-done.56
  467.4 4.7 collective-permute-start.50
  478.8 3.7 collective-permute-done.67
  486.7 8.4 %collective-permute-start.70 = (bf16[4,16,128]{2,1,0:T(8,128)(2,1)S(1)}, bf16[4,16,128]{2,1,0:T(8,128)(2,1)S(1)}, u32[]{:S(2)}, u32[]{:S(2)}) collective-permute-start(bf16[4,16,128]{2,1,0:T(8,128)(2,1)S(1)} %get-tuple-element.249), channel_id=1, source_target_pairs={{0,48},{4,52},{8,56},{12,60},{16,32},{20,36},{24,40},{28,44},{32,1... | collective-permute-start | bytes 49160 | tf_op jit(solution)/shard_map/ppermute | solution.py:43
  496.1 3.5 collective-permute-start.53
  500.4 51.3 %reduce-scatter.5.cloned.1.call-done = bf16[4,16,128]{2,1,0:T(8,128)(2,1)} async-done(((bf16[64,16,128]{2,1,0:T(8,128)(2,1)}), bf16[4,16,128]{2,1,0:T(8,128)(2,1)}) %reduce-scatter.5.cloned.1.call-update) | async-done | bytes 16400 | tf_op jit(solution)/shard_map/reduce_scatter | solution.py:709
  552.5 2.9 collective-permute-start.72
  559.6 3.8 collective-permute-start.74
  568.8 2.9 collective-permute-start.80
  575.2 4.5 collective-permute-done.80
  580.5 2.9 collective-permute-done.78
  (686 shorter events, 175.2 us)
Async XLA Ops:
  7.2 128.6 %all-gather.4.cloned.1.call-start = ((), (), s32[]{:S(2)}) async-start(), calls=%async_computation.2 | async-start | bytes 38043648 | tf_op jit(solution)/shard_map/all_gather | solution.py:526
  10.8 199.8 %all-gather.6.cloned.1.call-start = ((), (), s32[]{:S(2)}) async-start(), calls=%async_computation.3 | async-start | bytes 17301504 | tf_op jit(solution)/shard_map/all_gather | solution.py:522
  12.4 16.3 %collective-permute-start.17 = (bf16[128,2048]{1,0:T(8,128)(2,1)S(1)}, bf16[128,2048]{1,0:T(8,128)(2,1)S(1)}, u32[]{:S(2)}, u32[]{:S(2)}) collective-permute-start(bf16[128,2048]{1,0:T(8,128)(2,1)S(1)} %broadcast_select_fusion.2), channel_id=1, source_target_pairs={{0,64},{64,0},{1,65},{65,1},{2,66},{66,2},{3,67},{67,3},{4,68},{68... | collective-permute-start | bytes 1572872 | tf_op jit(solution)/shard_map/ppermute | solution.py:488
  30.0 269.5 %all-gather.8.cloned.1.call-start = ((), (), s32[]{:S(2)}) async-start(), calls=%async_computation.4 | async-start | bytes 17301504 | tf_op jit(solution)/shard_map/all_gather | solution.py:522
  30.8 454.2 %reduce-scatter.3.cloned.1.call-start = ((), (), s32[]{:S(2)}) async-start(), calls=%async_computation.5 | async-start | bytes 593920 | tf_op jit(solution)/shard_map/reduce_scatter | solution.py:706
  31.1 24.4 %collective-permute-start = (bf16[1,14592]{1,0:T(2,128)(2,1)S(1)}, bf16[1,14592]{1,0:T(2,128)(2,1)S(1)}, u32[]{:S(2)}, u32[]{:S(2)}) collective-permute-start(bf16[1,14592]{1,0:T(2,128)(2,1)S(1)} %constant_dynamic-update-slice_fusion), channel_id=1, source_target_pairs={{0,64},{64,0},{1,65},{65,1},{2,66},{66,2},{3,67},{67,3},{4,68},{68... | collective-permute-start | bytes 87560 | tf_op jit(solution)/shard_map/ppermute | solution.py:488
  41.2 15.8 %collective-permute-start.1 = (bf16[16,1536]{1,0:T(8,128)(2,1)S(1)}, bf16[16,1536]{1,0:T(8,128)(2,1)S(1)}, u32[]{:S(2)}, u32[]{:S(2)}) collective-permute-start(bf16[16,1536]{1,0:T(8,128)(2,1)S(1)} %maximum_maximum_fusion.1), channel_id=1, source_target_pairs={{0,64},{64,0},{1,65},{65,1},{2,66},{66,2},{3,67},{67,3},{4,68},{68... | collective-permute-start | bytes 147464 | tf_op jit(solution)/shard_map/ppermute | solution.py:488
  43.0 18.6 %collective-permute-start.5 = (bf16[16,4352]{1,0:T(8,128)(2,1)S(1)}, bf16[16,4352]{1,0:T(8,128)(2,1)S(1)}, u32[]{:S(2)}, u32[]{:S(2)}) collective-permute-start(bf16[16,4352]{1,0:T(8,128)(2,1)S(1)} %pad_maximum_fusion.20), channel_id=1, source_target_pairs={{0,64},{64,0},{1,65},{65,1},{2,66},{66,2},{3,67},{67,3},{4,68},{68... | collective-permute-start | bytes 417800 | tf_op jit(solution)/shard_map/ppermute | solution.py:488
  54.2 17.0 %collective-permute-start.13 = (bf16[16,10240]{1,0:T(8,128)(2,1)}, bf16[16,10240]{1,0:T(8,128)(2,1)S(1)}, u32[]{:S(2)}, u32[]{:S(2)}) collective-permute-start(bf16[16,10240]{1,0:T(8,128)(2,1)} %get-tuple-element.172), channel_id=1, source_target_pairs={{0,64},{64,0},{1,65},{65,1},{2,66},{66,2},{3,67},{67,3},{4,68},{68... | collective-permute-start | bytes 983048 | tf_op jit(solution)/shard_map/ppermute | solution.py:488
  139.1 11.3 %collective-permute-start.6 = (bf16[64,256]{1,0:T(8,128)(2,1)S(1)}, bf16[64,256]{1,0:T(8,128)(2,1)S(1)}, u32[]{:S(2)}, u32[]{:S(2)}) collective-permute-start(bf16[64,256]{1,0:T(8,128)(2,1)S(1)} %fusion.20), channel_id=1, source_target_pairs={{0,16},{4,20},{8,24},{12,28},{16,32},{20,36},{24,40},{28,44},{32,4... | collective-permute-start | bytes 98312 | tf_op jit(solution)/shard_map/ppermute | solution.py:38
  151.2 8.9 %collective-permute-start.10 = (bf16[320,256]{1,0:T(8,128)(2,1)S(1)}, bf16[320,256]{1,0:T(8,128)(2,1)S(1)}, u32[]{:S(2)}, u32[]{:S(2)}) collective-permute-start(bf16[320,256]{1,0:T(8,128)(2,1)S(1)} %get-tuple-element.281), channel_id=1, source_target_pairs={{0,3},{1,0},{2,1},{3,2},{4,7},{5,4},{6,5},{7,6},{8,11},{9,8},{10,9... | collective-permute-start | bytes 491528 | tf_op jit(solution)/shard_map/ppermute | solution.py:32
  159.0 8.4 %collective-permute-start.12 = (bf16[320,256]{1,0:T(8,128)(2,1)S(1)}, bf16[320,256]{1,0:T(8,128)(2,1)S(1)}, u32[]{:S(2)}, u32[]{:S(2)}) collective-permute-start(bf16[320,256]{1,0:T(8,128)(2,1)S(1)} %get-tuple-element.281), channel_id=1, source_target_pairs={{0,1},{1,2},{2,3},{3,0},{4,5},{5,6},{6,7},{7,4},{8,9},{9,10},{10,1... | collective-permute-start | bytes 491528 | tf_op jit(solution)/shard_map/ppermute | solution.py:32
  180.9 16.1 %collective-permute-start.16 = (bf16[64,2048]{1,0:T(8,128)(2,1)S(1)}, bf16[64,2048]{1,0:T(8,128)(2,1)S(1)}, u32[]{:S(2)}, u32[]{:S(2)}) collective-permute-start(bf16[64,2048]{1,0:T(8,128)(2,1)S(1)} %add_convert_fusion.3), channel_id=1, source_target_pairs={{0,1},{1,2},{2,3},{3,0},{4,5},{5,6},{6,7},{7,4},{8,9},{9,10},{10,1... | collective-permute-start | bytes 786440 | tf_op jit(solution)/shard_map/ppermute | solution.py:32
  180.9 16.0 %collective-permute-start.15 = (bf16[64,2048]{1,0:T(8,128)(2,1)S(1)}, bf16[64,2048]{1,0:T(8,128)(2,1)S(1)}, u32[]{:S(2)}, u32[]{:S(2)}) collective-permute-start(bf16[64,2048]{1,0:T(8,128)(2,1)S(1)} %add_convert_fusion.3), channel_id=1, source_target_pairs={{0,2},{1,3},{2,0},{3,1},{4,6},{5,7},{6,4},{7,5},{8,10},{9,11},{10,... | collective-permute-start | bytes 786440 | tf_op jit(solution)/shard_map/ppermute | solution.py:32
  181.6 16.2 %collective-permute-start.14 = (bf16[64,2048]{1,0:T(8,128)(2,1)S(1)}, bf16[64,2048]{1,0:T(8,128)(2,1)S(1)}, u32[]{:S(2)}, u32[]{:S(2)}) collective-permute-start(bf16[64,2048]{1,0:T(8,128)(2,1)S(1)} %add_convert_fusion.3), channel_id=1, source_target_pairs={{0,3},{1,0},{2,1},{3,2},{4,7},{5,4},{6,5},{7,6},{8,11},{9,8},{10,9... | collective-permute-start | bytes 786440 | tf_op jit(solution)/shard_map/ppermute | solution.py:32
  184.2 101.2 %collective-permute-start.33 = (bf16[64,2048]{1,0:T(8,128)(2,1)S(1)}, bf16[64,2048]{1,0:T(8,128)(2,1)}, u32[]{:S(2)}, u32[]{:S(2)}) collective-permute-start(bf16[64,2048]{1,0:T(8,128)(2,1)S(1)} %dynamic-slice_bitcast_fusion), channel_id=1, source_target_pairs={{0,1},{1,2},{2,3},{3,0},{4,5},{5,6},{6,7},{7,4},{8,9},{9,10},{10,1... | collective-permute-start | bytes 786440 | tf_op jit(solution)/shard_map/ppermute | solution.py:32
  185.1 101.0 %collective-permute-start.32 = (bf16[64,2048]{1,0:T(8,128)(2,1)S(1)}, bf16[64,2048]{1,0:T(8,128)(2,1)}, u32[]{:S(2)}, u32[]{:S(2)}) collective-permute-start(bf16[64,2048]{1,0:T(8,128)(2,1)S(1)} %dynamic-slice_bitcast_fusion), channel_id=1, source_target_pairs={{0,2},{1,3},{2,0},{3,1},{4,6},{5,7},{6,4},{7,5},{8,10},{9,11},{10,... | collective-permute-start | bytes 786440 | tf_op jit(solution)/shard_map/ppermute | solution.py:32
  222.9 14.4 %collective-permute-start.20 = (bf16[64,2048]{1,0:T(8,128)(2,1)S(1)}, bf16[64,2048]{1,0:T(8,128)(2,1)S(1)}, u32[]{:S(2)}, u32[]{:S(2)}) collective-permute-start(bf16[64,2048]{1,0:T(8,128)(2,1)S(1)} %get-tuple-element.138), channel_id=1, source_target_pairs={{0,3},{1,0},{2,1},{3,2},{4,7},{5,4},{6,5},{7,6},{8,11},{9,8},{10,9... | collective-permute-start | bytes 786440 | tf_op jit(solution)/shard_map/ppermute | solution.py:32
  225.7 15.3 %collective-permute-start.19 = (bf16[64,2048]{1,0:T(8,128)(2,1)S(1)}, bf16[64,2048]{1,0:T(8,128)(2,1)S(1)}, u32[]{:S(2)}, u32[]{:S(2)}) collective-permute-start(bf16[64,2048]{1,0:T(8,128)(2,1)S(1)} %get-tuple-element.139), channel_id=1, source_target_pairs={{0,2},{1,3},{2,0},{3,1},{4,6},{5,7},{6,4},{7,5},{8,10},{9,11},{10,... | collective-permute-start | bytes 786440 | tf_op jit(solution)/shard_map/ppermute | solution.py:32
  226.5 14.5 %collective-permute-start.18 = (bf16[64,2048]{1,0:T(8,128)(2,1)S(1)}, bf16[64,2048]{1,0:T(8,128)(2,1)S(1)}, u32[]{:S(2)}, u32[]{:S(2)}) collective-permute-start(bf16[64,2048]{1,0:T(8,128)(2,1)S(1)} %get-tuple-element.137), channel_id=1, source_target_pairs={{0,1},{1,2},{2,3},{3,0},{4,5},{5,6},{6,7},{7,4},{8,9},{9,10},{10,1... | collective-permute-start | bytes 786440 | tf_op jit(solution)/shard_map/ppermute | solution.py:32
  237.3 48.9 %collective-permute-start.31 = (bf16[64,2048]{1,0:T(8,128)(2,1)S(1)}, bf16[64,2048]{1,0:T(8,128)(2,1)}, u32[]{:S(2)}, u32[]{:S(2)}) collective-permute-start(bf16[64,2048]{1,0:T(8,128)(2,1)S(1)} %dynamic-slice_bitcast_fusion), channel_id=1, source_target_pairs={{0,3},{1,0},{2,1},{3,2},{4,7},{5,4},{6,5},{7,6},{8,11},{9,8},{10,9... | collective-permute-start | bytes 786440 | tf_op jit(solution)/shard_map/ppermute | solution.py:32
  281.2 10.1 %collective-permute-start.30 = (bf16[64,2048]{1,0:T(8,128)(2,1)S(1)}, bf16[64,2048]{1,0:T(8,128)(2,1)}, u32[]{:S(2)}, u32[]{:S(2)}) collective-permute-start(bf16[64,2048]{1,0:T(8,128)(2,1)S(1)} %add_convert_fusion.1), channel_id=1, source_target_pairs={{0,1},{1,2},{2,3},{3,0},{4,5},{5,6},{6,7},{7,4},{8,9},{9,10},{10,1... | collective-permute-start | bytes 786440 | tf_op jit(solution)/shard_map/ppermute | solution.py:32
  281.3 16.9 %collective-permute-start.29 = (bf16[64,2048]{1,0:T(8,128)(2,1)S(1)}, bf16[64,2048]{1,0:T(8,128)(2,1)}, u32[]{:S(2)}, u32[]{:S(2)}) collective-permute-start(bf16[64,2048]{1,0:T(8,128)(2,1)S(1)} %add_convert_fusion.1), channel_id=1, source_target_pairs={{0,2},{1,3},{2,0},{3,1},{4,6},{5,7},{6,4},{7,5},{8,10},{9,11},{10,... | collective-permute-start | bytes 786440 | tf_op jit(solution)/shard_map/ppermute | solution.py:32
  285.5 12.8 %collective-permute-start.28 = (bf16[64,2048]{1,0:T(8,128)(2,1)S(1)}, bf16[64,2048]{1,0:T(8,128)(2,1)}, u32[]{:S(2)}, u32[]{:S(2)}) collective-permute-start(bf16[64,2048]{1,0:T(8,128)(2,1)S(1)} %add_convert_fusion.1), channel_id=1, source_target_pairs={{0,3},{1,0},{2,1},{3,2},{4,7},{5,4},{6,5},{7,6},{8,11},{9,8},{10,9... | collective-permute-start | bytes 786440 | tf_op jit(solution)/shard_map/ppermute | solution.py:32
  321.4 14.4 %collective-permute-start.36 = (bf16[64,2048]{1,0:T(8,128)(2,1)S(1)}, bf16[64,2048]{1,0:T(8,128)(2,1)S(1)}, u32[]{:S(2)}, u32[]{:S(2)}) collective-permute-start(bf16[64,2048]{1,0:T(8,128)(2,1)S(1)} %get-tuple-element.135), channel_id=1, source_target_pairs={{0,3},{1,0},{2,1},{3,2},{4,7},{5,4},{6,5},{7,6},{8,11},{9,8},{10,9... | collective-permute-start | bytes 786440 | tf_op jit(solution)/shard_map/ppermute | solution.py:32
  324.4 11.5 %collective-permute-start.35 = (bf16[64,2048]{1,0:T(8,128)(2,1)S(1)}, bf16[64,2048]{1,0:T(8,128)(2,1)S(1)}, u32[]{:S(2)}, u32[]{:S(2)}) collective-permute-start(bf16[64,2048]{1,0:T(8,128)(2,1)S(1)} %get-tuple-element.136), channel_id=1, source_target_pairs={{0,2},{1,3},{2,0},{3,1},{4,6},{5,7},{6,4},{7,5},{8,10},{9,11},{10,... | collective-permute-start | bytes 786440 | tf_op jit(solution)/shard_map/ppermute | solution.py:32
  324.7 14.6 %collective-permute-start.34 = (bf16[64,2048]{1,0:T(8,128)(2,1)S(1)}, bf16[64,2048]{1,0:T(8,128)(2,1)S(1)}, u32[]{:S(2)}, u32[]{:S(2)}) collective-permute-start(bf16[64,2048]{1,0:T(8,128)(2,1)S(1)} %get-tuple-element.134), channel_id=1, source_target_pairs={{0,1},{1,2},{2,3},{3,0},{4,5},{5,6},{6,7},{7,4},{8,9},{9,10},{10,1... | collective-permute-start | bytes 786440 | tf_op jit(solution)/shard_map/ppermute | solution.py:32
  355.0 8.5 %collective-permute-start.38 = (bf16[320,256]{1,0:T(8,128)(2,1)S(1)}, bf16[320,256]{1,0:T(8,128)(2,1)S(1)}, u32[]{:S(2)}, u32[]{:S(2)}) collective-permute-start(bf16[320,256]{1,0:T(8,128)(2,1)S(1)} %get-tuple-element.149), channel_id=1, source_target_pairs={{0,2},{1,3},{2,0},{3,1},{4,6},{5,7},{6,4},{7,5},{8,10},{9,11},{10,... | collective-permute-start | bytes 491528 | tf_op jit(solution)/shard_map/ppermute | solution.py:32
  355.3 9.8 %collective-permute-start.37 = (bf16[320,256]{1,0:T(8,128)(2,1)S(1)}, bf16[320,256]{1,0:T(8,128)(2,1)S(1)}, u32[]{:S(2)}, u32[]{:S(2)}) collective-permute-start(bf16[320,256]{1,0:T(8,128)(2,1)S(1)} %get-tuple-element.147), channel_id=1, source_target_pairs={{0,1},{1,2},{2,3},{3,0},{4,5},{5,6},{6,7},{7,4},{8,9},{9,10},{10,1... | collective-permute-start | bytes 491528 | tf_op jit(solution)/shard_map/ppermute | solution.py:32
  376.2 16.0 %collective-permute-start.46 = (bf16[64,2048]{1,0:T(8,128)(2,1)}, bf16[64,2048]{1,0:T(8,128)(2,1)}, u32[]{:S(2)}, u32[]{:S(2)}) collective-permute-start(bf16[64,2048]{1,0:T(8,128)(2,1)} %get-tuple-element.109), channel_id=1, source_target_pairs={{0,1},{1,2},{2,3},{3,0},{4,5},{5,6},{6,7},{7,4},{8,9},{9,10},{10,1... | collective-permute-start | bytes 786440 | tf_op jit(solution)/shard_map/ppermute | solution.py:32
  376.3 15.9 %collective-permute-start.45 = (bf16[64,2048]{1,0:T(8,128)(2,1)}, bf16[64,2048]{1,0:T(8,128)(2,1)}, u32[]{:S(2)}, u32[]{:S(2)}) collective-permute-start(bf16[64,2048]{1,0:T(8,128)(2,1)} %get-tuple-element.109), channel_id=1, source_target_pairs={{0,2},{1,3},{2,0},{3,1},{4,6},{5,7},{6,4},{7,5},{8,10},{9,11},{10,... | collective-permute-start | bytes 786440 | tf_op jit(solution)/shard_map/ppermute | solution.py:32
  378.9 14.5 %collective-permute-start.44 = (bf16[64,2048]{1,0:T(8,128)(2,1)}, bf16[64,2048]{1,0:T(8,128)(2,1)}, u32[]{:S(2)}, u32[]{:S(2)}) collective-permute-start(bf16[64,2048]{1,0:T(8,128)(2,1)} %get-tuple-element.109), channel_id=1, source_target_pairs={{0,3},{1,0},{2,1},{3,2},{4,7},{5,4},{6,5},{7,6},{8,11},{9,8},{10,9... | collective-permute-start | bytes 786440 | tf_op jit(solution)/shard_map/ppermute | solution.py:32
  381.3 170.4 %reduce-scatter.5.cloned.1.call-start = ((), (), s32[]{:S(2)}) async-start(), calls=%async_computation.6 | async-start | bytes 278528 | tf_op jit(solution)/shard_map/reduce_scatter | solution.py:709
  406.0 14.4 %collective-permute-start.49 = (bf16[64,2048]{1,0:T(8,128)(2,1)S(1)}, bf16[64,2048]{1,0:T(8,128)(2,1)S(1)}, u32[]{:S(2)}, u32[]{:S(2)}) collective-permute-start(bf16[64,2048]{1,0:T(8,128)(2,1)S(1)} %get-tuple-element.132), channel_id=1, source_target_pairs={{0,3},{1,0},{2,1},{3,2},{4,7},{5,4},{6,5},{7,6},{8,11},{9,8},{10,9... | collective-permute-start | bytes 786440 | tf_op jit(solution)/shard_map/ppermute | solution.py:32
  408.9 11.5 %collective-permute-start.48 = (bf16[64,2048]{1,0:T(8,128)(2,1)S(1)}, bf16[64,2048]{1,0:T(8,128)(2,1)S(1)}, u32[]{:S(2)}, u32[]{:S(2)}) collective-permute-start(bf16[64,2048]{1,0:T(8,128)(2,1)S(1)} %get-tuple-element.133), channel_id=1, source_target_pairs={{0,2},{1,3},{2,0},{3,1},{4,6},{5,7},{6,4},{7,5},{8,10},{9,11},{10,... | collective-permute-start | bytes 786440 | tf_op jit(solution)/shard_map/ppermute | solution.py:32
  408.9 14.9 %collective-permute-start.47 = (bf16[64,2048]{1,0:T(8,128)(2,1)S(1)}, bf16[64,2048]{1,0:T(8,128)(2,1)S(1)}, u32[]{:S(2)}, u32[]{:S(2)}) collective-permute-start(bf16[64,2048]{1,0:T(8,128)(2,1)S(1)} %get-tuple-element.131), channel_id=1, source_target_pairs={{0,1},{1,2},{2,3},{3,0},{4,5},{5,6},{6,7},{7,4},{8,9},{9,10},{10,1... | collective-permute-start | bytes 786440 | tf_op jit(solution)/shard_map/ppermute | solution.py:32
  424.5 52.0 %collective-permute-start.52 = (bf16[64,2048]{1,0:T(8,128)(2,1)S(1)}, bf16[64,2048]{1,0:T(8,128)(2,1)S(1)}, u32[]{:S(2)}, u32[]{:S(2)}) collective-permute-start(bf16[64,2048]{1,0:T(8,128)(2,1)S(1)} %get-tuple-element.129), channel_id=1, source_target_pairs={{0,3},{1,0},{2,1},{3,2},{4,7},{5,4},{6,5},{7,6},{8,11},{9,8},{10,9... | collective-permute-start | bytes 786440 | tf_op jit(solution)/shard_map/ppermute | solution.py:32
  440.4 8.7 %collective-permute-start.55 = (bf16[320,256]{1,0:T(8,128)(2,1)S(1)}, bf16[320,256]{1,0:T(8,128)(2,1)S(1)}, u32[]{:S(2)}, u32[]{:S(2)}) collective-permute-start(bf16[320,256]{1,0:T(8,128)(2,1)S(1)} %get-tuple-element.146), channel_id=1, source_target_pairs={{0,2},{1,3},{2,0},{3,1},{4,6},{5,7},{6,4},{7,5},{8,10},{9,11},{10,... | collective-permute-start | bytes 491528 | tf_op jit(solution)/shard_map/ppermute | solution.py:32
  458.6 18.2 %collective-permute-start.51 = (bf16[64,2048]{1,0:T(8,128)(2,1)S(1)}, bf16[64,2048]{1,0:T(8,128)(2,1)S(1)}, u32[]{:S(2)}, u32[]{:S(2)}) collective-permute-start(bf16[64,2048]{1,0:T(8,128)(2,1)S(1)} %get-tuple-element.130), channel_id=1, source_target_pairs={{0,2},{1,3},{2,0},{3,1},{4,6},{5,7},{6,4},{7,5},{8,10},{9,11},{10,... | collective-permute-start | bytes 786440 | tf_op jit(solution)/shard_map/ppermute | solution.py:32
  464.9 9.2 %collective-permute-start.62 = (bf16[29,16,128]{2,1,0:T(8,128)(2,1)S(1)}, bf16[29,16,128]{2,1,0:T(8,128)(2,1)S(1)}, u32[]{:S(2)}, u32[]{:S(2)}) collective-permute-start(bf16[29,16,128]{2,1,0:T(8,128)(2,1)S(1)} %get-tuple-element.186), channel_id=1, source_target_pairs={{0,1},{1,2},{2,3},{3,0},{4,5},{5,6},{6,7},{7,4},{8,9},{9,10},{10,1... | collective-permute-start | bytes 356360 | tf_op jit(solution)/shard_map/ppermute | solution.py:32
  467.4 11.1 %collective-permute-start.50 = (bf16[64,2048]{1,0:T(8,128)(2,1)S(1)}, bf16[64,2048]{1,0:T(8,128)(2,1)S(1)}, u32[]{:S(2)}, u32[]{:S(2)}) collective-permute-start(bf16[64,2048]{1,0:T(8,128)(2,1)S(1)} %get-tuple-element.128), channel_id=1, source_target_pairs={{0,1},{1,2},{2,3},{3,0},{4,5},{5,6},{6,7},{7,4},{8,9},{9,10},{10,1... | collective-permute-start | bytes 786440 | tf_op jit(solution)/shard_map/ppermute | solution.py:32
  472.1 83.2 %collective-permute-start.61 = (bf16[64,2048]{1,0:T(8,128)(2,1)S(1)}, bf16[64,2048]{1,0:T(8,128)(2,1)S(1)}, u32[]{:S(2)}, u32[]{:S(2)}) collective-permute-start(bf16[64,2048]{1,0:T(8,128)(2,1)S(1)} %select_convert_fusion), channel_id=1, source_target_pairs={{0,64},{64,0},{1,65},{65,1},{2,66},{66,2},{3,67},{67,3},{4,68},{68... | collective-permute-start | bytes 786440 | tf_op jit(solution)/shard_map/ppermute | solution.py:488
  476.5 8.4 %collective-permute-start.66 = (bf16[4,4,16,128]{3,2,1,0:T(8,128)(2,1)S(1)}, bf16[4,4,16,128]{3,2,1,0:T(8,128)(2,1)S(1)}, u32[]{:S(2)}, u32[]{:S(2)}) collective-permute-start(bf16[4,4,16,128]{3,2,1,0:T(8,128)(2,1)S(1)} %get-tuple-element.217), channel_id=1, source_target_pairs={{0,8},{4,12},{8,0},{12,4},{16,24},{20,28},{24,16},{28,20},{32,40},... | collective-permute-start | bytes 196616 | tf_op jit(solution)/shard_map/ppermute | solution.py:43
  486.7 12.9 %collective-permute-start.70 = (bf16[4,16,128]{2,1,0:T(8,128)(2,1)S(1)}, bf16[4,16,128]{2,1,0:T(8,128)(2,1)S(1)}, u32[]{:S(2)}, u32[]{:S(2)}) collective-permute-start(bf16[4,16,128]{2,1,0:T(8,128)(2,1)S(1)} %get-tuple-element.249), channel_id=1, source_target_pairs={{0,48},{4,52},{8,56},{12,60},{16,32},{20,36},{24,40},{28,44},{32,1... | collective-permute-start | bytes 49160 | tf_op jit(solution)/shard_map/ppermute | solution.py:43
  496.1 71.5 %collective-permute-start.53 = (bf16[64,2048]{1,0:T(8,128)(2,1)S(1)}, bf16[64,2048]{1,0:T(8,128)(2,1)S(1)}, u32[]{:S(2)}, u32[]{:S(2)}) collective-permute-start(bf16[64,2048]{1,0:T(8,128)(2,1)S(1)} %broadcast_select_fusion.6), channel_id=1, source_target_pairs={{0,64},{64,0},{1,65},{65,1},{2,66},{66,2},{3,67},{67,3},{4,68},{68... | collective-permute-start | bytes 786440 | tf_op jit(solution)/shard_map/ppermute | solution.py:488
  568.8 10.9 %collective-permute-start.80 = (bf16[2,21,16,128]{3,2,1,0:T(8,128)(2,1)S(1)}, bf16[2,21,16,128]{3,2,1,0:T(8,128)(2,1)S(1)}, u32[]{:S(2)}, u32[]{:S(2)}) collective-permute-start(bf16[2,21,16,128]{3,2,1,0:T(8,128)(2,1)S(1)} %get-tuple-element.161), channel_id=1, source_target_pairs={{0,3},{1,0},{2,1},{3,2},{4,7},{5,4},{6,5},{7,6},{8,11},{9,8},{10,9... | collective-permute-start | bytes 516104 | tf_op jit(solution)/shard_map/ppermute | solution.py:32
  571.7 8.8 %collective-permute-start.79 = (bf16[2,21,16,128]{3,2,1,0:T(8,128)(2,1)S(1)}, bf16[2,21,16,128]{3,2,1,0:T(8,128)(2,1)S(1)}, u32[]{:S(2)}, u32[]{:S(2)}) collective-permute-start(bf16[2,21,16,128]{3,2,1,0:T(8,128)(2,1)S(1)} %get-tuple-element.161), channel_id=1, source_target_pairs={{0,2},{1,3},{2,0},{3,1},{4,6},{5,7},{6,4},{7,5},{8,10},{9,11},{10,... | collective-permute-start | bytes 516104 | tf_op jit(solution)/shard_map/ppermute | solution.py:32
  572.6 10.9 %collective-permute-start.78 = (bf16[2,21,16,128]{3,2,1,0:T(8,128)(2,1)S(1)}, bf16[2,21,16,128]{3,2,1,0:T(8,128)(2,1)S(1)}, u32[]{:S(2)}, u32[]{:S(2)}) collective-permute-start(bf16[2,21,16,128]{3,2,1,0:T(8,128)(2,1)S(1)} %get-tuple-element.161), channel_id=1, source_target_pairs={{0,1},{1,2},{2,3},{3,0},{4,5},{5,6},{6,7},{7,4},{8,9},{9,10},{10,1... | collective-permute-start | bytes 516104 | tf_op jit(solution)/shard_map/ppermute | solution.py:32
  (177 other events, 2766.6 us)
Sparse Core Ops, SparseCore 0:
  11.6 124.1 all-gather.3
  138.6 71.9 all-gather.5
  213.4 71.9 all-gather.7
  381.4 24.5 reduce-scatter.2
  486.8 64.8 reduce-scatter.4

commit v6 on v5

--- a/solution.py
+++ b/solution.py
@@ -144,7 +144,7 @@
 
 def attend_kernel(
     layer, head, query_ref, keyval_ref, bias_ref, table_ref, so_ref, eo_ref,
-    prob_ref, mixed_ref, low_ref, out_ref, buf, sem,
+    prob_ref, mixed_ref, low_ref, out_ref, buf, sem, prob_buf, prob_sem,
 ):
     ranks, chunks, rows, width = buf.shape
     copies = table_copies(table_ref, buf, sem, layer, width)
@@ -152,12 +152,17 @@
         copy.start()
     scale = 1.0 / math.sqrt(head)
     bias = jnp.concatenate([bias_ref[...].astype(f32)] * 4, axis=0)
-    for g in range(prob_ref.shape[0]):
+    prob_copies = [
+        pltpu.make_async_copy(prob_buf.at[g], prob_ref.at[g], prob_sem.at[g])
+        for g in range(prob_buf.shape[0])
+    ]
+    for g, prob_copy in enumerate(prob_copies):
         queries = side_blocks(query_ref, g, head)
         scores = against(queries, keyval_ref[:, :head]) * scale + bias
         lifted = jnp.exp(scores - jnp.max(scores, axis=-1, keepdims=True))
         probs = lifted * (1.0 / jnp.sum(lifted, axis=-1, keepdims=True))
-        prob_ref[g] = probs
+        prob_buf[g] = probs
+        prob_copy.start()
         put_blocks(mixed_ref, plain(probs.astype(bf16), keyval_ref[:, head:]).astype(bf16), g, head)
     mixed = mixed_ref[...]
     low = against(mixed, so_ref[...]).astype(bf16)
@@ -170,6 +175,8 @@
         for x in range(ranks):
             total = total + against(mixed[:, x * width : (x + 1) * width], buf[x, y])
         out_ref[:, columns] = total
+    for prob_copy in prob_copies:
+        prob_copy.wait()
 
 
 def attend(layer, queries, key_block, bias, table, so, eo, head):
@@ -180,14 +187,15 @@
     return pl.pallas_call(
         lambda *refs: attend_kernel(layer, head, *refs),
         in_specs=[held, held, held, remote, held, held],
-        out_specs=[held] * 4,
+        out_specs=[remote] + [held] * 3,
         out_shape=[
             jax.ShapeDtypeStruct((groups, 4 * rows, keys), f32),
             jax.ShapeDtypeStruct((rows, model), bf16),
             jax.ShapeDtypeStruct((rows, rank), bf16),
             jax.ShapeDtypeStruct((rows, model), f32),
         ],
-        scratch_shapes=table_scratch(table, model // table.shape[0]),
+        scratch_shapes=table_scratch(table, model // table.shape[0])
+        + [pltpu.VMEM((groups, 4 * rows, keys), f32), pltpu.SemaphoreType.DMA((groups,))],
         compiler_params=pltpu.CompilerParams(vmem_limit_bytes=36 * 2**20),
         cost_estimate=pl.CostEstimate(
             flops=4 * rows * model * (keys + 2 * model),
@@ -201,18 +209,25 @@
 def attend_back_kernel(
     layer, head, branch_ref, table_ref, so_ref, eo_ref, prob_ref, query_ref, keyval_ref, eq_ref, sq_ref,
     dq_ref, dkv_ref, inner_o_ref, inner_q_ref, part_ref,
-    out_buf, out_sem, query_buf, query_sem, mixed_buf, key_sum, value_sum,
+    out_buf, out_sem, query_buf, query_sem, prob_buf, prob_sem, mixed_buf, key_sum, value_sum,
 ):
     ranks, chunks, rows, width = out_buf.shape
     out_copies = table_copies(table_ref, out_buf, out_sem, layer, width)
     query_copies = table_copies(table_ref, query_buf, query_sem, layer, 0)
-    for copy in out_copies + query_copies:
+    prob_copies = [
+        pltpu.make_async_copy(prob_ref.at[g], prob_buf.at[g], prob_sem.at[g])
+        for g in range(prob_buf.shape[0])
+    ]
+    for g, prob_copy in enumerate(prob_copies):
+        for copy in out_copies[g * chunks : (g + 1) * chunks] + [prob_copy]:
+            copy.start()
+    for copy in query_copies:
         copy.start()
     scale = 1.0 / math.sqrt(head)
     branch = branch_ref[...]
     inner_o = against(branch, eo_ref[...]).astype(bf16)
     inner_o_ref[...] = inner_o
-    for g in range(prob_ref.shape[0]):
+    for g, prob_copy in enumerate(prob_copies):
         columns = pl.ds(g * width, width)
         total = plain(inner_o, so_ref[:, columns])
         for y in range(chunks):
@@ -220,7 +235,8 @@
             total = total + plain(branch[:, y * rows : (y + 1) * rows], out_buf[g, y])
         mixed_buf[:, columns] = total.astype(bf16)
         grad = side_blocks(mixed_buf, g, head)
-        probs = prob_ref[g]
+        prob_copy.wait()
+        probs = prob_buf[g]
         grad_probs = against(grad, keyval_ref[:, head:])
         delta = jnp.sum(grad_probs * probs, axis=-1, keepdims=True)
         grad_scores = (probs * (grad_probs - delta)).astype(bf16)
@@ -256,7 +272,7 @@
     width = model // table.shape[0]
     return pl.pallas_call(
         lambda *refs: attend_back_kernel(layer, head, *refs),
-        in_specs=[held, remote] + [held] * 7,
+        in_specs=[held, remote, held, held, remote] + [held] * 4,
         out_specs=[held] * 5,
         out_shape=[
             jax.ShapeDtypeStruct((rows, model), bf16),
@@ -268,6 +284,8 @@
         scratch_shapes=table_scratch(table, width)
         + table_scratch(table, width)
         + [
+            pltpu.VMEM((groups, 4 * rows, keys), f32),
+            pltpu.SemaphoreType.DMA((groups,)),
             pltpu.VMEM((rows, model), bf16),
             pltpu.VMEM((keys, head), f32),
             pltpu.VMEM((keys, head), f32),
@@ -701,27 +719,20 @@
     def at(block, index, axis):
         return lax.dynamic_index_in_dim(block, index, axis, keepdims=False)
 
-    def offloaded_grads(shared, quartered, owned):
-        pile = piled(shared, quartered)
-        mine = lax.psum_scatter(
-            pile.reshape((-1,) + pile.shape[2:]), "tensor", scatter_dimension=0, tiled=True
-        )
-        return lax.psum_scatter(owned_pile(mine, owned), "dp", scatter_dimension=0, tiled=True)
-
-    def scattered_grads(shared, quartered, owned):
-        pile = piled(shared, quartered)
+    def scattered_grads(layers):
+        pile = jnp.stack([piled(shared, quartered) for shared, quartered, _ in layers], axis=1)
         mine = at(pile, tensor, 0).astype(f32)
         for j in range(1, ranks):
             mine = mine + around(at(pile, (tensor + j) % ranks, 0), "tensor", j).astype(f32)
-        pile = owned_pile(mine, owned)
-        pile = pile.reshape((chips, 4, -1) + pile.shape[1:])
-        mine = at(pile, near, 1).astype(f32)
+        pile = jnp.stack([owned_pile(mine[i], layers[i][2]) for i in range(2)])
+        pile = pile.reshape((2, chips, 4, -1) + pile.shape[2:])
+        mine = at(pile, near, 2).astype(f32)
         for k in range(1, 4):
-            mine = mine + flipped(at(pile, near ^ k, 1), "dp", k).astype(f32)
+            mine = mine + flipped(at(pile, near ^ k, 2), "dp", k).astype(f32)
         pile = mine.astype(bf16)
-        mine = at(pile, turn, 0).astype(f32)
+        mine = at(pile, turn, 1).astype(f32)
         for k in range(1, chips):
-            mine = mine + flipped(at(pile, turn ^ k, 0), "dp", 4 * k).astype(f32)
+            mine = mine + flipped(at(pile, turn ^ k, 1), "dp", 4 * k).astype(f32)
         return mine.astype(bf16)
 
     def crossed(block, mask):
@@ -836,7 +847,9 @@
     )
     grad_middle = feed_grads(1, given, unit_one, rsd_one, partial_back)
     grad_one, more, quartered = backward_attend(1, kept_one, grad_middle)
-    mine_one = offloaded_grads(shared + more, quartered, owned)
+    layer_one = (shared + more, quartered, owned)
+    partial, _ = lax.optimization_barrier((partial, grad_middle))
+    final = feed_result(1, middle_one, partial).astype(bf16)
 
     su, eu, sd, ed = adapters[0][4:]
     branch_zero = spread(grad_one.astype(bf16))
@@ -852,18 +865,17 @@
         second_zero, branch_zero, low_u_zero, low_d_zero, inner_u, inner_d, active_zero, grad_up
     )
     grad_middle_zero = feed_grads(0, grad_one, unit_zero, rsd_zero, partial_back)
-    partial, _ = lax.optimization_barrier((partial, grad_middle_zero))
-    final = feed_result(1, middle_one, partial).astype(bf16)
     grad_zero, more, quartered = backward_attend(0, kept_zero, grad_middle_zero)
     shared = shared + more
-    mine_zero = scattered_grads(shared, quartered, owned)
-    grads = spread_grads(mine_zero, mine_one, shared, quartered, owned)
+    mine = scattered_grads([(shared, quartered, owned), layer_one])
+    grads = spread_grads(mine[0], mine[1], shared, quartered, owned)
 
     def both_micros(zero, one, kind):
         own = jnp.where(low_section, zero, one)
         received = swap(jnp.where(low_section, one, zero).astype(bf16)).astype(kind)
         return jnp.where(low_section, jnp.stack([own, received]), jnp.stack([received, own]))
 
+    passed, final, _ = lax.optimization_barrier((passed, final, grad_middle_zero))
     section_outputs = both_micros(passed, final, bf16)
     input_grads = both_micros(grad_zero, grad_one, f32)
     onehot = (bank_choice[:, None] == jnp.arange(banks)[None, :]).astype(f32)

time: 606 us -> 558 us (0.921)
  waiting for transfers between devices: 273 us -> 231 us
    reduce_scatter x2 -> x0, waiting for transfers between devices: 51.4 us -> none  [the longest x1 51.3 us: offloaded_grads(): lax.psum_scatter(owned_pile(mine, owned), 'dp', scatter_dimension=0, tile...]
    ppermute x7, waiting for transfers between devices: 12.3 us -> 26.7 us  [swap(): return lax.ppermute(value, 'section', sides)]
    all_gather x1, waiting for transfers between devices: 64.5 us -> 55.2 us  [gather_all(): lax.all_gather(row_major(shard), every, axis=0, tiled=True, axis_index_gr...]
    unnamed x325 -> x330, local copies, waits for them, and re-layouts: 24.1 us -> 24.2 us
  transfers between devices with their start and end apart: 86 -> 84, of which waited for: 50 -> 52; matrix products, arithmetic and copies ran while one was open for 8% -> 10% of each run, Pallas kernels for 11% -> 6%
where the time goes in v6:
time: 558 us; the launch traced here: 548 us
  waiting for transfers between devices  231 us (41%)
  starting transfers between devices  129 us (23%)
  Pallas kernels  86.5 us (16%)
  local copies, waits for them, and re-layouts  44.2 us (8%)
  other arithmetic  27.3 us (5%)
  between operations  21.3 us (4%)
  matrix products  8.77 us (2%)
    ppermute x45, waiting for transfers between devices, around(): lax.ppermute(block, axis, [(i, (i + distance) % size) for i in range(size)])  106 us
    ppermute x45, starting transfers between devices, around(): lax.ppermute(block, axis, [(i, (i + distance) % size) for i in range(size)])  64.4 us
    all_gather x1, waiting for transfers between devices, gather_all(): lax.all_gather(row_major(shard), every, axis=0, tiled=True, axis_index_gr...  55.2 us
    pallas_call x3, Pallas kernels, feed_call(): pl.pallas_call(kernel, in_specs=[remote if value.ndim == 4 else held for...  41.1 us
    ppermute x16, starting transfers between devices, along(): return lax.ppermute(block, axis, route)  32.1 us
    ppermute x7, waiting for transfers between devices, swap(): return lax.ppermute(value, 'section', sides)  26.7 us
    unnamed x330, local copies, waits for them, and re-layouts  24.2 us
    pallas_call x2, Pallas kernels, attend_back(): pl.pallas_call(lambda *refs: attend_back_kernel(layer, head, *refs), in_s...  22.3 us
  transfers between devices with their start and end apart: 84, of which 52 were waited for; matrix products, arithmetic and copies ran while one was open for 10% of the time, Pallas kernels for 6%

profile of v6, /device:TPU:0, one launch (start us, length us, event | category | flops | bytes accessed | tf_op | source)
XLA Modules:
  0.0 547.8 jit_solution(13375476420445581228)
XLA Ops:
  12.3 4.0 collective-permute-start.17
  16.4 12.2 %collective-permute-done.17 = bf16[128,2048]{1,0:T(8,128)(2,1)S(1)} collective-permute-done((bf16[128,2048]{1,0:T(8,128)(2,1)S(1)}, bf16[128,2048]{1,0:T(8,128)(2,1)S(1)}, u32[]{:S(2)}, u32[]{:S(2)}) %collective-permute-start.17) | collective-permute-done | bytes 524320 | tf_op jit(solution)/shard_map/ppermute | solution.py:506
  42.8 4.0 collective-permute-start.13
  48.9 3.6 collective-permute-start
  55.5 14.5 %collective-permute-done = bf16[1,14592]{1,0:T(2,128)(2,1)S(1)} collective-permute-done((bf16[1,14592]{1,0:T(2,128)(2,1)S(1)}, bf16[1,14592]{1,0:T(2,128)(2,1)S(1)}, u32[]{:S(2)}, u32[]{:S(2)}) %collective-permute-start) | collective-permute-done | bytes 29216 | tf_op jit(solution)/shard_map/ppermute | solution.py:506
  83.4 55.2 %all-gather.4.cloned.1.call-done = bf16[16384,1152]{1,0:T(8,128)(2,1)} async-done(((bf16[128,1152]{1,0:T(8,128)(2,1)}), bf16[16384,1152]{1,0:T(8,128)(2,1)}) %all-gather.4.cloned.1.call-update) | async-done | bytes 37748752 | tf_op jit(solution)/shard_map/all_gather | solution.py:544
  141.9 3.4 collective-permute-start.6
  147.6 4.1 collective-permute-start.8
  157.4 4.4 project_queries.2
  164.8 5.4 collective-permute-done.12
  170.3 7.2 %attend.2 = (f32[4,256,1280]{2,1,0:T(8,128)S(1)}, bf16[64,2048]{1,0:T(8,128)(2,1)S(1)}, bf16[64,16]{1,0:T(8,128)(2,1)S(1)}, f32[64,2048]{1,0:T(8,128)S(1)}) custom-call(bf16[64,2048]{1,0:T(8,128)(2,1)S(1)} %get-tuple-element.54.refs_0_.refs_5_, bf16[1280,256]{1,0:T(8,128)(2,1)S(1)} %constant_dynamic-update-slice_fusion.18.refs_1_.refs_6_, ...), custom_call_target="tpu_custom_call" | custom-call | flops 2818572288 | bytes 8388608 | tf_op jit(solution)/shard_map/attend/pallas_call | solution.py:187
  191.5 5.5 %collective-permute-done.16 = bf16[64,2048]{1,0:T(8,128)(2,1)S(1)} collective-permute-done((bf16[64,2048]{1,0:T(8,128)(2,1)S(1)}, bf16[64,2048]{1,0:T(8,128)(2,1)S(1)}, u32[]{:S(2)}, u32[]{:S(2)}) %collective-permute-start.16) | collective-permute-done | bytes 262176 | tf_op jit(solution)/shard_map/ppermute | solution.py:32
  197.1 16.3 %all-gather.6.cloned.1.call-done = bf16[4096,2048]{1,0:T(8,128)(2,1)} async-done(((bf16[128,2048]{1,0:T(8,128)(2,1)}), bf16[4096,2048]{1,0:T(8,128)(2,1)}) %all-gather.6.cloned.1.call-update) | async-done | bytes 16777232 | tf_op jit(solution)/shard_map/all_gather | solution.py:540
  213.4 12.1 %feed.1 = (bf16[256,2048]{1,0:T(8,128)(2,1)S(1)}, bf16[256,2048]{1,0:T(8,128)(2,1)S(1)}, bf16[256,16]{1,0:T(8,128)(2,1)S(1)}, bf16[256,16]{1,0:T(8,128)(2,1)S(1)}, bf16[256,2048]{1,0:T(8,128)(2,1)S(1)}) custom-call(bf16[256,2048]{1,0:T(8,128)(2,1)S(1)} %pad_maximum_fusion.1.second_ref, bf16[4,2,512,2048]{3,2,1,0:T(8,128)(2,1)} %bitcast.736, ...), custom_call_target="tpu_custom_call" | custom-call | flops 4294967296 | bytes 16777216 | tf_op jit(solution)/shard_map/feed/pallas_call | solution.py:439
  232.4 3.1 collective-permute-done.18
  236.4 6.3 %collective-permute-done.19 = bf16[64,2048]{1,0:T(8,128)(2,1)S(1)} collective-permute-done((bf16[64,2048]{1,0:T(8,128)(2,1)S(1)}, bf16[64,2048]{1,0:T(8,128)(2,1)S(1)}, u32[]{:S(2)}, u32[]{:S(2)}) %collective-permute-start.19) | collective-permute-done | bytes 262176 | tf_op jit(solution)/shard_map/ppermute | solution.py:32
  244.4 3.4 collective-permute-start.21
  249.8 3.6 collective-permute-start.23
  259.4 4.4 project_queries.3
  266.4 4.1 collective-permute-done.27
  270.5 7.2 %attend.3 = (f32[4,256,1280]{2,1,0:T(8,128)S(1)}, bf16[64,2048]{1,0:T(8,128)(2,1)S(1)}, bf16[64,16]{1,0:T(8,128)(2,1)S(1)}, f32[64,2048]{1,0:T(8,128)S(1)}) custom-call(bf16[64,2048]{1,0:T(8,128)(2,1)S(1)} %get-tuple-element.57.refs_0_.refs_5_, bf16[1280,256]{1,0:T(8,128)(2,1)S(1)} %constant_dynamic-update-slice_fusion.41.refs_1_.refs_6_, ...), custom_call_target="tpu_custom_call" | custom-call | flops 2818572288 | bytes 8388608 | tf_op jit(solution)/shard_map/attend/pallas_call | solution.py:187
  288.5 3.5 collective-permute-done.29
  292.0 7.2 %collective-permute-done.30 = bf16[64,2048]{1,0:T(8,128)(2,1)} collective-permute-done((bf16[64,2048]{1,0:T(8,128)(2,1)S(1)}, bf16[64,2048]{1,0:T(8,128)(2,1)}, u32[]{:S(2)}, u32[]{:S(2)}) %collective-permute-start.30) | collective-permute-done | bytes 262176 | tf_op jit(solution)/shard_map/ppermute | solution.py:32
  304.6 17.7 %feed_both.1 = (bf16[256,2048]{1,0:T(8,128)(2,1)S(1)}, bf16[256,16]{1,0:T(8,128)(2,1)S(1)}, bf16[256,16]{1,0:T(8,128)(2,1)S(1)}, bf16[256,2048]{1,0:T(8,128)(2,1...) custom-call(bf16[256,2048]{1,0:T(8,128)(2,1)S(1)} %pad_maximum_fusio, ...), custom_call_target="tpu_custom_call" | custom-call | flops 8589934592 | bytes 16777216 | tf_op jit(solution)/shard_map/feed_both/pallas_call | solution.py:439
  330.3 9.6 %collective-permute-done.34 = bf16[64,2048]{1,0:T(8,128)(2,1)S(1)} collective-permute-done((bf16[64,2048]{1,0:T(8,128)(2,1)S(1)}, bf16[64,2048]{1,0:T(8,128)(2,1)S(1)}, u32[]{:S(2)}, u32[]{:S(2)}) %collective-permute-start.34) | collective-permute-done | bytes 262176 | tf_op jit(solution)/shard_map/ppermute | solution.py:32
  343.7 11.2 %attend_back.2 = (bf16[64,2048]{1,0:T(8,128)(2,1)S(1)}, bf16[1280,256]{1,0:T(8,128)(2,1)S(1)}, bf16[64,16]{1,0:T(8,128)(2,1)S(1)}, bf16[64,16]{1,0:T(8,128)(2,1)S(1)}, f32[64,2048]{1,0:T(8,128)S(1)}) custom-call(bf16[64,2048]{1,0:T(8,128)(2,1)S(1)} %get-tuple-element.113.refs_0_, bf16[4,4,2,512,1152]{4,3,2,1,0:T(8,128)(2,1)} %bitcast.734, ...), custom_call_target="tpu_custom_call" | custom-call | flops 5637144576 | bytes 22020096 | tf_op jit(solution)/shard_map/attend_back/pallas_call | solution.py:273
  355.4 3.6 collective-permute-start.41
  361.8 4.7 collective-permute-done.41
  374.8 3.4 collective-permute-start.38
  385.1 3.5 concatenate.208
  393.4 4.1 collective-permute-done.47
  397.5 5.0 collective-permute-done.49
  403.6 11.3 %feed_back.1 = (bf16[256,2048]{1,0:T(8,128)(2,1)S(1)}, bf16[256,16]{1,0:T(8,128)(2,1)S(1)}, bf16[256,16]{1,0:T(8,128)(2,1)S(1)}, bf16[256,2048]{1,0:T(8,128)(2,1)S(1)}) custom-call(bf16[256,2048]{1,0:T(8,128)(2,1)S(1)} %pad_maximum_fusion.5.branch_ref, bf16[4,2,512,2048]{3,2,1,0:T(8,128)(2,1)} %bitcast.737, bf16[256,2048]{1,0:T(8,128)(2,1)S(1)} %copy-done.14, ...), custom_call_target="tpu_custom_call" | custom-call | flops 4294967296 | bytes 16777216 | tf_op jit(solution)/shard_map/feed_back/pallas_call | solution.py:439
  415.9 3.8 collective-permute-start.51
  421.2 3.5 collective-permute-done.50
  424.7 6.8 %collective-permute-done.51 = bf16[64,2048]{1,0:T(8,128)(2,1)S(1)} collective-permute-done((bf16[64,2048]{1,0:T(8,128)(2,1)S(1)}, bf16[64,2048]{1,0:T(8,128)(2,1)S(1)}, u32[]{:S(2)}, u32[]{:S(2)}) %collective-permute-start.51) | collective-permute-done | bytes 262176 | tf_op jit(solution)/shard_map/ppermute | solution.py:32
  432.4 11.2 %attend_back.3 = (bf16[64,2048]{1,0:T(8,128)(2,1)S(1)}, bf16[1280,256]{1,0:T(8,128)(2,1)S(1)}, bf16[64,16]{1,0:T(8,128)(2,1)S(1)}, bf16[64,16]{1,0:T(8,128)(2,1)S(1)}, f32[64,2048]{1,0:T(8,128)S(1)}) custom-call(bf16[64,2048]{1,0:T(8,128)(2,1)S(1)} %get-tuple-element.106.refs_0_, bf16[4,4,2,512,1152]{4,3,2,1,0:T(8,128)(2,1)} %bitcast.735, ...), custom_call_target="tpu_custom_call" | custom-call | flops 5637144576 | bytes 22020096 | tf_op jit(solution)/shard_map/attend_back/pallas_call | solution.py:273
  443.8 3.6 collective-permute-start.55
  450.3 4.7 collective-permute-done.55
  460.8 3.0 collective-permute-done.58
  465.4 4.1 collective-permute-done.60
  470.9 3.6 collective-permute-start.63
  475.2 5.2 collective-permute-done.62
  480.4 4.8 collective-permute-done.63
  488.0 4.2 collective-permute-done.66
  494.2 3.2 collective-permute-start.68
  523.9 3.4 collective-permute-start.79
  530.9 4.5 collective-permute-done.79
  (689 shorter events, 188.1 us)
Async XLA Ops:
  7.2 131.4 %all-gather.4.cloned.1.call-start = ((), (), s32[]{:S(2)}) async-start(), calls=%async_computation | async-start | bytes 38043648 | tf_op jit(solution)/shard_map/all_gather | solution.py:544
  10.8 202.6 %all-gather.6.cloned.1.call-start = ((), (), s32[]{:S(2)}) async-start(), calls=%async_computation.1 | async-start | bytes 17301504 | tf_op jit(solution)/shard_map/all_gather | solution.py:540
  12.3 16.3 %collective-permute-start.17 = (bf16[128,2048]{1,0:T(8,128)(2,1)S(1)}, bf16[128,2048]{1,0:T(8,128)(2,1)S(1)}, u32[]{:S(2)}, u32[]{:S(2)}) collective-permute-start(bf16[128,2048]{1,0:T(8,128)(2,1)S(1)} %broadcast_select_fusion.2), channel_id=1, source_target_pairs={{0,64},{64,0},{1,65},{65,1},{2,66},{66,2},{3,67},{67,3},{4,68},{68... | collective-permute-start | bytes 1572872 | tf_op jit(solution)/shard_map/ppermute | solution.py:506
  30.0 270.5 %all-gather.8.cloned.1.call-start = ((), (), s32[]{:S(2)}) async-start(), calls=%async_computation.2 | async-start | bytes 17301504 | tf_op jit(solution)/shard_map/all_gather | solution.py:540
  42.8 40.5 %collective-permute-start.13 = (bf16[16,10240]{1,0:T(8,128)(2,1)}, bf16[16,10240]{1,0:T(8,128)(2,1)S(1)}, u32[]{:S(2)}, u32[]{:S(2)}) collective-permute-start(bf16[16,10240]{1,0:T(8,128)(2,1)} %get-tuple-element.180), channel_id=1, source_target_pairs={{0,64},{64,0},{1,65},{65,1},{2,66},{66,2},{3,67},{67,3},{4,68},{68... | collective-permute-start | bytes 983048 | tf_op jit(solution)/shard_map/ppermute | solution.py:506
  48.5 28.9 %collective-permute-start.5 = (bf16[16,4352]{1,0:T(8,128)(2,1)S(1)}, bf16[16,4352]{1,0:T(8,128)(2,1)S(1)}, u32[]{:S(2)}, u32[]{:S(2)}) collective-permute-start(bf16[16,4352]{1,0:T(8,128)(2,1)S(1)} %pad_maximum_fusion.18), channel_id=1, source_target_pairs={{0,64},{64,0},{1,65},{65,1},{2,66},{66,2},{3,67},{67,3},{4,68},{68... | collective-permute-start | bytes 417800 | tf_op jit(solution)/shard_map/ppermute | solution.py:506
  48.9 21.1 %collective-permute-start = (bf16[1,14592]{1,0:T(2,128)(2,1)S(1)}, bf16[1,14592]{1,0:T(2,128)(2,1)S(1)}, u32[]{:S(2)}, u32[]{:S(2)}) collective-permute-start(bf16[1,14592]{1,0:T(2,128)(2,1)S(1)} %constant_dynamic-update-slice_fusion), channel_id=1, source_target_pairs={{0,64},{64,0},{1,65},{65,1},{2,66},{66,2},{3,67},{67,3},{4,68},{68... | collective-permute-start | bytes 87560 | tf_op jit(solution)/shard_map/ppermute | solution.py:506
  54.0 17.5 %collective-permute-start.1 = (bf16[16,1536]{1,0:T(8,128)(2,1)S(1)}, bf16[16,1536]{1,0:T(8,128)(2,1)S(1)}, u32[]{:S(2)}, u32[]{:S(2)}) collective-permute-start(bf16[16,1536]{1,0:T(8,128)(2,1)S(1)} %maximum_maximum_fusion.2), channel_id=1, source_target_pairs={{0,64},{64,0},{1,65},{65,1},{2,66},{66,2},{3,67},{67,3},{4,68},{68... | collective-permute-start | bytes 147464 | tf_op jit(solution)/shard_map/ppermute | solution.py:506
  141.9 11.3 %collective-permute-start.6 = (bf16[64,256]{1,0:T(8,128)(2,1)S(1)}, bf16[64,256]{1,0:T(8,128)(2,1)S(1)}, u32[]{:S(2)}, u32[]{:S(2)}) collective-permute-start(bf16[64,256]{1,0:T(8,128)(2,1)S(1)} %fusion.20), channel_id=1, source_target_pairs={{0,16},{4,20},{8,24},{12,28},{16,32},{20,36},{24,40},{28,44},{32,4... | collective-permute-start | bytes 98312 | tf_op jit(solution)/shard_map/ppermute | solution.py:38
  154.0 9.0 %collective-permute-start.10 = (bf16[320,256]{1,0:T(8,128)(2,1)S(1)}, bf16[320,256]{1,0:T(8,128)(2,1)S(1)}, u32[]{:S(2)}, u32[]{:S(2)}) collective-permute-start(bf16[320,256]{1,0:T(8,128)(2,1)S(1)} %get-tuple-element.287), channel_id=1, source_target_pairs={{0,3},{1,0},{2,1},{3,2},{4,7},{5,4},{6,5},{7,6},{8,11},{9,8},{10,9... | collective-permute-start | bytes 491528 | tf_op jit(solution)/shard_map/ppermute | solution.py:32
  156.5 8.3 %collective-permute-start.11 = (bf16[320,256]{1,0:T(8,128)(2,1)S(1)}, bf16[320,256]{1,0:T(8,128)(2,1)S(1)}, u32[]{:S(2)}, u32[]{:S(2)}) collective-permute-start(bf16[320,256]{1,0:T(8,128)(2,1)S(1)} %get-tuple-element.287), channel_id=1, source_target_pairs={{0,2},{1,3},{2,0},{3,1},{4,6},{5,7},{6,4},{7,5},{8,10},{9,11},{10,... | collective-permute-start | bytes 491528 | tf_op jit(solution)/shard_map/ppermute | solution.py:32
  161.8 8.5 %collective-permute-start.12 = (bf16[320,256]{1,0:T(8,128)(2,1)S(1)}, bf16[320,256]{1,0:T(8,128)(2,1)S(1)}, u32[]{:S(2)}, u32[]{:S(2)}) collective-permute-start(bf16[320,256]{1,0:T(8,128)(2,1)S(1)} %get-tuple-element.287), channel_id=1, source_target_pairs={{0,1},{1,2},{2,3},{3,0},{4,5},{5,6},{6,7},{7,4},{8,9},{9,10},{10,1... | collective-permute-start | bytes 491528 | tf_op jit(solution)/shard_map/ppermute | solution.py:32
  180.6 9.2 %collective-permute-start.14 = (bf16[64,2048]{1,0:T(8,128)(2,1)S(1)}, bf16[64,2048]{1,0:T(8,128)(2,1)S(1)}, u32[]{:S(2)}, u32[]{:S(2)}) collective-permute-start(bf16[64,2048]{1,0:T(8,128)(2,1)S(1)} %add_convert_fusion.3), channel_id=1, source_target_pairs={{0,3},{1,0},{2,1},{3,2},{4,7},{5,4},{6,5},{7,6},{8,11},{9,8},{10,9... | collective-permute-start | bytes 786440 | tf_op jit(solution)/shard_map/ppermute | solution.py:32
  180.7 10.8 %collective-permute-start.15 = (bf16[64,2048]{1,0:T(8,128)(2,1)S(1)}, bf16[64,2048]{1,0:T(8,128)(2,1)S(1)}, u32[]{:S(2)}, u32[]{:S(2)}) collective-permute-start(bf16[64,2048]{1,0:T(8,128)(2,1)S(1)} %add_convert_fusion.3), channel_id=1, source_target_pairs={{0,2},{1,3},{2,0},{3,1},{4,6},{5,7},{6,4},{7,5},{8,10},{9,11},{10,... | collective-permute-start | bytes 786440 | tf_op jit(solution)/shard_map/ppermute | solution.py:32
  182.4 14.6 %collective-permute-start.16 = (bf16[64,2048]{1,0:T(8,128)(2,1)S(1)}, bf16[64,2048]{1,0:T(8,128)(2,1)S(1)}, u32[]{:S(2)}, u32[]{:S(2)}) collective-permute-start(bf16[64,2048]{1,0:T(8,128)(2,1)S(1)} %add_convert_fusion.3), channel_id=1, source_target_pairs={{0,1},{1,2},{2,3},{3,0},{4,5},{5,6},{6,7},{7,4},{8,9},{9,10},{10,1... | collective-permute-start | bytes 786440 | tf_op jit(solution)/shard_map/ppermute | solution.py:32
  183.6 100.4 %collective-permute-start.31 = (bf16[64,2048]{1,0:T(8,128)(2,1)S(1)}, bf16[64,2048]{1,0:T(8,128)(2,1)}, u32[]{:S(2)}, u32[]{:S(2)}) collective-permute-start(bf16[64,2048]{1,0:T(8,128)(2,1)S(1)} %dynamic-slice_bitcast_fusion), channel_id=1, source_target_pairs={{0,3},{1,0},{2,1},{3,2},{4,7},{5,4},{6,5},{7,6},{8,11},{9,8},{10,9... | collective-permute-start | bytes 786440 | tf_op jit(solution)/shard_map/ppermute | solution.py:32
  185.7 100.4 %collective-permute-start.32 = (bf16[64,2048]{1,0:T(8,128)(2,1)S(1)}, bf16[64,2048]{1,0:T(8,128)(2,1)}, u32[]{:S(2)}, u32[]{:S(2)}) collective-permute-start(bf16[64,2048]{1,0:T(8,128)(2,1)S(1)} %dynamic-slice_bitcast_fusion), channel_id=1, source_target_pairs={{0,2},{1,3},{2,0},{3,1},{4,6},{5,7},{6,4},{7,5},{8,10},{9,11},{10,... | collective-permute-start | bytes 786440 | tf_op jit(solution)/shard_map/ppermute | solution.py:32
  225.7 9.7 %collective-permute-start.18 = (bf16[64,2048]{1,0:T(8,128)(2,1)S(1)}, bf16[64,2048]{1,0:T(8,128)(2,1)S(1)}, u32[]{:S(2)}, u32[]{:S(2)}) collective-permute-start(bf16[64,2048]{1,0:T(8,128)(2,1)S(1)} %get-tuple-element.137), channel_id=1, source_target_pairs={{0,1},{1,2},{2,3},{3,0},{4,5},{5,6},{6,7},{7,4},{8,9},{9,10},{10,1... | collective-permute-start | bytes 786440 | tf_op jit(solution)/shard_map/ppermute | solution.py:32
  227.2 15.5 %collective-permute-start.19 = (bf16[64,2048]{1,0:T(8,128)(2,1)S(1)}, bf16[64,2048]{1,0:T(8,128)(2,1)S(1)}, u32[]{:S(2)}, u32[]{:S(2)}) collective-permute-start(bf16[64,2048]{1,0:T(8,128)(2,1)S(1)} %get-tuple-element.139), channel_id=1, source_target_pairs={{0,2},{1,3},{2,0},{3,1},{4,6},{5,7},{6,4},{7,5},{8,10},{9,11},{10,... | collective-permute-start | bytes 786440 | tf_op jit(solution)/shard_map/ppermute | solution.py:32
  229.9 12.8 %collective-permute-start.20 = (bf16[64,2048]{1,0:T(8,128)(2,1)S(1)}, bf16[64,2048]{1,0:T(8,128)(2,1)S(1)}, u32[]{:S(2)}, u32[]{:S(2)}) collective-permute-start(bf16[64,2048]{1,0:T(8,128)(2,1)S(1)} %get-tuple-element.138), channel_id=1, source_target_pairs={{0,3},{1,0},{2,1},{3,2},{4,7},{5,4},{6,5},{7,6},{8,11},{9,8},{10,9... | collective-permute-start | bytes 786440 | tf_op jit(solution)/shard_map/ppermute | solution.py:32
  235.4 50.6 %collective-permute-start.33 = (bf16[64,2048]{1,0:T(8,128)(2,1)S(1)}, bf16[64,2048]{1,0:T(8,128)(2,1)}, u32[]{:S(2)}, u32[]{:S(2)}) collective-permute-start(bf16[64,2048]{1,0:T(8,128)(2,1)S(1)} %dynamic-slice_bitcast_fusion), channel_id=1, source_target_pairs={{0,1},{1,2},{2,3},{3,0},{4,5},{5,6},{6,7},{7,4},{8,9},{9,10},{10,1... | collective-permute-start | bytes 786440 | tf_op jit(solution)/shard_map/ppermute | solution.py:32
  282.9 9.1 %collective-permute-start.29 = (bf16[64,2048]{1,0:T(8,128)(2,1)S(1)}, bf16[64,2048]{1,0:T(8,128)(2,1)}, u32[]{:S(2)}, u32[]{:S(2)}) collective-permute-start(bf16[64,2048]{1,0:T(8,128)(2,1)S(1)} %add_convert_fusion.1), channel_id=1, source_target_pairs={{0,2},{1,3},{2,0},{3,1},{4,6},{5,7},{6,4},{7,5},{8,10},{9,11},{10,... | collective-permute-start | bytes 786440 | tf_op jit(solution)/shard_map/ppermute | solution.py:32
  284.0 15.2 %collective-permute-start.30 = (bf16[64,2048]{1,0:T(8,128)(2,1)S(1)}, bf16[64,2048]{1,0:T(8,128)(2,1)}, u32[]{:S(2)}, u32[]{:S(2)}) collective-permute-start(bf16[64,2048]{1,0:T(8,128)(2,1)S(1)} %add_convert_fusion.1), channel_id=1, source_target_pairs={{0,1},{1,2},{2,3},{3,0},{4,5},{5,6},{6,7},{7,4},{8,9},{9,10},{10,1... | collective-permute-start | bytes 786440 | tf_op jit(solution)/shard_map/ppermute | solution.py:32
  324.6 15.2 %collective-permute-start.34 = (bf16[64,2048]{1,0:T(8,128)(2,1)S(1)}, bf16[64,2048]{1,0:T(8,128)(2,1)S(1)}, u32[]{:S(2)}, u32[]{:S(2)}) collective-permute-start(bf16[64,2048]{1,0:T(8,128)(2,1)S(1)} %get-tuple-element.134), channel_id=1, source_target_pairs={{0,1},{1,2},{2,3},{3,0},{4,5},{5,6},{6,7},{7,4},{8,9},{9,10},{10,1... | collective-permute-start | bytes 786440 | tf_op jit(solution)/shard_map/ppermute | solution.py:32
  324.7 15.1 %collective-permute-start.35 = (bf16[64,2048]{1,0:T(8,128)(2,1)S(1)}, bf16[64,2048]{1,0:T(8,128)(2,1)S(1)}, u32[]{:S(2)}, u32[]{:S(2)}) collective-permute-start(bf16[64,2048]{1,0:T(8,128)(2,1)S(1)} %get-tuple-element.136), channel_id=1, source_target_pairs={{0,2},{1,3},{2,0},{3,1},{4,6},{5,7},{6,4},{7,5},{8,10},{9,11},{10,... | collective-permute-start | bytes 786440 | tf_op jit(solution)/shard_map/ppermute | solution.py:32
  325.9 14.6 %collective-permute-start.36 = (bf16[64,2048]{1,0:T(8,128)(2,1)S(1)}, bf16[64,2048]{1,0:T(8,128)(2,1)S(1)}, u32[]{:S(2)}, u32[]{:S(2)}) collective-permute-start(bf16[64,2048]{1,0:T(8,128)(2,1)S(1)} %get-tuple-element.135), channel_id=1, source_target_pairs={{0,3},{1,0},{2,1},{3,2},{4,7},{5,4},{6,5},{7,6},{8,11},{9,8},{10,9... | collective-permute-start | bytes 786440 | tf_op jit(solution)/shard_map/ppermute | solution.py:32
  355.4 11.1 %collective-permute-start.41 = (bf16[320,256]{1,0:T(8,128)(2,1)S(1)}, bf16[320,256]{1,0:T(8,128)(2,1)S(1)}, u32[]{:S(2)}, u32[]{:S(2)}) collective-permute-start(bf16[320,256]{1,0:T(8,128)(2,1)S(1)} %get-tuple-element.152), channel_id=1, source_target_pairs={{0,2},{1,3},{2,0},{3,1},{4,6},{5,7},{6,4},{7,5},{8,10},{9,11},{10,... | collective-permute-start | bytes 491528 | tf_op jit(solution)/shard_map/ppermute | solution.py:32
  366.6 8.2 %collective-permute-start.43 = (bf16[64,256]{1,0:T(8,128)(2,1)S(1)}, bf16[64,256]{1,0:T(8,128)(2,1)S(1)}, u32[]{:S(2)}, u32[]{:S(2)}) collective-permute-start(bf16[64,256]{1,0:T(8,128)(2,1)S(1)} %get-tuple-element.236), channel_id=1, source_target_pairs={{4,0},{8,4},{12,8},{16,12},{20,16},{24,20},{28,24},{32,28},{36,32}... | collective-permute-start | bytes 98312 | tf_op jit(solution)/shard_map/ppermute | solution.py:38
  367.9 10.3 %collective-permute-start.44 = (bf16[64,256]{1,0:T(8,128)(2,1)S(1)}, bf16[64,256]{1,0:T(8,128)(2,1)S(1)}, u32[]{:S(2)}, u32[]{:S(2)}) collective-permute-start(bf16[64,256]{1,0:T(8,128)(2,1)S(1)} %get-tuple-element.239), channel_id=1, source_target_pairs={{8,0},{12,4},{16,8},{20,12},{24,16},{28,20},{32,24},{36,28},{40,32... | collective-permute-start | bytes 98312 | tf_op jit(solution)/shard_map/ppermute | solution.py:38
  369.2 9.2 %collective-permute-start.45 = (bf16[64,256]{1,0:T(8,128)(2,1)S(1)}, bf16[64,256]{1,0:T(8,128)(2,1)S(1)}, u32[]{:S(2)}, u32[]{:S(2)}) collective-permute-start(bf16[64,256]{1,0:T(8,128)(2,1)S(1)} %get-tuple-element.238), channel_id=1, source_target_pairs={{12,0},{16,4},{20,8},{24,12},{28,16},{32,20},{36,24},{40,28},{44,3... | collective-permute-start | bytes 98312 | tf_op jit(solution)/shard_map/ppermute | solution.py:38
  374.6 14.0 %collective-permute-start.37 = (bf16[64,2048]{1,0:T(8,128)(2,1)}, bf16[64,2048]{1,0:T(8,128)(2,1)}, u32[]{:S(2)}, u32[]{:S(2)}) collective-permute-start(bf16[64,2048]{1,0:T(8,128)(2,1)} %get-tuple-element.131), channel_id=1, source_target_pairs={{0,1},{1,2},{2,3},{3,0},{4,5},{5,6},{6,7},{7,4},{8,9},{9,10},{10,1... | collective-permute-start | bytes 786440 | tf_op jit(solution)/shard_map/ppermute | solution.py:32
  374.8 16.4 %collective-permute-start.38 = (bf16[64,2048]{1,0:T(8,128)(2,1)}, bf16[64,2048]{1,0:T(8,128)(2,1)}, u32[]{:S(2)}, u32[]{:S(2)}) collective-permute-start(bf16[64,2048]{1,0:T(8,128)(2,1)} %get-tuple-element.133), channel_id=1, source_target_pairs={{0,2},{1,3},{2,0},{3,1},{4,6},{5,7},{6,4},{7,5},{8,10},{9,11},{10,... | collective-permute-start | bytes 786440 | tf_op jit(solution)/shard_map/ppermute | solution.py:32
  378.2 13.6 %collective-permute-start.39 = (bf16[64,2048]{1,0:T(8,128)(2,1)}, bf16[64,2048]{1,0:T(8,128)(2,1)}, u32[]{:S(2)}, u32[]{:S(2)}) collective-permute-start(bf16[64,2048]{1,0:T(8,128)(2,1)} %get-tuple-element.132), channel_id=1, source_target_pairs={{0,3},{1,0},{2,1},{3,2},{4,7},{5,4},{6,5},{7,6},{8,11},{9,8},{10,9... | collective-permute-start | bytes 786440 | tf_op jit(solution)/shard_map/ppermute | solution.py:32
  380.0 17.5 %collective-permute-start.47 = (bf16[64,2048]{1,0:T(8,128)(2,1)S(1)}, bf16[64,2048]{1,0:T(8,128)(2,1)}, u32[]{:S(2)}, u32[]{:S(2)}) collective-permute-start(bf16[64,2048]{1,0:T(8,128)(2,1)S(1)} %get-tuple-element.109), channel_id=1, source_target_pairs={{0,3},{1,0},{2,1},{3,2},{4,7},{5,4},{6,5},{7,6},{8,11},{9,8},{10,9... | collective-permute-start | bytes 786440 | tf_op jit(solution)/shard_map/ppermute | solution.py:32
  383.0 14.5 %collective-permute-start.48 = (bf16[64,2048]{1,0:T(8,128)(2,1)S(1)}, bf16[64,2048]{1,0:T(8,128)(2,1)}, u32[]{:S(2)}, u32[]{:S(2)}) collective-permute-start(bf16[64,2048]{1,0:T(8,128)(2,1)S(1)} %get-tuple-element.109), channel_id=1, source_target_pairs={{0,2},{1,3},{2,0},{3,1},{4,6},{5,7},{6,4},{7,5},{8,10},{9,11},{10,... | collective-permute-start | bytes 786440 | tf_op jit(solution)/shard_map/ppermute | solution.py:32
  388.6 13.8 %collective-permute-start.49 = (bf16[64,2048]{1,0:T(8,128)(2,1)S(1)}, bf16[64,2048]{1,0:T(8,128)(2,1)S(1)}, u32[]{:S(2)}, u32[]{:S(2)}) collective-permute-start(bf16[64,2048]{1,0:T(8,128)(2,1)S(1)} %get-tuple-element.109), channel_id=1, source_target_pairs={{0,1},{1,2},{2,3},{3,0},{4,5},{5,6},{6,7},{7,4},{8,9},{9,10},{10,1... | collective-permute-start | bytes 786440 | tf_op jit(solution)/shard_map/ppermute | solution.py:32
  415.0 9.7 %collective-permute-start.50 = (bf16[64,2048]{1,0:T(8,128)(2,1)S(1)}, bf16[64,2048]{1,0:T(8,128)(2,1)S(1)}, u32[]{:S(2)}, u32[]{:S(2)}) collective-permute-start(bf16[64,2048]{1,0:T(8,128)(2,1)S(1)} %get-tuple-element.128), channel_id=1, source_target_pairs={{0,1},{1,2},{2,3},{3,0},{4,5},{5,6},{6,7},{7,4},{8,9},{9,10},{10,1... | collective-permute-start | bytes 786440 | tf_op jit(solution)/shard_map/ppermute | solution.py:32
  415.9 15.6 %collective-permute-start.51 = (bf16[64,2048]{1,0:T(8,128)(2,1)S(1)}, bf16[64,2048]{1,0:T(8,128)(2,1)S(1)}, u32[]{:S(2)}, u32[]{:S(2)}) collective-permute-start(bf16[64,2048]{1,0:T(8,128)(2,1)S(1)} %get-tuple-element.130), channel_id=1, source_target_pairs={{0,2},{1,3},{2,0},{3,1},{4,6},{5,7},{6,4},{7,5},{8,10},{9,11},{10,... | collective-permute-start | bytes 786440 | tf_op jit(solution)/shard_map/ppermute | solution.py:32
  419.7 11.8 %collective-permute-start.52 = (bf16[64,2048]{1,0:T(8,128)(2,1)S(1)}, bf16[64,2048]{1,0:T(8,128)(2,1)S(1)}, u32[]{:S(2)}, u32[]{:S(2)}) collective-permute-start(bf16[64,2048]{1,0:T(8,128)(2,1)S(1)} %get-tuple-element.129), channel_id=1, source_target_pairs={{0,3},{1,0},{2,1},{3,2},{4,7},{5,4},{6,5},{7,6},{8,11},{9,8},{10,9... | collective-permute-start | bytes 786440 | tf_op jit(solution)/shard_map/ppermute | solution.py:32
  443.8 11.2 %collective-permute-start.55 = (bf16[320,256]{1,0:T(8,128)(2,1)S(1)}, bf16[320,256]{1,0:T(8,128)(2,1)S(1)}, u32[]{:S(2)}, u32[]{:S(2)}) collective-permute-start(bf16[320,256]{1,0:T(8,128)(2,1)S(1)} %get-tuple-element.149), channel_id=1, source_target_pairs={{0,2},{1,3},{2,0},{3,1},{4,6},{5,7},{6,4},{7,5},{8,10},{9,11},{10,... | collective-permute-start | bytes 491528 | tf_op jit(solution)/shard_map/ppermute | solution.py:32
  447.5 58.1 %collective-permute-start.53 = (bf16[64,2048]{1,0:T(8,128)(2,1)S(1)}, bf16[64,2048]{1,0:T(8,128)(2,1)S(1)}, u32[]{:S(2)}, u32[]{:S(2)}) collective-permute-start(bf16[64,2048]{1,0:T(8,128)(2,1)S(1)} %get-tuple-element.171), channel_id=1, source_target_pairs={{0,64},{64,0},{1,65},{65,1},{2,66},{66,2},{3,67},{67,3},{4,68},{68... | collective-permute-start | bytes 786440 | tf_op jit(solution)/shard_map/ppermute | solution.py:506
  459.2 10.3 %collective-permute-start.60 = (bf16[64,256]{1,0:T(8,128)(2,1)S(1)}, bf16[64,256]{1,0:T(8,128)(2,1)S(1)}, u32[]{:S(2)}, u32[]{:S(2)}) collective-permute-start(bf16[64,256]{1,0:T(8,128)(2,1)S(1)} %get-tuple-element.233), channel_id=1, source_target_pairs={{16,0},{20,4},{24,8},{28,12},{32,16},{36,20},{40,24},{44,28},{48,3... | collective-permute-start | bytes 98312 | tf_op jit(solution)/shard_map/ppermute | solution.py:38
  470.8 9.5 %collective-permute-start.62 = (bf16[2,29,16,128]{3,2,1,0:T(8,128)(2,1)S(1)}, bf16[2,29,16,128]{3,2,1,0:T(8,128)(2,1)S(1)}, u32[]{:S(2)}, u32[]{:S(2)}) collective-permute-start(bf16[2,29,16,128]{3,2,1,0:T(8,128)(2,1)S(1)} %get-tuple-element.140), channel_id=1, source_target_pairs={{0,1},{1,2},{2,3},{3,0},{4,5},{5,6},{6,7},{7,4},{8,9},{9,10},{10,1... | collective-permute-start | bytes 712712 | tf_op jit(solution)/shard_map/ppermute | solution.py:32
  470.9 14.3 %collective-permute-start.63 = (bf16[2,29,16,128]{3,2,1,0:T(8,128)(2,1)S(1)}, bf16[2,29,16,128]{3,2,1,0:T(8,128)(2,1)S(1)}, u32[]{:S(2)}, u32[]{:S(2)}) collective-permute-start(bf16[2,29,16,128]{3,2,1,0:T(8,128)(2,1)S(1)} %get-tuple-element.142), channel_id=1, source_target_pairs={{0,2},{1,3},{2,0},{3,1},{4,6},{5,7},{6,4},{7,5},{8,10},{9,11},{10,... | collective-permute-start | bytes 712712 | tf_op jit(solution)/shard_map/ppermute | solution.py:32
  474.5 10.9 %collective-permute-start.64 = (bf16[2,29,16,128]{3,2,1,0:T(8,128)(2,1)S(1)}, bf16[2,29,16,128]{3,2,1,0:T(8,128)(2,1)S(1)}, u32[]{:S(2)}, u32[]{:S(2)}) collective-permute-start(bf16[2,29,16,128]{3,2,1,0:T(8,128)(2,1)S(1)} %get-tuple-element.141), channel_id=1, source_target_pairs={{0,3},{1,0},{2,1},{3,2},{4,7},{5,4},{6,5},{7,6},{8,11},{9,8},{10,9... | collective-permute-start | bytes 712712 | tf_op jit(solution)/shard_map/ppermute | solution.py:32
  500.4 21.0 %collective-permute-start.61 = (bf16[64,2048]{1,0:T(8,128)(2,1)S(1)}, bf16[64,2048]{1,0:T(8,128)(2,1)S(1)}, u32[]{:S(2)}, u32[]{:S(2)}) collective-permute-start(bf16[64,2048]{1,0:T(8,128)(2,1)S(1)} %select_convert_fusion), channel_id=1, source_target_pairs={{0,64},{64,0},{1,65},{65,1},{2,66},{66,2},{3,67},{67,3},{4,68},{68... | collective-permute-start | bytes 786440 | tf_op jit(solution)/shard_map/ppermute | solution.py:506
  523.9 11.5 %collective-permute-start.79 = (bf16[2,21,16,128]{3,2,1,0:T(8,128)(2,1)S(1)}, bf16[2,21,16,128]{3,2,1,0:T(8,128)(2,1)S(1)}, u32[]{:S(2)}, u32[]{:S(2)}) collective-permute-start(bf16[2,21,16,128]{3,2,1,0:T(8,128)(2,1)S(1)} %get-tuple-element.164), channel_id=1, source_target_pairs={{0,2},{1,3},{2,0},{3,1},{4,6},{5,7},{6,4},{7,5},{8,10},{9,11},{10,... | collective-permute-start | bytes 516104 | tf_op jit(solution)/shard_map/ppermute | solution.py:32
  527.3 8.1 %collective-permute-start.80 = (bf16[2,21,16,128]{3,2,1,0:T(8,128)(2,1)S(1)}, bf16[2,21,16,128]{3,2,1,0:T(8,128)(2,1)S(1)}, u32[]{:S(2)}, u32[]{:S(2)}) collective-permute-start(bf16[2,21,16,128]{3,2,1,0:T(8,128)(2,1)S(1)} %get-tuple-element.164), channel_id=1, source_target_pairs={{0,3},{1,0},{2,1},{3,2},{4,7},{5,4},{6,5},{7,6},{8,11},{9,8},{10,9... | collective-permute-start | bytes 516104 | tf_op jit(solution)/shard_map/ppermute | solution.py:32
  (178 other events, 2743.8 us)
Sparse Core Ops, SparseCore 0:
  11.6 126.9 all-gather.3
  141.4 71.9 all-gather.5
  216.2 72.0 all-gather.7

commit v7 on v6

--- a/solution.py
+++ b/solution.py
@@ -118,7 +118,7 @@
 
 
 held = pl.BlockSpec(memory_space=pltpu.VMEM)
-remote = pl.BlockSpec(memory_space=pl.ANY)
+remote = pl.BlockSpec(memory_space=pltpu.HBM)
 
 
 def project_queries(layer, normed, table, bias, eq, sq):
@@ -160,10 +160,10 @@
         queries = side_blocks(query_ref, g, head)
         scores = against(queries, keyval_ref[:, :head]) * scale + bias
         lifted = jnp.exp(scores - jnp.max(scores, axis=-1, keepdims=True))
-        probs = lifted * (1.0 / jnp.sum(lifted, axis=-1, keepdims=True))
+        probs = (lifted * (1.0 / jnp.sum(lifted, axis=-1, keepdims=True))).astype(bf16)
         prob_buf[g] = probs
         prob_copy.start()
-        put_blocks(mixed_ref, plain(probs.astype(bf16), keyval_ref[:, head:]).astype(bf16), g, head)
+        put_blocks(mixed_ref, plain(probs, keyval_ref[:, head:]).astype(bf16), g, head)
     mixed = mixed_ref[...]
     low = against(mixed, so_ref[...]).astype(bf16)
     low_ref[...] = low
@@ -189,13 +189,13 @@
         in_specs=[held, held, held, remote, held, held],
         out_specs=[remote] + [held] * 3,
         out_shape=[
-            jax.ShapeDtypeStruct((groups, 4 * rows, keys), f32),
+            jax.ShapeDtypeStruct((groups, 4 * rows, keys), bf16),
             jax.ShapeDtypeStruct((rows, model), bf16),
             jax.ShapeDtypeStruct((rows, rank), bf16),
             jax.ShapeDtypeStruct((rows, model), f32),
         ],
         scratch_shapes=table_scratch(table, model // table.shape[0])
-        + [pltpu.VMEM((groups, 4 * rows, keys), f32), pltpu.SemaphoreType.DMA((groups,))],
+        + [pltpu.VMEM((groups, 4 * rows, keys), bf16), pltpu.SemaphoreType.DMA((groups,))],
         compiler_params=pltpu.CompilerParams(vmem_limit_bytes=36 * 2**20),
         cost_estimate=pl.CostEstimate(
             flops=4 * rows * model * (keys + 2 * model),
@@ -236,13 +236,15 @@
         mixed_buf[:, columns] = total.astype(bf16)
         grad = side_blocks(mixed_buf, g, head)
         prob_copy.wait()
-        probs = prob_buf[g]
+        low_probs = prob_buf[g]
+        probs = low_probs.astype(f32)
         grad_probs = against(grad, keyval_ref[:, head:])
         delta = jnp.sum(grad_probs * probs, axis=-1, keepdims=True)
+        delta = delta / jnp.sum(probs, axis=-1, keepdims=True)
         grad_scores = (probs * (grad_probs - delta)).astype(bf16)
         put_blocks(dq_ref, (plain(grad_scores, keyval_ref[:, :head]) * scale).astype(bf16), g, head)
         keys = across(grad_scores, side_blocks(query_ref, g, head))
-        values = across(probs.astype(bf16), grad)
+        values = across(low_probs, grad)
         if g == 0:
             key_sum[...] = keys
             value_sum[...] = values
@@ -284,7 +286,7 @@
         scratch_shapes=table_scratch(table, width)
         + table_scratch(table, width)
         + [
-            pltpu.VMEM((groups, 4 * rows, keys), f32),
+            pltpu.VMEM((groups, 4 * rows, keys), bf16),
             pltpu.SemaphoreType.DMA((groups,)),
             pltpu.VMEM((rows, model), bf16),
             pltpu.VMEM((keys, head), f32),
@@ -322,118 +324,126 @@
     return sum(plain(left[:, i * rows : (i + 1) * rows], buf[k, j, i]) for i in range(buf.shape[2]))
 
 
-def add_against(total, left, buf, k, j):
-    rows = buf.shape[3]
-    for i in range(buf.shape[2]):
-        columns = pl.ds(i * rows, rows)
-        if j == 0:
-            total[:, columns] = against(left, buf[k, j, i])
-        else:
-            total[:, columns] += against(left, buf[k, j, i])
+def against_chunk(left_ref, buf, k, i):
+    tile = buf.shape[4]
+    return sum(
+        against(left_ref[:, j * tile : (j + 1) * tile], buf[k, j, i]) for j in range(buf.shape[1])
+    )
+
+
+def gathered(part_refs, whole):
+    rows = part_refs[0].shape[0]
+    for j, part_ref in enumerate(part_refs):
+        whole[j * rows : (j + 1) * rows] = part_ref[...]
+    return whole[...]
 
 
 def feed_kernel(
-    second_ref, table_ref, bias_ref, eu_ref, sd_ref, su_ref, ed_ref,
-    active_ref, slope_ref, low_u_ref, low_d_ref, out_ref, buf, sems, total,
+    part0, part1, part2, part3, table_ref, bias_ref, eu_ref, sd_ref, su_ref, ed_ref,
+    active_ref, slope_ref, low_u_ref, low_d_ref, out_ref, buf, sems, whole,
 ):
-    _, count, _, _, tile = buf.shape
+    _, count, chunks, rows, tile = buf.shape
     copies = feed_copies(table_ref, buf, sems)
-    for up, down in copies:
+    for up, _ in copies:
         up.start()
+    for _, down in copies:
         down.start()
-    second = second_ref[...]
+    second = gathered((part0, part1, part2, part3), whole)
     low_u = against(second, su_ref[...]).astype(bf16)
     low_u_ref[...] = low_u
-    low = 0.0
     for j in range(count):
         columns = pl.ds(j * tile, tile)
         copies[j][0].wait()
         upward = plain_chunks(second, buf, 0, j)
         upward = upward + plain(low_u, eu_ref[:, columns]) + bias_ref[:, columns]
         active, slope = gelu_parts(upward)
-        active = active.astype(bf16)
-        active_ref[:, columns] = active
+        active_ref[:, columns] = active.astype(bf16)
         slope_ref[:, columns] = slope.astype(bf16)
-        low = low + against(active, sd_ref[:, columns])
-        copies[j][1].wait()
-        add_against(total, active, buf, 1, j)
-    low_d = low.astype(bf16)
+    low_d = against(active_ref[...], sd_ref[...]).astype(bf16)
     low_d_ref[...] = low_d
-    out_ref[...] = (total[...] + plain(low_d, ed_ref[...])).astype(bf16)
+    for _, down in copies:
+        down.wait()
+    for i in range(chunks):
+        columns = pl.ds(i * rows, rows)
+        out_ref[:, columns] = (
+            against_chunk(active_ref, buf, 1, i) + plain(low_d, ed_ref[:, columns])
+        ).astype(bf16)
 
 
 def feed_back_kernel(
-    branch_ref, table_ref, slope_ref, eu_ref, sd_ref, su_ref, ed_ref,
-    grad_up_ref, inner_d_ref, inner_u_ref, out_ref, buf, sems, total,
+    part0, part1, part2, part3, table_ref, slope_ref, eu_ref, sd_ref, su_ref, ed_ref,
+    grad_up_ref, inner_d_ref, inner_u_ref, out_ref, buf, sems, whole,
 ):
-    _, count, _, _, tile = buf.shape
+    _, count, chunks, rows, tile = buf.shape
     copies = feed_copies(table_ref, buf, sems)
-    for up, down in copies:
+    for _, down in copies:
         down.start()
+    for up, _ in copies:
         up.start()
-    branch = branch_ref[...]
+    branch = gathered((part0, part1, part2, part3), whole)
     inner_d = against(branch, ed_ref[...]).astype(bf16)
     inner_d_ref[...] = inner_d
-    inner = 0.0
     for j in range(count):
         columns = pl.ds(j * tile, tile)
         copies[j][1].wait()
         grad = plain_chunks(branch, buf, 1, j) + plain(inner_d, sd_ref[:, columns])
-        grad = (grad * slope_ref[:, columns].astype(f32)).astype(bf16)
-        grad_up_ref[:, columns] = grad
-        inner = inner + against(grad, eu_ref[:, columns])
-        copies[j][0].wait()
-        add_against(total, grad, buf, 0, j)
-    inner_u = inner.astype(bf16)
+        grad_up_ref[:, columns] = (grad * slope_ref[:, columns].astype(f32)).astype(bf16)
+    inner_u = against(grad_up_ref[...], eu_ref[...]).astype(bf16)
     inner_u_ref[...] = inner_u
-    out_ref[...] = (total[...] + plain(inner_u, su_ref[...])).astype(bf16)
+    for up, _ in copies:
+        up.wait()
+    for i in range(chunks):
+        columns = pl.ds(i * rows, rows)
+        out_ref[:, columns] = (
+            against_chunk(grad_up_ref, buf, 0, i) + plain(inner_u, su_ref[:, columns])
+        ).astype(bf16)
 
 
 def feed_both_kernel(
-    second_ref, branch_ref, table_ref, bias_ref, eu_ref, sd_ref, su_ref, ed_ref,
+    part0, part1, part2, part3, branch_ref, table_ref, bias_ref, eu_ref, sd_ref, su_ref, ed_ref,
     active_ref, low_u_ref, low_d_ref, out_ref, grad_up_ref, inner_d_ref, inner_u_ref, back_ref,
-    buf, sems, total, back_total,
+    buf, sems, whole,
 ):
-    _, count, _, _, tile = buf.shape
+    _, count, chunks, rows, tile = buf.shape
     copies = feed_copies(table_ref, buf, sems)
     for up, down in copies:
         up.start()
         down.start()
-    second = second_ref[...]
+    second = gathered((part0, part1, part2, part3), whole)
     branch = branch_ref[...]
     low_u = against(second, su_ref[...]).astype(bf16)
     low_u_ref[...] = low_u
     inner_d = against(branch, ed_ref[...]).astype(bf16)
     inner_d_ref[...] = inner_d
-    low = 0.0
-    inner = 0.0
     for j in range(count):
         columns = pl.ds(j * tile, tile)
         copies[j][0].wait()
         upward = plain_chunks(second, buf, 0, j)
         upward = upward + plain(low_u, eu_ref[:, columns]) + bias_ref[:, columns]
         active, slope = gelu_parts(upward)
-        active = active.astype(bf16)
-        active_ref[:, columns] = active
-        low = low + against(active, sd_ref[:, columns])
+        active_ref[:, columns] = active.astype(bf16)
         copies[j][1].wait()
-        add_against(total, active, buf, 1, j)
         grad = plain_chunks(branch, buf, 1, j) + plain(inner_d, sd_ref[:, columns])
-        grad = (grad * slope).astype(bf16)
-        grad_up_ref[:, columns] = grad
-        inner = inner + against(grad, eu_ref[:, columns])
-        add_against(back_total, grad, buf, 0, j)
-    inner_u = inner.astype(bf16)
+        grad_up_ref[:, columns] = (grad * slope).astype(bf16)
+    inner_u = against(grad_up_ref[...], eu_ref[...]).astype(bf16)
     inner_u_ref[...] = inner_u
-    back_ref[...] = (back_total[...] + plain(inner_u, su_ref[...])).astype(bf16)
-    low_d = low.astype(bf16)
+    low_d = against(active_ref[...], sd_ref[...]).astype(bf16)
     low_d_ref[...] = low_d
-    out_ref[...] = (total[...] + plain(low_d, ed_ref[...])).astype(bf16)
-
-
-def feed_call(kernel, name, inputs, outputs, hidden, totals):
+    for i in range(chunks):
+        columns = pl.ds(i * rows, rows)
+        back_ref[:, columns] = (
+            against_chunk(grad_up_ref, buf, 0, i) + plain(inner_u, su_ref[:, columns])
+        ).astype(bf16)
+        out_ref[:, columns] = (
+            against_chunk(active_ref, buf, 1, i) + plain(low_d, ed_ref[:, columns])
+        ).astype(bf16)
+
+
+def feed_call(kernel, name, parts, inputs, outputs, hidden, matmuls):
+    inputs = tuple(parts) + inputs
     table = [value for value in inputs if value.ndim == 4][0]
-    rows, model = inputs[0].shape
+    model = parts[0].shape[1]
+    rows = sum(part.shape[0] for part in parts)
     tile = 512
     chunks = table.shape[0]
     return pl.pallas_call(
@@ -444,11 +454,11 @@
         scratch_shapes=[
             pltpu.VMEM((2, hidden // tile, chunks, model // chunks, tile), bf16),
             pltpu.SemaphoreType.DMA((2, hidden // tile)),
-        ]
-        + [pltpu.VMEM((rows, model), f32)] * totals,
-        compiler_params=pltpu.CompilerParams(vmem_limit_bytes=44 * 2**20),
+            pltpu.VMEM((rows, model), bf16),
+        ],
+        compiler_params=pltpu.CompilerParams(vmem_limit_bytes=40 * 2**20),
         cost_estimate=pl.CostEstimate(
-            flops=4 * totals * rows * model * hidden,
+            flops=2 * matmuls * rows * model * hidden,
             bytes_accessed=4 * model * hidden,
             transcendentals=rows * hidden,
         ),
@@ -508,9 +518,11 @@
     def by_layer(own, other):
         return jnp.where(low_section, own, other), jnp.where(low_section, other, own)
 
+    def spread_parts(block):
+        return [block] + [around(block, "tensor", -j) for j in range(1, ranks)]
+
     def spread(block):
-        parts = [block] + [around(block, "tensor", -j) for j in range(1, ranks)]
-        return jnp.concatenate(parts, axis=0)
+        return jnp.concatenate(spread_parts(block), axis=0)
 
     def reduce_rows(partial):
         low = partial.astype(bf16)
@@ -685,7 +697,7 @@
     def feed_inputs(layer, middle):
         gain2, shift2, up_bias = small[layer][4:7]
         unit2, rsd2 = norm_parts(middle)
-        second = spread((unit2 * gain2 + shift2).astype(bf16))
+        second = spread_parts((unit2 * gain2 + shift2).astype(bf16))
         return unit2, rsd2, second, up_bias
 
     def feed_result(layer, middle, partial):
@@ -778,7 +790,14 @@
     def feed_grads(layer, grad, unit2, rsd2, partial):
         return grad + norm_back(unit2, rsd2, reduce_rows(partial) * small[layer][4])
 
-    def feed_adapters(second, branch, low_u, low_d, inner_u, inner_d, active, grad_up):
+    def feed_adapters(after, second, branch, *others):
+        parts = (after, *second, branch) if not isinstance(branch, list) else (after, *second, *branch)
+        _, *parts = lax.optimization_barrier(parts + others)
+        second = jnp.concatenate(parts[:ranks], axis=0)
+        parts = parts[ranks:]
+        count = len(parts) - len(others)
+        branch = jnp.concatenate(parts[:count], axis=0)
+        low_u, low_d, inner_u, inner_d, active, grad_up = parts[count:]
         shared = [across(inner_u, second), across(low_d, branch)]
         owned = [across(low_u, grad_up), across(inner_d, active)]
         return shared, owned
@@ -823,10 +842,11 @@
     active_zero, slope_zero, low_u_zero, low_d_zero, partial = feed_call(
         feed_kernel,
         "feed",
-        (second_zero, feed_tables[0], up_bias, eu, sd, su, ed),
+        second_zero,
+        (feed_tables[0], up_bias, eu, sd, su, ed),
         (local_f, local_f, rank, rank, width),
         local_f,
-        1,
+        2,
     )
     passed = feed_result(0, middle_zero, partial).astype(bf16)
 
@@ -837,34 +857,44 @@
     active, low_u, low_d, partial, grad_up, inner_d, inner_u, partial_back = feed_call(
         feed_both_kernel,
         "feed_both",
-        (second_one, branch_one, feed_tables[1], up_bias, eu, sd, su, ed),
+        second_one,
+        (branch_one, feed_tables[1], up_bias, eu, sd, su, ed),
         (local_f, rank, rank, width, local_f, rank, rank, width),
         local_f,
-        2,
-    )
+        4,
+    )
+    grad_middle = feed_grads(1, given, unit_one, rsd_one, partial_back)
     shared, owned = feed_adapters(
-        second_one, branch_one, low_u, low_d, inner_u, inner_d, active, grad_up
-    )
-    grad_middle = feed_grads(1, given, unit_one, rsd_one, partial_back)
+        grad_middle, second_one, branch_one, low_u, low_d, inner_u, inner_d, active, grad_up
+    )
     grad_one, more, quartered = backward_attend(1, kept_one, grad_middle)
     layer_one = (shared + more, quartered, owned)
     partial, _ = lax.optimization_barrier((partial, grad_middle))
     final = feed_result(1, middle_one, partial).astype(bf16)
 
     su, eu, sd, ed = adapters[0][4:]
-    branch_zero = spread(grad_one.astype(bf16))
+    branch_zero = spread_parts(grad_one.astype(bf16))
     grad_up, inner_d, inner_u, partial_back = feed_call(
         feed_back_kernel,
         "feed_back",
-        (branch_zero, feed_tables[0], slope_zero, eu, sd, su, ed),
+        branch_zero,
+        (feed_tables[0], slope_zero, eu, sd, su, ed),
         (local_f, rank, rank, width),
         local_f,
-        1,
-    )
+        2,
+    )
+    grad_middle_zero = feed_grads(0, grad_one, unit_zero, rsd_zero, partial_back)
     shared, owned = feed_adapters(
-        second_zero, branch_zero, low_u_zero, low_d_zero, inner_u, inner_d, active_zero, grad_up
-    )
-    grad_middle_zero = feed_grads(0, grad_one, unit_zero, rsd_zero, partial_back)
+        grad_middle_zero,
+        second_zero,
+        branch_zero,
+        low_u_zero,
+        low_d_zero,
+        inner_u,
+        inner_d,
+        active_zero,
+        grad_up,
+    )
     grad_zero, more, quartered = backward_attend(0, kept_zero, grad_middle_zero)
     shared = shared + more
     mine = scattered_grads([(shared, quartered, owned), layer_one])

time: 558 us -> 565 us (1.013)
  local copies, waits for them, and re-layouts: 44.2 us -> 52.8 us
    ppermute x45, waiting for transfers between devices: 106 us -> 92.8 us  [around(): lax.ppermute(block, axis, [(i, (i + distance) % size) for i in range(size)])]
    all_gather x2, waiting for transfers between devices: 16.3 us -> 26.2 us  [gather(): lax.all_gather(row_major(shard), both, axis=0, tiled=True, axis_index_gro...]
    unnamed x330 -> x348, local copies, waits for them, and re-layouts: 24.2 us -> 26.6 us
  transfers between devices with their start and end apart: 84 -> 84, of which waited for: 52 -> 45; matrix products, arithmetic and copies ran while one was open for 10% -> 11% of each run, Pallas kernels for 6% -> 8%
where the time goes in v7:
time: 565 us; the launch traced here: 555 us
  waiting for transfers between devices  227 us (40%)
  starting transfers between devices  129 us (23%)
  Pallas kernels  84.2 us (15%)
  local copies, waits for them, and re-layouts  52.8 us (9%)
  other arithmetic  31.8 us (6%)
  between operations  21 us (4%)
  matrix products  9.92 us (2%)
    ppermute x45, waiting for transfers between devices, around(): lax.ppermute(block, axis, [(i, (i + distance) % size) for i in range(size)])  92.8 us
    ppermute x45, starting transfers between devices, around(): lax.ppermute(block, axis, [(i, (i + distance) % size) for i in range(size)])  64.1 us
    all_gather x1, waiting for transfers between devices, gather_all(): lax.all_gather(row_major(shard), every, axis=0, tiled=True, axis_index_gr...  54.5 us
    pallas_call x3, Pallas kernels, feed_call(): pl.pallas_call(kernel, in_specs=[remote if value.ndim == 4 else held for...  38.1 us
    ppermute x16, starting transfers between devices, along(): return lax.ppermute(block, axis, route)  32.2 us
    ppermute x7, waiting for transfers between devices, swap(): return lax.ppermute(value, 'section', sides)  26.7 us
    unnamed x348, local copies, waits for them, and re-layouts  26.6 us
    all_gather x2, waiting for transfers between devices, gather(): lax.all_gather(row_major(shard), both, axis=0, tiled=True, axis_index_gro...  26.2 us
  transfers between devices with their start and end apart: 84, of which 45 were waited for; matrix products, arithmetic and copies ran while one was open for 11% of the time, Pallas kernels for 8%

profile of v7, /device:TPU:0, one launch (start us, length us, event | category | flops | bytes accessed | tf_op | source)
XLA Modules:
  0.0 555.3 jit_solution(15886035145105771389)
XLA Ops:
  12.3 4.0 collective-permute-start.17
  16.4 12.2 %collective-permute-done.17 = bf16[128,2048]{1,0:T(8,128)(2,1)S(1)} collective-permute-done((bf16[128,2048]{1,0:T(8,128)(2,1)S(1)}, bf16[128,2048]{1,0:T(8,128)(2,1)S(1)}, u32[]{:S(2)}, u32[]{:S(2)}) %collective-permute-start.17) | collective-permute-done | bytes 524320 | tf_op jit(solution)/shard_map/ppermute | solution.py:516
  42.8 4.0 collective-permute-start.13
  48.9 3.6 collective-permute-start
  55.5 14.5 %collective-permute-done = bf16[1,14592]{1,0:T(2,128)(2,1)S(1)} collective-permute-done((bf16[1,14592]{1,0:T(2,128)(2,1)S(1)}, bf16[1,14592]{1,0:T(2,128)(2,1)S(1)}, u32[]{:S(2)}, u32[]{:S(2)}) %collective-permute-start) | collective-permute-done | bytes 29216 | tf_op jit(solution)/shard_map/ppermute | solution.py:516
  73.3 2.7 collective-permute-start.3
  84.0 54.5 %all-gather.4.cloned.1.call-done = bf16[16384,1152]{1,0:T(8,128)(2,1)} async-done(((bf16[128,1152]{1,0:T(8,128)(2,1)}), bf16[16384,1152]{1,0:T(8,128)(2,1)}) %all-gather.4.cloned.1.call-update) | async-done | bytes 37748752 | tf_op jit(solution)/shard_map/all_gather | solution.py:556
  138.6 2.7 fusion.165
  141.8 3.4 collective-permute-start.6
  147.5 4.1 collective-permute-start.8
  157.4 4.4 project_queries.2
  164.8 5.7 %collective-permute-done.12 = bf16[320,256]{1,0:T(8,128)(2,1)S(1)} collective-permute-done((bf16[320,256]{1,0:T(8,128)(2,1)S(1)}, bf16[320,256]{1,0:T(8,128)(2,1)S(1)}, u32[]{:S(2)}, u32[]{:S(2)}) %collective-permute-start.12) | collective-permute-done | bytes 163872 | tf_op jit(solution)/shard_map/ppermute | solution.py:32
  170.5 7.4 %attend.2 = (bf16[4,256,1280]{2,1,0:T(8,128)(2,1)S(1)}, bf16[64,2048]{1,0:T(8,128)(2,1)S(1)}, bf16[64,16]{1,0:T(8,128)(2,1)S(1)}, f32[64,2048]{1,0:T(8,128)S(1)}) custom-call(bf16[64,2048]{1,0:T(8,128)(2,1)S(1)} %get-tuple-element.79.refs_0_.refs_5_, bf16[1280,256]{1,0:T(8,128)(2,1)S(1)} %constant_dynamic-update-slice_fusion.18.refs_1_.refs_6_, ...), custom_call_target="tpu_custom_call" | custom-call | flops 2818572288 | bytes 8388608 | tf_op jit(solution)/shard_map/attend/pallas_call | solution.py:187
  187.3 26.2 %all-gather.6.cloned.1.call-done = bf16[4096,2048]{1,0:T(8,128)(2,1)} async-done(((bf16[128,2048]{1,0:T(8,128)(2,1)}), bf16[4096,2048]{1,0:T(8,128)(2,1)}) %all-gather.6.cloned.1.call-update) | async-done | bytes 16777232 | tf_op jit(solution)/shard_map/all_gather | solution.py:552
  215.2 10.8 %feed.1 = (bf16[256,2048]{1,0:T(8,128)(2,1)S(1)}, bf16[256,2048]{1,0:T(8,128)(2,1)S(1)}, bf16[256,16]{1,0:T(8,128)(2,1)S(1)}, bf16[256,16]{1,0:T(8,128)(2,1)S(1)}, bf16[256,2048]{1,0:T(8,128)(2,1)S(1)}) custom-call(bf16[64,2048]{1,0:T(8,128)(2,1)S(1)} %add_convert_fusion.3.part0, bf16[64,2048]{1,0:T(8,128)(2,1)S(1)} %collective-permute-done.14.part1, ...), custom_call_target="tpu_custom_call" | custom-call | flops 4294967296 | bytes 16777216 | tf_op jit(solution)/shard_map/feed/pallas_call | solution.py:449
  227.8 2.7 collective-permute-start.19
  232.9 3.1 collective-permute-done.18
  236.9 6.3 %collective-permute-done.19 = bf16[64,2048]{1,0:T(8,128)(2,1)S(1)} collective-permute-done((bf16[64,2048]{1,0:T(8,128)(2,1)S(1)}, bf16[64,2048]{1,0:T(8,128)(2,1)S(1)}, u32[]{:S(2)}, u32[]{:S(2)}) %collective-permute-start.19) | collective-permute-done | bytes 262176 | tf_op jit(solution)/shard_map/ppermute | solution.py:32
  244.8 3.4 collective-permute-start.21
  250.2 3.6 collective-permute-start.23
  259.6 4.4 project_queries.3
  266.6 4.4 collective-permute-done.27
  271.1 7.4 %attend.3 = (bf16[4,256,1280]{2,1,0:T(8,128)(2,1)S(1)}, bf16[64,2048]{1,0:T(8,128)(2,1)S(1)}, bf16[64,16]{1,0:T(8,128)(2,1)S(1)}, f32[64,2048]{1,0:T(8,128)S(1)}) custom-call(bf16[64,2048]{1,0:T(8,128)(2,1)S(1)} %get-tuple-element.82.refs_0_.refs_5_, bf16[1280,256]{1,0:T(8,128)(2,1)S(1)} %constant_dynamic-update-slice_fusion.41.refs_1_.refs_6_, ...), custom_call_target="tpu_custom_call" | custom-call | flops 2818572288 | bytes 8388608 | tf_op jit(solution)/shard_map/attend/pallas_call | solution.py:187
  290.9 4.0 collective-permute-done.29.part2
  294.9 7.1 %collective-permute-done.30.part3 = bf16[64,2048]{1,0:T(8,128)(2,1)} collective-permute-done((bf16[64,2048]{1,0:T(8,128)(2,1)}, bf16[64,2048]{1,0:T(8,128)(2,1)}, u32[]{:S(2)}, u32[]{:S(2)}) %collective-permute-start.30) | collective-permute-done | bytes 262176 | tf_op jit(solution)/shard_map/ppermute | solution.py:32
  306.1 16.3 %feed_both.1 = (bf16[256,2048]{1,0:T(8,128)(2,1)S(1)}, bf16[256,16]{1,0:T(8,128)(2,1)S(1)}, bf16[256,16]{1,0:T(8,128)(2,1)S(1)}, bf16[256,2048]{1,0:T(8,128)(2,1...) custom-call(bf16[64,2048]{1,0:T(8,128)(2,1)} %add_convert_fusion.1.p, ...), custom_call_target="tpu_custom_call" | custom-call | flops 8589934592 | bytes 16777216 | tf_op jit(solution)/shard_map/feed_both/pallas_call | solution.py:449
  335.2 10.1 %collective-permute-done.34 = bf16[64,2048]{1,0:T(8,128)(2,1)} collective-permute-done((bf16[64,2048]{1,0:T(8,128)(2,1)}, bf16[64,2048]{1,0:T(8,128)(2,1)}, u32[]{:S(2)}, u32[]{:S(2)}) %collective-permute-start.34) | collective-permute-done | bytes 262176 | tf_op jit(solution)/shard_map/ppermute | solution.py:32
  349.1 11.2 %attend_back.2 = (bf16[64,2048]{1,0:T(8,128)(2,1)S(1)}, bf16[1280,256]{1,0:T(8,128)(2,1)S(1)}, bf16[64,16]{1,0:T(8,128)(2,1)S(1)}, bf16[64,16]{1,0:T(8,128)(2,1)S(1)}, f32[64,2048]{1,0:T(8,128)S(1)}) custom-call(bf16[64,2048]{1,0:T(8,128)(2,1)S(1)} %get-tuple-element.163.refs_0_, bf16[4,4,2,512,1152]{4,3,2,1,0:T(8,128)(2,1)} %bitcast.729, ...), custom_call_target="tpu_custom_call" | custom-call | flops 5637144576 | bytes 22020096 | tf_op jit(solution)/shard_map/attend_back/pallas_call | solution.py:275
  360.8 3.7 collective-permute-start.41
  368.4 3.6 collective-permute-done.41
  382.2 3.6 collective-permute-start.38
  391.1 5.5 concatenate.208
  399.3 2.6 collective-permute-start.39
  404.4 5.7 %collective-permute-done.49.part3 = bf16[64,2048]{1,0:T(8,128)(2,1)} collective-permute-done((bf16[64,2048]{1,0:T(8,128)(2,1)S(1)}, bf16[64,2048]{1,0:T(8,128)(2,1)}, u32[]{:S(2)}, u32[]{:S(2)}) %collective-permute-start.49) | collective-permute-done | bytes 262176 | tf_op jit(solution)/shard_map/ppermute | solution.py:32
  410.1 11.0 %feed_back.1 = (bf16[256,2048]{1,0:T(8,128)(2,1)S(1)}, bf16[256,16]{1,0:T(8,128)(2,1)S(1)}, bf16[256,16]{1,0:T(8,128)(2,1)S(1)}, bf16[256,2048]{1,0:T(8,128)(2,1)S(1)}) custom-call(bf16[64,2048]{1,0:T(8,128)(2,1)S(1)} %get-tuple-element.109.part0, bf16[64,2048]{1,0:T(8,128)(2,1)S(1)} %collective-permute-done.47.part1, ...), custom_call_target="tpu_custom_call" | custom-call | flops 4294967296 | bytes 16777216 | tf_op jit(solution)/shard_map/feed_back/pallas_call | solution.py:449
  426.4 9.9 %collective-permute-done.50 = bf16[64,2048]{1,0:T(8,128)(2,1)S(1)} collective-permute-done((bf16[64,2048]{1,0:T(8,128)(2,1)S(1)}, bf16[64,2048]{1,0:T(8,128)(2,1)S(1)}, u32[]{:S(2)}, u32[]{:S(2)}) %collective-permute-start.50) | collective-permute-done | bytes 262176 | tf_op jit(solution)/shard_map/ppermute | solution.py:32
  439.4 11.2 %attend_back.3 = (bf16[64,2048]{1,0:T(8,128)(2,1)S(1)}, bf16[1280,256]{1,0:T(8,128)(2,1)S(1)}, bf16[64,16]{1,0:T(8,128)(2,1)S(1)}, bf16[64,16]{1,0:T(8,128)(2,1)S(1)}, f32[64,2048]{1,0:T(8,128)S(1)}) custom-call(bf16[64,2048]{1,0:T(8,128)(2,1)S(1)} %get-tuple-element.156.refs_0_, bf16[4,4,2,512,1152]{4,3,2,1,0:T(8,128)(2,1)} %bitcast.730, ...), custom_call_target="tpu_custom_call" | custom-call | flops 5637144576 | bytes 22020096 | tf_op jit(solution)/shard_map/attend_back/pallas_call | solution.py:275
  451.0 3.9 collective-permute-start.55
  459.4 3.1 collective-permute-done.55
  468.3 3.2 collective-permute-done.58
  473.1 4.1 collective-permute-done.60
  478.7 3.6 collective-permute-start.63
  482.8 5.3 collective-permute-done.62
  488.1 4.8 collective-permute-done.63
  495.7 4.2 collective-permute-done.66
  501.9 3.2 collective-permute-start.68
  531.2 3.9 collective-permute-start.79
  538.6 4.5 collective-permute-done.79
  (703 shorter events, 189.4 us)
Async XLA Ops:
  7.2 131.4 %all-gather.4.cloned.1.call-start = ((), (), s32[]{:S(2)}) async-start(), calls=%async_computation | async-start | bytes 38043648 | tf_op jit(solution)/shard_map/all_gather | solution.py:556
  10.8 202.7 %all-gather.6.cloned.1.call-start = ((), (), s32[]{:S(2)}) async-start(), calls=%async_computation.1 | async-start | bytes 17301504 | tf_op jit(solution)/shard_map/all_gather | solution.py:552
  12.3 16.3 %collective-permute-start.17 = (bf16[128,2048]{1,0:T(8,128)(2,1)S(1)}, bf16[128,2048]{1,0:T(8,128)(2,1)S(1)}, u32[]{:S(2)}, u32[]{:S(2)}) collective-permute-start(bf16[128,2048]{1,0:T(8,128)(2,1)S(1)} %broadcast_select_fusion.2), channel_id=1, source_target_pairs={{0,64},{64,0},{1,65},{65,1},{2,66},{66,2},{3,67},{67,3},{4,68},{68... | collective-permute-start | bytes 1572872 | tf_op jit(solution)/shard_map/ppermute | solution.py:516
  30.0 258.9 %all-gather.8.cloned.1.call-start = ((), (), s32[]{:S(2)}) async-start(), calls=%async_computation.2 | async-start | bytes 17301504 | tf_op jit(solution)/shard_map/all_gather | solution.py:552
  42.8 40.5 %collective-permute-start.13 = (bf16[16,10240]{1,0:T(8,128)(2,1)}, bf16[16,10240]{1,0:T(8,128)(2,1)S(1)}, u32[]{:S(2)}, u32[]{:S(2)}) collective-permute-start(bf16[16,10240]{1,0:T(8,128)(2,1)} %get-tuple-element.230), channel_id=1, source_target_pairs={{0,64},{64,0},{1,65},{65,1},{2,66},{66,2},{3,67},{67,3},{4,68},{68... | collective-permute-start | bytes 983048 | tf_op jit(solution)/shard_map/ppermute | solution.py:516
  48.5 28.9 %collective-permute-start.5 = (bf16[16,4352]{1,0:T(8,128)(2,1)S(1)}, bf16[16,4352]{1,0:T(8,128)(2,1)S(1)}, u32[]{:S(2)}, u32[]{:S(2)}) collective-permute-start(bf16[16,4352]{1,0:T(8,128)(2,1)S(1)} %pad_maximum_fusion.15), channel_id=1, source_target_pairs={{0,64},{64,0},{1,65},{65,1},{2,66},{66,2},{3,67},{67,3},{4,68},{68... | collective-permute-start | bytes 417800 | tf_op jit(solution)/shard_map/ppermute | solution.py:516
  48.9 21.1 %collective-permute-start = (bf16[1,14592]{1,0:T(2,128)(2,1)S(1)}, bf16[1,14592]{1,0:T(2,128)(2,1)S(1)}, u32[]{:S(2)}, u32[]{:S(2)}) collective-permute-start(bf16[1,14592]{1,0:T(2,128)(2,1)S(1)} %constant_dynamic-update-slice_fusion), channel_id=1, source_target_pairs={{0,64},{64,0},{1,65},{65,1},{2,66},{66,2},{3,67},{67,3},{4,68},{68... | collective-permute-start | bytes 87560 | tf_op jit(solution)/shard_map/ppermute | solution.py:516
  54.0 17.5 %collective-permute-start.1 = (bf16[16,1536]{1,0:T(8,128)(2,1)S(1)}, bf16[16,1536]{1,0:T(8,128)(2,1)S(1)}, u32[]{:S(2)}, u32[]{:S(2)}) collective-permute-start(bf16[16,1536]{1,0:T(8,128)(2,1)S(1)} %maximum_maximum_fusion.2), channel_id=1, source_target_pairs={{0,64},{64,0},{1,65},{65,1},{2,66},{66,2},{3,67},{67,3},{4,68},{68... | collective-permute-start | bytes 147464 | tf_op jit(solution)/shard_map/ppermute | solution.py:516
  141.8 11.3 %collective-permute-start.6 = (bf16[64,256]{1,0:T(8,128)(2,1)S(1)}, bf16[64,256]{1,0:T(8,128)(2,1)S(1)}, u32[]{:S(2)}, u32[]{:S(2)}) collective-permute-start(bf16[64,256]{1,0:T(8,128)(2,1)S(1)} %fusion.20), channel_id=1, source_target_pairs={{0,16},{4,20},{8,24},{12,28},{16,32},{20,36},{24,40},{28,44},{32,4... | collective-permute-start | bytes 98312 | tf_op jit(solution)/shard_map/ppermute | solution.py:38
  153.9 9.2 %collective-permute-start.10 = (bf16[320,256]{1,0:T(8,128)(2,1)S(1)}, bf16[320,256]{1,0:T(8,128)(2,1)S(1)}, u32[]{:S(2)}, u32[]{:S(2)}) collective-permute-start(bf16[320,256]{1,0:T(8,128)(2,1)S(1)} %get-tuple-element.337), channel_id=1, source_target_pairs={{0,3},{1,0},{2,1},{3,2},{4,7},{5,4},{6,5},{7,6},{8,11},{9,8},{10,9... | collective-permute-start | bytes 491528 | tf_op jit(solution)/shard_map/ppermute | solution.py:32
  161.8 8.7 %collective-permute-start.12 = (bf16[320,256]{1,0:T(8,128)(2,1)S(1)}, bf16[320,256]{1,0:T(8,128)(2,1)S(1)}, u32[]{:S(2)}, u32[]{:S(2)}) collective-permute-start(bf16[320,256]{1,0:T(8,128)(2,1)S(1)} %get-tuple-element.337), channel_id=1, source_target_pairs={{0,1},{1,2},{2,3},{3,0},{4,5},{5,6},{6,7},{7,4},{8,9},{9,10},{10,1... | collective-permute-start | bytes 491528 | tf_op jit(solution)/shard_map/ppermute | solution.py:32
  180.2 33.3 %collective-permute-start.14 = (bf16[64,2048]{1,0:T(8,128)(2,1)S(1)}, bf16[64,2048]{1,0:T(8,128)(2,1)S(1)}, u32[]{:S(2)}, u32[]{:S(2)}) collective-permute-start(bf16[64,2048]{1,0:T(8,128)(2,1)S(1)} %add_convert_fusion.3.part0), channel_id=1, source_target_pairs={{0,3},{1,0},{2,1},{3,2},{4,7},{5,4},{6,5},{7,6},{8,11},{9,8},{10,9... | collective-permute-start | bytes 786440 | tf_op jit(solution)/shard_map/ppermute | solution.py:32
  180.4 33.1 %collective-permute-start.15 = (bf16[64,2048]{1,0:T(8,128)(2,1)S(1)}, bf16[64,2048]{1,0:T(8,128)(2,1)S(1)}, u32[]{:S(2)}, u32[]{:S(2)}) collective-permute-start(bf16[64,2048]{1,0:T(8,128)(2,1)S(1)} %add_convert_fusion.3.part0), channel_id=1, source_target_pairs={{0,2},{1,3},{2,0},{3,1},{4,6},{5,7},{6,4},{7,5},{8,10},{9,11},{10,... | collective-permute-start | bytes 786440 | tf_op jit(solution)/shard_map/ppermute | solution.py:32
  182.0 31.5 %collective-permute-start.16 = (bf16[64,2048]{1,0:T(8,128)(2,1)S(1)}, bf16[64,2048]{1,0:T(8,128)(2,1)S(1)}, u32[]{:S(2)}, u32[]{:S(2)}) collective-permute-start(bf16[64,2048]{1,0:T(8,128)(2,1)S(1)} %add_convert_fusion.3.part0), channel_id=1, source_target_pairs={{0,1},{1,2},{2,3},{3,0},{4,5},{5,6},{6,7},{7,4},{8,9},{9,10},{10,1... | collective-permute-start | bytes 786440 | tf_op jit(solution)/shard_map/ppermute | solution.py:32
  183.9 102.4 %collective-permute-start.31 = (bf16[64,2048]{1,0:T(8,128)(2,1)}, bf16[64,2048]{1,0:T(8,128)(2,1)}, u32[]{:S(2)}, u32[]{:S(2)}) collective-permute-start(bf16[64,2048]{1,0:T(8,128)(2,1)} %dynamic-slice_bitcast_fusion), channel_id=1, source_target_pairs={{0,3},{1,0},{2,1},{3,2},{4,7},{5,4},{6,5},{7,6},{8,11},{9,8},{10,9... | collective-permute-start | bytes 786440 | tf_op jit(solution)/shard_map/ppermute | solution.py:32
  185.9 101.7 %collective-permute-start.32 = (bf16[64,2048]{1,0:T(8,128)(2,1)}, bf16[64,2048]{1,0:T(8,128)(2,1)}, u32[]{:S(2)}, u32[]{:S(2)}) collective-permute-start(bf16[64,2048]{1,0:T(8,128)(2,1)} %dynamic-slice_bitcast_fusion), channel_id=1, source_target_pairs={{0,2},{1,3},{2,0},{3,1},{4,6},{5,7},{6,4},{7,5},{8,10},{9,11},{10,... | collective-permute-start | bytes 786440 | tf_op jit(solution)/shard_map/ppermute | solution.py:32
  226.2 9.7 %collective-permute-start.18 = (bf16[64,2048]{1,0:T(8,128)(2,1)S(1)}, bf16[64,2048]{1,0:T(8,128)(2,1)S(1)}, u32[]{:S(2)}, u32[]{:S(2)}) collective-permute-start(bf16[64,2048]{1,0:T(8,128)(2,1)S(1)} %get-tuple-element.187), channel_id=1, source_target_pairs={{0,1},{1,2},{2,3},{3,0},{4,5},{5,6},{6,7},{7,4},{8,9},{9,10},{10,1... | collective-permute-start | bytes 786440 | tf_op jit(solution)/shard_map/ppermute | solution.py:32
  227.8 15.5 %collective-permute-start.19 = (bf16[64,2048]{1,0:T(8,128)(2,1)S(1)}, bf16[64,2048]{1,0:T(8,128)(2,1)S(1)}, u32[]{:S(2)}, u32[]{:S(2)}) collective-permute-start(bf16[64,2048]{1,0:T(8,128)(2,1)S(1)} %get-tuple-element.189), channel_id=1, source_target_pairs={{0,2},{1,3},{2,0},{3,1},{4,6},{5,7},{6,4},{7,5},{8,10},{9,11},{10,... | collective-permute-start | bytes 786440 | tf_op jit(solution)/shard_map/ppermute | solution.py:32
  230.4 12.8 %collective-permute-start.20 = (bf16[64,2048]{1,0:T(8,128)(2,1)S(1)}, bf16[64,2048]{1,0:T(8,128)(2,1)S(1)}, u32[]{:S(2)}, u32[]{:S(2)}) collective-permute-start(bf16[64,2048]{1,0:T(8,128)(2,1)S(1)} %get-tuple-element.188), channel_id=1, source_target_pairs={{0,3},{1,0},{2,1},{3,2},{4,7},{5,4},{6,5},{7,6},{8,11},{9,8},{10,9... | collective-permute-start | bytes 786440 | tf_op jit(solution)/shard_map/ppermute | solution.py:32
  236.0 51.7 %collective-permute-start.33 = (bf16[64,2048]{1,0:T(8,128)(2,1)}, bf16[64,2048]{1,0:T(8,128)(2,1)S(1)}, u32[]{:S(2)}, u32[]{:S(2)}) collective-permute-start(bf16[64,2048]{1,0:T(8,128)(2,1)} %dynamic-slice_bitcast_fusion), channel_id=1, source_target_pairs={{0,1},{1,2},{2,3},{3,0},{4,5},{5,6},{6,7},{7,4},{8,9},{9,10},{10,1... | collective-permute-start | bytes 786440 | tf_op jit(solution)/shard_map/ppermute | solution.py:32
  285.5 9.4 %collective-permute-start.29 = (bf16[64,2048]{1,0:T(8,128)(2,1)}, bf16[64,2048]{1,0:T(8,128)(2,1)}, u32[]{:S(2)}, u32[]{:S(2)}) collective-permute-start(bf16[64,2048]{1,0:T(8,128)(2,1)} %add_convert_fusion.1.part0), channel_id=1, source_target_pairs={{0,2},{1,3},{2,0},{3,1},{4,6},{5,7},{6,4},{7,5},{8,10},{9,11},{10,... | collective-permute-start | bytes 786440 | tf_op jit(solution)/shard_map/ppermute | solution.py:32
  286.2 15.8 %collective-permute-start.30 = (bf16[64,2048]{1,0:T(8,128)(2,1)}, bf16[64,2048]{1,0:T(8,128)(2,1)}, u32[]{:S(2)}, u32[]{:S(2)}) collective-permute-start(bf16[64,2048]{1,0:T(8,128)(2,1)} %add_convert_fusion.1.part0), channel_id=1, source_target_pairs={{0,1},{1,2},{2,3},{3,0},{4,5},{5,6},{6,7},{7,4},{8,9},{9,10},{10,1... | collective-permute-start | bytes 786440 | tf_op jit(solution)/shard_map/ppermute | solution.py:32
  329.8 15.5 %collective-permute-start.34 = (bf16[64,2048]{1,0:T(8,128)(2,1)}, bf16[64,2048]{1,0:T(8,128)(2,1)}, u32[]{:S(2)}, u32[]{:S(2)}) collective-permute-start(bf16[64,2048]{1,0:T(8,128)(2,1)} %get-tuple-element.184), channel_id=1, source_target_pairs={{0,1},{1,2},{2,3},{3,0},{4,5},{5,6},{6,7},{7,4},{8,9},{9,10},{10,1... | collective-permute-start | bytes 786440 | tf_op jit(solution)/shard_map/ppermute | solution.py:32
  329.8 15.5 %collective-permute-start.35 = (bf16[64,2048]{1,0:T(8,128)(2,1)}, bf16[64,2048]{1,0:T(8,128)(2,1)}, u32[]{:S(2)}, u32[]{:S(2)}) collective-permute-start(bf16[64,2048]{1,0:T(8,128)(2,1)} %get-tuple-element.186), channel_id=1, source_target_pairs={{0,2},{1,3},{2,0},{3,1},{4,6},{5,7},{6,4},{7,5},{8,10},{9,11},{10,... | collective-permute-start | bytes 786440 | tf_op jit(solution)/shard_map/ppermute | solution.py:32
  330.8 15.1 %collective-permute-start.36 = (bf16[64,2048]{1,0:T(8,128)(2,1)}, bf16[64,2048]{1,0:T(8,128)(2,1)}, u32[]{:S(2)}, u32[]{:S(2)}) collective-permute-start(bf16[64,2048]{1,0:T(8,128)(2,1)} %get-tuple-element.185), channel_id=1, source_target_pairs={{0,3},{1,0},{2,1},{3,2},{4,7},{5,4},{6,5},{7,6},{8,11},{9,8},{10,9... | collective-permute-start | bytes 786440 | tf_op jit(solution)/shard_map/ppermute | solution.py:32
  360.8 11.2 %collective-permute-start.41 = (bf16[320,256]{1,0:T(8,128)(2,1)S(1)}, bf16[320,256]{1,0:T(8,128)(2,1)S(1)}, u32[]{:S(2)}, u32[]{:S(2)}) collective-permute-start(bf16[320,256]{1,0:T(8,128)(2,1)S(1)} %get-tuple-element.202), channel_id=1, source_target_pairs={{0,2},{1,3},{2,0},{3,1},{4,6},{5,7},{6,4},{7,5},{8,10},{9,11},{10,... | collective-permute-start | bytes 491528 | tf_op jit(solution)/shard_map/ppermute | solution.py:32
  372.1 10.1 %collective-permute-start.43 = (bf16[64,256]{1,0:T(8,128)(2,1)S(1)}, bf16[64,256]{1,0:T(8,128)(2,1)S(1)}, u32[]{:S(2)}, u32[]{:S(2)}) collective-permute-start(bf16[64,256]{1,0:T(8,128)(2,1)S(1)} %get-tuple-element.286), channel_id=1, source_target_pairs={{4,0},{8,4},{12,8},{16,12},{20,16},{24,20},{28,24},{32,28},{36,32}... | collective-permute-start | bytes 98312 | tf_op jit(solution)/shard_map/ppermute | solution.py:38
  373.5 12.2 %collective-permute-start.44 = (bf16[64,256]{1,0:T(8,128)(2,1)S(1)}, bf16[64,256]{1,0:T(8,128)(2,1)S(1)}, u32[]{:S(2)}, u32[]{:S(2)}) collective-permute-start(bf16[64,256]{1,0:T(8,128)(2,1)S(1)} %get-tuple-element.289), channel_id=1, source_target_pairs={{8,0},{12,4},{16,8},{20,12},{24,16},{28,20},{32,24},{36,28},{40,32... | collective-permute-start | bytes 98312 | tf_op jit(solution)/shard_map/ppermute | solution.py:38
  374.8 10.9 %collective-permute-start.45 = (bf16[64,256]{1,0:T(8,128)(2,1)S(1)}, bf16[64,256]{1,0:T(8,128)(2,1)S(1)}, u32[]{:S(2)}, u32[]{:S(2)}) collective-permute-start(bf16[64,256]{1,0:T(8,128)(2,1)S(1)} %get-tuple-element.288), channel_id=1, source_target_pairs={{12,0},{16,4},{20,8},{24,12},{28,16},{32,20},{36,24},{40,28},{44,3... | collective-permute-start | bytes 98312 | tf_op jit(solution)/shard_map/ppermute | solution.py:38
  376.1 9.7 %collective-permute-start.46 = (bf16[64,256]{1,0:T(8,128)(2,1)S(1)}, bf16[64,256]{1,0:T(8,128)(2,1)S(1)}, u32[]{:S(2)}, u32[]{:S(2)}) collective-permute-start(bf16[64,256]{1,0:T(8,128)(2,1)S(1)} %get-tuple-element.287), channel_id=1, source_target_pairs={{16,0},{20,4},{24,8},{28,12},{32,16},{36,20},{40,24},{44,28},{48,3... | collective-permute-start | bytes 98312 | tf_op jit(solution)/shard_map/ppermute | solution.py:38
  382.2 41.1 %collective-permute-start.37 = (bf16[64,2048]{1,0:T(8,128)(2,1)}, bf16[64,2048]{1,0:T(8,128)(2,1)}, u32[]{:S(2)}, u32[]{:S(2)}) collective-permute-start(bf16[64,2048]{1,0:T(8,128)(2,1)} %get-tuple-element.181), channel_id=1, source_target_pairs={{0,1},{1,2},{2,3},{3,0},{4,5},{5,6},{6,7},{7,4},{8,9},{9,10},{10,1... | collective-permute-start | bytes 786440 | tf_op jit(solution)/shard_map/ppermute | solution.py:32
  382.2 42.7 %collective-permute-start.38 = (bf16[64,2048]{1,0:T(8,128)(2,1)}, bf16[64,2048]{1,0:T(8,128)(2,1)}, u32[]{:S(2)}, u32[]{:S(2)}) collective-permute-start(bf16[64,2048]{1,0:T(8,128)(2,1)} %get-tuple-element.183), channel_id=1, source_target_pairs={{0,2},{1,3},{2,0},{3,1},{4,6},{5,7},{6,4},{7,5},{8,10},{9,11},{10,... | collective-permute-start | bytes 786440 | tf_op jit(solution)/shard_map/ppermute | solution.py:32
  388.0 11.3 %collective-permute-start.47 = (bf16[64,2048]{1,0:T(8,128)(2,1)S(1)}, bf16[64,2048]{1,0:T(8,128)(2,1)S(1)}, u32[]{:S(2)}, u32[]{:S(2)}) collective-permute-start(bf16[64,2048]{1,0:T(8,128)(2,1)S(1)} %get-tuple-element.109.part0), channel_id=1, source_target_pairs={{0,3},{1,0},{2,1},{3,2},{4,7},{5,4},{6,5},{7,6},{8,11},{9,8},{10,9... | collective-permute-start | bytes 786440 | tf_op jit(solution)/shard_map/ppermute | solution.py:32
  389.3 15.2 %collective-permute-start.48 = (bf16[64,2048]{1,0:T(8,128)(2,1)S(1)}, bf16[64,2048]{1,0:T(8,128)(2,1)}, u32[]{:S(2)}, u32[]{:S(2)}) collective-permute-start(bf16[64,2048]{1,0:T(8,128)(2,1)S(1)} %get-tuple-element.109.part0), channel_id=1, source_target_pairs={{0,2},{1,3},{2,0},{3,1},{4,6},{5,7},{6,4},{7,5},{8,10},{9,11},{10,... | collective-permute-start | bytes 786440 | tf_op jit(solution)/shard_map/ppermute | solution.py:32
  390.7 19.4 %collective-permute-start.49 = (bf16[64,2048]{1,0:T(8,128)(2,1)S(1)}, bf16[64,2048]{1,0:T(8,128)(2,1)}, u32[]{:S(2)}, u32[]{:S(2)}) collective-permute-start(bf16[64,2048]{1,0:T(8,128)(2,1)S(1)} %get-tuple-element.109.part0), channel_id=1, source_target_pairs={{0,1},{1,2},{2,3},{3,0},{4,5},{5,6},{6,7},{7,4},{8,9},{9,10},{10,1... | collective-permute-start | bytes 786440 | tf_op jit(solution)/shard_map/ppermute | solution.py:32
  399.3 25.7 %collective-permute-start.39 = (bf16[64,2048]{1,0:T(8,128)(2,1)}, bf16[64,2048]{1,0:T(8,128)(2,1)S(1)}, u32[]{:S(2)}, u32[]{:S(2)}) collective-permute-start(bf16[64,2048]{1,0:T(8,128)(2,1)} %get-tuple-element.182), channel_id=1, source_target_pairs={{0,3},{1,0},{2,1},{3,2},{4,7},{5,4},{6,5},{7,6},{8,11},{9,8},{10,9... | collective-permute-start | bytes 786440 | tf_op jit(solution)/shard_map/ppermute | solution.py:32
  421.2 15.1 %collective-permute-start.50 = (bf16[64,2048]{1,0:T(8,128)(2,1)S(1)}, bf16[64,2048]{1,0:T(8,128)(2,1)S(1)}, u32[]{:S(2)}, u32[]{:S(2)}) collective-permute-start(bf16[64,2048]{1,0:T(8,128)(2,1)S(1)} %get-tuple-element.178), channel_id=1, source_target_pairs={{0,1},{1,2},{2,3},{3,0},{4,5},{5,6},{6,7},{7,4},{8,9},{9,10},{10,1... | collective-permute-start | bytes 786440 | tf_op jit(solution)/shard_map/ppermute | solution.py:32
  421.3 15.1 %collective-permute-start.51 = (bf16[64,2048]{1,0:T(8,128)(2,1)S(1)}, bf16[64,2048]{1,0:T(8,128)(2,1)S(1)}, u32[]{:S(2)}, u32[]{:S(2)}) collective-permute-start(bf16[64,2048]{1,0:T(8,128)(2,1)S(1)} %get-tuple-element.180), channel_id=1, source_target_pairs={{0,2},{1,3},{2,0},{3,1},{4,6},{5,7},{6,4},{7,5},{8,10},{9,11},{10,... | collective-permute-start | bytes 786440 | tf_op jit(solution)/shard_map/ppermute | solution.py:32
  423.2 13.8 %collective-permute-start.52 = (bf16[64,2048]{1,0:T(8,128)(2,1)S(1)}, bf16[64,2048]{1,0:T(8,128)(2,1)S(1)}, u32[]{:S(2)}, u32[]{:S(2)}) collective-permute-start(bf16[64,2048]{1,0:T(8,128)(2,1)S(1)} %get-tuple-element.179), channel_id=1, source_target_pairs={{0,3},{1,0},{2,1},{3,2},{4,7},{5,4},{6,5},{7,6},{8,11},{9,8},{10,9... | collective-permute-start | bytes 786440 | tf_op jit(solution)/shard_map/ppermute | solution.py:32
  450.7 8.7 %collective-permute-start.54 = (bf16[320,256]{1,0:T(8,128)(2,1)S(1)}, bf16[320,256]{1,0:T(8,128)(2,1)S(1)}, u32[]{:S(2)}, u32[]{:S(2)}) collective-permute-start(bf16[320,256]{1,0:T(8,128)(2,1)S(1)} %get-tuple-element.197), channel_id=1, source_target_pairs={{0,1},{1,2},{2,3},{3,0},{4,5},{5,6},{6,7},{7,4},{8,9},{9,10},{10,1... | collective-permute-start | bytes 491528 | tf_op jit(solution)/shard_map/ppermute | solution.py:32
  451.0 11.5 %collective-permute-start.55 = (bf16[320,256]{1,0:T(8,128)(2,1)S(1)}, bf16[320,256]{1,0:T(8,128)(2,1)S(1)}, u32[]{:S(2)}, u32[]{:S(2)}) collective-permute-start(bf16[320,256]{1,0:T(8,128)(2,1)S(1)} %get-tuple-element.199), channel_id=1, source_target_pairs={{0,2},{1,3},{2,0},{3,1},{4,6},{5,7},{6,4},{7,5},{8,10},{9,11},{10,... | collective-permute-start | bytes 491528 | tf_op jit(solution)/shard_map/ppermute | solution.py:32
  455.0 58.4 %collective-permute-start.53 = (bf16[64,2048]{1,0:T(8,128)(2,1)S(1)}, bf16[64,2048]{1,0:T(8,128)(2,1)S(1)}, u32[]{:S(2)}, u32[]{:S(2)}) collective-permute-start(bf16[64,2048]{1,0:T(8,128)(2,1)S(1)} %get-tuple-element.221), channel_id=1, source_target_pairs={{0,64},{64,0},{1,65},{65,1},{2,66},{66,2},{3,67},{67,3},{4,68},{68... | collective-permute-start | bytes 786440 | tf_op jit(solution)/shard_map/ppermute | solution.py:516
  466.6 10.6 %collective-permute-start.60 = (bf16[64,256]{1,0:T(8,128)(2,1)S(1)}, bf16[64,256]{1,0:T(8,128)(2,1)S(1)}, u32[]{:S(2)}, u32[]{:S(2)}) collective-permute-start(bf16[64,256]{1,0:T(8,128)(2,1)S(1)} %get-tuple-element.283), channel_id=1, source_target_pairs={{16,0},{20,4},{24,8},{28,12},{32,16},{36,20},{40,24},{44,28},{48,3... | collective-permute-start | bytes 98312 | tf_op jit(solution)/shard_map/ppermute | solution.py:38
  478.6 9.5 %collective-permute-start.62 = (bf16[2,29,16,128]{3,2,1,0:T(8,128)(2,1)S(1)}, bf16[2,29,16,128]{3,2,1,0:T(8,128)(2,1)S(1)}, u32[]{:S(2)}, u32[]{:S(2)}) collective-permute-start(bf16[2,29,16,128]{3,2,1,0:T(8,128)(2,1)S(1)} %get-tuple-element.190), channel_id=1, source_target_pairs={{0,1},{1,2},{2,3},{3,0},{4,5},{5,6},{6,7},{7,4},{8,9},{9,10},{10,1... | collective-permute-start | bytes 712712 | tf_op jit(solution)/shard_map/ppermute | solution.py:32
  478.7 14.3 %collective-permute-start.63 = (bf16[2,29,16,128]{3,2,1,0:T(8,128)(2,1)S(1)}, bf16[2,29,16,128]{3,2,1,0:T(8,128)(2,1)S(1)}, u32[]{:S(2)}, u32[]{:S(2)}) collective-permute-start(bf16[2,29,16,128]{3,2,1,0:T(8,128)(2,1)S(1)} %get-tuple-element.192), channel_id=1, source_target_pairs={{0,2},{1,3},{2,0},{3,1},{4,6},{5,7},{6,4},{7,5},{8,10},{9,11},{10,... | collective-permute-start | bytes 712712 | tf_op jit(solution)/shard_map/ppermute | solution.py:32
  482.3 10.9 %collective-permute-start.64 = (bf16[2,29,16,128]{3,2,1,0:T(8,128)(2,1)S(1)}, bf16[2,29,16,128]{3,2,1,0:T(8,128)(2,1)S(1)}, u32[]{:S(2)}, u32[]{:S(2)}) collective-permute-start(bf16[2,29,16,128]{3,2,1,0:T(8,128)(2,1)S(1)} %get-tuple-element.191), channel_id=1, source_target_pairs={{0,3},{1,0},{2,1},{3,2},{4,7},{5,4},{6,5},{7,6},{8,11},{9,8},{10,9... | collective-permute-start | bytes 712712 | tf_op jit(solution)/shard_map/ppermute | solution.py:32
  508.1 21.0 %collective-permute-start.61 = (bf16[64,2048]{1,0:T(8,128)(2,1)S(1)}, bf16[64,2048]{1,0:T(8,128)(2,1)S(1)}, u32[]{:S(2)}, u32[]{:S(2)}) collective-permute-start(bf16[64,2048]{1,0:T(8,128)(2,1)S(1)} %select_convert_fusion), channel_id=1, source_target_pairs={{0,64},{64,0},{1,65},{65,1},{2,66},{66,2},{3,67},{67,3},{4,68},{68... | collective-permute-start | bytes 786440 | tf_op jit(solution)/shard_map/ppermute | solution.py:516
  531.2 11.9 %collective-permute-start.79 = (bf16[2,21,16,128]{3,2,1,0:T(8,128)(2,1)S(1)}, bf16[2,21,16,128]{3,2,1,0:T(8,128)(2,1)S(1)}, u32[]{:S(2)}, u32[]{:S(2)}) collective-permute-start(bf16[2,21,16,128]{3,2,1,0:T(8,128)(2,1)S(1)} %get-tuple-element.214), channel_id=1, source_target_pairs={{0,2},{1,3},{2,0},{3,1},{4,6},{5,7},{6,4},{7,5},{8,10},{9,11},{10,... | collective-permute-start | bytes 516104 | tf_op jit(solution)/shard_map/ppermute | solution.py:32
  (187 other events, 2799.5 us)
Sparse Core Ops, SparseCore 0:
  11.6 126.9 all-gather.3
  141.4 71.9 all-gather.5
  216.3 71.9 all-gather.7

commit v8 on v7

--- a/solution.py
+++ b/solution.py
@@ -134,7 +134,7 @@
             jax.ShapeDtypeStruct((rows, rank), bf16),
         ],
         scratch_shapes=table_scratch(table, width),
-        compiler_params=pltpu.CompilerParams(vmem_limit_bytes=20 * 2**20),
+        compiler_params=pltpu.CompilerParams(vmem_limit_bytes=12 * 2**20),
         cost_estimate=pl.CostEstimate(
             flops=8 * rows * model * model, bytes_accessed=2 * model * model, transcendentals=0
         ),
@@ -144,7 +144,7 @@
 
 def attend_kernel(
     layer, head, query_ref, keyval_ref, bias_ref, table_ref, so_ref, eo_ref,
-    prob_ref, mixed_ref, low_ref, out_ref, buf, sem, prob_buf, prob_sem,
+    prob_ref, mixed_ref, low_ref, out_ref, buf, sem,
 ):
     ranks, chunks, rows, width = buf.shape
     copies = table_copies(table_ref, buf, sem, layer, width)
@@ -152,17 +152,12 @@
         copy.start()
     scale = 1.0 / math.sqrt(head)
     bias = jnp.concatenate([bias_ref[...].astype(f32)] * 4, axis=0)
-    prob_copies = [
-        pltpu.make_async_copy(prob_buf.at[g], prob_ref.at[g], prob_sem.at[g])
-        for g in range(prob_buf.shape[0])
-    ]
-    for g, prob_copy in enumerate(prob_copies):
+    for g in range(prob_ref.shape[0]):
         queries = side_blocks(query_ref, g, head)
         scores = against(queries, keyval_ref[:, :head]) * scale + bias
         lifted = jnp.exp(scores - jnp.max(scores, axis=-1, keepdims=True))
         probs = (lifted * (1.0 / jnp.sum(lifted, axis=-1, keepdims=True))).astype(bf16)
-        prob_buf[g] = probs
-        prob_copy.start()
+        prob_ref[g] = probs
         put_blocks(mixed_ref, plain(probs, keyval_ref[:, head:]).astype(bf16), g, head)
     mixed = mixed_ref[...]
     low = against(mixed, so_ref[...]).astype(bf16)
@@ -175,8 +170,6 @@
         for x in range(ranks):
             total = total + against(mixed[:, x * width : (x + 1) * width], buf[x, y])
         out_ref[:, columns] = total
-    for prob_copy in prob_copies:
-        prob_copy.wait()
 
 
 def attend(layer, queries, key_block, bias, table, so, eo, head):
@@ -187,16 +180,15 @@
     return pl.pallas_call(
         lambda *refs: attend_kernel(layer, head, *refs),
         in_specs=[held, held, held, remote, held, held],
-        out_specs=[remote] + [held] * 3,
+        out_specs=[held] * 4,
         out_shape=[
             jax.ShapeDtypeStruct((groups, 4 * rows, keys), bf16),
             jax.ShapeDtypeStruct((rows, model), bf16),
             jax.ShapeDtypeStruct((rows, rank), bf16),
             jax.ShapeDtypeStruct((rows, model), f32),
         ],
-        scratch_shapes=table_scratch(table, model // table.shape[0])
-        + [pltpu.VMEM((groups, 4 * rows, keys), bf16), pltpu.SemaphoreType.DMA((groups,))],
-        compiler_params=pltpu.CompilerParams(vmem_limit_bytes=36 * 2**20),
+        scratch_shapes=table_scratch(table, model // table.shape[0]),
+        compiler_params=pltpu.CompilerParams(vmem_limit_bytes=20 * 2**20),
         cost_estimate=pl.CostEstimate(
             flops=4 * rows * model * (keys + 2 * model),
             bytes_accessed=2 * model * model,
@@ -209,25 +201,18 @@
 def attend_back_kernel(
     layer, head, branch_ref, table_ref, so_ref, eo_ref, prob_ref, query_ref, keyval_ref, eq_ref, sq_ref,
     dq_ref, dkv_ref, inner_o_ref, inner_q_ref, part_ref,
-    out_buf, out_sem, query_buf, query_sem, prob_buf, prob_sem, mixed_buf, key_sum, value_sum,
+    out_buf, out_sem, query_buf, query_sem, mixed_buf, key_sum, value_sum,
 ):
     ranks, chunks, rows, width = out_buf.shape
     out_copies = table_copies(table_ref, out_buf, out_sem, layer, width)
     query_copies = table_copies(table_ref, query_buf, query_sem, layer, 0)
-    prob_copies = [
-        pltpu.make_async_copy(prob_ref.at[g], prob_buf.at[g], prob_sem.at[g])
-        for g in range(prob_buf.shape[0])
-    ]
-    for g, prob_copy in enumerate(prob_copies):
-        for copy in out_copies[g * chunks : (g + 1) * chunks] + [prob_copy]:
-            copy.start()
-    for copy in query_copies:
+    for copy in out_copies + query_copies:
         copy.start()
     scale = 1.0 / math.sqrt(head)
     branch = branch_ref[...]
     inner_o = against(branch, eo_ref[...]).astype(bf16)
     inner_o_ref[...] = inner_o
-    for g, prob_copy in enumerate(prob_copies):
+    for g in range(prob_ref.shape[0]):
         columns = pl.ds(g * width, width)
         total = plain(inner_o, so_ref[:, columns])
         for y in range(chunks):
@@ -235,8 +220,7 @@
             total = total + plain(branch[:, y * rows : (y + 1) * rows], out_buf[g, y])
         mixed_buf[:, columns] = total.astype(bf16)
         grad = side_blocks(mixed_buf, g, head)
-        prob_copy.wait()
-        low_probs = prob_buf[g]
+        low_probs = prob_ref[g]
         probs = low_probs.astype(f32)
         grad_probs = against(grad, keyval_ref[:, head:])
         delta = jnp.sum(grad_probs * probs, axis=-1, keepdims=True)
@@ -274,7 +258,7 @@
     width = model // table.shape[0]
     return pl.pallas_call(
         lambda *refs: attend_back_kernel(layer, head, *refs),
-        in_specs=[held, remote, held, held, remote] + [held] * 4,
+        in_specs=[held, remote] + [held] * 7,
         out_specs=[held] * 5,
         out_shape=[
             jax.ShapeDtypeStruct((rows, model), bf16),
@@ -286,13 +270,11 @@
         scratch_shapes=table_scratch(table, width)
         + table_scratch(table, width)
         + [
-            pltpu.VMEM((groups, 4 * rows, keys), bf16),
-            pltpu.SemaphoreType.DMA((groups,)),
             pltpu.VMEM((rows, model), bf16),
             pltpu.VMEM((keys, head), f32),
             pltpu.VMEM((keys, head), f32),
         ],
-        compiler_params=pltpu.CompilerParams(vmem_limit_bytes=44 * 2**20),
+        compiler_params=pltpu.CompilerParams(vmem_limit_bytes=30 * 2**20),
         cost_estimate=pl.CostEstimate(
             flops=8 * rows * model * (keys + 2 * model),
             bytes_accessed=4 * model * model + 4 * groups * 4 * rows * keys,
@@ -338,11 +320,17 @@
     return whole[...]
 
 
+def feed_pack(pack_ref, model, hidden):
+    cuts = [model, 2 * model, 2 * model + hidden, 2 * model + 2 * hidden, 3 * model + 2 * hidden]
+    return [pack_ref.at[:, a:b] for a, b in zip(cuts[:-1], cuts[1:])]
+
+
 def feed_kernel(
-    part0, part1, part2, part3, table_ref, bias_ref, eu_ref, sd_ref, su_ref, ed_ref,
+    part0, part1, part2, part3, table_ref, bias_ref, pack_ref,
     active_ref, slope_ref, low_u_ref, low_d_ref, out_ref, buf, sems, whole,
 ):
     _, count, chunks, rows, tile = buf.shape
+    su_ref, eu_ref, sd_ref, ed_ref = feed_pack(pack_ref, chunks * rows, count * tile)
     copies = feed_copies(table_ref, buf, sems)
     for up, _ in copies:
         up.start()
@@ -371,10 +359,11 @@
 
 
 def feed_back_kernel(
-    part0, part1, part2, part3, table_ref, slope_ref, eu_ref, sd_ref, su_ref, ed_ref,
+    part0, part1, part2, part3, table_ref, slope_ref, pack_ref,
     grad_up_ref, inner_d_ref, inner_u_ref, out_ref, buf, sems, whole,
 ):
     _, count, chunks, rows, tile = buf.shape
+    su_ref, eu_ref, sd_ref, ed_ref = feed_pack(pack_ref, chunks * rows, count * tile)
     copies = feed_copies(table_ref, buf, sems)
     for _, down in copies:
         down.start()
@@ -400,11 +389,12 @@
 
 
 def feed_both_kernel(
-    part0, part1, part2, part3, branch_ref, table_ref, bias_ref, eu_ref, sd_ref, su_ref, ed_ref,
+    part0, part1, part2, part3, branch_ref, table_ref, bias_ref, pack_ref,
     active_ref, low_u_ref, low_d_ref, out_ref, grad_up_ref, inner_d_ref, inner_u_ref, back_ref,
     buf, sems, whole,
 ):
     _, count, chunks, rows, tile = buf.shape
+    su_ref, eu_ref, sd_ref, ed_ref = feed_pack(pack_ref, chunks * rows, count * tile)
     copies = feed_copies(table_ref, buf, sems)
     for up, down in copies:
         up.start()
@@ -456,7 +446,7 @@
             pltpu.SemaphoreType.DMA((2, hidden // tile)),
             pltpu.VMEM((rows, model), bf16),
         ],
-        compiler_params=pltpu.CompilerParams(vmem_limit_bytes=40 * 2**20),
+        compiler_params=pltpu.CompilerParams(vmem_limit_bytes=26 * 2**20),
         cost_estimate=pl.CostEstimate(
             flops=2 * matmuls * rows * model * hidden,
             bytes_accessed=4 * model * hidden,
@@ -649,8 +639,7 @@
         for layer in range(2)
     ]
     adapters = [
-        split(early_layers[layer], [width, width, 2 * head])
-        + split(late_layers[layer], [width, width, local_f, local_f, width])
+        split(early_layers[layer], [width, width, 2 * head]) + [late_layers[layer][:, :width]]
         for layer in range(2)
     ]
 
@@ -678,7 +667,7 @@
 
     def forward_attend(layer, hidden):
         gain1, shift1, kv_bias, out_bias = small[layer][:4]
-        sq, skv, ekv, eo = adapters[layer][:4]
+        sq, skv, ekv, eo = adapters[layer]
         unit1, rsd1 = norm_parts(hidden)
         normed = (unit1 * gain1 + shift1).astype(bf16)
         low_kv = against(normed, skv).astype(bf16)
@@ -804,7 +793,7 @@
 
     def backward_attend(layer, kept, grad_middle):
         gain1 = small[layer][0]
-        sq, skv, ekv, eo = adapters[layer][:4]
+        sq, skv, ekv, eo = adapters[layer]
         unit1, rsd1, normed, low_q, low_kv, queries, key_block, probs, mixed, low_o = kept
         branch = grad_middle.astype(bf16)
         grad_q, grad_block, inner_o, inner_q, partial = attend_back(
@@ -838,12 +827,11 @@
 
     middle_zero, kept_zero = forward_attend(0, fresh)
     unit_zero, rsd_zero, second_zero, up_bias = feed_inputs(0, middle_zero)
-    su, eu, sd, ed = adapters[0][4:]
     active_zero, slope_zero, low_u_zero, low_d_zero, partial = feed_call(
         feed_kernel,
         "feed",
         second_zero,
-        (feed_tables[0], up_bias, eu, sd, su, ed),
+        (feed_tables[0], up_bias, late_layers[0]),
         (local_f, local_f, rank, rank, width),
         local_f,
         2,
@@ -852,13 +840,12 @@
 
     middle_one, kept_one = forward_attend(1, passed.astype(f32))
     unit_one, rsd_one, second_one, up_bias = feed_inputs(1, middle_one)
-    su, eu, sd, ed = adapters[1][4:]
     branch_one = spread(given.astype(bf16))
     active, low_u, low_d, partial, grad_up, inner_d, inner_u, partial_back = feed_call(
         feed_both_kernel,
         "feed_both",
         second_one,
-        (branch_one, feed_tables[1], up_bias, eu, sd, su, ed),
+        (branch_one, feed_tables[1], up_bias, late_layers[1]),
         (local_f, rank, rank, width, local_f, rank, rank, width),
         local_f,
         4,
@@ -872,13 +859,12 @@
     partial, _ = lax.optimization_barrier((partial, grad_middle))
     final = feed_result(1, middle_one, partial).astype(bf16)
 
-    su, eu, sd, ed = adapters[0][4:]
     branch_zero = spread_parts(grad_one.astype(bf16))
     grad_up, inner_d, inner_u, partial_back = feed_call(
         feed_back_kernel,
         "feed_back",
         branch_zero,
-        (feed_tables[0], slope_zero, eu, sd, su, ed),
+        (feed_tables[0], slope_zero, late_layers[0]),
         (local_f, rank, rank, width),
         local_f,
         2,

time: 565 us -> 603 us (1.067)
  local copies, waits for them, and re-layouts: 52.8 us -> 90.4 us
  Pallas kernels: 84.2 us -> 93.8 us
  waiting for transfers between devices: 227 us -> 218 us
    unnamed x348 -> x346, local copies, waits for them, and re-layouts: 26.6 us -> 65.2 us
    all_gather x2, waiting for transfers between devices: 26.2 us -> 16.2 us  [gather(): lax.all_gather(row_major(shard), both, axis=0, tiled=True, axis_index_gro...]
  transfers between devices with their start and end apart: 84 -> 84, of which waited for: 45 -> 42; matrix products, arithmetic and copies ran while one was open for 11% -> 10% of each run, Pallas kernels for 8% -> 9%
where the time goes in v8:
time: 603 us; the launch traced here: 593 us
  waiting for transfers between devices  218 us (36%)
  starting transfers between devices  129 us (21%)
  Pallas kernels  93.8 us (16%)
  local copies, waits for them, and re-layouts  90.4 us (15%)
  other arithmetic  30.2 us (5%)
  between operations  21.4 us (4%)
  matrix products  9.82 us (2%)
    ppermute x45, waiting for transfers between devices, around(): lax.ppermute(block, axis, [(i, (i + distance) % size) for i in range(size)])  93.8 us
    unnamed x346, local copies, waits for them, and re-layouts  65.2 us
    ppermute x45, starting transfers between devices, around(): lax.ppermute(block, axis, [(i, (i + distance) % size) for i in range(size)])  63.1 us
    all_gather x1, waiting for transfers between devices, gather_all(): lax.all_gather(row_major(shard), every, axis=0, tiled=True, axis_index_gr...  55.3 us
    pallas_call x3, Pallas kernels, feed_call(): pl.pallas_call(kernel, in_specs=[remote if value.ndim == 4 else held for...  43.2 us
    ppermute x16, starting transfers between devices, along(): return lax.ppermute(block, axis, route)  32.2 us
    ppermute x7, waiting for transfers between devices, swap(): return lax.ppermute(value, 'section', sides)  26.7 us
    pallas_call x2, Pallas kernels, attend_back(): pl.pallas_call(lambda *refs: attend_back_kernel(layer, head, *refs), in_s...  23.3 us
  transfers between devices with their start and end apart: 84, of which 42 were waited for; matrix products, arithmetic and copies ran while one was open for 10% of the time, Pallas kernels for 9%

profile of v8, /device:TPU:0, one launch (start us, length us, event | category | flops | bytes accessed | tf_op | source)
XLA Modules:
  0.0 592.9 jit_solution(1381216566424429316)
XLA Ops:
  12.3 4.0 collective-permute-start.17
  16.4 12.2 %collective-permute-done.17 = bf16[128,2048]{1,0:T(8,128)(2,1)S(1)} collective-permute-done((bf16[128,2048]{1,0:T(8,128)(2,1)S(1)}, bf16[128,2048]{1,0:T(8,128)(2,1)S(1)}, u32[]{:S(2)}, u32[]{:S(2)}) %collective-permute-start.17) | collective-permute-done | bytes 524320 | tf_op jit(solution)/shard_map/ppermute | solution.py:506
  42.8 4.0 collective-permute-start.13
  48.9 3.6 collective-permute-start
  55.5 14.5 %collective-permute-done = bf16[1,14592]{1,0:T(2,128)(2,1)S(1)} collective-permute-done((bf16[1,14592]{1,0:T(2,128)(2,1)S(1)}, bf16[1,14592]{1,0:T(2,128)(2,1)S(1)}, u32[]{:S(2)}, u32[]{:S(2)}) %collective-permute-start) | collective-permute-done | bytes 29216 | tf_op jit(solution)/shard_map/ppermute | solution.py:506
  83.3 55.3 %all-gather.4.cloned.1.call-done = bf16[16384,1152]{1,0:T(8,128)(2,1)} async-done(((bf16[128,1152]{1,0:T(8,128)(2,1)}), bf16[16384,1152]{1,0:T(8,128)(2,1)}) %all-gather.4.cloned.1.call-update) | async-done | bytes 37748752 | tf_op jit(solution)/shard_map/all_gather | solution.py:546
  141.8 3.4 collective-permute-start.6
  147.6 4.1 collective-permute-start.8
  157.4 12.0 %copy-done.2 = bf16[16384,1152]{1,0:T(8,128)(2,1)S(1)} copy-done((bf16[16384,1152]{1,0:T(8,128)(2,1)S(1)}, bf16[16384,1152]{1,0:T(8,128)(2,1)}, u32[]{:S(2)}) %copy-start.2) | copy-done | bytes 37748760
  169.4 4.2 project_queries.2
  175.0 7.3 %collective-permute-done.12 = bf16[320,256]{1,0:T(8,128)(2,1)S(1)} collective-permute-done((bf16[320,256]{1,0:T(8,128)(2,1)S(1)}, bf16[320,256]{1,0:T(8,128)(2,1)S(1)}, u32[]{:S(2)}, u32[]{:S(2)}) %collective-permute-start.12) | collective-permute-done | bytes 163872 | tf_op jit(solution)/shard_map/ppermute | solution.py:32
  182.4 9.6 %attend.2 = (bf16[4,256,1280]{2,1,0:T(8,128)(2,1)S(1)}, bf16[64,2048]{1,0:T(8,128)(2,1)S(1)}, bf16[64,16]{1,0:T(8,128)(2,1)S(1)}, f32[64,2048]{1,0:T(8,128)S(1)}) custom-call(bf16[64,2048]{1,0:T(8,128)(2,1)S(1)} %get-tuple-element.79.refs_0_.refs_5_, bf16[1280,256]{1,0:T(8,128)(2,1)S(1)} %constant_dynamic-update-slice_fusion.18.refs_1_.refs_6_, ...), custom_call_target="tpu_custom_call" | custom-call | flops 2818572288 | bytes 8388608 | tf_op jit(solution)/shard_map/attend/pallas_call | solution.py:180
  197.2 16.2 %all-gather.6.cloned.1.call-done = bf16[4096,2048]{1,0:T(8,128)(2,1)} async-done(((bf16[128,2048]{1,0:T(8,128)(2,1)}), bf16[4096,2048]{1,0:T(8,128)(2,1)}) %all-gather.6.cloned.1.call-update) | async-done | bytes 16777232 | tf_op jit(solution)/shard_map/all_gather | solution.py:542
  213.4 6.0 %copy-done.4 = bf16[4096,2048]{1,0:T(8,128)(2,1)S(1)} copy-done((bf16[4096,2048]{1,0:T(8,128)(2,1)S(1)}, bf16[4096,2048]{1,0:T(8,128)(2,1)}, u32[]{:S(2)}) %copy-start.4) | copy-done | bytes 16777240
  219.5 12.5 %feed.1 = (bf16[256,2048]{1,0:T(8,128)(2,1)S(1)}, bf16[256,2048]{1,0:T(8,128)(2,1)S(1)}, bf16[256,16]{1,0:T(8,128)(2,1)S(1)}, bf16[256,16]{1,0:T(8,128)(2,1)S(1)}, bf16[256,2048]{1,0:T(8,128)(2,1)S(1)}) custom-call(bf16[64,2048]{1,0:T(8,128)(2,1)S(1)} %add_convert_fusion.3.part0, bf16[64,2048]{1,0:T(8,128)(2,1)S(1)} %collective-permute-done.14.part1, ...), custom_call_target="tpu_custom_call" | custom-call | flops 4294967296 | bytes 16777216 | tf_op jit(solution)/shard_map/feed/pallas_call | solution.py:439
  238.5 3.4 collective-permute-done.18
  241.9 6.5 %collective-permute-done.19 = bf16[64,2048]{1,0:T(8,128)(2,1)S(1)} collective-permute-done((bf16[64,2048]{1,0:T(8,128)(2,1)S(1)}, bf16[64,2048]{1,0:T(8,128)(2,1)S(1)}, u32[]{:S(2)}, u32[]{:S(2)}) %collective-permute-start.19) | collective-permute-done | bytes 262176 | tf_op jit(solution)/shard_map/ppermute | solution.py:32
  250.1 3.4 collective-permute-start.21
  259.3 3.4 collective-permute-start.23
  269.9 13.1 %copy-done.3 = bf16[16384,1152]{1,0:T(8,128)(2,1)S(1)} copy-done((bf16[16384,1152]{1,0:T(8,128)(2,1)S(1)}, bf16[16384,1152]{1,0:T(8,128)(2,1)}, u32[]{:S(2)}) %copy-start.3) | copy-done | bytes 37748760
  283.0 4.2 project_queries.3
  287.4 7.5 %collective-permute-done.27 = bf16[320,256]{1,0:T(8,128)(2,1)S(1)} collective-permute-done((bf16[320,256]{1,0:T(8,128)(2,1)S(1)}, bf16[320,256]{1,0:T(8,128)(2,1)S(1)}, u32[]{:S(2)}, u32[]{:S(2)}) %collective-permute-start.27) | collective-permute-done | bytes 163872 | tf_op jit(solution)/shard_map/ppermute | solution.py:32
  295.0 9.3 %attend.3 = (bf16[4,256,1280]{2,1,0:T(8,128)(2,1)S(1)}, bf16[64,2048]{1,0:T(8,128)(2,1)S(1)}, bf16[64,16]{1,0:T(8,128)(2,1)S(1)}, f32[64,2048]{1,0:T(8,128)S(1)}) custom-call(bf16[64,2048]{1,0:T(8,128)(2,1)S(1)} %get-tuple-element.82.refs_0_.refs_5_, bf16[1280,256]{1,0:T(8,128)(2,1)S(1)} %constant_dynamic-update-slice_fusion.41.refs_1_.refs_6_, ...), custom_call_target="tpu_custom_call" | custom-call | flops 2818572288 | bytes 8388608 | tf_op jit(solution)/shard_map/attend/pallas_call | solution.py:180
  312.3 6.3 %collective-permute-done.28.part1 = bf16[64,2048]{1,0:T(8,128)(2,1)} collective-permute-done((bf16[64,2048]{1,0:T(8,128)(2,1)}, bf16[64,2048]{1,0:T(8,128)(2,1)}, u32[]{:S(2)}, u32[]{:S(2)}) %collective-permute-start.28) | collective-permute-done | bytes 262176 | tf_op jit(solution)/shard_map/ppermute | solution.py:32
  320.2 5.2 collective-permute-done.30.part3
  326.3 5.8 copy-done.68
  332.1 18.1 %feed_both.1 = (bf16[256,2048]{1,0:T(8,128)(2,1)S(1)}, bf16[256,16]{1,0:T(8,128)(2,1)S(1)}, bf16[256,16]{1,0:T(8,128)(2,1)S(1)}, bf16[256,2048]{1,0:T(8,128)(2,1...) custom-call(bf16[64,2048]{1,0:T(8,128)(2,1)} %add_convert_fusion.1.p, ...), custom_call_target="tpu_custom_call" | custom-call | flops 8589934592 | bytes 16777216 | tf_op jit(solution)/shard_map/feed_both/pallas_call | solution.py:439
  362.6 10.5 %collective-permute-done.34 = bf16[64,2048]{1,0:T(8,128)(2,1)} collective-permute-done((bf16[64,2048]{1,0:T(8,128)(2,1)}, bf16[64,2048]{1,0:T(8,128)(2,1)}, u32[]{:S(2)}, u32[]{:S(2)}) %collective-permute-start.34) | collective-permute-done | bytes 262176 | tf_op jit(solution)/shard_map/ppermute | solution.py:32
  376.9 11.6 %attend_back.2 = (bf16[64,2048]{1,0:T(8,128)(2,1)S(1)}, bf16[1280,256]{1,0:T(8,128)(2,1)S(1)}, bf16[64,16]{1,0:T(8,128)(2,1)S(1)}, bf16[64,16]{1,0:T(8,128)(2,1)S(1)}, f32[64,2048]{1,0:T(8,128)S(1)}) custom-call(bf16[64,2048]{1,0:T(8,128)(2,1)S(1)} %get-tuple-element.163.refs_0_, bf16[4,4,2,512,1152]{4,3,2,1,0:T(8,128)(2,1)} %bitcast.719, ...), custom_call_target="tpu_custom_call" | custom-call | flops 5637144576 | bytes 22020096 | tf_op jit(solution)/shard_map/attend_back/pallas_call | solution.py:259
  389.2 3.6 collective-permute-start.41
  396.6 3.7 collective-permute-done.41
  411.3 3.6 collective-permute-start.38
  420.1 6.4 %concatenate.208 = bf16[84,16,128]{2,0,1:T(8,128)(2,1)} concatenate(bf16[16,16,128]{2,0,1:T(8,128)(2,1)} %bitcast.784, bf16[16,16,128]{2,0,1:T(8,128)(2,1)} %bitcast.783, bf16[16,16,128]{2,0,1:T(8,128)(2,1)} %bitcast.782, bf16[16,16,128]{2,0,1:T(8,128)(2,1)S(1)} %bitcast.781, bf16[16,16,128]{2,0,1:T(8,128)(2,1)S(1)} %bitcast.785, bf16[2,16,128]{2,0,1:T(2,128)(2,1)S(1)} %bitcast.828, ...), dimensions={0} | concatenate | bytes 688128 | tf_op jit(solution)/shard_map/concatenate | solution.py:707
  433.4 5.8 collective-permute-done.49.part3
  439.2 5.8 copy-done.5
  445.0 12.6 %feed_back.1 = (bf16[256,2048]{1,0:T(8,128)(2,1)S(1)}, bf16[256,16]{1,0:T(8,128)(2,1)S(1)}, bf16[256,16]{1,0:T(8,128)(2,1)S(1)}, bf16[256,2048]{1,0:T(8,128)(2,1)S(1)}) custom-call(bf16[64,2048]{1,0:T(8,128)(2,1)S(1)} %get-tuple-element.109.part0, bf16[64,2048]{1,0:T(8,128)(2,1)S(1)} %collective-permute-done.47.part1, ...), custom_call_target="tpu_custom_call" | custom-call | flops 4294967296 | bytes 16777216 | tf_op jit(solution)/shard_map/feed_back/pallas_call | solution.py:439
  462.8 10.1 %collective-permute-done.50 = bf16[64,2048]{1,0:T(8,128)(2,1)S(1)} collective-permute-done((bf16[64,2048]{1,0:T(8,128)(2,1)S(1)}, bf16[64,2048]{1,0:T(8,128)(2,1)S(1)}, u32[]{:S(2)}, u32[]{:S(2)}) %collective-permute-start.50) | collective-permute-done | bytes 262176 | tf_op jit(solution)/shard_map/ppermute | solution.py:32
  476.0 11.7 %attend_back.3 = (bf16[64,2048]{1,0:T(8,128)(2,1)S(1)}, bf16[1280,256]{1,0:T(8,128)(2,1)S(1)}, bf16[64,16]{1,0:T(8,128)(2,1)S(1)}, bf16[64,16]{1,0:T(8,128)(2,1)S(1)}, f32[64,2048]{1,0:T(8,128)S(1)}) custom-call(bf16[64,2048]{1,0:T(8,128)(2,1)S(1)} %get-tuple-element.156.refs_0_, bf16[4,4,2,512,1152]{4,3,2,1,0:T(8,128)(2,1)} %bitcast.720, ...), custom_call_target="tpu_custom_call" | custom-call | flops 5637144576 | bytes 22020096 | tf_op jit(solution)/shard_map/attend_back/pallas_call | solution.py:259
  488.0 3.8 collective-permute-start.55
  505.1 3.3 collective-permute-done.58
  509.9 4.1 collective-permute-done.60
  515.5 3.6 collective-permute-start.63
  519.7 5.2 collective-permute-done.62
  524.9 4.8 collective-permute-done.63
  532.5 4.2 collective-permute-done.66
  538.7 3.2 collective-permute-start.68
  568.5 3.9 collective-permute-start.79
  575.9 4.5 collective-permute-done.79
  (701 shorter events, 190.5 us)
Async XLA Ops:
  7.2 131.4 %all-gather.4.cloned.1.call-start = ((), (), s32[]{:S(2)}) async-start(), calls=%async_computation | async-start | bytes 38043648 | tf_op jit(solution)/shard_map/all_gather | solution.py:546
  10.8 202.6 %all-gather.6.cloned.1.call-start = ((), (), s32[]{:S(2)}) async-start(), calls=%async_computation.1 | async-start | bytes 17301504 | tf_op jit(solution)/shard_map/all_gather | solution.py:542
  12.3 16.3 %collective-permute-start.17 = (bf16[128,2048]{1,0:T(8,128)(2,1)S(1)}, bf16[128,2048]{1,0:T(8,128)(2,1)S(1)}, u32[]{:S(2)}, u32[]{:S(2)}) collective-permute-start(bf16[128,2048]{1,0:T(8,128)(2,1)S(1)} %broadcast_select_fusion.2), channel_id=1, source_target_pairs={{0,64},{64,0},{1,65},{65,1},{2,66},{66,2},{3,67},{67,3},{4,68},{68... | collective-permute-start | bytes 1572872 | tf_op jit(solution)/shard_map/ppermute | solution.py:506
  30.0 282.3 %all-gather.8.cloned.1.call-start = ((), (), s32[]{:S(2)}) async-start(), calls=%async_computation.2 | async-start | bytes 17301504 | tf_op jit(solution)/shard_map/all_gather | solution.py:542
  42.8 102.4 %collective-permute-start.13 = (bf16[16,10240]{1,0:T(8,128)(2,1)}, bf16[16,10240]{1,0:T(8,128)(2,1)S(1)}, u32[]{:S(2)}, u32[]{:S(2)}) collective-permute-start(bf16[16,10240]{1,0:T(8,128)(2,1)} %get-tuple-element.230), channel_id=1, source_target_pairs={{0,64},{64,0},{1,65},{65,1},{2,66},{66,2},{3,67},{67,3},{4,68},{68... | collective-permute-start | bytes 983048 | tf_op jit(solution)/shard_map/ppermute | solution.py:506
  48.5 28.9 %collective-permute-start.5 = (bf16[16,4352]{1,0:T(8,128)(2,1)S(1)}, bf16[16,4352]{1,0:T(8,128)(2,1)S(1)}, u32[]{:S(2)}, u32[]{:S(2)}) collective-permute-start(bf16[16,4352]{1,0:T(8,128)(2,1)S(1)} %pad_maximum_fusion.15), channel_id=1, source_target_pairs={{0,64},{64,0},{1,65},{65,1},{2,66},{66,2},{3,67},{67,3},{4,68},{68... | collective-permute-start | bytes 417800 | tf_op jit(solution)/shard_map/ppermute | solution.py:506
  48.9 21.1 %collective-permute-start = (bf16[1,14592]{1,0:T(2,128)(2,1)S(1)}, bf16[1,14592]{1,0:T(2,128)(2,1)S(1)}, u32[]{:S(2)}, u32[]{:S(2)}) collective-permute-start(bf16[1,14592]{1,0:T(2,128)(2,1)S(1)} %constant_dynamic-update-slice_fusion), channel_id=1, source_target_pairs={{0,64},{64,0},{1,65},{65,1},{2,66},{66,2},{3,67},{67,3},{4,68},{68... | collective-permute-start | bytes 87560 | tf_op jit(solution)/shard_map/ppermute | solution.py:506
  54.0 17.5 %collective-permute-start.1 = (bf16[16,1536]{1,0:T(8,128)(2,1)S(1)}, bf16[16,1536]{1,0:T(8,128)(2,1)S(1)}, u32[]{:S(2)}, u32[]{:S(2)}) collective-permute-start(bf16[16,1536]{1,0:T(8,128)(2,1)S(1)} %maximum_maximum_fusion.2), channel_id=1, source_target_pairs={{0,64},{64,0},{1,65},{65,1},{2,66},{66,2},{3,67},{67,3},{4,68},{68... | collective-permute-start | bytes 147464 | tf_op jit(solution)/shard_map/ppermute | solution.py:506
  141.8 11.3 %collective-permute-start.6 = (bf16[64,256]{1,0:T(8,128)(2,1)S(1)}, bf16[64,256]{1,0:T(8,128)(2,1)S(1)}, u32[]{:S(2)}, u32[]{:S(2)}) collective-permute-start(bf16[64,256]{1,0:T(8,128)(2,1)S(1)} %fusion.20), channel_id=1, source_target_pairs={{0,16},{4,20},{8,24},{12,28},{16,32},{20,36},{24,40},{28,44},{32,4... | collective-permute-start | bytes 98312 | tf_op jit(solution)/shard_map/ppermute | solution.py:38
  154.0 20.9 %collective-permute-start.10 = (bf16[320,256]{1,0:T(8,128)(2,1)S(1)}, bf16[320,256]{1,0:T(8,128)(2,1)S(1)}, u32[]{:S(2)}, u32[]{:S(2)}) collective-permute-start(bf16[320,256]{1,0:T(8,128)(2,1)S(1)} %get-tuple-element.327), channel_id=1, source_target_pairs={{0,3},{1,0},{2,1},{3,2},{4,7},{5,4},{6,5},{7,6},{8,11},{9,8},{10,9... | collective-permute-start | bytes 491528 | tf_op jit(solution)/shard_map/ppermute | solution.py:32
  156.6 18.4 %collective-permute-start.11 = (bf16[320,256]{1,0:T(8,128)(2,1)S(1)}, bf16[320,256]{1,0:T(8,128)(2,1)S(1)}, u32[]{:S(2)}, u32[]{:S(2)}) collective-permute-start(bf16[320,256]{1,0:T(8,128)(2,1)S(1)} %get-tuple-element.327), channel_id=1, source_target_pairs={{0,2},{1,3},{2,0},{3,1},{4,6},{5,7},{6,4},{7,5},{8,10},{9,11},{10,... | collective-permute-start | bytes 491528 | tf_op jit(solution)/shard_map/ppermute | solution.py:32
  194.5 18.9 %collective-permute-start.14 = (bf16[64,2048]{1,0:T(8,128)(2,1)S(1)}, bf16[64,2048]{1,0:T(8,128)(2,1)S(1)}, u32[]{:S(2)}, u32[]{:S(2)}) collective-permute-start(bf16[64,2048]{1,0:T(8,128)(2,1)S(1)} %add_convert_fusion.3.part0), channel_id=1, source_target_pairs={{0,3},{1,0},{2,1},{3,2},{4,7},{5,4},{6,5},{7,6},{8,11},{9,8},{10,9... | collective-permute-start | bytes 786440 | tf_op jit(solution)/shard_map/ppermute | solution.py:32
  194.6 18.8 %collective-permute-start.15 = (bf16[64,2048]{1,0:T(8,128)(2,1)S(1)}, bf16[64,2048]{1,0:T(8,128)(2,1)S(1)}, u32[]{:S(2)}, u32[]{:S(2)}) collective-permute-start(bf16[64,2048]{1,0:T(8,128)(2,1)S(1)} %add_convert_fusion.3.part0), channel_id=1, source_target_pairs={{0,2},{1,3},{2,0},{3,1},{4,6},{5,7},{6,4},{7,5},{8,10},{9,11},{10,... | collective-permute-start | bytes 786440 | tf_op jit(solution)/shard_map/ppermute | solution.py:32
  196.2 17.2 %collective-permute-start.16 = (bf16[64,2048]{1,0:T(8,128)(2,1)S(1)}, bf16[64,2048]{1,0:T(8,128)(2,1)S(1)}, u32[]{:S(2)}, u32[]{:S(2)}) collective-permute-start(bf16[64,2048]{1,0:T(8,128)(2,1)S(1)} %add_convert_fusion.3.part0), channel_id=1, source_target_pairs={{0,1},{1,2},{2,3},{3,0},{4,5},{5,6},{6,7},{7,4},{8,9},{9,10},{10,1... | collective-permute-start | bytes 786440 | tf_op jit(solution)/shard_map/ppermute | solution.py:32
  232.2 9.7 %collective-permute-start.18 = (bf16[64,2048]{1,0:T(8,128)(2,1)S(1)}, bf16[64,2048]{1,0:T(8,128)(2,1)S(1)}, u32[]{:S(2)}, u32[]{:S(2)}) collective-permute-start(bf16[64,2048]{1,0:T(8,128)(2,1)S(1)} %get-tuple-element.187), channel_id=1, source_target_pairs={{0,1},{1,2},{2,3},{3,0},{4,5},{5,6},{6,7},{7,4},{8,9},{9,10},{10,1... | collective-permute-start | bytes 786440 | tf_op jit(solution)/shard_map/ppermute | solution.py:32
  233.8 14.7 %collective-permute-start.19 = (bf16[64,2048]{1,0:T(8,128)(2,1)S(1)}, bf16[64,2048]{1,0:T(8,128)(2,1)S(1)}, u32[]{:S(2)}, u32[]{:S(2)}) collective-permute-start(bf16[64,2048]{1,0:T(8,128)(2,1)S(1)} %get-tuple-element.189), channel_id=1, source_target_pairs={{0,2},{1,3},{2,0},{3,1},{4,6},{5,7},{6,4},{7,5},{8,10},{9,11},{10,... | collective-permute-start | bytes 786440 | tf_op jit(solution)/shard_map/ppermute | solution.py:32
  236.4 12.1 %collective-permute-start.20 = (bf16[64,2048]{1,0:T(8,128)(2,1)S(1)}, bf16[64,2048]{1,0:T(8,128)(2,1)S(1)}, u32[]{:S(2)}, u32[]{:S(2)}) collective-permute-start(bf16[64,2048]{1,0:T(8,128)(2,1)S(1)} %get-tuple-element.188), channel_id=1, source_target_pairs={{0,3},{1,0},{2,1},{3,2},{4,7},{5,4},{6,5},{7,6},{8,11},{9,8},{10,9... | collective-permute-start | bytes 786440 | tf_op jit(solution)/shard_map/ppermute | solution.py:32
  253.5 57.1 %collective-permute-start.31 = (bf16[64,2048]{1,0:T(8,128)(2,1)S(1)}, bf16[64,2048]{1,0:T(8,128)(2,1)S(1)}, u32[]{:S(2)}, u32[]{:S(2)}) collective-permute-start(bf16[64,2048]{1,0:T(8,128)(2,1)S(1)} %dynamic-slice_bitcast_fusion), channel_id=1, source_target_pairs={{0,3},{1,0},{2,1},{3,2},{4,7},{5,4},{6,5},{7,6},{8,11},{9,8},{10,9... | collective-permute-start | bytes 786440 | tf_op jit(solution)/shard_map/ppermute | solution.py:32
  255.9 56.3 %collective-permute-start.32 = (bf16[64,2048]{1,0:T(8,128)(2,1)S(1)}, bf16[64,2048]{1,0:T(8,128)(2,1)S(1)}, u32[]{:S(2)}, u32[]{:S(2)}) collective-permute-start(bf16[64,2048]{1,0:T(8,128)(2,1)S(1)} %dynamic-slice_bitcast_fusion), channel_id=1, source_target_pairs={{0,2},{1,3},{2,0},{3,1},{4,6},{5,7},{6,4},{7,5},{8,10},{9,11},{10,... | collective-permute-start | bytes 786440 | tf_op jit(solution)/shard_map/ppermute | solution.py:32
  257.0 55.2 %collective-permute-start.33 = (bf16[64,2048]{1,0:T(8,128)(2,1)S(1)}, bf16[64,2048]{1,0:T(8,128)(2,1)S(1)}, u32[]{:S(2)}, u32[]{:S(2)}) collective-permute-start(bf16[64,2048]{1,0:T(8,128)(2,1)S(1)} %dynamic-slice_bitcast_fusion), channel_id=1, source_target_pairs={{0,1},{1,2},{2,3},{3,0},{4,5},{5,6},{6,7},{7,4},{8,9},{9,10},{10,1... | collective-permute-start | bytes 786440 | tf_op jit(solution)/shard_map/ppermute | solution.py:32
  265.9 21.3 %collective-permute-start.25 = (bf16[320,256]{1,0:T(8,128)(2,1)S(1)}, bf16[320,256]{1,0:T(8,128)(2,1)S(1)}, u32[]{:S(2)}, u32[]{:S(2)}) collective-permute-start(bf16[320,256]{1,0:T(8,128)(2,1)S(1)} %get-tuple-element.317), channel_id=1, source_target_pairs={{0,3},{1,0},{2,1},{3,2},{4,7},{5,4},{6,5},{7,6},{8,11},{9,8},{10,9... | collective-permute-start | bytes 491528 | tf_op jit(solution)/shard_map/ppermute | solution.py:32
  268.6 18.8 %collective-permute-start.26 = (bf16[320,256]{1,0:T(8,128)(2,1)S(1)}, bf16[320,256]{1,0:T(8,128)(2,1)S(1)}, u32[]{:S(2)}, u32[]{:S(2)}) collective-permute-start(bf16[320,256]{1,0:T(8,128)(2,1)S(1)} %get-tuple-element.317), channel_id=1, source_target_pairs={{0,2},{1,3},{2,0},{3,1},{4,6},{5,7},{6,4},{7,5},{8,10},{9,11},{10,... | collective-permute-start | bytes 491528 | tf_op jit(solution)/shard_map/ppermute | solution.py:32
  309.2 11.0 %collective-permute-start.29 = (bf16[64,2048]{1,0:T(8,128)(2,1)}, bf16[64,2048]{1,0:T(8,128)(2,1)}, u32[]{:S(2)}, u32[]{:S(2)}) collective-permute-start(bf16[64,2048]{1,0:T(8,128)(2,1)} %add_convert_fusion.1.part0), channel_id=1, source_target_pairs={{0,2},{1,3},{2,0},{3,1},{4,6},{5,7},{6,4},{7,5},{8,10},{9,11},{10,... | collective-permute-start | bytes 786440 | tf_op jit(solution)/shard_map/ppermute | solution.py:32
  310.6 14.8 %collective-permute-start.30 = (bf16[64,2048]{1,0:T(8,128)(2,1)}, bf16[64,2048]{1,0:T(8,128)(2,1)}, u32[]{:S(2)}, u32[]{:S(2)}) collective-permute-start(bf16[64,2048]{1,0:T(8,128)(2,1)} %add_convert_fusion.1.part0), channel_id=1, source_target_pairs={{0,1},{1,2},{2,3},{3,0},{4,5},{5,6},{6,7},{7,4},{8,9},{9,10},{10,1... | collective-permute-start | bytes 786440 | tf_op jit(solution)/shard_map/ppermute | solution.py:32
  357.7 15.4 %collective-permute-start.34 = (bf16[64,2048]{1,0:T(8,128)(2,1)}, bf16[64,2048]{1,0:T(8,128)(2,1)}, u32[]{:S(2)}, u32[]{:S(2)}) collective-permute-start(bf16[64,2048]{1,0:T(8,128)(2,1)} %get-tuple-element.184), channel_id=1, source_target_pairs={{0,1},{1,2},{2,3},{3,0},{4,5},{5,6},{6,7},{7,4},{8,9},{9,10},{10,1... | collective-permute-start | bytes 786440 | tf_op jit(solution)/shard_map/ppermute | solution.py:32
  357.7 15.4 %collective-permute-start.35 = (bf16[64,2048]{1,0:T(8,128)(2,1)}, bf16[64,2048]{1,0:T(8,128)(2,1)}, u32[]{:S(2)}, u32[]{:S(2)}) collective-permute-start(bf16[64,2048]{1,0:T(8,128)(2,1)} %get-tuple-element.186), channel_id=1, source_target_pairs={{0,2},{1,3},{2,0},{3,1},{4,6},{5,7},{6,4},{7,5},{8,10},{9,11},{10,... | collective-permute-start | bytes 786440 | tf_op jit(solution)/shard_map/ppermute | solution.py:32
  360.3 13.4 %collective-permute-start.36 = (bf16[64,2048]{1,0:T(8,128)(2,1)}, bf16[64,2048]{1,0:T(8,128)(2,1)}, u32[]{:S(2)}, u32[]{:S(2)}) collective-permute-start(bf16[64,2048]{1,0:T(8,128)(2,1)} %get-tuple-element.185), channel_id=1, source_target_pairs={{0,3},{1,0},{2,1},{3,2},{4,7},{5,4},{6,5},{7,6},{8,11},{9,8},{10,9... | collective-permute-start | bytes 786440 | tf_op jit(solution)/shard_map/ppermute | solution.py:32
  389.2 11.2 %collective-permute-start.41 = (bf16[320,256]{1,0:T(8,128)(2,1)S(1)}, bf16[320,256]{1,0:T(8,128)(2,1)S(1)}, u32[]{:S(2)}, u32[]{:S(2)}) collective-permute-start(bf16[320,256]{1,0:T(8,128)(2,1)S(1)} %get-tuple-element.202), channel_id=1, source_target_pairs={{0,2},{1,3},{2,0},{3,1},{4,6},{5,7},{6,4},{7,5},{8,10},{9,11},{10,... | collective-permute-start | bytes 491528 | tf_op jit(solution)/shard_map/ppermute | solution.py:32
  400.5 10.8 %collective-permute-start.43 = (bf16[64,256]{1,0:T(8,128)(2,1)S(1)}, bf16[64,256]{1,0:T(8,128)(2,1)S(1)}, u32[]{:S(2)}, u32[]{:S(2)}) collective-permute-start(bf16[64,256]{1,0:T(8,128)(2,1)S(1)} %get-tuple-element.276), channel_id=1, source_target_pairs={{4,0},{8,4},{12,8},{16,12},{20,16},{24,20},{28,24},{32,28},{36,32}... | collective-permute-start | bytes 98312 | tf_op jit(solution)/shard_map/ppermute | solution.py:38
  402.0 12.9 %collective-permute-start.44 = (bf16[64,256]{1,0:T(8,128)(2,1)S(1)}, bf16[64,256]{1,0:T(8,128)(2,1)S(1)}, u32[]{:S(2)}, u32[]{:S(2)}) collective-permute-start(bf16[64,256]{1,0:T(8,128)(2,1)S(1)} %get-tuple-element.279), channel_id=1, source_target_pairs={{8,0},{12,4},{16,8},{20,12},{24,16},{28,20},{32,24},{36,28},{40,32... | collective-permute-start | bytes 98312 | tf_op jit(solution)/shard_map/ppermute | solution.py:38
  403.3 11.6 %collective-permute-start.45 = (bf16[64,256]{1,0:T(8,128)(2,1)S(1)}, bf16[64,256]{1,0:T(8,128)(2,1)S(1)}, u32[]{:S(2)}, u32[]{:S(2)}) collective-permute-start(bf16[64,256]{1,0:T(8,128)(2,1)S(1)} %get-tuple-element.278), channel_id=1, source_target_pairs={{12,0},{16,4},{20,8},{24,12},{28,16},{32,20},{36,24},{40,28},{44,3... | collective-permute-start | bytes 98312 | tf_op jit(solution)/shard_map/ppermute | solution.py:38
  404.6 10.3 %collective-permute-start.46 = (bf16[64,256]{1,0:T(8,128)(2,1)S(1)}, bf16[64,256]{1,0:T(8,128)(2,1)S(1)}, u32[]{:S(2)}, u32[]{:S(2)}) collective-permute-start(bf16[64,256]{1,0:T(8,128)(2,1)S(1)} %get-tuple-element.277), channel_id=1, source_target_pairs={{16,0},{20,4},{24,8},{28,12},{32,16},{36,20},{40,24},{44,28},{48,3... | collective-permute-start | bytes 98312 | tf_op jit(solution)/shard_map/ppermute | solution.py:38
  411.2 48.5 %collective-permute-start.37 = (bf16[64,2048]{1,0:T(8,128)(2,1)}, bf16[64,2048]{1,0:T(8,128)(2,1)}, u32[]{:S(2)}, u32[]{:S(2)}) collective-permute-start(bf16[64,2048]{1,0:T(8,128)(2,1)} %get-tuple-element.181), channel_id=1, source_target_pairs={{0,1},{1,2},{2,3},{3,0},{4,5},{5,6},{6,7},{7,4},{8,9},{9,10},{10,1... | collective-permute-start | bytes 786440 | tf_op jit(solution)/shard_map/ppermute | solution.py:32
  411.3 49.9 %collective-permute-start.38 = (bf16[64,2048]{1,0:T(8,128)(2,1)}, bf16[64,2048]{1,0:T(8,128)(2,1)}, u32[]{:S(2)}, u32[]{:S(2)}) collective-permute-start(bf16[64,2048]{1,0:T(8,128)(2,1)} %get-tuple-element.183), channel_id=1, source_target_pairs={{0,2},{1,3},{2,0},{3,1},{4,6},{5,7},{6,4},{7,5},{8,10},{9,11},{10,... | collective-permute-start | bytes 786440 | tf_op jit(solution)/shard_map/ppermute | solution.py:32
  417.1 11.3 %collective-permute-start.47 = (bf16[64,2048]{1,0:T(8,128)(2,1)S(1)}, bf16[64,2048]{1,0:T(8,128)(2,1)S(1)}, u32[]{:S(2)}, u32[]{:S(2)}) collective-permute-start(bf16[64,2048]{1,0:T(8,128)(2,1)S(1)} %get-tuple-element.109.part0), channel_id=1, source_target_pairs={{0,3},{1,0},{2,1},{3,2},{4,7},{5,4},{6,5},{7,6},{8,11},{9,8},{10,9... | collective-permute-start | bytes 786440 | tf_op jit(solution)/shard_map/ppermute | solution.py:32
  417.7 15.7 %collective-permute-start.48 = (bf16[64,2048]{1,0:T(8,128)(2,1)S(1)}, bf16[64,2048]{1,0:T(8,128)(2,1)S(1)}, u32[]{:S(2)}, u32[]{:S(2)}) collective-permute-start(bf16[64,2048]{1,0:T(8,128)(2,1)S(1)} %get-tuple-element.109.part0), channel_id=1, source_target_pairs={{0,2},{1,3},{2,0},{3,1},{4,6},{5,7},{6,4},{7,5},{8,10},{9,11},{10,... | collective-permute-start | bytes 786440 | tf_op jit(solution)/shard_map/ppermute | solution.py:32
  419.6 19.6 %collective-permute-start.49 = (bf16[64,2048]{1,0:T(8,128)(2,1)S(1)}, bf16[64,2048]{1,0:T(8,128)(2,1)}, u32[]{:S(2)}, u32[]{:S(2)}) collective-permute-start(bf16[64,2048]{1,0:T(8,128)(2,1)S(1)} %get-tuple-element.109.part0), channel_id=1, source_target_pairs={{0,1},{1,2},{2,3},{3,0},{4,5},{5,6},{6,7},{7,4},{8,9},{9,10},{10,1... | collective-permute-start | bytes 786440 | tf_op jit(solution)/shard_map/ppermute | solution.py:32
  428.4 32.9 %collective-permute-start.39 = (bf16[64,2048]{1,0:T(8,128)(2,1)}, bf16[64,2048]{1,0:T(8,128)(2,1)S(1)}, u32[]{:S(2)}, u32[]{:S(2)}) collective-permute-start(bf16[64,2048]{1,0:T(8,128)(2,1)} %get-tuple-element.182), channel_id=1, source_target_pairs={{0,3},{1,0},{2,1},{3,2},{4,7},{5,4},{6,5},{7,6},{8,11},{9,8},{10,9... | collective-permute-start | bytes 786440 | tf_op jit(solution)/shard_map/ppermute | solution.py:32
  457.7 15.1 %collective-permute-start.50 = (bf16[64,2048]{1,0:T(8,128)(2,1)S(1)}, bf16[64,2048]{1,0:T(8,128)(2,1)S(1)}, u32[]{:S(2)}, u32[]{:S(2)}) collective-permute-start(bf16[64,2048]{1,0:T(8,128)(2,1)S(1)} %get-tuple-element.178), channel_id=1, source_target_pairs={{0,1},{1,2},{2,3},{3,0},{4,5},{5,6},{6,7},{7,4},{8,9},{9,10},{10,1... | collective-permute-start | bytes 786440 | tf_op jit(solution)/shard_map/ppermute | solution.py:32
  457.8 15.0 %collective-permute-start.51 = (bf16[64,2048]{1,0:T(8,128)(2,1)S(1)}, bf16[64,2048]{1,0:T(8,128)(2,1)S(1)}, u32[]{:S(2)}, u32[]{:S(2)}) collective-permute-start(bf16[64,2048]{1,0:T(8,128)(2,1)S(1)} %get-tuple-element.180), channel_id=1, source_target_pairs={{0,2},{1,3},{2,0},{3,1},{4,6},{5,7},{6,4},{7,5},{8,10},{9,11},{10,... | collective-permute-start | bytes 786440 | tf_op jit(solution)/shard_map/ppermute | solution.py:32
  459.7 13.8 %collective-permute-start.52 = (bf16[64,2048]{1,0:T(8,128)(2,1)S(1)}, bf16[64,2048]{1,0:T(8,128)(2,1)S(1)}, u32[]{:S(2)}, u32[]{:S(2)}) collective-permute-start(bf16[64,2048]{1,0:T(8,128)(2,1)S(1)} %get-tuple-element.179), channel_id=1, source_target_pairs={{0,3},{1,0},{2,1},{3,2},{4,7},{5,4},{6,5},{7,6},{8,11},{9,8},{10,9... | collective-permute-start | bytes 786440 | tf_op jit(solution)/shard_map/ppermute | solution.py:32
  488.0 11.3 %collective-permute-start.55 = (bf16[320,256]{1,0:T(8,128)(2,1)S(1)}, bf16[320,256]{1,0:T(8,128)(2,1)S(1)}, u32[]{:S(2)}, u32[]{:S(2)}) collective-permute-start(bf16[320,256]{1,0:T(8,128)(2,1)S(1)} %get-tuple-element.199), channel_id=1, source_target_pairs={{0,2},{1,3},{2,0},{3,1},{4,6},{5,7},{6,4},{7,5},{8,10},{9,11},{10,... | collective-permute-start | bytes 491528 | tf_op jit(solution)/shard_map/ppermute | solution.py:32
  491.9 58.3 %collective-permute-start.53 = (bf16[64,2048]{1,0:T(8,128)(2,1)S(1)}, bf16[64,2048]{1,0:T(8,128)(2,1)S(1)}, u32[]{:S(2)}, u32[]{:S(2)}) collective-permute-start(bf16[64,2048]{1,0:T(8,128)(2,1)S(1)} %get-tuple-element.221), channel_id=1, source_target_pairs={{0,64},{64,0},{1,65},{65,1},{2,66},{66,2},{3,67},{67,3},{4,68},{68... | collective-permute-start | bytes 786440 | tf_op jit(solution)/shard_map/ppermute | solution.py:506
  503.4 10.6 %collective-permute-start.60 = (bf16[64,256]{1,0:T(8,128)(2,1)S(1)}, bf16[64,256]{1,0:T(8,128)(2,1)S(1)}, u32[]{:S(2)}, u32[]{:S(2)}) collective-permute-start(bf16[64,256]{1,0:T(8,128)(2,1)S(1)} %get-tuple-element.273), channel_id=1, source_target_pairs={{16,0},{20,4},{24,8},{28,12},{32,16},{36,20},{40,24},{44,28},{48,3... | collective-permute-start | bytes 98312 | tf_op jit(solution)/shard_map/ppermute | solution.py:38
  515.5 14.3 %collective-permute-start.63 = (bf16[2,29,16,128]{3,2,1,0:T(8,128)(2,1)S(1)}, bf16[2,29,16,128]{3,2,1,0:T(8,128)(2,1)S(1)}, u32[]{:S(2)}, u32[]{:S(2)}) collective-permute-start(bf16[2,29,16,128]{3,2,1,0:T(8,128)(2,1)S(1)} %get-tuple-element.192), channel_id=1, source_target_pairs={{0,2},{1,3},{2,0},{3,1},{4,6},{5,7},{6,4},{7,5},{8,10},{9,11},{10,... | collective-permute-start | bytes 712712 | tf_op jit(solution)/shard_map/ppermute | solution.py:32
  519.1 10.9 %collective-permute-start.64 = (bf16[2,29,16,128]{3,2,1,0:T(8,128)(2,1)S(1)}, bf16[2,29,16,128]{3,2,1,0:T(8,128)(2,1)S(1)}, u32[]{:S(2)}, u32[]{:S(2)}) collective-permute-start(bf16[2,29,16,128]{3,2,1,0:T(8,128)(2,1)S(1)} %get-tuple-element.191), channel_id=1, source_target_pairs={{0,3},{1,0},{2,1},{3,2},{4,7},{5,4},{6,5},{7,6},{8,11},{9,8},{10,9... | collective-permute-start | bytes 712712 | tf_op jit(solution)/shard_map/ppermute | solution.py:32
  545.0 21.5 %collective-permute-start.61 = (bf16[64,2048]{1,0:T(8,128)(2,1)S(1)}, bf16[64,2048]{1,0:T(8,128)(2,1)S(1)}, u32[]{:S(2)}, u32[]{:S(2)}) collective-permute-start(bf16[64,2048]{1,0:T(8,128)(2,1)S(1)} %select_convert_fusion), channel_id=1, source_target_pairs={{0,64},{64,0},{1,65},{65,1},{2,66},{66,2},{3,67},{67,3},{4,68},{68... | collective-permute-start | bytes 786440 | tf_op jit(solution)/shard_map/ppermute | solution.py:506
  568.5 11.9 %collective-permute-start.79 = (bf16[2,21,16,128]{3,2,1,0:T(8,128)(2,1)S(1)}, bf16[2,21,16,128]{3,2,1,0:T(8,128)(2,1)S(1)}, u32[]{:S(2)}, u32[]{:S(2)}) collective-permute-start(bf16[2,21,16,128]{3,2,1,0:T(8,128)(2,1)S(1)} %get-tuple-element.214), channel_id=1, source_target_pairs={{0,2},{1,3},{2,0},{3,1},{4,6},{5,7},{6,4},{7,5},{8,10},{9,11},{10,... | collective-permute-start | bytes 516104 | tf_op jit(solution)/shard_map/ppermute | solution.py:32
  (186 other events, 2724.8 us)
Sparse Core Ops, SparseCore 0:
  11.6 126.9 all-gather.3
  141.4 71.9 all-gather.5
  216.2 71.9 all-gather.7

commit v9 on v8

--- a/solution.py
+++ b/solution.py
@@ -118,7 +118,7 @@
 
 
 held = pl.BlockSpec(memory_space=pltpu.VMEM)
-remote = pl.BlockSpec(memory_space=pltpu.HBM)
+remote = pl.BlockSpec(memory_space=pl.ANY)
 
 
 def project_queries(layer, normed, table, bias, eq, sq):
@@ -134,7 +134,7 @@
             jax.ShapeDtypeStruct((rows, rank), bf16),
         ],
         scratch_shapes=table_scratch(table, width),
-        compiler_params=pltpu.CompilerParams(vmem_limit_bytes=12 * 2**20),
+        compiler_params=pltpu.CompilerParams(vmem_limit_bytes=28 * 2**20),
         cost_estimate=pl.CostEstimate(
             flops=8 * rows * model * model, bytes_accessed=2 * model * model, transcendentals=0
         ),
@@ -188,7 +188,7 @@
             jax.ShapeDtypeStruct((rows, model), f32),
         ],
         scratch_shapes=table_scratch(table, model // table.shape[0]),
-        compiler_params=pltpu.CompilerParams(vmem_limit_bytes=20 * 2**20),
+        compiler_params=pltpu.CompilerParams(vmem_limit_bytes=36 * 2**20),
         cost_estimate=pl.CostEstimate(
             flops=4 * rows * model * (keys + 2 * model),
             bytes_accessed=2 * model * model,
@@ -274,7 +274,7 @@
             pltpu.VMEM((keys, head), f32),
             pltpu.VMEM((keys, head), f32),
         ],
-        compiler_params=pltpu.CompilerParams(vmem_limit_bytes=30 * 2**20),
+        compiler_params=pltpu.CompilerParams(vmem_limit_bytes=44 * 2**20),
         cost_estimate=pl.CostEstimate(
             flops=8 * rows * model * (keys + 2 * model),
             bytes_accessed=4 * model * model + 4 * groups * 4 * rows * keys,
@@ -313,21 +313,14 @@
     )
 
 
-def gathered(part_refs, whole):
-    rows = part_refs[0].shape[0]
-    for j, part_ref in enumerate(part_refs):
-        whole[j * rows : (j + 1) * rows] = part_ref[...]
-    return whole[...]
-
-
 def feed_pack(pack_ref, model, hidden):
     cuts = [model, 2 * model, 2 * model + hidden, 2 * model + 2 * hidden, 3 * model + 2 * hidden]
     return [pack_ref.at[:, a:b] for a, b in zip(cuts[:-1], cuts[1:])]
 
 
 def feed_kernel(
-    part0, part1, part2, part3, table_ref, bias_ref, pack_ref,
-    active_ref, slope_ref, low_u_ref, low_d_ref, out_ref, buf, sems, whole,
+    second_ref, table_ref, bias_ref, pack_ref,
+    active_ref, slope_ref, low_u_ref, low_d_ref, out_ref, buf, sems,
 ):
     _, count, chunks, rows, tile = buf.shape
     su_ref, eu_ref, sd_ref, ed_ref = feed_pack(pack_ref, chunks * rows, count * tile)
@@ -336,7 +329,7 @@
         up.start()
     for _, down in copies:
         down.start()
-    second = gathered((part0, part1, part2, part3), whole)
+    second = second_ref[...]
     low_u = against(second, su_ref[...]).astype(bf16)
     low_u_ref[...] = low_u
     for j in range(count):
@@ -359,8 +352,8 @@
 
 
 def feed_back_kernel(
-    part0, part1, part2, part3, table_ref, slope_ref, pack_ref,
-    grad_up_ref, inner_d_ref, inner_u_ref, out_ref, buf, sems, whole,
+    branch_ref, table_ref, slope_ref, pack_ref,
+    grad_up_ref, inner_d_ref, inner_u_ref, out_ref, buf, sems,
 ):
     _, count, chunks, rows, tile = buf.shape
     su_ref, eu_ref, sd_ref, ed_ref = feed_pack(pack_ref, chunks * rows, count * tile)
@@ -369,7 +362,7 @@
         down.start()
     for up, _ in copies:
         up.start()
-    branch = gathered((part0, part1, part2, part3), whole)
+    branch = branch_ref[...]
     inner_d = against(branch, ed_ref[...]).astype(bf16)
     inner_d_ref[...] = inner_d
     for j in range(count):
@@ -389,9 +382,9 @@
 
 
 def feed_both_kernel(
-    part0, part1, part2, part3, branch_ref, table_ref, bias_ref, pack_ref,
+    second_ref, branch_ref, table_ref, bias_ref, pack_ref,
     active_ref, low_u_ref, low_d_ref, out_ref, grad_up_ref, inner_d_ref, inner_u_ref, back_ref,
-    buf, sems, whole,
+    buf, sems,
 ):
     _, count, chunks, rows, tile = buf.shape
     su_ref, eu_ref, sd_ref, ed_ref = feed_pack(pack_ref, chunks * rows, count * tile)
@@ -399,7 +392,7 @@
     for up, down in copies:
         up.start()
         down.start()
-    second = gathered((part0, part1, part2, part3), whole)
+    second = second_ref[...]
     branch = branch_ref[...]
     low_u = against(second, su_ref[...]).astype(bf16)
     low_u_ref[...] = low_u
@@ -429,11 +422,9 @@
         ).astype(bf16)
 
 
-def feed_call(kernel, name, parts, inputs, outputs, hidden, matmuls):
-    inputs = tuple(parts) + inputs
+def feed_call(kernel, name, inputs, outputs, hidden, matmuls):
     table = [value for value in inputs if value.ndim == 4][0]
-    model = parts[0].shape[1]
-    rows = sum(part.shape[0] for part in parts)
+    rows, model = inputs[0].shape
     tile = 512
     chunks = table.shape[0]
     return pl.pallas_call(
@@ -444,9 +435,8 @@
         scratch_shapes=[
             pltpu.VMEM((2, hidden // tile, chunks, model // chunks, tile), bf16),
             pltpu.SemaphoreType.DMA((2, hidden // tile)),
-            pltpu.VMEM((rows, model), bf16),
         ],
-        compiler_params=pltpu.CompilerParams(vmem_limit_bytes=26 * 2**20),
+        compiler_params=pltpu.CompilerParams(vmem_limit_bytes=44 * 2**20),
         cost_estimate=pl.CostEstimate(
             flops=2 * matmuls * rows * model * hidden,
             bytes_accessed=4 * model * hidden,
@@ -508,11 +498,9 @@
     def by_layer(own, other):
         return jnp.where(low_section, own, other), jnp.where(low_section, other, own)
 
-    def spread_parts(block):
-        return [block] + [around(block, "tensor", -j) for j in range(1, ranks)]
-
     def spread(block):
-        return jnp.concatenate(spread_parts(block), axis=0)
+        parts = [block] + [around(block, "tensor", -j) for j in range(1, ranks)]
+        return jnp.concatenate(parts, axis=0)
 
     def reduce_rows(partial):
         low = partial.astype(bf16)
@@ -686,7 +674,7 @@
     def feed_inputs(layer, middle):
         gain2, shift2, up_bias = small[layer][4:7]
         unit2, rsd2 = norm_parts(middle)
-        second = spread_parts((unit2 * gain2 + shift2).astype(bf16))
+        second = spread((unit2 * gain2 + shift2).astype(bf16))
         return unit2, rsd2, second, up_bias
 
     def feed_result(layer, middle, partial):
@@ -779,14 +767,7 @@
     def feed_grads(layer, grad, unit2, rsd2, partial):
         return grad + norm_back(unit2, rsd2, reduce_rows(partial) * small[layer][4])
 
-    def feed_adapters(after, second, branch, *others):
-        parts = (after, *second, branch) if not isinstance(branch, list) else (after, *second, *branch)
-        _, *parts = lax.optimization_barrier(parts + others)
-        second = jnp.concatenate(parts[:ranks], axis=0)
-        parts = parts[ranks:]
-        count = len(parts) - len(others)
-        branch = jnp.concatenate(parts[:count], axis=0)
-        low_u, low_d, inner_u, inner_d, active, grad_up = parts[count:]
+    def feed_adapters(second, branch, low_u, low_d, inner_u, inner_d, active, grad_up):
         shared = [across(inner_u, second), across(low_d, branch)]
         owned = [across(low_u, grad_up), across(inner_d, active)]
         return shared, owned
@@ -830,8 +811,7 @@
     active_zero, slope_zero, low_u_zero, low_d_zero, partial = feed_call(
         feed_kernel,
         "feed",
-        second_zero,
-        (feed_tables[0], up_bias, late_layers[0]),
+        (second_zero, feed_tables[0], up_bias, late_layers[0]),
         (local_f, local_f, rank, rank, width),
         local_f,
         2,
@@ -844,34 +824,31 @@
     active, low_u, low_d, partial, grad_up, inner_d, inner_u, partial_back = feed_call(
         feed_both_kernel,
         "feed_both",
-        second_one,
-        (branch_one, feed_tables[1], up_bias, late_layers[1]),
+        (second_one, branch_one, feed_tables[1], up_bias, late_layers[1]),
         (local_f, rank, rank, width, local_f, rank, rank, width),
         local_f,
         4,
     )
     grad_middle = feed_grads(1, given, unit_one, rsd_one, partial_back)
     shared, owned = feed_adapters(
-        grad_middle, second_one, branch_one, low_u, low_d, inner_u, inner_d, active, grad_up
+        second_one, branch_one, low_u, low_d, inner_u, inner_d, active, grad_up
     )
     grad_one, more, quartered = backward_attend(1, kept_one, grad_middle)
     layer_one = (shared + more, quartered, owned)
     partial, _ = lax.optimization_barrier((partial, grad_middle))
     final = feed_result(1, middle_one, partial).astype(bf16)
 
-    branch_zero = spread_parts(grad_one.astype(bf16))
+    branch_zero = spread(grad_one.astype(bf16))
     grad_up, inner_d, inner_u, partial_back = feed_call(
         feed_back_kernel,
         "feed_back",
-        branch_zero,
-        (feed_tables[0], slope_zero, late_layers[0]),
+        (branch_zero, feed_tables[0], slope_zero, late_layers[0]),
         (local_f, rank, rank, width),
         local_f,
         2,
     )
     grad_middle_zero = feed_grads(0, grad_one, unit_zero, rsd_zero, partial_back)
     shared, owned = feed_adapters(
-        grad_middle_zero,
         second_zero,
         branch_zero,
         low_u_zero,

time: 603 us -> 549 us (0.910)
  local copies, waits for them, and re-layouts: 90.4 us -> 36.4 us
  waiting for transfers between devices: 218 us -> 232 us
  Pallas kernels: 93.8 us -> 85.8 us
    unnamed x346 -> x312, local copies, waits for them, and re-layouts: 65.2 us -> 17.7 us
    ppermute x45, waiting for transfers between devices: 93.8 us -> 108 us  [around(): lax.ppermute(block, axis, [(i, (i + distance) % size) for i in range(size)])]
    pallas_call x3, Pallas kernels: 43.2 us -> 35.2 us  [feed_call(): pl.pallas_call(kernel, in_specs=[remote if value.ndim == 4 else held for...]
  transfers between devices with their start and end apart: 84 -> 84, of which waited for: 42 -> 52; matrix products, arithmetic and copies ran while one was open for 10% -> 10% of each run, Pallas kernels for 9% -> 7%
where the time goes in v9:
time: 549 us; the launch traced here: 540 us
  waiting for transfers between devices  232 us (42%)
  starting transfers between devices  129 us (23%)
  Pallas kernels  85.8 us (16%)
  local copies, waits for them, and re-layouts  36.4 us (7%)
  other arithmetic  27.8 us (5%)
  between operations  21 us (4%)
  matrix products  8.34 us (2%)
    ppermute x45, waiting for transfers between devices, around(): lax.ppermute(block, axis, [(i, (i + distance) % size) for i in range(size)])  108 us
    ppermute x45, starting transfers between devices, around(): lax.ppermute(block, axis, [(i, (i + distance) % size) for i in range(size)])  65.1 us
    all_gather x1, waiting for transfers between devices, gather_all(): lax.all_gather(row_major(shard), every, axis=0, tiled=True, axis_index_gr...  56.1 us
    pallas_call x3, Pallas kernels, feed_call(): pl.pallas_call(kernel, in_specs=[remote if value.ndim == 4 else held for...  35.2 us
    ppermute x16, starting transfers between devices, along(): return lax.ppermute(block, axis, route)  32.1 us
    ppermute x7, waiting for transfers between devices, swap(): return lax.ppermute(value, 'section', sides)  26.3 us
    pallas_call x2, Pallas kernels, attend_back(): pl.pallas_call(lambda *refs: attend_back_kernel(layer, head, *refs), in_s...  23 us
    pallas_call x2, Pallas kernels, attend(): pl.pallas_call(lambda *refs: attend_kernel(layer, head, *refs), in_specs=...  18.9 us
  transfers between devices with their start and end apart: 84, of which 52 were waited for; matrix products, arithmetic and copies ran while one was open for 10% of the time, Pallas kernels for 7%

profile of v9, /device:TPU:0, one launch (start us, length us, event | category | flops | bytes accessed | tf_op | source)
XLA Modules:
  0.0 539.8 jit_solution(3356543484852506953)
XLA Ops:
  12.3 4.0 collective-permute-start.17
  16.4 12.2 %collective-permute-done.17 = bf16[128,2048]{1,0:T(8,128)(2,1)S(1)} collective-permute-done((bf16[128,2048]{1,0:T(8,128)(2,1)S(1)}, bf16[128,2048]{1,0:T(8,128)(2,1)S(1)}, u32[]{:S(2)}, u32[]{:S(2)}) %collective-permute-start.17) | collective-permute-done | bytes 524320 | tf_op jit(solution)/shard_map/ppermute | solution.py:496
  43.0 4.0 collective-permute-start.13
  49.1 3.6 collective-permute-start
  55.9 14.1 %collective-permute-done = bf16[1,14592]{1,0:T(2,128)(2,1)S(1)} collective-permute-done((bf16[1,14592]{1,0:T(2,128)(2,1)S(1)}, bf16[1,14592]{1,0:T(2,128)(2,1)S(1)}, u32[]{:S(2)}, u32[]{:S(2)}) %collective-permute-start) | collective-permute-done | bytes 29216 | tf_op jit(solution)/shard_map/ppermute | solution.py:496
  82.5 56.1 %all-gather.4.cloned.1.call-done = bf16[16384,1152]{1,0:T(8,128)(2,1)} async-done(((bf16[128,1152]{1,0:T(8,128)(2,1)}), bf16[16384,1152]{1,0:T(8,128)(2,1)}) %all-gather.4.cloned.1.call-update) | async-done | bytes 37748752 | tf_op jit(solution)/shard_map/all_gather | solution.py:534
  141.9 3.4 collective-permute-start.6
  148.7 4.1 collective-permute-start.8
  158.5 4.4 project_queries.2
  166.2 5.3 collective-permute-done.12
  171.5 9.4 %attend.2 = (bf16[4,256,1280]{2,1,0:T(8,128)(2,1)S(1)}, bf16[64,2048]{1,0:T(8,128)(2,1)S(1)}, bf16[64,16]{1,0:T(8,128)(2,1)S(1)}, f32[64,2048]{1,0:T(8,128)S(1)}) custom-call(bf16[64,2048]{1,0:T(8,128)(2,1)S(1)} %get-tuple-element.54.refs_0_.refs_5_, bf16[1280,256]{1,0:T(8,128)(2,1)S(1)} %constant_dynamic-update-slice_fusion.18.refs_1_.refs_6_, ...), custom_call_target="tpu_custom_call" | custom-call | flops 2818572288 | bytes 8388608 | tf_op jit(solution)/shard_map/attend/pallas_call | solution.py:180
  188.7 5.7 %collective-permute-done.14 = bf16[64,2048]{1,0:T(8,128)(2,1)S(1)} collective-permute-done((bf16[64,2048]{1,0:T(8,128)(2,1)S(1)}, bf16[64,2048]{1,0:T(8,128)(2,1)S(1)}, u32[]{:S(2)}, u32[]{:S(2)}) %collective-permute-start.14) | collective-permute-done | bytes 262176 | tf_op jit(solution)/shard_map/ppermute | solution.py:32
  194.5 4.7 collective-permute-done.16
  199.3 14.1 %all-gather.6.cloned.1.call-done = bf16[4096,2048]{1,0:T(8,128)(2,1)} async-done(((bf16[128,2048]{1,0:T(8,128)(2,1)}), bf16[4096,2048]{1,0:T(8,128)(2,1)}) %all-gather.6.cloned.1.call-update) | async-done | bytes 16777232 | tf_op jit(solution)/shard_map/all_gather | solution.py:530
  213.4 10.8 %feed.1 = (bf16[256,2048]{1,0:T(8,128)(2,1)S(1)}, bf16[256,2048]{1,0:T(8,128)(2,1)S(1)}, bf16[256,16]{1,0:T(8,128)(2,1)S(1)}, bf16[256,16]{1,0:T(8,128)(2,1)S(1)}, bf16[256,2048]{1,0:T(8,128)(2,1)S(1)}) custom-call(bf16[256,2048]{1,0:T(8,128)(2,1)S(1)} %pad_maximum_fusion.1.second_ref, bf16[4,2,512,2048]{3,2,1,0:T(8,128)(2,1)} %bitcast.734, ...), custom_call_target="tpu_custom_call" | custom-call | flops 4294967296 | bytes 16777216 | tf_op jit(solution)/shard_map/feed/pallas_call | solution.py:430
  230.7 3.4 collective-permute-done.18
  235.1 6.3 %collective-permute-done.19 = bf16[64,2048]{1,0:T(8,128)(2,1)S(1)} collective-permute-done((bf16[64,2048]{1,0:T(8,128)(2,1)S(1)}, bf16[64,2048]{1,0:T(8,128)(2,1)S(1)}, u32[]{:S(2)}, u32[]{:S(2)}) %collective-permute-start.19) | collective-permute-done | bytes 262176 | tf_op jit(solution)/shard_map/ppermute | solution.py:32
  243.2 3.4 collective-permute-start.21
  248.3 3.6 collective-permute-start.23
  257.8 4.4 project_queries.3
  265.0 4.3 collective-permute-done.27
  269.3 9.5 %attend.3 = (bf16[4,256,1280]{2,1,0:T(8,128)(2,1)S(1)}, bf16[64,2048]{1,0:T(8,128)(2,1)S(1)}, bf16[64,16]{1,0:T(8,128)(2,1)S(1)}, f32[64,2048]{1,0:T(8,128)S(1)}) custom-call(bf16[64,2048]{1,0:T(8,128)(2,1)S(1)} %get-tuple-element.57.refs_0_.refs_5_, bf16[1280,256]{1,0:T(8,128)(2,1)S(1)} %constant_dynamic-update-slice_fusion.41.refs_1_.refs_6_, ...), custom_call_target="tpu_custom_call" | custom-call | flops 2818572288 | bytes 8388608 | tf_op jit(solution)/shard_map/attend/pallas_call | solution.py:180
  289.6 3.8 collective-permute-done.29
  293.4 7.2 %collective-permute-done.30 = bf16[64,2048]{1,0:T(8,128)(2,1)} collective-permute-done((bf16[64,2048]{1,0:T(8,128)(2,1)S(1)}, bf16[64,2048]{1,0:T(8,128)(2,1)}, u32[]{:S(2)}, u32[]{:S(2)}) %collective-permute-start.30) | collective-permute-done | bytes 262176 | tf_op jit(solution)/shard_map/ppermute | solution.py:32
  303.5 14.4 %feed_both.1 = (bf16[256,2048]{1,0:T(8,128)(2,1)S(1)}, bf16[256,16]{1,0:T(8,128)(2,1)S(1)}, bf16[256,16]{1,0:T(8,128)(2,1)S(1)}, bf16[256,2048]{1,0:T(8,128)(2,1...) custom-call(bf16[256,2048]{1,0:T(8,128)(2,1)S(1)} %pad_maximum_fusio, ...), custom_call_target="tpu_custom_call" | custom-call | flops 8589934592 | bytes 16777216 | tf_op jit(solution)/shard_map/feed_both/pallas_call | solution.py:430
  325.7 9.4 %collective-permute-done.34 = bf16[64,2048]{1,0:T(8,128)(2,1)S(1)} collective-permute-done((bf16[64,2048]{1,0:T(8,128)(2,1)S(1)}, bf16[64,2048]{1,0:T(8,128)(2,1)S(1)}, u32[]{:S(2)}, u32[]{:S(2)}) %collective-permute-start.34) | collective-permute-done | bytes 262176 | tf_op jit(solution)/shard_map/ppermute | solution.py:32
  336.5 11.5 %attend_back.2 = (bf16[64,2048]{1,0:T(8,128)(2,1)S(1)}, bf16[1280,256]{1,0:T(8,128)(2,1)S(1)}, bf16[64,16]{1,0:T(8,128)(2,1)S(1)}, bf16[64,16]{1,0:T(8,128)(2,1)S(1)}, f32[64,2048]{1,0:T(8,128)S(1)}) custom-call(bf16[64,2048]{1,0:T(8,128)(2,1)S(1)} %get-tuple-element.113.refs_0_, bf16[4,4,2,512,1152]{4,3,2,1,0:T(8,128)(2,1)} %bitcast.732, ...), custom_call_target="tpu_custom_call" | custom-call | flops 5637144576 | bytes 22020096 | tf_op jit(solution)/shard_map/attend_back/pallas_call | solution.py:259
  348.6 3.6 collective-permute-start.41
  355.1 4.7 collective-permute-done.41
  367.9 3.6 collective-permute-start.38
  378.9 3.5 concatenate.208
  387.1 3.6 collective-permute-done.47
  390.8 5.0 collective-permute-done.49
  397.0 10.0 %feed_back.1 = (bf16[256,2048]{1,0:T(8,128)(2,1)S(1)}, bf16[256,16]{1,0:T(8,128)(2,1)S(1)}, bf16[256,16]{1,0:T(8,128)(2,1)S(1)}, bf16[256,2048]{1,0:T(8,128)(2,1)S(1)}) custom-call(bf16[256,2048]{1,0:T(8,128)(2,1)S(1)} %pad_maximum_fusion.5.branch_ref, bf16[4,2,512,2048]{3,2,1,0:T(8,128)(2,1)} %bitcast.735, bf16[256,2048]{1,0:T(8,128)(2,1)S(1)} %copy-done.17, ...), custom_call_target="tpu_custom_call" | custom-call | flops 4294967296 | bytes 16777216 | tf_op jit(solution)/shard_map/feed_back/pallas_call | solution.py:430
  407.6 4.2 collective-permute-start.51
  413.4 3.3 collective-permute-done.50
  416.7 6.8 %collective-permute-done.51 = bf16[64,2048]{1,0:T(8,128)(2,1)S(1)} collective-permute-done((bf16[64,2048]{1,0:T(8,128)(2,1)S(1)}, bf16[64,2048]{1,0:T(8,128)(2,1)S(1)}, u32[]{:S(2)}, u32[]{:S(2)}) %collective-permute-start.51) | collective-permute-done | bytes 262176 | tf_op jit(solution)/shard_map/ppermute | solution.py:32
  424.4 11.5 %attend_back.3 = (bf16[64,2048]{1,0:T(8,128)(2,1)S(1)}, bf16[1280,256]{1,0:T(8,128)(2,1)S(1)}, bf16[64,16]{1,0:T(8,128)(2,1)S(1)}, bf16[64,16]{1,0:T(8,128)(2,1)S(1)}, f32[64,2048]{1,0:T(8,128)S(1)}) custom-call(bf16[64,2048]{1,0:T(8,128)(2,1)S(1)} %get-tuple-element.106.refs_0_, bf16[4,4,2,512,1152]{4,3,2,1,0:T(8,128)(2,1)} %bitcast.733, ...), custom_call_target="tpu_custom_call" | custom-call | flops 5637144576 | bytes 22020096 | tf_op jit(solution)/shard_map/attend_back/pallas_call | solution.py:259
  436.1 3.6 collective-permute-start.55
  442.6 4.7 collective-permute-done.55
  457.7 4.1 collective-permute-done.60
  463.2 3.6 collective-permute-start.63
  467.4 5.3 collective-permute-done.62
  472.7 4.8 collective-permute-done.63
  480.3 4.2 collective-permute-done.66
  486.5 3.2 collective-permute-start.68
  515.7 3.9 collective-permute-start.79
  523.1 4.5 collective-permute-done.79
  (670 shorter events, 180.0 us)
Async XLA Ops:
  7.2 131.4 %all-gather.4.cloned.1.call-start = ((), (), s32[]{:S(2)}) async-start(), calls=%async_computation | async-start | bytes 38043648 | tf_op jit(solution)/shard_map/all_gather | solution.py:534
  10.8 202.6 %all-gather.6.cloned.1.call-start = ((), (), s32[]{:S(2)}) async-start(), calls=%async_computation.1 | async-start | bytes 17301504 | tf_op jit(solution)/shard_map/all_gather | solution.py:530
  12.3 16.3 %collective-permute-start.17 = (bf16[128,2048]{1,0:T(8,128)(2,1)S(1)}, bf16[128,2048]{1,0:T(8,128)(2,1)S(1)}, u32[]{:S(2)}, u32[]{:S(2)}) collective-permute-start(bf16[128,2048]{1,0:T(8,128)(2,1)S(1)} %broadcast_select_fusion.2), channel_id=1, source_target_pairs={{0,64},{64,0},{1,65},{65,1},{2,66},{66,2},{3,67},{67,3},{4,68},{68... | collective-permute-start | bytes 1572872 | tf_op jit(solution)/shard_map/ppermute | solution.py:496
  30.0 271.8 %all-gather.8.cloned.1.call-start = ((), (), s32[]{:S(2)}) async-start(), calls=%async_computation.2 | async-start | bytes 17301504 | tf_op jit(solution)/shard_map/all_gather | solution.py:530
  43.0 102.3 %collective-permute-start.13 = (bf16[16,10240]{1,0:T(8,128)(2,1)}, bf16[16,10240]{1,0:T(8,128)(2,1)}, u32[]{:S(2)}, u32[]{:S(2)}) collective-permute-start(bf16[16,10240]{1,0:T(8,128)(2,1)} %get-tuple-element.180), channel_id=1, source_target_pairs={{0,64},{64,0},{1,65},{65,1},{2,66},{66,2},{3,67},{67,3},{4,68},{68... | collective-permute-start | bytes 983048 | tf_op jit(solution)/shard_map/ppermute | solution.py:496
  48.8 28.7 %collective-permute-start.5 = (bf16[16,4352]{1,0:T(8,128)(2,1)S(1)}, bf16[16,4352]{1,0:T(8,128)(2,1)S(1)}, u32[]{:S(2)}, u32[]{:S(2)}) collective-permute-start(bf16[16,4352]{1,0:T(8,128)(2,1)S(1)} %pad_maximum_fusion.18), channel_id=1, source_target_pairs={{0,64},{64,0},{1,65},{65,1},{2,66},{66,2},{3,67},{67,3},{4,68},{68... | collective-permute-start | bytes 417800 | tf_op jit(solution)/shard_map/ppermute | solution.py:496
  49.1 20.8 %collective-permute-start = (bf16[1,14592]{1,0:T(2,128)(2,1)S(1)}, bf16[1,14592]{1,0:T(2,128)(2,1)S(1)}, u32[]{:S(2)}, u32[]{:S(2)}) collective-permute-start(bf16[1,14592]{1,0:T(2,128)(2,1)S(1)} %constant_dynamic-update-slice_fusion), channel_id=1, source_target_pairs={{0,64},{64,0},{1,65},{65,1},{2,66},{66,2},{3,67},{67,3},{4,68},{68... | collective-permute-start | bytes 87560 | tf_op jit(solution)/shard_map/ppermute | solution.py:496
  54.4 17.1 %collective-permute-start.1 = (bf16[16,1536]{1,0:T(8,128)(2,1)S(1)}, bf16[16,1536]{1,0:T(8,128)(2,1)S(1)}, u32[]{:S(2)}, u32[]{:S(2)}) collective-permute-start(bf16[16,1536]{1,0:T(8,128)(2,1)S(1)} %maximum_maximum_fusion.2), channel_id=1, source_target_pairs={{0,64},{64,0},{1,65},{65,1},{2,66},{66,2},{3,67},{67,3},{4,68},{68... | collective-permute-start | bytes 147464 | tf_op jit(solution)/shard_map/ppermute | solution.py:496
  141.9 12.3 %collective-permute-start.6 = (bf16[64,256]{1,0:T(8,128)(2,1)S(1)}, bf16[64,256]{1,0:T(8,128)(2,1)S(1)}, u32[]{:S(2)}, u32[]{:S(2)}) collective-permute-start(bf16[64,256]{1,0:T(8,128)(2,1)S(1)} %fusion.20), channel_id=1, source_target_pairs={{0,16},{4,20},{8,24},{12,28},{16,32},{20,36},{24,40},{28,44},{32,4... | collective-permute-start | bytes 98312 | tf_op jit(solution)/shard_map/ppermute | solution.py:38
  155.1 10.3 %collective-permute-start.10 = (bf16[320,256]{1,0:T(8,128)(2,1)S(1)}, bf16[320,256]{1,0:T(8,128)(2,1)S(1)}, u32[]{:S(2)}, u32[]{:S(2)}) collective-permute-start(bf16[320,256]{1,0:T(8,128)(2,1)S(1)} %get-tuple-element.277), channel_id=1, source_target_pairs={{0,3},{1,0},{2,1},{3,2},{4,7},{5,4},{6,5},{7,6},{8,11},{9,8},{10,9... | collective-permute-start | bytes 491528 | tf_op jit(solution)/shard_map/ppermute | solution.py:32
  157.6 8.5 %collective-permute-start.11 = (bf16[320,256]{1,0:T(8,128)(2,1)S(1)}, bf16[320,256]{1,0:T(8,128)(2,1)S(1)}, u32[]{:S(2)}, u32[]{:S(2)}) collective-permute-start(bf16[320,256]{1,0:T(8,128)(2,1)S(1)} %get-tuple-element.277), channel_id=1, source_target_pairs={{0,2},{1,3},{2,0},{3,1},{4,6},{5,7},{6,4},{7,5},{8,10},{9,11},{10,... | collective-permute-start | bytes 491528 | tf_op jit(solution)/shard_map/ppermute | solution.py:32
  162.9 8.6 %collective-permute-start.12 = (bf16[320,256]{1,0:T(8,128)(2,1)S(1)}, bf16[320,256]{1,0:T(8,128)(2,1)S(1)}, u32[]{:S(2)}, u32[]{:S(2)}) collective-permute-start(bf16[320,256]{1,0:T(8,128)(2,1)S(1)} %get-tuple-element.277), channel_id=1, source_target_pairs={{0,1},{1,2},{2,3},{3,0},{4,5},{5,6},{6,7},{7,4},{8,9},{9,10},{10,1... | collective-permute-start | bytes 491528 | tf_op jit(solution)/shard_map/ppermute | solution.py:32
  181.6 12.8 %collective-permute-start.14 = (bf16[64,2048]{1,0:T(8,128)(2,1)S(1)}, bf16[64,2048]{1,0:T(8,128)(2,1)S(1)}, u32[]{:S(2)}, u32[]{:S(2)}) collective-permute-start(bf16[64,2048]{1,0:T(8,128)(2,1)S(1)} %add_convert_fusion.3), channel_id=1, source_target_pairs={{0,3},{1,0},{2,1},{3,2},{4,7},{5,4},{6,5},{7,6},{8,11},{9,8},{10,9... | collective-permute-start | bytes 786440 | tf_op jit(solution)/shard_map/ppermute | solution.py:32
  182.9 11.6 %collective-permute-start.15 = (bf16[64,2048]{1,0:T(8,128)(2,1)S(1)}, bf16[64,2048]{1,0:T(8,128)(2,1)S(1)}, u32[]{:S(2)}, u32[]{:S(2)}) collective-permute-start(bf16[64,2048]{1,0:T(8,128)(2,1)S(1)} %add_convert_fusion.3), channel_id=1, source_target_pairs={{0,2},{1,3},{2,0},{3,1},{4,6},{5,7},{6,4},{7,5},{8,10},{9,11},{10,... | collective-permute-start | bytes 786440 | tf_op jit(solution)/shard_map/ppermute | solution.py:32
  184.6 14.6 %collective-permute-start.16 = (bf16[64,2048]{1,0:T(8,128)(2,1)S(1)}, bf16[64,2048]{1,0:T(8,128)(2,1)S(1)}, u32[]{:S(2)}, u32[]{:S(2)}) collective-permute-start(bf16[64,2048]{1,0:T(8,128)(2,1)S(1)} %add_convert_fusion.3), channel_id=1, source_target_pairs={{0,1},{1,2},{2,3},{3,0},{4,5},{5,6},{6,7},{7,4},{8,9},{9,10},{10,1... | collective-permute-start | bytes 786440 | tf_op jit(solution)/shard_map/ppermute | solution.py:32
  185.8 99.6 %collective-permute-start.31 = (bf16[64,2048]{1,0:T(8,128)(2,1)S(1)}, bf16[64,2048]{1,0:T(8,128)(2,1)}, u32[]{:S(2)}, u32[]{:S(2)}) collective-permute-start(bf16[64,2048]{1,0:T(8,128)(2,1)S(1)} %dynamic-slice_bitcast_fusion), channel_id=1, source_target_pairs={{0,3},{1,0},{2,1},{3,2},{4,7},{5,4},{6,5},{7,6},{8,11},{9,8},{10,9... | collective-permute-start | bytes 786440 | tf_op jit(solution)/shard_map/ppermute | solution.py:32
  187.9 99.4 %collective-permute-start.32 = (bf16[64,2048]{1,0:T(8,128)(2,1)S(1)}, bf16[64,2048]{1,0:T(8,128)(2,1)}, u32[]{:S(2)}, u32[]{:S(2)}) collective-permute-start(bf16[64,2048]{1,0:T(8,128)(2,1)S(1)} %dynamic-slice_bitcast_fusion), channel_id=1, source_target_pairs={{0,2},{1,3},{2,0},{3,1},{4,6},{5,7},{6,4},{7,5},{8,10},{9,11},{10,... | collective-permute-start | bytes 786440 | tf_op jit(solution)/shard_map/ppermute | solution.py:32
  224.4 9.7 %collective-permute-start.18 = (bf16[64,2048]{1,0:T(8,128)(2,1)S(1)}, bf16[64,2048]{1,0:T(8,128)(2,1)S(1)}, u32[]{:S(2)}, u32[]{:S(2)}) collective-permute-start(bf16[64,2048]{1,0:T(8,128)(2,1)S(1)} %get-tuple-element.137), channel_id=1, source_target_pairs={{0,1},{1,2},{2,3},{3,0},{4,5},{5,6},{6,7},{7,4},{8,9},{9,10},{10,1... | collective-permute-start | bytes 786440 | tf_op jit(solution)/shard_map/ppermute | solution.py:32
  225.9 15.4 %collective-permute-start.19 = (bf16[64,2048]{1,0:T(8,128)(2,1)S(1)}, bf16[64,2048]{1,0:T(8,128)(2,1)S(1)}, u32[]{:S(2)}, u32[]{:S(2)}) collective-permute-start(bf16[64,2048]{1,0:T(8,128)(2,1)S(1)} %get-tuple-element.139), channel_id=1, source_target_pairs={{0,2},{1,3},{2,0},{3,1},{4,6},{5,7},{6,4},{7,5},{8,10},{9,11},{10,... | collective-permute-start | bytes 786440 | tf_op jit(solution)/shard_map/ppermute | solution.py:32
  228.6 12.8 %collective-permute-start.20 = (bf16[64,2048]{1,0:T(8,128)(2,1)S(1)}, bf16[64,2048]{1,0:T(8,128)(2,1)S(1)}, u32[]{:S(2)}, u32[]{:S(2)}) collective-permute-start(bf16[64,2048]{1,0:T(8,128)(2,1)S(1)} %get-tuple-element.138), channel_id=1, source_target_pairs={{0,3},{1,0},{2,1},{3,2},{4,7},{5,4},{6,5},{7,6},{8,11},{9,8},{10,9... | collective-permute-start | bytes 786440 | tf_op jit(solution)/shard_map/ppermute | solution.py:32
  234.1 53.2 %collective-permute-start.33 = (bf16[64,2048]{1,0:T(8,128)(2,1)S(1)}, bf16[64,2048]{1,0:T(8,128)(2,1)}, u32[]{:S(2)}, u32[]{:S(2)}) collective-permute-start(bf16[64,2048]{1,0:T(8,128)(2,1)S(1)} %dynamic-slice_bitcast_fusion), channel_id=1, source_target_pairs={{0,1},{1,2},{2,3},{3,0},{4,5},{5,6},{6,7},{7,4},{8,9},{9,10},{10,1... | collective-permute-start | bytes 786440 | tf_op jit(solution)/shard_map/ppermute | solution.py:32
  284.2 9.2 %collective-permute-start.29 = (bf16[64,2048]{1,0:T(8,128)(2,1)S(1)}, bf16[64,2048]{1,0:T(8,128)(2,1)}, u32[]{:S(2)}, u32[]{:S(2)}) collective-permute-start(bf16[64,2048]{1,0:T(8,128)(2,1)S(1)} %add_convert_fusion.1), channel_id=1, source_target_pairs={{0,2},{1,3},{2,0},{3,1},{4,6},{5,7},{6,4},{7,5},{8,10},{9,11},{10,... | collective-permute-start | bytes 786440 | tf_op jit(solution)/shard_map/ppermute | solution.py:32
  285.4 15.2 %collective-permute-start.30 = (bf16[64,2048]{1,0:T(8,128)(2,1)S(1)}, bf16[64,2048]{1,0:T(8,128)(2,1)}, u32[]{:S(2)}, u32[]{:S(2)}) collective-permute-start(bf16[64,2048]{1,0:T(8,128)(2,1)S(1)} %add_convert_fusion.1), channel_id=1, source_target_pairs={{0,1},{1,2},{2,3},{3,0},{4,5},{5,6},{6,7},{7,4},{8,9},{9,10},{10,1... | collective-permute-start | bytes 786440 | tf_op jit(solution)/shard_map/ppermute | solution.py:32
  319.9 15.2 %collective-permute-start.34 = (bf16[64,2048]{1,0:T(8,128)(2,1)S(1)}, bf16[64,2048]{1,0:T(8,128)(2,1)S(1)}, u32[]{:S(2)}, u32[]{:S(2)}) collective-permute-start(bf16[64,2048]{1,0:T(8,128)(2,1)S(1)} %get-tuple-element.134), channel_id=1, source_target_pairs={{0,1},{1,2},{2,3},{3,0},{4,5},{5,6},{6,7},{7,4},{8,9},{9,10},{10,1... | collective-permute-start | bytes 786440 | tf_op jit(solution)/shard_map/ppermute | solution.py:32
  320.0 15.1 %collective-permute-start.35 = (bf16[64,2048]{1,0:T(8,128)(2,1)S(1)}, bf16[64,2048]{1,0:T(8,128)(2,1)S(1)}, u32[]{:S(2)}, u32[]{:S(2)}) collective-permute-start(bf16[64,2048]{1,0:T(8,128)(2,1)S(1)} %get-tuple-element.136), channel_id=1, source_target_pairs={{0,2},{1,3},{2,0},{3,1},{4,6},{5,7},{6,4},{7,5},{8,10},{9,11},{10,... | collective-permute-start | bytes 786440 | tf_op jit(solution)/shard_map/ppermute | solution.py:32
  321.2 14.6 %collective-permute-start.36 = (bf16[64,2048]{1,0:T(8,128)(2,1)S(1)}, bf16[64,2048]{1,0:T(8,128)(2,1)S(1)}, u32[]{:S(2)}, u32[]{:S(2)}) collective-permute-start(bf16[64,2048]{1,0:T(8,128)(2,1)S(1)} %get-tuple-element.135), channel_id=1, source_target_pairs={{0,3},{1,0},{2,1},{3,2},{4,7},{5,4},{6,5},{7,6},{8,11},{9,8},{10,9... | collective-permute-start | bytes 786440 | tf_op jit(solution)/shard_map/ppermute | solution.py:32
  348.6 11.2 %collective-permute-start.41 = (bf16[320,256]{1,0:T(8,128)(2,1)S(1)}, bf16[320,256]{1,0:T(8,128)(2,1)S(1)}, u32[]{:S(2)}, u32[]{:S(2)}) collective-permute-start(bf16[320,256]{1,0:T(8,128)(2,1)S(1)} %get-tuple-element.152), channel_id=1, source_target_pairs={{0,2},{1,3},{2,0},{3,1},{4,6},{5,7},{6,4},{7,5},{8,10},{9,11},{10,... | collective-permute-start | bytes 491528 | tf_op jit(solution)/shard_map/ppermute | solution.py:32
  361.2 10.3 %collective-permute-start.44 = (bf16[64,256]{1,0:T(8,128)(2,1)S(1)}, bf16[64,256]{1,0:T(8,128)(2,1)S(1)}, u32[]{:S(2)}, u32[]{:S(2)}) collective-permute-start(bf16[64,256]{1,0:T(8,128)(2,1)S(1)} %get-tuple-element.229), channel_id=1, source_target_pairs={{8,0},{12,4},{16,8},{20,12},{24,16},{28,20},{32,24},{36,28},{40,32... | collective-permute-start | bytes 98312 | tf_op jit(solution)/shard_map/ppermute | solution.py:38
  362.5 9.0 %collective-permute-start.45 = (bf16[64,256]{1,0:T(8,128)(2,1)S(1)}, bf16[64,256]{1,0:T(8,128)(2,1)S(1)}, u32[]{:S(2)}, u32[]{:S(2)}) collective-permute-start(bf16[64,256]{1,0:T(8,128)(2,1)S(1)} %get-tuple-element.228), channel_id=1, source_target_pairs={{12,0},{16,4},{20,8},{24,12},{28,16},{32,20},{36,24},{40,28},{44,3... | collective-permute-start | bytes 98312 | tf_op jit(solution)/shard_map/ppermute | solution.py:38
  363.8 8.3 %collective-permute-start.46 = (bf16[64,256]{1,0:T(8,128)(2,1)S(1)}, bf16[64,256]{1,0:T(8,128)(2,1)S(1)}, u32[]{:S(2)}, u32[]{:S(2)}) collective-permute-start(bf16[64,256]{1,0:T(8,128)(2,1)S(1)} %get-tuple-element.227), channel_id=1, source_target_pairs={{16,0},{20,4},{24,8},{28,12},{32,16},{36,20},{40,24},{44,28},{48,3... | collective-permute-start | bytes 98312 | tf_op jit(solution)/shard_map/ppermute | solution.py:38
  367.9 14.6 %collective-permute-start.37 = (bf16[64,2048]{1,0:T(8,128)(2,1)}, bf16[64,2048]{1,0:T(8,128)(2,1)}, u32[]{:S(2)}, u32[]{:S(2)}) collective-permute-start(bf16[64,2048]{1,0:T(8,128)(2,1)} %get-tuple-element.131), channel_id=1, source_target_pairs={{0,1},{1,2},{2,3},{3,0},{4,5},{5,6},{6,7},{7,4},{8,9},{9,10},{10,1... | collective-permute-start | bytes 786440 | tf_op jit(solution)/shard_map/ppermute | solution.py:32
  367.9 16.5 %collective-permute-start.38 = (bf16[64,2048]{1,0:T(8,128)(2,1)}, bf16[64,2048]{1,0:T(8,128)(2,1)}, u32[]{:S(2)}, u32[]{:S(2)}) collective-permute-start(bf16[64,2048]{1,0:T(8,128)(2,1)} %get-tuple-element.133), channel_id=1, source_target_pairs={{0,2},{1,3},{2,0},{3,1},{4,6},{5,7},{6,4},{7,5},{8,10},{9,11},{10,... | collective-permute-start | bytes 786440 | tf_op jit(solution)/shard_map/ppermute | solution.py:32
  371.5 13.5 %collective-permute-start.39 = (bf16[64,2048]{1,0:T(8,128)(2,1)}, bf16[64,2048]{1,0:T(8,128)(2,1)S(1)}, u32[]{:S(2)}, u32[]{:S(2)}) collective-permute-start(bf16[64,2048]{1,0:T(8,128)(2,1)} %get-tuple-element.132), channel_id=1, source_target_pairs={{0,3},{1,0},{2,1},{3,2},{4,7},{5,4},{6,5},{7,6},{8,11},{9,8},{10,9... | collective-permute-start | bytes 786440 | tf_op jit(solution)/shard_map/ppermute | solution.py:32
  374.2 16.6 %collective-permute-start.47 = (bf16[64,2048]{1,0:T(8,128)(2,1)}, bf16[64,2048]{1,0:T(8,128)(2,1)}, u32[]{:S(2)}, u32[]{:S(2)}) collective-permute-start(bf16[64,2048]{1,0:T(8,128)(2,1)} %get-tuple-element.109), channel_id=1, source_target_pairs={{0,3},{1,0},{2,1},{3,2},{4,7},{5,4},{6,5},{7,6},{8,11},{9,8},{10,9... | collective-permute-start | bytes 786440 | tf_op jit(solution)/shard_map/ppermute | solution.py:32
  376.8 13.9 %collective-permute-start.48 = (bf16[64,2048]{1,0:T(8,128)(2,1)}, bf16[64,2048]{1,0:T(8,128)(2,1)}, u32[]{:S(2)}, u32[]{:S(2)}) collective-permute-start(bf16[64,2048]{1,0:T(8,128)(2,1)} %get-tuple-element.109), channel_id=1, source_target_pairs={{0,2},{1,3},{2,0},{3,1},{4,6},{5,7},{6,4},{7,5},{8,10},{9,11},{10,... | collective-permute-start | bytes 786440 | tf_op jit(solution)/shard_map/ppermute | solution.py:32
  382.5 13.3 %collective-permute-start.49 = (bf16[64,2048]{1,0:T(8,128)(2,1)}, bf16[64,2048]{1,0:T(8,128)(2,1)S(1)}, u32[]{:S(2)}, u32[]{:S(2)}) collective-permute-start(bf16[64,2048]{1,0:T(8,128)(2,1)} %get-tuple-element.109), channel_id=1, source_target_pairs={{0,1},{1,2},{2,3},{3,0},{4,5},{5,6},{6,7},{7,4},{8,9},{9,10},{10,1... | collective-permute-start | bytes 786440 | tf_op jit(solution)/shard_map/ppermute | solution.py:32
  407.0 9.7 %collective-permute-start.50 = (bf16[64,2048]{1,0:T(8,128)(2,1)S(1)}, bf16[64,2048]{1,0:T(8,128)(2,1)S(1)}, u32[]{:S(2)}, u32[]{:S(2)}) collective-permute-start(bf16[64,2048]{1,0:T(8,128)(2,1)S(1)} %get-tuple-element.128), channel_id=1, source_target_pairs={{0,1},{1,2},{2,3},{3,0},{4,5},{5,6},{6,7},{7,4},{8,9},{9,10},{10,1... | collective-permute-start | bytes 786440 | tf_op jit(solution)/shard_map/ppermute | solution.py:32
  407.6 16.0 %collective-permute-start.51 = (bf16[64,2048]{1,0:T(8,128)(2,1)S(1)}, bf16[64,2048]{1,0:T(8,128)(2,1)S(1)}, u32[]{:S(2)}, u32[]{:S(2)}) collective-permute-start(bf16[64,2048]{1,0:T(8,128)(2,1)S(1)} %get-tuple-element.130), channel_id=1, source_target_pairs={{0,2},{1,3},{2,0},{3,1},{4,6},{5,7},{6,4},{7,5},{8,10},{9,11},{10,... | collective-permute-start | bytes 786440 | tf_op jit(solution)/shard_map/ppermute | solution.py:32
  411.7 11.8 %collective-permute-start.52 = (bf16[64,2048]{1,0:T(8,128)(2,1)S(1)}, bf16[64,2048]{1,0:T(8,128)(2,1)S(1)}, u32[]{:S(2)}, u32[]{:S(2)}) collective-permute-start(bf16[64,2048]{1,0:T(8,128)(2,1)S(1)} %get-tuple-element.129), channel_id=1, source_target_pairs={{0,3},{1,0},{2,1},{3,2},{4,7},{5,4},{6,5},{7,6},{8,11},{9,8},{10,9... | collective-permute-start | bytes 786440 | tf_op jit(solution)/shard_map/ppermute | solution.py:32
  436.1 11.2 %collective-permute-start.55 = (bf16[320,256]{1,0:T(8,128)(2,1)S(1)}, bf16[320,256]{1,0:T(8,128)(2,1)S(1)}, u32[]{:S(2)}, u32[]{:S(2)}) collective-permute-start(bf16[320,256]{1,0:T(8,128)(2,1)S(1)} %get-tuple-element.149), channel_id=1, source_target_pairs={{0,2},{1,3},{2,0},{3,1},{4,6},{5,7},{6,4},{7,5},{8,10},{9,11},{10,... | collective-permute-start | bytes 491528 | tf_op jit(solution)/shard_map/ppermute | solution.py:32
  439.8 58.1 %collective-permute-start.53 = (bf16[64,2048]{1,0:T(8,128)(2,1)S(1)}, bf16[64,2048]{1,0:T(8,128)(2,1)S(1)}, u32[]{:S(2)}, u32[]{:S(2)}) collective-permute-start(bf16[64,2048]{1,0:T(8,128)(2,1)S(1)} %get-tuple-element.171), channel_id=1, source_target_pairs={{0,64},{64,0},{1,65},{65,1},{2,66},{66,2},{3,67},{67,3},{4,68},{68... | collective-permute-start | bytes 786440 | tf_op jit(solution)/shard_map/ppermute | solution.py:496
  451.5 10.3 %collective-permute-start.60 = (bf16[64,256]{1,0:T(8,128)(2,1)S(1)}, bf16[64,256]{1,0:T(8,128)(2,1)S(1)}, u32[]{:S(2)}, u32[]{:S(2)}) collective-permute-start(bf16[64,256]{1,0:T(8,128)(2,1)S(1)} %get-tuple-element.223), channel_id=1, source_target_pairs={{16,0},{20,4},{24,8},{28,12},{32,16},{36,20},{40,24},{44,28},{48,3... | collective-permute-start | bytes 98312 | tf_op jit(solution)/shard_map/ppermute | solution.py:38
  463.1 9.6 %collective-permute-start.62 = (bf16[2,29,16,128]{3,2,1,0:T(8,128)(2,1)S(1)}, bf16[2,29,16,128]{3,2,1,0:T(8,128)(2,1)S(1)}, u32[]{:S(2)}, u32[]{:S(2)}) collective-permute-start(bf16[2,29,16,128]{3,2,1,0:T(8,128)(2,1)S(1)} %get-tuple-element.140), channel_id=1, source_target_pairs={{0,1},{1,2},{2,3},{3,0},{4,5},{5,6},{6,7},{7,4},{8,9},{9,10},{10,1... | collective-permute-start | bytes 712712 | tf_op jit(solution)/shard_map/ppermute | solution.py:32
  463.2 14.3 %collective-permute-start.63 = (bf16[2,29,16,128]{3,2,1,0:T(8,128)(2,1)S(1)}, bf16[2,29,16,128]{3,2,1,0:T(8,128)(2,1)S(1)}, u32[]{:S(2)}, u32[]{:S(2)}) collective-permute-start(bf16[2,29,16,128]{3,2,1,0:T(8,128)(2,1)S(1)} %get-tuple-element.142), channel_id=1, source_target_pairs={{0,2},{1,3},{2,0},{3,1},{4,6},{5,7},{6,4},{7,5},{8,10},{9,11},{10,... | collective-permute-start | bytes 712712 | tf_op jit(solution)/shard_map/ppermute | solution.py:32
  466.8 10.9 %collective-permute-start.64 = (bf16[2,29,16,128]{3,2,1,0:T(8,128)(2,1)S(1)}, bf16[2,29,16,128]{3,2,1,0:T(8,128)(2,1)S(1)}, u32[]{:S(2)}, u32[]{:S(2)}) collective-permute-start(bf16[2,29,16,128]{3,2,1,0:T(8,128)(2,1)S(1)} %get-tuple-element.141), channel_id=1, source_target_pairs={{0,3},{1,0},{2,1},{3,2},{4,7},{5,4},{6,5},{7,6},{8,11},{9,8},{10,9... | collective-permute-start | bytes 712712 | tf_op jit(solution)/shard_map/ppermute | solution.py:32
  492.7 21.0 %collective-permute-start.61 = (bf16[64,2048]{1,0:T(8,128)(2,1)S(1)}, bf16[64,2048]{1,0:T(8,128)(2,1)S(1)}, u32[]{:S(2)}, u32[]{:S(2)}) collective-permute-start(bf16[64,2048]{1,0:T(8,128)(2,1)S(1)} %select_convert_fusion), channel_id=1, source_target_pairs={{0,64},{64,0},{1,65},{65,1},{2,66},{66,2},{3,67},{67,3},{4,68},{68... | collective-permute-start | bytes 786440 | tf_op jit(solution)/shard_map/ppermute | solution.py:496
  515.7 11.9 %collective-permute-start.79 = (bf16[2,21,16,128]{3,2,1,0:T(8,128)(2,1)S(1)}, bf16[2,21,16,128]{3,2,1,0:T(8,128)(2,1)S(1)}, u32[]{:S(2)}, u32[]{:S(2)}) collective-permute-start(bf16[2,21,16,128]{3,2,1,0:T(8,128)(2,1)S(1)} %get-tuple-element.164), channel_id=1, source_target_pairs={{0,2},{1,3},{2,0},{3,1},{4,6},{5,7},{6,4},{7,5},{8,10},{9,11},{10,... | collective-permute-start | bytes 516104 | tf_op jit(solution)/shard_map/ppermute | solution.py:32
  519.6 8.1 %collective-permute-start.80 = (bf16[2,21,16,128]{3,2,1,0:T(8,128)(2,1)S(1)}, bf16[2,21,16,128]{3,2,1,0:T(8,128)(2,1)S(1)}, u32[]{:S(2)}, u32[]{:S(2)}) collective-permute-start(bf16[2,21,16,128]{3,2,1,0:T(8,128)(2,1)S(1)} %get-tuple-element.164), channel_id=1, source_target_pairs={{0,3},{1,0},{2,1},{3,2},{4,7},{5,4},{6,5},{7,6},{8,11},{9,8},{10,9... | collective-permute-start | bytes 516104 | tf_op jit(solution)/shard_map/ppermute | solution.py:32
  (169 other events, 2651.6 us)
Sparse Core Ops, SparseCore 0:
  11.6 126.9 all-gather.3
  141.4 71.9 all-gather.5
  216.3 72.0 all-gather.7

commit v10 on v9

--- a/solution.py
+++ b/solution.py
@@ -314,7 +314,7 @@
 
 
 def feed_pack(pack_ref, model, hidden):
-    cuts = [model, 2 * model, 2 * model + hidden, 2 * model + 2 * hidden, 3 * model + 2 * hidden]
+    cuts = [0, model, model + hidden, model + 2 * hidden, 2 * model + 2 * hidden]
     return [pack_ref.at[:, a:b] for a, b in zip(cuts[:-1], cuts[1:])]
 
 
@@ -575,39 +575,53 @@
     def pack(bank, parts):
         return jnp.concatenate([chosen(table, bank, flip) for table, flip in parts], axis=1)
 
-    def exchanged(parts):
-        return by_layer(pack(own_bank, parts), swap(pack(other_bank, parts)))
-
-    def cut_pack(parts):
-        own = jnp.concatenate([pack(own_bank, parts), query_rows], axis=1)
-        other = jnp.concatenate([pack(other_bank, parts), query_rows], axis=1)
-        return by_layer(own, swap(other))
-
+    cut_parts = [(query_expand, False), (output_shrink, True)]
+    whole_parts = [
+        (query_shrink, True),
+        (keyval_shrink, True),
+        (keyval_expand, False),
+        (output_expand, False),
+        (upward_shrink, True),
+        (upward_expand, False),
+        (downward_shrink, True),
+        (downward_expand, False),
+    ]
     query_rows = jnp.broadcast_to(query_bias, (rank, local_q))
-    cut_layers = jnp.stack(cut_pack([(query_expand, False), (output_shrink, True)]))
-    cut_parts = jnp.stack(
-        [cut_layers] + [around(cut_layers, "tensor", j) for j in range(1, ranks)]
-    )
-    cut_whole = jnp.stack(
+
+    def cut_pack(bank):
+        return jnp.concatenate([pack(bank, cut_parts), query_rows], axis=1)
+
+    shared_parts = [part for part in whole_parts if part[0] is not upward_expand and part[0] is not downward_shrink]
+    split_parts = [(upward_expand, False), (downward_shrink, True)]
+    shared_away = pack(other_bank, shared_parts)
+    quarter = shared_away.shape[1] // ranks
+    crossing = jnp.concatenate(
         [
-            lax.dynamic_index_in_dim(cut_parts, (tensor - r) % ranks, 0, keepdims=False)
-            for r in range(ranks)
+            cut_pack(other_bank),
+            lax.dynamic_slice_in_dim(shared_away, tensor * quarter, quarter, 1),
+            pack(other_bank, split_parts),
         ],
-        axis=2,
-    ).reshape(2, rank, ranks, 3, local_q)
-    eq_all, so_all, query_bias_all = [
-        cut_whole[:, :, :, k].reshape(2, rank, ranks * local_q) for k in range(3)
+        axis=1,
+    )
+    crossed_pack = swap(crossing)
+    cut_width = 3 * local_q
+    block = jnp.concatenate([cut_pack(own_bank), crossed_pack[:, : cut_width + quarter]], axis=1)
+    blocks = jnp.stack([block] + [around(block, "tensor", j) for j in range(1, ranks)])
+    blocks = [
+        lax.dynamic_index_in_dim(blocks, (tensor - r) % ranks, 0, keepdims=False)
+        for r in range(ranks)
     ]
-    early_layers = exchanged([(query_shrink, True), (keyval_shrink, True), (keyval_expand, False)])
-    late_layers = exchanged(
-        [
-            (output_expand, False),
-            (upward_shrink, True),
-            (upward_expand, False),
-            (downward_shrink, True),
-            (downward_expand, False),
-        ]
-    )
+
+    def joined(begin, size):
+        return jnp.concatenate([block[:, begin : begin + size] for block in blocks], axis=1)
+
+    cut_layers = [
+        by_layer(joined(k * local_q, local_q), joined(cut_width + k * local_q, local_q))
+        for k in range(3)
+    ]
+    eq_all, so_all, query_bias_all = cut_layers
+    shared_layers = by_layer(pack(own_bank, shared_parts), joined(2 * cut_width, quarter))
+    split_layers = by_layer(pack(own_bank, split_parts), crossed_pack[:, cut_width + quarter :])
 
     up_halves = halves(upward_weight[0])
     down_halves = halves(row_major(downward_weight[0].T))
@@ -626,10 +640,15 @@
         [part.astype(f32) for part in split(vector_layers[layer], vector_sizes)]
         for layer in range(2)
     ]
-    adapters = [
-        split(early_layers[layer], [width, width, 2 * head]) + [late_layers[layer][:, :width]]
-        for layer in range(2)
-    ]
+    adapters = []
+    feed_packs = []
+    for layer in range(2):
+        sq, skv, ekv, eo, su, ed = split(
+            shared_layers[layer], [width, width, 2 * head, width, width, width]
+        )
+        eu, sd = split(split_layers[layer], [local_f, local_f])
+        adapters.append((sq, skv, ekv, eo))
+        feed_packs.append(jnp.concatenate([su, eu, sd, ed], axis=1))
 
     inside = jnp.arange(rows, dtype=jnp.int32)
     query_place = data * span + tensor * rows + inside
@@ -663,7 +682,7 @@
         pieces = [along(keyval, "dp", back) for back in range(reach, 0, -1)] + [keyval]
         key_block = spread(jnp.concatenate(pieces, axis=0))
         queries, low_q = project_queries(
-            layer, normed, early_all, query_bias_all[layer, :1].astype(f32), eq_all[layer], sq
+            layer, normed, early_all, query_bias_all[layer][:1].astype(f32), eq_all[layer], sq
         )
         probs, mixed, low_o, attended = attend(
             layer, queries, key_block, bias, early_all, so_all[layer], eo, head
@@ -694,40 +713,55 @@
             return pile
         return jnp.concatenate([pile, jnp.zeros((lack,) + pile.shape[1:], pile.dtype)], axis=0)
 
-    def piled(shared, quartered):
-        pile = padded(jnp.concatenate([tiles(part) for part in shared], axis=0), ranks)
+    def piled(*groups):
+        piles = [
+            padded(jnp.concatenate([tiles(part) for part in group], axis=0), ranks) for group in groups
+        ]
         return jnp.concatenate(
-            [block.reshape((ranks, -1) + block.shape[1:]) for block in [pile] + [tiles(part) for part in quartered]],
-            axis=1,
+            [pile.reshape((ranks, -1) + pile.shape[1:]) for pile in piles], axis=1
         ).astype(bf16)
-
-    def owned_pile(mine, owned):
-        pile = jnp.concatenate([mine] + [tiles(part) for part in owned], axis=0).astype(bf16)
-        return padded(pile, lax.axis_size("dp"))
 
     def at(block, index, axis):
         return lax.dynamic_index_in_dim(block, index, axis, keepdims=False)
 
+    def summed_ranks(pile):
+        total = at(pile, tensor, 0).astype(f32)
+        for j in range(1, ranks):
+            block = at(pile, (tensor + j) % ranks, 0)
+            total = total + around(block, "tensor", j).astype(f32)
+        return total
+
     def scattered_grads(layers):
-        pile = jnp.stack([piled(shared, quartered) for shared, quartered, _ in layers], axis=1)
-        mine = at(pile, tensor, 0).astype(f32)
-        for j in range(1, ranks):
-            mine = mine + around(at(pile, (tensor + j) % ranks, 0), "tensor", j).astype(f32)
-        pile = jnp.stack([owned_pile(mine[i], layers[i][2]) for i in range(2)])
-        pile = pile.reshape((2, chips, 4, -1) + pile.shape[2:])
-        mine = at(pile, near, 2).astype(f32)
+        (shared, keyval, quartered, owned), other = layers
+        groups = [other[0], other[1]] + [[part] for part in other[2]]
+        early = summed_ranks(
+            jnp.concatenate(
+                [piled(*groups), piled(shared, *[[part] for part in quartered])], axis=1
+            )
+        )
+        late = summed_ranks(piled(keyval))
+        count = -(-sum(part.shape[1] // 128 for part in shared) // ranks)
+        border = sum(-(-sum(part.shape[1] // 128 for part in group) // ranks) for group in groups)
+        zero = early[border:]
+        piles = [
+            jnp.concatenate(
+                [zero[:count], late, zero[count:]] + [tiles(part) for part in owned], axis=0
+            ),
+            jnp.concatenate([early[:border]] + [tiles(part) for part in other[3]], axis=0),
+        ]
+        pile = jnp.stack([padded(block.astype(bf16), lax.axis_size("dp")) for block in piles])
+        pile = pile.reshape((2, 4, -1) + pile.shape[2:])
+        mine = at(pile, near, 1).astype(f32)
         for k in range(1, 4):
-            mine = mine + flipped(at(pile, near ^ k, 2), "dp", k).astype(f32)
-        pile = mine.astype(bf16)
-        mine = at(pile, turn, 1).astype(f32)
-        for k in range(1, chips):
-            mine = mine + flipped(at(pile, turn ^ k, 1), "dp", 4 * k).astype(f32)
-        return mine.astype(bf16)
+            mine = mine + flipped(at(pile, near ^ k, 1), "dp", k).astype(f32)
+        mine = mine.astype(bf16)
+        parts = jnp.stack([mine] + [flipped(mine, "dp", 4 * k) for k in range(1, chips)])
+        return sum(at(parts, turn ^ k, 0).astype(f32) for k in range(chips)).astype(bf16)
 
     def crossed(block, mask):
         return lax.ppermute(block, both, [(i, i ^ mask) for i in range(8 * chips)])
 
-    def spread_grads(zero, one, shared, quartered, owned):
+    def spread_grads(zero, one, shared, keyval, quartered, owned):
         own = jnp.where(low_section, zero, one)
         away = jnp.where(low_section, one, zero)
         dp_size = 4 * chips
@@ -739,29 +773,30 @@
         pair = jnp.where(
             low_section, jnp.stack([home, guest], axis=1), jnp.stack([guest, home], axis=1)
         )
-        parts = jnp.stack([pair] + [flipped(pair, "dp", 4 * k) for k in range(1, chips)])
-        parts = jnp.stack([at(parts, turn ^ k, 0) for k in range(chips)])
-        other = flipped(parts, "dp", 1)
+        other = flipped(pair, "dp", 1)
         core = near % 2
         parts = jnp.stack(
-            [jnp.where(core == 0, parts, other), jnp.where(core == 0, other, parts)], axis=2
-        )
-        pile = jnp.moveaxis(parts, 3, 0).reshape((2, -1) + parts.shape[5:])
-        shared_sizes = [part.shape[1] // 128 for part in shared]
-        quarter_sizes = [part.shape[1] // 128 // ranks for part in quartered]
-        owned_sizes = [part.shape[1] // 128 for part in owned]
-        each = -(-sum(shared_sizes) // ranks)
-        own = pile[:, :each]
+            [jnp.where(core == 0, pair, other), jnp.where(core == 0, other, pair)], axis=1
+        )
+        pile = jnp.moveaxis(parts, 2, 0).reshape((2, -1) + parts.shape[4:])
+        sizes = [[part.shape[1] // 128 for part in group] for group in (shared, keyval)]
+        counts = [-(-sum(group) // ranks) for group in sizes]
+        own = pile[:, : sum(counts)]
         parts = jnp.stack([own] + [around(own, "tensor", k) for k in range(1, ranks)])
-        ordered = jnp.concatenate([at(parts, (tensor - r) % ranks, 0) for r in range(ranks)], axis=1)
+        parts = [at(parts, (tensor - r) % ranks, 0) for r in range(ranks)]
         results = []
-        for whole, begin, sizes in [
-            (ordered, 0, shared_sizes),
-            (pile, each, quarter_sizes + owned_sizes),
-        ]:
-            for count in sizes:
+
+        def take(whole, begin, group):
+            for count in group:
                 results.append([flat(whole[m, begin : begin + count]) for m in range(2)])
                 begin += count
+
+        begin = 0
+        for count, group in zip(counts, sizes):
+            take(jnp.concatenate([part[:, begin : begin + count] for part in parts], axis=1), 0, group)
+            begin += count
+        rest = [part.shape[1] // 128 // ranks for part in quartered]
+        take(pile, begin, rest + [part.shape[1] // 128 for part in owned])
         return results
 
     def feed_grads(layer, grad, unit2, rsd2, partial):
@@ -794,24 +829,22 @@
         inner_kv = against(grad_kv, ekv).astype(bf16)
         grad_normed = partial + against(grad_kv, keyval_ws[layer]) + plain(inner_kv, skv)
         grad_hidden = grad_middle + norm_back(unit1, rsd1, grad_normed * gain1)
-        shared = [
-            across(low_o, branch),
-            across(inner_q, normed),
-            across(inner_kv, normed),
-            across(low_kv, grad_kv),
-        ]
+        shared = [across(low_o, branch), across(inner_q, normed)]
+        keyval = [across(inner_kv, normed), across(low_kv, grad_kv)]
         quartered = [across(low_q, grad_q), across(inner_o, mixed)]
-        return grad_hidden, shared, quartered
+        return grad_hidden, shared, keyval, quartered
 
     fresh = lax.dynamic_index_in_dim(block_input, section, 0, keepdims=False).astype(f32)
     given = lax.dynamic_index_in_dim(cotangent, section, 0, keepdims=False).astype(f32)
+    branch_one = spread(given.astype(bf16))
+    fresh, branch_one = lax.optimization_barrier((fresh, branch_one))
 
     middle_zero, kept_zero = forward_attend(0, fresh)
     unit_zero, rsd_zero, second_zero, up_bias = feed_inputs(0, middle_zero)
     active_zero, slope_zero, low_u_zero, low_d_zero, partial = feed_call(
         feed_kernel,
         "feed",
-        (second_zero, feed_tables[0], up_bias, late_layers[0]),
+        (second_zero, feed_tables[0], up_bias, feed_packs[0]),
         (local_f, local_f, rank, rank, width),
         local_f,
         2,
@@ -820,11 +853,10 @@
 
     middle_one, kept_one = forward_attend(1, passed.astype(f32))
     unit_one, rsd_one, second_one, up_bias = feed_inputs(1, middle_one)
-    branch_one = spread(given.astype(bf16))
     active, low_u, low_d, partial, grad_up, inner_d, inner_u, partial_back = feed_call(
         feed_both_kernel,
         "feed_both",
-        (second_one, branch_one, feed_tables[1], up_bias, late_layers[1]),
+        (second_one, branch_one, feed_tables[1], up_bias, feed_packs[1]),
         (local_f, rank, rank, width, local_f, rank, rank, width),
         local_f,
         4,
@@ -833,8 +865,8 @@
     shared, owned = feed_adapters(
         second_one, branch_one, low_u, low_d, inner_u, inner_d, active, grad_up
     )
-    grad_one, more, quartered = backward_attend(1, kept_one, grad_middle)
-    layer_one = (shared + more, quartered, owned)
+    grad_one, more, keyval, quartered = backward_attend(1, kept_one, grad_middle)
+    layer_one = (shared + more, keyval, quartered, owned)
     partial, _ = lax.optimization_barrier((partial, grad_middle))
     final = feed_result(1, middle_one, partial).astype(bf16)
 
@@ -842,7 +874,7 @@
     grad_up, inner_d, inner_u, partial_back = feed_call(
         feed_back_kernel,
         "feed_back",
-        (branch_zero, feed_tables[0], slope_zero, late_layers[0]),
+        (branch_zero, feed_tables[0], slope_zero, feed_packs[0]),
         (local_f, rank, rank, width),
         local_f,
         2,
@@ -858,10 +890,10 @@
         active_zero,
         grad_up,
     )
-    grad_zero, more, quartered = backward_attend(0, kept_zero, grad_middle_zero)
-    shared = shared + more
-    mine = scattered_grads([(shared, quartered, owned), layer_one])
-    grads = spread_grads(mine[0], mine[1], shared, quartered, owned)
+    grad_zero, more, keyval, quartered = backward_attend(0, kept_zero, grad_middle_zero)
+    layer_zero = (shared + more, keyval, quartered, owned)
+    mine = scattered_grads([layer_zero, layer_one])
+    grads = spread_grads(mine[0], mine[1], *layer_zero)
 
     def both_micros(zero, one, kind):
         own = jnp.where(low_section, zero, one)

time: 549 us -> 560 us (1.020)
  starting transfers between devices: 129 us -> 139 us
  waiting for transfers between devices: 232 us -> 222 us
    ppermute x45 -> x48, starting transfers between devices: 65.1 us -> 80.4 us  [around(): lax.ppermute(block, axis, [(i, (i + distance) % size) for i in range(size)])]
    ppermute x45 -> x48, waiting for transfers between devices: 108 us -> 117 us  [around(): lax.ppermute(block, axis, [(i, (i + distance) % size) for i in range(size)])]
    all_gather x2, waiting for transfers between devices: 14.1 us -> 4.69 us  [gather(): lax.all_gather(row_major(shard), both, axis=0, tiled=True, axis_index_gro...]
    concatenate x1 -> x4, local copies, waits for them, and re-layouts: 0.01 us -> 7.62 us  [the longest x1 5.7 us: scattered_grads(): jnp.concatenate([piled(*groups), piled(shared, *[[part] for part in quart...]
    ppermute x11 -> x8, starting transfers between devices: 13.9 us -> 9.74 us  [flipped(): return lax.ppermute(block, axis, [(i, i ^ bit) for i in range(size)])]
    ppermute x7 -> x5, waiting for transfers between devices: 26.3 us -> 23.5 us  [swap(): return lax.ppermute(value, 'section', sides)]
    ppermute x7 -> x5, starting transfers between devices: 14.1 us -> 12 us  [swap(): return lax.ppermute(value, 'section', sides)]
    unnamed x312 -> x315, local copies, waits for them, and re-layouts: 17.7 us -> 16.3 us
  transfers between devices with their start and end apart: 84 -> 82, of which waited for: 52 -> 50; matrix products, arithmetic and copies ran while one was open for 10% -> 11% of each run, Pallas kernels for 7% -> 7%
where the time goes in v10:
time: 560 us; the launch traced here: 550 us
  waiting for transfers between devices  222 us (40%)
  starting transfers between devices  139 us (25%)
  Pallas kernels  85.9 us (15%)
  local copies, waits for them, and re-layouts  38.9 us (7%)
  other arithmetic  32.3 us (6%)
  between operations  20.9 us (4%)
  matrix products  11 us (2%)
    ppermute x48, waiting for transfers between devices, around(): lax.ppermute(block, axis, [(i, (i + distance) % size) for i in range(size)])  117 us
    ppermute x48, starting transfers between devices, around(): lax.ppermute(block, axis, [(i, (i + distance) % size) for i in range(size)])  80.4 us
    all_gather x1, waiting for transfers between devices, gather_all(): lax.all_gather(row_major(shard), every, axis=0, tiled=True, axis_index_gr...  51.3 us
    pallas_call x3, Pallas kernels, feed_call(): pl.pallas_call(kernel, in_specs=[remote if value.ndim == 4 else held for...  35.2 us
    ppermute x16, starting transfers between devices, along(): return lax.ppermute(block, axis, route)  32.1 us
    ppermute x5, waiting for transfers between devices, swap(): return lax.ppermute(value, 'section', sides)  23.5 us
    pallas_call x2, Pallas kernels, attend_back(): pl.pallas_call(lambda *refs: attend_back_kernel(layer, head, *refs), in_s...  23 us
    pallas_call x2, Pallas kernels, attend(): pl.pallas_call(lambda *refs: attend_kernel(layer, head, *refs), in_specs=...  19.1 us
  transfers between devices with their start and end apart: 82, of which 50 were waited for; matrix products, arithmetic and copies ran while one was open for 11% of the time, Pallas kernels for 7%

profile of v10, /device:TPU:0, one launch (start us, length us, event | category | flops | bytes accessed | tf_op | source)
XLA Modules:
  0.0 550.2 jit_solution(3560580732045261052)
XLA Ops:
  12.3 4.0 collective-permute-start.18
  16.4 12.2 %collective-permute-done.18 = bf16[128,2048]{1,0:T(8,128)(2,1)S(1)} collective-permute-done((bf16[128,2048]{1,0:T(8,128)(2,1)S(1)}, bf16[128,2048]{1,0:T(8,128)(2,1)S(1)}, u32[]{:S(2)}, u32[]{:S(2)}) %collective-permute-start.18) | collective-permute-done | bytes 524320 | tf_op jit(solution)/shard_map/ppermute | solution.py:496
  47.9 4.1 collective-permute-start.4
  54.7 11.2 %collective-permute-done.3 = bf16[1,14592]{1,0:T(2,128)(2,1)S(1)} collective-permute-done((bf16[1,14592]{1,0:T(2,128)(2,1)S(1)}, bf16[1,14592]{1,0:T(2,128)(2,1)S(1)}, u32[]{:S(2)}, u32[]{:S(2)}) %collective-permute-start.3) | collective-permute-done | bytes 29216 | tf_op jit(solution)/shard_map/ppermute | solution.py:496
  84.1 51.3 %all-gather.4.cloned.1.call-done = bf16[16384,1152]{1,0:T(8,128)(2,1)} async-done(((bf16[128,1152]{1,0:T(8,128)(2,1)}), bf16[16384,1152]{1,0:T(8,128)(2,1)}) %all-gather.4.cloned.1.call-update) | async-done | bytes 37748752 | tf_op jit(solution)/shard_map/all_gather | solution.py:534
  138.6 3.4 collective-permute-start.8
  144.9 4.1 collective-permute-start.10
  154.8 4.4 project_queries.2
  159.2 12.9 %collective-permute-start.14 = (bf16[320,256]{1,0:T(8,128)(2,1)S(1)}, bf16[320,256]{1,0:T(8,128)(2,1)S(1)}, u32[]{:S(2)}, u32[]{:S(2)}) collective-permute-start(bf16[320,256]{1,0:T(8,128)(2,1)S(1)} %get-tuple-element.302), channel_id=1, source_target_pairs={{0,1},{1,2},{2,3},{3,0},{4,5},{5,6},{6,7},{7,4},{8,9},{9,10},{10,1... | collective-permute-start | bytes 491528 | tf_op jit(solution)/shard_map/ppermute | solution.py:32
  172.1 7.1 %collective-permute-done.14 = bf16[320,256]{1,0:T(8,128)(2,1)S(1)} collective-permute-done((bf16[320,256]{1,0:T(8,128)(2,1)S(1)}, bf16[320,256]{1,0:T(8,128)(2,1)S(1)}, u32[]{:S(2)}, u32[]{:S(2)}) %collective-permute-start.14) | collective-permute-done | bytes 163872 | tf_op jit(solution)/shard_map/ppermute | solution.py:32
  179.3 9.5 %attend.2 = (bf16[4,256,1280]{2,1,0:T(8,128)(2,1)S(1)}, bf16[64,2048]{1,0:T(8,128)(2,1)S(1)}, bf16[64,16]{1,0:T(8,128)(2,1)S(1)}, f32[64,2048]{1,0:T(8,128)S(1)}) custom-call(bf16[64,2048]{1,0:T(8,128)(2,1)S(1)} %get-tuple-element.57.refs_0_.refs_5_, bf16[1280,256]{1,0:T(8,128)(2,1)S(1)} %constant_dynamic-update-slice_fusion.26.refs_1_.refs_6_, ...), custom_call_target="tpu_custom_call" | custom-call | flops 2818572288 | bytes 8388608 | tf_op jit(solution)/shard_map/attend/pallas_call | solution.py:180
  192.6 6.4 %collective-permute-done.15 = bf16[64,2048]{1,0:T(8,128)(2,1)S(1)} collective-permute-done((bf16[64,2048]{1,0:T(8,128)(2,1)S(1)}, bf16[64,2048]{1,0:T(8,128)(2,1)S(1)}, u32[]{:S(2)}, u32[]{:S(2)}) %collective-permute-start.15) | collective-permute-done | bytes 262176 | tf_op jit(solution)/shard_map/ppermute | solution.py:32
  200.9 4.5 collective-permute-done.17
  205.5 4.7 all-gather.6.cloned.1.call-done
  210.2 10.8 %feed.1 = (bf16[256,2048]{1,0:T(8,128)(2,1)S(1)}, bf16[256,2048]{1,0:T(8,128)(2,1)S(1)}, bf16[256,16]{1,0:T(8,128)(2,1)S(1)}, bf16[256,16]{1,0:T(8,128)(2,1)S(1)}, bf16[256,2048]{1,0:T(8,128)(2,1)S(1)}) custom-call(bf16[256,2048]{1,0:T(8,128)(2,1)S(1)} %pad_maximum_fusion.2.second_ref, bf16[4,2,512,2048]{3,2,1,0:T(8,128)(2,1)} %bitcast.634, ...), custom_call_target="tpu_custom_call" | custom-call | flops 4294967296 | bytes 16777216 | tf_op jit(solution)/shard_map/feed/pallas_call | solution.py:430
  227.6 3.4 collective-permute-done.19
  231.0 6.5 %collective-permute-done.20 = bf16[64,2048]{1,0:T(8,128)(2,1)S(1)} collective-permute-done((bf16[64,2048]{1,0:T(8,128)(2,1)S(1)}, bf16[64,2048]{1,0:T(8,128)(2,1)S(1)}, u32[]{:S(2)}, u32[]{:S(2)}) %collective-permute-start.20) | collective-permute-done | bytes 262176 | tf_op jit(solution)/shard_map/ppermute | solution.py:32
  239.1 3.4 collective-permute-start.22
  243.8 4.2 collective-permute-start.24
  254.0 4.4 project_queries.3
  261.2 5.0 collective-permute-done.28
  266.3 9.5 %attend.3 = (bf16[4,256,1280]{2,1,0:T(8,128)(2,1)S(1)}, bf16[64,2048]{1,0:T(8,128)(2,1)S(1)}, bf16[64,16]{1,0:T(8,128)(2,1)S(1)}, f32[64,2048]{1,0:T(8,128)S(1)}) custom-call(bf16[64,2048]{1,0:T(8,128)(2,1)S(1)} %get-tuple-element.60.refs_0_.refs_5_, bf16[1280,256]{1,0:T(8,128)(2,1)S(1)} %constant_dynamic-update-slice_fusion.39.refs_1_.refs_6_, ...), custom_call_target="tpu_custom_call" | custom-call | flops 2818572288 | bytes 8388608 | tf_op jit(solution)/shard_map/attend/pallas_call | solution.py:180
  283.5 4.7 collective-permute-done.29
  290.3 5.5 %collective-permute-done.31 = bf16[64,2048]{1,0:T(8,128)(2,1)S(1)} collective-permute-done((bf16[64,2048]{1,0:T(8,128)(2,1)S(1)}, bf16[64,2048]{1,0:T(8,128)(2,1)S(1)}, u32[]{:S(2)}, u32[]{:S(2)}) %collective-permute-start.31) | collective-permute-done | bytes 262176 | tf_op jit(solution)/shard_map/ppermute | solution.py:32
  299.8 14.4 %feed_both.1 = (bf16[256,2048]{1,0:T(8,128)(2,1)S(1)}, bf16[256,16]{1,0:T(8,128)(2,1)S(1)}, bf16[256,16]{1,0:T(8,128)(2,1)S(1)}, bf16[256,2048]{1,0:T(8,128)(2,1...) custom-call(bf16[256,2048]{1,0:T(8,128)(2,1)S(1)} %copy-done.2, ...), custom_call_target="tpu_custom_call" | custom-call | flops 8589934592 | bytes 16777216 | tf_op jit(solution)/shard_map/feed_both/pallas_call | solution.py:430
  321.3 10.0 %collective-permute-done.32 = bf16[64,2048]{1,0:T(8,128)(2,1)S(1)} collective-permute-done((bf16[64,2048]{1,0:T(8,128)(2,1)S(1)}, bf16[64,2048]{1,0:T(8,128)(2,1)S(1)}, u32[]{:S(2)}, u32[]{:S(2)}) %collective-permute-start.32) | collective-permute-done | bytes 262176 | tf_op jit(solution)/shard_map/ppermute | solution.py:32
  332.6 11.5 %attend_back.2 = (bf16[64,2048]{1,0:T(8,128)(2,1)S(1)}, bf16[1280,256]{1,0:T(8,128)(2,1)S(1)}, bf16[64,16]{1,0:T(8,128)(2,1)S(1)}, bf16[64,16]{1,0:T(8,128)(2,1)S(1)}, f32[64,2048]{1,0:T(8,128)S(1)}) custom-call(bf16[64,2048]{1,0:T(8,128)(2,1)S(1)} %get-tuple-element.121.refs_0_, bf16[4,4,2,512,1152]{4,3,2,1,0:T(8,128)(2,1)} %bitcast.632, ...), custom_call_target="tpu_custom_call" | custom-call | flops 5637144576 | bytes 22020096 | tf_op jit(solution)/shard_map/attend_back/pallas_call | solution.py:259
  345.3 3.1 collective-permute-start.39
  351.3 4.7 collective-permute-done.39
  364.1 3.1 collective-permute-start.36
  375.7 4.2 collective-permute-done.36
  380.6 5.4 collective-permute-done.45
  386.1 5.1 collective-permute-done.47
  391.2 9.9 %feed_back.1 = (bf16[256,2048]{1,0:T(8,128)(2,1)S(1)}, bf16[256,16]{1,0:T(8,128)(2,1)S(1)}, bf16[256,16]{1,0:T(8,128)(2,1)S(1)}, bf16[256,2048]{1,0:T(8,128)(2,1)S(1)}) custom-call(bf16[256,2048]{1,0:T(8,128)(2,1)S(1)} %pad_maximum_fusion.5.branch_ref, bf16[4,2,512,2048]{3,2,1,0:T(8,128)(2,1)} %bitcast.635, bf16[256,2048]{1,0:T(8,128)(2,1)S(1)} %copy-done.16, ...), custom_call_target="tpu_custom_call" | custom-call | flops 4294967296 | bytes 16777216 | tf_op jit(solution)/shard_map/feed_back/pallas_call | solution.py:430
  402.3 3.6 collective-permute-start.49
  410.9 6.8 %collective-permute-done.49 = bf16[64,2048]{1,0:T(8,128)(2,1)S(1)} collective-permute-done((bf16[64,2048]{1,0:T(8,128)(2,1)S(1)}, bf16[64,2048]{1,0:T(8,128)(2,1)S(1)}, u32[]{:S(2)}, u32[]{:S(2)}) %collective-permute-start.49) | collective-permute-done | bytes 262176 | tf_op jit(solution)/shard_map/ppermute | solution.py:32
  419.2 11.5 %attend_back.3 = (bf16[64,2048]{1,0:T(8,128)(2,1)S(1)}, bf16[1280,256]{1,0:T(8,128)(2,1)S(1)}, bf16[64,16]{1,0:T(8,128)(2,1)S(1)}, bf16[64,16]{1,0:T(8,128)(2,1)S(1)}, f32[64,2048]{1,0:T(8,128)S(1)}) custom-call(bf16[64,2048]{1,0:T(8,128)(2,1)S(1)} %get-tuple-element.113.refs_0_, bf16[4,4,2,512,1152]{4,3,2,1,0:T(8,128)(2,1)} %bitcast.633, ...), custom_call_target="tpu_custom_call" | custom-call | flops 5637144576 | bytes 22020096 | tf_op jit(solution)/shard_map/attend_back/pallas_call | solution.py:259
  431.3 3.6 collective-permute-start.53
  437.8 4.7 collective-permute-done.53
  452.7 4.1 collective-permute-done.58
  460.6 5.7 %concatenate.195 = bf16[4,53,16,128]{3,1,2,0:T(8,128)(2,1)S(1)} concatenate(bf16[4,16,16,128]{3,1,2,0:T(8,128)(2,1)S(1)} %copy-done.65, bf16[4,5,16,128]{3,1,2,0:T(8,128)(2,1)S(1)} %copy.134, bf16[4,4,16,128]{3,1,2,0:T(4,128)(2,1)} %copy.135, bf16[4,4,16,128]{3,1,2,0:T(4,128)(2,1)S(1)} %copy-done.80, bf16[4,16,16,128]{3,1,2,0:T(8,128)(2,1)S(1)} %copy.137, ...), dimensions={1} | concatenate | bytes 1736704 | tf_op jit(solution)/shard_map/concatenate | solution.py:738
  466.9 4.4 collective-permute-start.64
  477.6 6.2 %collective-permute-done.61 = bf16[53,16,128]{2,0,1:T(8,128)(2,1)S(1)} collective-permute-done((bf16[53,16,128]{2,0,1:T(8,128)(2,1)S(1)}, bf16[53,16,128]{2,0,1:T(8,128)(2,1)S(1)}, u32[]{:S(2)}, u32[]{:S(2)}) %collective-permute-start.61) | collective-permute-done | bytes 217120 | tf_op jit(solution)/shard_map/ppermute | solution.py:32
  483.8 3.2 collective-permute-done.62
  490.8 4.2 collective-permute-done.67
  499.8 4.4 collective-permute-start.70
  505.9 4.9 collective-permute-done.70
  533.4 4.6 collective-permute-done.77
  (683 shorter events, 188.6 us)
Async XLA Ops:
  7.2 128.2 %all-gather.4.cloned.1.call-start = ((), (), s32[]{:S(2)}) async-start(), calls=%async_computation | async-start | bytes 38043648 | tf_op jit(solution)/shard_map/all_gather | solution.py:534
  10.8 199.5 %all-gather.6.cloned.1.call-start = ((), (), s32[]{:S(2)}) async-start(), calls=%async_computation.1 | async-start | bytes 17301504 | tf_op jit(solution)/shard_map/all_gather | solution.py:530
  12.3 16.3 %collective-permute-start.18 = (bf16[128,2048]{1,0:T(8,128)(2,1)S(1)}, bf16[128,2048]{1,0:T(8,128)(2,1)S(1)}, u32[]{:S(2)}, u32[]{:S(2)}) collective-permute-start(bf16[128,2048]{1,0:T(8,128)(2,1)S(1)} %broadcast_select_fusion.2), channel_id=1, source_target_pairs={{0,64},{64,0},{1,65},{65,1},{2,66},{66,2},{3,67},{67,3},{4,68},{68... | collective-permute-start | bytes 1572872 | tf_op jit(solution)/shard_map/ppermute | solution.py:496
  30.0 266.9 %all-gather.8.cloned.1.call-start = ((), (), s32[]{:S(2)}) async-start(), calls=%async_computation.2 | async-start | bytes 17301504 | tf_op jit(solution)/shard_map/all_gather | solution.py:530
  30.1 37.2 %collective-permute-start = (bf16[64,2048]{1,0:T(8,128)(2,1)S(1)}, bf16[64,2048]{1,0:T(8,128)(2,1)S(1)}, u32[]{:S(2)}, u32[]{:S(2)}) collective-permute-start(bf16[64,2048]{1,0:T(8,128)(2,1)S(1)} %dynamic-slice_bitcast_fusion), channel_id=1, source_target_pairs={{0,3},{1,0},{2,1},{3,2},{4,7},{5,4},{6,5},{7,6},{8,11},{9,8},{10,9... | collective-permute-start | bytes 786440 | tf_op jit(solution)/shard_map/ppermute | solution.py:32
  32.9 34.4 %collective-permute-start.1 = (bf16[64,2048]{1,0:T(8,128)(2,1)S(1)}, bf16[64,2048]{1,0:T(8,128)(2,1)S(1)}, u32[]{:S(2)}, u32[]{:S(2)}) collective-permute-start(bf16[64,2048]{1,0:T(8,128)(2,1)S(1)} %dynamic-slice_bitcast_fusion), channel_id=1, source_target_pairs={{0,2},{1,3},{2,0},{3,1},{4,6},{5,7},{6,4},{7,5},{8,10},{9,11},{10,... | collective-permute-start | bytes 786440 | tf_op jit(solution)/shard_map/ppermute | solution.py:32
  33.7 33.6 %collective-permute-start.2 = (bf16[64,2048]{1,0:T(8,128)(2,1)S(1)}, bf16[64,2048]{1,0:T(8,128)(2,1)}, u32[]{:S(2)}, u32[]{:S(2)}) collective-permute-start(bf16[64,2048]{1,0:T(8,128)(2,1)S(1)} %dynamic-slice_bitcast_fusion), channel_id=1, source_target_pairs={{0,1},{1,2},{2,3},{3,0},{4,5},{5,6},{6,7},{7,4},{8,9},{9,10},{10,1... | collective-permute-start | bytes 786440 | tf_op jit(solution)/shard_map/ppermute | solution.py:32
  47.9 21.0 %collective-permute-start.4 = (bf16[16,8256]{1,0:T(8,128)(2,1)S(1)}, bf16[16,8256]{1,0:T(8,128)(2,1)S(1)}, u32[]{:S(2)}, u32[]{:S(2)}) collective-permute-start(bf16[16,8256]{1,0:T(8,128)(2,1)S(1)} %concatenate.167), channel_id=1, source_target_pairs={{0,64},{64,0},{1,65},{65,1},{2,66},{66,2},{3,67},{67,3},{4,68},{68... | collective-permute-start | bytes 792584 | tf_op jit(solution)/shard_map/ppermute | solution.py:496
  52.2 13.7 %collective-permute-start.3 = (bf16[1,14592]{1,0:T(2,128)(2,1)S(1)}, bf16[1,14592]{1,0:T(2,128)(2,1)S(1)}, u32[]{:S(2)}, u32[]{:S(2)}) collective-permute-start(bf16[1,14592]{1,0:T(2,128)(2,1)S(1)} %constant_dynamic-update-slice_fusion), channel_id=1, source_target_pairs={{0,64},{64,0},{1,65},{65,1},{2,66},{66,2},{3,67},{67,3},{4,68},{68... | collective-permute-start | bytes 87560 | tf_op jit(solution)/shard_map/ppermute | solution.py:496
  138.6 11.9 %collective-permute-start.8 = (bf16[64,256]{1,0:T(8,128)(2,1)S(1)}, bf16[64,256]{1,0:T(8,128)(2,1)S(1)}, u32[]{:S(2)}, u32[]{:S(2)}) collective-permute-start(bf16[64,256]{1,0:T(8,128)(2,1)S(1)} %fusion.18), channel_id=1, source_target_pairs={{0,16},{4,20},{8,24},{12,28},{16,32},{20,36},{24,40},{28,44},{32,4... | collective-permute-start | bytes 98312 | tf_op jit(solution)/shard_map/ppermute | solution.py:38
  151.4 20.7 %collective-permute-start.12 = (bf16[320,256]{1,0:T(8,128)(2,1)S(1)}, bf16[320,256]{1,0:T(8,128)(2,1)S(1)}, u32[]{:S(2)}, u32[]{:S(2)}) collective-permute-start(bf16[320,256]{1,0:T(8,128)(2,1)S(1)} %get-tuple-element.302), channel_id=1, source_target_pairs={{0,3},{1,0},{2,1},{3,2},{4,7},{5,4},{6,5},{7,6},{8,11},{9,8},{10,9... | collective-permute-start | bytes 491528 | tf_op jit(solution)/shard_map/ppermute | solution.py:32
  153.9 18.2 %collective-permute-start.13 = (bf16[320,256]{1,0:T(8,128)(2,1)S(1)}, bf16[320,256]{1,0:T(8,128)(2,1)S(1)}, u32[]{:S(2)}, u32[]{:S(2)}) collective-permute-start(bf16[320,256]{1,0:T(8,128)(2,1)S(1)} %get-tuple-element.302), channel_id=1, source_target_pairs={{0,2},{1,3},{2,0},{3,1},{4,6},{5,7},{6,4},{7,5},{8,10},{9,11},{10,... | collective-permute-start | bytes 491528 | tf_op jit(solution)/shard_map/ppermute | solution.py:32
  159.2 20.1 %collective-permute-start.14 = (bf16[320,256]{1,0:T(8,128)(2,1)S(1)}, bf16[320,256]{1,0:T(8,128)(2,1)S(1)}, u32[]{:S(2)}, u32[]{:S(2)}) collective-permute-start(bf16[320,256]{1,0:T(8,128)(2,1)S(1)} %get-tuple-element.302), channel_id=1, source_target_pairs={{0,1},{1,2},{2,3},{3,0},{4,5},{5,6},{6,7},{7,4},{8,9},{9,10},{10,1... | collective-permute-start | bytes 491528 | tf_op jit(solution)/shard_map/ppermute | solution.py:32
  189.8 9.2 %collective-permute-start.15 = (bf16[64,2048]{1,0:T(8,128)(2,1)S(1)}, bf16[64,2048]{1,0:T(8,128)(2,1)S(1)}, u32[]{:S(2)}, u32[]{:S(2)}) collective-permute-start(bf16[64,2048]{1,0:T(8,128)(2,1)S(1)} %add_convert_fusion.3), channel_id=1, source_target_pairs={{0,3},{1,0},{2,1},{3,2},{4,7},{5,4},{6,5},{7,6},{8,11},{9,8},{10,9... | collective-permute-start | bytes 786440 | tf_op jit(solution)/shard_map/ppermute | solution.py:32
  190.2 10.7 %collective-permute-start.16 = (bf16[64,2048]{1,0:T(8,128)(2,1)S(1)}, bf16[64,2048]{1,0:T(8,128)(2,1)S(1)}, u32[]{:S(2)}, u32[]{:S(2)}) collective-permute-start(bf16[64,2048]{1,0:T(8,128)(2,1)S(1)} %add_convert_fusion.3), channel_id=1, source_target_pairs={{0,2},{1,3},{2,0},{3,1},{4,6},{5,7},{6,4},{7,5},{8,10},{9,11},{10,... | collective-permute-start | bytes 786440 | tf_op jit(solution)/shard_map/ppermute | solution.py:32
  191.6 13.9 %collective-permute-start.17 = (bf16[64,2048]{1,0:T(8,128)(2,1)S(1)}, bf16[64,2048]{1,0:T(8,128)(2,1)S(1)}, u32[]{:S(2)}, u32[]{:S(2)}) collective-permute-start(bf16[64,2048]{1,0:T(8,128)(2,1)S(1)} %add_convert_fusion.3), channel_id=1, source_target_pairs={{0,1},{1,2},{2,3},{3,0},{4,5},{5,6},{6,7},{7,4},{8,9},{9,10},{10,1... | collective-permute-start | bytes 786440 | tf_op jit(solution)/shard_map/ppermute | solution.py:32
  221.2 9.7 %collective-permute-start.19 = (bf16[64,2048]{1,0:T(8,128)(2,1)S(1)}, bf16[64,2048]{1,0:T(8,128)(2,1)S(1)}, u32[]{:S(2)}, u32[]{:S(2)}) collective-permute-start(bf16[64,2048]{1,0:T(8,128)(2,1)S(1)} %get-tuple-element.145), channel_id=1, source_target_pairs={{0,1},{1,2},{2,3},{3,0},{4,5},{5,6},{6,7},{7,4},{8,9},{9,10},{10,1... | collective-permute-start | bytes 786440 | tf_op jit(solution)/shard_map/ppermute | solution.py:32
  222.8 14.7 %collective-permute-start.20 = (bf16[64,2048]{1,0:T(8,128)(2,1)S(1)}, bf16[64,2048]{1,0:T(8,128)(2,1)S(1)}, u32[]{:S(2)}, u32[]{:S(2)}) collective-permute-start(bf16[64,2048]{1,0:T(8,128)(2,1)S(1)} %get-tuple-element.147), channel_id=1, source_target_pairs={{0,2},{1,3},{2,0},{3,1},{4,6},{5,7},{6,4},{7,5},{8,10},{9,11},{10,... | collective-permute-start | bytes 786440 | tf_op jit(solution)/shard_map/ppermute | solution.py:32
  225.5 12.1 %collective-permute-start.21 = (bf16[64,2048]{1,0:T(8,128)(2,1)S(1)}, bf16[64,2048]{1,0:T(8,128)(2,1)S(1)}, u32[]{:S(2)}, u32[]{:S(2)}) collective-permute-start(bf16[64,2048]{1,0:T(8,128)(2,1)S(1)} %get-tuple-element.146), channel_id=1, source_target_pairs={{0,3},{1,0},{2,1},{3,2},{4,7},{5,4},{6,5},{7,6},{8,11},{9,8},{10,9... | collective-permute-start | bytes 786440 | tf_op jit(solution)/shard_map/ppermute | solution.py:32
  239.1 10.5 %collective-permute-start.22 = (bf16[64,256]{1,0:T(8,128)(2,1)S(1)}, bf16[64,256]{1,0:T(8,128)(2,1)S(1)}, u32[]{:S(2)}, u32[]{:S(2)}) collective-permute-start(bf16[64,256]{1,0:T(8,128)(2,1)S(1)} %fusion.19), channel_id=1, source_target_pairs={{0,16},{4,20},{8,24},{12,28},{16,32},{20,36},{24,40},{28,44},{32,4... | collective-permute-start | bytes 98312 | tf_op jit(solution)/shard_map/ppermute | solution.py:38
  250.4 9.2 %collective-permute-start.26 = (bf16[320,256]{1,0:T(8,128)(2,1)S(1)}, bf16[320,256]{1,0:T(8,128)(2,1)S(1)}, u32[]{:S(2)}, u32[]{:S(2)}) collective-permute-start(bf16[320,256]{1,0:T(8,128)(2,1)S(1)} %get-tuple-element.292), channel_id=1, source_target_pairs={{0,3},{1,0},{2,1},{3,2},{4,7},{5,4},{6,5},{7,6},{8,11},{9,8},{10,9... | collective-permute-start | bytes 491528 | tf_op jit(solution)/shard_map/ppermute | solution.py:32
  279.1 9.0 %collective-permute-start.29 = (bf16[64,2048]{1,0:T(8,128)(2,1)S(1)}, bf16[64,2048]{1,0:T(8,128)(2,1)S(1)}, u32[]{:S(2)}, u32[]{:S(2)}) collective-permute-start(bf16[64,2048]{1,0:T(8,128)(2,1)S(1)} %add_convert_fusion.1), channel_id=1, source_target_pairs={{0,3},{1,0},{2,1},{3,2},{4,7},{5,4},{6,5},{7,6},{8,11},{9,8},{10,9... | collective-permute-start | bytes 786440 | tf_op jit(solution)/shard_map/ppermute | solution.py:32
  279.5 10.8 %collective-permute-start.30 = (bf16[64,2048]{1,0:T(8,128)(2,1)S(1)}, bf16[64,2048]{1,0:T(8,128)(2,1)S(1)}, u32[]{:S(2)}, u32[]{:S(2)}) collective-permute-start(bf16[64,2048]{1,0:T(8,128)(2,1)S(1)} %add_convert_fusion.1), channel_id=1, source_target_pairs={{0,2},{1,3},{2,0},{3,1},{4,6},{5,7},{6,4},{7,5},{8,10},{9,11},{10,... | collective-permute-start | bytes 786440 | tf_op jit(solution)/shard_map/ppermute | solution.py:32
  281.4 14.4 %collective-permute-start.31 = (bf16[64,2048]{1,0:T(8,128)(2,1)S(1)}, bf16[64,2048]{1,0:T(8,128)(2,1)S(1)}, u32[]{:S(2)}, u32[]{:S(2)}) collective-permute-start(bf16[64,2048]{1,0:T(8,128)(2,1)S(1)} %add_convert_fusion.1), channel_id=1, source_target_pairs={{0,1},{1,2},{2,3},{3,0},{4,5},{5,6},{6,7},{7,4},{8,9},{9,10},{10,1... | collective-permute-start | bytes 786440 | tf_op jit(solution)/shard_map/ppermute | solution.py:32
  316.1 15.2 %collective-permute-start.32 = (bf16[64,2048]{1,0:T(8,128)(2,1)S(1)}, bf16[64,2048]{1,0:T(8,128)(2,1)S(1)}, u32[]{:S(2)}, u32[]{:S(2)}) collective-permute-start(bf16[64,2048]{1,0:T(8,128)(2,1)S(1)} %get-tuple-element.142), channel_id=1, source_target_pairs={{0,1},{1,2},{2,3},{3,0},{4,5},{5,6},{6,7},{7,4},{8,9},{9,10},{10,1... | collective-permute-start | bytes 786440 | tf_op jit(solution)/shard_map/ppermute | solution.py:32
  316.4 14.9 %collective-permute-start.33 = (bf16[64,2048]{1,0:T(8,128)(2,1)S(1)}, bf16[64,2048]{1,0:T(8,128)(2,1)S(1)}, u32[]{:S(2)}, u32[]{:S(2)}) collective-permute-start(bf16[64,2048]{1,0:T(8,128)(2,1)S(1)} %get-tuple-element.144), channel_id=1, source_target_pairs={{0,2},{1,3},{2,0},{3,1},{4,6},{5,7},{6,4},{7,5},{8,10},{9,11},{10,... | collective-permute-start | bytes 786440 | tf_op jit(solution)/shard_map/ppermute | solution.py:32
  318.3 13.6 %collective-permute-start.34 = (bf16[64,2048]{1,0:T(8,128)(2,1)S(1)}, bf16[64,2048]{1,0:T(8,128)(2,1)S(1)}, u32[]{:S(2)}, u32[]{:S(2)}) collective-permute-start(bf16[64,2048]{1,0:T(8,128)(2,1)S(1)} %get-tuple-element.143), channel_id=1, source_target_pairs={{0,3},{1,0},{2,1},{3,2},{4,7},{5,4},{6,5},{7,6},{8,11},{9,8},{10,9... | collective-permute-start | bytes 786440 | tf_op jit(solution)/shard_map/ppermute | solution.py:32
  345.3 10.7 %collective-permute-start.39 = (bf16[320,256]{1,0:T(8,128)(2,1)S(1)}, bf16[320,256]{1,0:T(8,128)(2,1)S(1)}, u32[]{:S(2)}, u32[]{:S(2)}) collective-permute-start(bf16[320,256]{1,0:T(8,128)(2,1)S(1)} %get-tuple-element.166), channel_id=1, source_target_pairs={{0,2},{1,3},{2,0},{3,1},{4,6},{5,7},{6,4},{7,5},{8,10},{9,11},{10,... | collective-permute-start | bytes 491528 | tf_op jit(solution)/shard_map/ppermute | solution.py:32
  357.5 9.6 %collective-permute-start.42 = (bf16[64,256]{1,0:T(8,128)(2,1)S(1)}, bf16[64,256]{1,0:T(8,128)(2,1)S(1)}, u32[]{:S(2)}, u32[]{:S(2)}) collective-permute-start(bf16[64,256]{1,0:T(8,128)(2,1)S(1)} %get-tuple-element.257), channel_id=1, source_target_pairs={{8,0},{12,4},{16,8},{20,12},{24,16},{28,20},{32,24},{36,28},{40,32... | collective-permute-start | bytes 98312 | tf_op jit(solution)/shard_map/ppermute | solution.py:38
  363.5 11.3 %collective-permute-start.35 = (bf16[64,2048]{1,0:T(8,128)(2,1)S(1)}, bf16[64,2048]{1,0:T(8,128)(2,1)S(1)}, u32[]{:S(2)}, u32[]{:S(2)}) collective-permute-start(bf16[64,2048]{1,0:T(8,128)(2,1)S(1)} %get-tuple-element.139), channel_id=1, source_target_pairs={{0,1},{1,2},{2,3},{3,0},{4,5},{5,6},{6,7},{7,4},{8,9},{9,10},{10,1... | collective-permute-start | bytes 786440 | tf_op jit(solution)/shard_map/ppermute | solution.py:32
  364.1 15.8 %collective-permute-start.36 = (bf16[64,2048]{1,0:T(8,128)(2,1)S(1)}, bf16[64,2048]{1,0:T(8,128)(2,1)S(1)}, u32[]{:S(2)}, u32[]{:S(2)}) collective-permute-start(bf16[64,2048]{1,0:T(8,128)(2,1)S(1)} %get-tuple-element.141), channel_id=1, source_target_pairs={{0,2},{1,3},{2,0},{3,1},{4,6},{5,7},{6,4},{7,5},{8,10},{9,11},{10,... | collective-permute-start | bytes 786440 | tf_op jit(solution)/shard_map/ppermute | solution.py:32
  367.2 13.3 %collective-permute-start.37 = (bf16[64,2048]{1,0:T(8,128)(2,1)S(1)}, bf16[64,2048]{1,0:T(8,128)(2,1)S(1)}, u32[]{:S(2)}, u32[]{:S(2)}) collective-permute-start(bf16[64,2048]{1,0:T(8,128)(2,1)S(1)} %get-tuple-element.140), channel_id=1, source_target_pairs={{0,3},{1,0},{2,1},{3,2},{4,7},{5,4},{6,5},{7,6},{8,11},{9,8},{10,9... | collective-permute-start | bytes 786440 | tf_op jit(solution)/shard_map/ppermute | solution.py:32
  371.5 14.6 %collective-permute-start.45 = (bf16[64,2048]{1,0:T(8,128)(2,1)S(1)}, bf16[64,2048]{1,0:T(8,128)(2,1)S(1)}, u32[]{:S(2)}, u32[]{:S(2)}) collective-permute-start(bf16[64,2048]{1,0:T(8,128)(2,1)S(1)} %get-tuple-element.116), channel_id=1, source_target_pairs={{0,3},{1,0},{2,1},{3,2},{4,7},{5,4},{6,5},{7,6},{8,11},{9,8},{10,9... | collective-permute-start | bytes 786440 | tf_op jit(solution)/shard_map/ppermute | solution.py:32
  374.2 11.9 %collective-permute-start.46 = (bf16[64,2048]{1,0:T(8,128)(2,1)S(1)}, bf16[64,2048]{1,0:T(8,128)(2,1)S(1)}, u32[]{:S(2)}, u32[]{:S(2)}) collective-permute-start(bf16[64,2048]{1,0:T(8,128)(2,1)S(1)} %get-tuple-element.116), channel_id=1, source_target_pairs={{0,2},{1,3},{2,0},{3,1},{4,6},{5,7},{6,4},{7,5},{8,10},{9,11},{10,... | collective-permute-start | bytes 786440 | tf_op jit(solution)/shard_map/ppermute | solution.py:32
  374.8 16.3 %collective-permute-start.47 = (bf16[64,2048]{1,0:T(8,128)(2,1)S(1)}, bf16[64,2048]{1,0:T(8,128)(2,1)S(1)}, u32[]{:S(2)}, u32[]{:S(2)}) collective-permute-start(bf16[64,2048]{1,0:T(8,128)(2,1)S(1)} %get-tuple-element.116), channel_id=1, source_target_pairs={{0,1},{1,2},{2,3},{3,0},{4,5},{5,6},{6,7},{7,4},{8,9},{9,10},{10,1... | collective-permute-start | bytes 786440 | tf_op jit(solution)/shard_map/ppermute | solution.py:32
  401.3 9.6 %collective-permute-start.48 = (bf16[64,2048]{1,0:T(8,128)(2,1)S(1)}, bf16[64,2048]{1,0:T(8,128)(2,1)S(1)}, u32[]{:S(2)}, u32[]{:S(2)}) collective-permute-start(bf16[64,2048]{1,0:T(8,128)(2,1)S(1)} %get-tuple-element.136), channel_id=1, source_target_pairs={{0,1},{1,2},{2,3},{3,0},{4,5},{5,6},{6,7},{7,4},{8,9},{9,10},{10,1... | collective-permute-start | bytes 786440 | tf_op jit(solution)/shard_map/ppermute | solution.py:32
  402.3 15.4 %collective-permute-start.49 = (bf16[64,2048]{1,0:T(8,128)(2,1)S(1)}, bf16[64,2048]{1,0:T(8,128)(2,1)S(1)}, u32[]{:S(2)}, u32[]{:S(2)}) collective-permute-start(bf16[64,2048]{1,0:T(8,128)(2,1)S(1)} %get-tuple-element.138), channel_id=1, source_target_pairs={{0,2},{1,3},{2,0},{3,1},{4,6},{5,7},{6,4},{7,5},{8,10},{9,11},{10,... | collective-permute-start | bytes 786440 | tf_op jit(solution)/shard_map/ppermute | solution.py:32
  405.9 11.8 %collective-permute-start.50 = (bf16[64,2048]{1,0:T(8,128)(2,1)S(1)}, bf16[64,2048]{1,0:T(8,128)(2,1)S(1)}, u32[]{:S(2)}, u32[]{:S(2)}) collective-permute-start(bf16[64,2048]{1,0:T(8,128)(2,1)S(1)} %get-tuple-element.137), channel_id=1, source_target_pairs={{0,3},{1,0},{2,1},{3,2},{4,7},{5,4},{6,5},{7,6},{8,11},{9,8},{10,9... | collective-permute-start | bytes 786440 | tf_op jit(solution)/shard_map/ppermute | solution.py:32
  431.3 11.2 %collective-permute-start.53 = (bf16[320,256]{1,0:T(8,128)(2,1)S(1)}, bf16[320,256]{1,0:T(8,128)(2,1)S(1)}, u32[]{:S(2)}, u32[]{:S(2)}) collective-permute-start(bf16[320,256]{1,0:T(8,128)(2,1)S(1)} %get-tuple-element.163), channel_id=1, source_target_pairs={{0,2},{1,3},{2,0},{3,1},{4,6},{5,7},{6,4},{7,5},{8,10},{9,11},{10,... | collective-permute-start | bytes 491528 | tf_op jit(solution)/shard_map/ppermute | solution.py:32
  446.5 10.4 %collective-permute-start.58 = (bf16[64,256]{1,0:T(8,128)(2,1)S(1)}, bf16[64,256]{1,0:T(8,128)(2,1)S(1)}, u32[]{:S(2)}, u32[]{:S(2)}) collective-permute-start(bf16[64,256]{1,0:T(8,128)(2,1)S(1)} %get-tuple-element.251), channel_id=1, source_target_pairs={{16,0},{20,4},{24,8},{28,12},{32,16},{36,20},{40,24},{44,28},{48,3... | collective-permute-start | bytes 98312 | tf_op jit(solution)/shard_map/ppermute | solution.py:38
  449.2 64.5 %collective-permute-start.51 = (bf16[64,2048]{1,0:T(8,128)(2,1)}, bf16[64,2048]{1,0:T(8,128)(2,1)}, u32[]{:S(2)}, u32[]{:S(2)}) collective-permute-start(bf16[64,2048]{1,0:T(8,128)(2,1)} %get-tuple-element.183), channel_id=1, source_target_pairs={{0,64},{64,0},{1,65},{65,1},{2,66},{66,2},{3,67},{67,3},{4,68},{68... | collective-permute-start | bytes 786440 | tf_op jit(solution)/shard_map/ppermute | solution.py:496
  466.3 11.3 %collective-permute-start.60 = (bf16[53,16,128]{2,0,1:T(8,128)(2,1)S(1)}, bf16[53,16,128]{2,0,1:T(8,128)(2,1)S(1)}, u32[]{:S(2)}, u32[]{:S(2)}) collective-permute-start(bf16[53,16,128]{2,0,1:T(8,128)(2,1)S(1)} %get-tuple-element.148), channel_id=1, source_target_pairs={{0,1},{1,2},{2,3},{3,0},{4,5},{5,6},{6,7},{7,4},{8,9},{9,10},{10,1... | collective-permute-start | bytes 651272 | tf_op jit(solution)/shard_map/ppermute | solution.py:32
  466.5 9.4 %collective-permute-start.63 = (bf16[5,16,128]{2,1,0:T(8,128)(2,1)S(1)}, bf16[5,16,128]{2,1,0:T(8,128)(2,1)S(1)}, u32[]{:S(2)}, u32[]{:S(2)}) collective-permute-start(bf16[5,16,128]{2,1,0:T(8,128)(2,1)S(1)} %get-tuple-element.273), channel_id=1, source_target_pairs={{0,1},{1,2},{2,3},{3,0},{4,5},{5,6},{6,7},{7,4},{8,9},{9,10},{10,1... | collective-permute-start | bytes 61448 | tf_op jit(solution)/shard_map/ppermute | solution.py:32
  466.9 9.5 %collective-permute-start.64 = (bf16[5,16,128]{2,1,0:T(8,128)(2,1)S(1)}, bf16[5,16,128]{2,1,0:T(8,128)(2,1)S(1)}, u32[]{:S(2)}, u32[]{:S(2)}) collective-permute-start(bf16[5,16,128]{2,1,0:T(8,128)(2,1)S(1)} %get-tuple-element.275), channel_id=1, source_target_pairs={{0,2},{1,3},{2,0},{3,1},{4,6},{5,7},{6,4},{7,5},{8,10},{9,11},{10,... | collective-permute-start | bytes 61448 | tf_op jit(solution)/shard_map/ppermute | solution.py:32
  476.4 10.6 %collective-permute-start.62 = (bf16[53,16,128]{2,0,1:T(8,128)(2,1)S(1)}, bf16[53,16,128]{2,0,1:T(8,128)(2,1)S(1)}, u32[]{:S(2)}, u32[]{:S(2)}) collective-permute-start(bf16[53,16,128]{2,0,1:T(8,128)(2,1)S(1)} %get-tuple-element.149), channel_id=1, source_target_pairs={{0,3},{1,0},{2,1},{3,2},{4,7},{5,4},{6,5},{7,6},{8,11},{9,8},{10,9... | collective-permute-start | bytes 651272 | tf_op jit(solution)/shard_map/ppermute | solution.py:32
  499.8 11.0 %collective-permute-start.70 = (bf16[2,16,16,128]{3,2,1,0:T(8,128)(2,1)S(1)}, bf16[2,16,16,128]{3,2,1,0:T(8,128)(2,1)S(1)}, u32[]{:S(2)}, u32[]{:S(2)}) collective-permute-start(bf16[2,16,16,128]{3,2,1,0:T(8,128)(2,1)S(1)} %fusion.46), channel_id=1, source_target_pairs={{0,32},{4,36},{8,40},{12,44},{16,48},{20,52},{24,56},{28,60},{32,0... | collective-permute-start | bytes 393224 | tf_op jit(solution)/shard_map/ppermute | solution.py:43
  504.3 19.7 %collective-permute-start.59 = (bf16[64,2048]{1,0:T(8,128)(2,1)S(1)}, bf16[64,2048]{1,0:T(8,128)(2,1)S(1)}, u32[]{:S(2)}, u32[]{:S(2)}) collective-permute-start(bf16[64,2048]{1,0:T(8,128)(2,1)S(1)} %select_convert_fusion), channel_id=1, source_target_pairs={{0,64},{64,0},{1,65},{65,1},{2,66},{66,2},{3,67},{67,3},{4,68},{68... | collective-permute-start | bytes 786440 | tf_op jit(solution)/shard_map/ppermute | solution.py:496
  527.5 10.5 %collective-permute-start.77 = (bf16[2,21,16,128]{3,2,1,0:T(8,128)(2,1)S(1)}, bf16[2,21,16,128]{3,2,1,0:T(8,128)(2,1)S(1)}, u32[]{:S(2)}, u32[]{:S(2)}) collective-permute-start(bf16[2,21,16,128]{3,2,1,0:T(8,128)(2,1)S(1)} %get-tuple-element.176), channel_id=1, source_target_pairs={{0,2},{1,3},{2,0},{3,1},{4,6},{5,7},{6,4},{7,5},{8,10},{9,11},{10,... | collective-permute-start | bytes 516104 | tf_op jit(solution)/shard_map/ppermute | solution.py:32
  (169 other events, 2692.9 us)
Sparse Core Ops, SparseCore 0:
  11.6 123.6 all-gather.3
  138.2 71.9 all-gather.5
  213.1 72.0 all-gather.7

commit v11 on v9

--- a/solution.py
+++ b/solution.py
@@ -313,23 +313,35 @@
     )
 
 
+def own_copies(sources, buffers, sems):
+    copies = [
+        pltpu.make_async_copy(source, buffer, sems.at[i])
+        for i, (source, buffer) in enumerate(zip(sources, buffers))
+    ]
+    for copy in copies:
+        copy.start()
+    return copies
+
+
 def feed_pack(pack_ref, model, hidden):
-    cuts = [model, 2 * model, 2 * model + hidden, 2 * model + 2 * hidden, 3 * model + 2 * hidden]
+    cuts = [0, model, model + hidden, model + 2 * hidden, 2 * model + 2 * hidden]
     return [pack_ref.at[:, a:b] for a, b in zip(cuts[:-1], cuts[1:])]
 
 
 def feed_kernel(
     second_ref, table_ref, bias_ref, pack_ref,
-    active_ref, slope_ref, low_u_ref, low_d_ref, out_ref, buf, sems,
+    active_ref, slope_ref, low_u_ref, low_d_ref, out_ref, buf, sems, pack_buf, own_sems,
 ):
     _, count, chunks, rows, tile = buf.shape
-    su_ref, eu_ref, sd_ref, ed_ref = feed_pack(pack_ref, chunks * rows, count * tile)
+    su_ref, eu_ref, sd_ref, ed_ref = feed_pack(pack_buf, chunks * rows, count * tile)
     copies = feed_copies(table_ref, buf, sems)
+    own = own_copies([pack_ref], [pack_buf], own_sems)
     for up, _ in copies:
         up.start()
     for _, down in copies:
         down.start()
     second = second_ref[...]
+    own[0].wait()
     low_u = against(second, su_ref[...]).astype(bf16)
     low_u_ref[...] = low_u
     for j in range(count):
@@ -353,23 +365,26 @@
 
 def feed_back_kernel(
     branch_ref, table_ref, slope_ref, pack_ref,
-    grad_up_ref, inner_d_ref, inner_u_ref, out_ref, buf, sems,
+    grad_up_ref, inner_d_ref, inner_u_ref, out_ref, buf, sems, pack_buf, slope_buf, own_sems,
 ):
     _, count, chunks, rows, tile = buf.shape
-    su_ref, eu_ref, sd_ref, ed_ref = feed_pack(pack_ref, chunks * rows, count * tile)
+    su_ref, eu_ref, sd_ref, ed_ref = feed_pack(pack_buf, chunks * rows, count * tile)
     copies = feed_copies(table_ref, buf, sems)
+    own = own_copies([pack_ref, slope_ref], [pack_buf, slope_buf], own_sems)
     for _, down in copies:
         down.start()
     for up, _ in copies:
         up.start()
     branch = branch_ref[...]
+    own[0].wait()
     inner_d = against(branch, ed_ref[...]).astype(bf16)
     inner_d_ref[...] = inner_d
+    own[1].wait()
     for j in range(count):
         columns = pl.ds(j * tile, tile)
         copies[j][1].wait()
         grad = plain_chunks(branch, buf, 1, j) + plain(inner_d, sd_ref[:, columns])
-        grad_up_ref[:, columns] = (grad * slope_ref[:, columns].astype(f32)).astype(bf16)
+        grad_up_ref[:, columns] = (grad * slope_buf[:, columns].astype(f32)).astype(bf16)
     inner_u = against(grad_up_ref[...], eu_ref[...]).astype(bf16)
     inner_u_ref[...] = inner_u
     for up, _ in copies:
@@ -384,16 +399,19 @@
 def feed_both_kernel(
     second_ref, branch_ref, table_ref, bias_ref, pack_ref,
     active_ref, low_u_ref, low_d_ref, out_ref, grad_up_ref, inner_d_ref, inner_u_ref, back_ref,
-    buf, sems,
+    buf, sems, pack_buf, branch_buf, own_sems,
 ):
     _, count, chunks, rows, tile = buf.shape
-    su_ref, eu_ref, sd_ref, ed_ref = feed_pack(pack_ref, chunks * rows, count * tile)
+    su_ref, eu_ref, sd_ref, ed_ref = feed_pack(pack_buf, chunks * rows, count * tile)
     copies = feed_copies(table_ref, buf, sems)
+    own = own_copies([pack_ref, branch_ref], [pack_buf, branch_buf], own_sems)
     for up, down in copies:
         up.start()
         down.start()
     second = second_ref[...]
-    branch = branch_ref[...]
+    for copy in own:
+        copy.wait()
+    branch = branch_buf[...]
     low_u = against(second, su_ref[...]).astype(bf16)
     low_u_ref[...] = low_u
     inner_d = against(branch, ed_ref[...]).astype(bf16)
@@ -422,20 +440,24 @@
         ).astype(bf16)
 
 
-def feed_call(kernel, name, inputs, outputs, hidden, matmuls):
+def feed_call(kernel, name, inputs, copied, outputs, hidden, matmuls):
     table = [value for value in inputs if value.ndim == 4][0]
     rows, model = inputs[0].shape
     tile = 512
     chunks = table.shape[0]
     return pl.pallas_call(
         kernel,
-        in_specs=[remote if value.ndim == 4 else held for value in inputs],
+        in_specs=[
+            remote if value.ndim == 4 or i in copied else held for i, value in enumerate(inputs)
+        ],
         out_specs=[held] * len(outputs),
         out_shape=[jax.ShapeDtypeStruct((rows, width), bf16) for width in outputs],
         scratch_shapes=[
             pltpu.VMEM((2, hidden // tile, chunks, model // chunks, tile), bf16),
             pltpu.SemaphoreType.DMA((2, hidden // tile)),
-        ],
+        ]
+        + [pltpu.VMEM(inputs[i].shape, bf16) for i in copied]
+        + [pltpu.SemaphoreType.DMA((len(copied),))],
         compiler_params=pltpu.CompilerParams(vmem_limit_bytes=44 * 2**20),
         cost_estimate=pl.CostEstimate(
             flops=2 * matmuls * rows * model * hidden,
@@ -540,16 +562,24 @@
         cut = shard.shape[1] // 2
         return shard[:, :cut], shard[:, cut:]
 
-    keyval_half = jnp.where(tensor % 2 == 0, keyval_weight[0][:, :head], keyval_weight[0][:, head:])
     early_all = gather_all(
-        jnp.concatenate([query_weight[0], row_major(output_weight[0].T), keyval_half], axis=1)
-    )
-    keyval_ws = [
-        jnp.concatenate(
-            [early_all[x, :, layer, :, 2 * local_q :].reshape(width, head) for x in range(2)], axis=1
-        )
-        for layer in range(2)
-    ]
+        jnp.concatenate([query_weight[0], row_major(output_weight[0].T)], axis=1)
+    )
+
+    def crossed(block, mask):
+        return lax.ppermute(block, both, [(i, i ^ mask) for i in range(8 * chips)])
+
+    shard = keyval_weight[0]
+    pairs = by_layer(
+        jnp.stack([shard, crossed(shard, 2)]),
+        jnp.stack([crossed(shard, 4 * chips), crossed(shard, 4 * chips + 2)]),
+    )
+    quads = jnp.stack(pairs, axis=1)
+    quads = jnp.stack([quads] + [crossed(quads, 4 * k) for k in range(1, chips)])
+    blocks = jnp.stack([quads, crossed(quads, 1)], axis=2)
+    blocks = blocks.reshape((4 * chips, 2) + shard.shape)
+    keyval_all = jnp.take(blocks, jnp.arange(4 * chips, dtype=jnp.int32) ^ data, axis=0, mode="clip")
+    keyval_ws = [keyval_all[:, layer].reshape(width, 2 * head) for layer in range(2)]
 
     vectors = jnp.concatenate(
         [
@@ -575,39 +605,53 @@
     def pack(bank, parts):
         return jnp.concatenate([chosen(table, bank, flip) for table, flip in parts], axis=1)
 
-    def exchanged(parts):
-        return by_layer(pack(own_bank, parts), swap(pack(other_bank, parts)))
-
-    def cut_pack(parts):
-        own = jnp.concatenate([pack(own_bank, parts), query_rows], axis=1)
-        other = jnp.concatenate([pack(other_bank, parts), query_rows], axis=1)
-        return by_layer(own, swap(other))
-
+    cut_parts = [(query_expand, False), (output_shrink, True)]
+    whole_parts = [
+        (query_shrink, True),
+        (keyval_shrink, True),
+        (keyval_expand, False),
+        (output_expand, False),
+        (upward_shrink, True),
+        (upward_expand, False),
+        (downward_shrink, True),
+        (downward_expand, False),
+    ]
     query_rows = jnp.broadcast_to(query_bias, (rank, local_q))
-    cut_layers = jnp.stack(cut_pack([(query_expand, False), (output_shrink, True)]))
-    cut_parts = jnp.stack(
-        [cut_layers] + [around(cut_layers, "tensor", j) for j in range(1, ranks)]
-    )
-    cut_whole = jnp.stack(
+
+    def cut_pack(bank):
+        return jnp.concatenate([pack(bank, cut_parts), query_rows], axis=1)
+
+    shared_parts = [part for part in whole_parts if part[0] is not upward_expand and part[0] is not downward_shrink]
+    split_parts = [(upward_expand, False), (downward_shrink, True)]
+    shared_away = pack(other_bank, shared_parts)
+    quarter = shared_away.shape[1] // ranks
+    crossing = jnp.concatenate(
         [
-            lax.dynamic_index_in_dim(cut_parts, (tensor - r) % ranks, 0, keepdims=False)
-            for r in range(ranks)
+            cut_pack(other_bank),
+            lax.dynamic_slice_in_dim(shared_away, tensor * quarter, quarter, 1),
+            pack(other_bank, split_parts),
         ],
-        axis=2,
-    ).reshape(2, rank, ranks, 3, local_q)
-    eq_all, so_all, query_bias_all = [
-        cut_whole[:, :, :, k].reshape(2, rank, ranks * local_q) for k in range(3)
+        axis=1,
+    )
+    crossed_pack = swap(crossing)
+    cut_width = 3 * local_q
+    block = jnp.concatenate([cut_pack(own_bank), crossed_pack[:, : cut_width + quarter]], axis=1)
+    blocks = jnp.stack([block] + [around(block, "tensor", j) for j in range(1, ranks)])
+    blocks = [
+        lax.dynamic_index_in_dim(blocks, (tensor - r) % ranks, 0, keepdims=False)
+        for r in range(ranks)
     ]
-    early_layers = exchanged([(query_shrink, True), (keyval_shrink, True), (keyval_expand, False)])
-    late_layers = exchanged(
-        [
-            (output_expand, False),
-            (upward_shrink, True),
-            (upward_expand, False),
-            (downward_shrink, True),
-            (downward_expand, False),
-        ]
-    )
+
+    def joined(begin, size):
+        return jnp.concatenate([block[:, begin : begin + size] for block in blocks], axis=1)
+
+    cut_layers = [
+        by_layer(joined(k * local_q, local_q), joined(cut_width + k * local_q, local_q))
+        for k in range(3)
+    ]
+    eq_all, so_all, query_bias_all = cut_layers
+    shared_layers = by_layer(pack(own_bank, shared_parts), joined(2 * cut_width, quarter))
+    split_layers = by_layer(pack(own_bank, split_parts), crossed_pack[:, cut_width + quarter :])
 
     up_halves = halves(upward_weight[0])
     down_halves = halves(row_major(downward_weight[0].T))
@@ -626,10 +670,15 @@
         [part.astype(f32) for part in split(vector_layers[layer], vector_sizes)]
         for layer in range(2)
     ]
-    adapters = [
-        split(early_layers[layer], [width, width, 2 * head]) + [late_layers[layer][:, :width]]
-        for layer in range(2)
-    ]
+    adapters = []
+    feed_packs = []
+    for layer in range(2):
+        sq, skv, ekv, eo, su, ed = split(
+            shared_layers[layer], [width, width, 2 * head, width, width, width]
+        )
+        eu, sd = split(split_layers[layer], [local_f, local_f])
+        adapters.append((sq, skv, ekv, eo))
+        feed_packs.append(jnp.concatenate([su, eu, sd, ed], axis=1))
 
     inside = jnp.arange(rows, dtype=jnp.int32)
     query_place = data * span + tensor * rows + inside
@@ -663,7 +712,7 @@
         pieces = [along(keyval, "dp", back) for back in range(reach, 0, -1)] + [keyval]
         key_block = spread(jnp.concatenate(pieces, axis=0))
         queries, low_q = project_queries(
-            layer, normed, early_all, query_bias_all[layer, :1].astype(f32), eq_all[layer], sq
+            layer, normed, early_all, query_bias_all[layer][:1].astype(f32), eq_all[layer], sq
         )
         probs, mixed, low_o, attended = attend(
             layer, queries, key_block, bias, early_all, so_all[layer], eo, head
@@ -723,9 +772,6 @@
         for k in range(1, chips):
             mine = mine + flipped(at(pile, turn ^ k, 1), "dp", 4 * k).astype(f32)
         return mine.astype(bf16)
-
-    def crossed(block, mask):
-        return lax.ppermute(block, both, [(i, i ^ mask) for i in range(8 * chips)])
 
     def spread_grads(zero, one, shared, quartered, owned):
         own = jnp.where(low_section, zero, one)
@@ -805,13 +851,16 @@
 
     fresh = lax.dynamic_index_in_dim(block_input, section, 0, keepdims=False).astype(f32)
     given = lax.dynamic_index_in_dim(cotangent, section, 0, keepdims=False).astype(f32)
+    branch_one = spread(given.astype(bf16))
+    fresh, branch_one = lax.optimization_barrier((fresh, branch_one))
 
     middle_zero, kept_zero = forward_attend(0, fresh)
     unit_zero, rsd_zero, second_zero, up_bias = feed_inputs(0, middle_zero)
     active_zero, slope_zero, low_u_zero, low_d_zero, partial = feed_call(
         feed_kernel,
         "feed",
-        (second_zero, feed_tables[0], up_bias, late_layers[0]),
+        (second_zero, feed_tables[0], up_bias, feed_packs[0]),
+        (3,),
         (local_f, local_f, rank, rank, width),
         local_f,
         2,
@@ -820,11 +869,11 @@
 
     middle_one, kept_one = forward_attend(1, passed.astype(f32))
     unit_one, rsd_one, second_one, up_bias = feed_inputs(1, middle_one)
-    branch_one = spread(given.astype(bf16))
     active, low_u, low_d, partial, grad_up, inner_d, inner_u, partial_back = feed_call(
         feed_both_kernel,
         "feed_both",
-        (second_one, branch_one, feed_tables[1], up_bias, late_layers[1]),
+        (second_one, branch_one, feed_tables[1], up_bias, feed_packs[1]),
+        (4, 1),
         (local_f, rank, rank, width, local_f, rank, rank, width),
         local_f,
         4,
@@ -842,7 +891,8 @@
     grad_up, inner_d, inner_u, partial_back = feed_call(
         feed_back_kernel,
         "feed_back",
-        (branch_zero, feed_tables[0], slope_zero, late_layers[0]),
+        (branch_zero, feed_tables[0], slope_zero, feed_packs[0]),
+        (3, 2),
         (local_f, rank, rank, width),
         local_f,
         2,
@@ -859,9 +909,9 @@
         grad_up,
     )
     grad_zero, more, quartered = backward_attend(0, kept_zero, grad_middle_zero)
-    shared = shared + more
-    mine = scattered_grads([(shared, quartered, owned), layer_one])
-    grads = spread_grads(mine[0], mine[1], shared, quartered, owned)
+    layer_zero = (shared + more, quartered, owned)
+    mine = scattered_grads([layer_zero, layer_one])
+    grads = spread_grads(mine[0], mine[1], *layer_zero)
 
     def both_micros(zero, one, kind):
         own = jnp.where(low_section, zero, one)

time: 549 us -> 547 us (level)
  waiting for transfers between devices: 232 us -> 217 us
  other arithmetic: 27.8 us -> 34.9 us
    all_gather x1, waiting for transfers between devices: 56.1 us -> 3.54 us  [gather_all(): lax.all_gather(row_major(shard), every, axis=0, tiled=True, axis_index_gr...]
    all_gather x2, waiting for transfers between devices: 14.1 us -> 45.7 us  [gather(): lax.all_gather(row_major(shard), both, axis=0, tiled=True, axis_index_gro...]
    ppermute x7 -> x5, waiting for transfers between devices: 26.3 us -> 12.1 us  [swap(): return lax.ppermute(value, 'section', sides)]
    ppermute x2 -> x9, starting transfers between devices: 3.67 us -> 15.1 us  [crossed(): return lax.ppermute(block, both, [(i, i ^ mask) for i in range(8 * chips)])]
    ppermute x45, waiting for transfers between devices: 108 us -> 118 us  [around(): lax.ppermute(block, axis, [(i, (i + distance) % size) for i in range(size)])]
    ppermute x2 -> x9, waiting for transfers between devices: 2.39 us -> 12.3 us  [crossed(): return lax.ppermute(block, both, [(i, i ^ mask) for i in range(8 * chips)])]
    another operation x7 -> x10, other arithmetic: 0.57 us -> 7.26 us  [the longest x2 5.84 us: per_device(): blocks = jnp.stack([quads, crossed(quads, 1)], axis=2)]
    unnamed x312 -> x324, local copies, waits for them, and re-layouts: 17.7 us -> 15.1 us
  transfers between devices with their start and end apart: 84 -> 89, of which waited for: 52 -> 56; matrix products, arithmetic and copies ran while one was open for 10% -> 11% of each run, Pallas kernels for 7% -> 7%
where the time goes in v11:
time: 547 us; the launch traced here: 537 us
  waiting for transfers between devices  217 us (40%)
  starting transfers between devices  134 us (24%)
  Pallas kernels  85.6 us (16%)
  other arithmetic  34.9 us (6%)
  local copies, waits for them, and re-layouts  33.4 us (6%)
  between operations  21.1 us (4%)
  matrix products  10.3 us (2%)
    ppermute x45, waiting for transfers between devices, around(): lax.ppermute(block, axis, [(i, (i + distance) % size) for i in range(size)])  118 us
    ppermute x45, starting transfers between devices, around(): lax.ppermute(block, axis, [(i, (i + distance) % size) for i in range(size)])  62.9 us
    all_gather x2, waiting for transfers between devices, gather(): lax.all_gather(row_major(shard), both, axis=0, tiled=True, axis_index_gro...  45.7 us
    pallas_call x3, Pallas kernels, feed_call(): pl.pallas_call(kernel, in_specs=[remote if value.ndim == 4 or i in copied...  35.4 us
    ppermute x16, starting transfers between devices, along(): return lax.ppermute(block, axis, route)  28.8 us
    pallas_call x2, Pallas kernels, attend_back(): pl.pallas_call(lambda *refs: attend_back_kernel(layer, head, *refs), in_s...  22.9 us
    pallas_call x2, Pallas kernels, attend(): pl.pallas_call(lambda *refs: attend_kernel(layer, head, *refs), in_specs=...  18.6 us
    ppermute x11, starting transfers between devices, flipped(): return lax.ppermute(block, axis, [(i, i ^ bit) for i in range(size)])  15.1 us
  transfers between devices with their start and end apart: 89, of which 56 were waited for; matrix products, arithmetic and copies ran while one was open for 11% of the time, Pallas kernels for 7%

profile of v11, /device:TPU:0, one launch (start us, length us, event | category | flops | bytes accessed | tf_op | source)
XLA Modules:
  0.0 536.9 jit_solution(16491573681349062950)
XLA Ops:
  11.6 4.0 collective-permute-start.25
  15.7 12.1 %collective-permute-done.25 = bf16[128,2048]{1,0:T(8,128)(2,1)S(1)} collective-permute-done((bf16[128,2048]{1,0:T(8,128)(2,1)S(1)}, bf16[128,2048]{1,0:T(8,128)(2,1)S(1)}, u32[]{:S(2)}, u32[]{:S(2)}) %collective-permute-start.25) | collective-permute-done | bytes 524320 | tf_op jit(solution)/shard_map/ppermute | solution.py:518
  34.0 4.1 collective-permute-start.3
  67.3 4.4 collective-permute-start.11
  83.6 3.7 collective-permute-done.13
  89.8 3.2 collective-permute-done.6
  99.2 3.3 pad_maximum_fusion
  102.5 4.0 gather_fusion
  115.0 3.8 collective-permute-start.18
  122.9 6.8 %collective-permute-done.19 = bf16[320,256]{1,0:T(8,128)(2,1)S(1)} collective-permute-done((bf16[320,256]{1,0:T(8,128)(2,1)S(1)}, bf16[320,256]{1,0:T(8,128)(2,1)S(1)}, u32[]{:S(2)}, u32[]{:S(2)}) %collective-permute-start.19) | collective-permute-done | bytes 163872 | tf_op jit(solution)/shard_map/ppermute | solution.py:32
  131.3 5.2 collective-permute-done.21
  136.6 3.5 all-gather.4.cloned.1.call-done
  140.1 4.3 project_queries.2
  144.5 9.1 %attend.2 = (bf16[4,256,1280]{2,1,0:T(8,128)(2,1)S(1)}, bf16[64,2048]{1,0:T(8,128)(2,1)S(1)}, bf16[64,16]{1,0:T(8,128)(2,1)S(1)}, f32[64,2048]{1,0:T(8,128)S(1)}) custom-call(bf16[64,2048]{1,0:T(8,128)(2,1)S(1)} %get-tuple-element.57.refs_0_.refs_5_, bf16[1280,256]{1,0:T(8,128)(2,1)S(1)} %constant_dynamic-update-slice_fusion.26.refs_1_.refs_6_, ...), custom_call_target="tpu_custom_call" | custom-call | flops 2818572288 | bytes 8388608 | tf_op jit(solution)/shard_map/attend/pallas_call | solution.py:180
  158.7 4.9 collective-permute-done.22
  165.6 4.6 collective-permute-done.24
  170.3 45.7 %all-gather.6.cloned.1.call-done = bf16[4096,2048]{1,0:T(8,128)(2,1)} async-done(((bf16[128,2048]{1,0:T(8,128)(2,1)}), bf16[4096,2048]{1,0:T(8,128)(2,1)}) %all-gather.6.cloned.1.call-update) | async-done | bytes 16777232 | tf_op jit(solution)/shard_map/all_gather | solution.py:552
  216.0 10.9 %feed.1 = (bf16[256,2048]{1,0:T(8,128)(2,1)S(1)}, bf16[256,2048]{1,0:T(8,128)(2,1)S(1)}, bf16[256,16]{1,0:T(8,128)(2,1)S(1)}, bf16[256,16]{1,0:T(8,128)(2,1)S(1)}, bf16[256,2048]{1,0:T(8,128)(2,1)S(1)}) custom-call(bf16[256,2048]{1,0:T(8,128)(2,1)S(1)} %pad_maximum_fusion.3.second_ref, bf16[4,2,512,2048]{3,2,1,0:T(8,128)(2,1)} %bitcast.719, ...), custom_call_target="tpu_custom_call" | custom-call | flops 4294967296 | bytes 16777216 | tf_op jit(solution)/shard_map/feed/pallas_call | solution.py:448
  233.4 3.4 collective-permute-done.26
  236.8 6.5 %collective-permute-done.27 = bf16[64,2048]{1,0:T(8,128)(2,1)S(1)} collective-permute-done((bf16[64,2048]{1,0:T(8,128)(2,1)S(1)}, bf16[64,2048]{1,0:T(8,128)(2,1)S(1)}, u32[]{:S(2)}, u32[]{:S(2)}) %collective-permute-start.27) | collective-permute-done | bytes 262176 | tf_op jit(solution)/shard_map/ppermute | solution.py:32
  244.8 3.4 collective-permute-start.29
  249.6 4.2 collective-permute-start.31
  259.7 4.4 project_queries.3
  267.0 5.0 collective-permute-done.35
  272.0 9.5 %attend.3 = (bf16[4,256,1280]{2,1,0:T(8,128)(2,1)S(1)}, bf16[64,2048]{1,0:T(8,128)(2,1)S(1)}, bf16[64,16]{1,0:T(8,128)(2,1)S(1)}, f32[64,2048]{1,0:T(8,128)S(1)}) custom-call(bf16[64,2048]{1,0:T(8,128)(2,1)S(1)} %get-tuple-element.60.refs_0_.refs_5_, bf16[1280,256]{1,0:T(8,128)(2,1)S(1)} %constant_dynamic-update-slice_fusion.39.refs_1_.refs_6_, ...), custom_call_target="tpu_custom_call" | custom-call | flops 2818572288 | bytes 8388608 | tf_op jit(solution)/shard_map/attend/pallas_call | solution.py:180
  289.1 4.7 collective-permute-done.36
  295.9 5.5 %collective-permute-done.38 = bf16[64,2048]{1,0:T(8,128)(2,1)S(1)} collective-permute-done((bf16[64,2048]{1,0:T(8,128)(2,1)S(1)}, bf16[64,2048]{1,0:T(8,128)(2,1)S(1)}, u32[]{:S(2)}, u32[]{:S(2)}) %collective-permute-start.38) | collective-permute-done | bytes 262176 | tf_op jit(solution)/shard_map/ppermute | solution.py:32
  305.3 14.5 %feed_both.1 = (bf16[256,2048]{1,0:T(8,128)(2,1)S(1)}, bf16[256,16]{1,0:T(8,128)(2,1)S(1)}, bf16[256,16]{1,0:T(8,128)(2,1)S(1)}, bf16[256,2048]{1,0:T(8,128)(2,1...) custom-call(bf16[256,2048]{1,0:T(8,128)(2,1)S(1)} %copy-done.2, ...), custom_call_target="tpu_custom_call" | custom-call | flops 8589934592 | bytes 16777216 | tf_op jit(solution)/shard_map/feed_both/pallas_call | solution.py:448
  325.7 9.4 %collective-permute-done.39 = bf16[64,2048]{1,0:T(8,128)(2,1)S(1)} collective-permute-done((bf16[64,2048]{1,0:T(8,128)(2,1)S(1)}, bf16[64,2048]{1,0:T(8,128)(2,1)S(1)}, u32[]{:S(2)}, u32[]{:S(2)}) %collective-permute-start.39) | collective-permute-done | bytes 262176 | tf_op jit(solution)/shard_map/ppermute | solution.py:32
  336.5 11.5 %attend_back.2 = (bf16[64,2048]{1,0:T(8,128)(2,1)S(1)}, bf16[1280,256]{1,0:T(8,128)(2,1)S(1)}, bf16[64,16]{1,0:T(8,128)(2,1)S(1)}, bf16[64,16]{1,0:T(8,128)(2,1)S(1)}, f32[64,2048]{1,0:T(8,128)S(1)}) custom-call(bf16[64,2048]{1,0:T(8,128)(2,1)S(1)} %get-tuple-element.121.refs_0_, bf16[4,4,2,512,1024]{4,3,2,1,0:T(8,128)(2,1)} %bitcast.717, ...), custom_call_target="tpu_custom_call" | custom-call | flops 5637144576 | bytes 22020096 | tf_op jit(solution)/shard_map/attend_back/pallas_call | solution.py:259
  349.1 3.1 collective-permute-start.46
  355.3 5.5 %collective-permute-done.46 = bf16[320,256]{1,0:T(8,128)(2,1)S(1)} collective-permute-done((bf16[320,256]{1,0:T(8,128)(2,1)S(1)}, bf16[320,256]{1,0:T(8,128)(2,1)S(1)}, u32[]{:S(2)}, u32[]{:S(2)}) %collective-permute-start.46) | collective-permute-done | bytes 163872 | tf_op jit(solution)/shard_map/ppermute | solution.py:32
  381.0 5.4 %collective-permute-done.52 = bf16[64,2048]{1,0:T(8,128)(2,1)S(1)} collective-permute-done((bf16[64,2048]{1,0:T(8,128)(2,1)S(1)}, bf16[64,2048]{1,0:T(8,128)(2,1)S(1)}, u32[]{:S(2)}, u32[]{:S(2)}) %collective-permute-start.52) | collective-permute-done | bytes 262176 | tf_op jit(solution)/shard_map/ppermute | solution.py:32
  388.7 3.8 collective-permute-done.54
  392.6 10.0 %feed_back.1 = (bf16[256,2048]{1,0:T(8,128)(2,1)S(1)}, bf16[256,16]{1,0:T(8,128)(2,1)S(1)}, bf16[256,16]{1,0:T(8,128)(2,1)S(1)}, bf16[256,2048]{1,0:T(8,128)(2,1)S(1)}) custom-call(bf16[256,2048]{1,0:T(8,128)(2,1)S(1)} %pad_maximum_fusion.5.branch_ref, bf16[4,2,512,2048]{3,2,1,0:T(8,128)(2,1)} %bitcast.720, bf16[256,2048]{1,0:T(8,128)(2,1)S(1)} %copy-done.16, ...), custom_call_target="tpu_custom_call" | custom-call | flops 4294967296 | bytes 16777216 | tf_op jit(solution)/shard_map/feed_back/pallas_call | solution.py:448
  403.5 3.1 collective-permute-start.56
  408.2 4.3 collective-permute-done.55
  412.5 5.9 %collective-permute-done.56 = bf16[64,2048]{1,0:T(8,128)(2,1)S(1)} collective-permute-done((bf16[64,2048]{1,0:T(8,128)(2,1)S(1)}, bf16[64,2048]{1,0:T(8,128)(2,1)S(1)}, u32[]{:S(2)}, u32[]{:S(2)}) %collective-permute-start.56) | collective-permute-done | bytes 262176 | tf_op jit(solution)/shard_map/ppermute | solution.py:32
  419.2 11.5 %attend_back.3 = (bf16[64,2048]{1,0:T(8,128)(2,1)S(1)}, bf16[1280,256]{1,0:T(8,128)(2,1)S(1)}, bf16[64,16]{1,0:T(8,128)(2,1)S(1)}, bf16[64,16]{1,0:T(8,128)(2,1)S(1)}, f32[64,2048]{1,0:T(8,128)S(1)}) custom-call(bf16[64,2048]{1,0:T(8,128)(2,1)S(1)} %get-tuple-element.113.refs_0_, bf16[4,4,2,512,1024]{4,3,2,1,0:T(8,128)(2,1)} %bitcast.718, ...), custom_call_target="tpu_custom_call" | custom-call | flops 5637144576 | bytes 22020096 | tf_op jit(solution)/shard_map/attend_back/pallas_call | solution.py:259
  431.3 3.6 collective-permute-start.60
  437.8 4.7 collective-permute-done.60
  452.3 3.6 collective-permute-done.65
  459.5 3.1 collective-permute-start.68
  463.2 5.3 collective-permute-done.67
  468.5 4.7 collective-permute-done.68
  476.9 3.8 collective-permute-done.71
  513.1 3.5 collective-permute-start.84
  520.5 4.2 collective-permute-done.84
  (695 shorter events, 206.9 us)
Async XLA Ops:
  7.2 132.9 %all-gather.4.cloned.1.call-start = ((), (), s32[]{:S(2)}) async-start(), calls=%async_computation | async-start | bytes 33816576 | tf_op jit(solution)/shard_map/all_gather | solution.py:556
  10.0 206.0 %all-gather.6.cloned.1.call-start = ((), (), s32[]{:S(2)}) async-start(), calls=%async_computation.1 | async-start | bytes 17301504 | tf_op jit(solution)/shard_map/all_gather | solution.py:552
  11.6 16.2 %collective-permute-start.25 = (bf16[128,2048]{1,0:T(8,128)(2,1)S(1)}, bf16[128,2048]{1,0:T(8,128)(2,1)S(1)}, u32[]{:S(2)}, u32[]{:S(2)}) collective-permute-start(bf16[128,2048]{1,0:T(8,128)(2,1)S(1)} %broadcast_select_fusion.2), channel_id=1, source_target_pairs={{0,64},{64,0},{1,65},{65,1},{2,66},{66,2},{3,67},{67,3},{4,68},{68... | collective-permute-start | bytes 1572872 | tf_op jit(solution)/shard_map/ppermute | solution.py:518
  29.1 273.3 %all-gather.8.cloned.1.call-start = ((), (), s32[]{:S(2)}) async-start(), calls=%async_computation.2 | async-start | bytes 17301504 | tf_op jit(solution)/shard_map/all_gather | solution.py:552
  29.2 42.5 %collective-permute-start = (bf16[64,2048]{1,0:T(8,128)(2,1)S(1)}, bf16[64,2048]{1,0:T(8,128)(2,1)S(1)}, u32[]{:S(2)}, u32[]{:S(2)}) collective-permute-start(bf16[64,2048]{1,0:T(8,128)(2,1)S(1)} %dynamic-slice_bitcast_fusion), channel_id=1, source_target_pairs={{0,3},{1,0},{2,1},{3,2},{4,7},{5,4},{6,5},{7,6},{8,11},{9,8},{10,9... | collective-permute-start | bytes 786440 | tf_op jit(solution)/shard_map/ppermute | solution.py:32
  32.1 42.4 %collective-permute-start.1 = (bf16[64,2048]{1,0:T(8,128)(2,1)S(1)}, bf16[64,2048]{1,0:T(8,128)(2,1)S(1)}, u32[]{:S(2)}, u32[]{:S(2)}) collective-permute-start(bf16[64,2048]{1,0:T(8,128)(2,1)S(1)} %dynamic-slice_bitcast_fusion), channel_id=1, source_target_pairs={{0,2},{1,3},{2,0},{3,1},{4,6},{5,7},{6,4},{7,5},{8,10},{9,11},{10,... | collective-permute-start | bytes 786440 | tf_op jit(solution)/shard_map/ppermute | solution.py:32
  32.9 42.3 %collective-permute-start.2 = (bf16[64,2048]{1,0:T(8,128)(2,1)S(1)}, bf16[64,2048]{1,0:T(8,128)(2,1)}, u32[]{:S(2)}, u32[]{:S(2)}) collective-permute-start(bf16[64,2048]{1,0:T(8,128)(2,1)S(1)} %dynamic-slice_bitcast_fusion), channel_id=1, source_target_pairs={{0,1},{1,2},{2,3},{3,0},{4,5},{5,6},{6,7},{7,4},{8,9},{9,10},{10,1... | collective-permute-start | bytes 786440 | tf_op jit(solution)/shard_map/ppermute | solution.py:32
  34.0 22.6 %collective-permute-start.3 = (bf16[1,14592]{1,0:T(2,128)(2,1)S(1)}, bf16[1,14592]{1,0:T(2,128)(2,1)S(1)}, u32[]{:S(2)}, u32[]{:S(2)}) collective-permute-start(bf16[1,14592]{1,0:T(2,128)(2,1)S(1)} %constant_dynamic-update-slice_fusion), channel_id=1, source_target_pairs={{0,64},{64,0},{1,65},{65,1},{2,66},{66,2},{3,67},{67,3},{4,68},{68... | collective-permute-start | bytes 87560 | tf_op jit(solution)/shard_map/ppermute | solution.py:518
  38.1 20.2 %collective-permute-start.8 = (bf16[128,256]{1,0:T(8,128)(2,1)S(1)}, bf16[128,256]{1,0:T(8,128)(2,1)S(1)}, u32[]{:S(2)}, u32[]{:S(2)}) collective-permute-start(bf16[128,256]{1,0:T(8,128)(2,1)S(1)} %bitcast.786), channel_id=1, source_target_pairs={{0,8},{4,12},{8,0},{12,4},{16,24},{20,28},{24,16},{28,20},{32,40},... | collective-permute-start | bytes 196616 | tf_op jit(solution)/shard_map/ppermute | solution.py:570
  64.2 12.7 %collective-permute-start.4 = (bf16[16,8256]{1,0:T(8,128)(2,1)S(1)}, bf16[16,8256]{1,0:T(8,128)(2,1)S(1)}, u32[]{:S(2)}, u32[]{:S(2)}) collective-permute-start(bf16[16,8256]{1,0:T(8,128)(2,1)S(1)} %concatenate.231), channel_id=1, source_target_pairs={{0,64},{64,0},{1,65},{65,1},{2,66},{66,2},{3,67},{67,3},{4,68},{68... | collective-permute-start | bytes 792584 | tf_op jit(solution)/shard_map/ppermute | solution.py:518
  67.3 13.9 %collective-permute-start.11 = (bf16[2,2,128,256]{3,2,1,0:T(8,128)(2,1)}, bf16[2,2,128,256]{3,2,1,0:T(8,128)(2,1)S(1)}, u32[]{:S(2)}, u32[]{:S(2)}) collective-permute-start(bf16[2,2,128,256]{3,2,1,0:T(8,128)(2,1)} %get-tuple-element.224), channel_id=1, source_target_pairs={{0,16},{4,20},{8,24},{12,28},{16,0},{20,4},{24,8},{28,12},{32,48},... | collective-permute-start | bytes 786440 | tf_op jit(solution)/shard_map/ppermute | solution.py:570
  71.8 11.8 %collective-permute-start.12 = (bf16[2,2,128,256]{3,2,1,0:T(8,128)(2,1)}, bf16[2,2,128,256]{3,2,1,0:T(8,128)(2,1)}, u32[]{:S(2)}, u32[]{:S(2)}) collective-permute-start(bf16[2,2,128,256]{3,2,1,0:T(8,128)(2,1)} %get-tuple-element.224), channel_id=1, source_target_pairs={{0,32},{4,36},{8,40},{12,44},{16,48},{20,52},{24,56},{28,60},{32,0... | collective-permute-start | bytes 786440 | tf_op jit(solution)/shard_map/ppermute | solution.py:570
  74.5 12.8 %collective-permute-start.13 = (bf16[2,2,128,256]{3,2,1,0:T(8,128)(2,1)}, bf16[2,2,128,256]{3,2,1,0:T(8,128)(2,1)}, u32[]{:S(2)}, u32[]{:S(2)}) collective-permute-start(bf16[2,2,128,256]{3,2,1,0:T(8,128)(2,1)} %get-tuple-element.224), channel_id=1, source_target_pairs={{0,48},{4,52},{8,56},{12,60},{16,32},{20,36},{24,40},{28,44},{32,1... | collective-permute-start | bytes 786440 | tf_op jit(solution)/shard_map/ppermute | solution.py:570
  77.0 12.8 %collective-permute-start.5 = (bf16[16,5696]{1,0:T(8,128)(2,1)S(1)}, bf16[16,5696]{1,0:T(8,128)(2,1)S(1)}, u32[]{:S(2)}, u32[]{:S(2)}) collective-permute-start(bf16[16,5696]{1,0:T(8,128)(2,1)S(1)} %get-tuple-element.254), channel_id=1, source_target_pairs={{0,1},{1,2},{2,3},{3,0},{4,5},{5,6},{6,7},{7,4},{8,9},{9,10},{10,1... | collective-permute-start | bytes 546824 | tf_op jit(solution)/shard_map/ppermute | solution.py:32
  78.6 14.5 %collective-permute-start.6 = (bf16[16,5696]{1,0:T(8,128)(2,1)S(1)}, bf16[16,5696]{1,0:T(8,128)(2,1)S(1)}, u32[]{:S(2)}, u32[]{:S(2)}) collective-permute-start(bf16[16,5696]{1,0:T(8,128)(2,1)S(1)} %get-tuple-element.254), channel_id=1, source_target_pairs={{0,2},{1,3},{2,0},{3,1},{4,6},{5,7},{6,4},{7,5},{8,10},{9,11},{10,... | collective-permute-start | bytes 546824 | tf_op jit(solution)/shard_map/ppermute | solution.py:32
  81.2 12.9 %collective-permute-start.7 = (bf16[16,5696]{1,0:T(8,128)(2,1)S(1)}, bf16[16,5696]{1,0:T(8,128)(2,1)S(1)}, u32[]{:S(2)}, u32[]{:S(2)}) collective-permute-start(bf16[16,5696]{1,0:T(8,128)(2,1)S(1)} %get-tuple-element.254), channel_id=1, source_target_pairs={{0,3},{1,0},{2,1},{3,2},{4,7},{5,4},{6,5},{7,6},{8,11},{9,8},{10,9... | collective-permute-start | bytes 546824 | tf_op jit(solution)/shard_map/ppermute | solution.py:32
  119.7 10.0 %collective-permute-start.19 = (bf16[320,256]{1,0:T(8,128)(2,1)S(1)}, bf16[320,256]{1,0:T(8,128)(2,1)S(1)}, u32[]{:S(2)}, u32[]{:S(2)}) collective-permute-start(bf16[320,256]{1,0:T(8,128)(2,1)S(1)} %get-tuple-element.320), channel_id=1, source_target_pairs={{0,3},{1,0},{2,1},{3,2},{4,7},{5,4},{6,5},{7,6},{8,11},{9,8},{10,9... | collective-permute-start | bytes 491528 | tf_op jit(solution)/shard_map/ppermute | solution.py:32
  119.8 11.5 %collective-permute-start.20 = (bf16[320,256]{1,0:T(8,128)(2,1)S(1)}, bf16[320,256]{1,0:T(8,128)(2,1)S(1)}, u32[]{:S(2)}, u32[]{:S(2)}) collective-permute-start(bf16[320,256]{1,0:T(8,128)(2,1)S(1)} %get-tuple-element.320), channel_id=1, source_target_pairs={{0,2},{1,3},{2,0},{3,1},{4,6},{5,7},{6,4},{7,5},{8,10},{9,11},{10,... | collective-permute-start | bytes 491528 | tf_op jit(solution)/shard_map/ppermute | solution.py:32
  121.1 15.4 %collective-permute-start.21 = (bf16[320,256]{1,0:T(8,128)(2,1)S(1)}, bf16[320,256]{1,0:T(8,128)(2,1)S(1)}, u32[]{:S(2)}, u32[]{:S(2)}) collective-permute-start(bf16[320,256]{1,0:T(8,128)(2,1)S(1)} %get-tuple-element.320), channel_id=1, source_target_pairs={{0,1},{1,2},{2,3},{3,0},{4,5},{5,6},{6,7},{7,4},{8,9},{9,10},{10,1... | collective-permute-start | bytes 491528 | tf_op jit(solution)/shard_map/ppermute | solution.py:32
  154.9 10.7 %collective-permute-start.23 = (bf16[64,2048]{1,0:T(8,128)(2,1)S(1)}, bf16[64,2048]{1,0:T(8,128)(2,1)S(1)}, u32[]{:S(2)}, u32[]{:S(2)}) collective-permute-start(bf16[64,2048]{1,0:T(8,128)(2,1)S(1)} %add_convert_fusion.3), channel_id=1, source_target_pairs={{0,2},{1,3},{2,0},{3,1},{4,6},{5,7},{6,4},{7,5},{8,10},{9,11},{10,... | collective-permute-start | bytes 786440 | tf_op jit(solution)/shard_map/ppermute | solution.py:32
  157.9 12.3 %collective-permute-start.24 = (bf16[64,2048]{1,0:T(8,128)(2,1)S(1)}, bf16[64,2048]{1,0:T(8,128)(2,1)S(1)}, u32[]{:S(2)}, u32[]{:S(2)}) collective-permute-start(bf16[64,2048]{1,0:T(8,128)(2,1)S(1)} %add_convert_fusion.3), channel_id=1, source_target_pairs={{0,1},{1,2},{2,3},{3,0},{4,5},{5,6},{6,7},{7,4},{8,9},{9,10},{10,1... | collective-permute-start | bytes 786440 | tf_op jit(solution)/shard_map/ppermute | solution.py:32
  227.0 9.8 %collective-permute-start.26 = (bf16[64,2048]{1,0:T(8,128)(2,1)S(1)}, bf16[64,2048]{1,0:T(8,128)(2,1)S(1)}, u32[]{:S(2)}, u32[]{:S(2)}) collective-permute-start(bf16[64,2048]{1,0:T(8,128)(2,1)S(1)} %get-tuple-element.143), channel_id=1, source_target_pairs={{0,1},{1,2},{2,3},{3,0},{4,5},{5,6},{6,7},{7,4},{8,9},{9,10},{10,1... | collective-permute-start | bytes 786440 | tf_op jit(solution)/shard_map/ppermute | solution.py:32
  228.6 14.7 %collective-permute-start.27 = (bf16[64,2048]{1,0:T(8,128)(2,1)S(1)}, bf16[64,2048]{1,0:T(8,128)(2,1)S(1)}, u32[]{:S(2)}, u32[]{:S(2)}) collective-permute-start(bf16[64,2048]{1,0:T(8,128)(2,1)S(1)} %get-tuple-element.145), channel_id=1, source_target_pairs={{0,2},{1,3},{2,0},{3,1},{4,6},{5,7},{6,4},{7,5},{8,10},{9,11},{10,... | collective-permute-start | bytes 786440 | tf_op jit(solution)/shard_map/ppermute | solution.py:32
  231.3 12.1 %collective-permute-start.28 = (bf16[64,2048]{1,0:T(8,128)(2,1)S(1)}, bf16[64,2048]{1,0:T(8,128)(2,1)S(1)}, u32[]{:S(2)}, u32[]{:S(2)}) collective-permute-start(bf16[64,2048]{1,0:T(8,128)(2,1)S(1)} %get-tuple-element.144), channel_id=1, source_target_pairs={{0,3},{1,0},{2,1},{3,2},{4,7},{5,4},{6,5},{7,6},{8,11},{9,8},{10,9... | collective-permute-start | bytes 786440 | tf_op jit(solution)/shard_map/ppermute | solution.py:32
  244.8 10.5 %collective-permute-start.29 = (bf16[64,256]{1,0:T(8,128)(2,1)S(1)}, bf16[64,256]{1,0:T(8,128)(2,1)S(1)}, u32[]{:S(2)}, u32[]{:S(2)}) collective-permute-start(bf16[64,256]{1,0:T(8,128)(2,1)S(1)} %fusion.19), channel_id=1, source_target_pairs={{0,16},{4,20},{8,24},{12,28},{16,32},{20,36},{24,40},{28,44},{32,4... | collective-permute-start | bytes 98312 | tf_op jit(solution)/shard_map/ppermute | solution.py:38
  256.2 9.9 %collective-permute-start.33 = (bf16[320,256]{1,0:T(8,128)(2,1)S(1)}, bf16[320,256]{1,0:T(8,128)(2,1)S(1)}, u32[]{:S(2)}, u32[]{:S(2)}) collective-permute-start(bf16[320,256]{1,0:T(8,128)(2,1)S(1)} %get-tuple-element.310), channel_id=1, source_target_pairs={{0,3},{1,0},{2,1},{3,2},{4,7},{5,4},{6,5},{7,6},{8,11},{9,8},{10,9... | collective-permute-start | bytes 491528 | tf_op jit(solution)/shard_map/ppermute | solution.py:32
  285.1 10.8 %collective-permute-start.37 = (bf16[64,2048]{1,0:T(8,128)(2,1)S(1)}, bf16[64,2048]{1,0:T(8,128)(2,1)S(1)}, u32[]{:S(2)}, u32[]{:S(2)}) collective-permute-start(bf16[64,2048]{1,0:T(8,128)(2,1)S(1)} %add_convert_fusion.1), channel_id=1, source_target_pairs={{0,2},{1,3},{2,0},{3,1},{4,6},{5,7},{6,4},{7,5},{8,10},{9,11},{10,... | collective-permute-start | bytes 786440 | tf_op jit(solution)/shard_map/ppermute | solution.py:32
  287.0 14.4 %collective-permute-start.38 = (bf16[64,2048]{1,0:T(8,128)(2,1)S(1)}, bf16[64,2048]{1,0:T(8,128)(2,1)S(1)}, u32[]{:S(2)}, u32[]{:S(2)}) collective-permute-start(bf16[64,2048]{1,0:T(8,128)(2,1)S(1)} %add_convert_fusion.1), channel_id=1, source_target_pairs={{0,1},{1,2},{2,3},{3,0},{4,5},{5,6},{6,7},{7,4},{8,9},{9,10},{10,1... | collective-permute-start | bytes 786440 | tf_op jit(solution)/shard_map/ppermute | solution.py:32
  319.9 15.2 %collective-permute-start.39 = (bf16[64,2048]{1,0:T(8,128)(2,1)S(1)}, bf16[64,2048]{1,0:T(8,128)(2,1)S(1)}, u32[]{:S(2)}, u32[]{:S(2)}) collective-permute-start(bf16[64,2048]{1,0:T(8,128)(2,1)S(1)} %get-tuple-element.140), channel_id=1, source_target_pairs={{0,1},{1,2},{2,3},{3,0},{4,5},{5,6},{6,7},{7,4},{8,9},{9,10},{10,1... | collective-permute-start | bytes 786440 | tf_op jit(solution)/shard_map/ppermute | solution.py:32
  320.2 14.9 %collective-permute-start.40 = (bf16[64,2048]{1,0:T(8,128)(2,1)S(1)}, bf16[64,2048]{1,0:T(8,128)(2,1)S(1)}, u32[]{:S(2)}, u32[]{:S(2)}) collective-permute-start(bf16[64,2048]{1,0:T(8,128)(2,1)S(1)} %get-tuple-element.142), channel_id=1, source_target_pairs={{0,2},{1,3},{2,0},{3,1},{4,6},{5,7},{6,4},{7,5},{8,10},{9,11},{10,... | collective-permute-start | bytes 786440 | tf_op jit(solution)/shard_map/ppermute | solution.py:32
  322.1 13.6 %collective-permute-start.41 = (bf16[64,2048]{1,0:T(8,128)(2,1)S(1)}, bf16[64,2048]{1,0:T(8,128)(2,1)S(1)}, u32[]{:S(2)}, u32[]{:S(2)}) collective-permute-start(bf16[64,2048]{1,0:T(8,128)(2,1)S(1)} %get-tuple-element.141), channel_id=1, source_target_pairs={{0,3},{1,0},{2,1},{3,2},{4,7},{5,4},{6,5},{7,6},{8,11},{9,8},{10,9... | collective-permute-start | bytes 786440 | tf_op jit(solution)/shard_map/ppermute | solution.py:32
  349.1 11.6 %collective-permute-start.46 = (bf16[320,256]{1,0:T(8,128)(2,1)S(1)}, bf16[320,256]{1,0:T(8,128)(2,1)S(1)}, u32[]{:S(2)}, u32[]{:S(2)}) collective-permute-start(bf16[320,256]{1,0:T(8,128)(2,1)S(1)} %get-tuple-element.166), channel_id=1, source_target_pairs={{0,2},{1,3},{2,0},{3,1},{4,6},{5,7},{6,4},{7,5},{8,10},{9,11},{10,... | collective-permute-start | bytes 491528 | tf_op jit(solution)/shard_map/ppermute | solution.py:32
  353.1 25.5 %collective-permute-start.42 = (bf16[64,2048]{1,0:T(8,128)(2,1)S(1)}, bf16[64,2048]{1,0:T(8,128)(2,1)S(1)}, u32[]{:S(2)}, u32[]{:S(2)}) collective-permute-start(bf16[64,2048]{1,0:T(8,128)(2,1)S(1)} %get-tuple-element.137), channel_id=1, source_target_pairs={{0,1},{1,2},{2,3},{3,0},{4,5},{5,6},{6,7},{7,4},{8,9},{9,10},{10,1... | collective-permute-start | bytes 786440 | tf_op jit(solution)/shard_map/ppermute | solution.py:32
  366.1 13.2 %collective-permute-start.43 = (bf16[64,2048]{1,0:T(8,128)(2,1)S(1)}, bf16[64,2048]{1,0:T(8,128)(2,1)S(1)}, u32[]{:S(2)}, u32[]{:S(2)}) collective-permute-start(bf16[64,2048]{1,0:T(8,128)(2,1)S(1)} %get-tuple-element.139), channel_id=1, source_target_pairs={{0,2},{1,3},{2,0},{3,1},{4,6},{5,7},{6,4},{7,5},{8,10},{9,11},{10,... | collective-permute-start | bytes 786440 | tf_op jit(solution)/shard_map/ppermute | solution.py:32
  368.1 12.7 %collective-permute-start.44 = (bf16[64,2048]{1,0:T(8,128)(2,1)S(1)}, bf16[64,2048]{1,0:T(8,128)(2,1)S(1)}, u32[]{:S(2)}, u32[]{:S(2)}) collective-permute-start(bf16[64,2048]{1,0:T(8,128)(2,1)S(1)} %get-tuple-element.138), channel_id=1, source_target_pairs={{0,3},{1,0},{2,1},{3,2},{4,7},{5,4},{6,5},{7,6},{8,11},{9,8},{10,9... | collective-permute-start | bytes 786440 | tf_op jit(solution)/shard_map/ppermute | solution.py:32
  375.0 11.4 %collective-permute-start.52 = (bf16[64,2048]{1,0:T(8,128)(2,1)S(1)}, bf16[64,2048]{1,0:T(8,128)(2,1)S(1)}, u32[]{:S(2)}, u32[]{:S(2)}) collective-permute-start(bf16[64,2048]{1,0:T(8,128)(2,1)S(1)} %get-tuple-element.116), channel_id=1, source_target_pairs={{0,3},{1,0},{2,1},{3,2},{4,7},{5,4},{6,5},{7,6},{8,11},{9,8},{10,9... | collective-permute-start | bytes 786440 | tf_op jit(solution)/shard_map/ppermute | solution.py:32
  377.7 11.0 %collective-permute-start.53 = (bf16[64,2048]{1,0:T(8,128)(2,1)S(1)}, bf16[64,2048]{1,0:T(8,128)(2,1)S(1)}, u32[]{:S(2)}, u32[]{:S(2)}) collective-permute-start(bf16[64,2048]{1,0:T(8,128)(2,1)S(1)} %get-tuple-element.116), channel_id=1, source_target_pairs={{0,2},{1,3},{2,0},{3,1},{4,6},{5,7},{6,4},{7,5},{8,10},{9,11},{10,... | collective-permute-start | bytes 786440 | tf_op jit(solution)/shard_map/ppermute | solution.py:32
  378.7 13.9 %collective-permute-start.54 = (bf16[64,2048]{1,0:T(8,128)(2,1)S(1)}, bf16[64,2048]{1,0:T(8,128)(2,1)S(1)}, u32[]{:S(2)}, u32[]{:S(2)}) collective-permute-start(bf16[64,2048]{1,0:T(8,128)(2,1)S(1)} %get-tuple-element.116), channel_id=1, source_target_pairs={{0,1},{1,2},{2,3},{3,0},{4,5},{5,6},{6,7},{7,4},{8,9},{9,10},{10,1... | collective-permute-start | bytes 786440 | tf_op jit(solution)/shard_map/ppermute | solution.py:32
  402.8 9.8 %collective-permute-start.55 = (bf16[64,2048]{1,0:T(8,128)(2,1)S(1)}, bf16[64,2048]{1,0:T(8,128)(2,1)S(1)}, u32[]{:S(2)}, u32[]{:S(2)}) collective-permute-start(bf16[64,2048]{1,0:T(8,128)(2,1)S(1)} %get-tuple-element.134), channel_id=1, source_target_pairs={{0,1},{1,2},{2,3},{3,0},{4,5},{5,6},{6,7},{7,4},{8,9},{9,10},{10,1... | collective-permute-start | bytes 786440 | tf_op jit(solution)/shard_map/ppermute | solution.py:32
  403.5 15.0 %collective-permute-start.56 = (bf16[64,2048]{1,0:T(8,128)(2,1)S(1)}, bf16[64,2048]{1,0:T(8,128)(2,1)S(1)}, u32[]{:S(2)}, u32[]{:S(2)}) collective-permute-start(bf16[64,2048]{1,0:T(8,128)(2,1)S(1)} %get-tuple-element.136), channel_id=1, source_target_pairs={{0,2},{1,3},{2,0},{3,1},{4,6},{5,7},{6,4},{7,5},{8,10},{9,11},{10,... | collective-permute-start | bytes 786440 | tf_op jit(solution)/shard_map/ppermute | solution.py:32
  406.5 12.0 %collective-permute-start.57 = (bf16[64,2048]{1,0:T(8,128)(2,1)S(1)}, bf16[64,2048]{1,0:T(8,128)(2,1)S(1)}, u32[]{:S(2)}, u32[]{:S(2)}) collective-permute-start(bf16[64,2048]{1,0:T(8,128)(2,1)S(1)} %get-tuple-element.135), channel_id=1, source_target_pairs={{0,3},{1,0},{2,1},{3,2},{4,7},{5,4},{6,5},{7,6},{8,11},{9,8},{10,9... | collective-permute-start | bytes 786440 | tf_op jit(solution)/shard_map/ppermute | solution.py:32
  431.3 11.2 %collective-permute-start.60 = (bf16[320,256]{1,0:T(8,128)(2,1)S(1)}, bf16[320,256]{1,0:T(8,128)(2,1)S(1)}, u32[]{:S(2)}, u32[]{:S(2)}) collective-permute-start(bf16[320,256]{1,0:T(8,128)(2,1)S(1)} %get-tuple-element.163), channel_id=1, source_target_pairs={{0,2},{1,3},{2,0},{3,1},{4,6},{5,7},{6,4},{7,5},{8,10},{9,11},{10,... | collective-permute-start | bytes 491528 | tf_op jit(solution)/shard_map/ppermute | solution.py:32
  435.4 59.3 %collective-permute-start.58 = (bf16[64,2048]{1,0:T(8,128)(2,1)S(1)}, bf16[64,2048]{1,0:T(8,128)(2,1)S(1)}, u32[]{:S(2)}, u32[]{:S(2)}) collective-permute-start(bf16[64,2048]{1,0:T(8,128)(2,1)S(1)} %get-tuple-element.184), channel_id=1, source_target_pairs={{0,64},{64,0},{1,65},{65,1},{2,66},{66,2},{3,67},{67,3},{4,68},{68... | collective-permute-start | bytes 786440 | tf_op jit(solution)/shard_map/ppermute | solution.py:518
  459.0 9.6 %collective-permute-start.67 = (bf16[2,29,16,128]{3,2,1,0:T(8,128)(2,1)S(1)}, bf16[2,29,16,128]{3,2,1,0:T(8,128)(2,1)S(1)}, u32[]{:S(2)}, u32[]{:S(2)}) collective-permute-start(bf16[2,29,16,128]{3,2,1,0:T(8,128)(2,1)S(1)} %get-tuple-element.148), channel_id=1, source_target_pairs={{0,1},{1,2},{2,3},{3,0},{4,5},{5,6},{6,7},{7,4},{8,9},{9,10},{10,1... | collective-permute-start | bytes 712712 | tf_op jit(solution)/shard_map/ppermute | solution.py:32
  459.5 13.7 %collective-permute-start.68 = (bf16[2,29,16,128]{3,2,1,0:T(8,128)(2,1)S(1)}, bf16[2,29,16,128]{3,2,1,0:T(8,128)(2,1)S(1)}, u32[]{:S(2)}, u32[]{:S(2)}) collective-permute-start(bf16[2,29,16,128]{3,2,1,0:T(8,128)(2,1)S(1)} %get-tuple-element.150), channel_id=1, source_target_pairs={{0,2},{1,3},{2,0},{3,1},{4,6},{5,7},{6,4},{7,5},{8,10},{9,11},{10,... | collective-permute-start | bytes 712712 | tf_op jit(solution)/shard_map/ppermute | solution.py:32
  462.7 10.8 %collective-permute-start.69 = (bf16[2,29,16,128]{3,2,1,0:T(8,128)(2,1)S(1)}, bf16[2,29,16,128]{3,2,1,0:T(8,128)(2,1)S(1)}, u32[]{:S(2)}, u32[]{:S(2)}) collective-permute-start(bf16[2,29,16,128]{3,2,1,0:T(8,128)(2,1)S(1)} %get-tuple-element.149), channel_id=1, source_target_pairs={{0,3},{1,0},{2,1},{3,2},{4,7},{5,4},{6,5},{7,6},{8,11},{9,8},{10,9... | collective-permute-start | bytes 712712 | tf_op jit(solution)/shard_map/ppermute | solution.py:32
  489.0 21.9 %collective-permute-start.66 = (bf16[64,2048]{1,0:T(8,128)(2,1)S(1)}, bf16[64,2048]{1,0:T(8,128)(2,1)S(1)}, u32[]{:S(2)}, u32[]{:S(2)}) collective-permute-start(bf16[64,2048]{1,0:T(8,128)(2,1)S(1)} %select_convert_fusion), channel_id=1, source_target_pairs={{0,64},{64,0},{1,65},{65,1},{2,66},{66,2},{3,67},{67,3},{4,68},{68... | collective-permute-start | bytes 786440 | tf_op jit(solution)/shard_map/ppermute | solution.py:518
  513.1 11.6 %collective-permute-start.84 = (bf16[2,21,16,128]{3,2,1,0:T(8,128)(2,1)S(1)}, bf16[2,21,16,128]{3,2,1,0:T(8,128)(2,1)S(1)}, u32[]{:S(2)}, u32[]{:S(2)}) collective-permute-start(bf16[2,21,16,128]{3,2,1,0:T(8,128)(2,1)S(1)} %get-tuple-element.176), channel_id=1, source_target_pairs={{0,2},{1,3},{2,0},{3,1},{4,6},{5,7},{6,4},{7,5},{8,10},{9,11},{10,... | collective-permute-start | bytes 516104 | tf_op jit(solution)/shard_map/ppermute | solution.py:32
  (180 other events, 2356.6 us)
Sparse Core Ops, SparseCore 0:
  11.6 128.4 all-gather.3
  142.9 73.0 all-gather.5
  218.8 72.0 all-gather.7

commit v12 on v11

--- a/solution.py
+++ b/solution.py
@@ -562,24 +562,19 @@
         cut = shard.shape[1] // 2
         return shard[:, :cut], shard[:, cut:]
 
+    keyval_half = jnp.where(tensor % 2 == 0, keyval_weight[0][:, :head], keyval_weight[0][:, head:])
     early_all = gather_all(
-        jnp.concatenate([query_weight[0], row_major(output_weight[0].T)], axis=1)
-    )
+        jnp.concatenate([query_weight[0], row_major(output_weight[0].T), keyval_half], axis=1)
+    )
+    keyval_ws = [
+        jnp.concatenate(
+            [early_all[x, :, layer, :, 2 * local_q :].reshape(width, head) for x in range(2)], axis=1
+        )
+        for layer in range(2)
+    ]
 
     def crossed(block, mask):
         return lax.ppermute(block, both, [(i, i ^ mask) for i in range(8 * chips)])
-
-    shard = keyval_weight[0]
-    pairs = by_layer(
-        jnp.stack([shard, crossed(shard, 2)]),
-        jnp.stack([crossed(shard, 4 * chips), crossed(shard, 4 * chips + 2)]),
-    )
-    quads = jnp.stack(pairs, axis=1)
-    quads = jnp.stack([quads] + [crossed(quads, 4 * k) for k in range(1, chips)])
-    blocks = jnp.stack([quads, crossed(quads, 1)], axis=2)
-    blocks = blocks.reshape((4 * chips, 2) + shard.shape)
-    keyval_all = jnp.take(blocks, jnp.arange(4 * chips, dtype=jnp.int32) ^ data, axis=0, mode="clip")
-    keyval_ws = [keyval_all[:, layer].reshape(width, 2 * head) for layer in range(2)]
 
     vectors = jnp.concatenate(
         [
@@ -743,26 +738,30 @@
             return pile
         return jnp.concatenate([pile, jnp.zeros((lack,) + pile.shape[1:], pile.dtype)], axis=0)
 
-    def piled(shared, quartered):
-        pile = padded(jnp.concatenate([tiles(part) for part in shared], axis=0), ranks)
+    def piled(*groups):
+        piles = [
+            padded(jnp.concatenate([tiles(part) for part in group], axis=0), ranks) for group in groups
+        ]
         return jnp.concatenate(
-            [block.reshape((ranks, -1) + block.shape[1:]) for block in [pile] + [tiles(part) for part in quartered]],
-            axis=1,
+            [pile.reshape((ranks, -1) + pile.shape[1:]) for pile in piles], axis=1
         ).astype(bf16)
-
-    def owned_pile(mine, owned):
-        pile = jnp.concatenate([mine] + [tiles(part) for part in owned], axis=0).astype(bf16)
-        return padded(pile, lax.axis_size("dp"))
 
     def at(block, index, axis):
         return lax.dynamic_index_in_dim(block, index, axis, keepdims=False)
 
+    def summed_ranks(pile):
+        total = at(pile, tensor, 0).astype(f32)
+        for j in range(1, ranks):
+            block = at(pile, (tensor + j) % ranks, 0)
+            total = total + around(block, "tensor", j).astype(f32)
+        return total
+
     def scattered_grads(layers):
-        pile = jnp.stack([piled(shared, quartered) for shared, quartered, _ in layers], axis=1)
-        mine = at(pile, tensor, 0).astype(f32)
-        for j in range(1, ranks):
-            mine = mine + around(at(pile, (tensor + j) % ranks, 0), "tensor", j).astype(f32)
-        pile = jnp.stack([owned_pile(mine[i], layers[i][2]) for i in range(2)])
+        piles = [
+            jnp.concatenate([mine] + [tiles(part) for part in keyval + owned], axis=0).astype(bf16)
+            for mine, keyval, owned in layers
+        ]
+        pile = jnp.stack([padded(block, lax.axis_size("dp")) for block in piles])
         pile = pile.reshape((2, chips, 4, -1) + pile.shape[2:])
         mine = at(pile, near, 2).astype(f32)
         for k in range(1, 4):
@@ -773,7 +772,7 @@
             mine = mine + flipped(at(pile, turn ^ k, 1), "dp", 4 * k).astype(f32)
         return mine.astype(bf16)
 
-    def spread_grads(zero, one, shared, quartered, owned):
+    def spread_grads(zero, one, shared, keyval, quartered, owned):
         own = jnp.where(low_section, zero, one)
         away = jnp.where(low_section, one, zero)
         dp_size = 4 * chips
@@ -793,17 +792,23 @@
             [jnp.where(core == 0, parts, other), jnp.where(core == 0, other, parts)], axis=2
         )
         pile = jnp.moveaxis(parts, 3, 0).reshape((2, -1) + parts.shape[5:])
-        shared_sizes = [part.shape[1] // 128 for part in shared]
-        quarter_sizes = [part.shape[1] // 128 // ranks for part in quartered]
-        owned_sizes = [part.shape[1] // 128 for part in owned]
-        each = -(-sum(shared_sizes) // ranks)
-        own = pile[:, :each]
+        shared_sizes, keyval_sizes, quarter_sizes, owned_sizes = [
+            [part.shape[1] // 128 // cut for part in group]
+            for group, cut in [(shared, 1), (keyval, 1), (quartered, ranks), (owned, 1)]
+        ]
+        each = sum(shared_sizes) // ranks
+        border = each + sum(quarter_sizes)
+        own = jnp.concatenate([pile[:, :each], pile[:, border : border + sum(keyval_sizes)]], axis=1)
         parts = jnp.stack([own] + [around(own, "tensor", k) for k in range(1, ranks)])
-        ordered = jnp.concatenate([at(parts, (tensor - r) % ranks, 0) for r in range(ranks)], axis=1)
+        parts = [at(parts, (tensor - r) % ranks, 0) for r in range(ranks)]
+        ordered = jnp.concatenate([part[:, :each] for part in parts], axis=1)
+        total = sum(part[:, each:].astype(f32) for part in parts)
         results = []
         for whole, begin, sizes in [
             (ordered, 0, shared_sizes),
-            (pile, each, quarter_sizes + owned_sizes),
+            (total, 0, keyval_sizes),
+            (pile, each, quarter_sizes),
+            (pile, border + sum(keyval_sizes), owned_sizes),
         ]:
             for count in sizes:
                 results.append([flat(whole[m, begin : begin + count]) for m in range(2)])
@@ -818,7 +823,7 @@
         owned = [across(low_u, grad_up), across(inner_d, active)]
         return shared, owned
 
-    def backward_attend(layer, kept, grad_middle):
+    def backward_attend(layer, kept, grad_middle, shared, others):
         gain1 = small[layer][0]
         sq, skv, ekv, eo = adapters[layer]
         unit1, rsd1, normed, low_q, low_kv, queries, key_block, probs, mixed, low_o = kept
@@ -827,11 +832,32 @@
             layer, branch, early_all, so_all[layer], eo, probs, queries, key_block,
             eq_all[layer], sq, head,
         )
+        shared = shared + [across(low_o, branch), across(inner_q, normed)]
+        quartered = [across(low_q, grad_q), across(inner_o, mixed)]
         count = (reach + 1) * rows
-        blocks = grad_block[:count].astype(f32)
-        for j in range(1, ranks):
-            part = grad_block[j * count : (j + 1) * count]
-            blocks = blocks + around(part, "tensor", j).astype(f32)
+        pile = piled(shared, *[[part] for part in quartered])
+        if others is None:
+            blocks = grad_block[:count].astype(f32)
+            for j in range(1, ranks):
+                part = grad_block[j * count : (j + 1) * count]
+                blocks = blocks + around(part, "tensor", j).astype(f32)
+        else:
+            turned = jnp.stack(
+                [at(pile, (tensor + j) % ranks, 0) for j in range(ranks)]
+            )
+            turned_others = jnp.stack(
+                [at(others, (tensor + j) % ranks, 0) for j in range(ranks)]
+            )
+            keys = grad_block.reshape(ranks, count // rank, rank, 2, head).transpose(0, 1, 3, 2, 4)
+            keys = keys.reshape(ranks, -1, rank, head)
+            message = jnp.concatenate([keys, turned, turned_others], axis=1)
+            total = message[0].astype(f32)
+            for j in range(1, ranks):
+                total = total + around(message[j], "tensor", j).astype(f32)
+            places = count // rank * 2
+            blocks = total[:places].reshape(count // rank, 2, rank, head).transpose(0, 2, 1, 3)
+            blocks = blocks.reshape(count, 2 * head)
+            pile = total[places:]
         own = blocks[reach * rows :]
         for back in range(1, reach + 1):
             begin = (reach - back) * rows
@@ -840,22 +866,16 @@
         inner_kv = against(grad_kv, ekv).astype(bf16)
         grad_normed = partial + against(grad_kv, keyval_ws[layer]) + plain(inner_kv, skv)
         grad_hidden = grad_middle + norm_back(unit1, rsd1, grad_normed * gain1)
-        shared = [
-            across(low_o, branch),
-            across(inner_q, normed),
-            across(inner_kv, normed),
-            across(low_kv, grad_kv),
-        ]
-        quartered = [across(low_q, grad_q), across(inner_o, mixed)]
-        return grad_hidden, shared, quartered
+        keyval = [across(inner_kv, normed), across(low_kv, grad_kv)]
+        return grad_hidden, pile, shared, keyval, quartered
 
     fresh = lax.dynamic_index_in_dim(block_input, section, 0, keepdims=False).astype(f32)
     given = lax.dynamic_index_in_dim(cotangent, section, 0, keepdims=False).astype(f32)
-    branch_one = spread(given.astype(bf16))
-    fresh, branch_one = lax.optimization_barrier((fresh, branch_one))
-
     middle_zero, kept_zero = forward_attend(0, fresh)
     unit_zero, rsd_zero, second_zero, up_bias = feed_inputs(0, middle_zero)
+    own_rows, second_zero = lax.optimization_barrier((given.astype(bf16), second_zero))
+    branch_one = spread(own_rows)
+    second_zero, branch_one = lax.optimization_barrier((second_zero, branch_one))
     active_zero, slope_zero, low_u_zero, low_d_zero, partial = feed_call(
         feed_kernel,
         "feed",
@@ -882,8 +902,8 @@
     shared, owned = feed_adapters(
         second_one, branch_one, low_u, low_d, inner_u, inner_d, active, grad_up
     )
-    grad_one, more, quartered = backward_attend(1, kept_one, grad_middle)
-    layer_one = (shared + more, quartered, owned)
+    grad_one, pile_one, _, keyval_one, _ = backward_attend(1, kept_one, grad_middle, shared, None)
+    owned_one = owned
     partial, _ = lax.optimization_barrier((partial, grad_middle))
     final = feed_result(1, middle_one, partial).astype(bf16)
 
@@ -908,10 +928,14 @@
         active_zero,
         grad_up,
     )
-    grad_zero, more, quartered = backward_attend(0, kept_zero, grad_middle_zero)
-    layer_zero = (shared + more, quartered, owned)
-    mine = scattered_grads([layer_zero, layer_one])
-    grads = spread_grads(mine[0], mine[1], *layer_zero)
+    grad_zero, pile, shared, keyval, quartered = backward_attend(
+        0, kept_zero, grad_middle_zero, shared, pile_one
+    )
+    half_pile = pile.shape[0] // 2
+    mine = scattered_grads(
+        [(pile[:half_pile], keyval, owned), (pile[half_pile:], keyval_one, owned_one)]
+    )
+    grads = spread_grads(mine[0], mine[1], shared, keyval, quartered, owned)
 
     def both_micros(zero, one, kind):
         own = jnp.where(low_section, zero, one)

time: 547 us -> 544 us (level)
  waiting for transfers between devices: 217 us -> 236 us
  starting transfers between devices: 134 us -> 121 us
  other arithmetic: 34.9 us -> 28.6 us
    all_gather x1, waiting for transfers between devices: 3.54 us -> 51.6 us  [gather_all(): lax.all_gather(row_major(shard), every, axis=0, tiled=True, axis_index_gr...]
    all_gather x2, waiting for transfers between devices: 45.7 us -> 0.04 us  [gather(): lax.all_gather(row_major(shard), both, axis=0, tiled=True, axis_index_gro...]
    ppermute x5, waiting for transfers between devices: 12.1 us -> 26.8 us  [swap(): return lax.ppermute(value, 'section', sides)]
    ppermute x9 -> x2, starting transfers between devices: 15.1 us -> 3.49 us  [crossed(): return lax.ppermute(block, both, [(i, i ^ mask) for i in range(8 * chips)])]
    ppermute x9 -> x2, waiting for transfers between devices: 12.3 us -> 3.53 us  [crossed(): return lax.ppermute(block, both, [(i, i ^ mask) for i in range(8 * chips)])]
    another operation x9 -> x3, other arithmetic: 7.24 us -> 0.45 us  [the longest x2 5.84 us: per_device(): blocks = jnp.stack([quads, crossed(quads, 1)], axis=2)]
    ppermute x45 -> x42, waiting for transfers between devices: 118 us -> 125 us  [around(): lax.ppermute(block, axis, [(i, (i + distance) % size) for i in range(size)])]
    ppermute x45 -> x42, starting transfers between devices: 62.9 us -> 58.7 us  [around(): lax.ppermute(block, axis, [(i, (i + distance) % size) for i in range(size)])]
  transfers between devices with their start and end apart: 89 -> 79, of which waited for: 56 -> 56; matrix products, arithmetic and copies ran while one was open for 11% -> 9% of each run, Pallas kernels for 7% -> 7%
where the time goes in v12:
time: 544 us; the launch traced here: 536 us
  waiting for transfers between devices  236 us (43%)
  starting transfers between devices  121 us (22%)
  Pallas kernels  87 us (16%)
  local copies, waits for them, and re-layouts  28.7 us (5%)
  other arithmetic  28.6 us (5%)
  between operations  21.4 us (4%)
  matrix products  13.6 us (2%)
    ppermute x42, waiting for transfers between devices, around(): lax.ppermute(block, axis, [(i, (i + distance) % size) for i in range(size)])  125 us
    ppermute x42, starting transfers between devices, around(): lax.ppermute(block, axis, [(i, (i + distance) % size) for i in range(size)])  58.7 us
    all_gather x1, waiting for transfers between devices, gather_all(): lax.all_gather(row_major(shard), every, axis=0, tiled=True, axis_index_gr...  51.6 us
    pallas_call x3, Pallas kernels, feed_call(): pl.pallas_call(kernel, in_specs=[remote if value.ndim == 4 or i in copied...  35.4 us
    ppermute x16, starting transfers between devices, along(): return lax.ppermute(block, axis, route)  32.1 us
    ppermute x5, waiting for transfers between devices, swap(): return lax.ppermute(value, 'section', sides)  26.8 us
    pallas_call x2, Pallas kernels, attend_back(): pl.pallas_call(lambda *refs: attend_back_kernel(layer, head, *refs), in_s...  23.1 us
    pallas_call x2, Pallas kernels, attend(): pl.pallas_call(lambda *refs: attend_kernel(layer, head, *refs), in_specs=...  19.8 us
  transfers between devices with their start and end apart: 79, of which 56 were waited for; matrix products, arithmetic and copies ran while one was open for 9% of the time, Pallas kernels for 7%

profile of v12, /device:TPU:0, one launch (start us, length us, event | category | flops | bytes accessed | tf_op | source)
XLA Modules:
  0.0 536.1 jit_solution(2241149857124190677)
XLA Ops:
  12.3 4.0 collective-permute-start.18
  16.4 12.2 %collective-permute-done.18 = bf16[128,2048]{1,0:T(8,128)(2,1)S(1)} collective-permute-done((bf16[128,2048]{1,0:T(8,128)(2,1)S(1)}, bf16[128,2048]{1,0:T(8,128)(2,1)S(1)}, u32[]{:S(2)}, u32[]{:S(2)}) %collective-permute-start.18) | collective-permute-done | bytes 524320 | tf_op jit(solution)/shard_map/ppermute | solution.py:518
  48.1 4.1 collective-permute-start.1
  54.8 12.3 %collective-permute-done = bf16[1,14592]{1,0:T(2,128)(2,1)S(1)} collective-permute-done((bf16[1,14592]{1,0:T(2,128)(2,1)S(1)}, bf16[1,14592]{1,0:T(2,128)(2,1)S(1)}, u32[]{:S(2)}, u32[]{:S(2)}) %collective-permute-start) | collective-permute-done | bytes 29216 | tf_op jit(solution)/shard_map/ppermute | solution.py:518
  82.5 51.6 %all-gather.4.cloned.1.call-done = bf16[16384,1152]{1,0:T(8,128)(2,1)} async-done(((bf16[128,1152]{1,0:T(8,128)(2,1)}), bf16[16384,1152]{1,0:T(8,128)(2,1)}) %all-gather.4.cloned.1.call-update) | async-done | bytes 37748752 | tf_op jit(solution)/shard_map/all_gather | solution.py:556
  137.3 3.4 collective-permute-start.5
  143.0 4.1 collective-permute-start.7
  152.8 4.4 project_queries.2
  160.2 5.7 %collective-permute-done.11 = bf16[320,256]{1,0:T(8,128)(2,1)S(1)} collective-permute-done((bf16[320,256]{1,0:T(8,128)(2,1)S(1)}, bf16[320,256]{1,0:T(8,128)(2,1)S(1)}, u32[]{:S(2)}, u32[]{:S(2)}) %collective-permute-start.11) | collective-permute-done | bytes 163872 | tf_op jit(solution)/shard_map/ppermute | solution.py:32
  166.0 10.3 %attend.2 = (bf16[4,256,1280]{2,1,0:T(8,128)(2,1)S(1)}, bf16[64,2048]{1,0:T(8,128)(2,1)S(1)}, bf16[64,16]{1,0:T(8,128)(2,1)S(1)}, f32[64,2048]{1,0:T(8,128)S(1)}) custom-call(bf16[64,2048]{1,0:T(8,128)(2,1)S(1)} %get-tuple-element.58.refs_0_.refs_5_, bf16[1280,256]{1,0:T(8,128)(2,1)S(1)} %constant_dynamic-update-slice_fusion.26.refs_1_.refs_6_, ...), custom_call_target="tpu_custom_call" | custom-call | flops 2818572288 | bytes 8388608 | tf_op jit(solution)/shard_map/attend/pallas_call | solution.py:180
  181.5 4.8 collective-permute-done.12
  187.9 4.7 collective-permute-done.14
  195.6 6.3 %collective-permute-done.15 = bf16[64,2048]{1,0:T(8,128)(2,1)S(1)} collective-permute-done((bf16[64,2048]{1,0:T(8,128)(2,1)S(1)}, bf16[64,2048]{1,0:T(8,128)(2,1)S(1)}, u32[]{:S(2)}, u32[]{:S(2)}) %collective-permute-start.15) | collective-permute-done | bytes 262176 | tf_op jit(solution)/shard_map/ppermute | solution.py:32
  204.6 3.7 collective-permute-done.17
  209.4 10.8 %feed.1 = (bf16[256,2048]{1,0:T(8,128)(2,1)S(1)}, bf16[256,2048]{1,0:T(8,128)(2,1)S(1)}, bf16[256,16]{1,0:T(8,128)(2,1)S(1)}, bf16[256,16]{1,0:T(8,128)(2,1)S(1)}, bf16[256,2048]{1,0:T(8,128)(2,1)S(1)}) custom-call(bf16[256,2048]{1,0:T(8,128)(2,1)S(1)} %pad_maximum_fusion.2.second_ref, bf16[4,2,512,2048]{3,2,1,0:T(8,128)(2,1)} %bitcast.739, ...), custom_call_target="tpu_custom_call" | custom-call | flops 4294967296 | bytes 16777216 | tf_op jit(solution)/shard_map/feed/pallas_call | solution.py:448
  226.2 3.9 collective-permute-done.19
  230.0 6.1 %collective-permute-done.20 = bf16[64,2048]{1,0:T(8,128)(2,1)S(1)} collective-permute-done((bf16[64,2048]{1,0:T(8,128)(2,1)S(1)}, bf16[64,2048]{1,0:T(8,128)(2,1)S(1)}, u32[]{:S(2)}, u32[]{:S(2)}) %collective-permute-start.20) | collective-permute-done | bytes 262176 | tf_op jit(solution)/shard_map/ppermute | solution.py:32
  237.7 3.3 collective-permute-start.22
  242.4 4.3 collective-permute-start.24
  249.0 2.8 collective-permute-start.26
  252.5 4.4 project_queries.3
  259.8 5.0 collective-permute-done.28
  264.8 9.5 %attend.3 = (bf16[4,256,1280]{2,1,0:T(8,128)(2,1)S(1)}, bf16[64,2048]{1,0:T(8,128)(2,1)S(1)}, bf16[64,16]{1,0:T(8,128)(2,1)S(1)}, f32[64,2048]{1,0:T(8,128)S(1)}) custom-call(bf16[64,2048]{1,0:T(8,128)(2,1)S(1)} %get-tuple-element.64.refs_0_.refs_5_, bf16[1280,256]{1,0:T(8,128)(2,1)S(1)} %constant_dynamic-update-slice_fusion.39.refs_1_.refs_6_, ...), custom_call_target="tpu_custom_call" | custom-call | flops 2818572288 | bytes 8388608 | tf_op jit(solution)/shard_map/attend/pallas_call | solution.py:180
  279.4 4.7 collective-permute-done.29
  286.2 5.5 %collective-permute-done.31 = bf16[64,2048]{1,0:T(8,128)(2,1)S(1)} collective-permute-done((bf16[64,2048]{1,0:T(8,128)(2,1)S(1)}, bf16[64,2048]{1,0:T(8,128)(2,1)S(1)}, u32[]{:S(2)}, u32[]{:S(2)}) %collective-permute-start.31) | collective-permute-done | bytes 262176 | tf_op jit(solution)/shard_map/ppermute | solution.py:32
  293.5 14.5 %feed_both.1 = (bf16[256,2048]{1,0:T(8,128)(2,1)S(1)}, bf16[256,16]{1,0:T(8,128)(2,1)S(1)}, bf16[256,16]{1,0:T(8,128)(2,1)S(1)}, bf16[256,2048]{1,0:T(8,128)(2,1...) custom-call(bf16[256,2048]{1,0:T(8,128)(2,1)S(1)} %pad_maximum_fusio, ...), custom_call_target="tpu_custom_call" | custom-call | flops 8589934592 | bytes 16777216 | tf_op jit(solution)/shard_map/feed_both/pallas_call | solution.py:448
  315.0 8.2 %collective-permute-done.32 = bf16[64,2048]{1,0:T(8,128)(2,1)S(1)} collective-permute-done((bf16[64,2048]{1,0:T(8,128)(2,1)S(1)}, bf16[64,2048]{1,0:T(8,128)(2,1)S(1)}, u32[]{:S(2)}, u32[]{:S(2)}) %collective-permute-start.32) | collective-permute-done | bytes 262176 | tf_op jit(solution)/shard_map/ppermute | solution.py:32
  324.6 11.5 %attend_back.2 = (bf16[64,2048]{1,0:T(8,128)(2,1)S(1)}, bf16[1280,256]{1,0:T(8,128)(2,1)S(1)}, bf16[64,16]{1,0:T(8,128)(2,1)S(1)}, bf16[64,16]{1,0:T(8,128)(2,1)S(1)}, f32[64,2048]{1,0:T(8,128)S(1)}) custom-call(bf16[64,2048]{1,0:T(8,128)(2,1)S(1)} %get-tuple-element.123.refs_0_, bf16[4,4,2,512,1152]{4,3,2,1,0:T(8,128)(2,1)} %bitcast.737, ...), custom_call_target="tpu_custom_call" | custom-call | flops 5637144576 | bytes 22020096 | tf_op jit(solution)/shard_map/attend_back/pallas_call | solution.py:259
  337.2 3.1 collective-permute-start.39
  343.8 5.1 collective-permute-done.39
  363.2 2.9 collective-permute-start.45
  369.8 5.4 %collective-permute-done.45 = bf16[64,2048]{1,0:T(8,128)(2,1)S(1)} collective-permute-done((bf16[64,2048]{1,0:T(8,128)(2,1)S(1)}, bf16[64,2048]{1,0:T(8,128)(2,1)S(1)}, u32[]{:S(2)}, u32[]{:S(2)}) %collective-permute-start.45) | collective-permute-done | bytes 262176 | tf_op jit(solution)/shard_map/ppermute | solution.py:32
  376.9 3.8 collective-permute-done.47
  380.8 10.0 %feed_back.1 = (bf16[256,2048]{1,0:T(8,128)(2,1)S(1)}, bf16[256,16]{1,0:T(8,128)(2,1)S(1)}, bf16[256,16]{1,0:T(8,128)(2,1)S(1)}, bf16[256,2048]{1,0:T(8,128)(2,1)S(1)}) custom-call(bf16[256,2048]{1,0:T(8,128)(2,1)S(1)} %pad_maximum_fusion.6.branch_ref, bf16[4,2,512,2048]{3,2,1,0:T(8,128)(2,1)} %bitcast.740, bf16[256,2048]{1,0:T(8,128)(2,1)S(1)} %copy-done.17, ...), custom_call_target="tpu_custom_call" | custom-call | flops 4294967296 | bytes 16777216 | tf_op jit(solution)/shard_map/feed_back/pallas_call | solution.py:448
  392.6 3.1 collective-permute-start.49
  397.3 3.5 collective-permute-done.48
  400.8 6.8 %collective-permute-done.49 = bf16[64,2048]{1,0:T(8,128)(2,1)S(1)} collective-permute-done((bf16[64,2048]{1,0:T(8,128)(2,1)S(1)}, bf16[64,2048]{1,0:T(8,128)(2,1)S(1)}, u32[]{:S(2)}, u32[]{:S(2)}) %collective-permute-start.49) | collective-permute-done | bytes 262176 | tf_op jit(solution)/shard_map/ppermute | solution.py:32
  409.4 11.6 %attend_back.3 = (bf16[64,2048]{1,0:T(8,128)(2,1)S(1)}, bf16[1280,256]{1,0:T(8,128)(2,1)S(1)}, bf16[64,16]{1,0:T(8,128)(2,1)S(1)}, bf16[64,16]{1,0:T(8,128)(2,1)S(1)}, f32[64,2048]{1,0:T(8,128)S(1)}) custom-call(bf16[64,2048]{1,0:T(8,128)(2,1)S(1)} %get-tuple-element.115.refs_0_, bf16[4,4,2,512,1152]{4,3,2,1,0:T(8,128)(2,1)} %bitcast.738, ...), custom_call_target="tpu_custom_call" | custom-call | flops 5637144576 | bytes 22020096 | tf_op jit(solution)/shard_map/attend_back/pallas_call | solution.py:259
  428.2 3.3 collective-permute-start.53
  435.0 3.6 collective-permute-done.52
  438.6 8.7 %collective-permute-done.53 = bf16[88,16,128]{2,1,0:T(8,128)(2,1)S(1)} collective-permute-done((bf16[88,16,128]{2,1,0:T(8,128)(2,1)S(1)}, bf16[88,16,128]{2,1,0:T(8,128)(2,1)S(1)}, u32[]{:S(2)}, u32[]{:S(2)}) %collective-permute-start.53) | collective-permute-done | bytes 360480 | tf_op jit(solution)/shard_map/ppermute | solution.py:32
  457.5 4.2 collective-permute-done.58
  467.1 4.8 collective-permute-done.61
  474.8 3.0 collective-permute-start.63
  492.1 3.2 collective-permute-done.67
  507.9 3.1 collective-permute-start.74
  512.8 3.7 collective-permute-done.73
  516.5 7.1 %collective-permute-done.74 = bf16[2,34,16,128]{3,2,1,0:T(8,128)(2,1)S(1)} collective-permute-done((bf16[2,34,16,128]{3,2,1,0:T(8,128)(2,1)S(1)}, bf16[2,34,16,128]{3,2,1,0:T(8,128)(2,1)S(1)}, u32[]{:S(2)}, u32[]{:S(2)}) %collective-permute-start.74) | collective-permute-done | bytes 278560 | tf_op jit(solution)/shard_map/ppermute | solution.py:32
  (692 shorter events, 188.8 us)
Async XLA Ops:
  7.2 126.8 %all-gather.4.cloned.1.call-start = ((), (), s32[]{:S(2)}) async-start(), calls=%async_computation | async-start | bytes 38043648 | tf_op jit(solution)/shard_map/all_gather | solution.py:556
  10.8 198.6 %all-gather.6.cloned.1.call-start = ((), (), s32[]{:S(2)}) async-start(), calls=%async_computation.1 | async-start | bytes 17301504 | tf_op jit(solution)/shard_map/all_gather | solution.py:552
  12.3 16.3 %collective-permute-start.18 = (bf16[128,2048]{1,0:T(8,128)(2,1)S(1)}, bf16[128,2048]{1,0:T(8,128)(2,1)S(1)}, u32[]{:S(2)}, u32[]{:S(2)}) collective-permute-start(bf16[128,2048]{1,0:T(8,128)(2,1)S(1)} %broadcast_select_fusion.2), channel_id=1, source_target_pairs={{0,64},{64,0},{1,65},{65,1},{2,66},{66,2},{3,67},{67,3},{4,68},{68... | collective-permute-start | bytes 1572872 | tf_op jit(solution)/shard_map/ppermute | solution.py:518
  30.0 261.8 %all-gather.8.cloned.1.call-start = ((), (), s32[]{:S(2)}) async-start(), calls=%async_computation.2 | async-start | bytes 17301504 | tf_op jit(solution)/shard_map/all_gather | solution.py:552
  48.1 20.0 %collective-permute-start.1 = (bf16[16,8256]{1,0:T(8,128)(2,1)S(1)}, bf16[16,8256]{1,0:T(8,128)(2,1)S(1)}, u32[]{:S(2)}, u32[]{:S(2)}) collective-permute-start(bf16[16,8256]{1,0:T(8,128)(2,1)S(1)} %concatenate.175), channel_id=1, source_target_pairs={{0,64},{64,0},{1,65},{65,1},{2,66},{66,2},{3,67},{67,3},{4,68},{68... | collective-permute-start | bytes 792584 | tf_op jit(solution)/shard_map/ppermute | solution.py:518
  52.5 14.6 %collective-permute-start = (bf16[1,14592]{1,0:T(2,128)(2,1)S(1)}, bf16[1,14592]{1,0:T(2,128)(2,1)S(1)}, u32[]{:S(2)}, u32[]{:S(2)}) collective-permute-start(bf16[1,14592]{1,0:T(2,128)(2,1)S(1)} %constant_dynamic-update-slice_fusion), channel_id=1, source_target_pairs={{0,64},{64,0},{1,65},{65,1},{2,66},{66,2},{3,67},{67,3},{4,68},{68... | collective-permute-start | bytes 87560 | tf_op jit(solution)/shard_map/ppermute | solution.py:518
  68.2 8.8 %collective-permute-start.2 = (bf16[16,5696]{1,0:T(8,128)(2,1)S(1)}, bf16[16,5696]{1,0:T(8,128)(2,1)S(1)}, u32[]{:S(2)}, u32[]{:S(2)}) collective-permute-start(bf16[16,5696]{1,0:T(8,128)(2,1)S(1)} %get-tuple-element.262), channel_id=1, source_target_pairs={{0,1},{1,2},{2,3},{3,0},{4,5},{5,6},{6,7},{7,4},{8,9},{9,10},{10,1... | collective-permute-start | bytes 546824 | tf_op jit(solution)/shard_map/ppermute | solution.py:32
  69.6 9.4 %collective-permute-start.3 = (bf16[16,5696]{1,0:T(8,128)(2,1)S(1)}, bf16[16,5696]{1,0:T(8,128)(2,1)S(1)}, u32[]{:S(2)}, u32[]{:S(2)}) collective-permute-start(bf16[16,5696]{1,0:T(8,128)(2,1)S(1)} %get-tuple-element.262), channel_id=1, source_target_pairs={{0,2},{1,3},{2,0},{3,1},{4,6},{5,7},{6,4},{7,5},{8,10},{9,11},{10,... | collective-permute-start | bytes 546824 | tf_op jit(solution)/shard_map/ppermute | solution.py:32
  137.3 11.3 %collective-permute-start.5 = (bf16[64,256]{1,0:T(8,128)(2,1)S(1)}, bf16[64,256]{1,0:T(8,128)(2,1)S(1)}, u32[]{:S(2)}, u32[]{:S(2)}) collective-permute-start(bf16[64,256]{1,0:T(8,128)(2,1)S(1)} %fusion.19), channel_id=1, source_target_pairs={{0,16},{4,20},{8,24},{12,28},{16,32},{20,36},{24,40},{28,44},{32,4... | collective-permute-start | bytes 98312 | tf_op jit(solution)/shard_map/ppermute | solution.py:38
  149.4 9.2 %collective-permute-start.9 = (bf16[320,256]{1,0:T(8,128)(2,1)S(1)}, bf16[320,256]{1,0:T(8,128)(2,1)S(1)}, u32[]{:S(2)}, u32[]{:S(2)}) collective-permute-start(bf16[320,256]{1,0:T(8,128)(2,1)S(1)} %get-tuple-element.318), channel_id=1, source_target_pairs={{0,3},{1,0},{2,1},{3,2},{4,7},{5,4},{6,5},{7,6},{8,11},{9,8},{10,9... | collective-permute-start | bytes 491528 | tf_op jit(solution)/shard_map/ppermute | solution.py:32
  157.2 8.7 %collective-permute-start.11 = (bf16[320,256]{1,0:T(8,128)(2,1)S(1)}, bf16[320,256]{1,0:T(8,128)(2,1)S(1)}, u32[]{:S(2)}, u32[]{:S(2)}) collective-permute-start(bf16[320,256]{1,0:T(8,128)(2,1)S(1)} %get-tuple-element.318), channel_id=1, source_target_pairs={{0,1},{1,2},{2,3},{3,0},{4,5},{5,6},{6,7},{7,4},{8,9},{9,10},{10,1... | collective-permute-start | bytes 491528 | tf_op jit(solution)/shard_map/ppermute | solution.py:32
  177.0 9.2 %collective-permute-start.12 = (bf16[64,2048]{1,0:T(8,128)(2,1)S(1)}, bf16[64,2048]{1,0:T(8,128)(2,1)S(1)}, u32[]{:S(2)}, u32[]{:S(2)}) collective-permute-start(bf16[64,2048]{1,0:T(8,128)(2,1)S(1)} %add_convert_fusion.3), channel_id=1, source_target_pairs={{0,3},{1,0},{2,1},{3,2},{4,7},{5,4},{6,5},{7,6},{8,11},{9,8},{10,9... | collective-permute-start | bytes 786440 | tf_op jit(solution)/shard_map/ppermute | solution.py:32
  177.1 10.8 %collective-permute-start.13 = (bf16[64,2048]{1,0:T(8,128)(2,1)S(1)}, bf16[64,2048]{1,0:T(8,128)(2,1)S(1)}, u32[]{:S(2)}, u32[]{:S(2)}) collective-permute-start(bf16[64,2048]{1,0:T(8,128)(2,1)S(1)} %add_convert_fusion.3), channel_id=1, source_target_pairs={{0,2},{1,3},{2,0},{3,1},{4,6},{5,7},{6,4},{7,5},{8,10},{9,11},{10,... | collective-permute-start | bytes 786440 | tf_op jit(solution)/shard_map/ppermute | solution.py:32
  178.5 14.1 %collective-permute-start.14 = (bf16[64,2048]{1,0:T(8,128)(2,1)S(1)}, bf16[64,2048]{1,0:T(8,128)(2,1)S(1)}, u32[]{:S(2)}, u32[]{:S(2)}) collective-permute-start(bf16[64,2048]{1,0:T(8,128)(2,1)S(1)} %add_convert_fusion.3), channel_id=1, source_target_pairs={{0,1},{1,2},{2,3},{3,0},{4,5},{5,6},{6,7},{7,4},{8,9},{9,10},{10,1... | collective-permute-start | bytes 786440 | tf_op jit(solution)/shard_map/ppermute | solution.py:32
  192.7 9.2 %collective-permute-start.15 = (bf16[64,2048]{1,0:T(8,128)(2,1)S(1)}, bf16[64,2048]{1,0:T(8,128)(2,1)S(1)}, u32[]{:S(2)}, u32[]{:S(2)}) collective-permute-start(bf16[64,2048]{1,0:T(8,128)(2,1)S(1)} %dynamic-slice_bitcast_fusion.4), channel_id=1, source_target_pairs={{0,3},{1,0},{2,1},{3,2},{4,7},{5,4},{6,5},{7,6},{8,11},{9,8},{10,9... | collective-permute-start | bytes 786440 | tf_op jit(solution)/shard_map/ppermute | solution.py:32
  193.8 10.8 %collective-permute-start.16 = (bf16[64,2048]{1,0:T(8,128)(2,1)S(1)}, bf16[64,2048]{1,0:T(8,128)(2,1)S(1)}, u32[]{:S(2)}, u32[]{:S(2)}) collective-permute-start(bf16[64,2048]{1,0:T(8,128)(2,1)S(1)} %dynamic-slice_bitcast_fusion.4), channel_id=1, source_target_pairs={{0,2},{1,3},{2,0},{3,1},{4,6},{5,7},{6,4},{7,5},{8,10},{9,11},{10,... | collective-permute-start | bytes 786440 | tf_op jit(solution)/shard_map/ppermute | solution.py:32
  194.6 13.7 %collective-permute-start.17 = (bf16[64,2048]{1,0:T(8,128)(2,1)S(1)}, bf16[64,2048]{1,0:T(8,128)(2,1)S(1)}, u32[]{:S(2)}, u32[]{:S(2)}) collective-permute-start(bf16[64,2048]{1,0:T(8,128)(2,1)S(1)} %dynamic-slice_bitcast_fusion.4), channel_id=1, source_target_pairs={{0,1},{1,2},{2,3},{3,0},{4,5},{5,6},{6,7},{7,4},{8,9},{9,10},{10,1... | collective-permute-start | bytes 786440 | tf_op jit(solution)/shard_map/ppermute | solution.py:32
  220.4 9.6 %collective-permute-start.19 = (bf16[64,2048]{1,0:T(8,128)(2,1)S(1)}, bf16[64,2048]{1,0:T(8,128)(2,1)S(1)}, u32[]{:S(2)}, u32[]{:S(2)}) collective-permute-start(bf16[64,2048]{1,0:T(8,128)(2,1)S(1)} %get-tuple-element.154), channel_id=1, source_target_pairs={{0,1},{1,2},{2,3},{3,0},{4,5},{5,6},{6,7},{7,4},{8,9},{9,10},{10,1... | collective-permute-start | bytes 786440 | tf_op jit(solution)/shard_map/ppermute | solution.py:32
  221.3 14.7 %collective-permute-start.20 = (bf16[64,2048]{1,0:T(8,128)(2,1)S(1)}, bf16[64,2048]{1,0:T(8,128)(2,1)S(1)}, u32[]{:S(2)}, u32[]{:S(2)}) collective-permute-start(bf16[64,2048]{1,0:T(8,128)(2,1)S(1)} %get-tuple-element.156), channel_id=1, source_target_pairs={{0,2},{1,3},{2,0},{3,1},{4,6},{5,7},{6,4},{7,5},{8,10},{9,11},{10,... | collective-permute-start | bytes 786440 | tf_op jit(solution)/shard_map/ppermute | solution.py:32
  224.0 12.1 %collective-permute-start.21 = (bf16[64,2048]{1,0:T(8,128)(2,1)S(1)}, bf16[64,2048]{1,0:T(8,128)(2,1)S(1)}, u32[]{:S(2)}, u32[]{:S(2)}) collective-permute-start(bf16[64,2048]{1,0:T(8,128)(2,1)S(1)} %get-tuple-element.155), channel_id=1, source_target_pairs={{0,3},{1,0},{2,1},{3,2},{4,7},{5,4},{6,5},{7,6},{8,11},{9,8},{10,9... | collective-permute-start | bytes 786440 | tf_op jit(solution)/shard_map/ppermute | solution.py:32
  237.7 10.5 %collective-permute-start.22 = (bf16[64,256]{1,0:T(8,128)(2,1)S(1)}, bf16[64,256]{1,0:T(8,128)(2,1)S(1)}, u32[]{:S(2)}, u32[]{:S(2)}) collective-permute-start(bf16[64,256]{1,0:T(8,128)(2,1)S(1)} %fusion.20), channel_id=1, source_target_pairs={{0,16},{4,20},{8,24},{12,28},{16,32},{20,36},{24,40},{28,44},{32,4... | collective-permute-start | bytes 98312 | tf_op jit(solution)/shard_map/ppermute | solution.py:38
  249.0 9.1 %collective-permute-start.26 = (bf16[320,256]{1,0:T(8,128)(2,1)S(1)}, bf16[320,256]{1,0:T(8,128)(2,1)S(1)}, u32[]{:S(2)}, u32[]{:S(2)}) collective-permute-start(bf16[320,256]{1,0:T(8,128)(2,1)S(1)} %get-tuple-element.308), channel_id=1, source_target_pairs={{0,3},{1,0},{2,1},{3,2},{4,7},{5,4},{6,5},{7,6},{8,11},{9,8},{10,9... | collective-permute-start | bytes 491528 | tf_op jit(solution)/shard_map/ppermute | solution.py:32
  275.0 9.0 %collective-permute-start.29 = (bf16[64,2048]{1,0:T(8,128)(2,1)S(1)}, bf16[64,2048]{1,0:T(8,128)(2,1)S(1)}, u32[]{:S(2)}, u32[]{:S(2)}) collective-permute-start(bf16[64,2048]{1,0:T(8,128)(2,1)S(1)} %add_convert_fusion.1), channel_id=1, source_target_pairs={{0,3},{1,0},{2,1},{3,2},{4,7},{5,4},{6,5},{7,6},{8,11},{9,8},{10,9... | collective-permute-start | bytes 786440 | tf_op jit(solution)/shard_map/ppermute | solution.py:32
  275.4 10.8 %collective-permute-start.30 = (bf16[64,2048]{1,0:T(8,128)(2,1)S(1)}, bf16[64,2048]{1,0:T(8,128)(2,1)S(1)}, u32[]{:S(2)}, u32[]{:S(2)}) collective-permute-start(bf16[64,2048]{1,0:T(8,128)(2,1)S(1)} %add_convert_fusion.1), channel_id=1, source_target_pairs={{0,2},{1,3},{2,0},{3,1},{4,6},{5,7},{6,4},{7,5},{8,10},{9,11},{10,... | collective-permute-start | bytes 786440 | tf_op jit(solution)/shard_map/ppermute | solution.py:32
  277.3 14.4 %collective-permute-start.31 = (bf16[64,2048]{1,0:T(8,128)(2,1)S(1)}, bf16[64,2048]{1,0:T(8,128)(2,1)S(1)}, u32[]{:S(2)}, u32[]{:S(2)}) collective-permute-start(bf16[64,2048]{1,0:T(8,128)(2,1)S(1)} %add_convert_fusion.1), channel_id=1, source_target_pairs={{0,1},{1,2},{2,3},{3,0},{4,5},{5,6},{6,7},{7,4},{8,9},{9,10},{10,1... | collective-permute-start | bytes 786440 | tf_op jit(solution)/shard_map/ppermute | solution.py:32
  308.0 15.2 %collective-permute-start.32 = (bf16[64,2048]{1,0:T(8,128)(2,1)S(1)}, bf16[64,2048]{1,0:T(8,128)(2,1)S(1)}, u32[]{:S(2)}, u32[]{:S(2)}) collective-permute-start(bf16[64,2048]{1,0:T(8,128)(2,1)S(1)} %get-tuple-element.151), channel_id=1, source_target_pairs={{0,1},{1,2},{2,3},{3,0},{4,5},{5,6},{6,7},{7,4},{8,9},{9,10},{10,1... | collective-permute-start | bytes 786440 | tf_op jit(solution)/shard_map/ppermute | solution.py:32
  308.3 14.9 %collective-permute-start.33 = (bf16[64,2048]{1,0:T(8,128)(2,1)S(1)}, bf16[64,2048]{1,0:T(8,128)(2,1)S(1)}, u32[]{:S(2)}, u32[]{:S(2)}) collective-permute-start(bf16[64,2048]{1,0:T(8,128)(2,1)S(1)} %get-tuple-element.153), channel_id=1, source_target_pairs={{0,2},{1,3},{2,0},{3,1},{4,6},{5,7},{6,4},{7,5},{8,10},{9,11},{10,... | collective-permute-start | bytes 786440 | tf_op jit(solution)/shard_map/ppermute | solution.py:32
  310.3 13.6 %collective-permute-start.34 = (bf16[64,2048]{1,0:T(8,128)(2,1)S(1)}, bf16[64,2048]{1,0:T(8,128)(2,1)S(1)}, u32[]{:S(2)}, u32[]{:S(2)}) collective-permute-start(bf16[64,2048]{1,0:T(8,128)(2,1)S(1)} %get-tuple-element.152), channel_id=1, source_target_pairs={{0,3},{1,0},{2,1},{3,2},{4,7},{5,4},{6,5},{7,6},{8,11},{9,8},{10,9... | collective-permute-start | bytes 786440 | tf_op jit(solution)/shard_map/ppermute | solution.py:32
  337.2 11.7 %collective-permute-start.39 = (bf16[320,256]{1,0:T(8,128)(2,1)S(1)}, bf16[320,256]{1,0:T(8,128)(2,1)S(1)}, u32[]{:S(2)}, u32[]{:S(2)}) collective-permute-start(bf16[320,256]{1,0:T(8,128)(2,1)S(1)} %get-tuple-element.178), channel_id=1, source_target_pairs={{0,2},{1,3},{2,0},{3,1},{4,6},{5,7},{6,4},{7,5},{8,10},{9,11},{10,... | collective-permute-start | bytes 491528 | tf_op jit(solution)/shard_map/ppermute | solution.py:32
  340.3 8.6 %collective-permute-start.40 = (bf16[320,256]{1,0:T(8,128)(2,1)S(1)}, bf16[320,256]{1,0:T(8,128)(2,1)S(1)}, u32[]{:S(2)}, u32[]{:S(2)}) collective-permute-start(bf16[320,256]{1,0:T(8,128)(2,1)S(1)} %get-tuple-element.177), channel_id=1, source_target_pairs={{0,3},{1,0},{2,1},{3,2},{4,7},{5,4},{6,5},{7,6},{8,11},{9,8},{10,9... | collective-permute-start | bytes 491528 | tf_op jit(solution)/shard_map/ppermute | solution.py:32
  341.8 26.2 %collective-permute-start.35 = (bf16[64,2048]{1,0:T(8,128)(2,1)S(1)}, bf16[64,2048]{1,0:T(8,128)(2,1)S(1)}, u32[]{:S(2)}, u32[]{:S(2)}) collective-permute-start(bf16[64,2048]{1,0:T(8,128)(2,1)S(1)} %get-tuple-element.148), channel_id=1, source_target_pairs={{0,1},{1,2},{2,3},{3,0},{4,5},{5,6},{6,7},{7,4},{8,9},{9,10},{10,1... | collective-permute-start | bytes 786440 | tf_op jit(solution)/shard_map/ppermute | solution.py:32
  355.0 13.6 %collective-permute-start.36 = (bf16[64,2048]{1,0:T(8,128)(2,1)S(1)}, bf16[64,2048]{1,0:T(8,128)(2,1)S(1)}, u32[]{:S(2)}, u32[]{:S(2)}) collective-permute-start(bf16[64,2048]{1,0:T(8,128)(2,1)S(1)} %get-tuple-element.150), channel_id=1, source_target_pairs={{0,2},{1,3},{2,0},{3,1},{4,6},{5,7},{6,4},{7,5},{8,10},{9,11},{10,... | collective-permute-start | bytes 786440 | tf_op jit(solution)/shard_map/ppermute | solution.py:32
  356.3 13.3 %collective-permute-start.37 = (bf16[64,2048]{1,0:T(8,128)(2,1)S(1)}, bf16[64,2048]{1,0:T(8,128)(2,1)S(1)}, u32[]{:S(2)}, u32[]{:S(2)}) collective-permute-start(bf16[64,2048]{1,0:T(8,128)(2,1)S(1)} %get-tuple-element.149), channel_id=1, source_target_pairs={{0,3},{1,0},{2,1},{3,2},{4,7},{5,4},{6,5},{7,6},{8,11},{9,8},{10,9... | collective-permute-start | bytes 786440 | tf_op jit(solution)/shard_map/ppermute | solution.py:32
  363.2 12.1 %collective-permute-start.45 = (bf16[64,2048]{1,0:T(8,128)(2,1)S(1)}, bf16[64,2048]{1,0:T(8,128)(2,1)S(1)}, u32[]{:S(2)}, u32[]{:S(2)}) collective-permute-start(bf16[64,2048]{1,0:T(8,128)(2,1)S(1)} %get-tuple-element.118), channel_id=1, source_target_pairs={{0,3},{1,0},{2,1},{3,2},{4,7},{5,4},{6,5},{7,6},{8,11},{9,8},{10,9... | collective-permute-start | bytes 786440 | tf_op jit(solution)/shard_map/ppermute | solution.py:32
  366.1 10.8 %collective-permute-start.46 = (bf16[64,2048]{1,0:T(8,128)(2,1)S(1)}, bf16[64,2048]{1,0:T(8,128)(2,1)S(1)}, u32[]{:S(2)}, u32[]{:S(2)}) collective-permute-start(bf16[64,2048]{1,0:T(8,128)(2,1)S(1)} %get-tuple-element.118), channel_id=1, source_target_pairs={{0,2},{1,3},{2,0},{3,1},{4,6},{5,7},{6,4},{7,5},{8,10},{9,11},{10,... | collective-permute-start | bytes 786440 | tf_op jit(solution)/shard_map/ppermute | solution.py:32
  368.0 12.7 %collective-permute-start.47 = (bf16[64,2048]{1,0:T(8,128)(2,1)S(1)}, bf16[64,2048]{1,0:T(8,128)(2,1)S(1)}, u32[]{:S(2)}, u32[]{:S(2)}) collective-permute-start(bf16[64,2048]{1,0:T(8,128)(2,1)S(1)} %get-tuple-element.118), channel_id=1, source_target_pairs={{0,1},{1,2},{2,3},{3,0},{4,5},{5,6},{6,7},{7,4},{8,9},{9,10},{10,1... | collective-permute-start | bytes 786440 | tf_op jit(solution)/shard_map/ppermute | solution.py:32
  391.2 9.5 %collective-permute-start.48 = (bf16[64,2048]{1,0:T(8,128)(2,1)S(1)}, bf16[64,2048]{1,0:T(8,128)(2,1)S(1)}, u32[]{:S(2)}, u32[]{:S(2)}) collective-permute-start(bf16[64,2048]{1,0:T(8,128)(2,1)S(1)} %get-tuple-element.145), channel_id=1, source_target_pairs={{0,1},{1,2},{2,3},{3,0},{4,5},{5,6},{6,7},{7,4},{8,9},{9,10},{10,1... | collective-permute-start | bytes 786440 | tf_op jit(solution)/shard_map/ppermute | solution.py:32
  392.6 15.0 %collective-permute-start.49 = (bf16[64,2048]{1,0:T(8,128)(2,1)S(1)}, bf16[64,2048]{1,0:T(8,128)(2,1)S(1)}, u32[]{:S(2)}, u32[]{:S(2)}) collective-permute-start(bf16[64,2048]{1,0:T(8,128)(2,1)S(1)} %get-tuple-element.147), channel_id=1, source_target_pairs={{0,2},{1,3},{2,0},{3,1},{4,6},{5,7},{6,4},{7,5},{8,10},{9,11},{10,... | collective-permute-start | bytes 786440 | tf_op jit(solution)/shard_map/ppermute | solution.py:32
  395.6 11.9 %collective-permute-start.50 = (bf16[64,2048]{1,0:T(8,128)(2,1)S(1)}, bf16[64,2048]{1,0:T(8,128)(2,1)S(1)}, u32[]{:S(2)}, u32[]{:S(2)}) collective-permute-start(bf16[64,2048]{1,0:T(8,128)(2,1)S(1)} %get-tuple-element.146), channel_id=1, source_target_pairs={{0,3},{1,0},{2,1},{3,2},{4,7},{5,4},{6,5},{7,6},{8,11},{9,8},{10,9... | collective-permute-start | bytes 786440 | tf_op jit(solution)/shard_map/ppermute | solution.py:32
  425.0 9.1 %collective-permute-start.51 = (bf16[64,2048]{1,0:T(8,128)(2,1)S(1)}, bf16[64,2048]{1,0:T(8,128)(2,1)S(1)}, u32[]{:S(2)}, u32[]{:S(2)}) collective-permute-start(bf16[64,2048]{1,0:T(8,128)(2,1)S(1)} %get-tuple-element.180), channel_id=1, source_target_pairs={{0,64},{64,0},{1,65},{65,1},{2,66},{66,2},{3,67},{67,3},{4,68},{68... | collective-permute-start | bytes 786440 | tf_op jit(solution)/shard_map/ppermute | solution.py:518
  427.8 10.7 %collective-permute-start.52 = (bf16[88,16,128]{2,1,0:T(8,128)(2,1)S(1)}, bf16[88,16,128]{2,1,0:T(8,128)(2,1)S(1)}, u32[]{:S(2)}, u32[]{:S(2)}) collective-permute-start(bf16[88,16,128]{2,1,0:T(8,128)(2,1)S(1)} %get-tuple-element.138), channel_id=1, source_target_pairs={{0,1},{1,2},{2,3},{3,0},{4,5},{5,6},{6,7},{7,4},{8,9},{9,10},{10,1... | collective-permute-start | bytes 1081352 | tf_op jit(solution)/shard_map/ppermute | solution.py:32
  428.2 19.1 %collective-permute-start.53 = (bf16[88,16,128]{2,1,0:T(8,128)(2,1)S(1)}, bf16[88,16,128]{2,1,0:T(8,128)(2,1)S(1)}, u32[]{:S(2)}, u32[]{:S(2)}) collective-permute-start(bf16[88,16,128]{2,1,0:T(8,128)(2,1)S(1)} %get-tuple-element.140), channel_id=1, source_target_pairs={{0,2},{1,3},{2,0},{3,1},{4,6},{5,7},{6,4},{7,5},{8,10},{9,11},{10,... | collective-permute-start | bytes 1081352 | tf_op jit(solution)/shard_map/ppermute | solution.py:32
  431.5 15.8 %collective-permute-start.54 = (bf16[88,16,128]{2,1,0:T(8,128)(2,1)S(1)}, bf16[88,16,128]{2,1,0:T(8,128)(2,1)S(1)}, u32[]{:S(2)}, u32[]{:S(2)}) collective-permute-start(bf16[88,16,128]{2,1,0:T(8,128)(2,1)S(1)} %get-tuple-element.139), channel_id=1, source_target_pairs={{0,3},{1,0},{2,1},{3,2},{4,7},{5,4},{6,5},{7,6},{8,11},{9,8},{10,9... | collective-permute-start | bytes 1081352 | tf_op jit(solution)/shard_map/ppermute | solution.py:32
  451.8 9.9 %collective-permute-start.58 = (bf16[64,256]{1,0:T(8,128)(2,1)S(1)}, bf16[64,256]{1,0:T(8,128)(2,1)S(1)}, u32[]{:S(2)}, u32[]{:S(2)}) collective-permute-start(bf16[64,256]{1,0:T(8,128)(2,1)S(1)} %bitcast.843), channel_id=1, source_target_pairs={{16,0},{20,4},{24,8},{28,12},{32,16},{36,20},{40,24},{44,28},{48,3... | collective-permute-start | bytes 98312 | tf_op jit(solution)/shard_map/ppermute | solution.py:38
  486.1 18.5 %collective-permute-start.59 = (bf16[64,2048]{1,0:T(8,128)(2,1)S(1)}, bf16[64,2048]{1,0:T(8,128)(2,1)S(1)}, u32[]{:S(2)}, u32[]{:S(2)}) collective-permute-start(bf16[64,2048]{1,0:T(8,128)(2,1)S(1)} %select_convert_fusion), channel_id=1, source_target_pairs={{0,64},{64,0},{1,65},{65,1},{2,66},{66,2},{3,67},{67,3},{4,68},{68... | collective-permute-start | bytes 786440 | tf_op jit(solution)/shard_map/ppermute | solution.py:518
  506.5 10.0 %collective-permute-start.73 = (bf16[2,34,16,128]{3,2,1,0:T(8,128)(2,1)S(1)}, bf16[2,34,16,128]{3,2,1,0:T(8,128)(2,1)S(1)}, u32[]{:S(2)}, u32[]{:S(2)}) collective-permute-start(bf16[2,34,16,128]{3,2,1,0:T(8,128)(2,1)S(1)} %get-tuple-element.236), channel_id=1, source_target_pairs={{0,1},{1,2},{2,3},{3,0},{4,5},{5,6},{6,7},{7,4},{8,9},{9,10},{10,1... | collective-permute-start | bytes 835592 | tf_op jit(solution)/shard_map/ppermute | solution.py:32
  507.9 15.7 %collective-permute-start.74 = (bf16[2,34,16,128]{3,2,1,0:T(8,128)(2,1)S(1)}, bf16[2,34,16,128]{3,2,1,0:T(8,128)(2,1)S(1)}, u32[]{:S(2)}, u32[]{:S(2)}) collective-permute-start(bf16[2,34,16,128]{3,2,1,0:T(8,128)(2,1)S(1)} %get-tuple-element.236), channel_id=1, source_target_pairs={{0,2},{1,3},{2,0},{3,1},{4,6},{5,7},{6,4},{7,5},{8,10},{9,11},{10,... | collective-permute-start | bytes 835592 | tf_op jit(solution)/shard_map/ppermute | solution.py:32
  511.0 12.6 %collective-permute-start.75 = (bf16[2,34,16,128]{3,2,1,0:T(8,128)(2,1)S(1)}, bf16[2,34,16,128]{3,2,1,0:T(8,128)(2,1)S(1)}, u32[]{:S(2)}, u32[]{:S(2)}) collective-permute-start(bf16[2,34,16,128]{3,2,1,0:T(8,128)(2,1)S(1)} %get-tuple-element.236), channel_id=1, source_target_pairs={{0,3},{1,0},{2,1},{3,2},{4,7},{5,4},{6,5},{7,6},{8,11},{9,8},{10,9... | collective-permute-start | bytes 835592 | tf_op jit(solution)/shard_map/ppermute | solution.py:32
  (174 other events, 2955.3 us)
Sparse Core Ops, SparseCore 0:
  11.6 122.3 all-gather.3
  136.9 71.8 all-gather.5
  211.6 72.0 all-gather.7

commit v13 on v11

--- a/solution.py
+++ b/solution.py
@@ -562,24 +562,19 @@
         cut = shard.shape[1] // 2
         return shard[:, :cut], shard[:, cut:]
 
+    keyval_half = jnp.where(tensor % 2 == 0, keyval_weight[0][:, :head], keyval_weight[0][:, head:])
     early_all = gather_all(
-        jnp.concatenate([query_weight[0], row_major(output_weight[0].T)], axis=1)
-    )
+        jnp.concatenate([query_weight[0], row_major(output_weight[0].T), keyval_half], axis=1)
+    )
+    keyval_ws = [
+        jnp.concatenate(
+            [early_all[x, :, layer, :, 2 * local_q :].reshape(width, head) for x in range(2)], axis=1
+        )
+        for layer in range(2)
+    ]
 
     def crossed(block, mask):
         return lax.ppermute(block, both, [(i, i ^ mask) for i in range(8 * chips)])
-
-    shard = keyval_weight[0]
-    pairs = by_layer(
-        jnp.stack([shard, crossed(shard, 2)]),
-        jnp.stack([crossed(shard, 4 * chips), crossed(shard, 4 * chips + 2)]),
-    )
-    quads = jnp.stack(pairs, axis=1)
-    quads = jnp.stack([quads] + [crossed(quads, 4 * k) for k in range(1, chips)])
-    blocks = jnp.stack([quads, crossed(quads, 1)], axis=2)
-    blocks = blocks.reshape((4 * chips, 2) + shard.shape)
-    keyval_all = jnp.take(blocks, jnp.arange(4 * chips, dtype=jnp.int32) ^ data, axis=0, mode="clip")
-    keyval_ws = [keyval_all[:, layer].reshape(width, 2 * head) for layer in range(2)]
 
     vectors = jnp.concatenate(
         [
@@ -743,26 +738,34 @@
             return pile
         return jnp.concatenate([pile, jnp.zeros((lack,) + pile.shape[1:], pile.dtype)], axis=0)
 
-    def piled(shared, quartered):
-        pile = padded(jnp.concatenate([tiles(part) for part in shared], axis=0), ranks)
+    def piled(*groups):
+        piles = [
+            padded(jnp.concatenate([tiles(part) for part in group], axis=0), ranks) for group in groups
+        ]
         return jnp.concatenate(
-            [block.reshape((ranks, -1) + block.shape[1:]) for block in [pile] + [tiles(part) for part in quartered]],
-            axis=1,
+            [pile.reshape((ranks, -1) + pile.shape[1:]) for pile in piles], axis=1
         ).astype(bf16)
-
-    def owned_pile(mine, owned):
-        pile = jnp.concatenate([mine] + [tiles(part) for part in owned], axis=0).astype(bf16)
-        return padded(pile, lax.axis_size("dp"))
 
     def at(block, index, axis):
         return lax.dynamic_index_in_dim(block, index, axis, keepdims=False)
 
+    def summed_ranks(pile):
+        total = at(pile, tensor, 0).astype(f32)
+        for j in range(1, ranks):
+            block = at(pile, (tensor + j) % ranks, 0)
+            total = total + around(block, "tensor", j).astype(f32)
+        return total.astype(bf16)
+
+    def summed_beside(pile):
+        flat_pile = pile.reshape((-1,) + pile.shape[2:])
+        return lax.psum_scatter(flat_pile, "tensor", scatter_dimension=0, tiled=True)
+
     def scattered_grads(layers):
-        pile = jnp.stack([piled(shared, quartered) for shared, quartered, _ in layers], axis=1)
-        mine = at(pile, tensor, 0).astype(f32)
-        for j in range(1, ranks):
-            mine = mine + around(at(pile, (tensor + j) % ranks, 0), "tensor", j).astype(f32)
-        pile = jnp.stack([owned_pile(mine[i], layers[i][2]) for i in range(2)])
+        piles = [
+            jnp.concatenate(mine + [tiles(part).astype(bf16) for part in owned], axis=0)
+            for mine, owned in layers
+        ]
+        pile = jnp.stack([padded(block, lax.axis_size("dp")) for block in piles])
         pile = pile.reshape((2, chips, 4, -1) + pile.shape[2:])
         mine = at(pile, near, 2).astype(f32)
         for k in range(1, 4):
@@ -773,7 +776,7 @@
             mine = mine + flipped(at(pile, turn ^ k, 1), "dp", 4 * k).astype(f32)
         return mine.astype(bf16)
 
-    def spread_grads(zero, one, shared, quartered, owned):
+    def spread_grads(zero, one, fed, attended, quartered, owned):
         own = jnp.where(low_section, zero, one)
         away = jnp.where(low_section, one, zero)
         dp_size = 4 * chips
@@ -793,16 +796,19 @@
             [jnp.where(core == 0, parts, other), jnp.where(core == 0, other, parts)], axis=2
         )
         pile = jnp.moveaxis(parts, 3, 0).reshape((2, -1) + parts.shape[5:])
-        shared_sizes = [part.shape[1] // 128 for part in shared]
-        quarter_sizes = [part.shape[1] // 128 // ranks for part in quartered]
-        owned_sizes = [part.shape[1] // 128 for part in owned]
-        each = -(-sum(shared_sizes) // ranks)
+        fed_sizes, attended_sizes, quarter_sizes, owned_sizes = [
+            [part.shape[1] // 128 // cut for part in group]
+            for group, cut in [(fed, 1), (attended, 1), (quartered, ranks), (owned, 1)]
+        ]
+        counts = [-(-sum(sizes) // ranks) for sizes in (fed_sizes, attended_sizes)]
+        each = sum(counts)
         own = pile[:, :each]
         parts = jnp.stack([own] + [around(own, "tensor", k) for k in range(1, ranks)])
-        ordered = jnp.concatenate([at(parts, (tensor - r) % ranks, 0) for r in range(ranks)], axis=1)
+        parts = [at(parts, (tensor - r) % ranks, 0) for r in range(ranks)]
         results = []
         for whole, begin, sizes in [
-            (ordered, 0, shared_sizes),
+            (jnp.concatenate([part[:, : counts[0]] for part in parts], axis=1), 0, fed_sizes),
+            (jnp.concatenate([part[:, counts[0] :] for part in parts], axis=1), 0, attended_sizes),
             (pile, each, quarter_sizes + owned_sizes),
         ]:
             for count in sizes:
@@ -851,11 +857,11 @@
 
     fresh = lax.dynamic_index_in_dim(block_input, section, 0, keepdims=False).astype(f32)
     given = lax.dynamic_index_in_dim(cotangent, section, 0, keepdims=False).astype(f32)
-    branch_one = spread(given.astype(bf16))
-    fresh, branch_one = lax.optimization_barrier((fresh, branch_one))
-
     middle_zero, kept_zero = forward_attend(0, fresh)
     unit_zero, rsd_zero, second_zero, up_bias = feed_inputs(0, middle_zero)
+    own_rows, second_zero = lax.optimization_barrier((given.astype(bf16), second_zero))
+    branch_one = spread(own_rows)
+    second_zero, branch_one = lax.optimization_barrier((second_zero, branch_one))
     active_zero, slope_zero, low_u_zero, low_d_zero, partial = feed_call(
         feed_kernel,
         "feed",
@@ -882,8 +888,9 @@
     shared, owned = feed_adapters(
         second_one, branch_one, low_u, low_d, inner_u, inner_d, active, grad_up
     )
-    grad_one, more, quartered = backward_attend(1, kept_one, grad_middle)
-    layer_one = (shared + more, quartered, owned)
+    grad_one, attended, quartered = backward_attend(1, kept_one, grad_middle)
+    pile = piled(shared, attended, *[[part] for part in quartered])
+    layer_one = ([summed_beside(pile)], owned)
     partial, _ = lax.optimization_barrier((partial, grad_middle))
     final = feed_result(1, middle_one, partial).astype(bf16)
 
@@ -908,10 +915,11 @@
         active_zero,
         grad_up,
     )
-    grad_zero, more, quartered = backward_attend(0, kept_zero, grad_middle_zero)
-    layer_zero = (shared + more, quartered, owned)
-    mine = scattered_grads([layer_zero, layer_one])
-    grads = spread_grads(mine[0], mine[1], *layer_zero)
+    fed_mine = summed_beside(piled(shared))
+    grad_zero, attended, quartered = backward_attend(0, kept_zero, grad_middle_zero)
+    mine = summed_ranks(piled(attended, *[[part] for part in quartered]))
+    mine = scattered_grads([([fed_mine, mine], owned), layer_one])
+    grads = spread_grads(mine[0], mine[1], shared, attended, quartered, owned)
 
     def both_micros(zero, one, kind):
         own = jnp.where(low_section, zero, one)

time: 547 us -> 549 us (level)
  starting transfers between devices: 134 us -> 125 us
  other arithmetic: 34.9 us -> 40.6 us
    all_gather x1, waiting for transfers between devices: 3.54 us -> 52.5 us  [gather_all(): lax.all_gather(row_major(shard), every, axis=0, tiled=True, axis_index_gr...]
    all_gather x2, waiting for transfers between devices: 45.7 us -> 0.04 us  [gather(): lax.all_gather(row_major(shard), both, axis=0, tiled=True, axis_index_gro...]
    ppermute x5, waiting for transfers between devices: 12.1 us -> 24.6 us  [swap(): return lax.ppermute(value, 'section', sides)]
    ppermute x9 -> x2, starting transfers between devices: 15.1 us -> 3.93 us  [crossed(): return lax.ppermute(block, both, [(i, i ^ mask) for i in range(8 * chips)])]
    ppermute x9 -> x2, waiting for transfers between devices: 12.3 us -> 3.78 us  [crossed(): return lax.ppermute(block, both, [(i, i ^ mask) for i in range(8 * chips)])]
    another operation x9 -> x3, other arithmetic: 7.24 us -> 0.35 us  [the longest x2 5.84 us: per_device(): blocks = jnp.stack([quads, crossed(quads, 1)], axis=2)]
    unnamed x324 -> x302, local copies, waits for them, and re-layouts: 15.1 us -> 14.5 us
  transfers between devices with their start and end apart: 89 -> 84, of which waited for: 56 -> 52; matrix products, arithmetic and copies ran while one was open for 11% -> 13% of each run, Pallas kernels for 7% -> 11%
where the time goes in v13:
time: 549 us; the launch traced here: 540 us
  waiting for transfers between devices  222 us (40%)
  starting transfers between devices  125 us (23%)
  Pallas kernels  87.1 us (16%)
  other arithmetic  40.6 us (7%)
  local copies, waits for them, and re-layouts  30.9 us (6%)
  between operations  21.3 us (4%)
  matrix products  13.4 us (2%)
    ppermute x45, waiting for transfers between devices, around(): lax.ppermute(block, axis, [(i, (i + distance) % size) for i in range(size)])  116 us
    ppermute x45, starting transfers between devices, around(): lax.ppermute(block, axis, [(i, (i + distance) % size) for i in range(size)])  62.3 us
    all_gather x1, waiting for transfers between devices, gather_all(): lax.all_gather(row_major(shard), every, axis=0, tiled=True, axis_index_gr...  52.5 us
    pallas_call x3, Pallas kernels, feed_call(): pl.pallas_call(kernel, in_specs=[remote if value.ndim == 4 or i in copied...  35.4 us
    ppermute x16, starting transfers between devices, along(): return lax.ppermute(block, axis, route)  32.1 us
    ppermute x5, waiting for transfers between devices, swap(): return lax.ppermute(value, 'section', sides)  24.6 us
    pallas_call x2, Pallas kernels, attend_back(): pl.pallas_call(lambda *refs: attend_back_kernel(layer, head, *refs), in_s...  22.9 us
    pallas_call x2, Pallas kernels, attend(): pl.pallas_call(lambda *refs: attend_kernel(layer, head, *refs), in_specs=...  20 us
  transfers between devices with their start and end apart: 84, of which 52 were waited for; matrix products, arithmetic and copies ran while one was open for 13% of the time, Pallas kernels for 11%

profile of v13, /device:TPU:0, one launch (start us, length us, event | category | flops | bytes accessed | tf_op | source)
XLA Modules:
  0.0 540.1 jit_solution(4369605097741412959)
XLA Ops:
  12.3 4.0 collective-permute-start.18
  16.4 12.2 %collective-permute-done.18 = bf16[128,2048]{1,0:T(8,128)(2,1)S(1)} collective-permute-done((bf16[128,2048]{1,0:T(8,128)(2,1)S(1)}, bf16[128,2048]{1,0:T(8,128)(2,1)S(1)}, u32[]{:S(2)}, u32[]{:S(2)}) %collective-permute-start.18) | collective-permute-done | bytes 524320 | tf_op jit(solution)/shard_map/ppermute | solution.py:518
  47.7 4.2 collective-permute-start.1
  54.4 12.3 %collective-permute-done = bf16[1,14592]{1,0:T(2,128)(2,1)S(1)} collective-permute-done((bf16[1,14592]{1,0:T(2,128)(2,1)S(1)}, bf16[1,14592]{1,0:T(2,128)(2,1)S(1)}, u32[]{:S(2)}, u32[]{:S(2)}) %collective-permute-start) | collective-permute-done | bytes 29216 | tf_op jit(solution)/shard_map/ppermute | solution.py:518
  69.2 2.7 collective-permute-start.3
  74.0 2.6 collective-permute-done.2
  81.5 52.5 %all-gather.4.cloned.1.call-done = bf16[16384,1152]{1,0:T(8,128)(2,1)} async-done(((bf16[128,1152]{1,0:T(8,128)(2,1)}), bf16[16384,1152]{1,0:T(8,128)(2,1)}) %all-gather.4.cloned.1.call-update) | async-done | bytes 37748752 | tf_op jit(solution)/shard_map/all_gather | solution.py:556
  134.0 2.8 fusion.134
  137.3 3.4 collective-permute-start.5
  143.0 4.1 collective-permute-start.7
  152.8 4.4 project_queries.2
  160.3 5.5 %collective-permute-done.11 = bf16[320,256]{1,0:T(8,128)(2,1)S(1)} collective-permute-done((bf16[320,256]{1,0:T(8,128)(2,1)S(1)}, bf16[320,256]{1,0:T(8,128)(2,1)S(1)}, u32[]{:S(2)}, u32[]{:S(2)}) %collective-permute-start.11) | collective-permute-done | bytes 163872 | tf_op jit(solution)/shard_map/ppermute | solution.py:32
  165.8 10.5 %attend.2 = (bf16[4,256,1280]{2,1,0:T(8,128)(2,1)S(1)}, bf16[64,2048]{1,0:T(8,128)(2,1)S(1)}, bf16[64,16]{1,0:T(8,128)(2,1)S(1)}, f32[64,2048]{1,0:T(8,128)S(1)}) custom-call(bf16[64,2048]{1,0:T(8,128)(2,1)S(1)} %get-tuple-element.58.refs_0_.refs_5_, bf16[1280,256]{1,0:T(8,128)(2,1)S(1)} %constant_dynamic-update-slice_fusion.26.refs_1_.refs_6_, ...), custom_call_target="tpu_custom_call" | custom-call | flops 2818572288 | bytes 8388608 | tf_op jit(solution)/shard_map/attend/pallas_call | solution.py:180
  181.1 5.1 collective-permute-done.12
  187.9 4.7 collective-permute-done.14
  195.6 6.3 %collective-permute-done.15 = bf16[64,2048]{1,0:T(8,128)(2,1)S(1)} collective-permute-done((bf16[64,2048]{1,0:T(8,128)(2,1)S(1)}, bf16[64,2048]{1,0:T(8,128)(2,1)S(1)}, u32[]{:S(2)}, u32[]{:S(2)}) %collective-permute-start.15) | collective-permute-done | bytes 262176 | tf_op jit(solution)/shard_map/ppermute | solution.py:32
  201.9 2.7 collective-permute-done.16
  204.6 3.7 collective-permute-done.17
  209.4 10.8 %feed.1 = (bf16[256,2048]{1,0:T(8,128)(2,1)S(1)}, bf16[256,2048]{1,0:T(8,128)(2,1)S(1)}, bf16[256,16]{1,0:T(8,128)(2,1)S(1)}, bf16[256,16]{1,0:T(8,128)(2,1)S(1)}, bf16[256,2048]{1,0:T(8,128)(2,1)S(1)}) custom-call(bf16[256,2048]{1,0:T(8,128)(2,1)S(1)} %pad_maximum_fusion.1.second_ref, bf16[4,2,512,2048]{3,2,1,0:T(8,128)(2,1)} %bitcast.718, ...), custom_call_target="tpu_custom_call" | custom-call | flops 4294967296 | bytes 16777216 | tf_op jit(solution)/shard_map/feed/pallas_call | solution.py:448
  221.3 2.7 collective-permute-start.20
  226.1 3.9 collective-permute-done.19
  230.0 6.1 %collective-permute-done.20 = bf16[64,2048]{1,0:T(8,128)(2,1)S(1)} collective-permute-done((bf16[64,2048]{1,0:T(8,128)(2,1)S(1)}, bf16[64,2048]{1,0:T(8,128)(2,1)S(1)}, u32[]{:S(2)}, u32[]{:S(2)}) %collective-permute-start.20) | collective-permute-done | bytes 262176 | tf_op jit(solution)/shard_map/ppermute | solution.py:32
  237.7 3.4 collective-permute-start.22
  242.4 4.3 collective-permute-start.24
  249.0 2.8 collective-permute-start.26
  252.5 4.4 project_queries.3
  259.8 4.7 collective-permute-done.28
  264.5 9.5 %attend.3 = (bf16[4,256,1280]{2,1,0:T(8,128)(2,1)S(1)}, bf16[64,2048]{1,0:T(8,128)(2,1)S(1)}, bf16[64,16]{1,0:T(8,128)(2,1)S(1)}, f32[64,2048]{1,0:T(8,128)S(1)}) custom-call(bf16[64,2048]{1,0:T(8,128)(2,1)S(1)} %get-tuple-element.64.refs_0_.refs_5_, bf16[1280,256]{1,0:T(8,128)(2,1)S(1)} %constant_dynamic-update-slice_fusion.39.refs_1_.refs_6_, ...), custom_call_target="tpu_custom_call" | custom-call | flops 2818572288 | bytes 8388608 | tf_op jit(solution)/shard_map/attend/pallas_call | solution.py:180
  282.4 4.6 collective-permute-done.29
  289.2 5.5 %collective-permute-done.31 = bf16[64,2048]{1,0:T(8,128)(2,1)S(1)} collective-permute-done((bf16[64,2048]{1,0:T(8,128)(2,1)S(1)}, bf16[64,2048]{1,0:T(8,128)(2,1)S(1)}, u32[]{:S(2)}, u32[]{:S(2)}) %collective-permute-start.31) | collective-permute-done | bytes 262176 | tf_op jit(solution)/shard_map/ppermute | solution.py:32
  296.4 14.5 %feed_both.1 = (bf16[256,2048]{1,0:T(8,128)(2,1)S(1)}, bf16[256,16]{1,0:T(8,128)(2,1)S(1)}, bf16[256,16]{1,0:T(8,128)(2,1)S(1)}, bf16[256,2048]{1,0:T(8,128)(2,1...) custom-call(bf16[256,2048]{1,0:T(8,128)(2,1)S(1)} %pad_maximum_fusio, ...), custom_call_target="tpu_custom_call" | custom-call | flops 8589934592 | bytes 16777216 | tf_op jit(solution)/shard_map/feed_both/pallas_call | solution.py:448
  318.7 8.8 %collective-permute-done.32 = bf16[64,2048]{1,0:T(8,128)(2,1)S(1)} collective-permute-done((bf16[64,2048]{1,0:T(8,128)(2,1)S(1)}, bf16[64,2048]{1,0:T(8,128)(2,1)S(1)}, u32[]{:S(2)}, u32[]{:S(2)}) %collective-permute-start.32) | collective-permute-done | bytes 262176 | tf_op jit(solution)/shard_map/ppermute | solution.py:32
  331.0 11.5 %attend_back.2 = (bf16[64,2048]{1,0:T(8,128)(2,1)S(1)}, bf16[1280,256]{1,0:T(8,128)(2,1)S(1)}, bf16[64,16]{1,0:T(8,128)(2,1)S(1)}, bf16[64,16]{1,0:T(8,128)(2,1)S(1)}, f32[64,2048]{1,0:T(8,128)S(1)}) custom-call(bf16[64,2048]{1,0:T(8,128)(2,1)S(1)} %get-tuple-element.123.refs_0_, bf16[4,4,2,512,1152]{4,3,2,1,0:T(8,128)(2,1)} %bitcast.716, ...), custom_call_target="tpu_custom_call" | custom-call | flops 5637144576 | bytes 22020096 | tf_op jit(solution)/shard_map/attend_back/pallas_call | solution.py:259
  343.6 3.1 collective-permute-start.39
  350.3 5.0 collective-permute-done.39
  375.0 9.1 %collective-permute-done.45 = bf16[64,2048]{1,0:T(8,128)(2,1)S(1)} collective-permute-done((bf16[64,2048]{1,0:T(8,128)(2,1)S(1)}, bf16[64,2048]{1,0:T(8,128)(2,1)S(1)}, u32[]{:S(2)}, u32[]{:S(2)}) %collective-permute-start.45) | collective-permute-done | bytes 262176 | tf_op jit(solution)/shard_map/ppermute | solution.py:32
  384.1 4.6 collective-permute-start.37
  388.7 10.0 %feed_back.1 = (bf16[256,2048]{1,0:T(8,128)(2,1)S(1)}, bf16[256,16]{1,0:T(8,128)(2,1)S(1)}, bf16[256,16]{1,0:T(8,128)(2,1)S(1)}, bf16[256,2048]{1,0:T(8,128)(2,1)S(1)}) custom-call(bf16[256,2048]{1,0:T(8,128)(2,1)S(1)} %pad_maximum_fusion.5.branch_ref, bf16[4,2,512,2048]{3,2,1,0:T(8,128)(2,1)} %bitcast.719, bf16[256,2048]{1,0:T(8,128)(2,1)S(1)} %copy-done.17, ...), custom_call_target="tpu_custom_call" | custom-call | flops 4294967296 | bytes 16777216 | tf_op jit(solution)/shard_map/feed_back/pallas_call | solution.py:448
  411.0 9.9 %collective-permute-done.48 = bf16[64,2048]{1,0:T(8,128)(2,1)S(1)} collective-permute-done((bf16[64,2048]{1,0:T(8,128)(2,1)S(1)}, bf16[64,2048]{1,0:T(8,128)(2,1)S(1)}, u32[]{:S(2)}, u32[]{:S(2)}) %collective-permute-start.48) | collective-permute-done | bytes 262176 | tf_op jit(solution)/shard_map/ppermute | solution.py:32
  422.2 11.5 %attend_back.3 = (bf16[64,2048]{1,0:T(8,128)(2,1)S(1)}, bf16[1280,256]{1,0:T(8,128)(2,1)S(1)}, bf16[64,16]{1,0:T(8,128)(2,1)S(1)}, bf16[64,16]{1,0:T(8,128)(2,1)S(1)}, f32[64,2048]{1,0:T(8,128)S(1)}) custom-call(bf16[64,2048]{1,0:T(8,128)(2,1)S(1)} %get-tuple-element.115.refs_0_, bf16[4,4,2,512,1152]{4,3,2,1,0:T(8,128)(2,1)} %bitcast.717, ...), custom_call_target="tpu_custom_call" | custom-call | flops 5637144576 | bytes 22020096 | tf_op jit(solution)/shard_map/attend_back/pallas_call | solution.py:259
  434.1 3.4 collective-permute-start.53
  442.3 6.2 %collective-permute-done.53 = bf16[320,256]{1,0:T(8,128)(2,1)S(1)} collective-permute-done((bf16[320,256]{1,0:T(8,128)(2,1)S(1)}, bf16[320,256]{1,0:T(8,128)(2,1)S(1)}, u32[]{:S(2)}, u32[]{:S(2)}) %collective-permute-start.53) | collective-permute-done | bytes 163872 | tf_op jit(solution)/shard_map/ppermute | solution.py:32
  458.8 3.7 collective-permute-done.58
  471.2 3.0 collective-permute-done.60
  478.9 4.0 collective-permute-done.64
  497.8 2.8 collective-permute-start.70
  516.3 3.3 collective-permute-start.77
  523.6 4.1 collective-permute-done.77
  (673 shorter events, 194.1 us)
Async XLA Ops:
  7.2 126.8 %all-gather.4.cloned.1.call-start = ((), (), s32[]{:S(2)}) async-start(), calls=%async_computation.2 | async-start | bytes 38043648 | tf_op jit(solution)/shard_map/all_gather | solution.py:556
  10.8 198.6 %all-gather.6.cloned.1.call-start = ((), (), s32[]{:S(2)}) async-start(), calls=%async_computation.3 | async-start | bytes 17301504 | tf_op jit(solution)/shard_map/all_gather | solution.py:552
  12.3 16.3 %collective-permute-start.18 = (bf16[128,2048]{1,0:T(8,128)(2,1)S(1)}, bf16[128,2048]{1,0:T(8,128)(2,1)S(1)}, u32[]{:S(2)}, u32[]{:S(2)}) collective-permute-start(bf16[128,2048]{1,0:T(8,128)(2,1)S(1)} %broadcast_select_fusion.2), channel_id=1, source_target_pairs={{0,64},{64,0},{1,65},{65,1},{2,66},{66,2},{3,67},{67,3},{4,68},{68... | collective-permute-start | bytes 1572872 | tf_op jit(solution)/shard_map/ppermute | solution.py:518
  30.0 264.8 %all-gather.8.cloned.1.call-start = ((), (), s32[]{:S(2)}) async-start(), calls=%async_computation.4 | async-start | bytes 17301504 | tf_op jit(solution)/shard_map/all_gather | solution.py:552
  34.6 419.9 %reduce-scatter.3.cloned.1.call-start = ((), (), s32[]{:S(2)}) async-start(), calls=%async_computation.5 | async-start | bytes 163840 | tf_op jit(solution)/shard_map/reduce_scatter | solution.py:761
  47.7 20.0 %collective-permute-start.1 = (bf16[16,8256]{1,0:T(8,128)(2,1)S(1)}, bf16[16,8256]{1,0:T(8,128)(2,1)S(1)}, u32[]{:S(2)}, u32[]{:S(2)}) collective-permute-start(bf16[16,8256]{1,0:T(8,128)(2,1)S(1)} %concatenate.191), channel_id=1, source_target_pairs={{0,64},{64,0},{1,65},{65,1},{2,66},{66,2},{3,67},{67,3},{4,68},{68... | collective-permute-start | bytes 792584 | tf_op jit(solution)/shard_map/ppermute | solution.py:518
  52.2 14.6 %collective-permute-start = (bf16[1,14592]{1,0:T(2,128)(2,1)S(1)}, bf16[1,14592]{1,0:T(2,128)(2,1)S(1)}, u32[]{:S(2)}, u32[]{:S(2)}) collective-permute-start(bf16[1,14592]{1,0:T(2,128)(2,1)S(1)} %constant_dynamic-update-slice_fusion), channel_id=1, source_target_pairs={{0,64},{64,0},{1,65},{65,1},{2,66},{66,2},{3,67},{67,3},{4,68},{68... | collective-permute-start | bytes 87560 | tf_op jit(solution)/shard_map/ppermute | solution.py:518
  67.8 8.8 %collective-permute-start.2 = (bf16[16,5696]{1,0:T(8,128)(2,1)S(1)}, bf16[16,5696]{1,0:T(8,128)(2,1)S(1)}, u32[]{:S(2)}, u32[]{:S(2)}) collective-permute-start(bf16[16,5696]{1,0:T(8,128)(2,1)S(1)} %get-tuple-element.249), channel_id=1, source_target_pairs={{0,1},{1,2},{2,3},{3,0},{4,5},{5,6},{6,7},{7,4},{8,9},{9,10},{10,1... | collective-permute-start | bytes 546824 | tf_op jit(solution)/shard_map/ppermute | solution.py:32
  69.2 9.3 %collective-permute-start.3 = (bf16[16,5696]{1,0:T(8,128)(2,1)S(1)}, bf16[16,5696]{1,0:T(8,128)(2,1)S(1)}, u32[]{:S(2)}, u32[]{:S(2)}) collective-permute-start(bf16[16,5696]{1,0:T(8,128)(2,1)S(1)} %get-tuple-element.249), channel_id=1, source_target_pairs={{0,2},{1,3},{2,0},{3,1},{4,6},{5,7},{6,4},{7,5},{8,10},{9,11},{10,... | collective-permute-start | bytes 546824 | tf_op jit(solution)/shard_map/ppermute | solution.py:32
  137.3 11.3 %collective-permute-start.5 = (bf16[64,256]{1,0:T(8,128)(2,1)S(1)}, bf16[64,256]{1,0:T(8,128)(2,1)S(1)}, u32[]{:S(2)}, u32[]{:S(2)}) collective-permute-start(bf16[64,256]{1,0:T(8,128)(2,1)S(1)} %fusion.20), channel_id=1, source_target_pairs={{0,16},{4,20},{8,24},{12,28},{16,32},{20,36},{24,40},{28,44},{32,4... | collective-permute-start | bytes 98312 | tf_op jit(solution)/shard_map/ppermute | solution.py:38
  149.5 9.0 %collective-permute-start.9 = (bf16[320,256]{1,0:T(8,128)(2,1)S(1)}, bf16[320,256]{1,0:T(8,128)(2,1)S(1)}, u32[]{:S(2)}, u32[]{:S(2)}) collective-permute-start(bf16[320,256]{1,0:T(8,128)(2,1)S(1)} %get-tuple-element.315), channel_id=1, source_target_pairs={{0,3},{1,0},{2,1},{3,2},{4,7},{5,4},{6,5},{7,6},{8,11},{9,8},{10,9... | collective-permute-start | bytes 491528 | tf_op jit(solution)/shard_map/ppermute | solution.py:32
  157.2 8.5 %collective-permute-start.11 = (bf16[320,256]{1,0:T(8,128)(2,1)S(1)}, bf16[320,256]{1,0:T(8,128)(2,1)S(1)}, u32[]{:S(2)}, u32[]{:S(2)}) collective-permute-start(bf16[320,256]{1,0:T(8,128)(2,1)S(1)} %get-tuple-element.315), channel_id=1, source_target_pairs={{0,1},{1,2},{2,3},{3,0},{4,5},{5,6},{6,7},{7,4},{8,9},{9,10},{10,1... | collective-permute-start | bytes 491528 | tf_op jit(solution)/shard_map/ppermute | solution.py:32
  177.0 9.2 %collective-permute-start.12 = (bf16[64,2048]{1,0:T(8,128)(2,1)S(1)}, bf16[64,2048]{1,0:T(8,128)(2,1)S(1)}, u32[]{:S(2)}, u32[]{:S(2)}) collective-permute-start(bf16[64,2048]{1,0:T(8,128)(2,1)S(1)} %add_convert_fusion.3), channel_id=1, source_target_pairs={{0,3},{1,0},{2,1},{3,2},{4,7},{5,4},{6,5},{7,6},{8,11},{9,8},{10,9... | collective-permute-start | bytes 786440 | tf_op jit(solution)/shard_map/ppermute | solution.py:32
  177.1 10.8 %collective-permute-start.13 = (bf16[64,2048]{1,0:T(8,128)(2,1)S(1)}, bf16[64,2048]{1,0:T(8,128)(2,1)S(1)}, u32[]{:S(2)}, u32[]{:S(2)}) collective-permute-start(bf16[64,2048]{1,0:T(8,128)(2,1)S(1)} %add_convert_fusion.3), channel_id=1, source_target_pairs={{0,2},{1,3},{2,0},{3,1},{4,6},{5,7},{6,4},{7,5},{8,10},{9,11},{10,... | collective-permute-start | bytes 786440 | tf_op jit(solution)/shard_map/ppermute | solution.py:32
  178.1 14.4 %collective-permute-start.14 = (bf16[64,2048]{1,0:T(8,128)(2,1)S(1)}, bf16[64,2048]{1,0:T(8,128)(2,1)S(1)}, u32[]{:S(2)}, u32[]{:S(2)}) collective-permute-start(bf16[64,2048]{1,0:T(8,128)(2,1)S(1)} %add_convert_fusion.3), channel_id=1, source_target_pairs={{0,1},{1,2},{2,3},{3,0},{4,5},{5,6},{6,7},{7,4},{8,9},{9,10},{10,1... | collective-permute-start | bytes 786440 | tf_op jit(solution)/shard_map/ppermute | solution.py:32
  192.7 9.2 %collective-permute-start.15 = (bf16[64,2048]{1,0:T(8,128)(2,1)S(1)}, bf16[64,2048]{1,0:T(8,128)(2,1)S(1)}, u32[]{:S(2)}, u32[]{:S(2)}) collective-permute-start(bf16[64,2048]{1,0:T(8,128)(2,1)S(1)} %dynamic-slice_bitcast_fusion), channel_id=1, source_target_pairs={{0,3},{1,0},{2,1},{3,2},{4,7},{5,4},{6,5},{7,6},{8,11},{9,8},{10,9... | collective-permute-start | bytes 786440 | tf_op jit(solution)/shard_map/ppermute | solution.py:32
  193.8 10.8 %collective-permute-start.16 = (bf16[64,2048]{1,0:T(8,128)(2,1)S(1)}, bf16[64,2048]{1,0:T(8,128)(2,1)S(1)}, u32[]{:S(2)}, u32[]{:S(2)}) collective-permute-start(bf16[64,2048]{1,0:T(8,128)(2,1)S(1)} %dynamic-slice_bitcast_fusion), channel_id=1, source_target_pairs={{0,2},{1,3},{2,0},{3,1},{4,6},{5,7},{6,4},{7,5},{8,10},{9,11},{10,... | collective-permute-start | bytes 786440 | tf_op jit(solution)/shard_map/ppermute | solution.py:32
  194.3 14.0 %collective-permute-start.17 = (bf16[64,2048]{1,0:T(8,128)(2,1)S(1)}, bf16[64,2048]{1,0:T(8,128)(2,1)S(1)}, u32[]{:S(2)}, u32[]{:S(2)}) collective-permute-start(bf16[64,2048]{1,0:T(8,128)(2,1)S(1)} %dynamic-slice_bitcast_fusion), channel_id=1, source_target_pairs={{0,1},{1,2},{2,3},{3,0},{4,5},{5,6},{6,7},{7,4},{8,9},{9,10},{10,1... | collective-permute-start | bytes 786440 | tf_op jit(solution)/shard_map/ppermute | solution.py:32
  220.4 9.6 %collective-permute-start.19 = (bf16[64,2048]{1,0:T(8,128)(2,1)S(1)}, bf16[64,2048]{1,0:T(8,128)(2,1)S(1)}, u32[]{:S(2)}, u32[]{:S(2)}) collective-permute-start(bf16[64,2048]{1,0:T(8,128)(2,1)S(1)} %get-tuple-element.147), channel_id=1, source_target_pairs={{0,1},{1,2},{2,3},{3,0},{4,5},{5,6},{6,7},{7,4},{8,9},{9,10},{10,1... | collective-permute-start | bytes 786440 | tf_op jit(solution)/shard_map/ppermute | solution.py:32
  221.3 14.7 %collective-permute-start.20 = (bf16[64,2048]{1,0:T(8,128)(2,1)S(1)}, bf16[64,2048]{1,0:T(8,128)(2,1)S(1)}, u32[]{:S(2)}, u32[]{:S(2)}) collective-permute-start(bf16[64,2048]{1,0:T(8,128)(2,1)S(1)} %get-tuple-element.149), channel_id=1, source_target_pairs={{0,2},{1,3},{2,0},{3,1},{4,6},{5,7},{6,4},{7,5},{8,10},{9,11},{10,... | collective-permute-start | bytes 786440 | tf_op jit(solution)/shard_map/ppermute | solution.py:32
  224.0 12.1 %collective-permute-start.21 = (bf16[64,2048]{1,0:T(8,128)(2,1)S(1)}, bf16[64,2048]{1,0:T(8,128)(2,1)S(1)}, u32[]{:S(2)}, u32[]{:S(2)}) collective-permute-start(bf16[64,2048]{1,0:T(8,128)(2,1)S(1)} %get-tuple-element.148), channel_id=1, source_target_pairs={{0,3},{1,0},{2,1},{3,2},{4,7},{5,4},{6,5},{7,6},{8,11},{9,8},{10,9... | collective-permute-start | bytes 786440 | tf_op jit(solution)/shard_map/ppermute | solution.py:32
  237.7 10.5 %collective-permute-start.22 = (bf16[64,256]{1,0:T(8,128)(2,1)S(1)}, bf16[64,256]{1,0:T(8,128)(2,1)S(1)}, u32[]{:S(2)}, u32[]{:S(2)}) collective-permute-start(bf16[64,256]{1,0:T(8,128)(2,1)S(1)} %fusion.21), channel_id=1, source_target_pairs={{0,16},{4,20},{8,24},{12,28},{16,32},{20,36},{24,40},{28,44},{32,4... | collective-permute-start | bytes 98312 | tf_op jit(solution)/shard_map/ppermute | solution.py:38
  249.0 8.9 %collective-permute-start.26 = (bf16[320,256]{1,0:T(8,128)(2,1)S(1)}, bf16[320,256]{1,0:T(8,128)(2,1)S(1)}, u32[]{:S(2)}, u32[]{:S(2)}) collective-permute-start(bf16[320,256]{1,0:T(8,128)(2,1)S(1)} %get-tuple-element.305), channel_id=1, source_target_pairs={{0,3},{1,0},{2,1},{3,2},{4,7},{5,4},{6,5},{7,6},{8,11},{9,8},{10,9... | collective-permute-start | bytes 491528 | tf_op jit(solution)/shard_map/ppermute | solution.py:32
  277.9 9.0 %collective-permute-start.29 = (bf16[64,2048]{1,0:T(8,128)(2,1)S(1)}, bf16[64,2048]{1,0:T(8,128)(2,1)S(1)}, u32[]{:S(2)}, u32[]{:S(2)}) collective-permute-start(bf16[64,2048]{1,0:T(8,128)(2,1)S(1)} %add_convert_fusion.1), channel_id=1, source_target_pairs={{0,3},{1,0},{2,1},{3,2},{4,7},{5,4},{6,5},{7,6},{8,11},{9,8},{10,9... | collective-permute-start | bytes 786440 | tf_op jit(solution)/shard_map/ppermute | solution.py:32
  278.4 10.7 %collective-permute-start.30 = (bf16[64,2048]{1,0:T(8,128)(2,1)S(1)}, bf16[64,2048]{1,0:T(8,128)(2,1)S(1)}, u32[]{:S(2)}, u32[]{:S(2)}) collective-permute-start(bf16[64,2048]{1,0:T(8,128)(2,1)S(1)} %add_convert_fusion.1), channel_id=1, source_target_pairs={{0,2},{1,3},{2,0},{3,1},{4,6},{5,7},{6,4},{7,5},{8,10},{9,11},{10,... | collective-permute-start | bytes 786440 | tf_op jit(solution)/shard_map/ppermute | solution.py:32
  280.3 14.3 %collective-permute-start.31 = (bf16[64,2048]{1,0:T(8,128)(2,1)S(1)}, bf16[64,2048]{1,0:T(8,128)(2,1)S(1)}, u32[]{:S(2)}, u32[]{:S(2)}) collective-permute-start(bf16[64,2048]{1,0:T(8,128)(2,1)S(1)} %add_convert_fusion.1), channel_id=1, source_target_pairs={{0,1},{1,2},{2,3},{3,0},{4,5},{5,6},{6,7},{7,4},{8,9},{9,10},{10,1... | collective-permute-start | bytes 786440 | tf_op jit(solution)/shard_map/ppermute | solution.py:32
  312.3 15.2 %collective-permute-start.32 = (bf16[64,2048]{1,0:T(8,128)(2,1)S(1)}, bf16[64,2048]{1,0:T(8,128)(2,1)S(1)}, u32[]{:S(2)}, u32[]{:S(2)}) collective-permute-start(bf16[64,2048]{1,0:T(8,128)(2,1)S(1)} %get-tuple-element.144), channel_id=1, source_target_pairs={{0,1},{1,2},{2,3},{3,0},{4,5},{5,6},{6,7},{7,4},{8,9},{9,10},{10,1... | collective-permute-start | bytes 786440 | tf_op jit(solution)/shard_map/ppermute | solution.py:32
  312.5 15.0 %collective-permute-start.33 = (bf16[64,2048]{1,0:T(8,128)(2,1)S(1)}, bf16[64,2048]{1,0:T(8,128)(2,1)S(1)}, u32[]{:S(2)}, u32[]{:S(2)}) collective-permute-start(bf16[64,2048]{1,0:T(8,128)(2,1)S(1)} %get-tuple-element.146), channel_id=1, source_target_pairs={{0,2},{1,3},{2,0},{3,1},{4,6},{5,7},{6,4},{7,5},{8,10},{9,11},{10,... | collective-permute-start | bytes 786440 | tf_op jit(solution)/shard_map/ppermute | solution.py:32
  314.5 13.6 %collective-permute-start.34 = (bf16[64,2048]{1,0:T(8,128)(2,1)S(1)}, bf16[64,2048]{1,0:T(8,128)(2,1)S(1)}, u32[]{:S(2)}, u32[]{:S(2)}) collective-permute-start(bf16[64,2048]{1,0:T(8,128)(2,1)S(1)} %get-tuple-element.145), channel_id=1, source_target_pairs={{0,3},{1,0},{2,1},{3,2},{4,7},{5,4},{6,5},{7,6},{8,11},{9,8},{10,9... | collective-permute-start | bytes 786440 | tf_op jit(solution)/shard_map/ppermute | solution.py:32
  343.6 11.7 %collective-permute-start.39 = (bf16[320,256]{1,0:T(8,128)(2,1)S(1)}, bf16[320,256]{1,0:T(8,128)(2,1)S(1)}, u32[]{:S(2)}, u32[]{:S(2)}) collective-permute-start(bf16[320,256]{1,0:T(8,128)(2,1)S(1)} %get-tuple-element.165), channel_id=1, source_target_pairs={{0,2},{1,3},{2,0},{3,1},{4,6},{5,7},{6,4},{7,5},{8,10},{9,11},{10,... | collective-permute-start | bytes 491528 | tf_op jit(solution)/shard_map/ppermute | solution.py:32
  346.7 8.6 %collective-permute-start.40 = (bf16[320,256]{1,0:T(8,128)(2,1)S(1)}, bf16[320,256]{1,0:T(8,128)(2,1)S(1)}, u32[]{:S(2)}, u32[]{:S(2)}) collective-permute-start(bf16[320,256]{1,0:T(8,128)(2,1)S(1)} %get-tuple-element.164), channel_id=1, source_target_pairs={{0,3},{1,0},{2,1},{3,2},{4,7},{5,4},{6,5},{7,6},{8,11},{9,8},{10,9... | collective-permute-start | bytes 491528 | tf_op jit(solution)/shard_map/ppermute | solution.py:32
  348.2 55.8 %collective-permute-start.35 = (bf16[64,2048]{1,0:T(8,128)(2,1)}, bf16[64,2048]{1,0:T(8,128)(2,1)}, u32[]{:S(2)}, u32[]{:S(2)}) collective-permute-start(bf16[64,2048]{1,0:T(8,128)(2,1)} %get-tuple-element.141), channel_id=1, source_target_pairs={{0,1},{1,2},{2,3},{3,0},{4,5},{5,6},{6,7},{7,4},{8,9},{9,10},{10,1... | collective-permute-start | bytes 786440 | tf_op jit(solution)/shard_map/ppermute | solution.py:32
  362.3 41.7 %collective-permute-start.36 = (bf16[64,2048]{1,0:T(8,128)(2,1)}, bf16[64,2048]{1,0:T(8,128)(2,1)}, u32[]{:S(2)}, u32[]{:S(2)}) collective-permute-start(bf16[64,2048]{1,0:T(8,128)(2,1)} %get-tuple-element.143), channel_id=1, source_target_pairs={{0,2},{1,3},{2,0},{3,1},{4,6},{5,7},{6,4},{7,5},{8,10},{9,11},{10,... | collective-permute-start | bytes 786440 | tf_op jit(solution)/shard_map/ppermute | solution.py:32
  370.8 13.3 %collective-permute-start.45 = (bf16[64,2048]{1,0:T(8,128)(2,1)S(1)}, bf16[64,2048]{1,0:T(8,128)(2,1)S(1)}, u32[]{:S(2)}, u32[]{:S(2)}) collective-permute-start(bf16[64,2048]{1,0:T(8,128)(2,1)S(1)} %get-tuple-element.118), channel_id=1, source_target_pairs={{0,3},{1,0},{2,1},{3,2},{4,7},{5,4},{6,5},{7,6},{8,11},{9,8},{10,9... | collective-permute-start | bytes 786440 | tf_op jit(solution)/shard_map/ppermute | solution.py:32
  373.4 15.3 %collective-permute-start.46 = (bf16[64,2048]{1,0:T(8,128)(2,1)S(1)}, bf16[64,2048]{1,0:T(8,128)(2,1)S(1)}, u32[]{:S(2)}, u32[]{:S(2)}) collective-permute-start(bf16[64,2048]{1,0:T(8,128)(2,1)S(1)} %get-tuple-element.118), channel_id=1, source_target_pairs={{0,2},{1,3},{2,0},{3,1},{4,6},{5,7},{6,4},{7,5},{8,10},{9,11},{10,... | collective-permute-start | bytes 786440 | tf_op jit(solution)/shard_map/ppermute | solution.py:32
  373.7 14.9 %collective-permute-start.47 = (bf16[64,2048]{1,0:T(8,128)(2,1)S(1)}, bf16[64,2048]{1,0:T(8,128)(2,1)S(1)}, u32[]{:S(2)}, u32[]{:S(2)}) collective-permute-start(bf16[64,2048]{1,0:T(8,128)(2,1)S(1)} %get-tuple-element.118), channel_id=1, source_target_pairs={{0,1},{1,2},{2,3},{3,0},{4,5},{5,6},{6,7},{7,4},{8,9},{9,10},{10,1... | collective-permute-start | bytes 786440 | tf_op jit(solution)/shard_map/ppermute | solution.py:32
  384.1 19.9 %collective-permute-start.37 = (bf16[64,2048]{1,0:T(8,128)(2,1)}, bf16[64,2048]{1,0:T(8,128)(2,1)}, u32[]{:S(2)}, u32[]{:S(2)}) collective-permute-start(bf16[64,2048]{1,0:T(8,128)(2,1)} %get-tuple-element.142), channel_id=1, source_target_pairs={{0,3},{1,0},{2,1},{3,2},{4,7},{5,4},{6,5},{7,6},{8,11},{9,8},{10,9... | collective-permute-start | bytes 786440 | tf_op jit(solution)/shard_map/ppermute | solution.py:32
  400.1 74.9 %reduce-scatter.5.cloned.1.call-start = ((), (), s32[]{:S(2)}) async-start(), calls=%async_computation.6 | async-start | bytes 593920 | tf_op jit(solution)/shard_map/reduce_scatter | solution.py:761
  405.7 15.1 %collective-permute-start.48 = (bf16[64,2048]{1,0:T(8,128)(2,1)S(1)}, bf16[64,2048]{1,0:T(8,128)(2,1)S(1)}, u32[]{:S(2)}, u32[]{:S(2)}) collective-permute-start(bf16[64,2048]{1,0:T(8,128)(2,1)S(1)} %get-tuple-element.138), channel_id=1, source_target_pairs={{0,1},{1,2},{2,3},{3,0},{4,5},{5,6},{6,7},{7,4},{8,9},{9,10},{10,1... | collective-permute-start | bytes 786440 | tf_op jit(solution)/shard_map/ppermute | solution.py:32
  405.8 15.1 %collective-permute-start.49 = (bf16[64,2048]{1,0:T(8,128)(2,1)S(1)}, bf16[64,2048]{1,0:T(8,128)(2,1)S(1)}, u32[]{:S(2)}, u32[]{:S(2)}) collective-permute-start(bf16[64,2048]{1,0:T(8,128)(2,1)S(1)} %get-tuple-element.140), channel_id=1, source_target_pairs={{0,2},{1,3},{2,0},{3,1},{4,6},{5,7},{6,4},{7,5},{8,10},{9,11},{10,... | collective-permute-start | bytes 786440 | tf_op jit(solution)/shard_map/ppermute | solution.py:32
  407.3 14.1 %collective-permute-start.50 = (bf16[64,2048]{1,0:T(8,128)(2,1)S(1)}, bf16[64,2048]{1,0:T(8,128)(2,1)S(1)}, u32[]{:S(2)}, u32[]{:S(2)}) collective-permute-start(bf16[64,2048]{1,0:T(8,128)(2,1)S(1)} %get-tuple-element.139), channel_id=1, source_target_pairs={{0,3},{1,0},{2,1},{3,2},{4,7},{5,4},{6,5},{7,6},{8,11},{9,8},{10,9... | collective-permute-start | bytes 786440 | tf_op jit(solution)/shard_map/ppermute | solution.py:32
  433.8 8.5 %collective-permute-start.52 = (bf16[320,256]{1,0:T(8,128)(2,1)S(1)}, bf16[320,256]{1,0:T(8,128)(2,1)S(1)}, u32[]{:S(2)}, u32[]{:S(2)}) collective-permute-start(bf16[320,256]{1,0:T(8,128)(2,1)S(1)} %get-tuple-element.160), channel_id=1, source_target_pairs={{0,1},{1,2},{2,3},{3,0},{4,5},{5,6},{6,7},{7,4},{8,9},{9,10},{10,1... | collective-permute-start | bytes 491528 | tf_op jit(solution)/shard_map/ppermute | solution.py:32
  434.1 14.4 %collective-permute-start.53 = (bf16[320,256]{1,0:T(8,128)(2,1)S(1)}, bf16[320,256]{1,0:T(8,128)(2,1)S(1)}, u32[]{:S(2)}, u32[]{:S(2)}) collective-permute-start(bf16[320,256]{1,0:T(8,128)(2,1)S(1)} %get-tuple-element.162), channel_id=1, source_target_pairs={{0,2},{1,3},{2,0},{3,1},{4,6},{5,7},{6,4},{7,5},{8,10},{9,11},{10,... | collective-permute-start | bytes 491528 | tf_op jit(solution)/shard_map/ppermute | solution.py:32
  437.5 11.1 %collective-permute-start.54 = (bf16[320,256]{1,0:T(8,128)(2,1)S(1)}, bf16[320,256]{1,0:T(8,128)(2,1)S(1)}, u32[]{:S(2)}, u32[]{:S(2)}) collective-permute-start(bf16[320,256]{1,0:T(8,128)(2,1)S(1)} %get-tuple-element.161), channel_id=1, source_target_pairs={{0,3},{1,0},{2,1},{3,2},{4,7},{5,4},{6,5},{7,6},{8,11},{9,8},{10,9... | collective-permute-start | bytes 491528 | tf_op jit(solution)/shard_map/ppermute | solution.py:32
  438.5 57.5 %collective-permute-start.51 = (bf16[64,2048]{1,0:T(8,128)(2,1)}, bf16[64,2048]{1,0:T(8,128)(2,1)}, u32[]{:S(2)}, u32[]{:S(2)}) collective-permute-start(bf16[64,2048]{1,0:T(8,128)(2,1)} %get-tuple-element.182), channel_id=1, source_target_pairs={{0,64},{64,0},{1,65},{65,1},{2,66},{66,2},{3,67},{67,3},{4,68},{68... | collective-permute-start | bytes 786440 | tf_op jit(solution)/shard_map/ppermute | solution.py:518
  453.2 9.3 %collective-permute-start.58 = (bf16[64,256]{1,0:T(8,128)(2,1)}, bf16[64,256]{1,0:T(8,128)(2,1)}, u32[]{:S(2)}, u32[]{:S(2)}) collective-permute-start(bf16[64,256]{1,0:T(8,128)(2,1)} %get-tuple-element.253), channel_id=1, source_target_pairs={{16,0},{20,4},{24,8},{28,12},{32,16},{36,20},{40,24},{44,28},{48,3... | collective-permute-start | bytes 98312 | tf_op jit(solution)/shard_map/ppermute | solution.py:38
  490.8 23.2 %collective-permute-start.59 = (bf16[64,2048]{1,0:T(8,128)(2,1)S(1)}, bf16[64,2048]{1,0:T(8,128)(2,1)S(1)}, u32[]{:S(2)}, u32[]{:S(2)}) collective-permute-start(bf16[64,2048]{1,0:T(8,128)(2,1)S(1)} %select_convert_fusion), channel_id=1, source_target_pairs={{0,64},{64,0},{1,65},{65,1},{2,66},{66,2},{3,67},{67,3},{4,68},{68... | collective-permute-start | bytes 786440 | tf_op jit(solution)/shard_map/ppermute | solution.py:518
  516.3 11.4 %collective-permute-start.77 = (bf16[2,21,16,128]{3,2,1,0:T(8,128)(2,1)S(1)}, bf16[2,21,16,128]{3,2,1,0:T(8,128)(2,1)S(1)}, u32[]{:S(2)}, u32[]{:S(2)}) collective-permute-start(bf16[2,21,16,128]{3,2,1,0:T(8,128)(2,1)S(1)} %get-tuple-element.175), channel_id=1, source_target_pairs={{0,2},{1,3},{2,0},{3,1},{4,6},{5,7},{6,4},{7,5},{8,10},{9,11},{10,... | collective-permute-start | bytes 516104 | tf_op jit(solution)/shard_map/ppermute | solution.py:32
  (166 other events, 2915.8 us)
Sparse Core Ops, SparseCore 0:
  11.6 122.3 all-gather.3
  136.9 71.8 all-gather.5
  211.6 72.0 all-gather.7
  400.2 20.3 reduce-scatter.2
  423.5 26.5 reduce-scatter.4

commit v14 on v11

--- a/solution.py
+++ b/solution.py
@@ -562,24 +562,19 @@
         cut = shard.shape[1] // 2
         return shard[:, :cut], shard[:, cut:]
 
+    keyval_half = jnp.where(tensor % 2 == 0, keyval_weight[0][:, :head], keyval_weight[0][:, head:])
     early_all = gather_all(
-        jnp.concatenate([query_weight[0], row_major(output_weight[0].T)], axis=1)
-    )
+        jnp.concatenate([query_weight[0], row_major(output_weight[0].T), keyval_half], axis=1)
+    )
+    keyval_ws = [
+        jnp.concatenate(
+            [early_all[x, :, layer, :, 2 * local_q :].reshape(width, head) for x in range(2)], axis=1
+        )
+        for layer in range(2)
+    ]
 
     def crossed(block, mask):
         return lax.ppermute(block, both, [(i, i ^ mask) for i in range(8 * chips)])
-
-    shard = keyval_weight[0]
-    pairs = by_layer(
-        jnp.stack([shard, crossed(shard, 2)]),
-        jnp.stack([crossed(shard, 4 * chips), crossed(shard, 4 * chips + 2)]),
-    )
-    quads = jnp.stack(pairs, axis=1)
-    quads = jnp.stack([quads] + [crossed(quads, 4 * k) for k in range(1, chips)])
-    blocks = jnp.stack([quads, crossed(quads, 1)], axis=2)
-    blocks = blocks.reshape((4 * chips, 2) + shard.shape)
-    keyval_all = jnp.take(blocks, jnp.arange(4 * chips, dtype=jnp.int32) ^ data, axis=0, mode="clip")
-    keyval_ws = [keyval_all[:, layer].reshape(width, 2 * head) for layer in range(2)]
 
     vectors = jnp.concatenate(
         [
@@ -851,11 +846,11 @@
 
     fresh = lax.dynamic_index_in_dim(block_input, section, 0, keepdims=False).astype(f32)
     given = lax.dynamic_index_in_dim(cotangent, section, 0, keepdims=False).astype(f32)
-    branch_one = spread(given.astype(bf16))
-    fresh, branch_one = lax.optimization_barrier((fresh, branch_one))
-
     middle_zero, kept_zero = forward_attend(0, fresh)
     unit_zero, rsd_zero, second_zero, up_bias = feed_inputs(0, middle_zero)
+    own_rows, second_zero = lax.optimization_barrier((given.astype(bf16), second_zero))
+    branch_one = spread(own_rows)
+    second_zero, branch_one = lax.optimization_barrier((second_zero, branch_one))
     active_zero, slope_zero, low_u_zero, low_d_zero, partial = feed_call(
         feed_kernel,
         "feed",

time: 547 us -> 540 us (0.987)
  waiting for transfers between devices: 217 us -> 229 us
  starting transfers between devices: 134 us -> 124 us
    all_gather x1, waiting for transfers between devices: 3.54 us -> 52.7 us  [gather_all(): lax.all_gather(row_major(shard), every, axis=0, tiled=True, axis_index_gr...]
    all_gather x2, waiting for transfers between devices: 45.7 us -> 0.04 us  [gather(): lax.all_gather(row_major(shard), both, axis=0, tiled=True, axis_index_gro...]
    ppermute x5, waiting for transfers between devices: 12.1 us -> 24.5 us  [swap(): return lax.ppermute(value, 'section', sides)]
    ppermute x9 -> x2, starting transfers between devices: 15.1 us -> 3.69 us  [crossed(): return lax.ppermute(block, both, [(i, i ^ mask) for i in range(8 * chips)])]
    ppermute x9 -> x2, waiting for transfers between devices: 12.3 us -> 3.26 us  [crossed(): return lax.ppermute(block, both, [(i, i ^ mask) for i in range(8 * chips)])]
    ppermute x45, waiting for transfers between devices: 118 us -> 125 us  [around(): lax.ppermute(block, axis, [(i, (i + distance) % size) for i in range(size)])]
    another operation x8 -> x4, other arithmetic: 7.12 us -> 0.48 us  [the longest x2 5.84 us: per_device(): blocks = jnp.stack([quads, crossed(quads, 1)], axis=2)]
    unnamed x324 -> x296, local copies, waits for them, and re-layouts: 15.1 us -> 13.6 us
  transfers between devices with their start and end apart: 89 -> 82, of which waited for: 56 -> 55; matrix products, arithmetic and copies ran while one was open for 11% -> 10% of each run, Pallas kernels for 7% -> 7%
where the time goes in v14:
time: 540 us; the launch traced here: 531 us
  waiting for transfers between devices  229 us (42%)
  starting transfers between devices  124 us (23%)
  Pallas kernels  87.1 us (16%)
  other arithmetic  30.3 us (6%)
  local copies, waits for them, and re-layouts  29.3 us (5%)
  between operations  21.2 us (4%)
  matrix products  10.4 us (2%)
    ppermute x45, waiting for transfers between devices, around(): lax.ppermute(block, axis, [(i, (i + distance) % size) for i in range(size)])  125 us
    ppermute x45, starting transfers between devices, around(): lax.ppermute(block, axis, [(i, (i + distance) % size) for i in range(size)])  62 us
    all_gather x1, waiting for transfers between devices, gather_all(): lax.all_gather(row_major(shard), every, axis=0, tiled=True, axis_index_gr...  52.7 us
    pallas_call x3, Pallas kernels, feed_call(): pl.pallas_call(kernel, in_specs=[remote if value.ndim == 4 or i in copied...  35.4 us
    ppermute x16, starting transfers between devices, along(): return lax.ppermute(block, axis, route)  32.1 us
    ppermute x5, waiting for transfers between devices, swap(): return lax.ppermute(value, 'section', sides)  24.5 us
    pallas_call x2, Pallas kernels, attend_back(): pl.pallas_call(lambda *refs: attend_back_kernel(layer, head, *refs), in_s...  22.9 us
    pallas_call x2, Pallas kernels, attend(): pl.pallas_call(lambda *refs: attend_kernel(layer, head, *refs), in_specs=...  20 us
  transfers between devices with their start and end apart: 82, of which 55 were waited for; matrix products, arithmetic and copies ran while one was open for 10% of the time, Pallas kernels for 7%

profile of v14, /device:TPU:0, one launch (start us, length us, event | category | flops | bytes accessed | tf_op | source)
XLA Modules:
  0.0 531.2 jit_solution(2312528842014827279)
XLA Ops:
  12.3 4.0 collective-permute-start.18
  16.4 12.2 %collective-permute-done.18 = bf16[128,2048]{1,0:T(8,128)(2,1)S(1)} collective-permute-done((bf16[128,2048]{1,0:T(8,128)(2,1)S(1)}, bf16[128,2048]{1,0:T(8,128)(2,1)S(1)}, u32[]{:S(2)}, u32[]{:S(2)}) %collective-permute-start.18) | collective-permute-done | bytes 524320 | tf_op jit(solution)/shard_map/ppermute | solution.py:518
  47.7 4.2 collective-permute-start.1
  54.4 12.3 %collective-permute-done = bf16[1,14592]{1,0:T(2,128)(2,1)S(1)} collective-permute-done((bf16[1,14592]{1,0:T(2,128)(2,1)S(1)}, bf16[1,14592]{1,0:T(2,128)(2,1)S(1)}, u32[]{:S(2)}, u32[]{:S(2)}) %collective-permute-start) | collective-permute-done | bytes 29216 | tf_op jit(solution)/shard_map/ppermute | solution.py:518
  81.3 52.7 %all-gather.4.cloned.1.call-done = bf16[16384,1152]{1,0:T(8,128)(2,1)} async-done(((bf16[128,1152]{1,0:T(8,128)(2,1)}), bf16[16384,1152]{1,0:T(8,128)(2,1)}) %all-gather.4.cloned.1.call-update) | async-done | bytes 37748752 | tf_op jit(solution)/shard_map/all_gather | solution.py:556
  137.3 3.4 collective-permute-start.5
  143.0 4.1 collective-permute-start.7
  152.8 4.4 project_queries.2
  160.2 5.5 %collective-permute-done.11 = bf16[320,256]{1,0:T(8,128)(2,1)S(1)} collective-permute-done((bf16[320,256]{1,0:T(8,128)(2,1)S(1)}, bf16[320,256]{1,0:T(8,128)(2,1)S(1)}, u32[]{:S(2)}, u32[]{:S(2)}) %collective-permute-start.11) | collective-permute-done | bytes 163872 | tf_op jit(solution)/shard_map/ppermute | solution.py:32
  165.8 10.5 %attend.2 = (bf16[4,256,1280]{2,1,0:T(8,128)(2,1)S(1)}, bf16[64,2048]{1,0:T(8,128)(2,1)S(1)}, bf16[64,16]{1,0:T(8,128)(2,1)S(1)}, f32[64,2048]{1,0:T(8,128)S(1)}) custom-call(bf16[64,2048]{1,0:T(8,128)(2,1)S(1)} %get-tuple-element.58.refs_0_.refs_5_, bf16[1280,256]{1,0:T(8,128)(2,1)S(1)} %constant_dynamic-update-slice_fusion.26.refs_1_.refs_6_, ...), custom_call_target="tpu_custom_call" | custom-call | flops 2818572288 | bytes 8388608 | tf_op jit(solution)/shard_map/attend/pallas_call | solution.py:180
  181.1 5.2 collective-permute-done.12
  187.9 4.7 collective-permute-done.14
  195.6 6.3 %collective-permute-done.15 = bf16[64,2048]{1,0:T(8,128)(2,1)S(1)} collective-permute-done((bf16[64,2048]{1,0:T(8,128)(2,1)S(1)}, bf16[64,2048]{1,0:T(8,128)(2,1)S(1)}, u32[]{:S(2)}, u32[]{:S(2)}) %collective-permute-start.15) | collective-permute-done | bytes 262176 | tf_op jit(solution)/shard_map/ppermute | solution.py:32
  204.7 3.7 collective-permute-done.17
  209.4 10.8 %feed.1 = (bf16[256,2048]{1,0:T(8,128)(2,1)S(1)}, bf16[256,2048]{1,0:T(8,128)(2,1)S(1)}, bf16[256,16]{1,0:T(8,128)(2,1)S(1)}, bf16[256,16]{1,0:T(8,128)(2,1)S(1)}, bf16[256,2048]{1,0:T(8,128)(2,1)S(1)}) custom-call(bf16[256,2048]{1,0:T(8,128)(2,1)S(1)} %pad_maximum_fusion.1.second_ref, bf16[4,2,512,2048]{3,2,1,0:T(8,128)(2,1)} %bitcast.698, ...), custom_call_target="tpu_custom_call" | custom-call | flops 4294967296 | bytes 16777216 | tf_op jit(solution)/shard_map/feed/pallas_call | solution.py:448
  226.2 3.8 collective-permute-done.19
  230.0 6.1 %collective-permute-done.20 = bf16[64,2048]{1,0:T(8,128)(2,1)S(1)} collective-permute-done((bf16[64,2048]{1,0:T(8,128)(2,1)S(1)}, bf16[64,2048]{1,0:T(8,128)(2,1)S(1)}, u32[]{:S(2)}, u32[]{:S(2)}) %collective-permute-start.20) | collective-permute-done | bytes 262176 | tf_op jit(solution)/shard_map/ppermute | solution.py:32
  237.7 3.4 collective-permute-start.22
  242.4 4.2 collective-permute-start.24
  252.6 4.4 project_queries.3
  259.8 4.6 collective-permute-done.28
  264.5 9.5 %attend.3 = (bf16[4,256,1280]{2,1,0:T(8,128)(2,1)S(1)}, bf16[64,2048]{1,0:T(8,128)(2,1)S(1)}, bf16[64,16]{1,0:T(8,128)(2,1)S(1)}, f32[64,2048]{1,0:T(8,128)S(1)}) custom-call(bf16[64,2048]{1,0:T(8,128)(2,1)S(1)} %get-tuple-element.64.refs_0_.refs_5_, bf16[1280,256]{1,0:T(8,128)(2,1)S(1)} %constant_dynamic-update-slice_fusion.39.refs_1_.refs_6_, ...), custom_call_target="tpu_custom_call" | custom-call | flops 2818572288 | bytes 8388608 | tf_op jit(solution)/shard_map/attend/pallas_call | solution.py:180
  279.2 4.6 collective-permute-done.29
  286.1 5.4 %collective-permute-done.31 = bf16[64,2048]{1,0:T(8,128)(2,1)S(1)} collective-permute-done((bf16[64,2048]{1,0:T(8,128)(2,1)S(1)}, bf16[64,2048]{1,0:T(8,128)(2,1)S(1)}, u32[]{:S(2)}, u32[]{:S(2)}) %collective-permute-start.31) | collective-permute-done | bytes 262176 | tf_op jit(solution)/shard_map/ppermute | solution.py:32
  293.3 14.5 %feed_both.1 = (bf16[256,2048]{1,0:T(8,128)(2,1)S(1)}, bf16[256,16]{1,0:T(8,128)(2,1)S(1)}, bf16[256,16]{1,0:T(8,128)(2,1)S(1)}, bf16[256,2048]{1,0:T(8,128)(2,1...) custom-call(bf16[256,2048]{1,0:T(8,128)(2,1)S(1)} %pad_maximum_fusio, ...), custom_call_target="tpu_custom_call" | custom-call | flops 8589934592 | bytes 16777216 | tf_op jit(solution)/shard_map/feed_both/pallas_call | solution.py:448
  315.6 9.3 %collective-permute-done.32 = bf16[64,2048]{1,0:T(8,128)(2,1)S(1)} collective-permute-done((bf16[64,2048]{1,0:T(8,128)(2,1)S(1)}, bf16[64,2048]{1,0:T(8,128)(2,1)S(1)}, u32[]{:S(2)}, u32[]{:S(2)}) %collective-permute-start.32) | collective-permute-done | bytes 262176 | tf_op jit(solution)/shard_map/ppermute | solution.py:32
  326.3 11.5 %attend_back.2 = (bf16[64,2048]{1,0:T(8,128)(2,1)S(1)}, bf16[1280,256]{1,0:T(8,128)(2,1)S(1)}, bf16[64,16]{1,0:T(8,128)(2,1)S(1)}, bf16[64,16]{1,0:T(8,128)(2,1)S(1)}, f32[64,2048]{1,0:T(8,128)S(1)}) custom-call(bf16[64,2048]{1,0:T(8,128)(2,1)S(1)} %get-tuple-element.123.refs_0_, bf16[4,4,2,512,1152]{4,3,2,1,0:T(8,128)(2,1)} %bitcast.696, ...), custom_call_target="tpu_custom_call" | custom-call | flops 5637144576 | bytes 22020096 | tf_op jit(solution)/shard_map/attend_back/pallas_call | solution.py:259
  339.0 3.0 collective-permute-start.39
  344.9 4.7 collective-permute-done.39
  357.8 3.0 collective-permute-start.36
  375.8 4.2 collective-permute-done.45
  380.1 5.0 collective-permute-done.47
  386.3 10.0 %feed_back.1 = (bf16[256,2048]{1,0:T(8,128)(2,1)S(1)}, bf16[256,16]{1,0:T(8,128)(2,1)S(1)}, bf16[256,16]{1,0:T(8,128)(2,1)S(1)}, bf16[256,2048]{1,0:T(8,128)(2,1)S(1)}) custom-call(bf16[256,2048]{1,0:T(8,128)(2,1)S(1)} %pad_maximum_fusion.5.branch_ref, bf16[4,2,512,2048]{3,2,1,0:T(8,128)(2,1)} %bitcast.699, bf16[256,2048]{1,0:T(8,128)(2,1)S(1)} %copy-done.17, ...), custom_call_target="tpu_custom_call" | custom-call | flops 4294967296 | bytes 16777216 | tf_op jit(solution)/shard_map/feed_back/pallas_call | solution.py:448
  397.6 3.6 collective-permute-start.49
  402.6 3.6 collective-permute-done.48
  406.2 6.8 %collective-permute-done.49 = bf16[64,2048]{1,0:T(8,128)(2,1)S(1)} collective-permute-done((bf16[64,2048]{1,0:T(8,128)(2,1)S(1)}, bf16[64,2048]{1,0:T(8,128)(2,1)S(1)}, u32[]{:S(2)}, u32[]{:S(2)}) %collective-permute-start.49) | collective-permute-done | bytes 262176 | tf_op jit(solution)/shard_map/ppermute | solution.py:32
  413.7 11.5 %attend_back.3 = (bf16[64,2048]{1,0:T(8,128)(2,1)S(1)}, bf16[1280,256]{1,0:T(8,128)(2,1)S(1)}, bf16[64,16]{1,0:T(8,128)(2,1)S(1)}, bf16[64,16]{1,0:T(8,128)(2,1)S(1)}, f32[64,2048]{1,0:T(8,128)S(1)}) custom-call(bf16[64,2048]{1,0:T(8,128)(2,1)S(1)} %get-tuple-element.115.refs_0_, bf16[4,4,2,512,1152]{4,3,2,1,0:T(8,128)(2,1)} %bitcast.697, ...), custom_call_target="tpu_custom_call" | custom-call | flops 5637144576 | bytes 22020096 | tf_op jit(solution)/shard_map/attend_back/pallas_call | solution.py:259
  425.4 3.5 collective-permute-start.53
  431.9 4.6 collective-permute-done.53
  442.2 3.0 collective-permute-done.56
  446.8 4.0 collective-permute-done.58
  454.0 3.6 collective-permute-start.61
  458.1 5.4 %collective-permute-done.60 = bf16[2,29,16,128]{3,2,1,0:T(8,128)(2,1)S(1)} collective-permute-done((bf16[2,29,16,128]{3,2,1,0:T(8,128)(2,1)S(1)}, bf16[2,29,16,128]{3,2,1,0:T(8,128)(2,1)S(1)}, u32[]{:S(2)}, u32[]{:S(2)}) %collective-permute-start.60) | collective-permute-done | bytes 237600 | tf_op jit(solution)/shard_map/ppermute | solution.py:32
  463.5 4.8 collective-permute-done.61
  471.1 4.2 collective-permute-done.64
  477.3 3.1 collective-permute-start.66
  507.1 3.9 collective-permute-start.77
  514.5 4.5 collective-permute-done.77
  (650 shorter events, 184.6 us)
Async XLA Ops:
  7.2 126.8 %all-gather.4.cloned.1.call-start = ((), (), s32[]{:S(2)}) async-start(), calls=%async_computation | async-start | bytes 38043648 | tf_op jit(solution)/shard_map/all_gather | solution.py:556
  10.8 198.6 %all-gather.6.cloned.1.call-start = ((), (), s32[]{:S(2)}) async-start(), calls=%async_computation.1 | async-start | bytes 17301504 | tf_op jit(solution)/shard_map/all_gather | solution.py:552
  12.3 16.3 %collective-permute-start.18 = (bf16[128,2048]{1,0:T(8,128)(2,1)S(1)}, bf16[128,2048]{1,0:T(8,128)(2,1)S(1)}, u32[]{:S(2)}, u32[]{:S(2)}) collective-permute-start(bf16[128,2048]{1,0:T(8,128)(2,1)S(1)} %broadcast_select_fusion.2), channel_id=1, source_target_pairs={{0,64},{64,0},{1,65},{65,1},{2,66},{66,2},{3,67},{67,3},{4,68},{68... | collective-permute-start | bytes 1572872 | tf_op jit(solution)/shard_map/ppermute | solution.py:518
  30.0 261.6 %all-gather.8.cloned.1.call-start = ((), (), s32[]{:S(2)}) async-start(), calls=%async_computation.2 | async-start | bytes 17301504 | tf_op jit(solution)/shard_map/all_gather | solution.py:552
  47.7 20.0 %collective-permute-start.1 = (bf16[16,8256]{1,0:T(8,128)(2,1)S(1)}, bf16[16,8256]{1,0:T(8,128)(2,1)S(1)}, u32[]{:S(2)}, u32[]{:S(2)}) collective-permute-start(bf16[16,8256]{1,0:T(8,128)(2,1)S(1)} %concatenate.208), channel_id=1, source_target_pairs={{0,64},{64,0},{1,65},{65,1},{2,66},{66,2},{3,67},{67,3},{4,68},{68... | collective-permute-start | bytes 792584 | tf_op jit(solution)/shard_map/ppermute | solution.py:518
  52.1 14.6 %collective-permute-start = (bf16[1,14592]{1,0:T(2,128)(2,1)S(1)}, bf16[1,14592]{1,0:T(2,128)(2,1)S(1)}, u32[]{:S(2)}, u32[]{:S(2)}) collective-permute-start(bf16[1,14592]{1,0:T(2,128)(2,1)S(1)} %constant_dynamic-update-slice_fusion), channel_id=1, source_target_pairs={{0,64},{64,0},{1,65},{65,1},{2,66},{66,2},{3,67},{67,3},{4,68},{68... | collective-permute-start | bytes 87560 | tf_op jit(solution)/shard_map/ppermute | solution.py:518
  67.8 8.8 %collective-permute-start.2 = (bf16[16,5696]{1,0:T(8,128)(2,1)S(1)}, bf16[16,5696]{1,0:T(8,128)(2,1)S(1)}, u32[]{:S(2)}, u32[]{:S(2)}) collective-permute-start(bf16[16,5696]{1,0:T(8,128)(2,1)S(1)} %get-tuple-element.251), channel_id=1, source_target_pairs={{0,1},{1,2},{2,3},{3,0},{4,5},{5,6},{6,7},{7,4},{8,9},{9,10},{10,1... | collective-permute-start | bytes 546824 | tf_op jit(solution)/shard_map/ppermute | solution.py:32
  69.2 9.4 %collective-permute-start.3 = (bf16[16,5696]{1,0:T(8,128)(2,1)S(1)}, bf16[16,5696]{1,0:T(8,128)(2,1)S(1)}, u32[]{:S(2)}, u32[]{:S(2)}) collective-permute-start(bf16[16,5696]{1,0:T(8,128)(2,1)S(1)} %get-tuple-element.251), channel_id=1, source_target_pairs={{0,2},{1,3},{2,0},{3,1},{4,6},{5,7},{6,4},{7,5},{8,10},{9,11},{10,... | collective-permute-start | bytes 546824 | tf_op jit(solution)/shard_map/ppermute | solution.py:32
  137.3 11.3 %collective-permute-start.5 = (bf16[64,256]{1,0:T(8,128)(2,1)S(1)}, bf16[64,256]{1,0:T(8,128)(2,1)S(1)}, u32[]{:S(2)}, u32[]{:S(2)}) collective-permute-start(bf16[64,256]{1,0:T(8,128)(2,1)S(1)} %fusion.20), channel_id=1, source_target_pairs={{0,16},{4,20},{8,24},{12,28},{16,32},{20,36},{24,40},{28,44},{32,4... | collective-permute-start | bytes 98312 | tf_op jit(solution)/shard_map/ppermute | solution.py:38
  149.5 9.0 %collective-permute-start.9 = (bf16[320,256]{1,0:T(8,128)(2,1)S(1)}, bf16[320,256]{1,0:T(8,128)(2,1)S(1)}, u32[]{:S(2)}, u32[]{:S(2)}) collective-permute-start(bf16[320,256]{1,0:T(8,128)(2,1)S(1)} %get-tuple-element.317), channel_id=1, source_target_pairs={{0,3},{1,0},{2,1},{3,2},{4,7},{5,4},{6,5},{7,6},{8,11},{9,8},{10,9... | collective-permute-start | bytes 491528 | tf_op jit(solution)/shard_map/ppermute | solution.py:32
  157.2 8.5 %collective-permute-start.11 = (bf16[320,256]{1,0:T(8,128)(2,1)S(1)}, bf16[320,256]{1,0:T(8,128)(2,1)S(1)}, u32[]{:S(2)}, u32[]{:S(2)}) collective-permute-start(bf16[320,256]{1,0:T(8,128)(2,1)S(1)} %get-tuple-element.317), channel_id=1, source_target_pairs={{0,1},{1,2},{2,3},{3,0},{4,5},{5,6},{6,7},{7,4},{8,9},{9,10},{10,1... | collective-permute-start | bytes 491528 | tf_op jit(solution)/shard_map/ppermute | solution.py:32
  177.0 9.2 %collective-permute-start.12 = (bf16[64,2048]{1,0:T(8,128)(2,1)S(1)}, bf16[64,2048]{1,0:T(8,128)(2,1)S(1)}, u32[]{:S(2)}, u32[]{:S(2)}) collective-permute-start(bf16[64,2048]{1,0:T(8,128)(2,1)S(1)} %add_convert_fusion.3), channel_id=1, source_target_pairs={{0,3},{1,0},{2,1},{3,2},{4,7},{5,4},{6,5},{7,6},{8,11},{9,8},{10,9... | collective-permute-start | bytes 786440 | tf_op jit(solution)/shard_map/ppermute | solution.py:32
  177.1 10.8 %collective-permute-start.13 = (bf16[64,2048]{1,0:T(8,128)(2,1)S(1)}, bf16[64,2048]{1,0:T(8,128)(2,1)S(1)}, u32[]{:S(2)}, u32[]{:S(2)}) collective-permute-start(bf16[64,2048]{1,0:T(8,128)(2,1)S(1)} %add_convert_fusion.3), channel_id=1, source_target_pairs={{0,2},{1,3},{2,0},{3,1},{4,6},{5,7},{6,4},{7,5},{8,10},{9,11},{10,... | collective-permute-start | bytes 786440 | tf_op jit(solution)/shard_map/ppermute | solution.py:32
  178.1 14.5 %collective-permute-start.14 = (bf16[64,2048]{1,0:T(8,128)(2,1)S(1)}, bf16[64,2048]{1,0:T(8,128)(2,1)S(1)}, u32[]{:S(2)}, u32[]{:S(2)}) collective-permute-start(bf16[64,2048]{1,0:T(8,128)(2,1)S(1)} %add_convert_fusion.3), channel_id=1, source_target_pairs={{0,1},{1,2},{2,3},{3,0},{4,5},{5,6},{6,7},{7,4},{8,9},{9,10},{10,1... | collective-permute-start | bytes 786440 | tf_op jit(solution)/shard_map/ppermute | solution.py:32
  192.7 9.2 %collective-permute-start.15 = (bf16[64,2048]{1,0:T(8,128)(2,1)S(1)}, bf16[64,2048]{1,0:T(8,128)(2,1)S(1)}, u32[]{:S(2)}, u32[]{:S(2)}) collective-permute-start(bf16[64,2048]{1,0:T(8,128)(2,1)S(1)} %dynamic-slice_bitcast_fusion), channel_id=1, source_target_pairs={{0,3},{1,0},{2,1},{3,2},{4,7},{5,4},{6,5},{7,6},{8,11},{9,8},{10,9... | collective-permute-start | bytes 786440 | tf_op jit(solution)/shard_map/ppermute | solution.py:32
  193.9 10.8 %collective-permute-start.16 = (bf16[64,2048]{1,0:T(8,128)(2,1)S(1)}, bf16[64,2048]{1,0:T(8,128)(2,1)S(1)}, u32[]{:S(2)}, u32[]{:S(2)}) collective-permute-start(bf16[64,2048]{1,0:T(8,128)(2,1)S(1)} %dynamic-slice_bitcast_fusion), channel_id=1, source_target_pairs={{0,2},{1,3},{2,0},{3,1},{4,6},{5,7},{6,4},{7,5},{8,10},{9,11},{10,... | collective-permute-start | bytes 786440 | tf_op jit(solution)/shard_map/ppermute | solution.py:32
  194.3 14.1 %collective-permute-start.17 = (bf16[64,2048]{1,0:T(8,128)(2,1)S(1)}, bf16[64,2048]{1,0:T(8,128)(2,1)S(1)}, u32[]{:S(2)}, u32[]{:S(2)}) collective-permute-start(bf16[64,2048]{1,0:T(8,128)(2,1)S(1)} %dynamic-slice_bitcast_fusion), channel_id=1, source_target_pairs={{0,1},{1,2},{2,3},{3,0},{4,5},{5,6},{6,7},{7,4},{8,9},{9,10},{10,1... | collective-permute-start | bytes 786440 | tf_op jit(solution)/shard_map/ppermute | solution.py:32
  220.4 9.6 %collective-permute-start.19 = (bf16[64,2048]{1,0:T(8,128)(2,1)S(1)}, bf16[64,2048]{1,0:T(8,128)(2,1)S(1)}, u32[]{:S(2)}, u32[]{:S(2)}) collective-permute-start(bf16[64,2048]{1,0:T(8,128)(2,1)S(1)} %get-tuple-element.147), channel_id=1, source_target_pairs={{0,1},{1,2},{2,3},{3,0},{4,5},{5,6},{6,7},{7,4},{8,9},{9,10},{10,1... | collective-permute-start | bytes 786440 | tf_op jit(solution)/shard_map/ppermute | solution.py:32
  221.4 14.7 %collective-permute-start.20 = (bf16[64,2048]{1,0:T(8,128)(2,1)S(1)}, bf16[64,2048]{1,0:T(8,128)(2,1)S(1)}, u32[]{:S(2)}, u32[]{:S(2)}) collective-permute-start(bf16[64,2048]{1,0:T(8,128)(2,1)S(1)} %get-tuple-element.149), channel_id=1, source_target_pairs={{0,2},{1,3},{2,0},{3,1},{4,6},{5,7},{6,4},{7,5},{8,10},{9,11},{10,... | collective-permute-start | bytes 786440 | tf_op jit(solution)/shard_map/ppermute | solution.py:32
  224.1 12.1 %collective-permute-start.21 = (bf16[64,2048]{1,0:T(8,128)(2,1)S(1)}, bf16[64,2048]{1,0:T(8,128)(2,1)S(1)}, u32[]{:S(2)}, u32[]{:S(2)}) collective-permute-start(bf16[64,2048]{1,0:T(8,128)(2,1)S(1)} %get-tuple-element.148), channel_id=1, source_target_pairs={{0,3},{1,0},{2,1},{3,2},{4,7},{5,4},{6,5},{7,6},{8,11},{9,8},{10,9... | collective-permute-start | bytes 786440 | tf_op jit(solution)/shard_map/ppermute | solution.py:32
  237.7 10.5 %collective-permute-start.22 = (bf16[64,256]{1,0:T(8,128)(2,1)S(1)}, bf16[64,256]{1,0:T(8,128)(2,1)S(1)}, u32[]{:S(2)}, u32[]{:S(2)}) collective-permute-start(bf16[64,256]{1,0:T(8,128)(2,1)S(1)} %fusion.21), channel_id=1, source_target_pairs={{0,16},{4,20},{8,24},{12,28},{16,32},{20,36},{24,40},{28,44},{32,4... | collective-permute-start | bytes 98312 | tf_op jit(solution)/shard_map/ppermute | solution.py:38
  249.1 8.8 %collective-permute-start.26 = (bf16[320,256]{1,0:T(8,128)(2,1)S(1)}, bf16[320,256]{1,0:T(8,128)(2,1)S(1)}, u32[]{:S(2)}, u32[]{:S(2)}) collective-permute-start(bf16[320,256]{1,0:T(8,128)(2,1)S(1)} %get-tuple-element.307), channel_id=1, source_target_pairs={{0,3},{1,0},{2,1},{3,2},{4,7},{5,4},{6,5},{7,6},{8,11},{9,8},{10,9... | collective-permute-start | bytes 491528 | tf_op jit(solution)/shard_map/ppermute | solution.py:32
  274.8 9.0 %collective-permute-start.29 = (bf16[64,2048]{1,0:T(8,128)(2,1)S(1)}, bf16[64,2048]{1,0:T(8,128)(2,1)S(1)}, u32[]{:S(2)}, u32[]{:S(2)}) collective-permute-start(bf16[64,2048]{1,0:T(8,128)(2,1)S(1)} %add_convert_fusion.1), channel_id=1, source_target_pairs={{0,3},{1,0},{2,1},{3,2},{4,7},{5,4},{6,5},{7,6},{8,11},{9,8},{10,9... | collective-permute-start | bytes 786440 | tf_op jit(solution)/shard_map/ppermute | solution.py:32
  275.3 10.7 %collective-permute-start.30 = (bf16[64,2048]{1,0:T(8,128)(2,1)S(1)}, bf16[64,2048]{1,0:T(8,128)(2,1)S(1)}, u32[]{:S(2)}, u32[]{:S(2)}) collective-permute-start(bf16[64,2048]{1,0:T(8,128)(2,1)S(1)} %add_convert_fusion.1), channel_id=1, source_target_pairs={{0,2},{1,3},{2,0},{3,1},{4,6},{5,7},{6,4},{7,5},{8,10},{9,11},{10,... | collective-permute-start | bytes 786440 | tf_op jit(solution)/shard_map/ppermute | solution.py:32
  277.1 14.3 %collective-permute-start.31 = (bf16[64,2048]{1,0:T(8,128)(2,1)S(1)}, bf16[64,2048]{1,0:T(8,128)(2,1)S(1)}, u32[]{:S(2)}, u32[]{:S(2)}) collective-permute-start(bf16[64,2048]{1,0:T(8,128)(2,1)S(1)} %add_convert_fusion.1), channel_id=1, source_target_pairs={{0,1},{1,2},{2,3},{3,0},{4,5},{5,6},{6,7},{7,4},{8,9},{9,10},{10,1... | collective-permute-start | bytes 786440 | tf_op jit(solution)/shard_map/ppermute | solution.py:32
  309.7 15.2 %collective-permute-start.32 = (bf16[64,2048]{1,0:T(8,128)(2,1)S(1)}, bf16[64,2048]{1,0:T(8,128)(2,1)S(1)}, u32[]{:S(2)}, u32[]{:S(2)}) collective-permute-start(bf16[64,2048]{1,0:T(8,128)(2,1)S(1)} %get-tuple-element.144), channel_id=1, source_target_pairs={{0,1},{1,2},{2,3},{3,0},{4,5},{5,6},{6,7},{7,4},{8,9},{9,10},{10,1... | collective-permute-start | bytes 786440 | tf_op jit(solution)/shard_map/ppermute | solution.py:32
  310.0 14.9 %collective-permute-start.33 = (bf16[64,2048]{1,0:T(8,128)(2,1)S(1)}, bf16[64,2048]{1,0:T(8,128)(2,1)S(1)}, u32[]{:S(2)}, u32[]{:S(2)}) collective-permute-start(bf16[64,2048]{1,0:T(8,128)(2,1)S(1)} %get-tuple-element.146), channel_id=1, source_target_pairs={{0,2},{1,3},{2,0},{3,1},{4,6},{5,7},{6,4},{7,5},{8,10},{9,11},{10,... | collective-permute-start | bytes 786440 | tf_op jit(solution)/shard_map/ppermute | solution.py:32
  311.9 13.6 %collective-permute-start.34 = (bf16[64,2048]{1,0:T(8,128)(2,1)S(1)}, bf16[64,2048]{1,0:T(8,128)(2,1)S(1)}, u32[]{:S(2)}, u32[]{:S(2)}) collective-permute-start(bf16[64,2048]{1,0:T(8,128)(2,1)S(1)} %get-tuple-element.145), channel_id=1, source_target_pairs={{0,3},{1,0},{2,1},{3,2},{4,7},{5,4},{6,5},{7,6},{8,11},{9,8},{10,9... | collective-permute-start | bytes 786440 | tf_op jit(solution)/shard_map/ppermute | solution.py:32
  339.0 10.6 %collective-permute-start.39 = (bf16[320,256]{1,0:T(8,128)(2,1)S(1)}, bf16[320,256]{1,0:T(8,128)(2,1)S(1)}, u32[]{:S(2)}, u32[]{:S(2)}) collective-permute-start(bf16[320,256]{1,0:T(8,128)(2,1)S(1)} %get-tuple-element.168), channel_id=1, source_target_pairs={{0,2},{1,3},{2,0},{3,1},{4,6},{5,7},{6,4},{7,5},{8,10},{9,11},{10,... | collective-permute-start | bytes 491528 | tf_op jit(solution)/shard_map/ppermute | solution.py:32
  351.2 9.7 %collective-permute-start.42 = (bf16[64,256]{1,0:T(8,128)(2,1)S(1)}, bf16[64,256]{1,0:T(8,128)(2,1)S(1)}, u32[]{:S(2)}, u32[]{:S(2)}) collective-permute-start(bf16[64,256]{1,0:T(8,128)(2,1)S(1)} %get-tuple-element.269), channel_id=1, source_target_pairs={{8,0},{12,4},{16,8},{20,12},{24,16},{28,20},{32,24},{36,28},{40,32... | collective-permute-start | bytes 98312 | tf_op jit(solution)/shard_map/ppermute | solution.py:38
  352.5 8.6 %collective-permute-start.43 = (bf16[64,256]{1,0:T(8,128)(2,1)S(1)}, bf16[64,256]{1,0:T(8,128)(2,1)S(1)}, u32[]{:S(2)}, u32[]{:S(2)}) collective-permute-start(bf16[64,256]{1,0:T(8,128)(2,1)S(1)} %get-tuple-element.268), channel_id=1, source_target_pairs={{12,0},{16,4},{20,8},{24,12},{28,16},{32,20},{36,24},{40,28},{44,3... | collective-permute-start | bytes 98312 | tf_op jit(solution)/shard_map/ppermute | solution.py:38
  357.2 13.4 %collective-permute-start.35 = (bf16[64,2048]{1,0:T(8,128)(2,1)}, bf16[64,2048]{1,0:T(8,128)(2,1)}, u32[]{:S(2)}, u32[]{:S(2)}) collective-permute-start(bf16[64,2048]{1,0:T(8,128)(2,1)} %get-tuple-element.141), channel_id=1, source_target_pairs={{0,1},{1,2},{2,3},{3,0},{4,5},{5,6},{6,7},{7,4},{8,9},{9,10},{10,1... | collective-permute-start | bytes 786440 | tf_op jit(solution)/shard_map/ppermute | solution.py:32
  357.8 16.0 %collective-permute-start.36 = (bf16[64,2048]{1,0:T(8,128)(2,1)}, bf16[64,2048]{1,0:T(8,128)(2,1)}, u32[]{:S(2)}, u32[]{:S(2)}) collective-permute-start(bf16[64,2048]{1,0:T(8,128)(2,1)} %get-tuple-element.143), channel_id=1, source_target_pairs={{0,2},{1,3},{2,0},{3,1},{4,6},{5,7},{6,4},{7,5},{8,10},{9,11},{10,... | collective-permute-start | bytes 786440 | tf_op jit(solution)/shard_map/ppermute | solution.py:32
  360.9 13.6 %collective-permute-start.37 = (bf16[64,2048]{1,0:T(8,128)(2,1)}, bf16[64,2048]{1,0:T(8,128)(2,1)}, u32[]{:S(2)}, u32[]{:S(2)}) collective-permute-start(bf16[64,2048]{1,0:T(8,128)(2,1)} %get-tuple-element.142), channel_id=1, source_target_pairs={{0,3},{1,0},{2,1},{3,2},{4,7},{5,4},{6,5},{7,6},{8,11},{9,8},{10,9... | collective-permute-start | bytes 786440 | tf_op jit(solution)/shard_map/ppermute | solution.py:32
  365.8 14.3 %collective-permute-start.45 = (bf16[64,2048]{1,0:T(8,128)(2,1)}, bf16[64,2048]{1,0:T(8,128)(2,1)}, u32[]{:S(2)}, u32[]{:S(2)}) collective-permute-start(bf16[64,2048]{1,0:T(8,128)(2,1)} %get-tuple-element.118), channel_id=1, source_target_pairs={{0,3},{1,0},{2,1},{3,2},{4,7},{5,4},{6,5},{7,6},{8,11},{9,8},{10,9... | collective-permute-start | bytes 786440 | tf_op jit(solution)/shard_map/ppermute | solution.py:32
  368.4 11.7 %collective-permute-start.46 = (bf16[64,2048]{1,0:T(8,128)(2,1)}, bf16[64,2048]{1,0:T(8,128)(2,1)}, u32[]{:S(2)}, u32[]{:S(2)}) collective-permute-start(bf16[64,2048]{1,0:T(8,128)(2,1)} %get-tuple-element.118), channel_id=1, source_target_pairs={{0,2},{1,3},{2,0},{3,1},{4,6},{5,7},{6,4},{7,5},{8,10},{9,11},{10,... | collective-permute-start | bytes 786440 | tf_op jit(solution)/shard_map/ppermute | solution.py:32
  370.6 14.5 %collective-permute-start.47 = (bf16[64,2048]{1,0:T(8,128)(2,1)}, bf16[64,2048]{1,0:T(8,128)(2,1)S(1)}, u32[]{:S(2)}, u32[]{:S(2)}) collective-permute-start(bf16[64,2048]{1,0:T(8,128)(2,1)} %get-tuple-element.118), channel_id=1, source_target_pairs={{0,1},{1,2},{2,3},{3,0},{4,5},{5,6},{6,7},{7,4},{8,9},{9,10},{10,1... | collective-permute-start | bytes 786440 | tf_op jit(solution)/shard_map/ppermute | solution.py:32
  396.4 9.7 %collective-permute-start.48 = (bf16[64,2048]{1,0:T(8,128)(2,1)S(1)}, bf16[64,2048]{1,0:T(8,128)(2,1)S(1)}, u32[]{:S(2)}, u32[]{:S(2)}) collective-permute-start(bf16[64,2048]{1,0:T(8,128)(2,1)S(1)} %get-tuple-element.138), channel_id=1, source_target_pairs={{0,1},{1,2},{2,3},{3,0},{4,5},{5,6},{6,7},{7,4},{8,9},{9,10},{10,1... | collective-permute-start | bytes 786440 | tf_op jit(solution)/shard_map/ppermute | solution.py:32
  397.6 15.3 %collective-permute-start.49 = (bf16[64,2048]{1,0:T(8,128)(2,1)S(1)}, bf16[64,2048]{1,0:T(8,128)(2,1)S(1)}, u32[]{:S(2)}, u32[]{:S(2)}) collective-permute-start(bf16[64,2048]{1,0:T(8,128)(2,1)S(1)} %get-tuple-element.140), channel_id=1, source_target_pairs={{0,2},{1,3},{2,0},{3,1},{4,6},{5,7},{6,4},{7,5},{8,10},{9,11},{10,... | collective-permute-start | bytes 786440 | tf_op jit(solution)/shard_map/ppermute | solution.py:32
  401.2 11.8 %collective-permute-start.50 = (bf16[64,2048]{1,0:T(8,128)(2,1)S(1)}, bf16[64,2048]{1,0:T(8,128)(2,1)S(1)}, u32[]{:S(2)}, u32[]{:S(2)}) collective-permute-start(bf16[64,2048]{1,0:T(8,128)(2,1)S(1)} %get-tuple-element.139), channel_id=1, source_target_pairs={{0,3},{1,0},{2,1},{3,2},{4,7},{5,4},{6,5},{7,6},{8,11},{9,8},{10,9... | collective-permute-start | bytes 786440 | tf_op jit(solution)/shard_map/ppermute | solution.py:32
  425.4 11.2 %collective-permute-start.53 = (bf16[320,256]{1,0:T(8,128)(2,1)S(1)}, bf16[320,256]{1,0:T(8,128)(2,1)S(1)}, u32[]{:S(2)}, u32[]{:S(2)}) collective-permute-start(bf16[320,256]{1,0:T(8,128)(2,1)S(1)} %get-tuple-element.165), channel_id=1, source_target_pairs={{0,2},{1,3},{2,0},{3,1},{4,6},{5,7},{6,4},{7,5},{8,10},{9,11},{10,... | collective-permute-start | bytes 491528 | tf_op jit(solution)/shard_map/ppermute | solution.py:32
  429.2 59.5 %collective-permute-start.51 = (bf16[64,2048]{1,0:T(8,128)(2,1)S(1)}, bf16[64,2048]{1,0:T(8,128)(2,1)S(1)}, u32[]{:S(2)}, u32[]{:S(2)}) collective-permute-start(bf16[64,2048]{1,0:T(8,128)(2,1)S(1)} %get-tuple-element.185), channel_id=1, source_target_pairs={{0,64},{64,0},{1,65},{65,1},{2,66},{66,2},{3,67},{67,3},{4,68},{68... | collective-permute-start | bytes 786440 | tf_op jit(solution)/shard_map/ppermute | solution.py:518
  440.5 10.2 %collective-permute-start.58 = (bf16[64,256]{1,0:T(8,128)(2,1)S(1)}, bf16[64,256]{1,0:T(8,128)(2,1)S(1)}, u32[]{:S(2)}, u32[]{:S(2)}) collective-permute-start(bf16[64,256]{1,0:T(8,128)(2,1)S(1)} %get-tuple-element.263), channel_id=1, source_target_pairs={{16,0},{20,4},{24,8},{28,12},{32,16},{36,20},{40,24},{44,28},{48,3... | collective-permute-start | bytes 98312 | tf_op jit(solution)/shard_map/ppermute | solution.py:38
  453.9 9.6 %collective-permute-start.60 = (bf16[2,29,16,128]{3,2,1,0:T(8,128)(2,1)S(1)}, bf16[2,29,16,128]{3,2,1,0:T(8,128)(2,1)S(1)}, u32[]{:S(2)}, u32[]{:S(2)}) collective-permute-start(bf16[2,29,16,128]{3,2,1,0:T(8,128)(2,1)S(1)} %get-tuple-element.150), channel_id=1, source_target_pairs={{0,1},{1,2},{2,3},{3,0},{4,5},{5,6},{6,7},{7,4},{8,9},{9,10},{10,1... | collective-permute-start | bytes 712712 | tf_op jit(solution)/shard_map/ppermute | solution.py:32
  454.0 14.3 %collective-permute-start.61 = (bf16[2,29,16,128]{3,2,1,0:T(8,128)(2,1)S(1)}, bf16[2,29,16,128]{3,2,1,0:T(8,128)(2,1)S(1)}, u32[]{:S(2)}, u32[]{:S(2)}) collective-permute-start(bf16[2,29,16,128]{3,2,1,0:T(8,128)(2,1)S(1)} %get-tuple-element.152), channel_id=1, source_target_pairs={{0,2},{1,3},{2,0},{3,1},{4,6},{5,7},{6,4},{7,5},{8,10},{9,11},{10,... | collective-permute-start | bytes 712712 | tf_op jit(solution)/shard_map/ppermute | solution.py:32
  457.6 10.9 %collective-permute-start.62 = (bf16[2,29,16,128]{3,2,1,0:T(8,128)(2,1)S(1)}, bf16[2,29,16,128]{3,2,1,0:T(8,128)(2,1)S(1)}, u32[]{:S(2)}, u32[]{:S(2)}) collective-permute-start(bf16[2,29,16,128]{3,2,1,0:T(8,128)(2,1)S(1)} %get-tuple-element.151), channel_id=1, source_target_pairs={{0,3},{1,0},{2,1},{3,2},{4,7},{5,4},{6,5},{7,6},{8,11},{9,8},{10,9... | collective-permute-start | bytes 712712 | tf_op jit(solution)/shard_map/ppermute | solution.py:32
  483.4 21.6 %collective-permute-start.59 = (bf16[64,2048]{1,0:T(8,128)(2,1)S(1)}, bf16[64,2048]{1,0:T(8,128)(2,1)S(1)}, u32[]{:S(2)}, u32[]{:S(2)}) collective-permute-start(bf16[64,2048]{1,0:T(8,128)(2,1)S(1)} %select_convert_fusion), channel_id=1, source_target_pairs={{0,64},{64,0},{1,65},{65,1},{2,66},{66,2},{3,67},{67,3},{4,68},{68... | collective-permute-start | bytes 786440 | tf_op jit(solution)/shard_map/ppermute | solution.py:518
  507.1 11.9 %collective-permute-start.77 = (bf16[2,21,16,128]{3,2,1,0:T(8,128)(2,1)S(1)}, bf16[2,21,16,128]{3,2,1,0:T(8,128)(2,1)S(1)}, u32[]{:S(2)}, u32[]{:S(2)}) collective-permute-start(bf16[2,21,16,128]{3,2,1,0:T(8,128)(2,1)S(1)} %get-tuple-element.178), channel_id=1, source_target_pairs={{0,2},{1,3},{2,0},{3,1},{4,6},{5,7},{6,4},{7,5},{8,10},{9,11},{10,... | collective-permute-start | bytes 516104 | tf_op jit(solution)/shard_map/ppermute | solution.py:32
  (162 other events, 2826.6 us)
Sparse Core Ops, SparseCore 0:
  11.6 122.3 all-gather.3
  136.9 71.9 all-gather.5
  211.7 72.0 all-gather.7

commit v15 on v14

--- a/solution.py
+++ b/solution.py
@@ -199,14 +199,12 @@
 
 
 def attend_back_kernel(
-    layer, head, branch_ref, table_ref, so_ref, eo_ref, prob_ref, query_ref, keyval_ref, eq_ref, sq_ref,
-    dq_ref, dkv_ref, inner_o_ref, inner_q_ref, part_ref,
-    out_buf, out_sem, query_buf, query_sem, mixed_buf, key_sum, value_sum,
+    layer, head, branch_ref, table_ref, so_ref, eo_ref, prob_ref, query_ref, keyval_ref,
+    dq_ref, dkv_ref, inner_o_ref, out_buf, out_sem, mixed_buf, key_sum, value_sum,
 ):
     ranks, chunks, rows, width = out_buf.shape
     out_copies = table_copies(table_ref, out_buf, out_sem, layer, width)
-    query_copies = table_copies(table_ref, query_buf, query_sem, layer, 0)
-    for copy in out_copies + query_copies:
+    for copy in out_copies:
         copy.start()
     scale = 1.0 / math.sqrt(head)
     branch = branch_ref[...]
@@ -237,20 +235,47 @@
             value_sum[...] += values
     dkv_ref[:, :head] = (key_sum[...] * scale).astype(bf16)
     dkv_ref[:, head:] = value_sum[...].astype(bf16)
-    grad_q = dq_ref[...]
-    inner_q = against(grad_q, eq_ref[...]).astype(bf16)
-    inner_q_ref[...] = inner_q
-    for copy in query_copies:
+
+
+def query_back_kernel(layer, grad_ref, table_ref, eq_ref, sq_ref, inner_ref, part_ref, buf, sem):
+    ranks, chunks, rows, width = buf.shape
+    copies = table_copies(table_ref, buf, sem, layer, 0)
+    for copy in copies:
+        copy.start()
+    grad = grad_ref[...]
+    inner = against(grad, eq_ref[...]).astype(bf16)
+    inner_ref[...] = inner
+    for copy in copies:
         copy.wait()
     for y in range(chunks):
         columns = pl.ds(y * rows, rows)
-        total = plain(inner_q, sq_ref[:, columns])
+        total = plain(inner, sq_ref[:, columns])
         for x in range(ranks):
-            total = total + against(grad_q[:, x * width : (x + 1) * width], query_buf[x, y])
+            total = total + against(grad[:, x * width : (x + 1) * width], buf[x, y])
         part_ref[:, columns] = total
 
 
-def attend_back(layer, branch, table, so, eo, probs, queries, key_block, eq, sq, head):
+def query_back(layer, grad, table, eq, sq):
+    rows, model = grad.shape
+    rank = sq.shape[0]
+    return pl.pallas_call(
+        lambda *refs: query_back_kernel(layer, *refs),
+        in_specs=[held, remote, held, held],
+        out_specs=[held] * 2,
+        out_shape=[
+            jax.ShapeDtypeStruct((rows, rank), bf16),
+            jax.ShapeDtypeStruct((rows, model), f32),
+        ],
+        scratch_shapes=table_scratch(table, model // table.shape[0]),
+        compiler_params=pltpu.CompilerParams(vmem_limit_bytes=28 * 2**20),
+        cost_estimate=pl.CostEstimate(
+            flops=8 * rows * model * model, bytes_accessed=2 * model * model, transcendentals=0
+        ),
+        name="query_back",
+    )(grad, table, eq, sq)
+
+
+def attend_back(layer, branch, table, so, eo, probs, queries, key_block, head):
     rows, model = queries.shape
     keys = key_block.shape[0]
     groups = probs.shape[0]
@@ -258,17 +283,14 @@
     width = model // table.shape[0]
     return pl.pallas_call(
         lambda *refs: attend_back_kernel(layer, head, *refs),
-        in_specs=[held, remote] + [held] * 7,
-        out_specs=[held] * 5,
+        in_specs=[held, remote] + [held] * 5,
+        out_specs=[held] * 3,
         out_shape=[
             jax.ShapeDtypeStruct((rows, model), bf16),
             jax.ShapeDtypeStruct((keys, 2 * head), bf16),
             jax.ShapeDtypeStruct((rows, rank), bf16),
-            jax.ShapeDtypeStruct((rows, rank), bf16),
-            jax.ShapeDtypeStruct((rows, model), f32),
         ],
         scratch_shapes=table_scratch(table, width)
-        + table_scratch(table, width)
         + [
             pltpu.VMEM((rows, model), bf16),
             pltpu.VMEM((keys, head), f32),
@@ -276,12 +298,12 @@
         ],
         compiler_params=pltpu.CompilerParams(vmem_limit_bytes=44 * 2**20),
         cost_estimate=pl.CostEstimate(
-            flops=8 * rows * model * (keys + 2 * model),
-            bytes_accessed=4 * model * model + 4 * groups * 4 * rows * keys,
+            flops=8 * rows * model * (keys + model),
+            bytes_accessed=2 * model * model + 4 * groups * 4 * rows * keys,
             transcendentals=0,
         ),
         name="attend_back",
-    )(branch, table, so, eo, probs, queries, key_block, eq, sq)
+    )(branch, table, so, eo, probs, queries, key_block)
 
 
 def feed_copies(table_ref, buf, sems):
@@ -705,9 +727,12 @@
         low_kv = against(normed, skv).astype(bf16)
         keyval = (plain(normed, keyval_ws[layer]) + kv_bias + plain(low_kv, ekv)).astype(bf16)
         pieces = [along(keyval, "dp", back) for back in range(reach, 0, -1)] + [keyval]
-        key_block = spread(jnp.concatenate(pieces, axis=0))
+        own_keys = jnp.concatenate(pieces, axis=0)
+        blocks = [own_keys] + [around(own_keys, "tensor", -j) for j in range(1, ranks)]
+        query_rows, blocks[1] = lax.optimization_barrier((normed, blocks[1]))
+        key_block = jnp.concatenate(blocks, axis=0)
         queries, low_q = project_queries(
-            layer, normed, early_all, query_bias_all[layer][:1].astype(f32), eq_all[layer], sq
+            layer, query_rows, early_all, query_bias_all[layer][:1].astype(f32), eq_all[layer], sq
         )
         probs, mixed, low_o, attended = attend(
             layer, queries, key_block, bias, early_all, so_all[layer], eo, head
@@ -752,7 +777,7 @@
     def at(block, index, axis):
         return lax.dynamic_index_in_dim(block, index, axis, keepdims=False)
 
-    def scattered_grads(layers):
+    def scattered_grads(layers, late):
         pile = jnp.stack([piled(shared, quartered) for shared, quartered, _ in layers], axis=1)
         mine = at(pile, tensor, 0).astype(f32)
         for j in range(1, ranks):
@@ -762,11 +787,11 @@
         mine = at(pile, near, 2).astype(f32)
         for k in range(1, 4):
             mine = mine + flipped(at(pile, near ^ k, 2), "dp", k).astype(f32)
-        pile = mine.astype(bf16)
+        pile, late = lax.optimization_barrier((mine.astype(bf16), late))
         mine = at(pile, turn, 1).astype(f32)
         for k in range(1, chips):
             mine = mine + flipped(at(pile, turn ^ k, 1), "dp", 4 * k).astype(f32)
-        return mine.astype(bf16)
+        return mine.astype(bf16), late
 
     def spread_grads(zero, one, shared, quartered, owned):
         own = jnp.where(low_section, zero, one)
@@ -818,10 +843,10 @@
         sq, skv, ekv, eo = adapters[layer]
         unit1, rsd1, normed, low_q, low_kv, queries, key_block, probs, mixed, low_o = kept
         branch = grad_middle.astype(bf16)
-        grad_q, grad_block, inner_o, inner_q, partial = attend_back(
-            layer, branch, early_all, so_all[layer], eo, probs, queries, key_block,
-            eq_all[layer], sq, head,
+        grad_q, grad_block, inner_o = attend_back(
+            layer, branch, early_all, so_all[layer], eo, probs, queries, key_block, head
         )
+        inner_q, partial = query_back(layer, grad_q, early_all, eq_all[layer], sq)
         count = (reach + 1) * rows
         blocks = grad_block[:count].astype(f32)
         for j in range(1, ranks):
@@ -879,8 +904,7 @@
     )
     grad_one, more, quartered = backward_attend(1, kept_one, grad_middle)
     layer_one = (shared + more, quartered, owned)
-    partial, _ = lax.optimization_barrier((partial, grad_middle))
-    final = feed_result(1, middle_one, partial).astype(bf16)
+    partial_one = partial
 
     branch_zero = spread(grad_one.astype(bf16))
     grad_up, inner_d, inner_u, partial_back = feed_call(
@@ -905,7 +929,8 @@
     )
     grad_zero, more, quartered = backward_attend(0, kept_zero, grad_middle_zero)
     layer_zero = (shared + more, quartered, owned)
-    mine = scattered_grads([layer_zero, layer_one])
+    mine, partial_one = scattered_grads([layer_zero, layer_one], partial_one)
+    final = feed_result(1, middle_one, partial_one).astype(bf16)
     grads = spread_grads(mine[0], mine[1], *layer_zero)
 
     def both_micros(zero, one, kind):
@@ -913,7 +938,6 @@
         received = swap(jnp.where(low_section, one, zero).astype(bf16)).astype(kind)
         return jnp.where(low_section, jnp.stack([own, received]), jnp.stack([received, own]))
 
-    passed, final, _ = lax.optimization_barrier((passed, final, grad_middle_zero))
     section_outputs = both_micros(passed, final, bf16)
     input_grads = both_micros(grad_zero, grad_one, f32)
     onehot = (bank_choice[:, None] == jnp.arange(banks)[None, :]).astype(f32)

time: 540 us -> 537 us (level)
  starting transfers between devices: 124 us -> 116 us
  waiting for transfers between devices: 229 us -> 222 us
  local copies, waits for them, and re-layouts: 29.3 us -> 36.2 us
    ppermute x45, waiting for transfers between devices: 125 us -> 111 us  [around(): lax.ppermute(block, axis, [(i, (i + distance) % size) for i in range(size)])]
    pallas_call x0 -> x2, Pallas kernels: none -> 12.7 us  [query_back(): pl.pallas_call(lambda *refs: query_back_kernel(layer, *refs), in_specs=[h...]
    concatenate x3, local copies, waits for them, and re-layouts: 1.03 us -> 8.92 us  [padded(): jnp.concatenate([pile, jnp.zeros((lack,) + pile.shape[1:], pile.dtype)],...]
    pallas_call x2, Pallas kernels: 22.9 us -> 16.1 us  [attend_back(): pl.pallas_call(lambda *refs: attend_back_kernel(layer, head, *refs), in_s...]
    unnamed x296 -> x312, local copies, waits for them, and re-layouts: 13.6 us -> 12.1 us
  transfers between devices with their start and end apart: 82 -> 82, of which waited for: 55 -> 53; matrix products, arithmetic and copies ran while one was open for 10% -> 10% of each run, Pallas kernels for 7% -> 10%
where the time goes in v15:
time: 537 us; the launch traced here: 529 us
  waiting for transfers between devices  222 us (41%)
  starting transfers between devices  116 us (22%)
  Pallas kernels  91.7 us (17%)
  local copies, waits for them, and re-layouts  36.2 us (7%)
  other arithmetic  28.8 us (5%)
  between operations  21.1 us (4%)
  matrix products  13.3 us (2%)
    ppermute x45, waiting for transfers between devices, around(): lax.ppermute(block, axis, [(i, (i + distance) % size) for i in range(size)])  111 us
    ppermute x45, starting transfers between devices, around(): lax.ppermute(block, axis, [(i, (i + distance) % size) for i in range(size)])  59.3 us
    all_gather x1, waiting for transfers between devices, gather_all(): lax.all_gather(row_major(shard), every, axis=0, tiled=True, axis_index_gr...  56.3 us
    pallas_call x3, Pallas kernels, feed_call(): pl.pallas_call(kernel, in_specs=[remote if value.ndim == 4 or i in copied...  35.4 us
    ppermute x16, starting transfers between devices, along(): return lax.ppermute(block, axis, route)  29.5 us
    ppermute x5, waiting for transfers between devices, swap(): return lax.ppermute(value, 'section', sides)  25.3 us
    pallas_call x2, Pallas kernels, attend(): pl.pallas_call(lambda *refs: attend_kernel(layer, head, *refs), in_specs=...  18.4 us
    pallas_call x2, Pallas kernels, attend_back(): pl.pallas_call(lambda *refs: attend_back_kernel(layer, head, *refs), in_s...  16.1 us
  transfers between devices with their start and end apart: 82, of which 53 were waited for; matrix products, arithmetic and copies ran while one was open for 10% of the time, Pallas kernels for 10%

profile of v15, /device:TPU:0, one launch (start us, length us, event | category | flops | bytes accessed | tf_op | source)
XLA Modules:
  0.0 529.1 jit_solution(5588352335712103762)
XLA Ops:
  12.3 4.0 collective-permute-start.18
  16.4 12.2 %collective-permute-done.18 = bf16[128,2048]{1,0:T(8,128)(2,1)S(1)} collective-permute-done((bf16[128,2048]{1,0:T(8,128)(2,1)S(1)}, bf16[128,2048]{1,0:T(8,128)(2,1)S(1)}, u32[]{:S(2)}, u32[]{:S(2)}) %collective-permute-start.18) | collective-permute-done | bytes 524320 | tf_op jit(solution)/shard_map/ppermute | solution.py:540
  44.6 4.1 collective-permute-start.1
  51.1 11.5 %collective-permute-done = bf16[1,14592]{1,0:T(2,128)(2,1)S(1)} collective-permute-done((bf16[1,14592]{1,0:T(2,128)(2,1)S(1)}, bf16[1,14592]{1,0:T(2,128)(2,1)S(1)}, u32[]{:S(2)}, u32[]{:S(2)}) %collective-permute-start) | collective-permute-done | bytes 29216 | tf_op jit(solution)/shard_map/ppermute | solution.py:540
  64.9 2.8 collective-permute-start.3
  72.2 4.3 collective-permute-done.3
  78.1 56.3 %all-gather.4.cloned.1.call-done = bf16[16384,1152]{1,0:T(8,128)(2,1)} async-done(((bf16[128,1152]{1,0:T(8,128)(2,1)}), bf16[16384,1152]{1,0:T(8,128)(2,1)}) %all-gather.4.cloned.1.call-update) | async-done | bytes 37748752 | tf_op jit(solution)/shard_map/all_gather | solution.py:578
  137.7 3.4 collective-permute-start.5
  143.4 4.1 collective-permute-start.7
  156.8 3.9 collective-permute-done.10
  160.7 3.7 collective-permute-done.11
  164.5 4.5 project_queries.2
  169.1 9.2 %attend.2 = (bf16[4,256,1280]{2,1,0:T(8,128)(2,1)S(1)}, bf16[64,2048]{1,0:T(8,128)(2,1)S(1)}, bf16[64,16]{1,0:T(8,128)(2,1)S(1)}, f32[64,2048]{1,0:T(8,128)S(1)}) custom-call(bf16[64,2048]{1,0:T(8,128)(2,1)S(1)} %get-tuple-element.62.refs_0_.refs_5_, bf16[1280,256]{1,0:T(8,128)(2,1)S(1)} %constant_dynamic-update-slice_fusion.26.refs_1_.refs_6_, ...), custom_call_target="tpu_custom_call" | custom-call | flops 2818572288 | bytes 8388608 | tf_op jit(solution)/shard_map/attend/pallas_call | solution.py:180
  183.7 4.6 collective-permute-done.12
  188.3 2.8 collective-permute-done.13
  191.1 4.5 collective-permute-done.14
  198.2 6.7 %collective-permute-done.15 = bf16[64,2048]{1,0:T(8,128)(2,1)S(1)} collective-permute-done((bf16[64,2048]{1,0:T(8,128)(2,1)S(1)}, bf16[64,2048]{1,0:T(8,128)(2,1)S(1)}, u32[]{:S(2)}, u32[]{:S(2)}) %collective-permute-start.15) | collective-permute-done | bytes 262176 | tf_op jit(solution)/shard_map/ppermute | solution.py:32
  207.1 4.2 collective-permute-done.17
  212.4 10.8 %feed.1 = (bf16[256,2048]{1,0:T(8,128)(2,1)S(1)}, bf16[256,2048]{1,0:T(8,128)(2,1)S(1)}, bf16[256,16]{1,0:T(8,128)(2,1)S(1)}, bf16[256,16]{1,0:T(8,128)(2,1)S(1)}, bf16[256,2048]{1,0:T(8,128)(2,1)S(1)}) custom-call(bf16[256,2048]{1,0:T(8,128)(2,1)S(1)} %pad_maximum_fusion.1.second_ref, bf16[4,2,512,2048]{3,2,1,0:T(8,128)(2,1)} %bitcast.700, ...), custom_call_target="tpu_custom_call" | custom-call | flops 4294967296 | bytes 16777216 | tf_op jit(solution)/shard_map/feed/pallas_call | solution.py:470
  227.6 10.9 %collective-permute-done.19 = bf16[64,2048]{1,0:T(8,128)(2,1)S(1)} collective-permute-done((bf16[64,2048]{1,0:T(8,128)(2,1)S(1)}, bf16[64,2048]{1,0:T(8,128)(2,1)S(1)}, u32[]{:S(2)}, u32[]{:S(2)}) %collective-permute-start.19) | collective-permute-done | bytes 262176 | tf_op jit(solution)/shard_map/ppermute | solution.py:32
  246.1 3.3 collective-permute-start.24
  251.8 2.9 collective-permute-start.26
  256.5 3.2 collective-permute-done.26
  259.7 3.0 collective-permute-done.27
  262.7 4.0 collective-permute-done.28
  266.7 4.6 project_queries.3
  271.4 9.2 %attend.3 = (bf16[4,256,1280]{2,1,0:T(8,128)(2,1)S(1)}, bf16[64,2048]{1,0:T(8,128)(2,1)S(1)}, bf16[64,16]{1,0:T(8,128)(2,1)S(1)}, f32[64,2048]{1,0:T(8,128)S(1)}) custom-call(bf16[64,2048]{1,0:T(8,128)(2,1)S(1)} %get-tuple-element.70.refs_0_.refs_5_, bf16[1280,256]{1,0:T(8,128)(2,1)S(1)} %constant_dynamic-update-slice_fusion.39.refs_1_.refs_6_, ...), custom_call_target="tpu_custom_call" | custom-call | flops 2818572288 | bytes 8388608 | tf_op jit(solution)/shard_map/attend/pallas_call | solution.py:180
  284.6 5.8 %collective-permute-done.29 = bf16[64,2048]{1,0:T(8,128)(2,1)S(1)} collective-permute-done((bf16[64,2048]{1,0:T(8,128)(2,1)S(1)}, bf16[64,2048]{1,0:T(8,128)(2,1)S(1)}, u32[]{:S(2)}, u32[]{:S(2)}) %collective-permute-start.29) | collective-permute-done | bytes 262176 | tf_op jit(solution)/shard_map/ppermute | solution.py:32
  292.3 5.4 %collective-permute-done.31 = bf16[64,2048]{1,0:T(8,128)(2,1)S(1)} collective-permute-done((bf16[64,2048]{1,0:T(8,128)(2,1)S(1)}, bf16[64,2048]{1,0:T(8,128)(2,1)S(1)}, u32[]{:S(2)}, u32[]{:S(2)}) %collective-permute-start.31) | collective-permute-done | bytes 262176 | tf_op jit(solution)/shard_map/ppermute | solution.py:32
  299.5 14.5 %feed_both.1 = (bf16[256,2048]{1,0:T(8,128)(2,1)S(1)}, bf16[256,16]{1,0:T(8,128)(2,1)S(1)}, bf16[256,16]{1,0:T(8,128)(2,1)S(1)}, bf16[256,2048]{1,0:T(8,128)(2,1...) custom-call(bf16[256,2048]{1,0:T(8,128)(2,1)S(1)} %pad_maximum_fusio, ...), custom_call_target="tpu_custom_call" | custom-call | flops 8589934592 | bytes 16777216 | tf_op jit(solution)/shard_map/feed_both/pallas_call | solution.py:470
  321.4 9.8 %collective-permute-done.32 = bf16[64,2048]{1,0:T(8,128)(2,1)S(1)} collective-permute-done((bf16[64,2048]{1,0:T(8,128)(2,1)S(1)}, bf16[64,2048]{1,0:T(8,128)(2,1)S(1)}, u32[]{:S(2)}, u32[]{:S(2)}) %collective-permute-start.32) | collective-permute-done | bytes 262176 | tf_op jit(solution)/shard_map/ppermute | solution.py:32
  332.6 8.1 %attend_back.2 = (bf16[64,2048]{1,0:T(8,128)(2,1)S(1)}, bf16[1280,256]{1,0:T(8,128)(2,1)S(1)}, bf16[64,16]{1,0:T(8,128)(2,1)S(1)}) custom-call(bf16[64,2048]{1,0:T(8,128)(2,1)S(1)} %get-tuple-element.131.refs_0_, bf16[4,4,2,512,1152]{4,3,2,1,0:T(8,128)(2,1)} %bitcast.696, bf16[16,2048]{1,0:T(8,128)(2,1)S(1)} %copy-done.23, bf16[16,2048]{1,0:T(8,128)(2,1)S(1)} %copy-done.33, ...), custom_call_target="tpu_custom_call" | custom-call | flops 3489660928 | bytes 13631488 | tf_op jit(solution)/shard_map/attend_back/pallas_call | solution.py:284
  341.0 3.8 collective-permute-start.36
  344.8 6.3 %query_back.2 = (bf16[64,16]{1,0:T(8,128)(2,1)S(1)}, f32[64,2048]{1,0:T(8,128)S(1)}) custom-call(bf16[64,2048]{1,0:T(8,128)(2,1)S(1)} %get-tuple-element.76.refs_0_, bf16[4,4,2,512,1152]{4,3,2,1,0:T(8,128)(2,1)} %bitcast.697, bf16[16,2048]{1,0:T(8,128)(2,1)S(1)} %copy-done.25, bf16[16,2048]{1,0:T(8,128)(2,1)S(1)} %copy-done.31), custom_call_target="tpu_custom_call" | custom-call | flops 2147483648 | bytes 8388608 | tf_op jit(solution)/shard_map/query_back/pallas_call | solution.py:261
  361.8 3.6 collective-permute-done.41
  376.0 7.9 %concatenate.239 = bf16[84,16,128]{2,0,1:T(8,128)(2,1)} concatenate(bf16[16,16,128]{2,0,1:T(8,128)(2,1)} %bitcast.746, bf16[16,16,128]{2,0,1:T(8,128)(2,1)} %bitcast.745, bf16[16,16,128]{2,0,1:T(8,128)(2,1)} %bitcast.748, bf16[16,16,128]{2,0,1:T(8,128)(2,1)} %bitcast.747, bf16[16,16,128]{2,0,1:T(8,128)(2,1)S(1)} %bitcast.749, bf16[2,16,128]{2,0,1:T(2,128)(2,1)} %bitcast.791, ...), dimensions={0} | concatenate | bytes 688128 | tf_op jit(solution)/shard_map/concatenate | solution.py:764
  387.3 10.0 %feed_back.1 = (bf16[256,2048]{1,0:T(8,128)(2,1)S(1)}, bf16[256,16]{1,0:T(8,128)(2,1)S(1)}, bf16[256,16]{1,0:T(8,128)(2,1)S(1)}, bf16[256,2048]{1,0:T(8,128)(2,1)S(1)}) custom-call(bf16[256,2048]{1,0:T(8,128)(2,1)S(1)} %pad_maximum_fusion.5.branch_ref, bf16[4,2,512,2048]{3,2,1,0:T(8,128)(2,1)} %bitcast.701, bf16[256,2048]{1,0:T(8,128)(2,1)S(1)} %copy-done.17, ...), custom_call_target="tpu_custom_call" | custom-call | flops 4294967296 | bytes 16777216 | tf_op jit(solution)/shard_map/feed_back/pallas_call | solution.py:470
  403.1 9.5 %collective-permute-done.45 = bf16[64,2048]{1,0:T(8,128)(2,1)S(1)} collective-permute-done((bf16[64,2048]{1,0:T(8,128)(2,1)S(1)}, bf16[64,2048]{1,0:T(8,128)(2,1)S(1)}, u32[]{:S(2)}, u32[]{:S(2)}) %collective-permute-start.45) | collective-permute-done | bytes 262176 | tf_op jit(solution)/shard_map/ppermute | solution.py:32
  413.9 8.1 %attend_back.3 = (bf16[64,2048]{1,0:T(8,128)(2,1)S(1)}, bf16[1280,256]{1,0:T(8,128)(2,1)S(1)}, bf16[64,16]{1,0:T(8,128)(2,1)S(1)}) custom-call(bf16[64,2048]{1,0:T(8,128)(2,1)S(1)} %get-tuple-element.123.refs_0_, bf16[4,4,2,512,1152]{4,3,2,1,0:T(8,128)(2,1)} %bitcast.698, bf16[16,2048]{1,0:T(8,128)(2,1)S(1)} %get-tuple-element.280.refs_4_.refs_2_, ...), custom_call_target="tpu_custom_call" | custom-call | flops 3489660928 | bytes 13631488 | tf_op jit(solution)/shard_map/attend_back/pallas_call | solution.py:284
  422.9 3.3 collective-permute-start.49
  426.2 6.4 %query_back.3 = (bf16[64,16]{1,0:T(8,128)(2,1)S(1)}, f32[64,2048]{1,0:T(8,128)S(1)}) custom-call(bf16[64,2048]{1,0:T(8,128)(2,1)S(1)} %get-tuple-element.85.refs_0_, bf16[4,4,2,512,1152]{4,3,2,1,0:T(8,128)(2,1)} %bitcast.699, bf16[16,2048]{1,0:T(8,128)(2,1)S(1)} %get-tuple-element.282.refs_3_.refs_2_, bf16[16,2048]{1,0:T(8,128)(2,1)S(1)} %copy-done.27), custom_call_target="tpu_custom_call" | custom-call | flops 2147483648 | bytes 8388608 | tf_op jit(solution)/shard_map/query_back/pallas_call | solution.py:261
  443.6 3.6 collective-permute-done.54
  457.2 2.8 collective-permute-done.55
  459.9 4.2 collective-permute-done.56
  467.0 4.2 collective-permute-done.59
  485.5 2.8 collective-permute-start.62
  503.1 3.0 collective-permute-done.63
  507.9 2.8 collective-permute-start.77
  (666 shorter events, 183.7 us)
Async XLA Ops:
  7.2 127.2 %all-gather.4.cloned.1.call-start = ((), (), s32[]{:S(2)}) async-start(), calls=%async_computation | async-start | bytes 38043648 | tf_op jit(solution)/shard_map/all_gather | solution.py:578
  10.8 201.6 %all-gather.6.cloned.1.call-start = ((), (), s32[]{:S(2)}) async-start(), calls=%async_computation.1 | async-start | bytes 17301504 | tf_op jit(solution)/shard_map/all_gather | solution.py:574
  12.3 16.3 %collective-permute-start.18 = (bf16[128,2048]{1,0:T(8,128)(2,1)S(1)}, bf16[128,2048]{1,0:T(8,128)(2,1)S(1)}, u32[]{:S(2)}, u32[]{:S(2)}) collective-permute-start(bf16[128,2048]{1,0:T(8,128)(2,1)S(1)} %broadcast_select_fusion.2), channel_id=1, source_target_pairs={{0,64},{64,0},{1,65},{65,1},{2,66},{66,2},{3,67},{67,3},{4,68},{68... | collective-permute-start | bytes 1572872 | tf_op jit(solution)/shard_map/ppermute | solution.py:540
  30.0 267.8 %all-gather.8.cloned.1.call-start = ((), (), s32[]{:S(2)}) async-start(), calls=%async_computation.2 | async-start | bytes 17301504 | tf_op jit(solution)/shard_map/all_gather | solution.py:574
  44.6 19.0 %collective-permute-start.1 = (bf16[16,8256]{1,0:T(8,128)(2,1)S(1)}, bf16[16,8256]{1,0:T(8,128)(2,1)S(1)}, u32[]{:S(2)}, u32[]{:S(2)}) collective-permute-start(bf16[16,8256]{1,0:T(8,128)(2,1)S(1)} %concatenate.210), channel_id=1, source_target_pairs={{0,64},{64,0},{1,65},{65,1},{2,66},{66,2},{3,67},{67,3},{4,68},{68... | collective-permute-start | bytes 792584 | tf_op jit(solution)/shard_map/ppermute | solution.py:540
  49.0 13.6 %collective-permute-start = (bf16[1,14592]{1,0:T(2,128)(2,1)S(1)}, bf16[1,14592]{1,0:T(2,128)(2,1)S(1)}, u32[]{:S(2)}, u32[]{:S(2)}) collective-permute-start(bf16[1,14592]{1,0:T(2,128)(2,1)S(1)} %constant_dynamic-update-slice_fusion), channel_id=1, source_target_pairs={{0,64},{64,0},{1,65},{65,1},{2,66},{66,2},{3,67},{67,3},{4,68},{68... | collective-permute-start | bytes 87560 | tf_op jit(solution)/shard_map/ppermute | solution.py:540
  63.7 8.5 %collective-permute-start.2 = (bf16[16,5696]{1,0:T(8,128)(2,1)S(1)}, bf16[16,5696]{1,0:T(8,128)(2,1)S(1)}, u32[]{:S(2)}, u32[]{:S(2)}) collective-permute-start(bf16[16,5696]{1,0:T(8,128)(2,1)S(1)} %get-tuple-element.257), channel_id=1, source_target_pairs={{0,1},{1,2},{2,3},{3,0},{4,5},{5,6},{6,7},{7,4},{8,9},{9,10},{10,1... | collective-permute-start | bytes 546824 | tf_op jit(solution)/shard_map/ppermute | solution.py:32
  64.9 11.6 %collective-permute-start.3 = (bf16[16,5696]{1,0:T(8,128)(2,1)S(1)}, bf16[16,5696]{1,0:T(8,128)(2,1)S(1)}, u32[]{:S(2)}, u32[]{:S(2)}) collective-permute-start(bf16[16,5696]{1,0:T(8,128)(2,1)S(1)} %get-tuple-element.257), channel_id=1, source_target_pairs={{0,2},{1,3},{2,0},{3,1},{4,6},{5,7},{6,4},{7,5},{8,10},{9,11},{10,... | collective-permute-start | bytes 546824 | tf_op jit(solution)/shard_map/ppermute | solution.py:32
  67.7 8.8 %collective-permute-start.4 = (bf16[16,5696]{1,0:T(8,128)(2,1)S(1)}, bf16[16,5696]{1,0:T(8,128)(2,1)S(1)}, u32[]{:S(2)}, u32[]{:S(2)}) collective-permute-start(bf16[16,5696]{1,0:T(8,128)(2,1)S(1)} %get-tuple-element.257), channel_id=1, source_target_pairs={{0,3},{1,0},{2,1},{3,2},{4,7},{5,4},{6,5},{7,6},{8,11},{9,8},{10,9... | collective-permute-start | bytes 546824 | tf_op jit(solution)/shard_map/ppermute | solution.py:32
  137.7 11.3 %collective-permute-start.5 = (bf16[64,256]{1,0:T(8,128)(2,1)S(1)}, bf16[64,256]{1,0:T(8,128)(2,1)S(1)}, u32[]{:S(2)}, u32[]{:S(2)}) collective-permute-start(bf16[64,256]{1,0:T(8,128)(2,1)S(1)} %fusion.20), channel_id=1, source_target_pairs={{0,16},{4,20},{8,24},{12,28},{16,32},{20,36},{24,40},{28,44},{32,4... | collective-permute-start | bytes 98312 | tf_op jit(solution)/shard_map/ppermute | solution.py:38
  153.3 11.2 %collective-permute-start.11 = (bf16[320,256]{1,0:T(8,128)(2,1)S(1)}, bf16[320,256]{1,0:T(8,128)(2,1)S(1)}, u32[]{:S(2)}, u32[]{:S(2)}) collective-permute-start(bf16[320,256]{1,0:T(8,128)(2,1)S(1)} %get-tuple-element.324), channel_id=1, source_target_pairs={{0,1},{1,2},{2,3},{3,0},{4,5},{5,6},{6,7},{7,4},{8,9},{9,10},{10,1... | collective-permute-start | bytes 491528 | tf_op jit(solution)/shard_map/ppermute | solution.py:32
  179.1 9.2 %collective-permute-start.12 = (bf16[64,2048]{1,0:T(8,128)(2,1)S(1)}, bf16[64,2048]{1,0:T(8,128)(2,1)S(1)}, u32[]{:S(2)}, u32[]{:S(2)}) collective-permute-start(bf16[64,2048]{1,0:T(8,128)(2,1)S(1)} %add_convert_fusion.3), channel_id=1, source_target_pairs={{0,3},{1,0},{2,1},{3,2},{4,7},{5,4},{6,5},{7,6},{8,11},{9,8},{10,9... | collective-permute-start | bytes 786440 | tf_op jit(solution)/shard_map/ppermute | solution.py:32
  180.3 10.7 %collective-permute-start.13 = (bf16[64,2048]{1,0:T(8,128)(2,1)S(1)}, bf16[64,2048]{1,0:T(8,128)(2,1)S(1)}, u32[]{:S(2)}, u32[]{:S(2)}) collective-permute-start(bf16[64,2048]{1,0:T(8,128)(2,1)S(1)} %add_convert_fusion.3), channel_id=1, source_target_pairs={{0,2},{1,3},{2,0},{3,1},{4,6},{5,7},{6,4},{7,5},{8,10},{9,11},{10,... | collective-permute-start | bytes 786440 | tf_op jit(solution)/shard_map/ppermute | solution.py:32
  181.2 14.4 %collective-permute-start.14 = (bf16[64,2048]{1,0:T(8,128)(2,1)S(1)}, bf16[64,2048]{1,0:T(8,128)(2,1)S(1)}, u32[]{:S(2)}, u32[]{:S(2)}) collective-permute-start(bf16[64,2048]{1,0:T(8,128)(2,1)S(1)} %add_convert_fusion.3), channel_id=1, source_target_pairs={{0,1},{1,2},{2,3},{3,0},{4,5},{5,6},{6,7},{7,4},{8,9},{9,10},{10,1... | collective-permute-start | bytes 786440 | tf_op jit(solution)/shard_map/ppermute | solution.py:32
  195.7 9.2 %collective-permute-start.15 = (bf16[64,2048]{1,0:T(8,128)(2,1)S(1)}, bf16[64,2048]{1,0:T(8,128)(2,1)S(1)}, u32[]{:S(2)}, u32[]{:S(2)}) collective-permute-start(bf16[64,2048]{1,0:T(8,128)(2,1)S(1)} %dynamic-slice_bitcast_fusion), channel_id=1, source_target_pairs={{0,3},{1,0},{2,1},{3,2},{4,7},{5,4},{6,5},{7,6},{8,11},{9,8},{10,9... | collective-permute-start | bytes 786440 | tf_op jit(solution)/shard_map/ppermute | solution.py:32
  196.3 10.8 %collective-permute-start.16 = (bf16[64,2048]{1,0:T(8,128)(2,1)S(1)}, bf16[64,2048]{1,0:T(8,128)(2,1)S(1)}, u32[]{:S(2)}, u32[]{:S(2)}) collective-permute-start(bf16[64,2048]{1,0:T(8,128)(2,1)S(1)} %dynamic-slice_bitcast_fusion), channel_id=1, source_target_pairs={{0,2},{1,3},{2,0},{3,1},{4,6},{5,7},{6,4},{7,5},{8,10},{9,11},{10,... | collective-permute-start | bytes 786440 | tf_op jit(solution)/shard_map/ppermute | solution.py:32
  197.2 14.1 %collective-permute-start.17 = (bf16[64,2048]{1,0:T(8,128)(2,1)S(1)}, bf16[64,2048]{1,0:T(8,128)(2,1)S(1)}, u32[]{:S(2)}, u32[]{:S(2)}) collective-permute-start(bf16[64,2048]{1,0:T(8,128)(2,1)S(1)} %dynamic-slice_bitcast_fusion), channel_id=1, source_target_pairs={{0,1},{1,2},{2,3},{3,0},{4,5},{5,6},{6,7},{7,4},{8,9},{9,10},{10,1... | collective-permute-start | bytes 786440 | tf_op jit(solution)/shard_map/ppermute | solution.py:32
  223.4 15.1 %collective-permute-start.19 = (bf16[64,2048]{1,0:T(8,128)(2,1)S(1)}, bf16[64,2048]{1,0:T(8,128)(2,1)S(1)}, u32[]{:S(2)}, u32[]{:S(2)}) collective-permute-start(bf16[64,2048]{1,0:T(8,128)(2,1)S(1)} %get-tuple-element.155), channel_id=1, source_target_pairs={{0,1},{1,2},{2,3},{3,0},{4,5},{5,6},{6,7},{7,4},{8,9},{9,10},{10,1... | collective-permute-start | bytes 786440 | tf_op jit(solution)/shard_map/ppermute | solution.py:32
  223.5 15.0 %collective-permute-start.20 = (bf16[64,2048]{1,0:T(8,128)(2,1)S(1)}, bf16[64,2048]{1,0:T(8,128)(2,1)S(1)}, u32[]{:S(2)}, u32[]{:S(2)}) collective-permute-start(bf16[64,2048]{1,0:T(8,128)(2,1)S(1)} %get-tuple-element.157), channel_id=1, source_target_pairs={{0,2},{1,3},{2,0},{3,1},{4,6},{5,7},{6,4},{7,5},{8,10},{9,11},{10,... | collective-permute-start | bytes 786440 | tf_op jit(solution)/shard_map/ppermute | solution.py:32
  226.0 13.1 %collective-permute-start.21 = (bf16[64,2048]{1,0:T(8,128)(2,1)S(1)}, bf16[64,2048]{1,0:T(8,128)(2,1)S(1)}, u32[]{:S(2)}, u32[]{:S(2)}) collective-permute-start(bf16[64,2048]{1,0:T(8,128)(2,1)S(1)} %get-tuple-element.156), channel_id=1, source_target_pairs={{0,3},{1,0},{2,1},{3,2},{4,7},{5,4},{6,5},{7,6},{8,11},{9,8},{10,9... | collective-permute-start | bytes 786440 | tf_op jit(solution)/shard_map/ppermute | solution.py:32
  242.5 8.5 %collective-permute-start.22 = (bf16[64,256]{1,0:T(8,128)(2,1)S(1)}, bf16[64,256]{1,0:T(8,128)(2,1)S(1)}, u32[]{:S(2)}, u32[]{:S(2)}) collective-permute-start(bf16[64,256]{1,0:T(8,128)(2,1)S(1)} %fusion.21), channel_id=1, source_target_pairs={{0,16},{4,20},{8,24},{12,28},{16,32},{20,36},{24,40},{28,44},{32,4... | collective-permute-start | bytes 98312 | tf_op jit(solution)/shard_map/ppermute | solution.py:38
  255.4 11.3 %collective-permute-start.28 = (bf16[320,256]{1,0:T(8,128)(2,1)S(1)}, bf16[320,256]{1,0:T(8,128)(2,1)S(1)}, u32[]{:S(2)}, u32[]{:S(2)}) collective-permute-start(bf16[320,256]{1,0:T(8,128)(2,1)S(1)} %get-tuple-element.314), channel_id=1, source_target_pairs={{0,1},{1,2},{2,3},{3,0},{4,5},{5,6},{6,7},{7,4},{8,9},{9,10},{10,1... | collective-permute-start | bytes 491528 | tf_op jit(solution)/shard_map/ppermute | solution.py:32
  281.3 9.2 %collective-permute-start.29 = (bf16[64,2048]{1,0:T(8,128)(2,1)S(1)}, bf16[64,2048]{1,0:T(8,128)(2,1)S(1)}, u32[]{:S(2)}, u32[]{:S(2)}) collective-permute-start(bf16[64,2048]{1,0:T(8,128)(2,1)S(1)} %add_convert_fusion.1), channel_id=1, source_target_pairs={{0,3},{1,0},{2,1},{3,2},{4,7},{5,4},{6,5},{7,6},{8,11},{9,8},{10,9... | collective-permute-start | bytes 786440 | tf_op jit(solution)/shard_map/ppermute | solution.py:32
  281.6 10.7 %collective-permute-start.30 = (bf16[64,2048]{1,0:T(8,128)(2,1)S(1)}, bf16[64,2048]{1,0:T(8,128)(2,1)S(1)}, u32[]{:S(2)}, u32[]{:S(2)}) collective-permute-start(bf16[64,2048]{1,0:T(8,128)(2,1)S(1)} %add_convert_fusion.1), channel_id=1, source_target_pairs={{0,2},{1,3},{2,0},{3,1},{4,6},{5,7},{6,4},{7,5},{8,10},{9,11},{10,... | collective-permute-start | bytes 786440 | tf_op jit(solution)/shard_map/ppermute | solution.py:32
  282.4 15.3 %collective-permute-start.31 = (bf16[64,2048]{1,0:T(8,128)(2,1)S(1)}, bf16[64,2048]{1,0:T(8,128)(2,1)S(1)}, u32[]{:S(2)}, u32[]{:S(2)}) collective-permute-start(bf16[64,2048]{1,0:T(8,128)(2,1)S(1)} %add_convert_fusion.1), channel_id=1, source_target_pairs={{0,1},{1,2},{2,3},{3,0},{4,5},{5,6},{6,7},{7,4},{8,9},{9,10},{10,1... | collective-permute-start | bytes 786440 | tf_op jit(solution)/shard_map/ppermute | solution.py:32
  316.0 15.2 %collective-permute-start.32 = (bf16[64,2048]{1,0:T(8,128)(2,1)S(1)}, bf16[64,2048]{1,0:T(8,128)(2,1)S(1)}, u32[]{:S(2)}, u32[]{:S(2)}) collective-permute-start(bf16[64,2048]{1,0:T(8,128)(2,1)S(1)} %get-tuple-element.152), channel_id=1, source_target_pairs={{0,1},{1,2},{2,3},{3,0},{4,5},{5,6},{6,7},{7,4},{8,9},{9,10},{10,1... | collective-permute-start | bytes 786440 | tf_op jit(solution)/shard_map/ppermute | solution.py:32
  316.1 15.1 %collective-permute-start.33 = (bf16[64,2048]{1,0:T(8,128)(2,1)S(1)}, bf16[64,2048]{1,0:T(8,128)(2,1)S(1)}, u32[]{:S(2)}, u32[]{:S(2)}) collective-permute-start(bf16[64,2048]{1,0:T(8,128)(2,1)S(1)} %get-tuple-element.154), channel_id=1, source_target_pairs={{0,2},{1,3},{2,0},{3,1},{4,6},{5,7},{6,4},{7,5},{8,10},{9,11},{10,... | collective-permute-start | bytes 786440 | tf_op jit(solution)/shard_map/ppermute | solution.py:32
  318.3 13.5 %collective-permute-start.34 = (bf16[64,2048]{1,0:T(8,128)(2,1)S(1)}, bf16[64,2048]{1,0:T(8,128)(2,1)S(1)}, u32[]{:S(2)}, u32[]{:S(2)}) collective-permute-start(bf16[64,2048]{1,0:T(8,128)(2,1)S(1)} %get-tuple-element.153), channel_id=1, source_target_pairs={{0,3},{1,0},{2,1},{3,2},{4,7},{5,4},{6,5},{7,6},{8,11},{9,8},{10,9... | collective-permute-start | bytes 786440 | tf_op jit(solution)/shard_map/ppermute | solution.py:32
  340.7 11.1 %collective-permute-start.35 = (bf16[320,256]{1,0:T(8,128)(2,1)S(1)}, bf16[320,256]{1,0:T(8,128)(2,1)S(1)}, u32[]{:S(2)}, u32[]{:S(2)}) collective-permute-start(bf16[320,256]{1,0:T(8,128)(2,1)S(1)} %get-tuple-element.174), channel_id=1, source_target_pairs={{0,1},{1,2},{2,3},{3,0},{4,5},{5,6},{6,7},{7,4},{8,9},{9,10},{10,1... | collective-permute-start | bytes 491528 | tf_op jit(solution)/shard_map/ppermute | solution.py:32
  341.0 11.3 %collective-permute-start.36 = (bf16[320,256]{1,0:T(8,128)(2,1)S(1)}, bf16[320,256]{1,0:T(8,128)(2,1)S(1)}, u32[]{:S(2)}, u32[]{:S(2)}) collective-permute-start(bf16[320,256]{1,0:T(8,128)(2,1)S(1)} %get-tuple-element.176), channel_id=1, source_target_pairs={{0,2},{1,3},{2,0},{3,1},{4,6},{5,7},{6,4},{7,5},{8,10},{9,11},{10,... | collective-permute-start | bytes 491528 | tf_op jit(solution)/shard_map/ppermute | solution.py:32
  356.4 8.9 %collective-permute-start.41 = (bf16[64,256]{1,0:T(8,128)(2,1)S(1)}, bf16[64,256]{1,0:T(8,128)(2,1)S(1)}, u32[]{:S(2)}, u32[]{:S(2)}) collective-permute-start(bf16[64,256]{1,0:T(8,128)(2,1)S(1)} %get-tuple-element.273), channel_id=1, source_target_pairs={{16,0},{20,4},{24,8},{28,12},{32,16},{36,20},{40,24},{44,28},{48,3... | collective-permute-start | bytes 98312 | tf_op jit(solution)/shard_map/ppermute | solution.py:38
  369.1 15.8 %collective-permute-start.42 = (bf16[64,2048]{1,0:T(8,128)(2,1)}, bf16[64,2048]{1,0:T(8,128)(2,1)}, u32[]{:S(2)}, u32[]{:S(2)}) collective-permute-start(bf16[64,2048]{1,0:T(8,128)(2,1)} %get-tuple-element.126), channel_id=1, source_target_pairs={{0,3},{1,0},{2,1},{3,2},{4,7},{5,4},{6,5},{7,6},{8,11},{9,8},{10,9... | collective-permute-start | bytes 786440 | tf_op jit(solution)/shard_map/ppermute | solution.py:32
  371.3 13.7 %collective-permute-start.43 = (bf16[64,2048]{1,0:T(8,128)(2,1)}, bf16[64,2048]{1,0:T(8,128)(2,1)}, u32[]{:S(2)}, u32[]{:S(2)}) collective-permute-start(bf16[64,2048]{1,0:T(8,128)(2,1)} %get-tuple-element.126), channel_id=1, source_target_pairs={{0,2},{1,3},{2,0},{3,1},{4,6},{5,7},{6,4},{7,5},{8,10},{9,11},{10,... | collective-permute-start | bytes 786440 | tf_op jit(solution)/shard_map/ppermute | solution.py:32
  372.7 13.3 %collective-permute-start.44 = (bf16[64,2048]{1,0:T(8,128)(2,1)}, bf16[64,2048]{1,0:T(8,128)(2,1)}, u32[]{:S(2)}, u32[]{:S(2)}) collective-permute-start(bf16[64,2048]{1,0:T(8,128)(2,1)} %get-tuple-element.126), channel_id=1, source_target_pairs={{0,1},{1,2},{2,3},{3,0},{4,5},{5,6},{6,7},{7,4},{8,9},{9,10},{10,1... | collective-permute-start | bytes 786440 | tf_op jit(solution)/shard_map/ppermute | solution.py:32
  397.4 15.1 %collective-permute-start.45 = (bf16[64,2048]{1,0:T(8,128)(2,1)S(1)}, bf16[64,2048]{1,0:T(8,128)(2,1)S(1)}, u32[]{:S(2)}, u32[]{:S(2)}) collective-permute-start(bf16[64,2048]{1,0:T(8,128)(2,1)S(1)} %get-tuple-element.149), channel_id=1, source_target_pairs={{0,1},{1,2},{2,3},{3,0},{4,5},{5,6},{6,7},{7,4},{8,9},{9,10},{10,1... | collective-permute-start | bytes 786440 | tf_op jit(solution)/shard_map/ppermute | solution.py:32
  398.5 14.1 %collective-permute-start.46 = (bf16[64,2048]{1,0:T(8,128)(2,1)S(1)}, bf16[64,2048]{1,0:T(8,128)(2,1)S(1)}, u32[]{:S(2)}, u32[]{:S(2)}) collective-permute-start(bf16[64,2048]{1,0:T(8,128)(2,1)S(1)} %get-tuple-element.151), channel_id=1, source_target_pairs={{0,2},{1,3},{2,0},{3,1},{4,6},{5,7},{6,4},{7,5},{8,10},{9,11},{10,... | collective-permute-start | bytes 786440 | tf_op jit(solution)/shard_map/ppermute | solution.py:32
  401.2 12.0 %collective-permute-start.47 = (bf16[64,2048]{1,0:T(8,128)(2,1)S(1)}, bf16[64,2048]{1,0:T(8,128)(2,1)S(1)}, u32[]{:S(2)}, u32[]{:S(2)}) collective-permute-start(bf16[64,2048]{1,0:T(8,128)(2,1)S(1)} %get-tuple-element.150), channel_id=1, source_target_pairs={{0,3},{1,0},{2,1},{3,2},{4,7},{5,4},{6,5},{7,6},{8,11},{9,8},{10,9... | collective-permute-start | bytes 786440 | tf_op jit(solution)/shard_map/ppermute | solution.py:32
  422.0 11.4 %collective-permute-start.48 = (bf16[320,256]{1,0:T(8,128)(2,1)S(1)}, bf16[320,256]{1,0:T(8,128)(2,1)S(1)}, u32[]{:S(2)}, u32[]{:S(2)}) collective-permute-start(bf16[320,256]{1,0:T(8,128)(2,1)S(1)} %get-tuple-element.171), channel_id=1, source_target_pairs={{0,1},{1,2},{2,3},{3,0},{4,5},{5,6},{6,7},{7,4},{8,9},{9,10},{10,1... | collective-permute-start | bytes 491528 | tf_op jit(solution)/shard_map/ppermute | solution.py:32
  422.9 10.9 %collective-permute-start.49 = (bf16[320,256]{1,0:T(8,128)(2,1)S(1)}, bf16[320,256]{1,0:T(8,128)(2,1)S(1)}, u32[]{:S(2)}, u32[]{:S(2)}) collective-permute-start(bf16[320,256]{1,0:T(8,128)(2,1)S(1)} %get-tuple-element.173), channel_id=1, source_target_pairs={{0,2},{1,3},{2,0},{3,1},{4,6},{5,7},{6,4},{7,5},{8,10},{9,11},{10,... | collective-permute-start | bytes 491528 | tf_op jit(solution)/shard_map/ppermute | solution.py:32
  437.7 9.4 %collective-permute-start.54 = (bf16[64,256]{1,0:T(8,128)(2,1)S(1)}, bf16[64,256]{1,0:T(8,128)(2,1)S(1)}, u32[]{:S(2)}, u32[]{:S(2)}) collective-permute-start(bf16[64,256]{1,0:T(8,128)(2,1)S(1)} %get-tuple-element.269), channel_id=1, source_target_pairs={{16,0},{20,4},{24,8},{28,12},{32,16},{36,20},{40,24},{44,28},{48,3... | collective-permute-start | bytes 98312 | tf_op jit(solution)/shard_map/ppermute | solution.py:38
  450.3 9.6 %collective-permute-start.55 = (bf16[2,29,16,128]{3,2,1,0:T(8,128)(2,1)S(1)}, bf16[2,29,16,128]{3,2,1,0:T(8,128)(2,1)S(1)}, u32[]{:S(2)}, u32[]{:S(2)}) collective-permute-start(bf16[2,29,16,128]{3,2,1,0:T(8,128)(2,1)S(1)} %get-tuple-element.158), channel_id=1, source_target_pairs={{0,1},{1,2},{2,3},{3,0},{4,5},{5,6},{6,7},{7,4},{8,9},{9,10},{10,1... | collective-permute-start | bytes 712712 | tf_op jit(solution)/shard_map/ppermute | solution.py:32
  452.1 12.0 %collective-permute-start.56 = (bf16[2,29,16,128]{3,2,1,0:T(8,128)(2,1)S(1)}, bf16[2,29,16,128]{3,2,1,0:T(8,128)(2,1)S(1)}, u32[]{:S(2)}, u32[]{:S(2)}) collective-permute-start(bf16[2,29,16,128]{3,2,1,0:T(8,128)(2,1)S(1)} %get-tuple-element.160), channel_id=1, source_target_pairs={{0,2},{1,3},{2,0},{3,1},{4,6},{5,7},{6,4},{7,5},{8,10},{9,11},{10,... | collective-permute-start | bytes 712712 | tf_op jit(solution)/shard_map/ppermute | solution.py:32
  454.0 10.3 %collective-permute-start.57 = (bf16[2,29,16,128]{3,2,1,0:T(8,128)(2,1)S(1)}, bf16[2,29,16,128]{3,2,1,0:T(8,128)(2,1)S(1)}, u32[]{:S(2)}, u32[]{:S(2)}) collective-permute-start(bf16[2,29,16,128]{3,2,1,0:T(8,128)(2,1)S(1)} %get-tuple-element.159), channel_id=1, source_target_pairs={{0,3},{1,0},{2,1},{3,2},{4,7},{5,4},{6,5},{7,6},{8,11},{9,8},{10,9... | collective-permute-start | bytes 712712 | tf_op jit(solution)/shard_map/ppermute | solution.py:32
  455.9 11.1 %collective-permute-start.65 = (bf16[64,2048]{1,0:T(8,128)(2,1)S(1)}, bf16[64,2048]{1,0:T(8,128)(2,1)S(1)}, u32[]{:S(2)}, u32[]{:S(2)}) collective-permute-start(bf16[64,2048]{1,0:T(8,128)(2,1)S(1)} %select_convert_fusion), channel_id=1, source_target_pairs={{0,64},{64,0},{1,65},{65,1},{2,66},{66,2},{3,67},{67,3},{4,68},{68... | collective-permute-start | bytes 786440 | tf_op jit(solution)/shard_map/ppermute | solution.py:540
  483.1 8.7 %collective-permute-start.69 = (bf16[4,16,128]{2,1,0:T(8,128)(2,1)S(1)}, bf16[4,16,128]{2,1,0:T(8,128)(2,1)S(1)}, u32[]{:S(2)}, u32[]{:S(2)}) collective-permute-start(bf16[4,16,128]{2,1,0:T(8,128)(2,1)S(1)} %bitcast.778), channel_id=1, source_target_pairs={{0,8},{4,12},{8,0},{12,4},{16,24},{20,28},{24,16},{28,20},{32,40},... | collective-permute-start | bytes 49160 | tf_op jit(solution)/shard_map/ppermute | solution.py:43
  484.5 18.6 %collective-permute-start.61 = (bf16[64,2048]{1,0:T(8,128)(2,1)S(1)}, bf16[64,2048]{1,0:T(8,128)(2,1)S(1)}, u32[]{:S(2)}, u32[]{:S(2)}) collective-permute-start(bf16[64,2048]{1,0:T(8,128)(2,1)S(1)} %get-tuple-element.146), channel_id=1, source_target_pairs={{0,1},{1,2},{2,3},{3,0},{4,5},{5,6},{6,7},{7,4},{8,9},{9,10},{10,1... | collective-permute-start | bytes 786440 | tf_op jit(solution)/shard_map/ppermute | solution.py:32
  485.5 17.6 %collective-permute-start.62 = (bf16[64,2048]{1,0:T(8,128)(2,1)S(1)}, bf16[64,2048]{1,0:T(8,128)(2,1)S(1)}, u32[]{:S(2)}, u32[]{:S(2)}) collective-permute-start(bf16[64,2048]{1,0:T(8,128)(2,1)S(1)} %get-tuple-element.148), channel_id=1, source_target_pairs={{0,2},{1,3},{2,0},{3,1},{4,6},{5,7},{6,4},{7,5},{8,10},{9,11},{10,... | collective-permute-start | bytes 786440 | tf_op jit(solution)/shard_map/ppermute | solution.py:32
  507.5 8.8 %collective-permute-start.76 = (bf16[2,21,16,128]{3,2,1,0:T(8,128)(2,1)S(1)}, bf16[2,21,16,128]{3,2,1,0:T(8,128)(2,1)S(1)}, u32[]{:S(2)}, u32[]{:S(2)}) collective-permute-start(bf16[2,21,16,128]{3,2,1,0:T(8,128)(2,1)S(1)} %get-tuple-element.186), channel_id=1, source_target_pairs={{0,1},{1,2},{2,3},{3,0},{4,5},{5,6},{6,7},{7,4},{8,9},{9,10},{10,1... | collective-permute-start | bytes 516104 | tf_op jit(solution)/shard_map/ppermute | solution.py:32
  (169 other events, 2733.3 us)
Sparse Core Ops, SparseCore 0:
  11.6 122.7 all-gather.3
  137.3 71.9 all-gather.5
  212.1 71.9 all-gather.7

commit v16 on v15

--- a/solution.py
+++ b/solution.py
@@ -727,12 +727,9 @@
         low_kv = against(normed, skv).astype(bf16)
         keyval = (plain(normed, keyval_ws[layer]) + kv_bias + plain(low_kv, ekv)).astype(bf16)
         pieces = [along(keyval, "dp", back) for back in range(reach, 0, -1)] + [keyval]
-        own_keys = jnp.concatenate(pieces, axis=0)
-        blocks = [own_keys] + [around(own_keys, "tensor", -j) for j in range(1, ranks)]
-        query_rows, blocks[1] = lax.optimization_barrier((normed, blocks[1]))
-        key_block = jnp.concatenate(blocks, axis=0)
+        key_block = spread(jnp.concatenate(pieces, axis=0))
         queries, low_q = project_queries(
-            layer, query_rows, early_all, query_bias_all[layer][:1].astype(f32), eq_all[layer], sq
+            layer, normed, early_all, query_bias_all[layer][:1].astype(f32), eq_all[layer], sq
         )
         probs, mixed, low_o, attended = attend(
             layer, queries, key_block, bias, early_all, so_all[layer], eo, head

time: 537 us -> 532 us (level)
  waiting for transfers between devices: 222 us -> 205 us
  starting transfers between devices: 116 us -> 125 us
    ppermute x45, waiting for transfers between devices: 111 us -> 96.2 us  [around(): lax.ppermute(block, axis, [(i, (i + distance) % size) for i in range(size)])]
    ppermute x45, starting transfers between devices: 59.3 us -> 64.9 us  [around(): lax.ppermute(block, axis, [(i, (i + distance) % size) for i in range(size)])]
    unnamed x312 -> x300, local copies, waits for them, and re-layouts: 12.1 us -> 14.9 us
  transfers between devices with their start and end apart: 82 -> 82, of which waited for: 53 -> 52; matrix products, arithmetic and copies ran while one was open for 10% -> 11% of each run, Pallas kernels for 10% -> 10%
where the time goes in v16:
time: 532 us; the launch traced here: 524 us
  waiting for transfers between devices  205 us (39%)
  starting transfers between devices  125 us (23%)
  Pallas kernels  93 us (17%)
  local copies, waits for them, and re-layouts  38.9 us (7%)
  other arithmetic  29.3 us (6%)
  between operations  21.1 us (4%)
  matrix products  11.7 us (2%)
    ppermute x45, waiting for transfers between devices, around(): lax.ppermute(block, axis, [(i, (i + distance) % size) for i in range(size)])  96.2 us
    ppermute x45, starting transfers between devices, around(): lax.ppermute(block, axis, [(i, (i + distance) % size) for i in range(size)])  64.9 us
    all_gather x1, waiting for transfers between devices, gather_all(): lax.all_gather(row_major(shard), every, axis=0, tiled=True, axis_index_gr...  52.7 us
    pallas_call x3, Pallas kernels, feed_call(): pl.pallas_call(kernel, in_specs=[remote if value.ndim == 4 or i in copied...  35.4 us
    ppermute x16, starting transfers between devices, along(): return lax.ppermute(block, axis, route)  32 us
    ppermute x5, waiting for transfers between devices, swap(): return lax.ppermute(value, 'section', sides)  26.5 us
    pallas_call x2, Pallas kernels, attend(): pl.pallas_call(lambda *refs: attend_kernel(layer, head, *refs), in_specs=...  19.9 us
    pallas_call x2, Pallas kernels, attend_back(): pl.pallas_call(lambda *refs: attend_back_kernel(layer, head, *refs), in_s...  16.1 us
  transfers between devices with their start and end apart: 82, of which 52 were waited for; matrix products, arithmetic and copies ran while one was open for 11% of the time, Pallas kernels for 10%

profile of v16, /device:TPU:0, one launch (start us, length us, event | category | flops | bytes accessed | tf_op | source)
XLA Modules:
  0.0 523.5 jit_solution(4399460569413645659)
XLA Ops:
  12.3 4.0 collective-permute-start.18
  16.4 12.2 %collective-permute-done.18 = bf16[128,2048]{1,0:T(8,128)(2,1)S(1)} collective-permute-done((bf16[128,2048]{1,0:T(8,128)(2,1)S(1)}, bf16[128,2048]{1,0:T(8,128)(2,1)S(1)}, u32[]{:S(2)}, u32[]{:S(2)}) %collective-permute-start.18) | collective-permute-done | bytes 524320 | tf_op jit(solution)/shard_map/ppermute | solution.py:540
  47.7 4.2 collective-permute-start.1
  54.4 12.3 %collective-permute-done = bf16[1,14592]{1,0:T(2,128)(2,1)S(1)} collective-permute-done((bf16[1,14592]{1,0:T(2,128)(2,1)S(1)}, bf16[1,14592]{1,0:T(2,128)(2,1)S(1)}, u32[]{:S(2)}, u32[]{:S(2)}) %collective-permute-start) | collective-permute-done | bytes 29216 | tf_op jit(solution)/shard_map/ppermute | solution.py:540
  69.2 2.7 collective-permute-start.3
  73.9 2.6 collective-permute-done.2
  81.3 52.7 %all-gather.4.cloned.1.call-done = bf16[16384,1152]{1,0:T(8,128)(2,1)} async-done(((bf16[128,1152]{1,0:T(8,128)(2,1)}), bf16[16384,1152]{1,0:T(8,128)(2,1)}) %all-gather.4.cloned.1.call-update) | async-done | bytes 37748752 | tf_op jit(solution)/shard_map/all_gather | solution.py:578
  134.0 2.8 fusion.137
  137.3 3.4 collective-permute-start.5
  143.0 4.1 collective-permute-start.7
  152.8 4.4 project_queries.2
  160.2 5.7 %collective-permute-done.11 = bf16[320,256]{1,0:T(8,128)(2,1)S(1)} collective-permute-done((bf16[320,256]{1,0:T(8,128)(2,1)S(1)}, bf16[320,256]{1,0:T(8,128)(2,1)S(1)}, u32[]{:S(2)}, u32[]{:S(2)}) %collective-permute-start.11) | collective-permute-done | bytes 163872 | tf_op jit(solution)/shard_map/ppermute | solution.py:32
  166.0 10.4 %attend.2 = (bf16[4,256,1280]{2,1,0:T(8,128)(2,1)S(1)}, bf16[64,2048]{1,0:T(8,128)(2,1)S(1)}, bf16[64,16]{1,0:T(8,128)(2,1)S(1)}, f32[64,2048]{1,0:T(8,128)S(1)}) custom-call(bf16[64,2048]{1,0:T(8,128)(2,1)S(1)} %get-tuple-element.57.refs_0_.refs_5_, bf16[1280,256]{1,0:T(8,128)(2,1)S(1)} %constant_dynamic-update-slice_fusion.26.refs_1_.refs_6_, ...), custom_call_target="tpu_custom_call" | custom-call | flops 2818572288 | bytes 8388608 | tf_op jit(solution)/shard_map/attend/pallas_call | solution.py:180
  181.5 4.8 collective-permute-done.12
  187.9 4.7 collective-permute-done.14
  195.6 6.3 %collective-permute-done.15 = bf16[64,2048]{1,0:T(8,128)(2,1)S(1)} collective-permute-done((bf16[64,2048]{1,0:T(8,128)(2,1)S(1)}, bf16[64,2048]{1,0:T(8,128)(2,1)S(1)}, u32[]{:S(2)}, u32[]{:S(2)}) %collective-permute-start.15) | collective-permute-done | bytes 262176 | tf_op jit(solution)/shard_map/ppermute | solution.py:32
  201.9 2.7 collective-permute-done.16
  204.6 3.7 collective-permute-done.17
  209.4 10.8 %feed.1 = (bf16[256,2048]{1,0:T(8,128)(2,1)S(1)}, bf16[256,2048]{1,0:T(8,128)(2,1)S(1)}, bf16[256,16]{1,0:T(8,128)(2,1)S(1)}, bf16[256,16]{1,0:T(8,128)(2,1)S(1)}, bf16[256,2048]{1,0:T(8,128)(2,1)S(1)}) custom-call(bf16[256,2048]{1,0:T(8,128)(2,1)S(1)} %pad_maximum_fusion.1.second_ref, bf16[4,2,512,2048]{3,2,1,0:T(8,128)(2,1)} %bitcast.700, ...), custom_call_target="tpu_custom_call" | custom-call | flops 4294967296 | bytes 16777216 | tf_op jit(solution)/shard_map/feed/pallas_call | solution.py:470
  221.4 2.7 collective-permute-start.20
  226.2 3.8 collective-permute-done.19
  230.0 6.1 %collective-permute-done.20 = bf16[64,2048]{1,0:T(8,128)(2,1)S(1)} collective-permute-done((bf16[64,2048]{1,0:T(8,128)(2,1)S(1)}, bf16[64,2048]{1,0:T(8,128)(2,1)S(1)}, u32[]{:S(2)}, u32[]{:S(2)}) %collective-permute-start.20) | collective-permute-done | bytes 262176 | tf_op jit(solution)/shard_map/ppermute | solution.py:32
  237.7 3.4 collective-permute-start.22
  242.4 4.2 collective-permute-start.24
  249.0 2.9 collective-permute-start.26
  252.6 4.4 project_queries.3
  259.9 4.9 collective-permute-done.28
  264.8 9.5 %attend.3 = (bf16[4,256,1280]{2,1,0:T(8,128)(2,1)S(1)}, bf16[64,2048]{1,0:T(8,128)(2,1)S(1)}, bf16[64,16]{1,0:T(8,128)(2,1)S(1)}, f32[64,2048]{1,0:T(8,128)S(1)}) custom-call(bf16[64,2048]{1,0:T(8,128)(2,1)S(1)} %get-tuple-element.63.refs_0_.refs_5_, bf16[1280,256]{1,0:T(8,128)(2,1)S(1)} %constant_dynamic-update-slice_fusion.39.refs_1_.refs_6_, ...), custom_call_target="tpu_custom_call" | custom-call | flops 2818572288 | bytes 8388608 | tf_op jit(solution)/shard_map/attend/pallas_call | solution.py:180
  279.5 4.5 collective-permute-done.29
  286.2 5.5 %collective-permute-done.31 = bf16[64,2048]{1,0:T(8,128)(2,1)S(1)} collective-permute-done((bf16[64,2048]{1,0:T(8,128)(2,1)S(1)}, bf16[64,2048]{1,0:T(8,128)(2,1)S(1)}, u32[]{:S(2)}, u32[]{:S(2)}) %collective-permute-start.31) | collective-permute-done | bytes 262176 | tf_op jit(solution)/shard_map/ppermute | solution.py:32
  293.5 14.5 %feed_both.1 = (bf16[256,2048]{1,0:T(8,128)(2,1)S(1)}, bf16[256,16]{1,0:T(8,128)(2,1)S(1)}, bf16[256,16]{1,0:T(8,128)(2,1)S(1)}, bf16[256,2048]{1,0:T(8,128)(2,1...) custom-call(bf16[256,2048]{1,0:T(8,128)(2,1)S(1)} %pad_maximum_fusio, ...), custom_call_target="tpu_custom_call" | custom-call | flops 8589934592 | bytes 16777216 | tf_op jit(solution)/shard_map/feed_both/pallas_call | solution.py:470
  316.4 8.8 %collective-permute-done.32 = bf16[64,2048]{1,0:T(8,128)(2,1)S(1)} collective-permute-done((bf16[64,2048]{1,0:T(8,128)(2,1)S(1)}, bf16[64,2048]{1,0:T(8,128)(2,1)S(1)}, u32[]{:S(2)}, u32[]{:S(2)}) %collective-permute-start.32) | collective-permute-done | bytes 262176 | tf_op jit(solution)/shard_map/ppermute | solution.py:32
  326.5 8.1 %attend_back.2 = (bf16[64,2048]{1,0:T(8,128)(2,1)S(1)}, bf16[1280,256]{1,0:T(8,128)(2,1)S(1)}, bf16[64,16]{1,0:T(8,128)(2,1)S(1)}) custom-call(bf16[64,2048]{1,0:T(8,128)(2,1)S(1)} %get-tuple-element.123.refs_0_, bf16[4,4,2,512,1152]{4,3,2,1,0:T(8,128)(2,1)} %bitcast.696, bf16[16,2048]{1,0:T(8,128)(2,1)S(1)} %copy-done.23, bf16[16,2048]{1,0:T(8,128)(2,1)S(1)} %copy-done.33, ...), custom_call_target="tpu_custom_call" | custom-call | flops 3489660928 | bytes 13631488 | tf_op jit(solution)/shard_map/attend_back/pallas_call | solution.py:284
  335.8 3.0 collective-permute-start.36
  339.1 6.3 %query_back.2 = (bf16[64,16]{1,0:T(8,128)(2,1)S(1)}, f32[64,2048]{1,0:T(8,128)S(1)}) custom-call(bf16[64,2048]{1,0:T(8,128)(2,1)S(1)} %get-tuple-element.68.refs_0_, bf16[4,4,2,512,1152]{4,3,2,1,0:T(8,128)(2,1)} %bitcast.697, bf16[16,2048]{1,0:T(8,128)(2,1)S(1)} %copy-done.25, bf16[16,2048]{1,0:T(8,128)(2,1)S(1)} %copy-done.31), custom_call_target="tpu_custom_call" | custom-call | flops 2147483648 | bytes 8388608 | tf_op jit(solution)/shard_map/query_back/pallas_call | solution.py:261
  355.9 2.9 collective-permute-done.41
  369.2 7.9 %concatenate.239 = bf16[84,16,128]{2,0,1:T(8,128)(2,1)} concatenate(bf16[16,16,128]{2,0,1:T(8,128)(2,1)} %bitcast.746, bf16[16,16,128]{2,0,1:T(8,128)(2,1)} %bitcast.745, bf16[16,16,128]{2,0,1:T(8,128)(2,1)} %bitcast.748, bf16[16,16,128]{2,0,1:T(8,128)(2,1)} %bitcast.747, bf16[16,16,128]{2,0,1:T(8,128)(2,1)S(1)} %bitcast.749, bf16[2,16,128]{2,0,1:T(2,128)(2,1)} %bitcast.791, ...), dimensions={0} | concatenate | bytes 688128 | tf_op jit(solution)/shard_map/concatenate | solution.py:761
  381.1 10.0 %feed_back.1 = (bf16[256,2048]{1,0:T(8,128)(2,1)S(1)}, bf16[256,16]{1,0:T(8,128)(2,1)S(1)}, bf16[256,16]{1,0:T(8,128)(2,1)S(1)}, bf16[256,2048]{1,0:T(8,128)(2,1)S(1)}) custom-call(bf16[256,2048]{1,0:T(8,128)(2,1)S(1)} %pad_maximum_fusion.5.branch_ref, bf16[4,2,512,2048]{3,2,1,0:T(8,128)(2,1)} %bitcast.701, bf16[256,2048]{1,0:T(8,128)(2,1)S(1)} %copy-done.17, ...), custom_call_target="tpu_custom_call" | custom-call | flops 4294967296 | bytes 16777216 | tf_op jit(solution)/shard_map/feed_back/pallas_call | solution.py:470
  397.4 9.0 %collective-permute-done.45 = bf16[64,2048]{1,0:T(8,128)(2,1)S(1)} collective-permute-done((bf16[64,2048]{1,0:T(8,128)(2,1)S(1)}, bf16[64,2048]{1,0:T(8,128)(2,1)S(1)}, u32[]{:S(2)}, u32[]{:S(2)}) %collective-permute-start.45) | collective-permute-done | bytes 262176 | tf_op jit(solution)/shard_map/ppermute | solution.py:32
  407.7 8.1 %attend_back.3 = (bf16[64,2048]{1,0:T(8,128)(2,1)S(1)}, bf16[1280,256]{1,0:T(8,128)(2,1)S(1)}, bf16[64,16]{1,0:T(8,128)(2,1)S(1)}) custom-call(bf16[64,2048]{1,0:T(8,128)(2,1)S(1)} %get-tuple-element.115.refs_0_, bf16[4,4,2,512,1152]{4,3,2,1,0:T(8,128)(2,1)} %bitcast.698, bf16[16,2048]{1,0:T(8,128)(2,1)S(1)} %get-tuple-element.272.refs_4_.refs_2_, ...), custom_call_target="tpu_custom_call" | custom-call | flops 3489660928 | bytes 13631488 | tf_op jit(solution)/shard_map/attend_back/pallas_call | solution.py:284
  417.0 3.0 collective-permute-start.49
  420.3 6.6 %query_back.3 = (bf16[64,16]{1,0:T(8,128)(2,1)S(1)}, f32[64,2048]{1,0:T(8,128)S(1)}) custom-call(bf16[64,2048]{1,0:T(8,128)(2,1)S(1)} %get-tuple-element.77.refs_0_, bf16[4,4,2,512,1152]{4,3,2,1,0:T(8,128)(2,1)} %bitcast.699, bf16[16,2048]{1,0:T(8,128)(2,1)S(1)} %get-tuple-element.274.refs_3_.refs_2_, bf16[16,2048]{1,0:T(8,128)(2,1)S(1)} %copy-done.27), custom_call_target="tpu_custom_call" | custom-call | flops 2147483648 | bytes 8388608 | tf_op jit(solution)/shard_map/query_back/pallas_call | solution.py:261
  437.2 3.6 collective-permute-done.54
  453.5 4.2 collective-permute-done.56
  460.6 4.2 collective-permute-done.59
  479.3 2.7 collective-permute-start.62
  497.6 2.9 collective-permute-done.63
  501.4 3.3 collective-permute-start.77
  (656 shorter events, 187.2 us)
Async XLA Ops:
  7.2 126.8 %all-gather.4.cloned.1.call-start = ((), (), s32[]{:S(2)}) async-start(), calls=%async_computation | async-start | bytes 38043648 | tf_op jit(solution)/shard_map/all_gather | solution.py:578
  10.8 198.6 %all-gather.6.cloned.1.call-start = ((), (), s32[]{:S(2)}) async-start(), calls=%async_computation.1 | async-start | bytes 17301504 | tf_op jit(solution)/shard_map/all_gather | solution.py:574
  12.3 16.3 %collective-permute-start.18 = (bf16[128,2048]{1,0:T(8,128)(2,1)S(1)}, bf16[128,2048]{1,0:T(8,128)(2,1)S(1)}, u32[]{:S(2)}, u32[]{:S(2)}) collective-permute-start(bf16[128,2048]{1,0:T(8,128)(2,1)S(1)} %broadcast_select_fusion.2), channel_id=1, source_target_pairs={{0,64},{64,0},{1,65},{65,1},{2,66},{66,2},{3,67},{67,3},{4,68},{68... | collective-permute-start | bytes 1572872 | tf_op jit(solution)/shard_map/ppermute | solution.py:540
  30.0 261.8 %all-gather.8.cloned.1.call-start = ((), (), s32[]{:S(2)}) async-start(), calls=%async_computation.2 | async-start | bytes 17301504 | tf_op jit(solution)/shard_map/all_gather | solution.py:574
  47.7 20.0 %collective-permute-start.1 = (bf16[16,8256]{1,0:T(8,128)(2,1)S(1)}, bf16[16,8256]{1,0:T(8,128)(2,1)S(1)}, u32[]{:S(2)}, u32[]{:S(2)}) collective-permute-start(bf16[16,8256]{1,0:T(8,128)(2,1)S(1)} %concatenate.208), channel_id=1, source_target_pairs={{0,64},{64,0},{1,65},{65,1},{2,66},{66,2},{3,67},{67,3},{4,68},{68... | collective-permute-start | bytes 792584 | tf_op jit(solution)/shard_map/ppermute | solution.py:540
  52.1 14.6 %collective-permute-start = (bf16[1,14592]{1,0:T(2,128)(2,1)S(1)}, bf16[1,14592]{1,0:T(2,128)(2,1)S(1)}, u32[]{:S(2)}, u32[]{:S(2)}) collective-permute-start(bf16[1,14592]{1,0:T(2,128)(2,1)S(1)} %constant_dynamic-update-slice_fusion), channel_id=1, source_target_pairs={{0,64},{64,0},{1,65},{65,1},{2,66},{66,2},{3,67},{67,3},{4,68},{68... | collective-permute-start | bytes 87560 | tf_op jit(solution)/shard_map/ppermute | solution.py:540
  67.8 8.8 %collective-permute-start.2 = (bf16[16,5696]{1,0:T(8,128)(2,1)S(1)}, bf16[16,5696]{1,0:T(8,128)(2,1)S(1)}, u32[]{:S(2)}, u32[]{:S(2)}) collective-permute-start(bf16[16,5696]{1,0:T(8,128)(2,1)S(1)} %get-tuple-element.249), channel_id=1, source_target_pairs={{0,1},{1,2},{2,3},{3,0},{4,5},{5,6},{6,7},{7,4},{8,9},{9,10},{10,1... | collective-permute-start | bytes 546824 | tf_op jit(solution)/shard_map/ppermute | solution.py:32
  69.2 9.4 %collective-permute-start.3 = (bf16[16,5696]{1,0:T(8,128)(2,1)S(1)}, bf16[16,5696]{1,0:T(8,128)(2,1)S(1)}, u32[]{:S(2)}, u32[]{:S(2)}) collective-permute-start(bf16[16,5696]{1,0:T(8,128)(2,1)S(1)} %get-tuple-element.249), channel_id=1, source_target_pairs={{0,2},{1,3},{2,0},{3,1},{4,6},{5,7},{6,4},{7,5},{8,10},{9,11},{10,... | collective-permute-start | bytes 546824 | tf_op jit(solution)/shard_map/ppermute | solution.py:32
  137.3 11.3 %collective-permute-start.5 = (bf16[64,256]{1,0:T(8,128)(2,1)S(1)}, bf16[64,256]{1,0:T(8,128)(2,1)S(1)}, u32[]{:S(2)}, u32[]{:S(2)}) collective-permute-start(bf16[64,256]{1,0:T(8,128)(2,1)S(1)} %fusion.20), channel_id=1, source_target_pairs={{0,16},{4,20},{8,24},{12,28},{16,32},{20,36},{24,40},{28,44},{32,4... | collective-permute-start | bytes 98312 | tf_op jit(solution)/shard_map/ppermute | solution.py:38
  149.4 9.2 %collective-permute-start.9 = (bf16[320,256]{1,0:T(8,128)(2,1)S(1)}, bf16[320,256]{1,0:T(8,128)(2,1)S(1)}, u32[]{:S(2)}, u32[]{:S(2)}) collective-permute-start(bf16[320,256]{1,0:T(8,128)(2,1)S(1)} %get-tuple-element.315), channel_id=1, source_target_pairs={{0,3},{1,0},{2,1},{3,2},{4,7},{5,4},{6,5},{7,6},{8,11},{9,8},{10,9... | collective-permute-start | bytes 491528 | tf_op jit(solution)/shard_map/ppermute | solution.py:32
  157.2 8.7 %collective-permute-start.11 = (bf16[320,256]{1,0:T(8,128)(2,1)S(1)}, bf16[320,256]{1,0:T(8,128)(2,1)S(1)}, u32[]{:S(2)}, u32[]{:S(2)}) collective-permute-start(bf16[320,256]{1,0:T(8,128)(2,1)S(1)} %get-tuple-element.315), channel_id=1, source_target_pairs={{0,1},{1,2},{2,3},{3,0},{4,5},{5,6},{6,7},{7,4},{8,9},{9,10},{10,1... | collective-permute-start | bytes 491528 | tf_op jit(solution)/shard_map/ppermute | solution.py:32
  177.0 9.2 %collective-permute-start.12 = (bf16[64,2048]{1,0:T(8,128)(2,1)S(1)}, bf16[64,2048]{1,0:T(8,128)(2,1)S(1)}, u32[]{:S(2)}, u32[]{:S(2)}) collective-permute-start(bf16[64,2048]{1,0:T(8,128)(2,1)S(1)} %add_convert_fusion.3), channel_id=1, source_target_pairs={{0,3},{1,0},{2,1},{3,2},{4,7},{5,4},{6,5},{7,6},{8,11},{9,8},{10,9... | collective-permute-start | bytes 786440 | tf_op jit(solution)/shard_map/ppermute | solution.py:32
  177.1 10.8 %collective-permute-start.13 = (bf16[64,2048]{1,0:T(8,128)(2,1)S(1)}, bf16[64,2048]{1,0:T(8,128)(2,1)S(1)}, u32[]{:S(2)}, u32[]{:S(2)}) collective-permute-start(bf16[64,2048]{1,0:T(8,128)(2,1)S(1)} %add_convert_fusion.3), channel_id=1, source_target_pairs={{0,2},{1,3},{2,0},{3,1},{4,6},{5,7},{6,4},{7,5},{8,10},{9,11},{10,... | collective-permute-start | bytes 786440 | tf_op jit(solution)/shard_map/ppermute | solution.py:32
  178.4 14.1 %collective-permute-start.14 = (bf16[64,2048]{1,0:T(8,128)(2,1)S(1)}, bf16[64,2048]{1,0:T(8,128)(2,1)S(1)}, u32[]{:S(2)}, u32[]{:S(2)}) collective-permute-start(bf16[64,2048]{1,0:T(8,128)(2,1)S(1)} %add_convert_fusion.3), channel_id=1, source_target_pairs={{0,1},{1,2},{2,3},{3,0},{4,5},{5,6},{6,7},{7,4},{8,9},{9,10},{10,1... | collective-permute-start | bytes 786440 | tf_op jit(solution)/shard_map/ppermute | solution.py:32
  192.7 9.2 %collective-permute-start.15 = (bf16[64,2048]{1,0:T(8,128)(2,1)S(1)}, bf16[64,2048]{1,0:T(8,128)(2,1)S(1)}, u32[]{:S(2)}, u32[]{:S(2)}) collective-permute-start(bf16[64,2048]{1,0:T(8,128)(2,1)S(1)} %dynamic-slice_bitcast_fusion), channel_id=1, source_target_pairs={{0,3},{1,0},{2,1},{3,2},{4,7},{5,4},{6,5},{7,6},{8,11},{9,8},{10,9... | collective-permute-start | bytes 786440 | tf_op jit(solution)/shard_map/ppermute | solution.py:32
  193.9 10.8 %collective-permute-start.16 = (bf16[64,2048]{1,0:T(8,128)(2,1)S(1)}, bf16[64,2048]{1,0:T(8,128)(2,1)S(1)}, u32[]{:S(2)}, u32[]{:S(2)}) collective-permute-start(bf16[64,2048]{1,0:T(8,128)(2,1)S(1)} %dynamic-slice_bitcast_fusion), channel_id=1, source_target_pairs={{0,2},{1,3},{2,0},{3,1},{4,6},{5,7},{6,4},{7,5},{8,10},{9,11},{10,... | collective-permute-start | bytes 786440 | tf_op jit(solution)/shard_map/ppermute | solution.py:32
  194.6 13.7 %collective-permute-start.17 = (bf16[64,2048]{1,0:T(8,128)(2,1)S(1)}, bf16[64,2048]{1,0:T(8,128)(2,1)S(1)}, u32[]{:S(2)}, u32[]{:S(2)}) collective-permute-start(bf16[64,2048]{1,0:T(8,128)(2,1)S(1)} %dynamic-slice_bitcast_fusion), channel_id=1, source_target_pairs={{0,1},{1,2},{2,3},{3,0},{4,5},{5,6},{6,7},{7,4},{8,9},{9,10},{10,1... | collective-permute-start | bytes 786440 | tf_op jit(solution)/shard_map/ppermute | solution.py:32
  220.4 9.6 %collective-permute-start.19 = (bf16[64,2048]{1,0:T(8,128)(2,1)S(1)}, bf16[64,2048]{1,0:T(8,128)(2,1)S(1)}, u32[]{:S(2)}, u32[]{:S(2)}) collective-permute-start(bf16[64,2048]{1,0:T(8,128)(2,1)S(1)} %get-tuple-element.147), channel_id=1, source_target_pairs={{0,1},{1,2},{2,3},{3,0},{4,5},{5,6},{6,7},{7,4},{8,9},{9,10},{10,1... | collective-permute-start | bytes 786440 | tf_op jit(solution)/shard_map/ppermute | solution.py:32
  221.4 14.7 %collective-permute-start.20 = (bf16[64,2048]{1,0:T(8,128)(2,1)S(1)}, bf16[64,2048]{1,0:T(8,128)(2,1)S(1)}, u32[]{:S(2)}, u32[]{:S(2)}) collective-permute-start(bf16[64,2048]{1,0:T(8,128)(2,1)S(1)} %get-tuple-element.149), channel_id=1, source_target_pairs={{0,2},{1,3},{2,0},{3,1},{4,6},{5,7},{6,4},{7,5},{8,10},{9,11},{10,... | collective-permute-start | bytes 786440 | tf_op jit(solution)/shard_map/ppermute | solution.py:32
  224.1 12.1 %collective-permute-start.21 = (bf16[64,2048]{1,0:T(8,128)(2,1)S(1)}, bf16[64,2048]{1,0:T(8,128)(2,1)S(1)}, u32[]{:S(2)}, u32[]{:S(2)}) collective-permute-start(bf16[64,2048]{1,0:T(8,128)(2,1)S(1)} %get-tuple-element.148), channel_id=1, source_target_pairs={{0,3},{1,0},{2,1},{3,2},{4,7},{5,4},{6,5},{7,6},{8,11},{9,8},{10,9... | collective-permute-start | bytes 786440 | tf_op jit(solution)/shard_map/ppermute | solution.py:32
  237.7 10.5 %collective-permute-start.22 = (bf16[64,256]{1,0:T(8,128)(2,1)S(1)}, bf16[64,256]{1,0:T(8,128)(2,1)S(1)}, u32[]{:S(2)}, u32[]{:S(2)}) collective-permute-start(bf16[64,256]{1,0:T(8,128)(2,1)S(1)} %fusion.21), channel_id=1, source_target_pairs={{0,16},{4,20},{8,24},{12,28},{16,32},{20,36},{24,40},{28,44},{32,4... | collective-permute-start | bytes 98312 | tf_op jit(solution)/shard_map/ppermute | solution.py:38
  249.0 10.0 %collective-permute-start.26 = (bf16[320,256]{1,0:T(8,128)(2,1)S(1)}, bf16[320,256]{1,0:T(8,128)(2,1)S(1)}, u32[]{:S(2)}, u32[]{:S(2)}) collective-permute-start(bf16[320,256]{1,0:T(8,128)(2,1)S(1)} %get-tuple-element.305), channel_id=1, source_target_pairs={{0,3},{1,0},{2,1},{3,2},{4,7},{5,4},{6,5},{7,6},{8,11},{9,8},{10,9... | collective-permute-start | bytes 491528 | tf_op jit(solution)/shard_map/ppermute | solution.py:32
  275.0 9.0 %collective-permute-start.29 = (bf16[64,2048]{1,0:T(8,128)(2,1)S(1)}, bf16[64,2048]{1,0:T(8,128)(2,1)S(1)}, u32[]{:S(2)}, u32[]{:S(2)}) collective-permute-start(bf16[64,2048]{1,0:T(8,128)(2,1)S(1)} %add_convert_fusion.1), channel_id=1, source_target_pairs={{0,3},{1,0},{2,1},{3,2},{4,7},{5,4},{6,5},{7,6},{8,11},{9,8},{10,9... | collective-permute-start | bytes 786440 | tf_op jit(solution)/shard_map/ppermute | solution.py:32
  275.4 10.8 %collective-permute-start.30 = (bf16[64,2048]{1,0:T(8,128)(2,1)S(1)}, bf16[64,2048]{1,0:T(8,128)(2,1)S(1)}, u32[]{:S(2)}, u32[]{:S(2)}) collective-permute-start(bf16[64,2048]{1,0:T(8,128)(2,1)S(1)} %add_convert_fusion.1), channel_id=1, source_target_pairs={{0,2},{1,3},{2,0},{3,1},{4,6},{5,7},{6,4},{7,5},{8,10},{9,11},{10,... | collective-permute-start | bytes 786440 | tf_op jit(solution)/shard_map/ppermute | solution.py:32
  277.4 14.3 %collective-permute-start.31 = (bf16[64,2048]{1,0:T(8,128)(2,1)S(1)}, bf16[64,2048]{1,0:T(8,128)(2,1)S(1)}, u32[]{:S(2)}, u32[]{:S(2)}) collective-permute-start(bf16[64,2048]{1,0:T(8,128)(2,1)S(1)} %add_convert_fusion.1), channel_id=1, source_target_pairs={{0,1},{1,2},{2,3},{3,0},{4,5},{5,6},{6,7},{7,4},{8,9},{9,10},{10,1... | collective-permute-start | bytes 786440 | tf_op jit(solution)/shard_map/ppermute | solution.py:32
  310.0 15.2 %collective-permute-start.32 = (bf16[64,2048]{1,0:T(8,128)(2,1)S(1)}, bf16[64,2048]{1,0:T(8,128)(2,1)S(1)}, u32[]{:S(2)}, u32[]{:S(2)}) collective-permute-start(bf16[64,2048]{1,0:T(8,128)(2,1)S(1)} %get-tuple-element.144), channel_id=1, source_target_pairs={{0,1},{1,2},{2,3},{3,0},{4,5},{5,6},{6,7},{7,4},{8,9},{9,10},{10,1... | collective-permute-start | bytes 786440 | tf_op jit(solution)/shard_map/ppermute | solution.py:32
  310.3 14.9 %collective-permute-start.33 = (bf16[64,2048]{1,0:T(8,128)(2,1)S(1)}, bf16[64,2048]{1,0:T(8,128)(2,1)S(1)}, u32[]{:S(2)}, u32[]{:S(2)}) collective-permute-start(bf16[64,2048]{1,0:T(8,128)(2,1)S(1)} %get-tuple-element.146), channel_id=1, source_target_pairs={{0,2},{1,3},{2,0},{3,1},{4,6},{5,7},{6,4},{7,5},{8,10},{9,11},{10,... | collective-permute-start | bytes 786440 | tf_op jit(solution)/shard_map/ppermute | solution.py:32
  312.1 13.6 %collective-permute-start.34 = (bf16[64,2048]{1,0:T(8,128)(2,1)S(1)}, bf16[64,2048]{1,0:T(8,128)(2,1)S(1)}, u32[]{:S(2)}, u32[]{:S(2)}) collective-permute-start(bf16[64,2048]{1,0:T(8,128)(2,1)S(1)} %get-tuple-element.145), channel_id=1, source_target_pairs={{0,3},{1,0},{2,1},{3,2},{4,7},{5,4},{6,5},{7,6},{8,11},{9,8},{10,9... | collective-permute-start | bytes 786440 | tf_op jit(solution)/shard_map/ppermute | solution.py:32
  334.6 11.4 %collective-permute-start.35 = (bf16[320,256]{1,0:T(8,128)(2,1)S(1)}, bf16[320,256]{1,0:T(8,128)(2,1)S(1)}, u32[]{:S(2)}, u32[]{:S(2)}) collective-permute-start(bf16[320,256]{1,0:T(8,128)(2,1)S(1)} %get-tuple-element.166), channel_id=1, source_target_pairs={{0,1},{1,2},{2,3},{3,0},{4,5},{5,6},{6,7},{7,4},{8,9},{9,10},{10,1... | collective-permute-start | bytes 491528 | tf_op jit(solution)/shard_map/ppermute | solution.py:32
  335.8 10.6 %collective-permute-start.36 = (bf16[320,256]{1,0:T(8,128)(2,1)S(1)}, bf16[320,256]{1,0:T(8,128)(2,1)S(1)}, u32[]{:S(2)}, u32[]{:S(2)}) collective-permute-start(bf16[320,256]{1,0:T(8,128)(2,1)S(1)} %get-tuple-element.168), channel_id=1, source_target_pairs={{0,2},{1,3},{2,0},{3,1},{4,6},{5,7},{6,4},{7,5},{8,10},{9,11},{10,... | collective-permute-start | bytes 491528 | tf_op jit(solution)/shard_map/ppermute | solution.py:32
  362.6 15.6 %collective-permute-start.42 = (bf16[64,2048]{1,0:T(8,128)(2,1)}, bf16[64,2048]{1,0:T(8,128)(2,1)}, u32[]{:S(2)}, u32[]{:S(2)}) collective-permute-start(bf16[64,2048]{1,0:T(8,128)(2,1)} %get-tuple-element.118), channel_id=1, source_target_pairs={{0,3},{1,0},{2,1},{3,2},{4,7},{5,4},{6,5},{7,6},{8,11},{9,8},{10,9... | collective-permute-start | bytes 786440 | tf_op jit(solution)/shard_map/ppermute | solution.py:32
  365.2 13.0 %collective-permute-start.43 = (bf16[64,2048]{1,0:T(8,128)(2,1)}, bf16[64,2048]{1,0:T(8,128)(2,1)}, u32[]{:S(2)}, u32[]{:S(2)}) collective-permute-start(bf16[64,2048]{1,0:T(8,128)(2,1)} %get-tuple-element.118), channel_id=1, source_target_pairs={{0,2},{1,3},{2,0},{3,1},{4,6},{5,7},{6,4},{7,5},{8,10},{9,11},{10,... | collective-permute-start | bytes 786440 | tf_op jit(solution)/shard_map/ppermute | solution.py:32
  366.1 13.7 %collective-permute-start.44 = (bf16[64,2048]{1,0:T(8,128)(2,1)}, bf16[64,2048]{1,0:T(8,128)(2,1)}, u32[]{:S(2)}, u32[]{:S(2)}) collective-permute-start(bf16[64,2048]{1,0:T(8,128)(2,1)} %get-tuple-element.118), channel_id=1, source_target_pairs={{0,1},{1,2},{2,3},{3,0},{4,5},{5,6},{6,7},{7,4},{8,9},{9,10},{10,1... | collective-permute-start | bytes 786440 | tf_op jit(solution)/shard_map/ppermute | solution.py:32
  391.3 15.1 %collective-permute-start.45 = (bf16[64,2048]{1,0:T(8,128)(2,1)S(1)}, bf16[64,2048]{1,0:T(8,128)(2,1)S(1)}, u32[]{:S(2)}, u32[]{:S(2)}) collective-permute-start(bf16[64,2048]{1,0:T(8,128)(2,1)S(1)} %get-tuple-element.141), channel_id=1, source_target_pairs={{0,1},{1,2},{2,3},{3,0},{4,5},{5,6},{6,7},{7,4},{8,9},{9,10},{10,1... | collective-permute-start | bytes 786440 | tf_op jit(solution)/shard_map/ppermute | solution.py:32
  392.2 14.2 %collective-permute-start.46 = (bf16[64,2048]{1,0:T(8,128)(2,1)S(1)}, bf16[64,2048]{1,0:T(8,128)(2,1)S(1)}, u32[]{:S(2)}, u32[]{:S(2)}) collective-permute-start(bf16[64,2048]{1,0:T(8,128)(2,1)S(1)} %get-tuple-element.143), channel_id=1, source_target_pairs={{0,2},{1,3},{2,0},{3,1},{4,6},{5,7},{6,4},{7,5},{8,10},{9,11},{10,... | collective-permute-start | bytes 786440 | tf_op jit(solution)/shard_map/ppermute | solution.py:32
  394.4 12.7 %collective-permute-start.47 = (bf16[64,2048]{1,0:T(8,128)(2,1)S(1)}, bf16[64,2048]{1,0:T(8,128)(2,1)S(1)}, u32[]{:S(2)}, u32[]{:S(2)}) collective-permute-start(bf16[64,2048]{1,0:T(8,128)(2,1)S(1)} %get-tuple-element.142), channel_id=1, source_target_pairs={{0,3},{1,0},{2,1},{3,2},{4,7},{5,4},{6,5},{7,6},{8,11},{9,8},{10,9... | collective-permute-start | bytes 786440 | tf_op jit(solution)/shard_map/ppermute | solution.py:32
  415.8 11.9 %collective-permute-start.48 = (bf16[320,256]{1,0:T(8,128)(2,1)S(1)}, bf16[320,256]{1,0:T(8,128)(2,1)S(1)}, u32[]{:S(2)}, u32[]{:S(2)}) collective-permute-start(bf16[320,256]{1,0:T(8,128)(2,1)S(1)} %get-tuple-element.163), channel_id=1, source_target_pairs={{0,1},{1,2},{2,3},{3,0},{4,5},{5,6},{6,7},{7,4},{8,9},{9,10},{10,1... | collective-permute-start | bytes 491528 | tf_op jit(solution)/shard_map/ppermute | solution.py:32
  417.0 10.7 %collective-permute-start.49 = (bf16[320,256]{1,0:T(8,128)(2,1)S(1)}, bf16[320,256]{1,0:T(8,128)(2,1)S(1)}, u32[]{:S(2)}, u32[]{:S(2)}) collective-permute-start(bf16[320,256]{1,0:T(8,128)(2,1)S(1)} %get-tuple-element.165), channel_id=1, source_target_pairs={{0,2},{1,3},{2,0},{3,1},{4,6},{5,7},{6,4},{7,5},{8,10},{9,11},{10,... | collective-permute-start | bytes 491528 | tf_op jit(solution)/shard_map/ppermute | solution.py:32
  431.8 9.0 %collective-permute-start.54 = (bf16[64,256]{1,0:T(8,128)(2,1)S(1)}, bf16[64,256]{1,0:T(8,128)(2,1)S(1)}, u32[]{:S(2)}, u32[]{:S(2)}) collective-permute-start(bf16[64,256]{1,0:T(8,128)(2,1)S(1)} %get-tuple-element.261), channel_id=1, source_target_pairs={{16,0},{20,4},{24,8},{28,12},{32,16},{36,20},{40,24},{44,28},{48,3... | collective-permute-start | bytes 98312 | tf_op jit(solution)/shard_map/ppermute | solution.py:38
  443.9 9.6 %collective-permute-start.55 = (bf16[2,29,16,128]{3,2,1,0:T(8,128)(2,1)S(1)}, bf16[2,29,16,128]{3,2,1,0:T(8,128)(2,1)S(1)}, u32[]{:S(2)}, u32[]{:S(2)}) collective-permute-start(bf16[2,29,16,128]{3,2,1,0:T(8,128)(2,1)S(1)} %get-tuple-element.150), channel_id=1, source_target_pairs={{0,1},{1,2},{2,3},{3,0},{4,5},{5,6},{6,7},{7,4},{8,9},{9,10},{10,1... | collective-permute-start | bytes 712712 | tf_op jit(solution)/shard_map/ppermute | solution.py:32
  445.8 11.8 %collective-permute-start.56 = (bf16[2,29,16,128]{3,2,1,0:T(8,128)(2,1)S(1)}, bf16[2,29,16,128]{3,2,1,0:T(8,128)(2,1)S(1)}, u32[]{:S(2)}, u32[]{:S(2)}) collective-permute-start(bf16[2,29,16,128]{3,2,1,0:T(8,128)(2,1)S(1)} %get-tuple-element.152), channel_id=1, source_target_pairs={{0,2},{1,3},{2,0},{3,1},{4,6},{5,7},{6,4},{7,5},{8,10},{9,11},{10,... | collective-permute-start | bytes 712712 | tf_op jit(solution)/shard_map/ppermute | solution.py:32
  447.6 10.3 %collective-permute-start.57 = (bf16[2,29,16,128]{3,2,1,0:T(8,128)(2,1)S(1)}, bf16[2,29,16,128]{3,2,1,0:T(8,128)(2,1)S(1)}, u32[]{:S(2)}, u32[]{:S(2)}) collective-permute-start(bf16[2,29,16,128]{3,2,1,0:T(8,128)(2,1)S(1)} %get-tuple-element.151), channel_id=1, source_target_pairs={{0,3},{1,0},{2,1},{3,2},{4,7},{5,4},{6,5},{7,6},{8,11},{9,8},{10,9... | collective-permute-start | bytes 712712 | tf_op jit(solution)/shard_map/ppermute | solution.py:32
  449.6 11.0 %collective-permute-start.65 = (bf16[64,2048]{1,0:T(8,128)(2,1)S(1)}, bf16[64,2048]{1,0:T(8,128)(2,1)S(1)}, u32[]{:S(2)}, u32[]{:S(2)}) collective-permute-start(bf16[64,2048]{1,0:T(8,128)(2,1)S(1)} %select_convert_fusion), channel_id=1, source_target_pairs={{0,64},{64,0},{1,65},{65,1},{2,66},{66,2},{3,67},{67,3},{4,68},{68... | collective-permute-start | bytes 786440 | tf_op jit(solution)/shard_map/ppermute | solution.py:540
  476.5 8.9 %collective-permute-start.69 = (bf16[4,16,128]{2,1,0:T(8,128)(2,1)S(1)}, bf16[4,16,128]{2,1,0:T(8,128)(2,1)S(1)}, u32[]{:S(2)}, u32[]{:S(2)}) collective-permute-start(bf16[4,16,128]{2,1,0:T(8,128)(2,1)S(1)} %bitcast.778), channel_id=1, source_target_pairs={{0,8},{4,12},{8,0},{12,4},{16,24},{20,28},{24,16},{28,20},{32,40},... | collective-permute-start | bytes 49160 | tf_op jit(solution)/shard_map/ppermute | solution.py:43
  477.8 19.7 %collective-permute-start.61 = (bf16[64,2048]{1,0:T(8,128)(2,1)S(1)}, bf16[64,2048]{1,0:T(8,128)(2,1)S(1)}, u32[]{:S(2)}, u32[]{:S(2)}) collective-permute-start(bf16[64,2048]{1,0:T(8,128)(2,1)S(1)} %get-tuple-element.138), channel_id=1, source_target_pairs={{0,1},{1,2},{2,3},{3,0},{4,5},{5,6},{6,7},{7,4},{8,9},{9,10},{10,1... | collective-permute-start | bytes 786440 | tf_op jit(solution)/shard_map/ppermute | solution.py:32
  479.3 18.2 %collective-permute-start.62 = (bf16[64,2048]{1,0:T(8,128)(2,1)S(1)}, bf16[64,2048]{1,0:T(8,128)(2,1)S(1)}, u32[]{:S(2)}, u32[]{:S(2)}) collective-permute-start(bf16[64,2048]{1,0:T(8,128)(2,1)S(1)} %get-tuple-element.140), channel_id=1, source_target_pairs={{0,2},{1,3},{2,0},{3,1},{4,6},{5,7},{6,4},{7,5},{8,10},{9,11},{10,... | collective-permute-start | bytes 786440 | tf_op jit(solution)/shard_map/ppermute | solution.py:32
  501.3 9.3 %collective-permute-start.76 = (bf16[2,21,16,128]{3,2,1,0:T(8,128)(2,1)S(1)}, bf16[2,21,16,128]{3,2,1,0:T(8,128)(2,1)S(1)}, u32[]{:S(2)}, u32[]{:S(2)}) collective-permute-start(bf16[2,21,16,128]{3,2,1,0:T(8,128)(2,1)S(1)} %get-tuple-element.178), channel_id=1, source_target_pairs={{0,1},{1,2},{2,3},{3,0},{4,5},{5,6},{6,7},{7,4},{8,9},{9,10},{10,1... | collective-permute-start | bytes 516104 | tf_op jit(solution)/shard_map/ppermute | solution.py:32
  501.4 9.3 %collective-permute-start.77 = (bf16[2,21,16,128]{3,2,1,0:T(8,128)(2,1)S(1)}, bf16[2,21,16,128]{3,2,1,0:T(8,128)(2,1)S(1)}, u32[]{:S(2)}, u32[]{:S(2)}) collective-permute-start(bf16[2,21,16,128]{3,2,1,0:T(8,128)(2,1)S(1)} %get-tuple-element.178), channel_id=1, source_target_pairs={{0,2},{1,3},{2,0},{3,1},{4,6},{5,7},{6,4},{7,5},{8,10},{9,11},{10,... | collective-permute-start | bytes 516104 | tf_op jit(solution)/shard_map/ppermute | solution.py:32
  (164 other events, 2780.4 us)
Sparse Core Ops, SparseCore 0:
  11.6 122.3 all-gather.3
  136.9 71.9 all-gather.5
  211.7 72.0 all-gather.7

commit v17 on v16

--- a/solution.py
+++ b/solution.py
@@ -420,7 +420,7 @@
 
 def feed_both_kernel(
     second_ref, branch_ref, table_ref, bias_ref, pack_ref,
-    active_ref, low_u_ref, low_d_ref, out_ref, grad_up_ref, inner_d_ref, inner_u_ref, back_ref,
+    active_ref, low_u_ref, grad_up_ref, inner_d_ref, inner_u_ref, back_ref,
     buf, sems, pack_buf, branch_buf, own_sems,
 ):
     _, count, chunks, rows, tile = buf.shape
@@ -450,13 +450,29 @@
         grad_up_ref[:, columns] = (grad * slope).astype(bf16)
     inner_u = against(grad_up_ref[...], eu_ref[...]).astype(bf16)
     inner_u_ref[...] = inner_u
-    low_d = against(active_ref[...], sd_ref[...]).astype(bf16)
-    low_d_ref[...] = low_d
     for i in range(chunks):
         columns = pl.ds(i * rows, rows)
         back_ref[:, columns] = (
             against_chunk(grad_up_ref, buf, 0, i) + plain(inner_u, su_ref[:, columns])
         ).astype(bf16)
+
+
+def feed_down_kernel(
+    active_ref, table_ref, pack_ref, low_d_ref, out_ref, buf, sems, pack_buf, own_sems
+):
+    _, count, chunks, rows, tile = buf.shape
+    _, _, sd_ref, ed_ref = feed_pack(pack_buf, chunks * rows, count * tile)
+    copies = feed_copies(table_ref, buf, sems)
+    own = own_copies([pack_ref], [pack_buf], own_sems)
+    for _, down in copies:
+        down.start()
+    own[0].wait()
+    low_d = against(active_ref[...], sd_ref[...]).astype(bf16)
+    low_d_ref[...] = low_d
+    for _, down in copies:
+        down.wait()
+    for i in range(chunks):
+        columns = pl.ds(i * rows, rows)
         out_ref[:, columns] = (
             against_chunk(active_ref, buf, 1, i) + plain(low_d, ed_ref[:, columns])
         ).astype(bf16)
@@ -886,14 +902,23 @@
 
     middle_one, kept_one = forward_attend(1, passed.astype(f32))
     unit_one, rsd_one, second_one, up_bias = feed_inputs(1, middle_one)
-    active, low_u, low_d, partial, grad_up, inner_d, inner_u, partial_back = feed_call(
+    active, low_u, grad_up, inner_d, inner_u, partial_back = feed_call(
         feed_both_kernel,
         "feed_both",
         (second_one, branch_one, feed_tables[1], up_bias, feed_packs[1]),
         (4, 1),
-        (local_f, rank, rank, width, local_f, rank, rank, width),
+        (local_f, rank, local_f, rank, rank, width),
         local_f,
-        4,
+        3,
+    )
+    low_d, partial = feed_call(
+        feed_down_kernel,
+        "feed_down",
+        (active, feed_tables[1], feed_packs[1]),
+        (2,),
+        (rank, width),
+        local_f,
+        1,
     )
     grad_middle = feed_grads(1, given, unit_one, rsd_one, partial_back)
     shared, owned = feed_adapters(

time: 532 us -> 536 us (level)
    pallas_call x3 -> x4, Pallas kernels: 35.4 us -> 39.2 us  [feed_call(): pl.pallas_call(kernel, in_specs=[remote if value.ndim == 4 or i in copied...]
    unnamed x300 -> x302, local copies, waits for them, and re-layouts: 14.9 us -> 14.9 us
  transfers between devices with their start and end apart: 82 -> 82, of which waited for: 52 -> 53; matrix products, arithmetic and copies ran while one was open for 11% -> 11% of each run, Pallas kernels for 10% -> 10%
where the time goes in v17:
time: 536 us; the launch traced here: 527 us
  waiting for transfers between devices  205 us (38%)
  starting transfers between devices  124 us (23%)
  Pallas kernels  96.6 us (18%)
  local copies, waits for them, and re-layouts  38.9 us (7%)
  other arithmetic  29.2 us (5%)
  between operations  21.1 us (4%)
  matrix products  11.8 us (2%)
    ppermute x45, waiting for transfers between devices, around(): lax.ppermute(block, axis, [(i, (i + distance) % size) for i in range(size)])  96.8 us
    ppermute x45, starting transfers between devices, around(): lax.ppermute(block, axis, [(i, (i + distance) % size) for i in range(size)])  64.5 us
    all_gather x1, waiting for transfers between devices, gather_all(): lax.all_gather(row_major(shard), every, axis=0, tiled=True, axis_index_gr...  52.7 us
    pallas_call x4, Pallas kernels, feed_call(): pl.pallas_call(kernel, in_specs=[remote if value.ndim == 4 or i in copied...  39.2 us
    ppermute x16, starting transfers between devices, along(): return lax.ppermute(block, axis, route)  32.1 us
    ppermute x5, waiting for transfers between devices, swap(): return lax.ppermute(value, 'section', sides)  26.3 us
    pallas_call x2, Pallas kernels, attend(): pl.pallas_call(lambda *refs: attend_kernel(layer, head, *refs), in_specs=...  19.9 us
    pallas_call x2, Pallas kernels, attend_back(): pl.pallas_call(lambda *refs: attend_back_kernel(layer, head, *refs), in_s...  16.1 us
  transfers between devices with their start and end apart: 82, of which 53 were waited for; matrix products, arithmetic and copies ran while one was open for 11% of the time, Pallas kernels for 10%

profile of v17, /device:TPU:0, one launch (start us, length us, event | category | flops | bytes accessed | tf_op | source)
XLA Modules:
  0.0 527.1 jit_solution(14947722770674163080)
XLA Ops:
  12.3 4.0 collective-permute-start.18
  16.4 12.2 %collective-permute-done.18 = bf16[128,2048]{1,0:T(8,128)(2,1)S(1)} collective-permute-done((bf16[128,2048]{1,0:T(8,128)(2,1)S(1)}, bf16[128,2048]{1,0:T(8,128)(2,1)S(1)}, u32[]{:S(2)}, u32[]{:S(2)}) %collective-permute-start.18) | collective-permute-done | bytes 524320 | tf_op jit(solution)/shard_map/ppermute | solution.py:556
  47.7 4.2 collective-permute-start.1
  54.4 12.3 %collective-permute-done = bf16[1,14592]{1,0:T(2,128)(2,1)S(1)} collective-permute-done((bf16[1,14592]{1,0:T(2,128)(2,1)S(1)}, bf16[1,14592]{1,0:T(2,128)(2,1)S(1)}, u32[]{:S(2)}, u32[]{:S(2)}) %collective-permute-start) | collective-permute-done | bytes 29216 | tf_op jit(solution)/shard_map/ppermute | solution.py:556
  69.2 2.7 collective-permute-start.3
  81.3 52.7 %all-gather.4.cloned.1.call-done = bf16[16384,1152]{1,0:T(8,128)(2,1)} async-done(((bf16[128,1152]{1,0:T(8,128)(2,1)}), bf16[16384,1152]{1,0:T(8,128)(2,1)}) %all-gather.4.cloned.1.call-update) | async-done | bytes 37748752 | tf_op jit(solution)/shard_map/all_gather | solution.py:594
  134.0 2.8 fusion.137
  137.3 3.4 collective-permute-start.5
  143.0 4.1 collective-permute-start.7
  152.8 4.4 project_queries.2
  160.2 5.7 %collective-permute-done.11 = bf16[320,256]{1,0:T(8,128)(2,1)S(1)} collective-permute-done((bf16[320,256]{1,0:T(8,128)(2,1)S(1)}, bf16[320,256]{1,0:T(8,128)(2,1)S(1)}, u32[]{:S(2)}, u32[]{:S(2)}) %collective-permute-start.11) | collective-permute-done | bytes 163872 | tf_op jit(solution)/shard_map/ppermute | solution.py:32
  166.0 10.3 %attend.2 = (bf16[4,256,1280]{2,1,0:T(8,128)(2,1)S(1)}, bf16[64,2048]{1,0:T(8,128)(2,1)S(1)}, bf16[64,16]{1,0:T(8,128)(2,1)S(1)}, f32[64,2048]{1,0:T(8,128)S(1)}) custom-call(bf16[64,2048]{1,0:T(8,128)(2,1)S(1)} %get-tuple-element.57.refs_0_.refs_5_, bf16[1280,256]{1,0:T(8,128)(2,1)S(1)} %constant_dynamic-update-slice_fusion.26.refs_1_.refs_6_, ...), custom_call_target="tpu_custom_call" | custom-call | flops 2818572288 | bytes 8388608 | tf_op jit(solution)/shard_map/attend/pallas_call | solution.py:180
  181.5 4.8 collective-permute-done.12
  187.9 4.7 collective-permute-done.14
  195.6 6.3 %collective-permute-done.15 = bf16[64,2048]{1,0:T(8,128)(2,1)S(1)} collective-permute-done((bf16[64,2048]{1,0:T(8,128)(2,1)S(1)}, bf16[64,2048]{1,0:T(8,128)(2,1)S(1)}, u32[]{:S(2)}, u32[]{:S(2)}) %collective-permute-start.15) | collective-permute-done | bytes 262176 | tf_op jit(solution)/shard_map/ppermute | solution.py:32
  201.9 2.7 collective-permute-done.16
  204.6 3.7 collective-permute-done.17
  209.4 10.8 %feed.1 = (bf16[256,2048]{1,0:T(8,128)(2,1)S(1)}, bf16[256,2048]{1,0:T(8,128)(2,1)S(1)}, bf16[256,16]{1,0:T(8,128)(2,1)S(1)}, bf16[256,16]{1,0:T(8,128)(2,1)S(1)}, bf16[256,2048]{1,0:T(8,128)(2,1)S(1)}) custom-call(bf16[256,2048]{1,0:T(8,128)(2,1)S(1)} %pad_maximum_fusion.1.second_ref, bf16[4,2,512,2048]{3,2,1,0:T(8,128)(2,1)} %bitcast.700, ...), custom_call_target="tpu_custom_call" | custom-call | flops 4294967296 | bytes 16777216 | tf_op jit(solution)/shard_map/feed/pallas_call | solution.py:486
  221.4 2.7 collective-permute-start.20
  226.2 3.8 collective-permute-done.19
  230.0 6.1 %collective-permute-done.20 = bf16[64,2048]{1,0:T(8,128)(2,1)S(1)} collective-permute-done((bf16[64,2048]{1,0:T(8,128)(2,1)S(1)}, bf16[64,2048]{1,0:T(8,128)(2,1)S(1)}, u32[]{:S(2)}, u32[]{:S(2)}) %collective-permute-start.20) | collective-permute-done | bytes 262176 | tf_op jit(solution)/shard_map/ppermute | solution.py:32
  237.7 3.4 collective-permute-start.22
  242.4 4.2 collective-permute-start.24
  249.0 2.9 collective-permute-start.26
  252.5 4.4 project_queries.3
  259.8 4.9 collective-permute-done.28
  264.8 9.5 %attend.3 = (bf16[4,256,1280]{2,1,0:T(8,128)(2,1)S(1)}, bf16[64,2048]{1,0:T(8,128)(2,1)S(1)}, bf16[64,16]{1,0:T(8,128)(2,1)S(1)}, f32[64,2048]{1,0:T(8,128)S(1)}) custom-call(bf16[64,2048]{1,0:T(8,128)(2,1)S(1)} %get-tuple-element.63.refs_0_.refs_5_, bf16[1280,256]{1,0:T(8,128)(2,1)S(1)} %constant_dynamic-update-slice_fusion.39.refs_1_.refs_6_, ...), custom_call_target="tpu_custom_call" | custom-call | flops 2818572288 | bytes 8388608 | tf_op jit(solution)/shard_map/attend/pallas_call | solution.py:180
  279.4 4.7 collective-permute-done.29
  286.2 5.5 %collective-permute-done.31 = bf16[64,2048]{1,0:T(8,128)(2,1)S(1)} collective-permute-done((bf16[64,2048]{1,0:T(8,128)(2,1)S(1)}, bf16[64,2048]{1,0:T(8,128)(2,1)S(1)}, u32[]{:S(2)}, u32[]{:S(2)}) %collective-permute-start.31) | collective-permute-done | bytes 262176 | tf_op jit(solution)/shard_map/ppermute | solution.py:32
  293.5 12.1 %feed_both.1 = (bf16[256,2048]{1,0:T(8,128)(2,1)S(1)}, bf16[256,16]{1,0:T(8,128)(2,1)S(1)}, bf16[256,2048]{1,0:T(8,128)(2,1)S(1)}, bf16[256,16]{1,0:T(8,128)(2,1...) custom-call(bf16[256,2048]{1,0:T(8,128)(2,1)S(1)} %pad_maximum_fusion.4.second_ref, ...), custom_call_target="tpu_custom_call" | custom-call | flops 6442450944 | bytes 16777216 | tf_op jit(solution)/shard_map/feed_both/pallas_call | solution.py:486
  306.5 6.3 %feed_down.1 = (bf16[256,16]{1,0:T(8,128)(2,1)S(1)}, bf16[256,2048]{1,0:T(8,128)(2,1)S(1)}) custom-call(bf16[256,2048]{1,0:T(8,128)(2,1)S(1)} %get-tuple-element.84.active_ref, bf16[4,2,512,2048]{3,2,1,0:T(8,128)(2,1)} %bitcast.703, bf16[16,8192]{1,0:T(8,128)(2,1)S(1)} %copy-done.17), custom_call_target="tpu_custom_call" | custom-call | flops 2147483648 | bytes 16777216 | tf_op jit(solution)/shard_map/feed_down/pallas_call | solution.py:486
  320.1 8.8 %collective-permute-done.32 = bf16[64,2048]{1,0:T(8,128)(2,1)S(1)} collective-permute-done((bf16[64,2048]{1,0:T(8,128)(2,1)S(1)}, bf16[64,2048]{1,0:T(8,128)(2,1)S(1)}, u32[]{:S(2)}, u32[]{:S(2)}) %collective-permute-start.32) | collective-permute-done | bytes 262176 | tf_op jit(solution)/shard_map/ppermute | solution.py:32
  330.4 8.1 %attend_back.2 = (bf16[64,2048]{1,0:T(8,128)(2,1)S(1)}, bf16[1280,256]{1,0:T(8,128)(2,1)S(1)}, bf16[64,16]{1,0:T(8,128)(2,1)S(1)}) custom-call(bf16[64,2048]{1,0:T(8,128)(2,1)S(1)} %get-tuple-element.123.refs_0_, bf16[4,4,2,512,1152]{4,3,2,1,0:T(8,128)(2,1)} %bitcast.696, bf16[16,2048]{1,0:T(8,128)(2,1)S(1)} %copy-done.25, bf16[16,2048]{1,0:T(8,128)(2,1)S(1)} %copy-done.35, ...), custom_call_target="tpu_custom_call" | custom-call | flops 3489660928 | bytes 13631488 | tf_op jit(solution)/shard_map/attend_back/pallas_call | solution.py:284
  339.5 3.1 collective-permute-start.36
  342.8 6.3 %query_back.2 = (bf16[64,16]{1,0:T(8,128)(2,1)S(1)}, f32[64,2048]{1,0:T(8,128)S(1)}) custom-call(bf16[64,2048]{1,0:T(8,128)(2,1)S(1)} %get-tuple-element.68.refs_0_, bf16[4,4,2,512,1152]{4,3,2,1,0:T(8,128)(2,1)} %bitcast.697, bf16[16,2048]{1,0:T(8,128)(2,1)S(1)} %copy-done.27, bf16[16,2048]{1,0:T(8,128)(2,1)S(1)} %copy-done.33), custom_call_target="tpu_custom_call" | custom-call | flops 2147483648 | bytes 8388608 | tf_op jit(solution)/shard_map/query_back/pallas_call | solution.py:261
  359.7 2.9 collective-permute-done.41
  366.4 2.6 collective-permute-start.42
  373.0 7.9 %concatenate.239 = bf16[84,16,128]{2,0,1:T(8,128)(2,1)} concatenate(bf16[16,16,128]{2,0,1:T(8,128)(2,1)} %bitcast.748, bf16[16,16,128]{2,0,1:T(8,128)(2,1)} %bitcast.747, bf16[16,16,128]{2,0,1:T(8,128)(2,1)} %bitcast.750, bf16[16,16,128]{2,0,1:T(8,128)(2,1)} %bitcast.749, bf16[16,16,128]{2,0,1:T(8,128)(2,1)S(1)} %bitcast.751, bf16[2,16,128]{2,0,1:T(2,128)(2,1)} %bitcast.793, ...), dimensions={0} | concatenate | bytes 688128 | tf_op jit(solution)/shard_map/concatenate | solution.py:777
  385.0 10.0 %feed_back.1 = (bf16[256,2048]{1,0:T(8,128)(2,1)S(1)}, bf16[256,16]{1,0:T(8,128)(2,1)S(1)}, bf16[256,16]{1,0:T(8,128)(2,1)S(1)}, bf16[256,2048]{1,0:T(8,128)(2,1)S(1)}) custom-call(bf16[256,2048]{1,0:T(8,128)(2,1)S(1)} %pad_maximum_fusion.5.branch_ref, bf16[4,2,512,2048]{3,2,1,0:T(8,128)(2,1)} %bitcast.701, bf16[256,2048]{1,0:T(8,128)(2,1)S(1)} %copy-done.19, ...), custom_call_target="tpu_custom_call" | custom-call | flops 4294967296 | bytes 16777216 | tf_op jit(solution)/shard_map/feed_back/pallas_call | solution.py:486
  401.2 9.0 %collective-permute-done.45 = bf16[64,2048]{1,0:T(8,128)(2,1)S(1)} collective-permute-done((bf16[64,2048]{1,0:T(8,128)(2,1)S(1)}, bf16[64,2048]{1,0:T(8,128)(2,1)S(1)}, u32[]{:S(2)}, u32[]{:S(2)}) %collective-permute-start.45) | collective-permute-done | bytes 262176 | tf_op jit(solution)/shard_map/ppermute | solution.py:32
  411.5 8.1 %attend_back.3 = (bf16[64,2048]{1,0:T(8,128)(2,1)S(1)}, bf16[1280,256]{1,0:T(8,128)(2,1)S(1)}, bf16[64,16]{1,0:T(8,128)(2,1)S(1)}) custom-call(bf16[64,2048]{1,0:T(8,128)(2,1)S(1)} %get-tuple-element.115.refs_0_, bf16[4,4,2,512,1152]{4,3,2,1,0:T(8,128)(2,1)} %bitcast.698, bf16[16,2048]{1,0:T(8,128)(2,1)S(1)} %get-tuple-element.272.refs_4_.refs_2_, ...), custom_call_target="tpu_custom_call" | custom-call | flops 3489660928 | bytes 13631488 | tf_op jit(solution)/shard_map/attend_back/pallas_call | solution.py:284
  420.8 3.0 collective-permute-start.49
  424.1 6.4 %query_back.3 = (bf16[64,16]{1,0:T(8,128)(2,1)S(1)}, f32[64,2048]{1,0:T(8,128)S(1)}) custom-call(bf16[64,2048]{1,0:T(8,128)(2,1)S(1)} %get-tuple-element.77.refs_0_, bf16[4,4,2,512,1152]{4,3,2,1,0:T(8,128)(2,1)} %bitcast.699, bf16[16,2048]{1,0:T(8,128)(2,1)S(1)} %get-tuple-element.274.refs_3_.refs_2_, bf16[16,2048]{1,0:T(8,128)(2,1)S(1)} %copy-done.29), custom_call_target="tpu_custom_call" | custom-call | flops 2147483648 | bytes 8388608 | tf_op jit(solution)/shard_map/query_back/pallas_call | solution.py:261
  441.0 3.6 collective-permute-done.54
  457.3 4.2 collective-permute-done.56
  464.4 4.2 collective-permute-done.59
  501.1 2.9 collective-permute-done.63
  505.0 3.3 collective-permute-start.77
  (659 shorter events, 189.4 us)
Async XLA Ops:
  7.2 126.8 %all-gather.4.cloned.1.call-start = ((), (), s32[]{:S(2)}) async-start(), calls=%async_computation | async-start | bytes 38043648 | tf_op jit(solution)/shard_map/all_gather | solution.py:594
  10.8 198.6 %all-gather.6.cloned.1.call-start = ((), (), s32[]{:S(2)}) async-start(), calls=%async_computation.1 | async-start | bytes 17301504 | tf_op jit(solution)/shard_map/all_gather | solution.py:590
  12.3 16.3 %collective-permute-start.18 = (bf16[128,2048]{1,0:T(8,128)(2,1)S(1)}, bf16[128,2048]{1,0:T(8,128)(2,1)S(1)}, u32[]{:S(2)}, u32[]{:S(2)}) collective-permute-start(bf16[128,2048]{1,0:T(8,128)(2,1)S(1)} %broadcast_select_fusion.2), channel_id=1, source_target_pairs={{0,64},{64,0},{1,65},{65,1},{2,66},{66,2},{3,67},{67,3},{4,68},{68... | collective-permute-start | bytes 1572872 | tf_op jit(solution)/shard_map/ppermute | solution.py:556
  30.0 261.8 %all-gather.8.cloned.1.call-start = ((), (), s32[]{:S(2)}) async-start(), calls=%async_computation.2 | async-start | bytes 17301504 | tf_op jit(solution)/shard_map/all_gather | solution.py:590
  47.7 20.0 %collective-permute-start.1 = (bf16[16,8256]{1,0:T(8,128)(2,1)S(1)}, bf16[16,8256]{1,0:T(8,128)(2,1)S(1)}, u32[]{:S(2)}, u32[]{:S(2)}) collective-permute-start(bf16[16,8256]{1,0:T(8,128)(2,1)S(1)} %concatenate.208), channel_id=1, source_target_pairs={{0,64},{64,0},{1,65},{65,1},{2,66},{66,2},{3,67},{67,3},{4,68},{68... | collective-permute-start | bytes 792584 | tf_op jit(solution)/shard_map/ppermute | solution.py:556
  52.1 14.6 %collective-permute-start = (bf16[1,14592]{1,0:T(2,128)(2,1)S(1)}, bf16[1,14592]{1,0:T(2,128)(2,1)S(1)}, u32[]{:S(2)}, u32[]{:S(2)}) collective-permute-start(bf16[1,14592]{1,0:T(2,128)(2,1)S(1)} %constant_dynamic-update-slice_fusion), channel_id=1, source_target_pairs={{0,64},{64,0},{1,65},{65,1},{2,66},{66,2},{3,67},{67,3},{4,68},{68... | collective-permute-start | bytes 87560 | tf_op jit(solution)/shard_map/ppermute | solution.py:556
  67.8 8.8 %collective-permute-start.2 = (bf16[16,5696]{1,0:T(8,128)(2,1)S(1)}, bf16[16,5696]{1,0:T(8,128)(2,1)S(1)}, u32[]{:S(2)}, u32[]{:S(2)}) collective-permute-start(bf16[16,5696]{1,0:T(8,128)(2,1)S(1)} %get-tuple-element.249), channel_id=1, source_target_pairs={{0,1},{1,2},{2,3},{3,0},{4,5},{5,6},{6,7},{7,4},{8,9},{9,10},{10,1... | collective-permute-start | bytes 546824 | tf_op jit(solution)/shard_map/ppermute | solution.py:32
  69.2 9.4 %collective-permute-start.3 = (bf16[16,5696]{1,0:T(8,128)(2,1)S(1)}, bf16[16,5696]{1,0:T(8,128)(2,1)S(1)}, u32[]{:S(2)}, u32[]{:S(2)}) collective-permute-start(bf16[16,5696]{1,0:T(8,128)(2,1)S(1)} %get-tuple-element.249), channel_id=1, source_target_pairs={{0,2},{1,3},{2,0},{3,1},{4,6},{5,7},{6,4},{7,5},{8,10},{9,11},{10,... | collective-permute-start | bytes 546824 | tf_op jit(solution)/shard_map/ppermute | solution.py:32
  137.3 11.3 %collective-permute-start.5 = (bf16[64,256]{1,0:T(8,128)(2,1)S(1)}, bf16[64,256]{1,0:T(8,128)(2,1)S(1)}, u32[]{:S(2)}, u32[]{:S(2)}) collective-permute-start(bf16[64,256]{1,0:T(8,128)(2,1)S(1)} %fusion.20), channel_id=1, source_target_pairs={{0,16},{4,20},{8,24},{12,28},{16,32},{20,36},{24,40},{28,44},{32,4... | collective-permute-start | bytes 98312 | tf_op jit(solution)/shard_map/ppermute | solution.py:38
  149.4 9.2 %collective-permute-start.9 = (bf16[320,256]{1,0:T(8,128)(2,1)S(1)}, bf16[320,256]{1,0:T(8,128)(2,1)S(1)}, u32[]{:S(2)}, u32[]{:S(2)}) collective-permute-start(bf16[320,256]{1,0:T(8,128)(2,1)S(1)} %get-tuple-element.315), channel_id=1, source_target_pairs={{0,3},{1,0},{2,1},{3,2},{4,7},{5,4},{6,5},{7,6},{8,11},{9,8},{10,9... | collective-permute-start | bytes 491528 | tf_op jit(solution)/shard_map/ppermute | solution.py:32
  157.2 8.7 %collective-permute-start.11 = (bf16[320,256]{1,0:T(8,128)(2,1)S(1)}, bf16[320,256]{1,0:T(8,128)(2,1)S(1)}, u32[]{:S(2)}, u32[]{:S(2)}) collective-permute-start(bf16[320,256]{1,0:T(8,128)(2,1)S(1)} %get-tuple-element.315), channel_id=1, source_target_pairs={{0,1},{1,2},{2,3},{3,0},{4,5},{5,6},{6,7},{7,4},{8,9},{9,10},{10,1... | collective-permute-start | bytes 491528 | tf_op jit(solution)/shard_map/ppermute | solution.py:32
  177.0 9.2 %collective-permute-start.12 = (bf16[64,2048]{1,0:T(8,128)(2,1)S(1)}, bf16[64,2048]{1,0:T(8,128)(2,1)S(1)}, u32[]{:S(2)}, u32[]{:S(2)}) collective-permute-start(bf16[64,2048]{1,0:T(8,128)(2,1)S(1)} %add_convert_fusion.3), channel_id=1, source_target_pairs={{0,3},{1,0},{2,1},{3,2},{4,7},{5,4},{6,5},{7,6},{8,11},{9,8},{10,9... | collective-permute-start | bytes 786440 | tf_op jit(solution)/shard_map/ppermute | solution.py:32
  177.1 10.8 %collective-permute-start.13 = (bf16[64,2048]{1,0:T(8,128)(2,1)S(1)}, bf16[64,2048]{1,0:T(8,128)(2,1)S(1)}, u32[]{:S(2)}, u32[]{:S(2)}) collective-permute-start(bf16[64,2048]{1,0:T(8,128)(2,1)S(1)} %add_convert_fusion.3), channel_id=1, source_target_pairs={{0,2},{1,3},{2,0},{3,1},{4,6},{5,7},{6,4},{7,5},{8,10},{9,11},{10,... | collective-permute-start | bytes 786440 | tf_op jit(solution)/shard_map/ppermute | solution.py:32
  178.5 14.1 %collective-permute-start.14 = (bf16[64,2048]{1,0:T(8,128)(2,1)S(1)}, bf16[64,2048]{1,0:T(8,128)(2,1)S(1)}, u32[]{:S(2)}, u32[]{:S(2)}) collective-permute-start(bf16[64,2048]{1,0:T(8,128)(2,1)S(1)} %add_convert_fusion.3), channel_id=1, source_target_pairs={{0,1},{1,2},{2,3},{3,0},{4,5},{5,6},{6,7},{7,4},{8,9},{9,10},{10,1... | collective-permute-start | bytes 786440 | tf_op jit(solution)/shard_map/ppermute | solution.py:32
  192.7 9.2 %collective-permute-start.15 = (bf16[64,2048]{1,0:T(8,128)(2,1)S(1)}, bf16[64,2048]{1,0:T(8,128)(2,1)S(1)}, u32[]{:S(2)}, u32[]{:S(2)}) collective-permute-start(bf16[64,2048]{1,0:T(8,128)(2,1)S(1)} %dynamic-slice_bitcast_fusion), channel_id=1, source_target_pairs={{0,3},{1,0},{2,1},{3,2},{4,7},{5,4},{6,5},{7,6},{8,11},{9,8},{10,9... | collective-permute-start | bytes 786440 | tf_op jit(solution)/shard_map/ppermute | solution.py:32
  193.8 10.8 %collective-permute-start.16 = (bf16[64,2048]{1,0:T(8,128)(2,1)S(1)}, bf16[64,2048]{1,0:T(8,128)(2,1)S(1)}, u32[]{:S(2)}, u32[]{:S(2)}) collective-permute-start(bf16[64,2048]{1,0:T(8,128)(2,1)S(1)} %dynamic-slice_bitcast_fusion), channel_id=1, source_target_pairs={{0,2},{1,3},{2,0},{3,1},{4,6},{5,7},{6,4},{7,5},{8,10},{9,11},{10,... | collective-permute-start | bytes 786440 | tf_op jit(solution)/shard_map/ppermute | solution.py:32
  194.6 13.7 %collective-permute-start.17 = (bf16[64,2048]{1,0:T(8,128)(2,1)S(1)}, bf16[64,2048]{1,0:T(8,128)(2,1)S(1)}, u32[]{:S(2)}, u32[]{:S(2)}) collective-permute-start(bf16[64,2048]{1,0:T(8,128)(2,1)S(1)} %dynamic-slice_bitcast_fusion), channel_id=1, source_target_pairs={{0,1},{1,2},{2,3},{3,0},{4,5},{5,6},{6,7},{7,4},{8,9},{9,10},{10,1... | collective-permute-start | bytes 786440 | tf_op jit(solution)/shard_map/ppermute | solution.py:32
  220.4 9.6 %collective-permute-start.19 = (bf16[64,2048]{1,0:T(8,128)(2,1)S(1)}, bf16[64,2048]{1,0:T(8,128)(2,1)S(1)}, u32[]{:S(2)}, u32[]{:S(2)}) collective-permute-start(bf16[64,2048]{1,0:T(8,128)(2,1)S(1)} %get-tuple-element.147), channel_id=1, source_target_pairs={{0,1},{1,2},{2,3},{3,0},{4,5},{5,6},{6,7},{7,4},{8,9},{9,10},{10,1... | collective-permute-start | bytes 786440 | tf_op jit(solution)/shard_map/ppermute | solution.py:32
  221.4 14.7 %collective-permute-start.20 = (bf16[64,2048]{1,0:T(8,128)(2,1)S(1)}, bf16[64,2048]{1,0:T(8,128)(2,1)S(1)}, u32[]{:S(2)}, u32[]{:S(2)}) collective-permute-start(bf16[64,2048]{1,0:T(8,128)(2,1)S(1)} %get-tuple-element.149), channel_id=1, source_target_pairs={{0,2},{1,3},{2,0},{3,1},{4,6},{5,7},{6,4},{7,5},{8,10},{9,11},{10,... | collective-permute-start | bytes 786440 | tf_op jit(solution)/shard_map/ppermute | solution.py:32
  224.0 12.1 %collective-permute-start.21 = (bf16[64,2048]{1,0:T(8,128)(2,1)S(1)}, bf16[64,2048]{1,0:T(8,128)(2,1)S(1)}, u32[]{:S(2)}, u32[]{:S(2)}) collective-permute-start(bf16[64,2048]{1,0:T(8,128)(2,1)S(1)} %get-tuple-element.148), channel_id=1, source_target_pairs={{0,3},{1,0},{2,1},{3,2},{4,7},{5,4},{6,5},{7,6},{8,11},{9,8},{10,9... | collective-permute-start | bytes 786440 | tf_op jit(solution)/shard_map/ppermute | solution.py:32
  237.7 10.5 %collective-permute-start.22 = (bf16[64,256]{1,0:T(8,128)(2,1)S(1)}, bf16[64,256]{1,0:T(8,128)(2,1)S(1)}, u32[]{:S(2)}, u32[]{:S(2)}) collective-permute-start(bf16[64,256]{1,0:T(8,128)(2,1)S(1)} %fusion.21), channel_id=1, source_target_pairs={{0,16},{4,20},{8,24},{12,28},{16,32},{20,36},{24,40},{28,44},{32,4... | collective-permute-start | bytes 98312 | tf_op jit(solution)/shard_map/ppermute | solution.py:38
  249.0 9.1 %collective-permute-start.26 = (bf16[320,256]{1,0:T(8,128)(2,1)S(1)}, bf16[320,256]{1,0:T(8,128)(2,1)S(1)}, u32[]{:S(2)}, u32[]{:S(2)}) collective-permute-start(bf16[320,256]{1,0:T(8,128)(2,1)S(1)} %get-tuple-element.305), channel_id=1, source_target_pairs={{0,3},{1,0},{2,1},{3,2},{4,7},{5,4},{6,5},{7,6},{8,11},{9,8},{10,9... | collective-permute-start | bytes 491528 | tf_op jit(solution)/shard_map/ppermute | solution.py:32
  275.0 9.0 %collective-permute-start.29 = (bf16[64,2048]{1,0:T(8,128)(2,1)S(1)}, bf16[64,2048]{1,0:T(8,128)(2,1)S(1)}, u32[]{:S(2)}, u32[]{:S(2)}) collective-permute-start(bf16[64,2048]{1,0:T(8,128)(2,1)S(1)} %add_convert_fusion.1), channel_id=1, source_target_pairs={{0,3},{1,0},{2,1},{3,2},{4,7},{5,4},{6,5},{7,6},{8,11},{9,8},{10,9... | collective-permute-start | bytes 786440 | tf_op jit(solution)/shard_map/ppermute | solution.py:32
  275.4 10.8 %collective-permute-start.30 = (bf16[64,2048]{1,0:T(8,128)(2,1)S(1)}, bf16[64,2048]{1,0:T(8,128)(2,1)S(1)}, u32[]{:S(2)}, u32[]{:S(2)}) collective-permute-start(bf16[64,2048]{1,0:T(8,128)(2,1)S(1)} %add_convert_fusion.1), channel_id=1, source_target_pairs={{0,2},{1,3},{2,0},{3,1},{4,6},{5,7},{6,4},{7,5},{8,10},{9,11},{10,... | collective-permute-start | bytes 786440 | tf_op jit(solution)/shard_map/ppermute | solution.py:32
  277.3 14.4 %collective-permute-start.31 = (bf16[64,2048]{1,0:T(8,128)(2,1)S(1)}, bf16[64,2048]{1,0:T(8,128)(2,1)S(1)}, u32[]{:S(2)}, u32[]{:S(2)}) collective-permute-start(bf16[64,2048]{1,0:T(8,128)(2,1)S(1)} %add_convert_fusion.1), channel_id=1, source_target_pairs={{0,1},{1,2},{2,3},{3,0},{4,5},{5,6},{6,7},{7,4},{8,9},{9,10},{10,1... | collective-permute-start | bytes 786440 | tf_op jit(solution)/shard_map/ppermute | solution.py:32
  313.8 15.2 %collective-permute-start.32 = (bf16[64,2048]{1,0:T(8,128)(2,1)S(1)}, bf16[64,2048]{1,0:T(8,128)(2,1)S(1)}, u32[]{:S(2)}, u32[]{:S(2)}) collective-permute-start(bf16[64,2048]{1,0:T(8,128)(2,1)S(1)} %get-tuple-element.144), channel_id=1, source_target_pairs={{0,1},{1,2},{2,3},{3,0},{4,5},{5,6},{6,7},{7,4},{8,9},{9,10},{10,1... | collective-permute-start | bytes 786440 | tf_op jit(solution)/shard_map/ppermute | solution.py:32
  314.1 14.9 %collective-permute-start.33 = (bf16[64,2048]{1,0:T(8,128)(2,1)S(1)}, bf16[64,2048]{1,0:T(8,128)(2,1)S(1)}, u32[]{:S(2)}, u32[]{:S(2)}) collective-permute-start(bf16[64,2048]{1,0:T(8,128)(2,1)S(1)} %get-tuple-element.146), channel_id=1, source_target_pairs={{0,2},{1,3},{2,0},{3,1},{4,6},{5,7},{6,4},{7,5},{8,10},{9,11},{10,... | collective-permute-start | bytes 786440 | tf_op jit(solution)/shard_map/ppermute | solution.py:32
  316.0 13.6 %collective-permute-start.34 = (bf16[64,2048]{1,0:T(8,128)(2,1)S(1)}, bf16[64,2048]{1,0:T(8,128)(2,1)S(1)}, u32[]{:S(2)}, u32[]{:S(2)}) collective-permute-start(bf16[64,2048]{1,0:T(8,128)(2,1)S(1)} %get-tuple-element.145), channel_id=1, source_target_pairs={{0,3},{1,0},{2,1},{3,2},{4,7},{5,4},{6,5},{7,6},{8,11},{9,8},{10,9... | collective-permute-start | bytes 786440 | tf_op jit(solution)/shard_map/ppermute | solution.py:32
  338.5 11.4 %collective-permute-start.35 = (bf16[320,256]{1,0:T(8,128)(2,1)S(1)}, bf16[320,256]{1,0:T(8,128)(2,1)S(1)}, u32[]{:S(2)}, u32[]{:S(2)}) collective-permute-start(bf16[320,256]{1,0:T(8,128)(2,1)S(1)} %get-tuple-element.166), channel_id=1, source_target_pairs={{0,1},{1,2},{2,3},{3,0},{4,5},{5,6},{6,7},{7,4},{8,9},{9,10},{10,1... | collective-permute-start | bytes 491528 | tf_op jit(solution)/shard_map/ppermute | solution.py:32
  339.5 10.7 %collective-permute-start.36 = (bf16[320,256]{1,0:T(8,128)(2,1)S(1)}, bf16[320,256]{1,0:T(8,128)(2,1)S(1)}, u32[]{:S(2)}, u32[]{:S(2)}) collective-permute-start(bf16[320,256]{1,0:T(8,128)(2,1)S(1)} %get-tuple-element.168), channel_id=1, source_target_pairs={{0,2},{1,3},{2,0},{3,1},{4,6},{5,7},{6,4},{7,5},{8,10},{9,11},{10,... | collective-permute-start | bytes 491528 | tf_op jit(solution)/shard_map/ppermute | solution.py:32
  366.4 15.6 %collective-permute-start.42 = (bf16[64,2048]{1,0:T(8,128)(2,1)}, bf16[64,2048]{1,0:T(8,128)(2,1)}, u32[]{:S(2)}, u32[]{:S(2)}) collective-permute-start(bf16[64,2048]{1,0:T(8,128)(2,1)} %get-tuple-element.118), channel_id=1, source_target_pairs={{0,3},{1,0},{2,1},{3,2},{4,7},{5,4},{6,5},{7,6},{8,11},{9,8},{10,9... | collective-permute-start | bytes 786440 | tf_op jit(solution)/shard_map/ppermute | solution.py:32
  369.0 12.9 %collective-permute-start.43 = (bf16[64,2048]{1,0:T(8,128)(2,1)}, bf16[64,2048]{1,0:T(8,128)(2,1)}, u32[]{:S(2)}, u32[]{:S(2)}) collective-permute-start(bf16[64,2048]{1,0:T(8,128)(2,1)} %get-tuple-element.118), channel_id=1, source_target_pairs={{0,2},{1,3},{2,0},{3,1},{4,6},{5,7},{6,4},{7,5},{8,10},{9,11},{10,... | collective-permute-start | bytes 786440 | tf_op jit(solution)/shard_map/ppermute | solution.py:32
  369.9 13.7 %collective-permute-start.44 = (bf16[64,2048]{1,0:T(8,128)(2,1)}, bf16[64,2048]{1,0:T(8,128)(2,1)}, u32[]{:S(2)}, u32[]{:S(2)}) collective-permute-start(bf16[64,2048]{1,0:T(8,128)(2,1)} %get-tuple-element.118), channel_id=1, source_target_pairs={{0,1},{1,2},{2,3},{3,0},{4,5},{5,6},{6,7},{7,4},{8,9},{9,10},{10,1... | collective-permute-start | bytes 786440 | tf_op jit(solution)/shard_map/ppermute | solution.py:32
  395.1 15.1 %collective-permute-start.45 = (bf16[64,2048]{1,0:T(8,128)(2,1)S(1)}, bf16[64,2048]{1,0:T(8,128)(2,1)S(1)}, u32[]{:S(2)}, u32[]{:S(2)}) collective-permute-start(bf16[64,2048]{1,0:T(8,128)(2,1)S(1)} %get-tuple-element.141), channel_id=1, source_target_pairs={{0,1},{1,2},{2,3},{3,0},{4,5},{5,6},{6,7},{7,4},{8,9},{9,10},{10,1... | collective-permute-start | bytes 786440 | tf_op jit(solution)/shard_map/ppermute | solution.py:32
  396.1 14.1 %collective-permute-start.46 = (bf16[64,2048]{1,0:T(8,128)(2,1)S(1)}, bf16[64,2048]{1,0:T(8,128)(2,1)S(1)}, u32[]{:S(2)}, u32[]{:S(2)}) collective-permute-start(bf16[64,2048]{1,0:T(8,128)(2,1)S(1)} %get-tuple-element.143), channel_id=1, source_target_pairs={{0,2},{1,3},{2,0},{3,1},{4,6},{5,7},{6,4},{7,5},{8,10},{9,11},{10,... | collective-permute-start | bytes 786440 | tf_op jit(solution)/shard_map/ppermute | solution.py:32
  398.2 12.7 %collective-permute-start.47 = (bf16[64,2048]{1,0:T(8,128)(2,1)S(1)}, bf16[64,2048]{1,0:T(8,128)(2,1)S(1)}, u32[]{:S(2)}, u32[]{:S(2)}) collective-permute-start(bf16[64,2048]{1,0:T(8,128)(2,1)S(1)} %get-tuple-element.142), channel_id=1, source_target_pairs={{0,3},{1,0},{2,1},{3,2},{4,7},{5,4},{6,5},{7,6},{8,11},{9,8},{10,9... | collective-permute-start | bytes 786440 | tf_op jit(solution)/shard_map/ppermute | solution.py:32
  419.6 11.7 %collective-permute-start.48 = (bf16[320,256]{1,0:T(8,128)(2,1)S(1)}, bf16[320,256]{1,0:T(8,128)(2,1)S(1)}, u32[]{:S(2)}, u32[]{:S(2)}) collective-permute-start(bf16[320,256]{1,0:T(8,128)(2,1)S(1)} %get-tuple-element.163), channel_id=1, source_target_pairs={{0,1},{1,2},{2,3},{3,0},{4,5},{5,6},{6,7},{7,4},{8,9},{9,10},{10,1... | collective-permute-start | bytes 491528 | tf_op jit(solution)/shard_map/ppermute | solution.py:32
  420.8 10.6 %collective-permute-start.49 = (bf16[320,256]{1,0:T(8,128)(2,1)S(1)}, bf16[320,256]{1,0:T(8,128)(2,1)S(1)}, u32[]{:S(2)}, u32[]{:S(2)}) collective-permute-start(bf16[320,256]{1,0:T(8,128)(2,1)S(1)} %get-tuple-element.165), channel_id=1, source_target_pairs={{0,2},{1,3},{2,0},{3,1},{4,6},{5,7},{6,4},{7,5},{8,10},{9,11},{10,... | collective-permute-start | bytes 491528 | tf_op jit(solution)/shard_map/ppermute | solution.py:32
  435.4 9.1 %collective-permute-start.54 = (bf16[64,256]{1,0:T(8,128)(2,1)S(1)}, bf16[64,256]{1,0:T(8,128)(2,1)S(1)}, u32[]{:S(2)}, u32[]{:S(2)}) collective-permute-start(bf16[64,256]{1,0:T(8,128)(2,1)S(1)} %get-tuple-element.261), channel_id=1, source_target_pairs={{16,0},{20,4},{24,8},{28,12},{32,16},{36,20},{40,24},{44,28},{48,3... | collective-permute-start | bytes 98312 | tf_op jit(solution)/shard_map/ppermute | solution.py:38
  447.7 9.6 %collective-permute-start.55 = (bf16[2,29,16,128]{3,2,1,0:T(8,128)(2,1)S(1)}, bf16[2,29,16,128]{3,2,1,0:T(8,128)(2,1)S(1)}, u32[]{:S(2)}, u32[]{:S(2)}) collective-permute-start(bf16[2,29,16,128]{3,2,1,0:T(8,128)(2,1)S(1)} %get-tuple-element.150), channel_id=1, source_target_pairs={{0,1},{1,2},{2,3},{3,0},{4,5},{5,6},{6,7},{7,4},{8,9},{9,10},{10,1... | collective-permute-start | bytes 712712 | tf_op jit(solution)/shard_map/ppermute | solution.py:32
  449.5 12.0 %collective-permute-start.56 = (bf16[2,29,16,128]{3,2,1,0:T(8,128)(2,1)S(1)}, bf16[2,29,16,128]{3,2,1,0:T(8,128)(2,1)S(1)}, u32[]{:S(2)}, u32[]{:S(2)}) collective-permute-start(bf16[2,29,16,128]{3,2,1,0:T(8,128)(2,1)S(1)} %get-tuple-element.152), channel_id=1, source_target_pairs={{0,2},{1,3},{2,0},{3,1},{4,6},{5,7},{6,4},{7,5},{8,10},{9,11},{10,... | collective-permute-start | bytes 712712 | tf_op jit(solution)/shard_map/ppermute | solution.py:32
  451.4 10.3 %collective-permute-start.57 = (bf16[2,29,16,128]{3,2,1,0:T(8,128)(2,1)S(1)}, bf16[2,29,16,128]{3,2,1,0:T(8,128)(2,1)S(1)}, u32[]{:S(2)}, u32[]{:S(2)}) collective-permute-start(bf16[2,29,16,128]{3,2,1,0:T(8,128)(2,1)S(1)} %get-tuple-element.151), channel_id=1, source_target_pairs={{0,3},{1,0},{2,1},{3,2},{4,7},{5,4},{6,5},{7,6},{8,11},{9,8},{10,9... | collective-permute-start | bytes 712712 | tf_op jit(solution)/shard_map/ppermute | solution.py:32
  453.2 11.1 %collective-permute-start.65 = (bf16[64,2048]{1,0:T(8,128)(2,1)S(1)}, bf16[64,2048]{1,0:T(8,128)(2,1)S(1)}, u32[]{:S(2)}, u32[]{:S(2)}) collective-permute-start(bf16[64,2048]{1,0:T(8,128)(2,1)S(1)} %select_convert_fusion), channel_id=1, source_target_pairs={{0,64},{64,0},{1,65},{65,1},{2,66},{66,2},{3,67},{67,3},{4,68},{68... | collective-permute-start | bytes 786440 | tf_op jit(solution)/shard_map/ppermute | solution.py:556
  480.3 8.5 %collective-permute-start.69 = (bf16[4,16,128]{2,1,0:T(8,128)(2,1)S(1)}, bf16[4,16,128]{2,1,0:T(8,128)(2,1)S(1)}, u32[]{:S(2)}, u32[]{:S(2)}) collective-permute-start(bf16[4,16,128]{2,1,0:T(8,128)(2,1)S(1)} %bitcast.780), channel_id=1, source_target_pairs={{0,8},{4,12},{8,0},{12,4},{16,24},{20,28},{24,16},{28,20},{32,40},... | collective-permute-start | bytes 49160 | tf_op jit(solution)/shard_map/ppermute | solution.py:43
  481.5 19.6 %collective-permute-start.61 = (bf16[64,2048]{1,0:T(8,128)(2,1)S(1)}, bf16[64,2048]{1,0:T(8,128)(2,1)S(1)}, u32[]{:S(2)}, u32[]{:S(2)}) collective-permute-start(bf16[64,2048]{1,0:T(8,128)(2,1)S(1)} %get-tuple-element.138), channel_id=1, source_target_pairs={{0,1},{1,2},{2,3},{3,0},{4,5},{5,6},{6,7},{7,4},{8,9},{9,10},{10,1... | collective-permute-start | bytes 786440 | tf_op jit(solution)/shard_map/ppermute | solution.py:32
  483.0 18.1 %collective-permute-start.62 = (bf16[64,2048]{1,0:T(8,128)(2,1)S(1)}, bf16[64,2048]{1,0:T(8,128)(2,1)S(1)}, u32[]{:S(2)}, u32[]{:S(2)}) collective-permute-start(bf16[64,2048]{1,0:T(8,128)(2,1)S(1)} %get-tuple-element.140), channel_id=1, source_target_pairs={{0,2},{1,3},{2,0},{3,1},{4,6},{5,7},{6,4},{7,5},{8,10},{9,11},{10,... | collective-permute-start | bytes 786440 | tf_op jit(solution)/shard_map/ppermute | solution.py:32
  505.0 9.2 %collective-permute-start.76 = (bf16[2,21,16,128]{3,2,1,0:T(8,128)(2,1)S(1)}, bf16[2,21,16,128]{3,2,1,0:T(8,128)(2,1)S(1)}, u32[]{:S(2)}, u32[]{:S(2)}) collective-permute-start(bf16[2,21,16,128]{3,2,1,0:T(8,128)(2,1)S(1)} %get-tuple-element.178), channel_id=1, source_target_pairs={{0,1},{1,2},{2,3},{3,0},{4,5},{5,6},{6,7},{7,4},{8,9},{9,10},{10,1... | collective-permute-start | bytes 516104 | tf_op jit(solution)/shard_map/ppermute | solution.py:32
  505.0 9.2 %collective-permute-start.77 = (bf16[2,21,16,128]{3,2,1,0:T(8,128)(2,1)S(1)}, bf16[2,21,16,128]{3,2,1,0:T(8,128)(2,1)S(1)}, u32[]{:S(2)}, u32[]{:S(2)}) collective-permute-start(bf16[2,21,16,128]{3,2,1,0:T(8,128)(2,1)S(1)} %get-tuple-element.178), channel_id=1, source_target_pairs={{0,2},{1,3},{2,0},{3,1},{4,6},{5,7},{6,4},{7,5},{8,10},{9,11},{10,... | collective-permute-start | bytes 516104 | tf_op jit(solution)/shard_map/ppermute | solution.py:32
  (165 other events, 2797.0 us)
Sparse Core Ops, SparseCore 0:
  11.6 122.3 all-gather.3
  136.9 71.8 all-gather.5
  211.7 72.0 all-gather.7
